TPU v7x, 32 devices: a whole 2x2x4 slice. The times are simulated.
32 devices in a mesh: groups: 2 (over y), shard: 4 (over z), head: 2 (over x), sub: 2 (over core).
Axes of the slice: x: 2, y: 2, z: 4, core: 2. Of those that a mesh axis runs over, the one named last changes fastest.
Arguments:
- grid_features: bfloat16 [64, 64, 1024], P(('groups', 'shard', 'sub'), None, 'head'), parts along dimension 0, may hold values from -6 to 6
- owners: int32 [64, 1], P(('groups', 'shard', 'sub')), parts along dimension 0, may hold values from 0 to 3; in each aligned block of 4 rows (0 to 3, 4 to 7, ...) at most 2 rows name the same one
- adjacency: int32 [64, 8], P(('groups', 'shard', 'sub')), parts along dimension 0, may hold values from 0 to 15, all different within a row
- mesh_nodes: bfloat16 [2048, 1024], P(('groups', 'shard', 'sub')), parts along dimension 0, may hold values from -130 to 130
- norm_gain: float32 [1024], replicated, may hold values from 0.1 to 1.9
- query_weight: bfloat16 [1024, 1024], P(None, 'head'), may hold values from -0.15625 to 0.15625
- key_weight: bfloat16 [1024, 1024], P(None, 'head'), may hold values from -0.15625 to 0.15625
- value_weight: bfloat16 [1024, 1024], P(None, 'head'), may hold values from -0.1875 to 0.1875
- output_weight: bfloat16 [1024, 1024], P('head'), may hold values from -0.1875 to 0.1875
- up_weight: bfloat16 [1024, 4096], P(None, 'head'), may hold values from -0.1875 to 0.1875
- down_weight: bfloat16 [4096, 1024], P('head'), may hold values from -0.09375 to 0.09375
Outputs:
- decoded: bfloat16 [128, 64, 1024], P(('groups', 'shard', 'sub'), None, 'head'), parts along dimension 0
There are 2 independent parts, one for each index of `groups`. A program takes and returns all parts, laid end to end along the dimension named above; an argument that names none is the same for every part. Nothing has to cross between parts.
Inputs may be any that keep to these rules, and one draw needn't show every extreme that they name: `owners`: within the 4 blocks of one device at most 2 have the same owner, and in every draw some device has exactly 2 blocks of one owner. `adjacency`: each grid block names 8 different mesh blocks, and every mesh block is named by some grid block.
All inputs are finite; a program needn't handle non-finite values.
Results may differ from a plain program's by a relative error of at most 0.011.
Values may be sent and summed in bfloat16 or wider, within the bound.
No kernel may reach another device: no remote copies, remote signals or barrier semaphores. Data moves between devices by JAX's collectives and lax.ppermute only.
A program may use at most 128 MiB of HBM per device.

v0:
```python
import math

import jax
import jax.numpy as jnp
from jax import lax
from jax.sharding import PartitionSpec as P

D = 1024
HEAD_DIM = 64
CAP = 2


epsilon = 1e-05


def attend(queries, key_table, value_table, chosen, scaling):
    count = chosen.shape[0]
    picked_keys = key_table[chosen]
    picked_keys = picked_keys.reshape(count, -1, picked_keys.shape[3], picked_keys.shape[4])
    picked_values = value_table[chosen]
    picked_values = picked_values.reshape(count, -1, picked_values.shape[3], picked_values.shape[4])
    scores = (
        jnp.einsum("gqhe,gkhe->ghqk", queries, picked_keys, preferred_element_type=jnp.float32)
        * scaling
    )
    highest = jnp.max(scores, axis=-1, keepdims=True)
    weights = jnp.exp(scores - highest)
    weights = (weights / jnp.sum(weights, axis=-1, keepdims=True)).astype(jnp.bfloat16)
    result = jnp.einsum(
        "ghqk,gkhe->gqhe", weights, picked_values, preferred_element_type=jnp.float32
    )
    return result.astype(jnp.bfloat16)


def local(
    grid_features,
    owners,
    adjacency,
    mesh_nodes,
    norm_gain,
    query_weight,
    key_weight,
    value_weight,
    output_weight,
    up_weight,
    down_weight,
):
    shard_count = lax.axis_size("shard")
    head_count = lax.axis_size("head")
    local_blocks, block_rows, feature_share = grid_features.shape
    slots = shard_count * CAP
    owner_col = owners[:, 0]
    position = jnp.arange(local_blocks, dtype=jnp.int32)
    earlier = (owner_col[:, None] == owner_col[None, :]) & (position[None, :] < position[:, None])
    target = owner_col * CAP + jnp.sum(earlier.astype(jnp.int32), axis=1)
    dispatch = (target[:, None] == jnp.arange(slots, dtype=jnp.int32)[None, :]).astype(jnp.bfloat16)
    offset = lax.axis_index("head") * (D // head_count)
    projected = jnp.stack(
        (
            jnp.dot(mesh_nodes, key_weight, preferred_element_type=jnp.float32).astype(
                jnp.bfloat16
            ),
            jnp.dot(mesh_nodes, value_weight, preferred_element_type=jnp.float32).astype(
                jnp.bfloat16
            ),
        )
    )
    tables = lax.all_gather(projected, ("shard", "sub"), axis=1, tiled=True)
    head_local = query_weight.shape[1] // HEAD_DIM
    key_table = tables[0].reshape(-1, block_rows, head_local, HEAD_DIM)
    value_table = tables[1].reshape(-1, block_rows, head_local, HEAD_DIM)
    send_lists = jnp.full((slots, adjacency.shape[1]), -1, jnp.int32).at[target].set(adjacency)
    send_lists = send_lists.reshape(shard_count, CAP, -1)
    complete = lax.all_gather(grid_features, "head", axis=2, tiled=True)
    outgoing = jnp.einsum(
        "gs,gbd->sbd", dispatch, complete, preferred_element_type=jnp.float32
    ).astype(jnp.bfloat16)
    arrived, lists = (
        lax.all_to_all(
            outgoing.reshape(shard_count, CAP, block_rows, D),
            "shard",
            split_axis=0,
            concat_axis=0,
            tiled=True,
        ),
        lax.all_to_all(send_lists, "shard", split_axis=0, concat_axis=0, tiled=True),
    )
    arrived = arrived.reshape(slots, block_rows, D)
    residual = lax.dynamic_slice_in_dim(arrived, offset, D // head_count, 2)
    lists = lists.reshape(slots, -1)
    count = arrived.shape[0]
    values_f = arrived.astype(jnp.float32)
    average = jnp.mean(values_f, axis=-1, keepdims=True)
    centered = values_f - average
    variance = jnp.mean(centered * centered, axis=-1, keepdims=True)
    normed = (centered * lax.rsqrt(variance + epsilon) * norm_gain).astype(jnp.bfloat16)
    flattened = normed.reshape(-1, D)
    queries = jnp.dot(flattened, query_weight, preferred_element_type=jnp.float32).astype(
        jnp.bfloat16
    )
    blocks_each = math.gcd(count, max(1, 512 // block_rows))
    steps_count = count // blocks_each
    queries = queries.reshape(steps_count, blocks_each, block_rows, head_local, HEAD_DIM)

    def attend_step(operands):
        return attend(operands[0], key_table, value_table, operands[1], HEAD_DIM ** (-0.5))

    attended = lax.map(
        attend_step, (queries, jnp.maximum(lists, 0).reshape(steps_count, blocks_each, -1))
    )
    attended = attended.reshape(-1, head_local * HEAD_DIM)
    hidden = jax.nn.gelu(
        jnp.dot(flattened, up_weight, preferred_element_type=jnp.float32), approximate=False
    ).astype(jnp.bfloat16)
    branch = jnp.dot(attended, output_weight, preferred_element_type=jnp.float32)
    branch = branch + jnp.dot(hidden, down_weight, preferred_element_type=jnp.float32)
    branch = branch.reshape(count, block_rows, D)
    reduced = lax.psum_scatter(
        branch.astype(jnp.bfloat16), "head", scatter_dimension=2, tiled=True
    ).astype(jnp.float32)
    occupied = lists[:, 0] >= 0
    summed = residual.astype(jnp.float32) + reduced
    return jnp.where(occupied[:, None, None], summed, 0.0).astype(jnp.bfloat16)


def solution(mesh):
    return jax.shard_map(
        local,
        mesh=mesh,
        in_specs=(
            P(("groups", "shard", "sub"), None, "head"),
            P(("groups", "shard", "sub"), None),
            P(("groups", "shard", "sub"), None),
            P(("groups", "shard", "sub"), None),
            P(),
            P(None, "head"),
            P(None, "head"),
            P(None, "head"),
            P("head", None),
            P(None, "head"),
            P("head", None),
        ),
        out_specs=P(("groups", "shard", "sub"), None, "head"),
        check_vma=False,
    )
```

profile of v0, /device:TPU:0, one launch (start us, length us, event | category | flops | bytes accessed | tf_op | source)
XLA Modules:
  0.0 169.4 jit_solution(6054629422002956868)
XLA Ops:
  6.5 0.0 copy-start
  6.5 0.0 copy-start.4
  6.5 0.0 copy-start.3
  6.5 1.0 convert_reduce_fusion.1
  7.5 0.7 fusion.41
  8.2 1.3 scatter_custom_fusion
  9.5 6.3 %all-to-all-start = ((s32[4,2,8]{2,1,0:T(2,128)}), s32[4,2,8]{2,1,0:T(2,128)S(1)}, u32[]{:S(2)}, u32[]{:S(2)}) async-start(s32[4,2,8]{2,1,0:T(2,128)} %bitcast.3), calls=%async_computation | async-start | bytes 8192 | tf_op jit(solution)/shard_map/all_to_all | solution.py:86
  15.8 1.2 copy.29
  17.0 8.4 %all_gather.6 = bf16[4,64,1024]{2,0,1:T(4,128)(2,1)S(1)} all-gather(bf16[4,64,512]{2,0,1:T(4,128)(2,1)S(1)} %copy.29), channel_id=1, replica_groups=mesh['groups'=2,'shard'=4,'head'=2,'sub'=2] {'head'}, dimensions={2}, use_global_device_ids=true | all-gather | bytes 786432 | tf_op jit(solution)/shard_map/all_gather | solution.py:74
  25.4 0.6 convolution_convert_fusion
  26.0 1.6 copy.37
  27.6 0.0 copy-start.5
  27.6 0.0 all-to-all-done
  27.6 4.9 %all-to-all-start.1 = ((bf16[4,2,64,1024]{3,2,1,0:T(8,128)(2,1)}), bf16[4,2,64,1024]{3,2,1,0:T(8,128)(2,1)S(1)}, u32[]{:S(2)}, u32[]{:S(2)}) async-start(bf16[4,2,64,1024]{3,2,1,0:T(8,128)(2,1)} %bitcast.7), calls=%async_computation.1 | async-start | bytes 2097152 | tf_op jit(solution)/shard_map/all_to_all | solution.py:79
  32.5 0.0 all-gather.2.cloned.1.call-start
  32.5 0.0 copy-done.4
  32.5 0.0 copy-done.3
  32.5 0.3 fusion.31
  32.9 1.5 fusion.32
  34.4 0.7 pad_maximum_fusion
  35.1 0.0 all-gather.2.cloned.1.call-update
  35.2 0.0 reduce-scatter.2.cloned.1.call-start
  35.2 0.1 reshape.103
  35.3 36.1 %all-to-all-done.1 = bf16[4,2,64,1024]{3,2,1,0:T(8,128)(2,1)S(1)} async-done(((bf16[4,2,64,1024]{3,2,1,0:T(8,128)(2,1)}), bf16[4,2,64,1024]{3,2,1,0:T(8,128)(2,1)S(1)}, u32[]{:S(2)}, u32[]{:S(2)}) %all-to-all-start.1) | async-done | bytes 1048608 | tf_op jit(solution)/shard_map/all_to_all | solution.py:79
  71.5 0.0 copy-start.1
  71.5 0.2 convert_reduce_fusion
  71.7 0.1 div.21
  71.8 0.4 multiply_reduce_fusion.1
  72.2 0.1 rsqrt.12
  72.3 0.0 copy-done.5
  72.3 0.4 fusion.22
  72.7 2.7 %convolution_convert_fusion.1 = bf16[512,512]{1,0:T(8,128)(2,1)} fusion(bf16[512,1024]{1,0:T(8,128)(2,1)S(1)} %fusion.22, bf16[1024,512]{1,0:T(8,128)(2,1)} %param.16), kind=kOutput, calls=%fused_computation.43 | convolution fusion | flops 537133056 | bytes 2621440 | tf_op jit(solution)/shard_map/dot_general | solution.py:98
  75.4 2.5 %squeeze.10 = bf16[8,64,8,64]{3,2,1,0:T(8,128)(2,1)} reshape(bf16[512,512]{1,0:T(8,128)(2,1)} %convolution_convert_fusion.1) | data formatting | bytes 1048576 | tf_op jit(solution)/shard_map/while/body/jit(dynamic_index_in_dim)/squeeze | solution.py:108
  77.9 0.0 copy-done.1
  77.9 16.7 %fusion.23 = f32[512,1024]{1,0:T(8,128)} fusion(bf16[2048,1024]{1,0:T(8,128)(2,1)} %param.21, bf16[512,1024]{1,0:T(8,128)(2,1)S(1)} %fusion.22, bf16[1024,2048]{1,0:T(8,128)(2,1)} %param.20), kind=kOutput, calls=%fused_computation.39 | convolution fusion | flops 4363124736 | bytes 11534336 | tf_op jit(solution)/shard_map/dot_general | solution.py:116
  94.6 0.0 all-gather.2.cloned.1.call-done
  94.6 3.0 %fusion.74 = (bf16[1,1024,512]{2,1,0:T(8,128)(2,1)}, bf16[1,1024,512]{2,1,0:T(8,128)(2,1)}) fusion(bf16[2,1024,512]{2,1,0:T(8,128)(2,1)} %all-gather.2.cloned.1.call-done), kind=kLoop, calls=%fused_computation.101 | loop fusion | bytes 4194304 | tf_op jit(solution)/shard_map/slice | solution.py:71
  97.6 2.8 %reshape_squeeze.7 = bf16[16,64,8,64]{3,2,1,0:T(8,128)(2,1)S(1)} reshape(bf16[1,1024,512]{2,1,0:T(8,128)(2,1)} %get-tuple-element.16) | data formatting | bytes 2097152 | tf_op jit(solution)/shard_map/reshape;squeeze | solution.py:70
  100.4 5.4 %gather_fusion.1 = bf16[64,64,8,64]{3,2,1,0:T(8,128)(2,1)} fusion(bf16[16,64,8,64]{3,2,1,0:T(8,128)(2,1)S(1)} %reshape_squeeze.7, s32[1024]{0:T(1024)S(1)} %pad_clamp_fusion), kind=kCustom, calls=%fused_computation.1 | custom fusion | bytes 8388864 | tf_op jit(solution)/shard_map/while/body/eval_jaxpr/gather | solution.py:18
  105.8 6.8 %fusion.1 = f32[8,8,64,512]{3,2,1,0:T(8,128)S(1)} fusion(bf16[8,512,8,64]{3,2,1,0:T(8,128)(2,1)} %bitcast.49, bf16[8,64,8,64]{3,2,1,0:T(8,128)(2,1)} %squeeze.10), kind=kOutput, calls=%fused_computation.4 | convolution fusion | flops 268435456 | bytes 13107200 | tf_op jit(solution)/shard_map/while/body/eval_jaxpr/gqhe,gkhe->ghqk/dot_general | solution.py:23
  112.6 4.1 %fusion.75 = (f32[8,8,64]{2,1,0:T(8,128)S(1)}, f32[8,8,64,512]{3,2,1,0:T(8,128)}) fusion(f32[8,8,64,512]{3,2,1,0:T(8,128)S(1)} %fusion.1), kind=kOutput, calls=%fused_computation.102 | output fusion | flops 8389119 | bytes 16793600 | tf_op jit(solution)/shard_map/while/body/eval_jaxpr/sub | solution.py:27
  116.7 2.8 %reshape_squeeze.6 = bf16[16,64,8,64]{3,2,1,0:T(8,128)(2,1)S(1)} reshape(bf16[1,1024,512]{2,1,0:T(8,128)(2,1)} %get-tuple-element.15) | data formatting | bytes 2097152 | tf_op jit(solution)/shard_map/reshape;squeeze | solution.py:71
  119.5 5.4 %gather_fusion = bf16[64,64,8,64]{3,2,1,0:T(8,128)(2,1)} fusion(bf16[16,64,8,64]{3,2,1,0:T(8,128)(2,1)S(1)} %reshape_squeeze.6, s32[1024]{0:T(1024)S(1)} %pad_clamp_fusion), kind=kCustom, calls=%fused_computation | custom fusion | bytes 8388864 | tf_op jit(solution)/shard_map/while/body/eval_jaxpr/gather | solution.py:20
  124.8 8.9 %fusion.28 = bf16[8,64,8,64]{1,3,2,0:T(8,128)(2,1)S(1)} fusion(f32[8,8,64,512]{3,2,1,0:T(8,128)} %get-tuple-element.28, f32[8,8,64]{2,1,0:T(8,128)S(1)} %get-tuple-element.26, bf16[8,512,8,64]{3,2,1,0:T(8,128)(2,1)} %bitcast.51), kind=kOutput, calls=%fused_computation.42 | convolution fusion | flops 272891904 | bytes 13123584 | tf_op jit(solution)/shard_map/while/body/eval_jaxpr/ghqk,gkhe->gqhe/dot_general | solution.py:29
  133.7 0.7 copy.36
  134.5 0.0 copy-start.2
  134.5 1.4 reshape.99
  135.9 0.0 copy-done
  135.9 3.5 %add_convert_fusion = bf16[512,1024]{1,0:T(8,128)(2,1)} fusion(f32[512,1024]{1,0:T(8,128)} %fusion.23, bf16[512,512]{1,0:T(8,128)(2,1)} %reshape.99, bf16[512,1024]{1,0:T(8,128)(2,1)S(1)} %copy-done), kind=kOutput, calls=%fused_computation.37 | convolution fusion | flops 537919488 | bytes 4718592 | tf_op jit(solution)/shard_map/dot_general | solution.py:115
  139.4 0.0 reduce-scatter.2.cloned.1.call-update
  139.4 0.1 fusion.34
  139.5 21.1 %reduce-scatter.2.cloned.1.call-done = bf16[8,64,512]{2,1,0:T(8,128)(2,1)} async-done(((bf16[8,64,1024]{2,1,0:T(8,128)(2,1)}), bf16[8,64,512]{2,1,0:T(8,128)(2,1)}) %reduce-scatter.2.cloned.1.call-update) | async-done | bytes 524304 | tf_op jit(solution)/shard_map/reduce_scatter | solution.py:118
  160.6 0.0 copy-done.2
  160.6 2.1 %select_convert_fusion = bf16[8,64,512]{2,1,0:T(8,128)(2,1)} fusion(bf16[8,64,512]{2,1,0:T(8,128)(2,1)} %reduce-scatter.2.cloned.1.call-done, bf16[8,64,1024]{2,1,0:T(8,128)(2,1)S(1)} %bitcast.50, s32[]{:T(128)S(6)} %select_n.16, pred[8]{0:T(512)(128)(4,1)S(1)} %fusion.34), kind=kLoop, calls=%fused_computation.50 | loop fusion | flops 1310720 | bytes 1572876 | tf_op jit(solution)/shard_map/convert_element_type | solution.py:123
  (4 shorter events, 0.0 us)
Async XLA Ops:
  6.5 129.3 %copy-start = (bf16[512,1024]{1,0:T(8,128)(2,1)S(1)}, bf16[512,1024]{1,0:T(8,128)(2,1)}, u32[]{:S(2)}) copy-start(bf16[512,1024]{1,0:T(8,128)(2,1)} %param.19) | copy-start | bytes 3145732
  6.5 26.0 %copy-start.4 = (bf16[128,1024]{1,0:T(8,128)(2,1)S(1)}, bf16[128,1024]{1,0:T(8,128)(2,1)}, u32[]{:S(2)}) copy-start(bf16[128,1024]{1,0:T(8,128)(2,1)} %param.14) | copy-start | bytes 786436
  6.5 26.0 %copy-start.3 = (bf16[1024,512]{1,0:T(8,128)(2,1)S(1)}, bf16[1024,512]{1,0:T(8,128)(2,1)}, u32[]{:S(2)}) copy-start(bf16[1024,512]{1,0:T(8,128)(2,1)} %param.17) | copy-start | bytes 3145732
  9.5 18.1 %all-to-all-start = ((s32[4,2,8]{2,1,0:T(2,128)}), s32[4,2,8]{2,1,0:T(2,128)S(1)}, u32[]{:S(2)}, u32[]{:S(2)}) async-start(s32[4,2,8]{2,1,0:T(2,128)} %bitcast.3), calls=%async_computation | async-start | bytes 8192 | tf_op jit(solution)/shard_map/all_to_all | solution.py:86
  27.6 44.7 %copy-start.5 = (f32[1024]{0:T(1024)S(1)}, f32[1024]{0:T(1024)}, u32[]{:S(2)}) copy-start(f32[1024]{0:T(1024)} %param.15) | copy-start | bytes 12292
  27.6 43.9 %all-to-all-start.1 = ((bf16[4,2,64,1024]{3,2,1,0:T(8,128)(2,1)}), bf16[4,2,64,1024]{3,2,1,0:T(8,128)(2,1)S(1)}, u32[]{:S(2)}, u32[]{:S(2)}) async-start(bf16[4,2,64,1024]{3,2,1,0:T(8,128)(2,1)} %bitcast.7), calls=%async_computation.1 | async-start | bytes 2097152 | tf_op jit(solution)/shard_map/all_to_all | solution.py:79
  32.5 62.1 %all-gather.2.cloned.1.call-start = ((), (), s32[]{:S(2)}) async-start(), calls=%async_computation.3 | async-start | bytes 2359296 | tf_op jit(solution)/shard_map/all_gather | solution.py:68
  35.2 125.4 %reduce-scatter.2.cloned.1.call-start = ((), (), s32[]{:S(2)}) async-start(), calls=%async_computation.4 | async-start | bytes 1572864 | tf_op jit(solution)/shard_map/reduce_scatter | solution.py:118
  71.5 6.4 %copy-start.1 = (bf16[4,2,64,1024]{3,2,1,0:T(8,128)(2,1)}, bf16[4,2,64,1024]{3,2,1,0:T(8,128)(2,1)S(1)}, u32[]{:S(2)}) copy-start(bf16[4,2,64,1024]{3,2,1,0:T(8,128)(2,1)S(1)} %all-to-all-done.1) | copy-start | bytes 3145732
  134.5 26.1 %copy-start.2 = (bf16[4,2,64,1024]{3,2,1,0:T(8,128)(2,1)S(1)}, bf16[4,2,64,1024]{3,2,1,0:T(8,128)(2,1)}, u32[]{:S(2)}) copy-start(bf16[4,2,64,1024]{3,2,1,0:T(8,128)(2,1)} %copy-done.1) | copy-start | bytes 3145732
Sparse Core Ops, SparseCore 0:
  35.3 39.8 all-gather.1
  139.5 21.0 reduce-scatter.1
where the time goes:
time: 170 us; the launch traced here: 169 us
  waiting for transfers between devices  57.2 us (34%)
  matrix products  41 us (24%)
  local copies, waits for them, and re-layouts  28.2 us (17%)
  between operations  13.5 us (8%)
  starting transfers between devices  11.3 us (7%)
  other arithmetic  9.74 us (6%)
  blocking collectives  8.44 us (5%)
    all_to_all x1, waiting for transfers between devices, local(): lax.all_to_all(outgoing.reshape(shard_count, CAP, block_rows, D), 'shard'...  36.1 us
    reduce_scatter x1, waiting for transfers between devices, local(): lax.psum_scatter(branch.astype(jnp.bfloat16), 'head', scatter_dimension=2...  21.1 us
    dot_general x1, matrix products, local(): jnp.dot(hidden, down_weight, preferred_element_type=jnp.float32)  16.7 us
    dot_general x1, matrix products, attend(): jnp.einsum('ghqk,gkhe->gqhe', weights, picked_values, preferred_element_t...  8.86 us
    all_gather x1, blocking collectives, local(): complete = lax.all_gather(grid_features, 'head', axis=2, tiled=True)  8.44 us
    dot_general x1, matrix products, attend(): jnp.einsum('gqhe,gkhe->ghqk', queries, picked_keys, preferred_element_typ...  6.8 us
    all_to_all x1, starting transfers between devices, local(): lax.all_to_all(send_lists, 'shard', split_axis=0, concat_axis=0, tiled=True)  6.32 us
    gather x1, local copies, waits for them, and re-layouts, attend(): picked_keys = key_table[chosen]  5.36 us
  transfers between devices with their start and end apart: 4, of which 2 were waited for; matrix products, arithmetic and copies ran while one was open for 17% of the time, Pallas kernels for 0%

commit v1 on v0

--- a/solution.py
+++ b/solution.py
@@ -1,19 +1,398 @@
+import functools
 import math
 
 import jax
 import jax.numpy as jnp
 from jax import lax
+from jax.experimental import pallas as pl
+from jax.experimental.pallas import tpu as pltpu
 from jax.sharding import PartitionSpec as P
 
 D = 1024
 HEAD_DIM = 64
 CAP = 2
+BLOCK = 64
+QUAD = 4
+WIDE = QUAD * HEAD_DIM
+MIB = 1 << 20
 
 
 epsilon = 1e-05
 
 
-def attend(queries, key_table, value_table, chosen, scaling):
+def dot(a, b):
+    return jnp.dot(a, b, preferred_element_type=jnp.float32)
+
+
+def gelu(x):
+    return 0.5 * x * (1.0 + lax.erf(x * (2.0**-0.5)))
+
+
+def whole(space):
+    return pl.BlockSpec(memory_space=space)
+
+
+def mlp_kernel(
+    own, other, gain, wq, wup, wdn, q_out, mlp_out, x_s, wq_s, wup_s, wdn_s, x_sem, w_sem
+):
+    h = lax.axis_index("head")
+    half = own.shape[1]
+    units = wup.shape[1]
+    chunk = units // wup_s.shape[0]
+    mine = pl.ds(pl.multiple_of(h * half, half), half)
+    theirs = pl.ds(pl.multiple_of((1 - h) * half, half), half)
+    copies = [
+        pltpu.make_async_copy(own, x_s.at[:, mine], x_sem.at[0]),
+        pltpu.make_async_copy(other, x_s.at[:, theirs], x_sem.at[1]),
+        pltpu.make_async_copy(wq, wq_s, x_sem.at[2]),
+    ]
+    for copy in copies:
+        copy.start()
+    ups, downs = [], []
+    for c in range(wup_s.shape[0]):
+        span = pl.ds(c * chunk, chunk)
+        ups.append(pltpu.make_async_copy(wup.at[:, span], wup_s.at[c], w_sem.at[0, c]))
+        ups[c].start()
+        pair = []
+        for part, columns in enumerate((theirs, mine)):
+            pair.append(
+                pltpu.make_async_copy(
+                    wdn.at[span, columns],
+                    wdn_s.at[span, pl.ds(part * half, half)],
+                    w_sem.at[1 + part, c],
+                )
+            )
+            pair[part].start()
+        downs.append(pair)
+    copies[0].wait()
+    copies[1].wait()
+    x = x_s[...].astype(jnp.float32)
+    centered = x - jnp.mean(x, axis=-1, keepdims=True)
+    variance = jnp.mean(centered * centered, axis=-1, keepdims=True)
+    normed = (centered * lax.rsqrt(variance + epsilon) * gain[...]).astype(jnp.bfloat16)
+    copies[2].wait()
+    q_out[...] = dot(normed, wq_s[...]).astype(jnp.bfloat16)
+    for c in range(wup_s.shape[0]):
+        ups[c].wait()
+        hidden = gelu(dot(normed, wup_s[c])).astype(jnp.bfloat16)
+        downs[c][0].wait()
+        downs[c][1].wait()
+        term = dot(hidden, wdn_s[c * chunk : (c + 1) * chunk, :])
+        if c == 0:
+            mlp_out[...] = term
+        else:
+            mlp_out[...] += term
+
+
+def run_mlp(own, other, gain, wq, wup, wdn):
+    rows, half = own.shape
+    width = wq.shape[0]
+    units = wup.shape[1]
+    parts = 4
+    return pl.pallas_call(
+        mlp_kernel,
+        out_shape=(
+            jax.ShapeDtypeStruct((rows, wq.shape[1]), jnp.bfloat16),
+            jax.ShapeDtypeStruct((rows, width), jnp.float32),
+        ),
+        in_specs=[
+            whole(pl.ANY),
+            whole(pl.ANY),
+            whole(pltpu.VMEM),
+            whole(pl.ANY),
+            whole(pl.ANY),
+            whole(pl.ANY),
+        ],
+        out_specs=(whole(pltpu.VMEM), whole(pltpu.VMEM)),
+        scratch_shapes=[
+            pltpu.VMEM((rows, width), jnp.bfloat16),
+            pltpu.VMEM(wq.shape, jnp.bfloat16),
+            pltpu.VMEM((parts, width, units // parts), jnp.bfloat16),
+            pltpu.VMEM((units, width), jnp.bfloat16),
+            pltpu.SemaphoreType.DMA((3,)),
+            pltpu.SemaphoreType.DMA((3, parts)),
+        ],
+        compiler_params=pltpu.CompilerParams(vmem_limit_bytes=32 * MIB),
+        cost_estimate=pl.CostEstimate(
+            flops=2 * rows * width * (wq.shape[1] + 2 * units),
+            bytes_accessed=2 * width * (wq.shape[1] + 2 * units),
+            transcendentals=rows * units,
+        ),
+        name="mlp",
+    )(own, other, gain, wq, wup, wdn)
+
+
+def project_kernel(own, *refs):
+    pieces, (wk, wv, out, rows_s, w_s, p_sem, w_sem) = refs[:-7], refs[-7:]
+    width = wk.shape[1]
+    weights = [
+        pltpu.make_async_copy(wk, w_s.at[:, pl.ds(0, width)], w_sem.at[0]),
+        pltpu.make_async_copy(wv, w_s.at[:, pl.ds(width, width)], w_sem.at[1]),
+    ]
+    for copy in weights:
+        copy.start()
+    copies = [pltpu.make_async_copy(own, rows_s.at[pl.ds(0, 2 * BLOCK), :], p_sem.at[0])]
+    for i, piece in enumerate(pieces):
+        copies.append(
+            pltpu.make_async_copy(
+                piece, rows_s.at[pl.ds((2 + i) * BLOCK, BLOCK), :], p_sem.at[1 + i]
+            )
+        )
+    for copy in copies:
+        copy.start()
+    for copy in weights:
+        copy.wait()
+    for copy in copies:
+        copy.wait()
+    out[...] = dot(rows_s[...], w_s[...]).astype(jnp.bfloat16)
+
+
+def run_project(own, pieces, wk, wv):
+    rows = own.shape[0] + len(pieces) * BLOCK
+    width = wk.shape[1]
+    return pl.pallas_call(
+        project_kernel,
+        out_shape=jax.ShapeDtypeStruct((rows, 2 * width), jnp.bfloat16),
+        in_specs=[whole(pl.ANY)] * (3 + len(pieces)),
+        out_specs=whole(pltpu.VMEM),
+        scratch_shapes=[
+            pltpu.VMEM((rows, own.shape[1]), jnp.bfloat16),
+            pltpu.VMEM((wk.shape[0], 2 * width), jnp.bfloat16),
+            pltpu.SemaphoreType.DMA((1 + len(pieces),)),
+            pltpu.SemaphoreType.DMA((2,)),
+        ],
+        compiler_params=pltpu.CompilerParams(vmem_limit_bytes=24 * MIB),
+        cost_estimate=pl.CostEstimate(
+            flops=4 * rows * wk.shape[0] * width,
+            bytes_accessed=4 * wk.shape[0] * width + 4 * rows * wk.shape[0],
+            transcendentals=0,
+        ),
+        name="project",
+    )(own, *pieces, wk, wv)
+
+
+def attend_kernel(
+    shards, adjacency, q, kv_mine, kv_sibling, mlp, wo, send, keep, table, att_s, wo_s, t_sem, w_sem
+):
+    s = lax.axis_index("shard")
+    h = lax.axis_index("head")
+    u = lax.axis_index("sub")
+    half = wo.shape[0]
+    per_core = kv_mine.shape[0]
+    tables = [
+        pltpu.make_async_copy(kv_mine, table.at[pl.ds(0, per_core)], t_sem.at[0]),
+        pltpu.make_async_copy(kv_sibling, table.at[pl.ds(per_core, per_core)], t_sem.at[1]),
+    ]
+    for copy in tables:
+        copy.start()
+    weights = []
+    for part, head in enumerate((1 - h, h)):
+        columns = pl.ds(pl.multiple_of(head * half, half), half)
+        weights.append(
+            pltpu.make_async_copy(
+                wo.at[:, columns], wo_s.at[:, pl.ds(part * half, half)], w_sem.at[part]
+            )
+        )
+        weights[part].start()
+    rows_of = lax.broadcasted_iota(jnp.int32, (WIDE, WIDE), 0) // HEAD_DIM
+    lanes_of = lax.broadcasted_iota(jnp.int32, (WIDE, WIDE), 1) // HEAD_DIM
+    diagonal = rows_of == lanes_of
+    lane_head = lax.broadcasted_iota(jnp.int32, (BLOCK, WIDE), 1) // HEAD_DIM
+    scale = HEAD_DIM**-0.5 * math.log2(math.e)
+    for copy in tables:
+        copy.wait()
+    for b in range(adjacency.shape[0]):
+        places = []
+        for j in range(adjacency.shape[1]):
+            m = adjacency[b, j]
+            part = lax.rem(m, 2)
+            core = lax.rem(m // 2, 2)
+            distance = lax.rem(s - m // 4 + shards, shards)
+            part = jnp.where(distance == 0, part, part ^ h)
+            places.append((core ^ u) * per_core + distance * 2 + part)
+        for g in range(half // WIDE):
+            columns = slice(g * WIDE, (g + 1) * WIDE)
+            keys = jnp.concatenate([table[p, :, columns] for p in places], axis=0)
+            vcolumns = slice(half + g * WIDE, half + (g + 1) * WIDE)
+            values = jnp.concatenate([table[p, :, vcolumns] for p in places], axis=0)
+            q_rows = q[b * BLOCK : (b + 1) * BLOCK, columns]
+            stacked = jnp.concatenate([q_rows] * QUAD, axis=0)
+            stacked = jnp.where(diagonal, stacked, jnp.zeros_like(stacked))
+            scores = lax.dot_general(
+                stacked, keys, (((1,), (1,)), ((), ())), preferred_element_type=jnp.float32
+            )
+            highest = jnp.max(scores, axis=-1, keepdims=True)
+            weights_f = jnp.exp2((scores - highest) * scale)
+            total = jnp.sum(weights_f, axis=-1, keepdims=True)
+            probs = (weights_f * (1.0 / total)).astype(jnp.bfloat16)
+            mixed = dot(probs, values)
+            merged = mixed[0:BLOCK, :]
+            for i in range(1, QUAD):
+                merged = jnp.where(lane_head == i, mixed[i * BLOCK : (i + 1) * BLOCK, :], merged)
+            att_s[b * BLOCK : (b + 1) * BLOCK, columns] = merged.astype(jnp.bfloat16)
+    for copy in weights:
+        copy.wait()
+    branch = mlp[...] + dot(att_s[...], wo_s[...])
+    send[...] = branch[:, :half].astype(jnp.bfloat16)
+    keep[...] = branch[:, half:].astype(jnp.bfloat16)
+
+
+def run_attend(adjacency, q, kv_mine, kv_sibling, mlp, wo, shards):
+    rows, half = q.shape
+    nodes = 2 * kv_mine.shape[0] * BLOCK
+    part = jax.ShapeDtypeStruct((rows, half), jnp.bfloat16)
+    return pl.pallas_call(
+        functools.partial(attend_kernel, shards),
+        out_shape=(part, part),
+        in_specs=[
+            whole(pltpu.SMEM),
+            whole(pltpu.VMEM),
+            whole(pl.ANY),
+            whole(pl.ANY),
+            whole(pltpu.VMEM),
+            whole(pl.ANY),
+        ],
+        out_specs=(whole(pltpu.VMEM), whole(pltpu.VMEM)),
+        scratch_shapes=[
+            pltpu.VMEM((2 * kv_mine.shape[0],) + kv_mine.shape[1:], jnp.bfloat16),
+            pltpu.VMEM((rows, half), jnp.bfloat16),
+            pltpu.VMEM(wo.shape, jnp.bfloat16),
+            pltpu.SemaphoreType.DMA((2,)),
+            pltpu.SemaphoreType.DMA((2,)),
+        ],
+        compiler_params=pltpu.CompilerParams(vmem_limit_bytes=32 * MIB),
+        cost_estimate=pl.CostEstimate(
+            flops=2 * rows * half * (D + 8 * 8 * BLOCK),
+            bytes_accessed=4 * nodes * half + 2 * half * D + 4 * rows * D,
+            transcendentals=rows * 8 * BLOCK * half // HEAD_DIM,
+        ),
+        name="attend",
+    )(adjacency, q, kv_mine, kv_sibling, mlp, wo)
+
+
+def combine_kernel(owners, grid_features, keep, received, *outs):
+    s = lax.axis_index("shard")
+    shards = len(outs)
+    count = grid_features.shape[0]
+    half = keep.shape[1]
+    names = [owners[t, 0] for t in range(count)]
+    for d in range(shards):
+        target = lax.rem(s + d, shards)
+        for j in range(CAP):
+            outs[d][j] = jnp.zeros((BLOCK, half), jnp.bfloat16)
+        seen = jnp.int32(0)
+        for t in range(count):
+            hit = names[t] == target
+            rank = seen
+
+            @pl.when(hit)
+            def _():
+                rows = slice(t * BLOCK, (t + 1) * BLOCK)
+                partials = keep[rows, :].astype(jnp.float32) + received[rows, :].astype(jnp.float32)
+                updated = grid_features[t].astype(jnp.float32) + partials
+                outs[d][rank] = updated.astype(jnp.bfloat16)
+
+            seen = seen + hit.astype(jnp.int32)
+
+
+def run_combine(owners, grid_features, keep, received, shards):
+    count, rows, half = grid_features.shape
+    slot = jax.ShapeDtypeStruct((CAP, rows, half), jnp.bfloat16)
+    return pl.pallas_call(
+        combine_kernel,
+        out_shape=(slot,) * shards,
+        in_specs=[whole(pltpu.SMEM)] + [whole(pltpu.VMEM)] * 3,
+        out_specs=(whole(pltpu.VMEM),) * shards,
+        compiler_params=pltpu.CompilerParams(vmem_limit_bytes=16 * MIB),
+        cost_estimate=pl.CostEstimate(
+            flops=3 * count * rows * half,
+            bytes_accessed=2 * rows * half * (3 * count + CAP * shards),
+            transcendentals=0,
+        ),
+        name="combine",
+    )(owners, grid_features, keep, received)
+
+
+def place_kernel(*refs):
+    arrived, (out, sem) = refs[:-2], refs[-2:]
+    s = lax.axis_index("shard")
+    shards = len(arrived)
+    copies = []
+    for d in range(shards):
+        source = lax.rem(s - d + shards, shards)
+        copies.append(
+            pltpu.make_async_copy(arrived[d], out.at[pl.ds(source * CAP, CAP)], sem.at[d])
+        )
+        copies[d].start()
+    for copy in copies:
+        copy.wait()
+
+
+def run_place(arrived):
+    shards = len(arrived)
+    shape = arrived[0].shape
+    return pl.pallas_call(
+        place_kernel,
+        out_shape=jax.ShapeDtypeStruct((shards * CAP,) + shape[1:], jnp.bfloat16),
+        in_specs=[whole(pl.ANY)] * shards,
+        out_specs=whole(pl.ANY),
+        scratch_shapes=[pltpu.SemaphoreType.DMA((shards,))],
+        name="place",
+    )(*arrived)
+
+
+def shifted(x, distance, size):
+    return lax.ppermute(x, "shard", [(i, (i + distance) % size) for i in range(size)])
+
+
+def swapped(x, axis):
+    return lax.ppermute(x, axis, [(0, 1), (1, 0)])
+
+
+def paired(
+    grid_features,
+    owners,
+    adjacency,
+    mesh_nodes,
+    norm_gain,
+    query_weight,
+    key_weight,
+    value_weight,
+    output_weight,
+    up_weight,
+    down_weight,
+):
+    shards = lax.axis_size("shard")
+    count, rows, half = grid_features.shape
+    flat = grid_features.reshape(count * rows, half)
+    mesh_half = lax.dynamic_slice_in_dim(mesh_nodes, lax.axis_index("head") * BLOCK, BLOCK, 0)
+    other = swapped(flat, "head")
+    pieces = []
+    for d in range(1, shards):
+        piece = shifted(mesh_half, d, shards)
+        pieces += [piece, swapped(piece, "head")]
+    queries, mlp = run_mlp(
+        flat, other, norm_gain.reshape(1, -1), query_weight, up_weight, down_weight
+    )
+    kv_mine = run_project(mesh_nodes, pieces, key_weight, value_weight)
+    kv_sibling = swapped(kv_mine, "sub")
+    blocked = (2 * shards, BLOCK, 2 * half)
+    send, keep = run_attend(
+        adjacency,
+        queries,
+        kv_mine.reshape(blocked),
+        kv_sibling.reshape(blocked),
+        mlp,
+        output_weight,
+        shards,
+    )
+    received = swapped(send, "head")
+    slots = run_combine(owners, grid_features, keep, received, shards)
+    arrived = [slots[0]] + [shifted(slots[d], d, shards) for d in range(1, shards)]
+    return run_place(arrived)
+
+
+def attend_plain(queries, key_table, value_table, chosen, scaling):
     count = chosen.shape[0]
     picked_keys = key_table[chosen]
     picked_keys = picked_keys.reshape(count, -1, picked_keys.shape[3], picked_keys.shape[4])
@@ -32,7 +411,7 @@
     return result.astype(jnp.bfloat16)
 
 
-def local(
+def general(
     grid_features,
     owners,
     adjacency,
@@ -103,7 +482,7 @@
     queries = queries.reshape(steps_count, blocks_each, block_rows, head_local, HEAD_DIM)
 
     def attend_step(operands):
-        return attend(operands[0], key_table, value_table, operands[1], HEAD_DIM ** (-0.5))
+        return attend_plain(operands[0], key_table, value_table, operands[1], HEAD_DIM ** (-0.5))
 
     attended = lax.map(
         attend_step, (queries, jnp.maximum(lists, 0).reshape(steps_count, blocks_each, -1))
@@ -121,6 +500,14 @@
     occupied = lists[:, 0] >= 0
     summed = residual.astype(jnp.float32) + reduced
     return jnp.where(occupied[:, None, None], summed, 0.0).astype(jnp.bfloat16)
+
+
+def local(grid_features, owners, adjacency, mesh_nodes, *parameters):
+    pairs = lax.axis_size("head") == 2 and lax.axis_size("sub") == 2
+    small = grid_features.shape[0] <= 4 and mesh_nodes.shape[0] == 2 * BLOCK
+    if pairs and small and grid_features.shape[1] == BLOCK:
+        return paired(grid_features, owners, adjacency, mesh_nodes, *parameters)
+    return general(grid_features, owners, adjacency, mesh_nodes, *parameters)
 
 
 def solution(mesh):

time: 170 us -> 90.5 us (0.53)
  matrix products: 41 us -> 0 us
  Pallas kernels: 0 us -> 29.6 us
  waiting for transfers between devices: 57.2 us -> 32.9 us
  local copies, waits for them, and re-layouts: 28.2 us -> 9.28 us
  between operations: 13.5 us -> 0.12 us
  other arithmetic: 9.74 us -> 0 us
  blocking collectives: 8.44 us -> 0 us
  starting transfers between devices: 11.3 us -> 18.3 us
    dot_general x8 -> x0, matrix products: 41 us -> none  [the longest x1 16.7 us: local(): jnp.dot(hidden, down_weight, preferred_element_type=jnp.float32)]
    all_to_all x2 -> x0, waiting for transfers between devices: 36.2 us -> none  [the longest x1 36.1 us: local(): lax.all_to_all(outgoing.reshape(shard_count, CAP, block_rows, D), 'shard'...]
    ppermute x0 -> x12, waiting for transfers between devices: none -> 32.9 us  [the longest x6 19.5 us: swapped(): return lax.ppermute(x, axis, [(0, 1), (1, 0)])]
    pallas_call x0 -> x5, Pallas kernels: none -> 29.6 us  [the longest x1 17 us: run_place(): pl.pallas_call(place_kernel, out_shape=jax.ShapeDtypeStruct((shards * CAP...]
    reduce_scatter x1 -> x0, waiting for transfers between devices: 21.1 us -> none  [local(): lax.psum_scatter(branch.astype(jnp.bfloat16), 'head', scatter_dimension=2...]
    ppermute x0 -> x12, starting transfers between devices: none -> 18.3 us  [the longest x6 11.4 us: shifted(): lax.ppermute(x, 'shard', [(i, (i + distance) % size) for i in range(size)])]
    all_to_all x2 -> x0, starting transfers between devices: 11.3 us -> none  [the longest x1 6.32 us: local(): lax.all_to_all(send_lists, 'shard', split_axis=0, concat_axis=0, tiled=True)]
    gather x2 -> x0, local copies, waits for them, and re-layouts: 10.7 us -> none  [the longest x1 5.36 us: attend(): picked_keys = key_table[chosen]]
  transfers between devices with their start and end apart: 4 -> 12, of which waited for: 2 -> 8; matrix products, arithmetic and copies ran while one was open for 17% -> 0% of each run, Pallas kernels for 0% -> 6%
where the time goes in v1:
time: 90.5 us; the launch traced here: 90.2 us
  waiting for transfers between devices  32.9 us (36%)
  Pallas kernels  29.6 us (33%)
  starting transfers between devices  18.3 us (20%)
  local copies, waits for them, and re-layouts  9.28 us (10%)
    ppermute x6, waiting for transfers between devices, swapped(): return lax.ppermute(x, axis, [(0, 1), (1, 0)])  19.5 us
    pallas_call x1, Pallas kernels, run_place(): pl.pallas_call(place_kernel, out_shape=jax.ShapeDtypeStruct((shards * CAP...  17 us
    ppermute x6, waiting for transfers between devices, shifted(): lax.ppermute(x, 'shard', [(i, (i + distance) % size) for i in range(size)])  13.4 us
    ppermute x6, starting transfers between devices, shifted(): lax.ppermute(x, 'shard', [(i, (i + distance) % size) for i in range(size)])  11.4 us
    unnamed x31, local copies, waits for them, and re-layouts  8.22 us
    ppermute x6, starting transfers between devices, swapped(): return lax.ppermute(x, axis, [(0, 1), (1, 0)])  6.95 us
    pallas_call x1, Pallas kernels, run_mlp(): pl.pallas_call(mlp_kernel, out_shape=(jax.ShapeDtypeStruct((rows, wq.shap...  5.44 us
    pallas_call x1, Pallas kernels, run_attend(): pl.pallas_call(functools.partial(attend_kernel, shards), out_shape=(part,...  3.64 us
  transfers between devices with their start and end apart: 12, of which 8 were waited for; matrix products, arithmetic and copies ran while one was open for 0% of the time, Pallas kernels for 6%

profile of v1, /device:TPU:0, one launch (start us, length us, event | category | flops | bytes accessed | tf_op | source)
XLA Modules:
  0.0 90.2 jit_solution(15654213111469721485)
XLA Ops:
  0.0 0.0 copy-start.3
  0.0 0.0 copy-start
  0.0 1.1 %constant_dynamic-slice_fusion = bf16[64,1024]{1,0:T(8,128)(2,1)S(1)} fusion(bf16[128,1024]{1,0:T(8,128)(2,1)} %own.1, s32[]{:T(128)S(6)} %select_n.3), kind=kLoop, calls=%fused_computation | loop fusion | bytes 262148 | tf_op jit(solution)/shard_map/dynamic_slice | solution.py:368
  1.1 3.1 %collective-permute-start.1 = (bf16[64,1024]{1,0:T(8,128)(2,1)S(1)}, bf16[64,1024]{1,0:T(8,128)(2,1)S(1)}, u32[]{:S(2)}, u32[]{:S(2)}) collective-permute-start(bf16[64,1024]{1,0:T(8,128)(2,1)S(1)} %constant_dynamic-slice_fusion), channel_id=1, source_target_pairs={{0,4},{4,8},{8,12},{12,0},{1,5},{5,9},{9,13},{13,1},{2,6},{6,10},{... | collective-permute-start | bytes 393224 | tf_op jit(solution)/shard_map/ppermute | solution.py:345
  4.1 2.6 %collective-permute-start.3 = (bf16[64,1024]{1,0:T(8,128)(2,1)S(1)}, bf16[64,1024]{1,0:T(8,128)(2,1)S(1)}, u32[]{:S(2)}, u32[]{:S(2)}) collective-permute-start(bf16[64,1024]{1,0:T(8,128)(2,1)S(1)} %constant_dynamic-slice_fusion), channel_id=1, source_target_pairs={{0,8},{4,12},{8,0},{12,4},{1,9},{5,13},{9,1},{13,5},{2,10},{6,14},... | collective-permute-start | bytes 393224 | tf_op jit(solution)/shard_map/ppermute | solution.py:345
  6.7 1.3 %collective-permute-start.5 = (bf16[64,1024]{1,0:T(8,128)(2,1)S(1)}, bf16[64,1024]{1,0:T(8,128)(2,1)S(1)}, u32[]{:S(2)}, u32[]{:S(2)}) collective-permute-start(bf16[64,1024]{1,0:T(8,128)(2,1)S(1)} %constant_dynamic-slice_fusion), channel_id=1, source_target_pairs={{0,12},{4,0},{8,4},{12,8},{1,13},{5,1},{9,5},{13,9},{2,14},{6,2},{... | collective-permute-start | bytes 393224 | tf_op jit(solution)/shard_map/ppermute | solution.py:345
  8.1 2.5 %collective-permute-done.1.refs_0_ = bf16[64,1024]{1,0:T(8,128)(2,1)S(1)} collective-permute-done((bf16[64,1024]{1,0:T(8,128)(2,1)S(1)}, bf16[64,1024]{1,0:T(8,128)(2,1)S(1)}, u32[]{:S(2)}, u32[]{:S(2)}) %collective-permute-start.1) | collective-permute-done | bytes 131104 | tf_op jit(solution)/shard_map/ppermute | solution.py:345
  10.6 1.7 %collective-permute-start.2 = (bf16[64,1024]{1,0:T(8,128)(2,1)S(1)}, bf16[64,1024]{1,0:T(8,128)(2,1)S(1)}, u32[]{:S(2)}, u32[]{:S(2)}) collective-permute-start(bf16[64,1024]{1,0:T(8,128)(2,1)S(1)} %collective-permute-done.1.refs_0_), channel_id=1, source_target_pairs={{0,2},{2,0},{1,3},{3,1},{4,6},{6,4},{5,7},{7,5},{8,10},{10,8},{9,1... | collective-permute-start | bytes 393224 | tf_op jit(solution)/shard_map/ppermute | solution.py:349
  12.3 3.0 %collective-permute-done.3.refs_2_ = bf16[64,1024]{1,0:T(8,128)(2,1)S(1)} collective-permute-done((bf16[64,1024]{1,0:T(8,128)(2,1)S(1)}, bf16[64,1024]{1,0:T(8,128)(2,1)S(1)}, u32[]{:S(2)}, u32[]{:S(2)}) %collective-permute-start.3) | collective-permute-done | bytes 131104 | tf_op jit(solution)/shard_map/ppermute | solution.py:345
  15.4 1.5 %collective-permute-start.4 = (bf16[64,1024]{1,0:T(8,128)(2,1)S(1)}, bf16[64,1024]{1,0:T(8,128)(2,1)S(1)}, u32[]{:S(2)}, u32[]{:S(2)}) collective-permute-start(bf16[64,1024]{1,0:T(8,128)(2,1)S(1)} %collective-permute-done.3.refs_2_), channel_id=1, source_target_pairs={{0,2},{2,0},{1,3},{3,1},{4,6},{6,4},{5,7},{7,5},{8,10},{10,8},{9,1... | collective-permute-start | bytes 393224 | tf_op jit(solution)/shard_map/ppermute | solution.py:349
  16.9 0.0 collective-permute-done.5.refs_4_
  16.9 0.5 collective-permute-start.6
  17.4 0.0 collective-permute-done.2.refs_1_
  17.4 4.3 %collective-permute-done.4.refs_3_ = bf16[64,1024]{1,0:T(8,128)(2,1)S(1)} collective-permute-done((bf16[64,1024]{1,0:T(8,128)(2,1)S(1)}, bf16[64,1024]{1,0:T(8,128)(2,1)S(1)}, u32[]{:S(2)}, u32[]{:S(2)}) %collective-permute-start.4) | collective-permute-done | bytes 131104 | tf_op jit(solution)/shard_map/ppermute | solution.py:349
  21.8 1.8 %collective-permute-done.6.refs_5_ = bf16[64,1024]{1,0:T(8,128)(2,1)S(1)} collective-permute-done((bf16[64,1024]{1,0:T(8,128)(2,1)S(1)}, bf16[64,1024]{1,0:T(8,128)(2,1)S(1)}, u32[]{:S(2)}, u32[]{:S(2)}) %collective-permute-start.6) | collective-permute-done | bytes 131104 | tf_op jit(solution)/shard_map/ppermute | solution.py:349
  23.5 0.0 copy-start.4
  23.5 1.2 %copy-done.4 = bf16[1024,512]{1,0:T(8,128)(2,1)S(1)} copy-done((bf16[1024,512]{1,0:T(8,128)(2,1)S(1)}, bf16[1024,512]{1,0:T(8,128)(2,1)}, u32[]{:S(2)}) %copy-start.4) | copy-done | bytes 1048600
  24.7 0.0 copy-start.5
  24.7 1.2 %copy-done.5 = bf16[1024,512]{1,0:T(8,128)(2,1)S(1)} copy-done((bf16[1024,512]{1,0:T(8,128)(2,1)S(1)}, bf16[1024,512]{1,0:T(8,128)(2,1)}, u32[]{:S(2)}) %copy-start.5) | copy-done | bytes 1048600
  26.0 0.0 copy-start.6
  26.0 0.9 %copy-done.6 = bf16[128,1024]{1,0:T(8,128)(2,1)S(1)} copy-done((bf16[128,1024]{1,0:T(8,128)(2,1)S(1)}, bf16[128,1024]{1,0:T(8,128)(2,1)}, u32[]{:S(2)}) %copy-start.6) | copy-done | bytes 262168
  26.9 0.0 copy-start.8
  26.9 2.7 %project.1 = bf16[512,1024]{1,0:T(8,128)(2,1)S(1)} custom-call(bf16[128,1024]{1,0:T(8,128)(2,1)S(1)} %copy-done.6, bf16[64,1024]{1,0:T(8,128)(2,1)S(1)} %collective-permute-done.1.refs_0_, bf16[64,1024]{1,0:T(8,128)(2,1)S(1)} %collective-permute-done.2.refs_1_, bf16[64,1024]{1,0:T(8,128)(2,1)S(1)} %collective-permute-done.3.refs_2_, ...), custom_call_target="tpu_custom_call" | custom-call | flops 1073741824 | bytes 4194304 | tf_op jit(solution)/shard_map/project/pallas_call | solution.py:153
  29.6 0.1 collective-permute-start.7
  29.7 0.0 copy-done.3
  29.7 1.6 %collective-permute-start = (bf16[256,512]{1,0:T(8,128)(2,1)S(1)}, bf16[256,512]{1,0:T(8,128)(2,1)S(1)}, u32[]{:S(2)}, u32[]{:S(2)}) collective-permute-start(bf16[256,512]{1,0:T(8,128)(2,1)S(1)} %bitcast.4), channel_id=1, source_target_pairs={{0,2},{2,0},{1,3},{3,1},{4,6},{6,4},{5,7},{7,5},{8,10},{10,8},{9,1... | collective-permute-start | bytes 786440 | tf_op jit(solution)/shard_map/ppermute | solution.py:349
  31.3 7.2 %collective-permute-done.other = bf16[256,512]{1,0:T(8,128)(2,1)S(1)} collective-permute-done((bf16[256,512]{1,0:T(8,128)(2,1)S(1)}, bf16[256,512]{1,0:T(8,128)(2,1)S(1)}, u32[]{:S(2)}, u32[]{:S(2)}) %collective-permute-start) | collective-permute-done | bytes 262176 | tf_op jit(solution)/shard_map/ppermute | solution.py:349
  38.4 0.0 copy-done
  38.4 0.0 copy-done.8
  38.4 0.0 copy-start.1
  38.4 2.2 %copy-done.1 = bf16[2048,1024]{1,0:T(8,128)(2,1)S(1)} copy-done((bf16[2048,1024]{1,0:T(8,128)(2,1)S(1)}, bf16[2048,1024]{1,0:T(8,128)(2,1)}, u32[]{:S(2)}) %copy-start.1) | copy-done | bytes 4194328
  40.6 0.0 copy-start.2
  40.6 1.2 %copy-done.2 = bf16[1024,512]{1,0:T(8,128)(2,1)S(1)} copy-done((bf16[1024,512]{1,0:T(8,128)(2,1)S(1)}, bf16[1024,512]{1,0:T(8,128)(2,1)}, u32[]{:S(2)}) %copy-start.2) | copy-done | bytes 1048600
  41.8 0.0 copy-start.9
  41.9 0.0 copy-start.10
  41.9 5.4 %mlp.1 = (bf16[256,512]{1,0:T(8,128)(2,1)S(1)}, f32[256,1024]{1,0:T(8,128)S(1)}) custom-call(bf16[256,512]{1,0:T(8,128)(2,1)S(1)} %bitcast.5, bf16[256,512]{1,0:T(8,128)(2,1)S(1)} %collective-permute-done.other, f32[1,1024]{1,0:T(1,128)S(1)} %bitcast.7, bf16[1024,512]{1,0:T(8,128)(2,1)S(1)} %copy-done.2, bf16[1024,2048]{1,0:T(8,128)(2,1)S(1)} %copy-done, ...), custom_call_target="tpu_custom_call" | custom-call | flops 2415919104 | bytes 9437184 | tf_op jit(solution)/shard_map/mlp/pallas_call | solution.py:92
  47.3 0.0 copy-start.14
  47.3 0.0 collective-permute-done.7
  47.3 0.0 copy-done.9
  47.3 0.0 copy-done.10
  47.3 3.6 %attend.1 = (bf16[256,512]{1,0:T(8,128)(2,1)S(1)}, bf16[256,512]{1,0:T(8,128)(2,1)S(1)}) custom-call(s32[4,8]{1,0:T(4,128)S(1)} %copy-done.10, bf16[256,512]{1,0:T(8,128)(2,1)S(1)} %get-tuple-element.13.q, bf16[8,64,1024]{2,1,0:T(8,128)(2,1)S(1)} %bitcast.6, bf16[8,64,1024]{2,1,0:T(8,128)(2,1)S(1)} %bitcast.8, f32[256,1024]{1,0:T(8,128)S(1)} %get-tuple-element.14.mlp, ...), custom_call_target="tpu_custom_call" | custom-call | flops 1342177280 | bytes 4194304 | tf_op jit(solution)/shard_map/attend/pallas_call | solution.py:244
  51.0 1.6 %collective-permute-start.8 = (bf16[256,512]{1,0:T(8,128)(2,1)S(1)}, bf16[256,512]{1,0:T(8,128)(2,1)S(1)}, u32[]{:S(2)}, u32[]{:S(2)}) collective-permute-start(bf16[256,512]{1,0:T(8,128)(2,1)S(1)} %get-tuple-element.16), channel_id=1, source_target_pairs={{0,2},{2,0},{1,3},{3,1},{4,6},{6,4},{5,7},{7,5},{8,10},{10,8},{9,1... | collective-permute-start | bytes 786440 | tf_op jit(solution)/shard_map/ppermute | solution.py:349
  52.5 0.0 copy-done.14
  52.5 0.1 copy.12.owners
  52.6 6.3 %collective-permute-done.8.received = bf16[256,512]{1,0:T(8,128)(2,1)S(1)} collective-permute-done((bf16[256,512]{1,0:T(8,128)(2,1)S(1)}, bf16[256,512]{1,0:T(8,128)(2,1)S(1)}, u32[]{:S(2)}, u32[]{:S(2)}) %collective-permute-start.8) | collective-permute-done | bytes 262176 | tf_op jit(solution)/shard_map/ppermute | solution.py:349
  58.9 0.8 combine.1
  59.7 0.0 copy-start.7
  59.7 0.6 copy-done.7
  60.3 2.4 %collective-permute-start.10 = (bf16[2,64,512]{2,1,0:T(8,128)(2,1)S(1)}, bf16[2,64,512]{2,1,0:T(8,128)(2,1)S(1)}, u32[]{:S(2)}, u32[]{:S(2)}) collective-permute-start(bf16[2,64,512]{2,1,0:T(8,128)(2,1)S(1)} %get-tuple-element.19), channel_id=1, source_target_pairs={{0,8},{4,12},{8,0},{12,4},{1,9},{5,13},{9,1},{13,5},{2,10},{6,14},... | collective-permute-start | bytes 393224 | tf_op jit(solution)/shard_map/ppermute | solution.py:345
  62.7 2.0 %collective-permute-start.11 = (bf16[2,64,512]{2,1,0:T(8,128)(2,1)S(1)}, bf16[2,64,512]{2,1,0:T(8,128)(2,1)S(1)}, u32[]{:S(2)}, u32[]{:S(2)}) collective-permute-start(bf16[2,64,512]{2,1,0:T(8,128)(2,1)S(1)} %get-tuple-element.20), channel_id=1, source_target_pairs={{0,12},{4,0},{8,4},{12,8},{1,13},{5,1},{9,5},{13,9},{2,14},{6,2},{... | collective-permute-start | bytes 393224 | tf_op jit(solution)/shard_map/ppermute | solution.py:345
  64.7 0.0 collective-permute-start.9
  64.7 6.3 %collective-permute-done.10.refs_2_ = bf16[2,64,512]{2,1,0:T(8,128)(2,1)S(1)} collective-permute-done((bf16[2,64,512]{2,1,0:T(8,128)(2,1)S(1)}, bf16[2,64,512]{2,1,0:T(8,128)(2,1)S(1)}, u32[]{:S(2)}, u32[]{:S(2)}) %collective-permute-start.10) | collective-permute-done | bytes 131104 | tf_op jit(solution)/shard_map/ppermute | solution.py:345
  71.0 0.0 copy-start.11
  71.0 0.0 collective-permute-done.11.refs_3_
  71.0 0.0 copy-start.12
  71.0 1.6 %collective-permute-done.9.refs_1_ = bf16[2,64,512]{2,1,0:T(8,128)(2,1)S(1)} collective-permute-done((bf16[2,64,512]{2,1,0:T(8,128)(2,1)S(1)}, bf16[2,64,512]{2,1,0:T(8,128)(2,1)S(1)}, u32[]{:S(2)}, u32[]{:S(2)}) %collective-permute-start.9) | collective-permute-done | bytes 131104 | tf_op jit(solution)/shard_map/ppermute | solution.py:345
  72.6 0.0 copy-start.13
  72.6 0.0 copy-done.11
  72.6 0.0 copy-done.12
  72.6 0.6 copy-done.13
  73.2 17.0 %place.1 = bf16[8,64,512]{2,1,0:T(8,128)(2,1)} custom-call(bf16[2,64,512]{2,1,0:T(8,128)(2,1)} %copy-done.7, bf16[2,64,512]{2,1,0:T(8,128)(2,1)} %copy-done.13, bf16[2,64,512]{2,1,0:T(8,128)(2,1)} %copy-done.11, bf16[2,64,512]{2,1,0:T(8,128)(2,1)} %copy-done.12), custom_call_target="tpu_custom_call" | custom-call | tf_op jit(solution)/shard_map/place/pallas_call | solution.py:334
Async XLA Ops:
  0.0 29.7 %copy-start.3 = (bf16[4,64,512]{2,1,0:T(8,128)(2,1)S(1)}, bf16[4,64,512]{2,1,0:T(8,128)(2,1)}, u32[]{:S(2)}) copy-start(bf16[4,64,512]{2,1,0:T(8,128)(2,1)} %grid_features.1) | copy-start | bytes 786436
  0.0 38.4 %copy-start = (bf16[1024,2048]{1,0:T(8,128)(2,1)S(1)}, bf16[1024,2048]{1,0:T(8,128)(2,1)}, u32[]{:S(2)}) copy-start(bf16[1024,2048]{1,0:T(8,128)(2,1)} %wup.1) | copy-start | bytes 12582916
  1.1 9.5 %collective-permute-start.1 = (bf16[64,1024]{1,0:T(8,128)(2,1)S(1)}, bf16[64,1024]{1,0:T(8,128)(2,1)S(1)}, u32[]{:S(2)}, u32[]{:S(2)}) collective-permute-start(bf16[64,1024]{1,0:T(8,128)(2,1)S(1)} %constant_dynamic-slice_fusion), channel_id=1, source_target_pairs={{0,4},{4,8},{8,12},{12,0},{1,5},{5,9},{9,13},{13,1},{2,6},{6,10},{... | collective-permute-start | bytes 393224 | tf_op jit(solution)/shard_map/ppermute | solution.py:345
  4.1 11.2 %collective-permute-start.3 = (bf16[64,1024]{1,0:T(8,128)(2,1)S(1)}, bf16[64,1024]{1,0:T(8,128)(2,1)S(1)}, u32[]{:S(2)}, u32[]{:S(2)}) collective-permute-start(bf16[64,1024]{1,0:T(8,128)(2,1)S(1)} %constant_dynamic-slice_fusion), channel_id=1, source_target_pairs={{0,8},{4,12},{8,0},{12,4},{1,9},{5,13},{9,1},{13,5},{2,10},{6,14},... | collective-permute-start | bytes 393224 | tf_op jit(solution)/shard_map/ppermute | solution.py:345
  6.7 10.1 %collective-permute-start.5 = (bf16[64,1024]{1,0:T(8,128)(2,1)S(1)}, bf16[64,1024]{1,0:T(8,128)(2,1)S(1)}, u32[]{:S(2)}, u32[]{:S(2)}) collective-permute-start(bf16[64,1024]{1,0:T(8,128)(2,1)S(1)} %constant_dynamic-slice_fusion), channel_id=1, source_target_pairs={{0,12},{4,0},{8,4},{12,8},{1,13},{5,1},{9,5},{13,9},{2,14},{6,2},{... | collective-permute-start | bytes 393224 | tf_op jit(solution)/shard_map/ppermute | solution.py:345
  10.6 6.8 %collective-permute-start.2 = (bf16[64,1024]{1,0:T(8,128)(2,1)S(1)}, bf16[64,1024]{1,0:T(8,128)(2,1)S(1)}, u32[]{:S(2)}, u32[]{:S(2)}) collective-permute-start(bf16[64,1024]{1,0:T(8,128)(2,1)S(1)} %collective-permute-done.1.refs_0_), channel_id=1, source_target_pairs={{0,2},{2,0},{1,3},{3,1},{4,6},{6,4},{5,7},{7,5},{8,10},{10,8},{9,1... | collective-permute-start | bytes 393224 | tf_op jit(solution)/shard_map/ppermute | solution.py:349
  15.4 6.4 %collective-permute-start.4 = (bf16[64,1024]{1,0:T(8,128)(2,1)S(1)}, bf16[64,1024]{1,0:T(8,128)(2,1)S(1)}, u32[]{:S(2)}, u32[]{:S(2)}) collective-permute-start(bf16[64,1024]{1,0:T(8,128)(2,1)S(1)} %collective-permute-done.3.refs_2_), channel_id=1, source_target_pairs={{0,2},{2,0},{1,3},{3,1},{4,6},{6,4},{5,7},{7,5},{8,10},{10,8},{9,1... | collective-permute-start | bytes 393224 | tf_op jit(solution)/shard_map/ppermute | solution.py:349
  16.9 6.6 %collective-permute-start.6 = (bf16[64,1024]{1,0:T(8,128)(2,1)S(1)}, bf16[64,1024]{1,0:T(8,128)(2,1)S(1)}, u32[]{:S(2)}, u32[]{:S(2)}) collective-permute-start(bf16[64,1024]{1,0:T(8,128)(2,1)S(1)} %collective-permute-done.5.refs_4_), channel_id=1, source_target_pairs={{0,2},{2,0},{1,3},{3,1},{4,6},{6,4},{5,7},{7,5},{8,10},{10,8},{9,1... | collective-permute-start | bytes 393224 | tf_op jit(solution)/shard_map/ppermute | solution.py:349
  23.5 1.2 %copy-start.4 = (bf16[1024,512]{1,0:T(8,128)(2,1)S(1)}, bf16[1024,512]{1,0:T(8,128)(2,1)}, u32[]{:S(2)}) copy-start(bf16[1024,512]{1,0:T(8,128)(2,1)} %refs_6_.1) | copy-start | bytes 3145732
  24.7 1.2 %copy-start.5 = (bf16[1024,512]{1,0:T(8,128)(2,1)S(1)}, bf16[1024,512]{1,0:T(8,128)(2,1)}, u32[]{:S(2)}) copy-start(bf16[1024,512]{1,0:T(8,128)(2,1)} %refs_7_.1) | copy-start | bytes 3145732
  26.0 0.9 %copy-start.6 = (bf16[128,1024]{1,0:T(8,128)(2,1)S(1)}, bf16[128,1024]{1,0:T(8,128)(2,1)}, u32[]{:S(2)}) copy-start(bf16[128,1024]{1,0:T(8,128)(2,1)} %own.1) | copy-start | bytes 786436
  26.9 11.5 %copy-start.8 = (f32[1024]{0:T(1024)S(1)}, f32[1024]{0:T(1024)}, u32[]{:S(2)}) copy-start(f32[1024]{0:T(1024)} %param.15) | copy-start | bytes 12292
  29.6 17.7 %collective-permute-start.7 = (bf16[512,1024]{1,0:T(8,128)(2,1)S(1)}, bf16[512,1024]{1,0:T(8,128)(2,1)S(1)}, u32[]{:S(2)}, u32[]{:S(2)}) collective-permute-start(bf16[512,1024]{1,0:T(8,128)(2,1)S(1)} %project.1), channel_id=1, source_target_pairs={{0,1},{1,0},{2,3},{3,2},{4,5},{5,4},{6,7},{7,6},{8,9},{9,8},{10,11... | collective-permute-start | bytes 3145736 | tf_op jit(solution)/shard_map/ppermute | solution.py:349
  29.7 8.7 %collective-permute-start = (bf16[256,512]{1,0:T(8,128)(2,1)S(1)}, bf16[256,512]{1,0:T(8,128)(2,1)S(1)}, u32[]{:S(2)}, u32[]{:S(2)}) collective-permute-start(bf16[256,512]{1,0:T(8,128)(2,1)S(1)} %bitcast.4), channel_id=1, source_target_pairs={{0,2},{2,0},{1,3},{3,1},{4,6},{6,4},{5,7},{7,5},{8,10},{10,8},{9,1... | collective-permute-start | bytes 786440 | tf_op jit(solution)/shard_map/ppermute | solution.py:349
  38.4 2.2 %copy-start.1 = (bf16[2048,1024]{1,0:T(8,128)(2,1)S(1)}, bf16[2048,1024]{1,0:T(8,128)(2,1)}, u32[]{:S(2)}) copy-start(bf16[2048,1024]{1,0:T(8,128)(2,1)} %wdn.1) | copy-start | bytes 12582916
  40.6 1.2 %copy-start.2 = (bf16[1024,512]{1,0:T(8,128)(2,1)S(1)}, bf16[1024,512]{1,0:T(8,128)(2,1)}, u32[]{:S(2)}) copy-start(bf16[1024,512]{1,0:T(8,128)(2,1)} %wq.1) | copy-start | bytes 3145732
  41.8 5.5 %copy-start.9 = (bf16[512,1024]{1,0:T(8,128)(2,1)S(1)}, bf16[512,1024]{1,0:T(8,128)(2,1)}, u32[]{:S(2)}) copy-start(bf16[512,1024]{1,0:T(8,128)(2,1)} %wo.1) | copy-start | bytes 3145732
  41.9 5.5 %copy-start.10 = (s32[4,8]{1,0:T(4,128)S(1)}, s32[4,8]{1,0:T(4,128)}, u32[]{:S(2)}) copy-start(s32[4,8]{1,0:T(4,128)} %adjacency.1) | copy-start | bytes 388
  47.3 5.3 %copy-start.14 = (s32[4,1]{0,1:T(1,128)S(1)}, s32[4,1]{0,1:T(1,128)}, u32[]{:S(2)}) copy-start(s32[4,1]{0,1:T(1,128)} %param.12) | copy-start | bytes 52
  51.0 7.9 %collective-permute-start.8 = (bf16[256,512]{1,0:T(8,128)(2,1)S(1)}, bf16[256,512]{1,0:T(8,128)(2,1)S(1)}, u32[]{:S(2)}, u32[]{:S(2)}) collective-permute-start(bf16[256,512]{1,0:T(8,128)(2,1)S(1)} %get-tuple-element.16), channel_id=1, source_target_pairs={{0,2},{2,0},{1,3},{3,1},{4,6},{6,4},{5,7},{7,5},{8,10},{10,8},{9,1... | collective-permute-start | bytes 786440 | tf_op jit(solution)/shard_map/ppermute | solution.py:349
  59.7 0.7 copy-start.7
  60.3 10.7 %collective-permute-start.10 = (bf16[2,64,512]{2,1,0:T(8,128)(2,1)S(1)}, bf16[2,64,512]{2,1,0:T(8,128)(2,1)S(1)}, u32[]{:S(2)}, u32[]{:S(2)}) collective-permute-start(bf16[2,64,512]{2,1,0:T(8,128)(2,1)S(1)} %get-tuple-element.19), channel_id=1, source_target_pairs={{0,8},{4,12},{8,0},{12,4},{1,9},{5,13},{9,1},{13,5},{2,10},{6,14},... | collective-permute-start | bytes 393224 | tf_op jit(solution)/shard_map/ppermute | solution.py:345
  62.7 8.3 %collective-permute-start.11 = (bf16[2,64,512]{2,1,0:T(8,128)(2,1)S(1)}, bf16[2,64,512]{2,1,0:T(8,128)(2,1)S(1)}, u32[]{:S(2)}, u32[]{:S(2)}) collective-permute-start(bf16[2,64,512]{2,1,0:T(8,128)(2,1)S(1)} %get-tuple-element.20), channel_id=1, source_target_pairs={{0,12},{4,0},{8,4},{12,8},{1,13},{5,1},{9,5},{13,9},{2,14},{6,2},{... | collective-permute-start | bytes 393224 | tf_op jit(solution)/shard_map/ppermute | solution.py:345
  64.7 7.9 %collective-permute-start.9 = (bf16[2,64,512]{2,1,0:T(8,128)(2,1)S(1)}, bf16[2,64,512]{2,1,0:T(8,128)(2,1)S(1)}, u32[]{:S(2)}, u32[]{:S(2)}) collective-permute-start(bf16[2,64,512]{2,1,0:T(8,128)(2,1)S(1)} %get-tuple-element.18), channel_id=1, source_target_pairs={{0,4},{4,8},{8,12},{12,0},{1,5},{5,9},{9,13},{13,1},{2,6},{6,10},{... | collective-permute-start | bytes 393224 | tf_op jit(solution)/shard_map/ppermute | solution.py:345
  71.0 1.6 %copy-start.11 = (bf16[2,64,512]{2,1,0:T(8,128)(2,1)}, bf16[2,64,512]{2,1,0:T(8,128)(2,1)S(1)}, u32[]{:S(2)}) copy-start(bf16[2,64,512]{2,1,0:T(8,128)(2,1)S(1)} %collective-permute-done.10.refs_2_) | copy-start | bytes 393220
  71.0 1.6 %copy-start.12 = (bf16[2,64,512]{2,1,0:T(8,128)(2,1)}, bf16[2,64,512]{2,1,0:T(8,128)(2,1)S(1)}, u32[]{:S(2)}) copy-start(bf16[2,64,512]{2,1,0:T(8,128)(2,1)S(1)} %collective-permute-done.11.refs_3_) | copy-start | bytes 393220
  72.6 0.6 copy-start.13

commit v2 on v1

--- a/solution.py
+++ b/solution.py
@@ -1,4 +1,3 @@
-import functools
 import math
 
 import jax
@@ -28,12 +27,16 @@
     return 0.5 * x * (1.0 + lax.erf(x * (2.0**-0.5)))
 
 
+def in_hbm(x):
+    return pltpu.with_memory_space_constraint(x, pltpu.HBM)
+
+
 def whole(space):
     return pl.BlockSpec(memory_space=space)
 
 
 def mlp_kernel(
-    own, other, gain, wq, wup, wdn, q_out, mlp_out, x_s, wq_s, wup_s, wdn_s, x_sem, w_sem
+    own, other, gain, wq, wup, wdn, q_out, mlp_out, x_s, gain_s, wq_s, wup_s, wdn_s, x_sem, w_sem
 ):
     h = lax.axis_index("head")
     half = own.shape[1]
@@ -45,6 +48,7 @@
         pltpu.make_async_copy(own, x_s.at[:, mine], x_sem.at[0]),
         pltpu.make_async_copy(other, x_s.at[:, theirs], x_sem.at[1]),
         pltpu.make_async_copy(wq, wq_s, x_sem.at[2]),
+        pltpu.make_async_copy(gain, gain_s, x_sem.at[3]),
     ]
     for copy in copies:
         copy.start()
@@ -66,10 +70,11 @@
         downs.append(pair)
     copies[0].wait()
     copies[1].wait()
+    copies[3].wait()
     x = x_s[...].astype(jnp.float32)
     centered = x - jnp.mean(x, axis=-1, keepdims=True)
     variance = jnp.mean(centered * centered, axis=-1, keepdims=True)
-    normed = (centered * lax.rsqrt(variance + epsilon) * gain[...]).astype(jnp.bfloat16)
+    normed = (centered * lax.rsqrt(variance + epsilon) * gain_s[...]).astype(jnp.bfloat16)
     copies[2].wait()
     q_out[...] = dot(normed, wq_s[...]).astype(jnp.bfloat16)
     for c in range(wup_s.shape[0]):
@@ -96,30 +101,31 @@
             jax.ShapeDtypeStruct((rows, width), jnp.float32),
         ),
         in_specs=[
+            whole(pltpu.HBM),
             whole(pl.ANY),
-            whole(pl.ANY),
-            whole(pltpu.VMEM),
-            whole(pl.ANY),
-            whole(pl.ANY),
-            whole(pl.ANY),
+            whole(pltpu.HBM),
+            whole(pltpu.HBM),
+            whole(pltpu.HBM),
+            whole(pltpu.HBM),
         ],
         out_specs=(whole(pltpu.VMEM), whole(pltpu.VMEM)),
         scratch_shapes=[
             pltpu.VMEM((rows, width), jnp.bfloat16),
+            pltpu.VMEM(gain.shape, jnp.float32),
             pltpu.VMEM(wq.shape, jnp.bfloat16),
             pltpu.VMEM((parts, width, units // parts), jnp.bfloat16),
             pltpu.VMEM((units, width), jnp.bfloat16),
-            pltpu.SemaphoreType.DMA((3,)),
+            pltpu.SemaphoreType.DMA((4,)),
             pltpu.SemaphoreType.DMA((3, parts)),
         ],
-        compiler_params=pltpu.CompilerParams(vmem_limit_bytes=32 * MIB),
+        compiler_params=pltpu.CompilerParams(vmem_limit_bytes=16 * MIB),
         cost_estimate=pl.CostEstimate(
             flops=2 * rows * width * (wq.shape[1] + 2 * units),
             bytes_accessed=2 * width * (wq.shape[1] + 2 * units),
             transcendentals=rows * units,
         ),
         name="mlp",
-    )(own, other, gain, wq, wup, wdn)
+    )(in_hbm(own), other, in_hbm(gain), in_hbm(wq), in_hbm(wup), in_hbm(wdn))
 
 
 def project_kernel(own, *refs):
@@ -131,15 +137,15 @@
     ]
     for copy in weights:
         copy.start()
-    copies = [pltpu.make_async_copy(own, rows_s.at[pl.ds(0, 2 * BLOCK), :], p_sem.at[0])]
-    for i, piece in enumerate(pieces):
+    copies = []
+    first = 0
+    for i, piece in enumerate((own, *pieces)):
+        rows = piece.shape[0]
         copies.append(
-            pltpu.make_async_copy(
-                piece, rows_s.at[pl.ds((2 + i) * BLOCK, BLOCK), :], p_sem.at[1 + i]
-            )
+            pltpu.make_async_copy(piece, rows_s.at[pl.ds(first, rows), :], p_sem.at[i])
         )
-    for copy in copies:
-        copy.start()
+        copies[i].start()
+        first += rows
     for copy in weights:
         copy.wait()
     for copy in copies:
@@ -148,12 +154,14 @@
 
 
 def run_project(own, pieces, wk, wv):
-    rows = own.shape[0] + len(pieces) * BLOCK
+    rows = own.shape[0] + sum(piece.shape[0] for piece in pieces)
     width = wk.shape[1]
     return pl.pallas_call(
         project_kernel,
         out_shape=jax.ShapeDtypeStruct((rows, 2 * width), jnp.bfloat16),
-        in_specs=[whole(pl.ANY)] * (3 + len(pieces)),
+        in_specs=[whole(pltpu.HBM)]
+        + [whole(pl.ANY)] * len(pieces)
+        + [whole(pltpu.HBM)] * 2,
         out_specs=whole(pltpu.VMEM),
         scratch_shapes=[
             pltpu.VMEM((rows, own.shape[1]), jnp.bfloat16),
@@ -161,18 +169,18 @@
             pltpu.SemaphoreType.DMA((1 + len(pieces),)),
             pltpu.SemaphoreType.DMA((2,)),
         ],
-        compiler_params=pltpu.CompilerParams(vmem_limit_bytes=24 * MIB),
+        compiler_params=pltpu.CompilerParams(vmem_limit_bytes=12 * MIB),
         cost_estimate=pl.CostEstimate(
             flops=4 * rows * wk.shape[0] * width,
             bytes_accessed=4 * wk.shape[0] * width + 4 * rows * wk.shape[0],
             transcendentals=0,
         ),
         name="project",
-    )(own, *pieces, wk, wv)
+    )(in_hbm(own), *pieces, in_hbm(wk), in_hbm(wv))
 
 
 def attend_kernel(
-    shards, adjacency, q, kv_mine, kv_sibling, mlp, wo, send, keep, table, att_s, wo_s, t_sem, w_sem
+    adjacency, q, kv_mine, kv_sibling, mlp, wo, send, keep, table, att_s, wo_s, t_sem, w_sem
 ):
     s = lax.axis_index("shard")
     h = lax.axis_index("head")
@@ -207,8 +215,8 @@
             m = adjacency[b, j]
             part = lax.rem(m, 2)
             core = lax.rem(m // 2, 2)
-            distance = lax.rem(s - m // 4 + shards, shards)
-            part = jnp.where(distance == 0, part, part ^ h)
+            distance = s ^ (m // 4)
+            part = jnp.where(distance <= 1, part, part ^ h)
             places.append((core ^ u) * per_core + distance * 2 + part)
         for g in range(half // WIDE):
             columns = slice(g * WIDE, (g + 1) * WIDE)
@@ -237,12 +245,12 @@
     keep[...] = branch[:, half:].astype(jnp.bfloat16)
 
 
-def run_attend(adjacency, q, kv_mine, kv_sibling, mlp, wo, shards):
+def run_attend(adjacency, q, kv_mine, kv_sibling, mlp, wo):
     rows, half = q.shape
     nodes = 2 * kv_mine.shape[0] * BLOCK
     part = jax.ShapeDtypeStruct((rows, half), jnp.bfloat16)
     return pl.pallas_call(
-        functools.partial(attend_kernel, shards),
+        attend_kernel,
         out_shape=(part, part),
         in_specs=[
             whole(pltpu.SMEM),
@@ -250,7 +258,7 @@
             whole(pl.ANY),
             whole(pl.ANY),
             whole(pltpu.VMEM),
-            whole(pl.ANY),
+            whole(pltpu.HBM),
         ],
         out_specs=(whole(pltpu.VMEM), whole(pltpu.VMEM)),
         scratch_shapes=[
@@ -260,14 +268,14 @@
             pltpu.SemaphoreType.DMA((2,)),
             pltpu.SemaphoreType.DMA((2,)),
         ],
-        compiler_params=pltpu.CompilerParams(vmem_limit_bytes=32 * MIB),
+        compiler_params=pltpu.CompilerParams(vmem_limit_bytes=16 * MIB),
         cost_estimate=pl.CostEstimate(
             flops=2 * rows * half * (D + 8 * 8 * BLOCK),
             bytes_accessed=4 * nodes * half + 2 * half * D + 4 * rows * D,
             transcendentals=rows * 8 * BLOCK * half // HEAD_DIM,
         ),
         name="attend",
-    )(adjacency, q, kv_mine, kv_sibling, mlp, wo)
+    )(adjacency, q, kv_mine, kv_sibling, mlp, in_hbm(wo))
 
 
 def combine_kernel(owners, grid_features, keep, received, *outs):
@@ -277,7 +285,7 @@
     half = keep.shape[1]
     names = [owners[t, 0] for t in range(count)]
     for d in range(shards):
-        target = lax.rem(s + d, shards)
+        target = s ^ d
         for j in range(CAP):
             outs[d][j] = jnp.zeros((BLOCK, half), jnp.bfloat16)
         seen = jnp.int32(0)
@@ -303,7 +311,7 @@
         out_shape=(slot,) * shards,
         in_specs=[whole(pltpu.SMEM)] + [whole(pltpu.VMEM)] * 3,
         out_specs=(whole(pltpu.VMEM),) * shards,
-        compiler_params=pltpu.CompilerParams(vmem_limit_bytes=16 * MIB),
+        compiler_params=pltpu.CompilerParams(vmem_limit_bytes=8 * MIB),
         cost_estimate=pl.CostEstimate(
             flops=3 * count * rows * half,
             bytes_accessed=2 * rows * half * (3 * count + CAP * shards),
@@ -319,7 +327,7 @@
     shards = len(arrived)
     copies = []
     for d in range(shards):
-        source = lax.rem(s - d + shards, shards)
+        source = s ^ d
         copies.append(
             pltpu.make_async_copy(arrived[d], out.at[pl.ds(source * CAP, CAP)], sem.at[d])
         )
@@ -334,15 +342,16 @@
     return pl.pallas_call(
         place_kernel,
         out_shape=jax.ShapeDtypeStruct((shards * CAP,) + shape[1:], jnp.bfloat16),
-        in_specs=[whole(pl.ANY)] * shards,
-        out_specs=whole(pl.ANY),
+        in_specs=[whole(pltpu.VMEM)] * shards,
+        out_specs=whole(pltpu.HBM),
         scratch_shapes=[pltpu.SemaphoreType.DMA((shards,))],
+        compiler_params=pltpu.CompilerParams(vmem_limit_bytes=4 * MIB),
         name="place",
     )(*arrived)
 
 
-def shifted(x, distance, size):
-    return lax.ppermute(x, "shard", [(i, (i + distance) % size) for i in range(size)])
+def crossed(x, distance, size):
+    return lax.ppermute(x, "shard", [(i, i ^ distance) for i in range(size)])
 
 
 def swapped(x, axis):
@@ -365,15 +374,16 @@
     shards = lax.axis_size("shard")
     count, rows, half = grid_features.shape
     flat = grid_features.reshape(count * rows, half)
+    other = swapped(flat, "head")
     mesh_half = lax.dynamic_slice_in_dim(mesh_nodes, lax.axis_index("head") * BLOCK, BLOCK, 0)
-    other = swapped(flat, "head")
-    pieces = []
-    for d in range(1, shards):
-        piece = shifted(mesh_half, d, shards)
+    pieces = [crossed(mesh_nodes, 1, shards)]
+    for d in range(2, shards):
+        piece = crossed(mesh_half, d, shards)
         pieces += [piece, swapped(piece, "head")]
     queries, mlp = run_mlp(
         flat, other, norm_gain.reshape(1, -1), query_weight, up_weight, down_weight
     )
+    queries, mlp, *pieces = lax.optimization_barrier((queries, mlp, *pieces))
     kv_mine = run_project(mesh_nodes, pieces, key_weight, value_weight)
     kv_sibling = swapped(kv_mine, "sub")
     blocked = (2 * shards, BLOCK, 2 * half)
@@ -384,11 +394,10 @@
         kv_sibling.reshape(blocked),
         mlp,
         output_weight,
-        shards,
     )
     received = swapped(send, "head")
     slots = run_combine(owners, grid_features, keep, received, shards)
-    arrived = [slots[0]] + [shifted(slots[d], d, shards) for d in range(1, shards)]
+    arrived = [slots[0]] + [crossed(slots[d], d, shards) for d in range(1, shards)]
     return run_place(arrived)
 
 
@@ -504,6 +513,7 @@
 
 def local(grid_features, owners, adjacency, mesh_nodes, *parameters):
     pairs = lax.axis_size("head") == 2 and lax.axis_size("sub") == 2
+    pairs = pairs and lax.axis_size("shard") in (2, 4, 8)
     small = grid_features.shape[0] <= 4 and mesh_nodes.shape[0] == 2 * BLOCK
     if pairs and small and grid_features.shape[1] == BLOCK:
         return paired(grid_features, owners, adjacency, mesh_nodes, *parameters)

time: 90.5 us -> 59.9 us (0.66)
  Pallas kernels: 29.6 us -> 15.7 us
  local copies, waits for them, and re-layouts: 9.28 us -> 1.02 us
  waiting for transfers between devices: 32.9 us -> 28.7 us
  starting transfers between devices: 18.3 us -> 14.2 us
    pallas_call x1, Pallas kernels: 17 us -> 0.82 us  [run_place(): pl.pallas_call(place_kernel, out_shape=jax.ShapeDtypeStruct((shards * CAP...]
    ppermute x6 -> x5, waiting for transfers between devices: 19.5 us -> 10.4 us  [swapped(): return lax.ppermute(x, axis, [(0, 1), (1, 0)])]
    unnamed x31 -> x7, local copies, waits for them, and re-layouts: 8.22 us -> 0.11 us
    ppermute x6, waiting for transfers between devices: 13.4 us -> 18.3 us  [crossed(): return lax.ppermute(x, 'shard', [(i, i ^ distance) for i in range(size)])]
    ppermute x6, starting transfers between devices: 11.4 us -> 8.69 us  [crossed(): return lax.ppermute(x, 'shard', [(i, i ^ distance) for i in range(size)])]
    pallas_call x1, Pallas kernels: 5.44 us -> 7.64 us  [run_mlp(): pl.pallas_call(mlp_kernel, out_shape=(jax.ShapeDtypeStruct((rows, wq.shap...]
    ppermute x6 -> x5, starting transfers between devices: 6.95 us -> 5.56 us  [swapped(): return lax.ppermute(x, axis, [(0, 1), (1, 0)])]
  transfers between devices with their start and end apart: 12 -> 11, of which waited for: 8 -> 6; matrix products, arithmetic and copies ran while one was open for 0% -> 2% of each run, Pallas kernels for 6% -> 13%
where the time goes in v2:
time: 59.9 us; the launch traced here: 59.7 us
  waiting for transfers between devices  28.7 us (48%)
  Pallas kernels  15.7 us (26%)
  starting transfers between devices  14.2 us (24%)
  local copies, waits for them, and re-layouts  1.02 us (2%)
    ppermute x6, waiting for transfers between devices, crossed(): return lax.ppermute(x, 'shard', [(i, i ^ distance) for i in range(size)])  18.3 us
    ppermute x5, waiting for transfers between devices, swapped(): return lax.ppermute(x, axis, [(0, 1), (1, 0)])  10.4 us
    ppermute x6, starting transfers between devices, crossed(): return lax.ppermute(x, 'shard', [(i, i ^ distance) for i in range(size)])  8.69 us
    pallas_call x1, Pallas kernels, run_mlp(): pl.pallas_call(mlp_kernel, out_shape=(jax.ShapeDtypeStruct((rows, wq.shap...  7.64 us
    ppermute x5, starting transfers between devices, swapped(): return lax.ppermute(x, axis, [(0, 1), (1, 0)])  5.56 us
    pallas_call x1, Pallas kernels, run_attend(): pl.pallas_call(attend_kernel, out_shape=(part, part), in_specs=[whole(plt...  3.48 us
    pallas_call x1, Pallas kernels, run_project(): pl.pallas_call(project_kernel, out_shape=jax.ShapeDtypeStruct((rows, 2 *...  2.96 us
  transfers between devices with their start and end apart: 11, of which 6 were waited for; matrix products, arithmetic and copies ran while one was open for 2% of the time, Pallas kernels for 13%

profile of v2, /device:TPU:0, one launch (start us, length us, event | category | flops | bytes accessed | tf_op | source)
XLA Modules:
  0.0 59.7 jit_solution(10332949727627616801)
XLA Ops:
  0.0 2.9 %collective-permute-start = (bf16[256,512]{1,0:T(8,128)(2,1)}, bf16[256,512]{1,0:T(8,128)(2,1)S(1)}, u32[]{:S(2)}, u32[]{:S(2)}) collective-permute-start(bf16[256,512]{1,0:T(8,128)(2,1)} %bitcast.4), channel_id=1, source_target_pairs={{0,2},{2,0},{1,3},{3,1},{4,6},{6,4},{5,7},{7,5},{8,10},{10,8},{9,1... | collective-permute-start | bytes 786440 | tf_op jit(solution)/shard_map/ppermute | solution.py:358
  2.9 0.9 %constant_dynamic-slice_fusion = bf16[64,1024]{1,0:T(8,128)(2,1)S(1)} fusion(bf16[128,1024]{1,0:T(8,128)(2,1)} %own.1, s32[]{:T(128)S(6)} %select_n.3), kind=kLoop, calls=%fused_computation | loop fusion | bytes 262148 | tf_op jit(solution)/shard_map/dynamic_slice | solution.py:378
  3.9 2.7 %collective-permute-start.2 = (bf16[64,1024]{1,0:T(8,128)(2,1)S(1)}, bf16[64,1024]{1,0:T(8,128)(2,1)S(1)}, u32[]{:S(2)}, u32[]{:S(2)}) collective-permute-start(bf16[64,1024]{1,0:T(8,128)(2,1)S(1)} %constant_dynamic-slice_fusion), channel_id=1, source_target_pairs={{0,8},{4,12},{8,0},{12,4},{1,9},{5,13},{9,1},{13,5},{2,10},{6,14},... | collective-permute-start | bytes 393224 | tf_op jit(solution)/shard_map/ppermute | solution.py:354
  6.5 1.3 %collective-permute-start.4 = (bf16[64,1024]{1,0:T(8,128)(2,1)S(1)}, bf16[64,1024]{1,0:T(8,128)(2,1)S(1)}, u32[]{:S(2)}, u32[]{:S(2)}) collective-permute-start(bf16[64,1024]{1,0:T(8,128)(2,1)S(1)} %constant_dynamic-slice_fusion), channel_id=1, source_target_pairs={{0,12},{4,8},{8,4},{12,0},{1,13},{5,9},{9,5},{13,1},{2,14},{6,10},... | collective-permute-start | bytes 393224 | tf_op jit(solution)/shard_map/ppermute | solution.py:354
  7.9 0.2 collective-permute-start.1
  8.1 8.5 %collective-permute-done.2.refs_1_ = bf16[64,1024]{1,0:T(8,128)(2,1)S(1)} collective-permute-done((bf16[64,1024]{1,0:T(8,128)(2,1)S(1)}, bf16[64,1024]{1,0:T(8,128)(2,1)S(1)}, u32[]{:S(2)}, u32[]{:S(2)}) %collective-permute-start.2) | collective-permute-done | bytes 131104 | tf_op jit(solution)/shard_map/ppermute | solution.py:354
  16.6 0.5 collective-permute-start.3
  17.0 0.0 collective-permute-done.4.refs_3_
  17.0 1.6 %collective-permute-start.5 = (bf16[64,1024]{1,0:T(8,128)(2,1)S(1)}, bf16[64,1024]{1,0:T(8,128)(2,1)S(1)}, u32[]{:S(2)}, u32[]{:S(2)}) collective-permute-start(bf16[64,1024]{1,0:T(8,128)(2,1)S(1)} %collective-permute-done.4.refs_3_), channel_id=1, source_target_pairs={{0,2},{2,0},{1,3},{3,1},{4,6},{6,4},{5,7},{7,5},{8,10},{10,8},{9,1... | collective-permute-start | bytes 393224 | tf_op jit(solution)/shard_map/ppermute | solution.py:358
  18.6 0.0 collective-permute-done.other
  18.6 7.6 %mlp.1 = (bf16[256,512]{1,0:T(8,128)(2,1)S(1)}, f32[256,1024]{1,0:T(8,128)S(1)}) custom-call(bf16[256,512]{1,0:T(8,128)(2,1)} %bitcast.5, bf16[256,512]{1,0:T(8,128)(2,1)S(1)} %collective-permute-done.other, f32[1,1024]{1,0:T(1,128)} %bitcast.8, bf16[1024,512]{1,0:T(8,128)(2,1)} %wq.1, bf16[1024,2048]{1,0:T(8,128)(2,1)} %wup.1, bf16[2048,1024]{1,0:T(8,128)(2,1)} %wdn.1), custom_call_target="tpu_custom_call" | custom-call | flops 2415919104 | bytes 9437184 | tf_op jit(solution)/shard_map/mlp/pallas_call | solution.py:97
  26.2 0.0 copy-start.1
  26.3 0.0 collective-permute-done.3.refs_2_
  26.3 0.0 collective-permute-done.5.refs_4_
  26.3 0.0 collective-permute-done.1.refs_0_
  26.3 0.0 copy-start.2
  26.3 0.0 copy-start
  26.3 3.0 %project.1 = bf16[512,1024]{1,0:T(8,128)(2,1)S(1)} custom-call(bf16[128,1024]{1,0:T(8,128)(2,1)} %own.1, bf16[128,1024]{1,0:T(8,128)(2,1)S(1)} %collective-permute-done.1.refs_0_, bf16[64,1024]{1,0:T(8,128)(2,1)S(1)} %collective-permute-done.2.refs_1_, bf16[64,1024]{1,0:T(8,128)(2,1)S(1)} %collective-permute-done.3.refs_2_, ...), custom_call_target="tpu_custom_call" | custom-call | flops 1073741824 | bytes 4194304 | tf_op jit(solution)/shard_map/project/pallas_call | solution.py:159
  29.3 0.1 collective-permute-start.6
  29.4 2.6 %collective-permute-done.6 = bf16[512,1024]{1,0:T(8,128)(2,1)S(1)} collective-permute-done((bf16[512,1024]{1,0:T(8,128)(2,1)S(1)}, bf16[512,1024]{1,0:T(8,128)(2,1)S(1)}, u32[]{:S(2)}, u32[]{:S(2)}) %collective-permute-start.6) | collective-permute-done | bytes 1048608 | tf_op jit(solution)/shard_map/ppermute | solution.py:358
  32.0 0.0 copy-done.1
  32.0 3.5 %attend.1 = (bf16[256,512]{1,0:T(8,128)(2,1)S(1)}, bf16[256,512]{1,0:T(8,128)(2,1)S(1)}) custom-call(s32[4,8]{1,0:T(4,128)S(1)} %copy-done.1, bf16[256,512]{1,0:T(8,128)(2,1)S(1)} %get-tuple-element.22.q, bf16[8,64,1024]{2,1,0:T(8,128)(2,1)S(1)} %bitcast.6, bf16[8,64,1024]{2,1,0:T(8,128)(2,1)S(1)} %bitcast.7, f32[256,1024]{1,0:T(8,128)S(1)} %get-tuple-element.28.mlp, ...), custom_call_target="tpu_custom_call" | custom-call | flops 1342177280 | bytes 4194304 | tf_op jit(solution)/shard_map/attend/pallas_call | solution.py:252
  35.5 0.5 collective-permute-start.7
  36.0 0.0 copy-done.2
  36.0 0.1 copy.12.owners
  36.1 7.8 %collective-permute-done.7.received = bf16[256,512]{1,0:T(8,128)(2,1)S(1)} collective-permute-done((bf16[256,512]{1,0:T(8,128)(2,1)S(1)}, bf16[256,512]{1,0:T(8,128)(2,1)S(1)}, u32[]{:S(2)}, u32[]{:S(2)}) %collective-permute-start.7) | collective-permute-done | bytes 262176 | tf_op jit(solution)/shard_map/ppermute | solution.py:358
  43.9 0.0 copy-done
  43.9 0.8 %combine.1 = (bf16[2,64,512]{2,1,0:T(8,128)(2,1)S(1)}, bf16[2,64,512]{2,1,0:T(8,128)(2,1)S(1)}, bf16[2,64,512]{2,1,0:T(8,128)(2,1)S(1)}, bf16[2,64,512]{2,1,0:T(8,128)(2,1)S(1)}) custom-call(s32[4,1]{1,0:T(4,128)S(1)} %copy.12.owners, bf16[4,64,512]{2,1,0:T(8,128)(2,1)S(1)} %copy-done, bf16[256,512]{1,0:T(8,128)(2,1)S(1)} %get-tuple-element.29.keep, ...), custom_call_target="tpu_custom_call" | custom-call | flops 393216 | bytes 1310720 | tf_op jit(solution)/shard_map/combine/pallas_call | solution.py:309
  44.7 2.5 %collective-permute-start.10 = (bf16[2,64,512]{2,1,0:T(8,128)(2,1)S(1)}, bf16[2,64,512]{2,1,0:T(8,128)(2,1)S(1)}, u32[]{:S(2)}, u32[]{:S(2)}) collective-permute-start(bf16[2,64,512]{2,1,0:T(8,128)(2,1)S(1)} %get-tuple-element.34), channel_id=1, source_target_pairs={{0,12},{4,8},{8,4},{12,0},{1,13},{5,9},{9,5},{13,1},{2,14},{6,10},... | collective-permute-start | bytes 393224 | tf_op jit(solution)/shard_map/ppermute | solution.py:354
  47.2 0.9 %collective-permute-start.8 = (bf16[2,64,512]{2,1,0:T(8,128)(2,1)S(1)}, bf16[2,64,512]{2,1,0:T(8,128)(2,1)S(1)}, u32[]{:S(2)}, u32[]{:S(2)}) collective-permute-start(bf16[2,64,512]{2,1,0:T(8,128)(2,1)S(1)} %get-tuple-element.32), channel_id=1, source_target_pairs={{0,4},{4,0},{8,12},{12,8},{1,5},{5,1},{9,13},{13,9},{2,6},{6,2},{1... | collective-permute-start | bytes 393224 | tf_op jit(solution)/shard_map/ppermute | solution.py:354
  48.1 1.0 %collective-permute-start.9 = (bf16[2,64,512]{2,1,0:T(8,128)(2,1)S(1)}, bf16[2,64,512]{2,1,0:T(8,128)(2,1)S(1)}, u32[]{:S(2)}, u32[]{:S(2)}) collective-permute-start(bf16[2,64,512]{2,1,0:T(8,128)(2,1)S(1)} %get-tuple-element.33), channel_id=1, source_target_pairs={{0,8},{4,12},{8,0},{12,4},{1,9},{5,13},{9,1},{13,5},{2,10},{6,14},... | collective-permute-start | bytes 393224 | tf_op jit(solution)/shard_map/ppermute | solution.py:354
  49.1 3.8 %collective-permute-done.10.refs_3_ = bf16[2,64,512]{2,1,0:T(8,128)(2,1)S(1)} collective-permute-done((bf16[2,64,512]{2,1,0:T(8,128)(2,1)S(1)}, bf16[2,64,512]{2,1,0:T(8,128)(2,1)S(1)}, u32[]{:S(2)}, u32[]{:S(2)}) %collective-permute-start.10) | collective-permute-done | bytes 131104 | tf_op jit(solution)/shard_map/ppermute | solution.py:354
  53.0 1.8 %collective-permute-done.8.refs_1_ = bf16[2,64,512]{2,1,0:T(8,128)(2,1)S(1)} collective-permute-done((bf16[2,64,512]{2,1,0:T(8,128)(2,1)S(1)}, bf16[2,64,512]{2,1,0:T(8,128)(2,1)S(1)}, u32[]{:S(2)}, u32[]{:S(2)}) %collective-permute-start.8) | collective-permute-done | bytes 131104 | tf_op jit(solution)/shard_map/ppermute | solution.py:354
  54.8 4.2 %collective-permute-done.9.refs_2_ = bf16[2,64,512]{2,1,0:T(8,128)(2,1)S(1)} collective-permute-done((bf16[2,64,512]{2,1,0:T(8,128)(2,1)S(1)}, bf16[2,64,512]{2,1,0:T(8,128)(2,1)S(1)}, u32[]{:S(2)}, u32[]{:S(2)}) %collective-permute-start.9) | collective-permute-done | bytes 131104 | tf_op jit(solution)/shard_map/ppermute | solution.py:354
  58.9 0.8 %place.1 = bf16[8,64,512]{2,1,0:T(8,128)(2,1)} custom-call(bf16[2,64,512]{2,1,0:T(8,128)(2,1)S(1)} %get-tuple-element.31.refs_0_, bf16[2,64,512]{2,1,0:T(8,128)(2,1)S(1)} %collective-permute-done.8.refs_1_, bf16[2,64,512]{2,1,0:T(8,128)(2,1)S(1)} %collective-permute-done.9.refs_2_, bf16[2,64,512]{2,1,0:T(8,128)(2,1)S(1)} %collective-permute-done.10.refs_3_), custom_call_target="tpu_custom_call" | custom-call | tf_op jit(solution)/shard_map/place/pallas_call | solution.py:342
Async XLA Ops:
  0.0 18.6 %collective-permute-start = (bf16[256,512]{1,0:T(8,128)(2,1)}, bf16[256,512]{1,0:T(8,128)(2,1)S(1)}, u32[]{:S(2)}, u32[]{:S(2)}) collective-permute-start(bf16[256,512]{1,0:T(8,128)(2,1)} %bitcast.4), channel_id=1, source_target_pairs={{0,2},{2,0},{1,3},{3,1},{4,6},{6,4},{5,7},{7,5},{8,10},{10,8},{9,1... | collective-permute-start | bytes 786440 | tf_op jit(solution)/shard_map/ppermute | solution.py:358
  3.9 12.7 %collective-permute-start.2 = (bf16[64,1024]{1,0:T(8,128)(2,1)S(1)}, bf16[64,1024]{1,0:T(8,128)(2,1)S(1)}, u32[]{:S(2)}, u32[]{:S(2)}) collective-permute-start(bf16[64,1024]{1,0:T(8,128)(2,1)S(1)} %constant_dynamic-slice_fusion), channel_id=1, source_target_pairs={{0,8},{4,12},{8,0},{12,4},{1,9},{5,13},{9,1},{13,5},{2,10},{6,14},... | collective-permute-start | bytes 393224 | tf_op jit(solution)/shard_map/ppermute | solution.py:354
  6.5 10.5 %collective-permute-start.4 = (bf16[64,1024]{1,0:T(8,128)(2,1)S(1)}, bf16[64,1024]{1,0:T(8,128)(2,1)S(1)}, u32[]{:S(2)}, u32[]{:S(2)}) collective-permute-start(bf16[64,1024]{1,0:T(8,128)(2,1)S(1)} %constant_dynamic-slice_fusion), channel_id=1, source_target_pairs={{0,12},{4,8},{8,4},{12,0},{1,13},{5,9},{9,5},{13,1},{2,14},{6,10},... | collective-permute-start | bytes 393224 | tf_op jit(solution)/shard_map/ppermute | solution.py:354
  7.9 18.4 %collective-permute-start.1 = (bf16[128,1024]{1,0:T(8,128)(2,1)}, bf16[128,1024]{1,0:T(8,128)(2,1)S(1)}, u32[]{:S(2)}, u32[]{:S(2)}) collective-permute-start(bf16[128,1024]{1,0:T(8,128)(2,1)} %own.1), channel_id=1, source_target_pairs={{0,4},{4,0},{8,12},{12,8},{1,5},{5,1},{9,13},{13,9},{2,6},{6,2},{1... | collective-permute-start | bytes 786440 | tf_op jit(solution)/shard_map/ppermute | solution.py:354
  16.6 9.7 %collective-permute-start.3 = (bf16[64,1024]{1,0:T(8,128)(2,1)S(1)}, bf16[64,1024]{1,0:T(8,128)(2,1)S(1)}, u32[]{:S(2)}, u32[]{:S(2)}) collective-permute-start(bf16[64,1024]{1,0:T(8,128)(2,1)S(1)} %collective-permute-done.2.refs_1_), channel_id=1, source_target_pairs={{0,2},{2,0},{1,3},{3,1},{4,6},{6,4},{5,7},{7,5},{8,10},{10,8},{9,1... | collective-permute-start | bytes 393224 | tf_op jit(solution)/shard_map/ppermute | solution.py:358
  17.0 9.2 %collective-permute-start.5 = (bf16[64,1024]{1,0:T(8,128)(2,1)S(1)}, bf16[64,1024]{1,0:T(8,128)(2,1)S(1)}, u32[]{:S(2)}, u32[]{:S(2)}) collective-permute-start(bf16[64,1024]{1,0:T(8,128)(2,1)S(1)} %collective-permute-done.4.refs_3_), channel_id=1, source_target_pairs={{0,2},{2,0},{1,3},{3,1},{4,6},{6,4},{5,7},{7,5},{8,10},{10,8},{9,1... | collective-permute-start | bytes 393224 | tf_op jit(solution)/shard_map/ppermute | solution.py:358
  26.2 5.8 %copy-start.1 = (s32[4,8]{1,0:T(4,128)S(1)}, s32[4,8]{1,0:T(4,128)}, u32[]{:S(2)}) copy-start(s32[4,8]{1,0:T(4,128)} %adjacency.1) | copy-start | bytes 388
  26.3 9.7 %copy-start.2 = (s32[4,1]{0,1:T(1,128)S(1)}, s32[4,1]{0,1:T(1,128)}, u32[]{:S(2)}) copy-start(s32[4,1]{0,1:T(1,128)} %param.12) | copy-start | bytes 52
  26.3 17.6 %copy-start = (bf16[4,64,512]{2,1,0:T(8,128)(2,1)S(1)}, bf16[4,64,512]{2,1,0:T(8,128)(2,1)}, u32[]{:S(2)}) copy-start(bf16[4,64,512]{2,1,0:T(8,128)(2,1)} %grid_features.1) | copy-start | bytes 786436
  29.3 2.7 %collective-permute-start.6 = (bf16[512,1024]{1,0:T(8,128)(2,1)S(1)}, bf16[512,1024]{1,0:T(8,128)(2,1)S(1)}, u32[]{:S(2)}, u32[]{:S(2)}) collective-permute-start(bf16[512,1024]{1,0:T(8,128)(2,1)S(1)} %project.1), channel_id=1, source_target_pairs={{0,1},{1,0},{2,3},{3,2},{4,5},{5,4},{6,7},{7,6},{8,9},{9,8},{10,11... | collective-permute-start | bytes 3145736 | tf_op jit(solution)/shard_map/ppermute | solution.py:358
  35.5 8.4 %collective-permute-start.7 = (bf16[256,512]{1,0:T(8,128)(2,1)S(1)}, bf16[256,512]{1,0:T(8,128)(2,1)S(1)}, u32[]{:S(2)}, u32[]{:S(2)}) collective-permute-start(bf16[256,512]{1,0:T(8,128)(2,1)S(1)} %get-tuple-element.30), channel_id=1, source_target_pairs={{0,2},{2,0},{1,3},{3,1},{4,6},{6,4},{5,7},{7,5},{8,10},{10,8},{9,1... | collective-permute-start | bytes 786440 | tf_op jit(solution)/shard_map/ppermute | solution.py:358
  44.7 8.3 %collective-permute-start.10 = (bf16[2,64,512]{2,1,0:T(8,128)(2,1)S(1)}, bf16[2,64,512]{2,1,0:T(8,128)(2,1)S(1)}, u32[]{:S(2)}, u32[]{:S(2)}) collective-permute-start(bf16[2,64,512]{2,1,0:T(8,128)(2,1)S(1)} %get-tuple-element.34), channel_id=1, source_target_pairs={{0,12},{4,8},{8,4},{12,0},{1,13},{5,9},{9,5},{13,1},{2,14},{6,10},... | collective-permute-start | bytes 393224 | tf_op jit(solution)/shard_map/ppermute | solution.py:354
  47.2 7.6 %collective-permute-start.8 = (bf16[2,64,512]{2,1,0:T(8,128)(2,1)S(1)}, bf16[2,64,512]{2,1,0:T(8,128)(2,1)S(1)}, u32[]{:S(2)}, u32[]{:S(2)}) collective-permute-start(bf16[2,64,512]{2,1,0:T(8,128)(2,1)S(1)} %get-tuple-element.32), channel_id=1, source_target_pairs={{0,4},{4,0},{8,12},{12,8},{1,5},{5,1},{9,13},{13,9},{2,6},{6,2},{1... | collective-permute-start | bytes 393224 | tf_op jit(solution)/shard_map/ppermute | solution.py:354
  48.1 10.8 %collective-permute-start.9 = (bf16[2,64,512]{2,1,0:T(8,128)(2,1)S(1)}, bf16[2,64,512]{2,1,0:T(8,128)(2,1)S(1)}, u32[]{:S(2)}, u32[]{:S(2)}) collective-permute-start(bf16[2,64,512]{2,1,0:T(8,128)(2,1)S(1)} %get-tuple-element.33), channel_id=1, source_target_pairs={{0,8},{4,12},{8,0},{12,4},{1,9},{5,13},{9,1},{13,5},{2,10},{6,14},... | collective-permute-start | bytes 393224 | tf_op jit(solution)/shard_map/ppermute | solution.py:354

commit v3 on v2

--- a/solution.py
+++ b/solution.py
@@ -52,6 +52,8 @@
     ]
     for copy in copies:
         copy.start()
+    for i in (0, 1, 3):
+        copies[i].wait()
     ups, downs = [], []
     for c in range(wup_s.shape[0]):
         span = pl.ds(c * chunk, chunk)
@@ -68,9 +70,6 @@
             )
             pair[part].start()
         downs.append(pair)
-    copies[0].wait()
-    copies[1].wait()
-    copies[3].wait()
     x = x_s[...].astype(jnp.float32)
     centered = x - jnp.mean(x, axis=-1, keepdims=True)
     variance = jnp.mean(centered * centered, axis=-1, keepdims=True)
@@ -128,7 +127,7 @@
     )(in_hbm(own), other, in_hbm(gain), in_hbm(wq), in_hbm(wup), in_hbm(wdn))
 
 
-def project_kernel(own, *refs):
+def project_kernel(*refs):
     pieces, (wk, wv, out, rows_s, w_s, p_sem, w_sem) = refs[:-7], refs[-7:]
     width = wk.shape[1]
     weights = [
@@ -139,7 +138,7 @@
         copy.start()
     copies = []
     first = 0
-    for i, piece in enumerate((own, *pieces)):
+    for i, piece in enumerate(pieces):
         rows = piece.shape[0]
         copies.append(
             pltpu.make_async_copy(piece, rows_s.at[pl.ds(first, rows), :], p_sem.at[i])
@@ -153,46 +152,46 @@
     out[...] = dot(rows_s[...], w_s[...]).astype(jnp.bfloat16)
 
 
-def run_project(own, pieces, wk, wv):
-    rows = own.shape[0] + sum(piece.shape[0] for piece in pieces)
-    width = wk.shape[1]
+def run_project(pieces, wk, wv):
+    rows = sum(piece.shape[0] for piece in pieces)
+    depth, width = wk.shape
     return pl.pallas_call(
         project_kernel,
         out_shape=jax.ShapeDtypeStruct((rows, 2 * width), jnp.bfloat16),
-        in_specs=[whole(pltpu.HBM)]
-        + [whole(pl.ANY)] * len(pieces)
-        + [whole(pltpu.HBM)] * 2,
+        in_specs=[whole(pl.ANY)] * len(pieces) + [whole(pltpu.HBM)] * 2,
         out_specs=whole(pltpu.VMEM),
         scratch_shapes=[
-            pltpu.VMEM((rows, own.shape[1]), jnp.bfloat16),
-            pltpu.VMEM((wk.shape[0], 2 * width), jnp.bfloat16),
-            pltpu.SemaphoreType.DMA((1 + len(pieces),)),
+            pltpu.VMEM((rows, depth), jnp.bfloat16),
+            pltpu.VMEM((depth, 2 * width), jnp.bfloat16),
+            pltpu.SemaphoreType.DMA((len(pieces),)),
             pltpu.SemaphoreType.DMA((2,)),
         ],
         compiler_params=pltpu.CompilerParams(vmem_limit_bytes=12 * MIB),
         cost_estimate=pl.CostEstimate(
-            flops=4 * rows * wk.shape[0] * width,
-            bytes_accessed=4 * wk.shape[0] * width + 4 * rows * wk.shape[0],
+            flops=80 * rows * depth * width,
+            bytes_accessed=80 * depth * width + 4 * rows * depth,
             transcendentals=0,
         ),
         name="project",
-    )(in_hbm(own), *pieces, in_hbm(wk), in_hbm(wv))
+    )(*pieces, in_hbm(wk), in_hbm(wv))
 
 
 def attend_kernel(
-    adjacency, q, kv_mine, kv_sibling, mlp, wo, send, keep, table, att_s, wo_s, t_sem, w_sem
+    adjacency, q, mine_a, mine_b, sibling_a, sibling_b, mlp, wo,
+    send, keep, table, att_s, wo_s, t_sem, w_sem,
 ):
     s = lax.axis_index("shard")
     h = lax.axis_index("head")
     u = lax.axis_index("sub")
     half = wo.shape[0]
-    per_core = kv_mine.shape[0]
-    tables = [
-        pltpu.make_async_copy(kv_mine, table.at[pl.ds(0, per_core)], t_sem.at[0]),
-        pltpu.make_async_copy(kv_sibling, table.at[pl.ds(per_core, per_core)], t_sem.at[1]),
-    ]
-    for copy in tables:
-        copy.start()
+    per_core = mine_a.shape[0] + mine_b.shape[0]
+    tables = []
+    first = 0
+    for i, part in enumerate((mine_a, mine_b, sibling_a, sibling_b)):
+        blocks = part.shape[0]
+        tables.append(pltpu.make_async_copy(part, table.at[pl.ds(first, blocks)], t_sem.at[i]))
+        tables[i].start()
+        first += blocks
     weights = []
     for part, head in enumerate((1 - h, h)):
         columns = pl.ds(pl.multiple_of(head * half, half), half)
@@ -216,7 +215,7 @@
             part = lax.rem(m, 2)
             core = lax.rem(m // 2, 2)
             distance = s ^ (m // 4)
-            part = jnp.where(distance <= 1, part, part ^ h)
+            distance = jnp.where(distance <= 1, distance, 2 + ((distance - 2) ^ h))
             places.append((core ^ u) * per_core + distance * 2 + part)
         for g in range(half // WIDE):
             columns = slice(g * WIDE, (g + 1) * WIDE)
@@ -245,37 +244,32 @@
     keep[...] = branch[:, half:].astype(jnp.bfloat16)
 
 
-def run_attend(adjacency, q, kv_mine, kv_sibling, mlp, wo):
+def run_attend(adjacency, q, tables, mlp, wo):
     rows, half = q.shape
-    nodes = 2 * kv_mine.shape[0] * BLOCK
+    blocks = sum(part.shape[0] for part in tables)
     part = jax.ShapeDtypeStruct((rows, half), jnp.bfloat16)
     return pl.pallas_call(
         attend_kernel,
         out_shape=(part, part),
-        in_specs=[
-            whole(pltpu.SMEM),
-            whole(pltpu.VMEM),
-            whole(pl.ANY),
-            whole(pl.ANY),
-            whole(pltpu.VMEM),
-            whole(pltpu.HBM),
-        ],
+        in_specs=[whole(pltpu.SMEM), whole(pltpu.VMEM)]
+        + [whole(pl.ANY)] * len(tables)
+        + [whole(pltpu.VMEM), whole(pltpu.HBM)],
         out_specs=(whole(pltpu.VMEM), whole(pltpu.VMEM)),
         scratch_shapes=[
-            pltpu.VMEM((2 * kv_mine.shape[0],) + kv_mine.shape[1:], jnp.bfloat16),
+            pltpu.VMEM((blocks,) + tables[0].shape[1:], jnp.bfloat16),
             pltpu.VMEM((rows, half), jnp.bfloat16),
             pltpu.VMEM(wo.shape, jnp.bfloat16),
-            pltpu.SemaphoreType.DMA((2,)),
+            pltpu.SemaphoreType.DMA((len(tables),)),
             pltpu.SemaphoreType.DMA((2,)),
         ],
         compiler_params=pltpu.CompilerParams(vmem_limit_bytes=16 * MIB),
         cost_estimate=pl.CostEstimate(
             flops=2 * rows * half * (D + 8 * 8 * BLOCK),
-            bytes_accessed=4 * nodes * half + 2 * half * D + 4 * rows * D,
+            bytes_accessed=4 * blocks * BLOCK * half + 2 * half * D + 4 * rows * D,
             transcendentals=rows * 8 * BLOCK * half // HEAD_DIM,
         ),
         name="attend",
-    )(adjacency, q, kv_mine, kv_sibling, mlp, in_hbm(wo))
+    )(adjacency, q, *tables, mlp, in_hbm(wo))
 
 
 def combine_kernel(owners, grid_features, keep, received, *outs):
@@ -352,6 +346,11 @@
 
 def crossed(x, distance, size):
     return lax.ppermute(x, "shard", [(i, i ^ distance) for i in range(size)])
+
+
+def fetched(x, size):
+    pairs = [(2 * i + h, 2 * (i ^ (2 + h)) + h) for i in range(size) for h in range(2)]
+    return lax.ppermute(x, ("shard", "head"), pairs)
 
 
 def swapped(x, axis):
@@ -375,26 +374,21 @@
     count, rows, half = grid_features.shape
     flat = grid_features.reshape(count * rows, half)
     other = swapped(flat, "head")
-    mesh_half = lax.dynamic_slice_in_dim(mesh_nodes, lax.axis_index("head") * BLOCK, BLOCK, 0)
-    pieces = [crossed(mesh_nodes, 1, shards)]
-    for d in range(2, shards):
-        piece = crossed(mesh_half, d, shards)
-        pieces += [piece, swapped(piece, "head")]
+    far = fetched(mesh_nodes, shards)
+    near = crossed(mesh_nodes, 1, shards)
     queries, mlp = run_mlp(
         flat, other, norm_gain.reshape(1, -1), query_weight, up_weight, down_weight
     )
-    queries, mlp, *pieces = lax.optimization_barrier((queries, mlp, *pieces))
-    kv_mine = run_project(mesh_nodes, pieces, key_weight, value_weight)
-    kv_sibling = swapped(kv_mine, "sub")
-    blocked = (2 * shards, BLOCK, 2 * half)
-    send, keep = run_attend(
-        adjacency,
-        queries,
-        kv_mine.reshape(blocked),
-        kv_sibling.reshape(blocked),
-        mlp,
-        output_weight,
-    )
+    queries, mlp, far = lax.optimization_barrier((queries, mlp, far))
+    farther = swapped(far, "head")
+    mine_a = run_project((mesh_nodes, near, far), key_weight, value_weight)
+    sibling_a = swapped(mine_a, "sub")
+    mine_b = run_project((farther,), key_weight, value_weight)
+    sibling_b = swapped(mine_b, "sub")
+    tables = [
+        table.reshape(-1, BLOCK, 2 * half) for table in (mine_a, mine_b, sibling_a, sibling_b)
+    ]
+    send, keep = run_attend(adjacency, queries, tables, mlp, output_weight)
     received = swapped(send, "head")
     slots = run_combine(owners, grid_features, keep, received, shards)
     arrived = [slots[0]] + [crossed(slots[d], d, shards) for d in range(1, shards)]
@@ -513,7 +507,7 @@
 
 def local(grid_features, owners, adjacency, mesh_nodes, *parameters):
     pairs = lax.axis_size("head") == 2 and lax.axis_size("sub") == 2
-    pairs = pairs and lax.axis_size("shard") in (2, 4, 8)
+    pairs = pairs and lax.axis_size("shard") == 4
     small = grid_features.shape[0] <= 4 and mesh_nodes.shape[0] == 2 * BLOCK
     if pairs and small and grid_features.shape[1] == BLOCK:
         return paired(grid_features, owners, adjacency, mesh_nodes, *parameters)

time: 59.9 us -> 56.9 us (0.950)
  starting transfers between devices: 14.2 us -> 12.7 us
  local copies, waits for them, and re-layouts: 1.02 us -> 0.11 us
    ppermute x6 -> x4, waiting for transfers between devices: 18.3 us -> 9.89 us  [crossed(): return lax.ppermute(x, 'shard', [(i, i ^ distance) for i in range(size)])]
    ppermute x5, waiting for transfers between devices: 10.4 us -> 16.1 us  [swapped(): return lax.ppermute(x, axis, [(0, 1), (1, 0)])]
    ppermute x0 -> x1, starting transfers between devices: none -> 2.59 us  [fetched(): return lax.ppermute(x, ('shard', 'head'), pairs)]
    ppermute x0 -> x1, waiting for transfers between devices: none -> 2.22 us  [fetched(): return lax.ppermute(x, ('shard', 'head'), pairs)]
    ppermute x5, starting transfers between devices: 5.56 us -> 3.43 us  [swapped(): return lax.ppermute(x, axis, [(0, 1), (1, 0)])]
    ppermute x6 -> x4, starting transfers between devices: 8.69 us -> 6.72 us  [crossed(): return lax.ppermute(x, 'shard', [(i, i ^ distance) for i in range(size)])]
    pallas_call x1, Pallas kernels: 7.64 us -> 5.86 us  [run_mlp(): pl.pallas_call(mlp_kernel, out_shape=(jax.ShapeDtypeStruct((rows, wq.shap...]
    pallas_call x1 -> x2, Pallas kernels: 2.96 us -> 4.6 us  [run_project(): pl.pallas_call(project_kernel, out_shape=jax.ShapeDtypeStruct((rows, 2 *...]
  transfers between devices with their start and end apart: 11 -> 10, of which waited for: 6 -> 7; matrix products, arithmetic and copies ran while one was open for 2% -> 0% of each run, Pallas kernels for 13% -> 18%
where the time goes in v3:
time: 56.9 us; the launch traced here: 56.7 us
  waiting for transfers between devices  28.2 us (50%)
  Pallas kernels  15.6 us (27%)
  starting transfers between devices  12.7 us (22%)
    ppermute x5, waiting for transfers between devices, swapped(): return lax.ppermute(x, axis, [(0, 1), (1, 0)])  16.1 us
    ppermute x4, waiting for transfers between devices, crossed(): return lax.ppermute(x, 'shard', [(i, i ^ distance) for i in range(size)])  9.89 us
    ppermute x4, starting transfers between devices, crossed(): return lax.ppermute(x, 'shard', [(i, i ^ distance) for i in range(size)])  6.72 us
    pallas_call x1, Pallas kernels, run_mlp(): pl.pallas_call(mlp_kernel, out_shape=(jax.ShapeDtypeStruct((rows, wq.shap...  5.86 us
    pallas_call x2, Pallas kernels, run_project(): pl.pallas_call(project_kernel, out_shape=jax.ShapeDtypeStruct((rows, 2 *...  4.6 us
    pallas_call x1, Pallas kernels, run_attend(): pl.pallas_call(attend_kernel, out_shape=(part, part), in_specs=[whole(plt...  3.52 us
    ppermute x5, starting transfers between devices, swapped(): return lax.ppermute(x, axis, [(0, 1), (1, 0)])  3.43 us
    ppermute x1, starting transfers between devices, fetched(): return lax.ppermute(x, ('shard', 'head'), pairs)  2.59 us
  transfers between devices with their start and end apart: 10, of which 7 were waited for; matrix products, arithmetic and copies ran while one was open for 0% of the time, Pallas kernels for 18%

profile of v3, /device:TPU:0, one launch (start us, length us, event | category | flops | bytes accessed | tf_op | source)
XLA Modules:
  0.0 56.7 jit_solution(13376266140024391928)
XLA Ops:
  0.0 2.9 %collective-permute-start = (bf16[256,512]{1,0:T(8,128)(2,1)}, bf16[256,512]{1,0:T(8,128)(2,1)S(1)}, u32[]{:S(2)}, u32[]{:S(2)}) collective-permute-start(bf16[256,512]{1,0:T(8,128)(2,1)} %bitcast.6), channel_id=1, source_target_pairs={{0,2},{2,0},{1,3},{3,1},{4,6},{6,4},{5,7},{7,5},{8,10},{10,8},{9,1... | collective-permute-start | bytes 786440 | tf_op jit(solution)/shard_map/ppermute | solution.py:357
  2.9 2.6 %collective-permute-start.1 = (bf16[128,1024]{1,0:T(8,128)(2,1)}, bf16[128,1024]{1,0:T(8,128)(2,1)S(1)}, u32[]{:S(2)}, u32[]{:S(2)}) collective-permute-start(bf16[128,1024]{1,0:T(8,128)(2,1)} %refs_0_.1), channel_id=1, source_target_pairs={{0,8},{2,14},{4,12},{6,10},{8,0},{10,6},{12,4},{14,2},{1,9},{3,15}... | collective-permute-start | bytes 786440 | tf_op jit(solution)/shard_map/ppermute | solution.py:353
  5.5 1.6 %collective-permute-start.2 = (bf16[128,1024]{1,0:T(8,128)(2,1)}, bf16[128,1024]{1,0:T(8,128)(2,1)S(1)}, u32[]{:S(2)}, u32[]{:S(2)}) collective-permute-start(bf16[128,1024]{1,0:T(8,128)(2,1)} %refs_0_.1), channel_id=1, source_target_pairs={{0,4},{4,0},{8,12},{12,8},{1,5},{5,1},{9,13},{13,9},{2,6},{6,2},{1... | collective-permute-start | bytes 786440 | tf_op jit(solution)/shard_map/ppermute | solution.py:348
  7.1 2.3 %collective-permute-done.other = bf16[256,512]{1,0:T(8,128)(2,1)S(1)} collective-permute-done((bf16[256,512]{1,0:T(8,128)(2,1)}, bf16[256,512]{1,0:T(8,128)(2,1)S(1)}, u32[]{:S(2)}, u32[]{:S(2)}) %collective-permute-start) | collective-permute-done | bytes 262176 | tf_op jit(solution)/shard_map/ppermute | solution.py:357
  9.5 0.0 copy-start.1
  9.5 5.9 %mlp.1 = (bf16[256,512]{1,0:T(8,128)(2,1)S(1)}, f32[256,1024]{1,0:T(8,128)S(1)}) custom-call(bf16[256,512]{1,0:T(8,128)(2,1)} %bitcast.7, bf16[256,512]{1,0:T(8,128)(2,1)S(1)} %collective-permute-done.other, f32[1,1024]{1,0:T(1,128)} %bitcast.12, bf16[1024,512]{1,0:T(8,128)(2,1)} %wq.1, bf16[1024,2048]{1,0:T(8,128)(2,1)} %wup.1, bf16[2048,1024]{1,0:T(8,128)(2,1)} %wdn.1), custom_call_target="tpu_custom_call" | custom-call | flops 2415919104 | bytes 9437184 | tf_op jit(solution)/shard_map/mlp/pallas_call | solution.py:96
  15.3 2.2 %collective-permute-done.1.refs_2_ = bf16[128,1024]{1,0:T(8,128)(2,1)S(1)} collective-permute-done((bf16[128,1024]{1,0:T(8,128)(2,1)}, bf16[128,1024]{1,0:T(8,128)(2,1)S(1)}, u32[]{:S(2)}, u32[]{:S(2)}) %collective-permute-start.1) | collective-permute-done | bytes 262176 | tf_op jit(solution)/shard_map/ppermute | solution.py:353
  17.5 0.0 collective-permute-start.3
  17.5 0.2 collective-permute-done.2.refs_1_
  17.7 0.0 copy-done.1
  17.7 2.6 %project.2 = bf16[384,1024]{1,0:T(8,128)(2,1)S(1)} custom-call(bf16[128,1024]{1,0:T(8,128)(2,1)S(1)} %copy-done.1, bf16[128,1024]{1,0:T(8,128)(2,1)S(1)} %collective-permute-done.2.refs_1_, bf16[128,1024]{1,0:T(8,128)(2,1)S(1)} %collective-permute-done.1.refs_2_, bf16[1024,512]{1,0:T(8,128)(2,1)} %refs_1_.1, bf16[1024,512]{1,0:T(8,128)(2,1)} %refs_2_.1), custom_call_target="tpu_custom_call" | custom-call | flops 16106127360 | bytes 43515904 | tf_op jit(solution)/shard_map/project/pallas_call | solution.py:158
  20.3 0.0 copy-start.2
  20.3 0.1 collective-permute-start.4
  20.4 4.2 %collective-permute-done.3.refs_0_ = bf16[128,1024]{1,0:T(8,128)(2,1)S(1)} collective-permute-done((bf16[128,1024]{1,0:T(8,128)(2,1)S(1)}, bf16[128,1024]{1,0:T(8,128)(2,1)S(1)}, u32[]{:S(2)}, u32[]{:S(2)}) %collective-permute-start.3) | collective-permute-done | bytes 262176 | tf_op jit(solution)/shard_map/ppermute | solution.py:357
  24.6 2.0 %project.3 = bf16[128,1024]{1,0:T(8,128)(2,1)S(1)} custom-call(bf16[128,1024]{1,0:T(8,128)(2,1)S(1)} %collective-permute-done.3.refs_0_, bf16[1024,512]{1,0:T(8,128)(2,1)} %refs_1_.1, bf16[1024,512]{1,0:T(8,128)(2,1)} %refs_2_.1), custom_call_target="tpu_custom_call" | custom-call | flops 5368709120 | bytes 42467328 | tf_op jit(solution)/shard_map/project/pallas_call | solution.py:158
  26.7 0.0 copy-start.3
  26.7 0.0 copy-start
  26.7 0.1 collective-permute-start.5
  26.8 1.5 %collective-permute-done.5 = bf16[128,1024]{1,0:T(8,128)(2,1)S(1)} collective-permute-done((bf16[128,1024]{1,0:T(8,128)(2,1)S(1)}, bf16[128,1024]{1,0:T(8,128)(2,1)S(1)}, u32[]{:S(2)}, u32[]{:S(2)}) %collective-permute-start.5) | collective-permute-done | bytes 262176 | tf_op jit(solution)/shard_map/ppermute | solution.py:357
  28.3 0.0 collective-permute-done.4
  28.3 0.0 copy-done.2
  28.3 3.5 %attend.1 = (bf16[256,512]{1,0:T(8,128)(2,1)S(1)}, bf16[256,512]{1,0:T(8,128)(2,1)S(1)}) custom-call(s32[4,8]{1,0:T(4,128)S(1)} %copy-done.2, bf16[256,512]{1,0:T(8,128)(2,1)S(1)} %get-tuple-element.18.q, bf16[6,64,1024]{2,1,0:T(8,128)(2,1)S(1)} %bitcast.8, bf16[2,64,1024]{2,1,0:T(8,128)(2,1)S(1)} %bitcast.10, bf16[6,64,1024]{2,1,0:T(8,128)(2,1)S(1)} %bitcast.9, ...), custom_call_target="tpu_custom_call" | custom-call | flops 1342177280 | bytes 4194304 | tf_op jit(solution)/shard_map/attend/pallas_call | solution.py:251
  31.8 0.3 collective-permute-start.6
  32.2 0.0 copy-done.3
  32.2 0.1 copy.12.owners
  32.3 8.0 %collective-permute-done.6.received = bf16[256,512]{1,0:T(8,128)(2,1)S(1)} collective-permute-done((bf16[256,512]{1,0:T(8,128)(2,1)S(1)}, bf16[256,512]{1,0:T(8,128)(2,1)S(1)}, u32[]{:S(2)}, u32[]{:S(2)}) %collective-permute-start.6) | collective-permute-done | bytes 262176 | tf_op jit(solution)/shard_map/ppermute | solution.py:357
  40.2 0.0 copy-done
  40.2 0.8 %combine.1 = (bf16[2,64,512]{2,1,0:T(8,128)(2,1)S(1)}, bf16[2,64,512]{2,1,0:T(8,128)(2,1)S(1)}, bf16[2,64,512]{2,1,0:T(8,128)(2,1)S(1)}, bf16[2,64,512]{2,1,0:T(8,128)(2,1)S(1)}) custom-call(s32[4,1]{1,0:T(4,128)S(1)} %copy.12.owners, bf16[4,64,512]{2,1,0:T(8,128)(2,1)S(1)} %copy-done, bf16[256,512]{1,0:T(8,128)(2,1)S(1)} %get-tuple-element.21.keep, ...), custom_call_target="tpu_custom_call" | custom-call | flops 393216 | bytes 1310720 | tf_op jit(solution)/shard_map/combine/pallas_call | solution.py:303
  41.0 1.9 %collective-permute-start.7 = (bf16[2,64,512]{2,1,0:T(8,128)(2,1)S(1)}, bf16[2,64,512]{2,1,0:T(8,128)(2,1)S(1)}, u32[]{:S(2)}, u32[]{:S(2)}) collective-permute-start(bf16[2,64,512]{2,1,0:T(8,128)(2,1)S(1)} %get-tuple-element.24), channel_id=1, source_target_pairs={{0,4},{4,0},{8,12},{12,8},{1,5},{5,1},{9,13},{13,9},{2,6},{6,2},{1... | collective-permute-start | bytes 393224 | tf_op jit(solution)/shard_map/ppermute | solution.py:348
  42.9 3.3 %collective-permute-start.8 = (bf16[2,64,512]{2,1,0:T(8,128)(2,1)S(1)}, bf16[2,64,512]{2,1,0:T(8,128)(2,1)S(1)}, u32[]{:S(2)}, u32[]{:S(2)}) collective-permute-start(bf16[2,64,512]{2,1,0:T(8,128)(2,1)S(1)} %get-tuple-element.25), channel_id=1, source_target_pairs={{0,8},{4,12},{8,0},{12,4},{1,9},{5,13},{9,1},{13,5},{2,10},{6,14},... | collective-permute-start | bytes 393224 | tf_op jit(solution)/shard_map/ppermute | solution.py:348
  46.1 0.0 collective-permute-start.9
  46.2 0.0 collective-permute-done.7.refs_1_
  46.2 9.7 %collective-permute-done.8.refs_2_ = bf16[2,64,512]{2,1,0:T(8,128)(2,1)S(1)} collective-permute-done((bf16[2,64,512]{2,1,0:T(8,128)(2,1)S(1)}, bf16[2,64,512]{2,1,0:T(8,128)(2,1)S(1)}, u32[]{:S(2)}, u32[]{:S(2)}) %collective-permute-start.8) | collective-permute-done | bytes 131104 | tf_op jit(solution)/shard_map/ppermute | solution.py:348
  55.9 0.0 collective-permute-done.9.refs_3_
  55.9 0.8 %place.1 = bf16[8,64,512]{2,1,0:T(8,128)(2,1)} custom-call(bf16[2,64,512]{2,1,0:T(8,128)(2,1)S(1)} %get-tuple-element.23.refs_0_, bf16[2,64,512]{2,1,0:T(8,128)(2,1)S(1)} %collective-permute-done.7.refs_1_, bf16[2,64,512]{2,1,0:T(8,128)(2,1)S(1)} %collective-permute-done.8.refs_2_, bf16[2,64,512]{2,1,0:T(8,128)(2,1)S(1)} %collective-permute-done.9.refs_3_), custom_call_target="tpu_custom_call" | custom-call | tf_op jit(solution)/shard_map/place/pallas_call | solution.py:336
Async XLA Ops:
  0.0 9.5 %collective-permute-start = (bf16[256,512]{1,0:T(8,128)(2,1)}, bf16[256,512]{1,0:T(8,128)(2,1)S(1)}, u32[]{:S(2)}, u32[]{:S(2)}) collective-permute-start(bf16[256,512]{1,0:T(8,128)(2,1)} %bitcast.6), channel_id=1, source_target_pairs={{0,2},{2,0},{1,3},{3,1},{4,6},{6,4},{5,7},{7,5},{8,10},{10,8},{9,1... | collective-permute-start | bytes 786440 | tf_op jit(solution)/shard_map/ppermute | solution.py:357
  2.9 14.6 %collective-permute-start.1 = (bf16[128,1024]{1,0:T(8,128)(2,1)}, bf16[128,1024]{1,0:T(8,128)(2,1)S(1)}, u32[]{:S(2)}, u32[]{:S(2)}) collective-permute-start(bf16[128,1024]{1,0:T(8,128)(2,1)} %refs_0_.1), channel_id=1, source_target_pairs={{0,8},{2,14},{4,12},{6,10},{8,0},{10,6},{12,4},{14,2},{1,9},{3,15}... | collective-permute-start | bytes 786440 | tf_op jit(solution)/shard_map/ppermute | solution.py:353
  5.5 12.2 %collective-permute-start.2 = (bf16[128,1024]{1,0:T(8,128)(2,1)}, bf16[128,1024]{1,0:T(8,128)(2,1)S(1)}, u32[]{:S(2)}, u32[]{:S(2)}) collective-permute-start(bf16[128,1024]{1,0:T(8,128)(2,1)} %refs_0_.1), channel_id=1, source_target_pairs={{0,4},{4,0},{8,12},{12,8},{1,5},{5,1},{9,13},{13,9},{2,6},{6,2},{1... | collective-permute-start | bytes 786440 | tf_op jit(solution)/shard_map/ppermute | solution.py:348
  9.5 8.3 %copy-start.1 = (bf16[128,1024]{1,0:T(8,128)(2,1)S(1)}, bf16[128,1024]{1,0:T(8,128)(2,1)}, u32[]{:S(2)}) copy-start(bf16[128,1024]{1,0:T(8,128)(2,1)} %refs_0_.1) | copy-start | bytes 786436
  17.5 7.1 %collective-permute-start.3 = (bf16[128,1024]{1,0:T(8,128)(2,1)S(1)}, bf16[128,1024]{1,0:T(8,128)(2,1)S(1)}, u32[]{:S(2)}, u32[]{:S(2)}) collective-permute-start(bf16[128,1024]{1,0:T(8,128)(2,1)S(1)} %collective-permute-done.1.refs_2_), channel_id=1, source_target_pairs={{0,2},{2,0},{1,3},{3,1},{4,6},{6,4},{5,7},{7,5},{8,10},{10,8},{9,1... | collective-permute-start | bytes 786440 | tf_op jit(solution)/shard_map/ppermute | solution.py:357
  20.3 8.0 %copy-start.2 = (s32[4,8]{1,0:T(4,128)S(1)}, s32[4,8]{1,0:T(4,128)}, u32[]{:S(2)}) copy-start(s32[4,8]{1,0:T(4,128)} %adjacency.1) | copy-start | bytes 388
  20.3 8.0 %collective-permute-start.4 = (bf16[384,1024]{1,0:T(8,128)(2,1)S(1)}, bf16[384,1024]{1,0:T(8,128)(2,1)S(1)}, u32[]{:S(2)}, u32[]{:S(2)}) collective-permute-start(bf16[384,1024]{1,0:T(8,128)(2,1)S(1)} %project.2), channel_id=1, source_target_pairs={{0,1},{1,0},{2,3},{3,2},{4,5},{5,4},{6,7},{7,6},{8,9},{9,8},{10,11... | collective-permute-start | bytes 2359304 | tf_op jit(solution)/shard_map/ppermute | solution.py:357
  26.7 5.5 %copy-start.3 = (s32[4,1]{0,1:T(1,128)S(1)}, s32[4,1]{0,1:T(1,128)}, u32[]{:S(2)}) copy-start(s32[4,1]{0,1:T(1,128)} %param.12) | copy-start | bytes 52
  26.7 13.6 %copy-start = (bf16[4,64,512]{2,1,0:T(8,128)(2,1)S(1)}, bf16[4,64,512]{2,1,0:T(8,128)(2,1)}, u32[]{:S(2)}) copy-start(bf16[4,64,512]{2,1,0:T(8,128)(2,1)} %grid_features.1) | copy-start | bytes 786436
  26.7 1.6 %collective-permute-start.5 = (bf16[128,1024]{1,0:T(8,128)(2,1)S(1)}, bf16[128,1024]{1,0:T(8,128)(2,1)S(1)}, u32[]{:S(2)}, u32[]{:S(2)}) collective-permute-start(bf16[128,1024]{1,0:T(8,128)(2,1)S(1)} %project.3), channel_id=1, source_target_pairs={{0,1},{1,0},{2,3},{3,2},{4,5},{5,4},{6,7},{7,6},{8,9},{9,8},{10,11... | collective-permute-start | bytes 786440 | tf_op jit(solution)/shard_map/ppermute | solution.py:357
  31.8 8.4 %collective-permute-start.6 = (bf16[256,512]{1,0:T(8,128)(2,1)S(1)}, bf16[256,512]{1,0:T(8,128)(2,1)S(1)}, u32[]{:S(2)}, u32[]{:S(2)}) collective-permute-start(bf16[256,512]{1,0:T(8,128)(2,1)S(1)} %get-tuple-element.22), channel_id=1, source_target_pairs={{0,2},{2,0},{1,3},{3,1},{4,6},{6,4},{5,7},{7,5},{8,10},{10,8},{9,1... | collective-permute-start | bytes 786440 | tf_op jit(solution)/shard_map/ppermute | solution.py:357
  41.0 5.1 %collective-permute-start.7 = (bf16[2,64,512]{2,1,0:T(8,128)(2,1)S(1)}, bf16[2,64,512]{2,1,0:T(8,128)(2,1)S(1)}, u32[]{:S(2)}, u32[]{:S(2)}) collective-permute-start(bf16[2,64,512]{2,1,0:T(8,128)(2,1)S(1)} %get-tuple-element.24), channel_id=1, source_target_pairs={{0,4},{4,0},{8,12},{12,8},{1,5},{5,1},{9,13},{13,9},{2,6},{6,2},{1... | collective-permute-start | bytes 393224 | tf_op jit(solution)/shard_map/ppermute | solution.py:348
  42.9 13.0 %collective-permute-start.8 = (bf16[2,64,512]{2,1,0:T(8,128)(2,1)S(1)}, bf16[2,64,512]{2,1,0:T(8,128)(2,1)S(1)}, u32[]{:S(2)}, u32[]{:S(2)}) collective-permute-start(bf16[2,64,512]{2,1,0:T(8,128)(2,1)S(1)} %get-tuple-element.25), channel_id=1, source_target_pairs={{0,8},{4,12},{8,0},{12,4},{1,9},{5,13},{9,1},{13,5},{2,10},{6,14},... | collective-permute-start | bytes 393224 | tf_op jit(solution)/shard_map/ppermute | solution.py:348
  46.1 9.7 %collective-permute-start.9 = (bf16[2,64,512]{2,1,0:T(8,128)(2,1)S(1)}, bf16[2,64,512]{2,1,0:T(8,128)(2,1)S(1)}, u32[]{:S(2)}, u32[]{:S(2)}) collective-permute-start(bf16[2,64,512]{2,1,0:T(8,128)(2,1)S(1)} %get-tuple-element.26), channel_id=1, source_target_pairs={{0,12},{4,8},{8,4},{12,0},{1,13},{5,9},{9,5},{13,1},{2,14},{6,10},... | collective-permute-start | bytes 393224 | tf_op jit(solution)/shard_map/ppermute | solution.py:348

commit v4 on v0

--- a/solution.py
+++ b/solution.py
@@ -3,17 +3,395 @@
 import jax
 import jax.numpy as jnp
 from jax import lax
+from jax.experimental import pallas as pl
+from jax.experimental.pallas import tpu as pltpu
 from jax.sharding import PartitionSpec as P
 
 D = 1024
 HEAD_DIM = 64
 CAP = 2
+BLOCK = 64
+QUAD = 4
+WIDE = QUAD * HEAD_DIM
+CHUNKS = 2
+ROWS = BLOCK // CHUNKS
+MIB = 1 << 20
 
 
 epsilon = 1e-05
 
 
-def attend(queries, key_table, value_table, chosen, scaling):
+def dot(a, b):
+    return jnp.dot(a, b, preferred_element_type=jnp.float32)
+
+
+def gelu(x):
+    return 0.5 * x * (1.0 + lax.erf(x * (2.0**-0.5)))
+
+
+def in_vmem(x):
+    return pltpu.with_memory_space_constraint(x, pltpu.VMEM)
+
+
+def in_hbm(x):
+    return pltpu.with_memory_space_constraint(x, pltpu.HBM)
+
+
+def whole(space):
+    return pl.BlockSpec(memory_space=space)
+
+
+def vmem(count):
+    return [whole(pltpu.VMEM)] * count
+
+
+def params(mib):
+    return pltpu.CompilerParams(vmem_limit_bytes=mib * MIB)
+
+
+def halves(width):
+    h = lax.axis_index("head")
+    mine = pl.ds(pl.multiple_of(h * width, width), width)
+    theirs = pl.ds(pl.multiple_of((1 - h) * width, width), width)
+    return mine, theirs
+
+
+def mlp_kernel(own, other, gain, wq, wup, wdn, q_out, mlp_out, normed_s):
+    half = own.shape[1]
+    units = wup.shape[1]
+    chunk = units // 4
+    mine, theirs = halves(half)
+    x_own = own[...].astype(jnp.float32)
+    x_other = other[...].astype(jnp.float32)
+
+    def mean(a, b):
+        total = jnp.sum(a, axis=-1, keepdims=True) + jnp.sum(b, axis=-1, keepdims=True)
+        return total * (0.5 / half)
+
+    average = mean(x_own, x_other)
+    x_own = x_own - average
+    x_other = x_other - average
+    factor = lax.rsqrt(mean(x_own * x_own, x_other * x_other) + epsilon)
+    normed_s[:, mine] = (x_own * factor * gain[:, mine]).astype(jnp.bfloat16)
+    normed_s[:, theirs] = (x_other * factor * gain[:, theirs]).astype(jnp.bfloat16)
+    normed = normed_s[...]
+    q_out[...] = dot(normed, wq[...]).astype(jnp.bfloat16)
+    for c in range(units // chunk):
+        span = slice(c * chunk, (c + 1) * chunk)
+        hidden = gelu(dot(normed, wup[:, span])).astype(jnp.bfloat16)
+        term = dot(hidden, wdn[span, :])
+        if c == 0:
+            mlp_out[...] = term
+        else:
+            mlp_out[...] += term
+
+
+def run_mlp(own, other, gain, wq, wup, wdn):
+    rows = own.shape[0]
+    width = wq.shape[0]
+    units = wup.shape[1]
+    return pl.pallas_call(
+        mlp_kernel,
+        out_shape=(
+            jax.ShapeDtypeStruct((rows, wq.shape[1]), jnp.bfloat16),
+            jax.ShapeDtypeStruct((rows, width), jnp.float32),
+        ),
+        in_specs=vmem(6),
+        out_specs=tuple(vmem(2)),
+        scratch_shapes=[pltpu.VMEM((rows, width), jnp.bfloat16)],
+        compiler_params=params(16),
+        cost_estimate=pl.CostEstimate(
+            flops=2 * rows * width * (wq.shape[1] + 2 * units),
+            bytes_accessed=2 * width * (wq.shape[1] + 2 * units),
+            transcendentals=rows * units,
+        ),
+        name="mlp",
+    )(own, other, gain, wq, wup, wdn)
+
+
+def stage_kernel(*refs):
+    sources, copies_to, sem = refs[: len(refs) // 2], refs[len(refs) // 2 : -1], refs[-1]
+    copies = []
+    for i, (source, target) in enumerate(zip(sources, copies_to)):
+        copies.append(pltpu.make_async_copy(source, target, sem.at[i]))
+        copies[i].start()
+    for copy in copies:
+        copy.wait()
+
+
+def run_stage(*arrays):
+    size = sum(2 * array.size for array in arrays)
+    return pl.pallas_call(
+        stage_kernel,
+        out_shape=tuple(jax.ShapeDtypeStruct(array.shape, array.dtype) for array in arrays),
+        in_specs=[whole(pltpu.HBM)] * len(arrays),
+        out_specs=tuple(vmem(len(arrays))),
+        scratch_shapes=[pltpu.SemaphoreType.DMA((len(arrays),))],
+        compiler_params=params(16),
+        cost_estimate=pl.CostEstimate(flops=0, bytes_accessed=20 * size, transcendentals=0),
+        name="stage",
+    )(*(in_hbm(array) for array in arrays))
+
+
+def project_kernel(*refs):
+    pieces, (wk, wv, out) = refs[:-3], refs[-3:]
+    width = wk.shape[1]
+    rows = jnp.concatenate([piece[...] for piece in pieces], axis=0)
+    out[:, :width] = dot(rows, wk[...]).astype(jnp.bfloat16)
+    out[:, width:] = dot(rows, wv[...]).astype(jnp.bfloat16)
+
+
+def run_project(pieces, wk, wv):
+    rows = sum(piece.shape[0] for piece in pieces)
+    depth, width = wk.shape
+    return pl.pallas_call(
+        project_kernel,
+        out_shape=jax.ShapeDtypeStruct((rows, 2 * width), jnp.bfloat16),
+        in_specs=vmem(len(pieces) + 2),
+        out_specs=whole(pltpu.VMEM),
+        compiler_params=params(8),
+        cost_estimate=pl.CostEstimate(
+            flops=80 * rows * depth * width,
+            bytes_accessed=80 * depth * width + 80 * rows * depth,
+            transcendentals=0,
+        ),
+        name="project",
+    )(*pieces, in_vmem(wk), in_vmem(wv))
+
+
+def attend_rows(c, adjacency, q, table, mlp, wo, send, keep, att_s):
+    s = lax.axis_index("shard")
+    h = lax.axis_index("head")
+    u = lax.axis_index("sub")
+    half = wo.shape[0]
+    per_core = table.shape[0] // 2
+    mine, theirs = halves(half)
+    rows = slice(c * ROWS, (c + 1) * ROWS)
+    rows_of = lax.broadcasted_iota(jnp.int32, (QUAD * ROWS, WIDE), 0) // ROWS
+    lanes_of = lax.broadcasted_iota(jnp.int32, (QUAD * ROWS, WIDE), 1) // HEAD_DIM
+    diagonal = rows_of == lanes_of
+    lane_head = lax.broadcasted_iota(jnp.int32, (ROWS, WIDE), 1) // HEAD_DIM
+    scale = HEAD_DIM**-0.5 * math.log2(math.e)
+    count = adjacency.shape[0]
+    for b in range(count):
+        places = []
+        for j in range(adjacency.shape[1]):
+            m = adjacency[b, j]
+            part = lax.rem(m, 2)
+            core = lax.rem(m // 2, 2)
+            distance = s ^ (m // 4)
+            distance = jnp.where(distance <= 1, distance, 2 + ((distance - 2) ^ h))
+            places.append((core ^ u) * per_core + distance * 2 + part)
+        for g in range(half // WIDE):
+            columns = slice(g * WIDE, (g + 1) * WIDE)
+            keys = jnp.concatenate([table[p, :, columns] for p in places], axis=0)
+            vcolumns = slice(half + g * WIDE, half + (g + 1) * WIDE)
+            values = jnp.concatenate([table[p, :, vcolumns] for p in places], axis=0)
+            stacked = jnp.concatenate([q[b, rows, columns]] * QUAD, axis=0)
+            stacked = jnp.where(diagonal, stacked, jnp.zeros_like(stacked))
+            scores = lax.dot_general(
+                stacked, keys, (((1,), (1,)), ((), ())), preferred_element_type=jnp.float32
+            )
+            highest = jnp.max(scores, axis=-1, keepdims=True)
+            weights = jnp.exp2((scores - highest) * scale)
+            total = jnp.sum(weights, axis=-1, keepdims=True)
+            probs = (weights * (1.0 / total)).astype(jnp.bfloat16)
+            mixed = dot(probs, values)
+            merged = mixed[0:ROWS, :]
+            for i in range(1, QUAD):
+                merged = jnp.where(lane_head == i, mixed[i * ROWS : (i + 1) * ROWS, :], merged)
+            att_s[b * ROWS : (b + 1) * ROWS, columns] = merged.astype(jnp.bfloat16)
+    for out, span in ((send, theirs), (keep, mine)):
+        extra = mlp[:, rows, span].reshape(count * ROWS, half)
+        out[...] = (extra + dot(att_s[...], wo[:, span])).astype(jnp.bfloat16)
+
+
+def first_kernel(
+    adjacency, q, mine_a, mine_b, sibling_a, sibling_b, mlp, wo, send, keep, table, att_s, sem
+):
+    copies = []
+    first = 0
+    for i, part in enumerate((mine_a, mine_b, sibling_a, sibling_b)):
+        blocks = part.shape[0]
+        copies.append(pltpu.make_async_copy(part, table.at[pl.ds(first, blocks)], sem.at[i]))
+        copies[i].start()
+        first += blocks
+    for copy in copies:
+        copy.wait()
+    attend_rows(0, adjacency, q, table, mlp, wo, send, keep, att_s)
+
+
+def later_kernel(c):
+    def kernel(adjacency, q, table, mlp, wo, send, keep, att_s):
+        attend_rows(c, adjacency, q, table, mlp, wo, send, keep, att_s)
+
+    return kernel
+
+
+def run_attend(c, adjacency, q, tables, mlp, wo):
+    count, _, half = q.shape
+    rows = count * ROWS
+    part = jax.ShapeDtypeStruct((rows, half), jnp.bfloat16)
+    blocks = sum(table.shape[0] for table in tables)
+    shared = jax.ShapeDtypeStruct((blocks,) + tables[0].shape[1:], jnp.bfloat16)
+    outs = (part, part, shared) if c == 0 else (part, part)
+    scratch = [pltpu.VMEM((rows, half), jnp.bfloat16)]
+    return pl.pallas_call(
+        first_kernel if c == 0 else later_kernel(c),
+        out_shape=outs,
+        in_specs=[whole(pltpu.SMEM)] + vmem(len(tables) + 3),
+        out_specs=tuple(vmem(len(outs))),
+        scratch_shapes=scratch + [pltpu.SemaphoreType.DMA((len(tables),))] * (c == 0),
+        compiler_params=params(16),
+        cost_estimate=pl.CostEstimate(
+            flops=20 * rows * half * (D + 8 * 8 * BLOCK),
+            bytes_accessed=40 * blocks * BLOCK * half + 20 * half * D + 40 * rows * D,
+            transcendentals=rows * 8 * BLOCK * half // HEAD_DIM,
+        ),
+        name="attend",
+    )(adjacency, q, *tables, mlp, in_vmem(wo))
+
+
+def combine_kernel(c):
+    def kernel(owners, grid_features, keep, received, *outs):
+        s = lax.axis_index("shard")
+        shards = len(outs)
+        count = grid_features.shape[0]
+        names = [owners[t, 0] for t in range(count)]
+        for d in range(shards):
+            target = s ^ d
+            for j in range(CAP):
+                outs[d][j] = jnp.zeros(outs[d].shape[1:], jnp.bfloat16)
+            seen = jnp.int32(0)
+            for t in range(count):
+                hit = names[t] == target
+                rank = seen
+
+                @pl.when(hit)
+                def _():
+                    rows = slice(t * ROWS, (t + 1) * ROWS)
+                    partials = keep[rows, :].astype(jnp.float32)
+                    partials = partials + received[rows, :].astype(jnp.float32)
+                    residual = grid_features[t, c * ROWS : (c + 1) * ROWS, :]
+                    updated = residual.astype(jnp.float32) + partials
+                    outs[d][rank] = updated.astype(jnp.bfloat16)
+
+                seen = seen + hit.astype(jnp.int32)
+
+    return kernel
+
+
+def run_combine(c, owners, grid_features, keep, received, shards):
+    count, _, half = grid_features.shape
+    slot = jax.ShapeDtypeStruct((CAP, ROWS, half), jnp.bfloat16)
+    return pl.pallas_call(
+        combine_kernel(c),
+        out_shape=(slot,) * shards,
+        in_specs=[whole(pltpu.SMEM)] + vmem(3),
+        out_specs=tuple(vmem(shards)),
+        compiler_params=params(8),
+        cost_estimate=pl.CostEstimate(
+            flops=3000 * count * ROWS * half,
+            bytes_accessed=400 * ROWS * half * (3 * count + CAP * shards),
+            transcendentals=0,
+        ),
+        name="combine",
+    )(owners, grid_features, keep, received)
+
+
+def place_kernel(c, shards):
+    def kernel(*refs):
+        arrived, (out, sem) = refs[:shards], refs[-2:]
+        s = lax.axis_index("shard")
+        rows = pl.ds(c * ROWS, ROWS)
+        copies = []
+        for d in range(shards):
+            slots = pl.ds((s ^ d) * CAP, CAP)
+            copies.append(pltpu.make_async_copy(arrived[d], out.at[slots, rows, :], sem.at[d]))
+            copies[d].start()
+        for copy in copies:
+            copy.wait()
+
+    return kernel
+
+
+def run_place(c, arrived, placed):
+    shards = len(arrived)
+    half = arrived[0].shape[2]
+    size = 2 * CAP * shards * ROWS * half
+    return pl.pallas_call(
+        place_kernel(c, shards),
+        out_shape=jax.ShapeDtypeStruct((shards * CAP, BLOCK, half), jnp.bfloat16),
+        in_specs=vmem(shards) + [whole(pltpu.HBM)] * len(placed),
+        out_specs=whole(pltpu.HBM),
+        scratch_shapes=[pltpu.SemaphoreType.DMA((shards,))],
+        input_output_aliases={shards: 0} if placed else {},
+        compiler_params=params(4),
+        cost_estimate=pl.CostEstimate(flops=0, bytes_accessed=20 * size, transcendentals=0),
+        name="place",
+    )(*arrived, *placed)
+
+
+def crossed(x, distance, size):
+    return lax.ppermute(x, "shard", [(i, i ^ distance) for i in range(size)])
+
+
+def fetched(x, size):
+    pairs = [(2 * i + h, 2 * (i ^ (2 + h)) + h) for i in range(size) for h in range(2)]
+    return lax.ppermute(x, ("shard", "head"), pairs)
+
+
+def swapped(x, axis):
+    return lax.ppermute(x, axis, [(0, 1), (1, 0)])
+
+
+def paired(
+    grid_features,
+    owners,
+    adjacency,
+    mesh_nodes,
+    norm_gain,
+    query_weight,
+    key_weight,
+    value_weight,
+    output_weight,
+    up_weight,
+    down_weight,
+):
+    shards = lax.axis_size("shard")
+    count, rows, half = grid_features.shape
+    flat = grid_features.reshape(count * rows, half)
+    far = fetched(mesh_nodes, shards)
+    near = crossed(mesh_nodes, 1, shards)
+    other = swapped(flat, "head")
+    staged = run_stage(flat, norm_gain.reshape(1, -1), query_weight, up_weight, down_weight)
+    queries, mlp = run_mlp(staged[0], other, *staged[1:])
+    queries, mlp, far = lax.optimization_barrier((queries, mlp, far))
+    farther = swapped(far, "head")
+    mine_a = run_project((mesh_nodes, near, far), key_weight, value_weight)
+    sibling_a = swapped(mine_a, "sub")
+    mine_b = run_project((farther,), key_weight, value_weight)
+    sibling_b = swapped(mine_b, "sub")
+    tables = [
+        table.reshape(-1, BLOCK, 2 * half) for table in (mine_a, mine_b, sibling_a, sibling_b)
+    ]
+    queries = queries.reshape(count, rows, half)
+    mlp = mlp.reshape(count, rows, 2 * half)
+    placed = []
+    slots = None
+    for c in range(CHUNKS):
+        send, keep, *table = run_attend(c, adjacency, queries, tables, mlp, output_weight)
+        tables = table or tables
+        received = swapped(send, "head")
+        if slots is not None:
+            received, _ = lax.optimization_barrier((received, slots[0]))
+        slots = run_combine(c, owners, grid_features, keep, received, shards)
+        arrived = [slots[0]] + [crossed(slots[d], d, shards) for d in range(1, shards)]
+        placed = [run_place(c, arrived, placed)]
+    return placed[0]
+
+
+def attend_plain(queries, key_table, value_table, chosen, scaling):
     count = chosen.shape[0]
     picked_keys = key_table[chosen]
     picked_keys = picked_keys.reshape(count, -1, picked_keys.shape[3], picked_keys.shape[4])
@@ -32,7 +410,7 @@
     return result.astype(jnp.bfloat16)
 
 
-def local(
+def general(
     grid_features,
     owners,
     adjacency,
@@ -103,7 +481,7 @@
     queries = queries.reshape(steps_count, blocks_each, block_rows, head_local, HEAD_DIM)
 
     def attend_step(operands):
-        return attend(operands[0], key_table, value_table, operands[1], HEAD_DIM ** (-0.5))
+        return attend_plain(operands[0], key_table, value_table, operands[1], HEAD_DIM ** (-0.5))
 
     attended = lax.map(
         attend_step, (queries, jnp.maximum(lists, 0).reshape(steps_count, blocks_each, -1))
@@ -121,6 +499,14 @@
     occupied = lists[:, 0] >= 0
     summed = residual.astype(jnp.float32) + reduced
     return jnp.where(occupied[:, None, None], summed, 0.0).astype(jnp.bfloat16)
+
+
+def local(grid_features, owners, adjacency, mesh_nodes, *parameters):
+    sizes = [lax.axis_size(axis) for axis in ("shard", "head", "sub")]
+    small = grid_features.shape[:2] == (4, BLOCK) and mesh_nodes.shape[0] == 2 * BLOCK
+    if sizes == [4, 2, 2] and small:
+        return paired(grid_features, owners, adjacency, mesh_nodes, *parameters)
+    return general(grid_features, owners, adjacency, mesh_nodes, *parameters)
 
 
 def solution(mesh):

time: 170 us -> 55.7 us (0.33)
  waiting for transfers between devices: 57.2 us -> 16 us
  matrix products: 41 us -> 0 us
  local copies, waits for them, and re-layouts: 28.2 us -> 0.13 us
  Pallas kernels: 0 us -> 20.2 us
  between operations: 13.5 us -> 0.17 us
  other arithmetic: 9.74 us -> 0 us
  blocking collectives: 8.44 us -> 0 us
  starting transfers between devices: 11.3 us -> 19.1 us
    dot_general x8 -> x0, matrix products: 41 us -> none  [the longest x1 16.7 us: local(): jnp.dot(hidden, down_weight, preferred_element_type=jnp.float32)]
    all_to_all x2 -> x0, waiting for transfers between devices: 36.2 us -> none  [the longest x1 36.1 us: local(): lax.all_to_all(outgoing.reshape(shard_count, CAP, block_rows, D), 'shard'...]
    reduce_scatter x1 -> x0, waiting for transfers between devices: 21.1 us -> none  [local(): lax.psum_scatter(branch.astype(jnp.bfloat16), 'head', scatter_dimension=2...]
    pallas_call x0 -> x10, Pallas kernels: none -> 20.2 us  [the longest x2 8.59 us: run_attend(): pl.pallas_call(first_kernel if c == 0 else later_kernel(c), out_shape=out...]
    ppermute x0 -> x14, starting transfers between devices: none -> 19.1 us  [the longest x7 11.3 us: crossed(): return lax.ppermute(x, 'shard', [(i, i ^ distance) for i in range(size)])]
    ppermute x0 -> x14, waiting for transfers between devices: none -> 16 us  [the longest x6 7.34 us: swapped(): return lax.ppermute(x, axis, [(0, 1), (1, 0)])]
    all_to_all x2 -> x0, starting transfers between devices: 11.3 us -> none  [the longest x1 6.32 us: local(): lax.all_to_all(send_lists, 'shard', split_axis=0, concat_axis=0, tiled=True)]
    gather x2 -> x0, local copies, waits for them, and re-layouts: 10.7 us -> none  [the longest x1 5.36 us: attend(): picked_keys = key_table[chosen]]
  transfers between devices with their start and end apart: 4 -> 14, of which waited for: 2 -> 7; matrix products, arithmetic and copies ran while one was open for 17% -> 0% of each run, Pallas kernels for 0% -> 27%
where the time goes in v4:
time: 55.7 us; the launch traced here: 55.5 us
  Pallas kernels  20.2 us (36%)
  starting transfers between devices  19.1 us (34%)
  waiting for transfers between devices  16 us (29%)
    ppermute x7, starting transfers between devices, crossed(): return lax.ppermute(x, 'shard', [(i, i ^ distance) for i in range(size)])  11.3 us
    pallas_call x2, Pallas kernels, run_attend(): pl.pallas_call(first_kernel if c == 0 else later_kernel(c), out_shape=out...  8.59 us
    ppermute x6, waiting for transfers between devices, swapped(): return lax.ppermute(x, axis, [(0, 1), (1, 0)])  7.34 us
    ppermute x7, waiting for transfers between devices, crossed(): return lax.ppermute(x, 'shard', [(i, i ^ distance) for i in range(size)])  5.57 us
    ppermute x6, starting transfers between devices, swapped(): return lax.ppermute(x, axis, [(0, 1), (1, 0)])  5.22 us
    pallas_call x1, Pallas kernels, run_stage(): pl.pallas_call(stage_kernel, out_shape=tuple((jax.ShapeDtypeStruct(array....  3.9 us
    pallas_call x1, Pallas kernels, run_mlp(): pl.pallas_call(mlp_kernel, out_shape=(jax.ShapeDtypeStruct((rows, wq.shap...  3.4 us
    ppermute x1, waiting for transfers between devices, fetched(): return lax.ppermute(x, ('shard', 'head'), pairs)  3.08 us
  transfers between devices with their start and end apart: 14, of which 7 were waited for; matrix products, arithmetic and copies ran while one was open for 0% of the time, Pallas kernels for 27%

profile of v4, /device:TPU:0, one launch (start us, length us, event | category | flops | bytes accessed | tf_op | source)
XLA Modules:
  0.0 55.5 jit_solution(4937079392803946702)
XLA Ops:
  0.0 2.9 %collective-permute-start = (bf16[256,512]{1,0:T(8,128)(2,1)}, bf16[256,512]{1,0:T(8,128)(2,1)S(1)}, u32[]{:S(2)}, u32[]{:S(2)}) collective-permute-start(bf16[256,512]{1,0:T(8,128)(2,1)} %bitcast.8), channel_id=1, source_target_pairs={{0,2},{2,0},{1,3},{3,1},{4,6},{6,4},{5,7},{7,5},{8,10},{10,8},{9,1... | collective-permute-start | bytes 786440 | tf_op jit(solution)/shard_map/ppermute | solution.py:345
  2.9 2.6 %collective-permute-start.1 = (bf16[128,1024]{1,0:T(8,128)(2,1)}, bf16[128,1024]{1,0:T(8,128)(2,1)S(1)}, u32[]{:S(2)}, u32[]{:S(2)}) collective-permute-start(bf16[128,1024]{1,0:T(8,128)(2,1)} %refs_0_.1), channel_id=1, source_target_pairs={{0,8},{2,14},{4,12},{6,10},{8,0},{10,6},{12,4},{14,2},{1,9},{3,15}... | collective-permute-start | bytes 786440 | tf_op jit(solution)/shard_map/ppermute | solution.py:341
  5.5 1.6 %collective-permute-start.2 = (bf16[128,1024]{1,0:T(8,128)(2,1)}, bf16[128,1024]{1,0:T(8,128)(2,1)S(1)}, u32[]{:S(2)}, u32[]{:S(2)}) collective-permute-start(bf16[128,1024]{1,0:T(8,128)(2,1)} %refs_0_.1), channel_id=1, source_target_pairs={{0,4},{4,0},{8,12},{12,8},{1,5},{5,1},{9,13},{13,9},{2,6},{6,2},{1... | collective-permute-start | bytes 786440 | tf_op jit(solution)/shard_map/ppermute | solution.py:336
  7.1 3.9 %stage.1 = (bf16[256,512]{1,0:T(8,128)(2,1)S(1)}, f32[1,1024]{1,0:T(1,128)S(1)}, bf16[1024,512]{1,0:T(8,128)(2,1)S(1)}, bf16[1024,2048]{1,0:T(8,128)(2,1)S(1)}, bf16[2048,1024]{1,0:T(8,128)(2,1)S(1)}) custom-call(bf16[256,512]{1,0:T(8,128)(2,1)} %bitcast.9, f32[1,1024]{1,0:T(1,128)} %bitcast.18, bf16[1024,512]{1,0:T(8,128)(2,1)} %refs_2_.2, ...), custom_call_target="tpu_custom_call" | custom-call | bytes 194027520 | tf_op jit(solution)/shard_map/stage/pallas_call | solution.py:124
  11.0 0.0 collective-permute-done.other
  11.0 0.0 copy-start.1
  11.0 0.0 copy-start.2
  11.0 0.0 copy-start.4
  11.1 3.4 %mlp.1 = (bf16[256,512]{1,0:T(8,128)(2,1)S(1)}, f32[256,1024]{1,0:T(8,128)S(1)}) custom-call(bf16[256,512]{1,0:T(8,128)(2,1)S(1)} %get-tuple-element.29.own, bf16[256,512]{1,0:T(8,128)(2,1)S(1)} %collective-permute-done.other, f32[1,1024]{1,0:T(1,128)S(1)} %get-tuple-element.30.gain, bf16[1024,512]{1,0:T(8,128)(2,1)S(1)} %get-tuple-element.31.wq, ...), custom_call_target="tpu_custom_call" | custom-call | flops 2415919104 | bytes 9437184 | tf_op jit(solution)/shard_map/mlp/pallas_call | solution.py:93
  14.5 3.1 %collective-permute-done.1.refs_2_ = bf16[128,1024]{1,0:T(8,128)(2,1)S(1)} collective-permute-done((bf16[128,1024]{1,0:T(8,128)(2,1)}, bf16[128,1024]{1,0:T(8,128)(2,1)S(1)}, u32[]{:S(2)}, u32[]{:S(2)}) %collective-permute-start.1) | collective-permute-done | bytes 262176 | tf_op jit(solution)/shard_map/ppermute | solution.py:341
  17.5 0.0 collective-permute-start.3
  17.5 0.2 collective-permute-done.2.refs_1_
  17.7 0.0 copy-done.1
  17.7 0.0 copy-done.2
  17.7 0.0 copy-done.4
  17.7 1.0 %project.2 = bf16[384,1024]{1,0:T(8,128)(2,1)S(1)} custom-call(bf16[128,1024]{1,0:T(8,128)(2,1)S(1)} %copy-done.4, bf16[128,1024]{1,0:T(8,128)(2,1)S(1)} %collective-permute-done.2.refs_1_, bf16[128,1024]{1,0:T(8,128)(2,1)S(1)} %collective-permute-done.1.refs_2_, bf16[1024,512]{1,0:T(8,128)(2,1)S(1)} %copy-done.1, bf16[1024,512]{1,0:T(8,128)(2,1)S(1)} %copy-done.2), custom_call_target="tpu_custom_call" | custom-call | flops 16106127360 | bytes 73400320 | tf_op jit(solution)/shard_map/project/pallas_call | solution.py:147
  18.7 0.0 copy-start.3
  18.7 0.0 copy-start.5
  18.8 0.1 collective-permute-start.4
  18.8 5.8 %collective-permute-done.3.refs_0_ = bf16[128,1024]{1,0:T(8,128)(2,1)S(1)} collective-permute-done((bf16[128,1024]{1,0:T(8,128)(2,1)S(1)}, bf16[128,1024]{1,0:T(8,128)(2,1)S(1)}, u32[]{:S(2)}, u32[]{:S(2)}) %collective-permute-start.3) | collective-permute-done | bytes 262176 | tf_op jit(solution)/shard_map/ppermute | solution.py:345
  24.6 0.4 project.3
  25.1 0.1 collective-permute-start.5
  25.2 1.5 %collective-permute-done.5 = bf16[128,1024]{1,0:T(8,128)(2,1)S(1)} collective-permute-done((bf16[128,1024]{1,0:T(8,128)(2,1)S(1)}, bf16[128,1024]{1,0:T(8,128)(2,1)S(1)}, u32[]{:S(2)}, u32[]{:S(2)}) %collective-permute-start.5) | collective-permute-done | bytes 262176 | tf_op jit(solution)/shard_map/ppermute | solution.py:345
  26.7 0.0 collective-permute-done.4
  26.7 0.0 copy-done.3
  26.7 0.0 copy-done.5
  26.7 4.4 %attend.2 = (bf16[128,512]{1,0:T(8,128)(2,1)S(1)}, bf16[128,512]{1,0:T(8,128)(2,1)S(1)}, bf16[16,64,1024]{2,1,0:T(8,128)(2,1)S(1)}) custom-call(s32[4,8]{1,0:T(4,128)S(1)} %copy-done.5, bf16[4,64,512]{2,1,0:T(8,128)(2,1)S(1)} %bitcast.14, bf16[6,64,1024]{2,1,0:T(8,128)(2,1)S(1)} %bitcast.12, bf16[2,64,1024]{2,1,0:T(8,128)(2,1)S(1)} %bitcast.16, ...), custom_call_target="tpu_custom_call" | custom-call | flops 6710886400 | bytes 36700160 | tf_op jit(solution)/shard_map/attend/pallas_call | solution.py:239
  31.1 0.3 collective-permute-start.7
  31.4 0.0 copy-start.6
  31.4 0.0 copy-start
  31.4 4.2 %attend.3 = (bf16[128,512]{1,0:T(8,128)(2,1)S(1)}, bf16[128,512]{1,0:T(8,128)(2,1)S(1)}) custom-call(s32[4,8]{1,0:T(4,128)S(1)} %copy-done.5, bf16[4,64,512]{2,1,0:T(8,128)(2,1)S(1)} %bitcast.15, bf16[16,64,1024]{2,1,0:T(8,128)(2,1)S(1)} %get-tuple-element.39.table, f32[4,64,1024]{2,1,0:T(8,128)S(1)} %bitcast.11, bf16[512,1024]{1,0:T(8,128)(2,1)S(1)} %copy-done.3), custom_call_target="tpu_custom_call" | custom-call | flops 6710886400 | bytes 36700160 | tf_op jit(solution)/shard_map/attend/pallas_call | solution.py:239
  35.6 1.8 %collective-permute-start.6 = (bf16[128,512]{1,0:T(8,128)(2,1)S(1)}, bf16[128,512]{1,0:T(8,128)(2,1)S(1)}, u32[]{:S(2)}, u32[]{:S(2)}) collective-permute-start(bf16[128,512]{1,0:T(8,128)(2,1)S(1)} %get-tuple-element.41), channel_id=1, source_target_pairs={{0,2},{2,0},{1,3},{3,1},{4,6},{6,4},{5,7},{7,5},{8,10},{10,8},{9,1... | collective-permute-start | bytes 393224 | tf_op jit(solution)/shard_map/ppermute | solution.py:345
  37.4 0.0 copy-done.6
  37.4 0.1 copy.14.owners
  37.5 0.0 collective-permute-done.7.received
  37.5 0.0 copy-done
  37.5 0.7 %combine.2 = (bf16[2,32,512]{2,1,0:T(8,128)(2,1)S(1)}, bf16[2,32,512]{2,1,0:T(8,128)(2,1)S(1)}, bf16[2,32,512]{2,1,0:T(8,128)(2,1)S(1)}, bf16[2,32,512]{2,1,0:T(8,128)(2,1)S(1)}) custom-call(s32[4,1]{1,0:T(4,128)S(1)} %copy.14.owners, bf16[4,64,512]{2,1,0:T(8,128)(2,1)S(1)} %copy-done, bf16[128,512]{1,0:T(8,128)(2,1)S(1)} %get-tuple-element.42.keep, ...), custom_call_target="tpu_custom_call" | custom-call | flops 196608000 | bytes 131072000 | tf_op jit(solution)/shard_map/combine/pallas_call | solution.py:287
  38.3 1.9 %collective-permute-start.11 = (bf16[2,32,512]{2,1,0:T(8,128)(2,1)S(1)}, bf16[2,32,512]{2,1,0:T(8,128)(2,1)S(1)}, u32[]{:S(2)}, u32[]{:S(2)}) collective-permute-start(bf16[2,32,512]{2,1,0:T(8,128)(2,1)S(1)} %get-tuple-element.50), channel_id=1, source_target_pairs={{0,4},{4,0},{8,12},{12,8},{1,5},{5,1},{9,13},{13,9},{2,6},{6,2},{1... | collective-permute-start | bytes 196616 | tf_op jit(solution)/shard_map/ppermute | solution.py:336
  40.1 3.3 %collective-permute-start.12 = (bf16[2,32,512]{2,1,0:T(8,128)(2,1)S(1)}, bf16[2,32,512]{2,1,0:T(8,128)(2,1)S(1)}, u32[]{:S(2)}, u32[]{:S(2)}) collective-permute-start(bf16[2,32,512]{2,1,0:T(8,128)(2,1)S(1)} %get-tuple-element.51), channel_id=1, source_target_pairs={{0,8},{4,12},{8,0},{12,4},{1,9},{5,13},{9,1},{13,5},{2,10},{6,14},... | collective-permute-start | bytes 196616 | tf_op jit(solution)/shard_map/ppermute | solution.py:336
  43.4 0.0 collective-permute-start.13
  43.4 0.0 collective-permute-done.6.received
  43.4 0.7 %combine.3 = (bf16[2,32,512]{2,1,0:T(8,128)(2,1)S(1)}, bf16[2,32,512]{2,1,0:T(8,128)(2,1)S(1)}, bf16[2,32,512]{2,1,0:T(8,128)(2,1)S(1)}, bf16[2,32,512]{2,1,0:T(8,128)(2,1)S(1)}) custom-call(s32[4,1]{1,0:T(4,128)S(1)} %copy.14.owners, bf16[4,64,512]{2,1,0:T(8,128)(2,1)S(1)} %copy-done, bf16[128,512]{1,0:T(8,128)(2,1)S(1)} %get-tuple-element.40.keep, ...), custom_call_target="tpu_custom_call" | custom-call | flops 196608000 | bytes 131072000 | tf_op jit(solution)/shard_map/combine/pallas_call | solution.py:287
  44.1 3.9 %collective-permute-start.10 = (bf16[2,32,512]{2,1,0:T(8,128)(2,1)S(1)}, bf16[2,32,512]{2,1,0:T(8,128)(2,1)S(1)}, u32[]{:S(2)}, u32[]{:S(2)}) collective-permute-start(bf16[2,32,512]{2,1,0:T(8,128)(2,1)S(1)} %get-tuple-element.49), channel_id=1, source_target_pairs={{0,12},{4,8},{8,4},{12,0},{1,13},{5,9},{9,5},{13,1},{2,14},{6,10},... | collective-permute-start | bytes 196616 | tf_op jit(solution)/shard_map/ppermute | solution.py:336
  48.0 0.0 collective-permute-start.8
  48.0 0.0 collective-permute-done.11.refs_1_
  48.0 0.6 %collective-permute-start.9 = (bf16[2,32,512]{2,1,0:T(8,128)(2,1)S(1)}, bf16[2,32,512]{2,1,0:T(8,128)(2,1)S(1)}, u32[]{:S(2)}, u32[]{:S(2)}) collective-permute-start(bf16[2,32,512]{2,1,0:T(8,128)(2,1)S(1)} %get-tuple-element.48), channel_id=1, source_target_pairs={{0,8},{4,12},{8,0},{12,4},{1,9},{5,13},{9,1},{13,5},{2,10},{6,14},... | collective-permute-start | bytes 196616 | tf_op jit(solution)/shard_map/ppermute | solution.py:336
  48.7 0.0 collective-permute-done.12.refs_2_
  48.7 1.2 %collective-permute-done.13.refs_3_ = bf16[2,32,512]{2,1,0:T(8,128)(2,1)S(1)} collective-permute-done((bf16[2,32,512]{2,1,0:T(8,128)(2,1)S(1)}, bf16[2,32,512]{2,1,0:T(8,128)(2,1)S(1)}, u32[]{:S(2)}, u32[]{:S(2)}) %collective-permute-start.13) | collective-permute-done | bytes 65568 | tf_op jit(solution)/shard_map/ppermute | solution.py:336
  49.9 0.7 %place.2.refs_4_ = bf16[8,64,512]{2,1,0:T(8,128)(2,1)} custom-call(bf16[2,32,512]{2,1,0:T(8,128)(2,1)S(1)} %get-tuple-element.44.refs_0_, bf16[2,32,512]{2,1,0:T(8,128)(2,1)S(1)} %collective-permute-done.11.refs_1_, bf16[2,32,512]{2,1,0:T(8,128)(2,1)S(1)} %collective-permute-done.12.refs_2_, bf16[2,32,512]{2,1,0:T(8,128)(2,1)S(1)} %collective-permute-done.13.refs_3_), custom_call_target="tpu_custom_call" | custom-call | bytes 5242880 | tf_op jit(solution)/shard_map/place/pallas_call | solution.py:322
  50.6 0.0 collective-permute-done.10.refs_3_
  50.6 2.0 %collective-permute-done.8.refs_1_ = bf16[2,32,512]{2,1,0:T(8,128)(2,1)S(1)} collective-permute-done((bf16[2,32,512]{2,1,0:T(8,128)(2,1)S(1)}, bf16[2,32,512]{2,1,0:T(8,128)(2,1)S(1)}, u32[]{:S(2)}, u32[]{:S(2)}) %collective-permute-start.8) | collective-permute-done | bytes 65568 | tf_op jit(solution)/shard_map/ppermute | solution.py:336
  52.6 2.2 %collective-permute-done.9.refs_2_ = bf16[2,32,512]{2,1,0:T(8,128)(2,1)S(1)} collective-permute-done((bf16[2,32,512]{2,1,0:T(8,128)(2,1)S(1)}, bf16[2,32,512]{2,1,0:T(8,128)(2,1)S(1)}, u32[]{:S(2)}, u32[]{:S(2)}) %collective-permute-start.9) | collective-permute-done | bytes 65568 | tf_op jit(solution)/shard_map/ppermute | solution.py:336
  54.8 0.7 %place.3 = bf16[8,64,512]{2,1,0:T(8,128)(2,1)} custom-call(bf16[2,32,512]{2,1,0:T(8,128)(2,1)S(1)} %get-tuple-element.46.refs_0_, bf16[2,32,512]{2,1,0:T(8,128)(2,1)S(1)} %collective-permute-done.8.refs_1_, bf16[2,32,512]{2,1,0:T(8,128)(2,1)S(1)} %collective-permute-done.9.refs_2_, ...), custom_call_target="tpu_custom_call", output_to_operand_aliasing={{}: (4, {})} | custom-call | bytes 5242880 | tf_op jit(solution)/shard_map/place/pallas_call | solution.py:322
Async XLA Ops:
  0.0 11.0 %collective-permute-start = (bf16[256,512]{1,0:T(8,128)(2,1)}, bf16[256,512]{1,0:T(8,128)(2,1)S(1)}, u32[]{:S(2)}, u32[]{:S(2)}) collective-permute-start(bf16[256,512]{1,0:T(8,128)(2,1)} %bitcast.8), channel_id=1, source_target_pairs={{0,2},{2,0},{1,3},{3,1},{4,6},{6,4},{5,7},{7,5},{8,10},{10,8},{9,1... | collective-permute-start | bytes 786440 | tf_op jit(solution)/shard_map/ppermute | solution.py:345
  2.9 14.6 %collective-permute-start.1 = (bf16[128,1024]{1,0:T(8,128)(2,1)}, bf16[128,1024]{1,0:T(8,128)(2,1)S(1)}, u32[]{:S(2)}, u32[]{:S(2)}) collective-permute-start(bf16[128,1024]{1,0:T(8,128)(2,1)} %refs_0_.1), channel_id=1, source_target_pairs={{0,8},{2,14},{4,12},{6,10},{8,0},{10,6},{12,4},{14,2},{1,9},{3,15}... | collective-permute-start | bytes 786440 | tf_op jit(solution)/shard_map/ppermute | solution.py:341
  5.5 12.2 %collective-permute-start.2 = (bf16[128,1024]{1,0:T(8,128)(2,1)}, bf16[128,1024]{1,0:T(8,128)(2,1)S(1)}, u32[]{:S(2)}, u32[]{:S(2)}) collective-permute-start(bf16[128,1024]{1,0:T(8,128)(2,1)} %refs_0_.1), channel_id=1, source_target_pairs={{0,4},{4,0},{8,12},{12,8},{1,5},{5,1},{9,13},{13,9},{2,6},{6,2},{1... | collective-permute-start | bytes 786440 | tf_op jit(solution)/shard_map/ppermute | solution.py:336
  11.0 6.7 %copy-start.1 = (bf16[1024,512]{1,0:T(8,128)(2,1)S(1)}, bf16[1024,512]{1,0:T(8,128)(2,1)}, u32[]{:S(2)}) copy-start(bf16[1024,512]{1,0:T(8,128)(2,1)} %refs_1_.1) | copy-start | bytes 3145732
  11.0 6.7 %copy-start.2 = (bf16[1024,512]{1,0:T(8,128)(2,1)S(1)}, bf16[1024,512]{1,0:T(8,128)(2,1)}, u32[]{:S(2)}) copy-start(bf16[1024,512]{1,0:T(8,128)(2,1)} %refs_2_.3) | copy-start | bytes 3145732
  11.0 6.7 %copy-start.4 = (bf16[128,1024]{1,0:T(8,128)(2,1)S(1)}, bf16[128,1024]{1,0:T(8,128)(2,1)}, u32[]{:S(2)}) copy-start(bf16[128,1024]{1,0:T(8,128)(2,1)} %refs_0_.1) | copy-start | bytes 786436
  17.5 7.1 %collective-permute-start.3 = (bf16[128,1024]{1,0:T(8,128)(2,1)S(1)}, bf16[128,1024]{1,0:T(8,128)(2,1)S(1)}, u32[]{:S(2)}, u32[]{:S(2)}) collective-permute-start(bf16[128,1024]{1,0:T(8,128)(2,1)S(1)} %collective-permute-done.1.refs_2_), channel_id=1, source_target_pairs={{0,2},{2,0},{1,3},{3,1},{4,6},{6,4},{5,7},{7,5},{8,10},{10,8},{9,1... | collective-permute-start | bytes 786440 | tf_op jit(solution)/shard_map/ppermute | solution.py:345
  18.7 8.0 %copy-start.3 = (bf16[512,1024]{1,0:T(8,128)(2,1)S(1)}, bf16[512,1024]{1,0:T(8,128)(2,1)}, u32[]{:S(2)}) copy-start(bf16[512,1024]{1,0:T(8,128)(2,1)} %wo.3) | copy-start | bytes 3145732
  18.7 8.0 %copy-start.5 = (s32[4,8]{1,0:T(4,128)S(1)}, s32[4,8]{1,0:T(4,128)}, u32[]{:S(2)}) copy-start(s32[4,8]{1,0:T(4,128)} %adjacency.3) | copy-start | bytes 388
  18.8 7.9 %collective-permute-start.4 = (bf16[384,1024]{1,0:T(8,128)(2,1)S(1)}, bf16[384,1024]{1,0:T(8,128)(2,1)S(1)}, u32[]{:S(2)}, u32[]{:S(2)}) collective-permute-start(bf16[384,1024]{1,0:T(8,128)(2,1)S(1)} %project.2), channel_id=1, source_target_pairs={{0,1},{1,0},{2,3},{3,2},{4,5},{5,4},{6,7},{7,6},{8,9},{9,8},{10,11... | collective-permute-start | bytes 2359304 | tf_op jit(solution)/shard_map/ppermute | solution.py:345
  25.1 1.6 %collective-permute-start.5 = (bf16[128,1024]{1,0:T(8,128)(2,1)S(1)}, bf16[128,1024]{1,0:T(8,128)(2,1)S(1)}, u32[]{:S(2)}, u32[]{:S(2)}) collective-permute-start(bf16[128,1024]{1,0:T(8,128)(2,1)S(1)} %project.3), channel_id=1, source_target_pairs={{0,1},{1,0},{2,3},{3,2},{4,5},{5,4},{6,7},{7,6},{8,9},{9,8},{10,11... | collective-permute-start | bytes 786440 | tf_op jit(solution)/shard_map/ppermute | solution.py:345
  31.1 6.5 %collective-permute-start.7 = (bf16[128,512]{1,0:T(8,128)(2,1)S(1)}, bf16[128,512]{1,0:T(8,128)(2,1)S(1)}, u32[]{:S(2)}, u32[]{:S(2)}) collective-permute-start(bf16[128,512]{1,0:T(8,128)(2,1)S(1)} %get-tuple-element.43), channel_id=1, source_target_pairs={{0,2},{2,0},{1,3},{3,1},{4,6},{6,4},{5,7},{7,5},{8,10},{10,8},{9,1... | collective-permute-start | bytes 393224 | tf_op jit(solution)/shard_map/ppermute | solution.py:345
  31.4 6.0 %copy-start.6 = (s32[4,1]{0,1:T(1,128)S(1)}, s32[4,1]{0,1:T(1,128)}, u32[]{:S(2)}) copy-start(s32[4,1]{0,1:T(1,128)} %param.12) | copy-start | bytes 52
  31.4 6.1 %copy-start = (bf16[4,64,512]{2,1,0:T(8,128)(2,1)S(1)}, bf16[4,64,512]{2,1,0:T(8,128)(2,1)}, u32[]{:S(2)}) copy-start(bf16[4,64,512]{2,1,0:T(8,128)(2,1)} %grid_features.3) | copy-start | bytes 786436
  35.6 7.8 %collective-permute-start.6 = (bf16[128,512]{1,0:T(8,128)(2,1)S(1)}, bf16[128,512]{1,0:T(8,128)(2,1)S(1)}, u32[]{:S(2)}, u32[]{:S(2)}) collective-permute-start(bf16[128,512]{1,0:T(8,128)(2,1)S(1)} %get-tuple-element.41), channel_id=1, source_target_pairs={{0,2},{2,0},{1,3},{3,1},{4,6},{6,4},{5,7},{7,5},{8,10},{10,8},{9,1... | collective-permute-start | bytes 393224 | tf_op jit(solution)/shard_map/ppermute | solution.py:345
  38.3 9.8 %collective-permute-start.11 = (bf16[2,32,512]{2,1,0:T(8,128)(2,1)S(1)}, bf16[2,32,512]{2,1,0:T(8,128)(2,1)S(1)}, u32[]{:S(2)}, u32[]{:S(2)}) collective-permute-start(bf16[2,32,512]{2,1,0:T(8,128)(2,1)S(1)} %get-tuple-element.50), channel_id=1, source_target_pairs={{0,4},{4,0},{8,12},{12,8},{1,5},{5,1},{9,13},{13,9},{2,6},{6,2},{1... | collective-permute-start | bytes 196616 | tf_op jit(solution)/shard_map/ppermute | solution.py:336
  40.1 8.5 %collective-permute-start.12 = (bf16[2,32,512]{2,1,0:T(8,128)(2,1)S(1)}, bf16[2,32,512]{2,1,0:T(8,128)(2,1)S(1)}, u32[]{:S(2)}, u32[]{:S(2)}) collective-permute-start(bf16[2,32,512]{2,1,0:T(8,128)(2,1)S(1)} %get-tuple-element.51), channel_id=1, source_target_pairs={{0,8},{4,12},{8,0},{12,4},{1,9},{5,13},{9,1},{13,5},{2,10},{6,14},... | collective-permute-start | bytes 196616 | tf_op jit(solution)/shard_map/ppermute | solution.py:336
  43.4 6.5 %collective-permute-start.13 = (bf16[2,32,512]{2,1,0:T(8,128)(2,1)S(1)}, bf16[2,32,512]{2,1,0:T(8,128)(2,1)S(1)}, u32[]{:S(2)}, u32[]{:S(2)}) collective-permute-start(bf16[2,32,512]{2,1,0:T(8,128)(2,1)S(1)} %get-tuple-element.52), channel_id=1, source_target_pairs={{0,12},{4,8},{8,4},{12,0},{1,13},{5,9},{9,5},{13,1},{2,14},{6,10},... | collective-permute-start | bytes 196616 | tf_op jit(solution)/shard_map/ppermute | solution.py:336
  44.1 6.5 %collective-permute-start.10 = (bf16[2,32,512]{2,1,0:T(8,128)(2,1)S(1)}, bf16[2,32,512]{2,1,0:T(8,128)(2,1)S(1)}, u32[]{:S(2)}, u32[]{:S(2)}) collective-permute-start(bf16[2,32,512]{2,1,0:T(8,128)(2,1)S(1)} %get-tuple-element.49), channel_id=1, source_target_pairs={{0,12},{4,8},{8,4},{12,0},{1,13},{5,9},{9,5},{13,1},{2,14},{6,10},... | collective-permute-start | bytes 196616 | tf_op jit(solution)/shard_map/ppermute | solution.py:336
  48.0 4.6 %collective-permute-start.8 = (bf16[2,32,512]{2,1,0:T(8,128)(2,1)S(1)}, bf16[2,32,512]{2,1,0:T(8,128)(2,1)S(1)}, u32[]{:S(2)}, u32[]{:S(2)}) collective-permute-start(bf16[2,32,512]{2,1,0:T(8,128)(2,1)S(1)} %get-tuple-element.47), channel_id=1, source_target_pairs={{0,4},{4,0},{8,12},{12,8},{1,5},{5,1},{9,13},{13,9},{2,6},{6,2},{1... | collective-permute-start | bytes 196616 | tf_op jit(solution)/shard_map/ppermute | solution.py:336
  48.0 6.8 %collective-permute-start.9 = (bf16[2,32,512]{2,1,0:T(8,128)(2,1)S(1)}, bf16[2,32,512]{2,1,0:T(8,128)(2,1)S(1)}, u32[]{:S(2)}, u32[]{:S(2)}) collective-permute-start(bf16[2,32,512]{2,1,0:T(8,128)(2,1)S(1)} %get-tuple-element.48), channel_id=1, source_target_pairs={{0,8},{4,12},{8,0},{12,4},{1,9},{5,13},{9,1},{13,5},{2,10},{6,14},... | collective-permute-start | bytes 196616 | tf_op jit(solution)/shard_map/ppermute | solution.py:336

commit v5 on v4

--- a/solution.py
+++ b/solution.py
@@ -1,3 +1,4 @@
+import functools
 import math
 
 import jax
@@ -14,7 +15,6 @@
 QUAD = 4
 WIDE = QUAD * HEAD_DIM
 CHUNKS = 2
-ROWS = BLOCK // CHUNKS
 MIB = 1 << 20
 
 
@@ -29,10 +29,6 @@
     return 0.5 * x * (1.0 + lax.erf(x * (2.0**-0.5)))
 
 
-def in_vmem(x):
-    return pltpu.with_memory_space_constraint(x, pltpu.VMEM)
-
-
 def in_hbm(x):
     return pltpu.with_memory_space_constraint(x, pltpu.HBM)
 
@@ -47,33 +43,25 @@
 
 def params(mib):
     return pltpu.CompilerParams(vmem_limit_bytes=mib * MIB)
-
-
-def halves(width):
-    h = lax.axis_index("head")
-    mine = pl.ds(pl.multiple_of(h * width, width), width)
-    theirs = pl.ds(pl.multiple_of((1 - h) * width, width), width)
-    return mine, theirs
 
 
 def mlp_kernel(own, other, gain, wq, wup, wdn, q_out, mlp_out, normed_s):
     half = own.shape[1]
     units = wup.shape[1]
     chunk = units // 4
-    mine, theirs = halves(half)
+    x_other = other[...].astype(jnp.float32)
     x_own = own[...].astype(jnp.float32)
-    x_other = other[...].astype(jnp.float32)
 
     def mean(a, b):
         total = jnp.sum(a, axis=-1, keepdims=True) + jnp.sum(b, axis=-1, keepdims=True)
         return total * (0.5 / half)
 
-    average = mean(x_own, x_other)
+    average = mean(x_other, x_own)
+    x_other = x_other - average
     x_own = x_own - average
-    x_other = x_other - average
-    factor = lax.rsqrt(mean(x_own * x_own, x_other * x_other) + epsilon)
-    normed_s[:, mine] = (x_own * factor * gain[:, mine]).astype(jnp.bfloat16)
-    normed_s[:, theirs] = (x_other * factor * gain[:, theirs]).astype(jnp.bfloat16)
+    factor = lax.rsqrt(mean(x_other * x_other, x_own * x_own) + epsilon)
+    normed_s[:, :half] = (x_other * factor * gain[:, :half]).astype(jnp.bfloat16)
+    normed_s[:, half:] = (x_own * factor * gain[:, half:]).astype(jnp.bfloat16)
     normed = normed_s[...]
     q_out[...] = dot(normed, wq[...]).astype(jnp.bfloat16)
     for c in range(units // chunk):
@@ -109,24 +97,37 @@
     )(own, other, gain, wq, wup, wdn)
 
 
-def stage_kernel(*refs):
-    sources, copies_to, sem = refs[: len(refs) // 2], refs[len(refs) // 2 : -1], refs[-1]
+def stage_kernel(axes, *refs):
+    sources, targets, sem = refs[: len(axes)], refs[len(axes) : -1], refs[-1]
+    h = lax.axis_index("head")
     copies = []
-    for i, (source, target) in enumerate(zip(sources, copies_to)):
-        copies.append(pltpu.make_async_copy(source, target, sem.at[i]))
-        copies[i].start()
+    for source, target, axis in zip(sources, targets, axes):
+        if axis is None:
+            copies.append(pltpu.make_async_copy(source, target, sem.at[len(copies)]))
+            continue
+        half = source.shape[axis] // 2
+        for part, head in enumerate((1 - h, h)):
+            span = pl.ds(pl.multiple_of(head * half, half), half)
+            place = pl.ds(part * half, half)
+            if axis == 0:
+                pair = (source.at[span, :], target.at[place, :])
+            else:
+                pair = (source.at[:, span], target.at[:, place])
+            copies.append(pltpu.make_async_copy(*pair, sem.at[len(copies)]))
+    for copy in copies:
+        copy.start()
     for copy in copies:
         copy.wait()
 
 
-def run_stage(*arrays):
+def run_stage(arrays, axes):
     size = sum(2 * array.size for array in arrays)
     return pl.pallas_call(
-        stage_kernel,
+        functools.partial(stage_kernel, axes),
         out_shape=tuple(jax.ShapeDtypeStruct(array.shape, array.dtype) for array in arrays),
         in_specs=[whole(pltpu.HBM)] * len(arrays),
         out_specs=tuple(vmem(len(arrays))),
-        scratch_shapes=[pltpu.SemaphoreType.DMA((len(arrays),))],
+        scratch_shapes=[pltpu.SemaphoreType.DMA((2 * len(arrays),))],
         compiler_params=params(16),
         cost_estimate=pl.CostEstimate(flops=0, bytes_accessed=20 * size, transcendentals=0),
         name="stage",
@@ -156,24 +157,66 @@
             transcendentals=0,
         ),
         name="project",
-    )(*pieces, in_vmem(wk), in_vmem(wv))
-
-
-def attend_rows(c, adjacency, q, table, mlp, wo, send, keep, att_s):
+    )(*pieces, wk, wv)
+
+
+def table_kernel(mine, sibling, table, sem):
+    copies = [
+        pltpu.make_async_copy(mine, table.at[0, pl.ds(0, mine.shape[0])], sem.at[0]),
+        pltpu.make_async_copy(sibling, table.at[1, pl.ds(0, mine.shape[0])], sem.at[1]),
+    ]
+    for copy in copies:
+        copy.start()
+    for copy in copies:
+        copy.wait()
+
+
+def run_table(mine, sibling, blocks):
+    return pl.pallas_call(
+        table_kernel,
+        out_shape=jax.ShapeDtypeStruct((2, blocks) + mine.shape[1:], jnp.bfloat16),
+        in_specs=vmem(2),
+        out_specs=whole(pltpu.VMEM),
+        scratch_shapes=[pltpu.SemaphoreType.DMA((2,))],
+        compiler_params=params(8),
+        cost_estimate=pl.CostEstimate(
+            flops=0, bytes_accessed=80 * mine.size, transcendentals=0
+        ),
+        name="table",
+    )(mine, sibling)
+
+
+def project_out(c, att, mlp, wo, send, keep):
+    width = send.shape[1]
+    half = att.shape[1]
+    for out, first in ((send, 0), (keep, half)):
+        span = slice(first + c * width, first + (c + 1) * width)
+        out[...] = (mlp[:, span] + dot(att[...], wo[:, span])).astype(jnp.bfloat16)
+
+
+def attend_kernel(
+    adjacency, q, mine, sibling, table_in, mlp, wo, send, keep, att, table, sem
+):
+    del table_in
     s = lax.axis_index("shard")
     h = lax.axis_index("head")
     u = lax.axis_index("sub")
     half = wo.shape[0]
-    per_core = table.shape[0] // 2
-    mine, theirs = halves(half)
-    rows = slice(c * ROWS, (c + 1) * ROWS)
-    rows_of = lax.broadcasted_iota(jnp.int32, (QUAD * ROWS, WIDE), 0) // ROWS
-    lanes_of = lax.broadcasted_iota(jnp.int32, (QUAD * ROWS, WIDE), 1) // HEAD_DIM
+    ready = table.shape[1] - mine.shape[0]
+    copies = []
+    for i, part in enumerate((mine, sibling)):
+        target = table.at[i, pl.ds(ready, part.shape[0])]
+        copies.append(pltpu.make_async_copy(part, target, sem.at[i]))
+        copies[i].start()
+    rows_of = lax.broadcasted_iota(jnp.int32, (WIDE, WIDE), 0) // BLOCK
+    lanes_of = lax.broadcasted_iota(jnp.int32, (WIDE, WIDE), 1) // HEAD_DIM
     diagonal = rows_of == lanes_of
-    lane_head = lax.broadcasted_iota(jnp.int32, (ROWS, WIDE), 1) // HEAD_DIM
+    lane_head = lax.broadcasted_iota(jnp.int32, (BLOCK, WIDE), 1) // HEAD_DIM
     scale = HEAD_DIM**-0.5 * math.log2(math.e)
-    count = adjacency.shape[0]
-    for b in range(count):
+    for copy in copies:
+        copy.wait()
+    for b in range(adjacency.shape[0]):
+        rows = slice(b * BLOCK, (b + 1) * BLOCK)
         places = []
         for j in range(adjacency.shape[1]):
             m = adjacency[b, j]
@@ -181,13 +224,13 @@
             core = lax.rem(m // 2, 2)
             distance = s ^ (m // 4)
             distance = jnp.where(distance <= 1, distance, 2 + ((distance - 2) ^ h))
-            places.append((core ^ u) * per_core + distance * 2 + part)
+            places.append((core ^ u, distance * 2 + part))
         for g in range(half // WIDE):
             columns = slice(g * WIDE, (g + 1) * WIDE)
-            keys = jnp.concatenate([table[p, :, columns] for p in places], axis=0)
+            keys = jnp.concatenate([table[i, p, :, columns] for i, p in places], axis=0)
             vcolumns = slice(half + g * WIDE, half + (g + 1) * WIDE)
-            values = jnp.concatenate([table[p, :, vcolumns] for p in places], axis=0)
-            stacked = jnp.concatenate([q[b, rows, columns]] * QUAD, axis=0)
+            values = jnp.concatenate([table[i, p, :, vcolumns] for i, p in places], axis=0)
+            stacked = jnp.concatenate([q[rows, columns]] * QUAD, axis=0)
             stacked = jnp.where(diagonal, stacked, jnp.zeros_like(stacked))
             scores = lax.dot_general(
                 stacked, keys, (((1,), (1,)), ((), ())), preferred_element_type=jnp.float32
@@ -197,51 +240,29 @@
             total = jnp.sum(weights, axis=-1, keepdims=True)
             probs = (weights * (1.0 / total)).astype(jnp.bfloat16)
             mixed = dot(probs, values)
-            merged = mixed[0:ROWS, :]
+            merged = mixed[0:BLOCK, :]
             for i in range(1, QUAD):
-                merged = jnp.where(lane_head == i, mixed[i * ROWS : (i + 1) * ROWS, :], merged)
-            att_s[b * ROWS : (b + 1) * ROWS, columns] = merged.astype(jnp.bfloat16)
-    for out, span in ((send, theirs), (keep, mine)):
-        extra = mlp[:, rows, span].reshape(count * ROWS, half)
-        out[...] = (extra + dot(att_s[...], wo[:, span])).astype(jnp.bfloat16)
-
-
-def first_kernel(
-    adjacency, q, mine_a, mine_b, sibling_a, sibling_b, mlp, wo, send, keep, table, att_s, sem
-):
-    copies = []
-    first = 0
-    for i, part in enumerate((mine_a, mine_b, sibling_a, sibling_b)):
-        blocks = part.shape[0]
-        copies.append(pltpu.make_async_copy(part, table.at[pl.ds(first, blocks)], sem.at[i]))
-        copies[i].start()
-        first += blocks
-    for copy in copies:
-        copy.wait()
-    attend_rows(0, adjacency, q, table, mlp, wo, send, keep, att_s)
-
-
-def later_kernel(c):
-    def kernel(adjacency, q, table, mlp, wo, send, keep, att_s):
-        attend_rows(c, adjacency, q, table, mlp, wo, send, keep, att_s)
-
-    return kernel
-
-
-def run_attend(c, adjacency, q, tables, mlp, wo):
-    count, _, half = q.shape
-    rows = count * ROWS
-    part = jax.ShapeDtypeStruct((rows, half), jnp.bfloat16)
-    blocks = sum(table.shape[0] for table in tables)
-    shared = jax.ShapeDtypeStruct((blocks,) + tables[0].shape[1:], jnp.bfloat16)
-    outs = (part, part, shared) if c == 0 else (part, part)
-    scratch = [pltpu.VMEM((rows, half), jnp.bfloat16)]
-    return pl.pallas_call(
-        first_kernel if c == 0 else later_kernel(c),
-        out_shape=outs,
-        in_specs=[whole(pltpu.SMEM)] + vmem(len(tables) + 3),
-        out_specs=tuple(vmem(len(outs))),
-        scratch_shapes=scratch + [pltpu.SemaphoreType.DMA((len(tables),))] * (c == 0),
+                merged = jnp.where(lane_head == i, mixed[i * BLOCK : (i + 1) * BLOCK, :], merged)
+            att[rows, columns] = merged.astype(jnp.bfloat16)
+    project_out(0, att, mlp, wo, send, keep)
+
+
+def run_attend(adjacency, q, mine, sibling, table, mlp, wo):
+    rows, half = q.shape
+    part = jax.ShapeDtypeStruct((rows, half // CHUNKS), jnp.bfloat16)
+    blocks = table.shape[0] * table.shape[1]
+    send, keep, att, _ = pl.pallas_call(
+        attend_kernel,
+        out_shape=(
+            part,
+            part,
+            jax.ShapeDtypeStruct(q.shape, jnp.bfloat16),
+            jax.ShapeDtypeStruct(table.shape, jnp.bfloat16),
+        ),
+        in_specs=[whole(pltpu.SMEM)] + vmem(6),
+        out_specs=tuple(vmem(4)),
+        scratch_shapes=[pltpu.SemaphoreType.DMA((2,))],
+        input_output_aliases={4: 3},
         compiler_params=params(16),
         cost_estimate=pl.CostEstimate(
             flops=20 * rows * half * (D + 8 * 8 * BLOCK),
@@ -249,85 +270,100 @@
             transcendentals=rows * 8 * BLOCK * half // HEAD_DIM,
         ),
         name="attend",
-    )(adjacency, q, *tables, mlp, in_vmem(wo))
-
-
-def combine_kernel(c):
-    def kernel(owners, grid_features, keep, received, *outs):
-        s = lax.axis_index("shard")
-        shards = len(outs)
-        count = grid_features.shape[0]
-        names = [owners[t, 0] for t in range(count)]
-        for d in range(shards):
-            target = s ^ d
-            for j in range(CAP):
-                outs[d][j] = jnp.zeros(outs[d].shape[1:], jnp.bfloat16)
-            seen = jnp.int32(0)
-            for t in range(count):
-                hit = names[t] == target
-                rank = seen
-
-                @pl.when(hit)
-                def _():
-                    rows = slice(t * ROWS, (t + 1) * ROWS)
-                    partials = keep[rows, :].astype(jnp.float32)
-                    partials = partials + received[rows, :].astype(jnp.float32)
-                    residual = grid_features[t, c * ROWS : (c + 1) * ROWS, :]
-                    updated = residual.astype(jnp.float32) + partials
-                    outs[d][rank] = updated.astype(jnp.bfloat16)
-
-                seen = seen + hit.astype(jnp.int32)
-
-    return kernel
+    )(adjacency, q, mine, sibling, table, mlp, wo)
+    return send, keep, att
+
+
+def run_project_out(c, att, mlp, wo):
+    rows, half = att.shape
+    part = jax.ShapeDtypeStruct((rows, half // CHUNKS), jnp.bfloat16)
+    return pl.pallas_call(
+        functools.partial(project_out, c),
+        out_shape=(part, part),
+        in_specs=vmem(3),
+        out_specs=tuple(vmem(2)),
+        compiler_params=params(8),
+        cost_estimate=pl.CostEstimate(
+            flops=200 * rows * half * D,
+            bytes_accessed=200 * half * D,
+            transcendentals=0,
+        ),
+        name="project_out",
+    )(att, mlp, wo)
+
+
+def combine_kernel(c, owners, grid_features, keep, received, *outs):
+    s = lax.axis_index("shard")
+    count = grid_features.shape[0]
+    width = keep.shape[1]
+    names = [owners[t, 0] for t in range(count)]
+    for d, out in enumerate(outs):
+        for j in range(CAP):
+            out[j] = jnp.zeros(out.shape[1:], jnp.bfloat16)
+        seen = jnp.int32(0)
+        for t in range(count):
+            hit = names[t] == s ^ d
+            rank = seen
+
+            @pl.when(hit)
+            def _():
+                rows = slice(t * BLOCK, (t + 1) * BLOCK)
+                partials = keep[rows, :].astype(jnp.float32)
+                partials = partials + received[rows, :].astype(jnp.float32)
+                residual = grid_features[t, :, c * width : (c + 1) * width]
+                out[rank] = (residual.astype(jnp.float32) + partials).astype(jnp.bfloat16)
+
+            seen = seen + hit.astype(jnp.int32)
 
 
 def run_combine(c, owners, grid_features, keep, received, shards):
-    count, _, half = grid_features.shape
-    slot = jax.ShapeDtypeStruct((CAP, ROWS, half), jnp.bfloat16)
-    return pl.pallas_call(
-        combine_kernel(c),
+    count, rows, _ = grid_features.shape
+    width = keep.shape[1]
+    slot = jax.ShapeDtypeStruct((CAP, rows, width), jnp.bfloat16)
+    return pl.pallas_call(
+        functools.partial(combine_kernel, c),
         out_shape=(slot,) * shards,
         in_specs=[whole(pltpu.SMEM)] + vmem(3),
         out_specs=tuple(vmem(shards)),
         compiler_params=params(8),
         cost_estimate=pl.CostEstimate(
-            flops=3000 * count * ROWS * half,
-            bytes_accessed=400 * ROWS * half * (3 * count + CAP * shards),
+            flops=3000 * count * rows * width,
+            bytes_accessed=400 * rows * width * (3 * count + CAP * shards),
             transcendentals=0,
         ),
         name="combine",
     )(owners, grid_features, keep, received)
 
 
-def place_kernel(c, shards):
-    def kernel(*refs):
-        arrived, (out, sem) = refs[:shards], refs[-2:]
-        s = lax.axis_index("shard")
-        rows = pl.ds(c * ROWS, ROWS)
-        copies = []
-        for d in range(shards):
-            slots = pl.ds((s ^ d) * CAP, CAP)
-            copies.append(pltpu.make_async_copy(arrived[d], out.at[slots, rows, :], sem.at[d]))
-            copies[d].start()
-        for copy in copies:
-            copy.wait()
-
-    return kernel
+def place_kernel(c, *refs):
+    out, sem = refs[-2:]
+    s = lax.axis_index("shard")
+    copies = []
+    for d in range(sem.shape[0]):
+        width = refs[d].shape[2]
+        columns = pl.ds(c * width, width)
+        slots = pl.ds((s ^ d) * CAP, CAP)
+        copies.append(pltpu.make_async_copy(refs[d], out.at[slots, :, columns], sem.at[d]))
+        copies[d].start()
+    for copy in copies:
+        copy.wait()
 
 
 def run_place(c, arrived, placed):
     shards = len(arrived)
-    half = arrived[0].shape[2]
-    size = 2 * CAP * shards * ROWS * half
-    return pl.pallas_call(
-        place_kernel(c, shards),
-        out_shape=jax.ShapeDtypeStruct((shards * CAP, BLOCK, half), jnp.bfloat16),
+    _, rows, width = arrived[0].shape
+    shape = (shards * CAP, rows, CHUNKS * width)
+    return pl.pallas_call(
+        functools.partial(place_kernel, c),
+        out_shape=jax.ShapeDtypeStruct(shape, jnp.bfloat16),
         in_specs=vmem(shards) + [whole(pltpu.HBM)] * len(placed),
         out_specs=whole(pltpu.HBM),
         scratch_shapes=[pltpu.SemaphoreType.DMA((shards,))],
         input_output_aliases={shards: 0} if placed else {},
         compiler_params=params(4),
-        cost_estimate=pl.CostEstimate(flops=0, bytes_accessed=20 * size, transcendentals=0),
+        cost_estimate=pl.CostEstimate(
+            flops=0, bytes_accessed=40 * CAP * shards * rows * width, transcendentals=0
+        ),
         name="place",
     )(*arrived, *placed)
 
@@ -362,26 +398,40 @@
     count, rows, half = grid_features.shape
     flat = grid_features.reshape(count * rows, half)
     far = fetched(mesh_nodes, shards)
-    near = crossed(mesh_nodes, 1, shards)
     other = swapped(flat, "head")
-    staged = run_stage(flat, norm_gain.reshape(1, -1), query_weight, up_weight, down_weight)
-    queries, mlp = run_mlp(staged[0], other, *staged[1:])
+    staged = run_stage(
+        (
+            flat,
+            norm_gain.reshape(1, -1),
+            query_weight,
+            up_weight,
+            down_weight,
+            output_weight,
+            key_weight,
+            value_weight,
+            mesh_nodes,
+        ),
+        (None, 1, 0, 0, 1, 1, None, None, None),
+    )
+    flat, gain, wq, wup, wdn, wo, wk, wv, mesh = staged
+    near = crossed(mesh, 1, shards)
+    queries, mlp = run_mlp(flat, other, gain, wq, wup, wdn)
     queries, mlp, far = lax.optimization_barrier((queries, mlp, far))
     farther = swapped(far, "head")
-    mine_a = run_project((mesh_nodes, near, far), key_weight, value_weight)
+    blocked = (-1, BLOCK, 2 * half)
+    mine_a = run_project((mesh, near, far), wk, wv)
     sibling_a = swapped(mine_a, "sub")
-    mine_b = run_project((farther,), key_weight, value_weight)
+    table = run_table(mine_a.reshape(blocked), sibling_a.reshape(blocked), 2 * shards)
+    mine_b = run_project((farther,), wk, wv)
     sibling_b = swapped(mine_b, "sub")
-    tables = [
-        table.reshape(-1, BLOCK, 2 * half) for table in (mine_a, mine_b, sibling_a, sibling_b)
-    ]
-    queries = queries.reshape(count, rows, half)
-    mlp = mlp.reshape(count, rows, 2 * half)
+    send, keep, att = run_attend(
+        adjacency, queries, mine_b.reshape(blocked), sibling_b.reshape(blocked), table, mlp, wo
+    )
     placed = []
     slots = None
     for c in range(CHUNKS):
-        send, keep, *table = run_attend(c, adjacency, queries, tables, mlp, output_weight)
-        tables = table or tables
+        if c > 0:
+            send, keep = run_project_out(c, att, mlp, wo)
         received = swapped(send, "head")
         if slots is not None:
             received, _ = lax.optimization_barrier((received, slots[0]))

time: 55.7 us -> 53 us (0.952)
  Pallas kernels: 20.2 us -> 16 us
  waiting for transfers between devices: 16 us -> 17.4 us
    pallas_call x7 -> x8, Pallas kernels: 15.3 us -> 11.3 us  [the longest x1 4.87 us: run_stage(): pl.pallas_call(functools.partial(stage_kernel, axes), out_shape=tuple((ja...]
    ppermute x7, waiting for transfers between devices: 5.57 us -> 8.92 us  [crossed(): return lax.ppermute(x, 'shard', [(i, i ^ distance) for i in range(size)])]
    ppermute x6, waiting for transfers between devices: 7.34 us -> 6.36 us  [swapped(): return lax.ppermute(x, axis, [(0, 1), (1, 0)])]
    ppermute x1, waiting for transfers between devices: 3.08 us -> 2.14 us  [fetched(): return lax.ppermute(x, ('shard', 'head'), pairs)]
  transfers between devices with their start and end apart: 14 -> 14, of which waited for: 7 -> 9; matrix products, arithmetic and copies ran while one was open for 0% -> 0% of each run, Pallas kernels for 27% -> 23%
where the time goes in v5:
time: 53 us; the launch traced here: 52.9 us
  starting transfers between devices  19.2 us (36%)
  waiting for transfers between devices  17.4 us (33%)
  Pallas kernels  16 us (30%)
    ppermute x7, starting transfers between devices, crossed(): return lax.ppermute(x, 'shard', [(i, i ^ distance) for i in range(size)])  11.4 us
    ppermute x7, waiting for transfers between devices, crossed(): return lax.ppermute(x, 'shard', [(i, i ^ distance) for i in range(size)])  8.92 us
    ppermute x6, waiting for transfers between devices, swapped(): return lax.ppermute(x, axis, [(0, 1), (1, 0)])  6.36 us
    ppermute x6, starting transfers between devices, swapped(): return lax.ppermute(x, axis, [(0, 1), (1, 0)])  5.24 us
    pallas_call x1, Pallas kernels, run_stage(): pl.pallas_call(functools.partial(stage_kernel, axes), out_shape=tuple((ja...  4.87 us
    pallas_call x1, Pallas kernels, run_mlp(): pl.pallas_call(mlp_kernel, out_shape=(jax.ShapeDtypeStruct((rows, wq.shap...  3.33 us
    pallas_call x1, Pallas kernels, run_attend(): pl.pallas_call(attend_kernel, out_shape=(part, part, jax.ShapeDtypeStruct...  3.13 us
    ppermute x1, starting transfers between devices, fetched(): return lax.ppermute(x, ('shard', 'head'), pairs)  2.59 us
  transfers between devices with their start and end apart: 14, of which 9 were waited for; matrix products, arithmetic and copies ran while one was open for 0% of the time, Pallas kernels for 23%

profile of v5, /device:TPU:0, one launch (start us, length us, event | category | flops | bytes accessed | tf_op | source)
XLA Modules:
  0.0 52.9 jit_solution(11553401193216914593)
XLA Ops:
  0.0 2.9 %collective-permute-start = (bf16[256,512]{1,0:T(8,128)(2,1)}, bf16[256,512]{1,0:T(8,128)(2,1)S(1)}, u32[]{:S(2)}, u32[]{:S(2)}) collective-permute-start(bf16[256,512]{1,0:T(8,128)(2,1)} %bitcast.8), channel_id=1, source_target_pairs={{0,2},{2,0},{1,3},{3,1},{4,6},{6,4},{5,7},{7,5},{8,10},{10,8},{9,1... | collective-permute-start | bytes 786440 | tf_op jit(solution)/shard_map/ppermute | solution.py:381
  2.9 2.6 %collective-permute-start.1 = (bf16[128,1024]{1,0:T(8,128)(2,1)}, bf16[128,1024]{1,0:T(8,128)(2,1)S(1)}, u32[]{:S(2)}, u32[]{:S(2)}) collective-permute-start(bf16[128,1024]{1,0:T(8,128)(2,1)} %refs_8_.1), channel_id=1, source_target_pairs={{0,8},{2,14},{4,12},{6,10},{8,0},{10,6},{12,4},{14,2},{1,9},{3,15}... | collective-permute-start | bytes 786440 | tf_op jit(solution)/shard_map/ppermute | solution.py:377
  5.5 4.9 %stage.1 = (bf16[256,512]{1,0:T(8,128)(2,1)S(1)}, f32[1,1024]{1,0:T(1,128)S(1)}, bf16[1024,512]{1,0:T(8,128)(2,1)S(1)}, bf16[1024,2048]{1,0:T(8,128)(2,1)S(1)}, ...) custom-call(bf16[256,512]{1,0:T(8,128)(2,1)} %bitcast.9, ...), custom_call_target="tpu_custom_call" | custom-call | bytes 262184960 | tf_op jit(solution)/shard_map/stage/pallas_call | solution.py:125
  10.4 1.6 %collective-permute-start.4 = (bf16[128,1024]{1,0:T(8,128)(2,1)S(1)}, bf16[128,1024]{1,0:T(8,128)(2,1)S(1)}, u32[]{:S(2)}, u32[]{:S(2)}) collective-permute-start(bf16[128,1024]{1,0:T(8,128)(2,1)S(1)} %get-tuple-element.44.refs_0_), channel_id=1, source_target_pairs={{0,4},{4,0},{8,12},{12,8},{1,5},{5,1},{9,13},{13,9},{2,6},{6,2},{1... | collective-permute-start | bytes 786440 | tf_op jit(solution)/shard_map/ppermute | solution.py:372
  12.1 0.0 collective-permute-done.other
  12.1 3.3 %mlp.1 = (bf16[256,512]{1,0:T(8,128)(2,1)S(1)}, f32[256,1024]{1,0:T(8,128)S(1)}) custom-call(bf16[256,512]{1,0:T(8,128)(2,1)S(1)} %get-tuple-element.33.own, bf16[256,512]{1,0:T(8,128)(2,1)S(1)} %collective-permute-done.other, f32[1,1024]{1,0:T(1,128)S(1)} %get-tuple-element.34.gain, bf16[1024,512]{1,0:T(8,128)(2,1)S(1)} %get-tuple-element.35.wq, ...), custom_call_target="tpu_custom_call" | custom-call | flops 2415919104 | bytes 9437184 | tf_op jit(solution)/shard_map/mlp/pallas_call | solution.py:81
  15.4 2.1 %collective-permute-done.1.refs_2_ = bf16[128,1024]{1,0:T(8,128)(2,1)S(1)} collective-permute-done((bf16[128,1024]{1,0:T(8,128)(2,1)}, bf16[128,1024]{1,0:T(8,128)(2,1)S(1)}, u32[]{:S(2)}, u32[]{:S(2)}) %collective-permute-start.1) | collective-permute-done | bytes 262176 | tf_op jit(solution)/shard_map/ppermute | solution.py:377
  17.5 0.0 collective-permute-start.2
  17.5 4.9 %collective-permute-done.4.refs_1_ = bf16[128,1024]{1,0:T(8,128)(2,1)S(1)} collective-permute-done((bf16[128,1024]{1,0:T(8,128)(2,1)S(1)}, bf16[128,1024]{1,0:T(8,128)(2,1)S(1)}, u32[]{:S(2)}, u32[]{:S(2)}) %collective-permute-start.4) | collective-permute-done | bytes 262176 | tf_op jit(solution)/shard_map/ppermute | solution.py:372
  22.4 1.0 %project.3 = bf16[384,1024]{1,0:T(8,128)(2,1)S(1)} custom-call(bf16[128,1024]{1,0:T(8,128)(2,1)S(1)} %get-tuple-element.44.refs_0_, bf16[128,1024]{1,0:T(8,128)(2,1)S(1)} %collective-permute-done.4.refs_1_, bf16[128,1024]{1,0:T(8,128)(2,1)S(1)} %collective-permute-done.1.refs_2_, bf16[1024,512]{1,0:T(8,128)(2,1)S(1)} %get-tuple-element.42.refs_1_.refs_3_, ...), custom_call_target="tpu_custom_call" | custom-call | flops 16106127360 | bytes 73400320 | tf_op jit(solution)/shard_map/project/pallas_call | solution.py:148
  23.4 0.0 copy-start.1
  23.4 0.1 collective-permute-start.5
  23.5 1.1 %collective-permute-done.2.refs_0_ = bf16[128,1024]{1,0:T(8,128)(2,1)S(1)} collective-permute-done((bf16[128,1024]{1,0:T(8,128)(2,1)S(1)}, bf16[128,1024]{1,0:T(8,128)(2,1)S(1)}, u32[]{:S(2)}, u32[]{:S(2)}) %collective-permute-start.2) | collective-permute-done | bytes 262176 | tf_op jit(solution)/shard_map/ppermute | solution.py:381
  24.6 0.4 project.2
  25.1 0.1 collective-permute-start.3
  25.2 0.6 %collective-permute-done.5 = bf16[384,1024]{1,0:T(8,128)(2,1)S(1)} collective-permute-done((bf16[384,1024]{1,0:T(8,128)(2,1)S(1)}, bf16[384,1024]{1,0:T(8,128)(2,1)S(1)}, u32[]{:S(2)}, u32[]{:S(2)}) %collective-permute-start.5) | collective-permute-done | bytes 786464 | tf_op jit(solution)/shard_map/ppermute | solution.py:381
  25.8 0.1 table.1.table_in
  25.9 0.8 %collective-permute-done.3 = bf16[128,1024]{1,0:T(8,128)(2,1)S(1)} collective-permute-done((bf16[128,1024]{1,0:T(8,128)(2,1)S(1)}, bf16[128,1024]{1,0:T(8,128)(2,1)S(1)}, u32[]{:S(2)}, u32[]{:S(2)}) %collective-permute-start.3) | collective-permute-done | bytes 262176 | tf_op jit(solution)/shard_map/ppermute | solution.py:381
  26.7 0.0 copy-done.1
  26.7 3.1 %attend.1 = (bf16[256,256]{1,0:T(8,128)(2,1)S(1)}, bf16[256,256]{1,0:T(8,128)(2,1)S(1)}, bf16[256,512]{1,0:T(8,128)(2,1)S(1)}, bf16[2,8,64,1024]{3,2,1,0:T(8,128)(2,1)S(1)}) custom-call(s32[4,8]{1,0:T(4,128)S(1)} %copy-done.1, bf16[256,512]{1,0:T(8,128)(2,1)S(1)} %get-tuple-element.40.q, ...), custom_call_target="tpu_custom_call", output_to_operand_aliasing={{3}: (4, {})} | custom-call | flops 13421772800 | bytes 41943040 | tf_op jit(solution)/shard_map/attend/pallas_call | solution.py:254
  29.8 0.3 collective-permute-start.7
  30.2 0.0 copy-start.2
  30.2 0.0 copy-start
  30.2 0.3 project_out.1
  30.5 1.8 %collective-permute-start.6 = (bf16[256,256]{1,0:T(8,128)(2,1)S(1)}, bf16[256,256]{1,0:T(8,128)(2,1)S(1)}, u32[]{:S(2)}, u32[]{:S(2)}) collective-permute-start(bf16[256,256]{1,0:T(8,128)(2,1)S(1)} %get-tuple-element.49), channel_id=1, source_target_pairs={{0,2},{2,0},{1,3},{3,1},{4,6},{6,4},{5,7},{7,5},{8,10},{10,8},{9,1... | collective-permute-start | bytes 393224 | tf_op jit(solution)/shard_map/ppermute | solution.py:381
  32.3 0.0 copy-done.2
  32.3 0.1 copy.15.owners
  32.4 3.8 %collective-permute-done.7.received = bf16[256,256]{1,0:T(8,128)(2,1)S(1)} collective-permute-done((bf16[256,256]{1,0:T(8,128)(2,1)S(1)}, bf16[256,256]{1,0:T(8,128)(2,1)S(1)}, u32[]{:S(2)}, u32[]{:S(2)}) %collective-permute-start.7) | collective-permute-done | bytes 131104 | tf_op jit(solution)/shard_map/ppermute | solution.py:381
  36.2 0.0 copy-done
  36.2 0.7 %combine.2 = (bf16[2,64,256]{2,1,0:T(8,128)(2,1)S(1)}, bf16[2,64,256]{2,1,0:T(8,128)(2,1)S(1)}, bf16[2,64,256]{2,1,0:T(8,128)(2,1)S(1)}, bf16[2,64,256]{2,1,0:T(8,128)(2,1)S(1)}) custom-call(s32[4,1]{1,0:T(4,128)S(1)} %copy.15.owners, bf16[4,64,512]{2,1,0:T(8,128)(2,1)S(1)} %copy-done, bf16[256,256]{1,0:T(8,128)(2,1)S(1)} %get-tuple-element.50.keep, ...), custom_call_target="tpu_custom_call" | custom-call | flops 196608000 | bytes 131072000 | tf_op jit(solution)/shard_map/combine/pallas_call | solution.py:323
  36.9 1.9 %collective-permute-start.11 = (bf16[2,64,256]{2,1,0:T(8,128)(2,1)S(1)}, bf16[2,64,256]{2,1,0:T(8,128)(2,1)S(1)}, u32[]{:S(2)}, u32[]{:S(2)}) collective-permute-start(bf16[2,64,256]{2,1,0:T(8,128)(2,1)S(1)} %get-tuple-element.58), channel_id=1, source_target_pairs={{0,4},{4,0},{8,12},{12,8},{1,5},{5,1},{9,13},{13,9},{2,6},{6,2},{1... | collective-permute-start | bytes 196616 | tf_op jit(solution)/shard_map/ppermute | solution.py:372
  38.9 3.3 %collective-permute-start.12 = (bf16[2,64,256]{2,1,0:T(8,128)(2,1)S(1)}, bf16[2,64,256]{2,1,0:T(8,128)(2,1)S(1)}, u32[]{:S(2)}, u32[]{:S(2)}) collective-permute-start(bf16[2,64,256]{2,1,0:T(8,128)(2,1)S(1)} %get-tuple-element.59), channel_id=1, source_target_pairs={{0,8},{4,12},{8,0},{12,4},{1,9},{5,13},{9,1},{13,5},{2,10},{6,14},... | collective-permute-start | bytes 196616 | tf_op jit(solution)/shard_map/ppermute | solution.py:372
  42.1 0.0 collective-permute-start.13
  42.1 0.0 collective-permute-done.6.received
  42.1 0.7 %combine.3 = (bf16[2,64,256]{2,1,0:T(8,128)(2,1)S(1)}, bf16[2,64,256]{2,1,0:T(8,128)(2,1)S(1)}, bf16[2,64,256]{2,1,0:T(8,128)(2,1)S(1)}, bf16[2,64,256]{2,1,0:T(8,128)(2,1)S(1)}) custom-call(s32[4,1]{1,0:T(4,128)S(1)} %copy.15.owners, bf16[4,64,512]{2,1,0:T(8,128)(2,1)S(1)} %copy-done, bf16[256,256]{1,0:T(8,128)(2,1)S(1)} %get-tuple-element.48.keep, ...), custom_call_target="tpu_custom_call" | custom-call | flops 196608000 | bytes 131072000 | tf_op jit(solution)/shard_map/combine/pallas_call | solution.py:323
  42.9 3.9 %collective-permute-start.10 = (bf16[2,64,256]{2,1,0:T(8,128)(2,1)S(1)}, bf16[2,64,256]{2,1,0:T(8,128)(2,1)S(1)}, u32[]{:S(2)}, u32[]{:S(2)}) collective-permute-start(bf16[2,64,256]{2,1,0:T(8,128)(2,1)S(1)} %get-tuple-element.57), channel_id=1, source_target_pairs={{0,12},{4,8},{8,4},{12,0},{1,13},{5,9},{9,5},{13,1},{2,14},{6,10},... | collective-permute-start | bytes 196616 | tf_op jit(solution)/shard_map/ppermute | solution.py:372
  46.7 0.0 collective-permute-start.8
  46.7 0.0 collective-permute-done.11.refs_1_
  46.8 0.6 %collective-permute-start.9 = (bf16[2,64,256]{2,1,0:T(8,128)(2,1)S(1)}, bf16[2,64,256]{2,1,0:T(8,128)(2,1)S(1)}, u32[]{:S(2)}, u32[]{:S(2)}) collective-permute-start(bf16[2,64,256]{2,1,0:T(8,128)(2,1)S(1)} %get-tuple-element.56), channel_id=1, source_target_pairs={{0,8},{4,12},{8,0},{12,4},{1,9},{5,13},{9,1},{13,5},{2,10},{6,14},... | collective-permute-start | bytes 196616 | tf_op jit(solution)/shard_map/ppermute | solution.py:372
  47.4 0.0 collective-permute-done.12.refs_2_
  47.4 1.0 %collective-permute-done.13.refs_3_ = bf16[2,64,256]{2,1,0:T(8,128)(2,1)S(1)} collective-permute-done((bf16[2,64,256]{2,1,0:T(8,128)(2,1)S(1)}, bf16[2,64,256]{2,1,0:T(8,128)(2,1)S(1)}, u32[]{:S(2)}, u32[]{:S(2)}) %collective-permute-start.13) | collective-permute-done | bytes 65568 | tf_op jit(solution)/shard_map/ppermute | solution.py:372
  48.4 0.7 %place.2.refs_4_ = bf16[8,64,512]{2,1,0:T(8,128)(2,1)} custom-call(bf16[2,64,256]{2,1,0:T(8,128)(2,1)S(1)} %get-tuple-element.52.refs_0_, bf16[2,64,256]{2,1,0:T(8,128)(2,1)S(1)} %collective-permute-done.11.refs_1_, bf16[2,64,256]{2,1,0:T(8,128)(2,1)S(1)} %collective-permute-done.12.refs_2_, bf16[2,64,256]{2,1,0:T(8,128)(2,1)S(1)} %collective-permute-done.13.refs_3_), custom_call_target="tpu_custom_call" | custom-call | bytes 5242880 | tf_op jit(solution)/shard_map/place/pallas_call | solution.py:356
  49.1 0.2 collective-permute-done.10.refs_3_
  49.3 2.9 %collective-permute-done.8.refs_1_ = bf16[2,64,256]{2,1,0:T(8,128)(2,1)S(1)} collective-permute-done((bf16[2,64,256]{2,1,0:T(8,128)(2,1)S(1)}, bf16[2,64,256]{2,1,0:T(8,128)(2,1)S(1)}, u32[]{:S(2)}, u32[]{:S(2)}) %collective-permute-start.8) | collective-permute-done | bytes 65568 | tf_op jit(solution)/shard_map/ppermute | solution.py:372
  52.1 0.0 collective-permute-done.9.refs_2_
  52.1 0.7 %place.3 = bf16[8,64,512]{2,1,0:T(8,128)(2,1)} custom-call(bf16[2,64,256]{2,1,0:T(8,128)(2,1)S(1)} %get-tuple-element.54.refs_0_, bf16[2,64,256]{2,1,0:T(8,128)(2,1)S(1)} %collective-permute-done.8.refs_1_, bf16[2,64,256]{2,1,0:T(8,128)(2,1)S(1)} %collective-permute-done.9.refs_2_, ...), custom_call_target="tpu_custom_call", output_to_operand_aliasing={{}: (4, {})} | custom-call | bytes 5242880 | tf_op jit(solution)/shard_map/place/pallas_call | solution.py:356
Async XLA Ops:
  0.0 12.1 %collective-permute-start = (bf16[256,512]{1,0:T(8,128)(2,1)}, bf16[256,512]{1,0:T(8,128)(2,1)S(1)}, u32[]{:S(2)}, u32[]{:S(2)}) collective-permute-start(bf16[256,512]{1,0:T(8,128)(2,1)} %bitcast.8), channel_id=1, source_target_pairs={{0,2},{2,0},{1,3},{3,1},{4,6},{6,4},{5,7},{7,5},{8,10},{10,8},{9,1... | collective-permute-start | bytes 786440 | tf_op jit(solution)/shard_map/ppermute | solution.py:381
  2.9 14.6 %collective-permute-start.1 = (bf16[128,1024]{1,0:T(8,128)(2,1)}, bf16[128,1024]{1,0:T(8,128)(2,1)S(1)}, u32[]{:S(2)}, u32[]{:S(2)}) collective-permute-start(bf16[128,1024]{1,0:T(8,128)(2,1)} %refs_8_.1), channel_id=1, source_target_pairs={{0,8},{2,14},{4,12},{6,10},{8,0},{10,6},{12,4},{14,2},{1,9},{3,15}... | collective-permute-start | bytes 786440 | tf_op jit(solution)/shard_map/ppermute | solution.py:377
  10.4 12.0 %collective-permute-start.4 = (bf16[128,1024]{1,0:T(8,128)(2,1)S(1)}, bf16[128,1024]{1,0:T(8,128)(2,1)S(1)}, u32[]{:S(2)}, u32[]{:S(2)}) collective-permute-start(bf16[128,1024]{1,0:T(8,128)(2,1)S(1)} %get-tuple-element.44.refs_0_), channel_id=1, source_target_pairs={{0,4},{4,0},{8,12},{12,8},{1,5},{5,1},{9,13},{13,9},{2,6},{6,2},{1... | collective-permute-start | bytes 786440 | tf_op jit(solution)/shard_map/ppermute | solution.py:372
  17.5 7.1 %collective-permute-start.2 = (bf16[128,1024]{1,0:T(8,128)(2,1)S(1)}, bf16[128,1024]{1,0:T(8,128)(2,1)S(1)}, u32[]{:S(2)}, u32[]{:S(2)}) collective-permute-start(bf16[128,1024]{1,0:T(8,128)(2,1)S(1)} %collective-permute-done.1.refs_2_), channel_id=1, source_target_pairs={{0,2},{2,0},{1,3},{3,1},{4,6},{6,4},{5,7},{7,5},{8,10},{10,8},{9,1... | collective-permute-start | bytes 786440 | tf_op jit(solution)/shard_map/ppermute | solution.py:381
  23.4 3.3 %copy-start.1 = (s32[4,8]{1,0:T(4,128)S(1)}, s32[4,8]{1,0:T(4,128)}, u32[]{:S(2)}) copy-start(s32[4,8]{1,0:T(4,128)} %adjacency.1) | copy-start | bytes 388
  23.4 2.4 %collective-permute-start.5 = (bf16[384,1024]{1,0:T(8,128)(2,1)S(1)}, bf16[384,1024]{1,0:T(8,128)(2,1)S(1)}, u32[]{:S(2)}, u32[]{:S(2)}) collective-permute-start(bf16[384,1024]{1,0:T(8,128)(2,1)S(1)} %project.3), channel_id=1, source_target_pairs={{0,1},{1,0},{2,3},{3,2},{4,5},{5,4},{6,7},{7,6},{8,9},{9,8},{10,11... | collective-permute-start | bytes 2359304 | tf_op jit(solution)/shard_map/ppermute | solution.py:381
  25.1 1.6 %collective-permute-start.3 = (bf16[128,1024]{1,0:T(8,128)(2,1)S(1)}, bf16[128,1024]{1,0:T(8,128)(2,1)S(1)}, u32[]{:S(2)}, u32[]{:S(2)}) collective-permute-start(bf16[128,1024]{1,0:T(8,128)(2,1)S(1)} %project.2), channel_id=1, source_target_pairs={{0,1},{1,0},{2,3},{3,2},{4,5},{5,4},{6,7},{7,6},{8,9},{9,8},{10,11... | collective-permute-start | bytes 786440 | tf_op jit(solution)/shard_map/ppermute | solution.py:381
  29.8 6.4 %collective-permute-start.7 = (bf16[256,256]{1,0:T(8,128)(2,1)S(1)}, bf16[256,256]{1,0:T(8,128)(2,1)S(1)}, u32[]{:S(2)}, u32[]{:S(2)}) collective-permute-start(bf16[256,256]{1,0:T(8,128)(2,1)S(1)} %get-tuple-element.51), channel_id=1, source_target_pairs={{0,2},{2,0},{1,3},{3,1},{4,6},{6,4},{5,7},{7,5},{8,10},{10,8},{9,1... | collective-permute-start | bytes 393224 | tf_op jit(solution)/shard_map/ppermute | solution.py:381
  30.2 2.1 %copy-start.2 = (s32[4,1]{0,1:T(1,128)S(1)}, s32[4,1]{0,1:T(1,128)}, u32[]{:S(2)}) copy-start(s32[4,1]{0,1:T(1,128)} %param.12) | copy-start | bytes 52
  30.2 6.1 %copy-start = (bf16[4,64,512]{2,1,0:T(8,128)(2,1)S(1)}, bf16[4,64,512]{2,1,0:T(8,128)(2,1)}, u32[]{:S(2)}) copy-start(bf16[4,64,512]{2,1,0:T(8,128)(2,1)} %grid_features.3) | copy-start | bytes 786436
  30.5 11.7 %collective-permute-start.6 = (bf16[256,256]{1,0:T(8,128)(2,1)S(1)}, bf16[256,256]{1,0:T(8,128)(2,1)S(1)}, u32[]{:S(2)}, u32[]{:S(2)}) collective-permute-start(bf16[256,256]{1,0:T(8,128)(2,1)S(1)} %get-tuple-element.49), channel_id=1, source_target_pairs={{0,2},{2,0},{1,3},{3,1},{4,6},{6,4},{5,7},{7,5},{8,10},{10,8},{9,1... | collective-permute-start | bytes 393224 | tf_op jit(solution)/shard_map/ppermute | solution.py:381
  36.9 9.8 %collective-permute-start.11 = (bf16[2,64,256]{2,1,0:T(8,128)(2,1)S(1)}, bf16[2,64,256]{2,1,0:T(8,128)(2,1)S(1)}, u32[]{:S(2)}, u32[]{:S(2)}) collective-permute-start(bf16[2,64,256]{2,1,0:T(8,128)(2,1)S(1)} %get-tuple-element.58), channel_id=1, source_target_pairs={{0,4},{4,0},{8,12},{12,8},{1,5},{5,1},{9,13},{13,9},{2,6},{6,2},{1... | collective-permute-start | bytes 196616 | tf_op jit(solution)/shard_map/ppermute | solution.py:372
  38.9 8.5 %collective-permute-start.12 = (bf16[2,64,256]{2,1,0:T(8,128)(2,1)S(1)}, bf16[2,64,256]{2,1,0:T(8,128)(2,1)S(1)}, u32[]{:S(2)}, u32[]{:S(2)}) collective-permute-start(bf16[2,64,256]{2,1,0:T(8,128)(2,1)S(1)} %get-tuple-element.59), channel_id=1, source_target_pairs={{0,8},{4,12},{8,0},{12,4},{1,9},{5,13},{9,1},{13,5},{2,10},{6,14},... | collective-permute-start | bytes 196616 | tf_op jit(solution)/shard_map/ppermute | solution.py:372
  42.1 6.2 %collective-permute-start.13 = (bf16[2,64,256]{2,1,0:T(8,128)(2,1)S(1)}, bf16[2,64,256]{2,1,0:T(8,128)(2,1)S(1)}, u32[]{:S(2)}, u32[]{:S(2)}) collective-permute-start(bf16[2,64,256]{2,1,0:T(8,128)(2,1)S(1)} %get-tuple-element.60), channel_id=1, source_target_pairs={{0,12},{4,8},{8,4},{12,0},{1,13},{5,9},{9,5},{13,1},{2,14},{6,10},... | collective-permute-start | bytes 196616 | tf_op jit(solution)/shard_map/ppermute | solution.py:372
  42.9 6.4 %collective-permute-start.10 = (bf16[2,64,256]{2,1,0:T(8,128)(2,1)S(1)}, bf16[2,64,256]{2,1,0:T(8,128)(2,1)S(1)}, u32[]{:S(2)}, u32[]{:S(2)}) collective-permute-start(bf16[2,64,256]{2,1,0:T(8,128)(2,1)S(1)} %get-tuple-element.57), channel_id=1, source_target_pairs={{0,12},{4,8},{8,4},{12,0},{1,13},{5,9},{9,5},{13,1},{2,14},{6,10},... | collective-permute-start | bytes 196616 | tf_op jit(solution)/shard_map/ppermute | solution.py:372
  46.7 5.4 %collective-permute-start.8 = (bf16[2,64,256]{2,1,0:T(8,128)(2,1)S(1)}, bf16[2,64,256]{2,1,0:T(8,128)(2,1)S(1)}, u32[]{:S(2)}, u32[]{:S(2)}) collective-permute-start(bf16[2,64,256]{2,1,0:T(8,128)(2,1)S(1)} %get-tuple-element.55), channel_id=1, source_target_pairs={{0,4},{4,0},{8,12},{12,8},{1,5},{5,1},{9,13},{13,9},{2,6},{6,2},{1... | collective-permute-start | bytes 196616 | tf_op jit(solution)/shard_map/ppermute | solution.py:372
  46.8 5.4 %collective-permute-start.9 = (bf16[2,64,256]{2,1,0:T(8,128)(2,1)S(1)}, bf16[2,64,256]{2,1,0:T(8,128)(2,1)S(1)}, u32[]{:S(2)}, u32[]{:S(2)}) collective-permute-start(bf16[2,64,256]{2,1,0:T(8,128)(2,1)S(1)} %get-tuple-element.56), channel_id=1, source_target_pairs={{0,8},{4,12},{8,0},{12,4},{1,9},{5,13},{9,1},{13,5},{2,10},{6,14},... | collective-permute-start | bytes 196616 | tf_op jit(solution)/shard_map/ppermute | solution.py:372

commit v6 on v5

--- a/solution.py
+++ b/solution.py
@@ -95,6 +95,26 @@
         ),
         name="mlp",
     )(own, other, gain, wq, wup, wdn)
+
+
+def pick_kernel(mesh, out, sem):
+    first = pl.multiple_of(lax.axis_index("head") * BLOCK, BLOCK)
+    copy = pltpu.make_async_copy(mesh.at[pl.ds(first, BLOCK), :], out, sem)
+    copy.start()
+    copy.wait()
+
+
+def run_pick(mesh):
+    return pl.pallas_call(
+        pick_kernel,
+        out_shape=jax.ShapeDtypeStruct((BLOCK, mesh.shape[1]), mesh.dtype),
+        in_specs=[whole(pltpu.HBM)],
+        out_specs=whole(pltpu.VMEM),
+        scratch_shapes=[pltpu.SemaphoreType.DMA(())],
+        compiler_params=params(4),
+        cost_estimate=pl.CostEstimate(flops=0, bytes_accessed=4 * mesh.size, transcendentals=0),
+        name="pick",
+    )(in_hbm(mesh))
 
 
 def stage_kernel(axes, *refs):
@@ -152,8 +172,8 @@
         out_specs=whole(pltpu.VMEM),
         compiler_params=params(8),
         cost_estimate=pl.CostEstimate(
-            flops=80 * rows * depth * width,
-            bytes_accessed=80 * depth * width + 80 * rows * depth,
+            flops=800 * rows * depth * width,
+            bytes_accessed=800 * depth * width + 800 * rows * depth,
             transcendentals=0,
         ),
         name="project",
@@ -223,7 +243,7 @@
             part = lax.rem(m, 2)
             core = lax.rem(m // 2, 2)
             distance = s ^ (m // 4)
-            distance = jnp.where(distance <= 1, distance, 2 + ((distance - 2) ^ h))
+            part = jnp.where(distance <= 1, part, part ^ h)
             places.append((core ^ u, distance * 2 + part))
         for g in range(half // WIDE):
             columns = slice(g * WIDE, (g + 1) * WIDE)
@@ -292,39 +312,30 @@
     )(att, mlp, wo)
 
 
-def combine_kernel(c, owners, grid_features, keep, received, *outs):
-    s = lax.axis_index("shard")
+def combine_kernel(c, owners, grid_features, keep, received, out):
     count = grid_features.shape[0]
     width = keep.shape[1]
     names = [owners[t, 0] for t in range(count)]
-    for d, out in enumerate(outs):
-        for j in range(CAP):
-            out[j] = jnp.zeros(out.shape[1:], jnp.bfloat16)
-        seen = jnp.int32(0)
-        for t in range(count):
-            hit = names[t] == s ^ d
-            rank = seen
-
-            @pl.when(hit)
-            def _():
-                rows = slice(t * BLOCK, (t + 1) * BLOCK)
-                partials = keep[rows, :].astype(jnp.float32)
-                partials = partials + received[rows, :].astype(jnp.float32)
-                residual = grid_features[t, :, c * width : (c + 1) * width]
-                out[rank] = (residual.astype(jnp.float32) + partials).astype(jnp.bfloat16)
-
-            seen = seen + hit.astype(jnp.int32)
+    out[...] = jnp.zeros(out.shape, jnp.bfloat16)
+    for t in range(count):
+        rank = jnp.int32(0)
+        for earlier in range(t):
+            rank += (names[earlier] == names[t]).astype(jnp.int32)
+        rows = slice(t * BLOCK, (t + 1) * BLOCK)
+        partials = keep[rows, :].astype(jnp.float32) + received[rows, :].astype(jnp.float32)
+        residual = grid_features[t, :, c * width : (c + 1) * width]
+        updated = residual.astype(jnp.float32) + partials
+        out[names[t] * CAP + rank] = updated.astype(jnp.bfloat16)
 
 
 def run_combine(c, owners, grid_features, keep, received, shards):
     count, rows, _ = grid_features.shape
     width = keep.shape[1]
-    slot = jax.ShapeDtypeStruct((CAP, rows, width), jnp.bfloat16)
     return pl.pallas_call(
         functools.partial(combine_kernel, c),
-        out_shape=(slot,) * shards,
+        out_shape=jax.ShapeDtypeStruct((shards * CAP, rows, width), jnp.bfloat16),
         in_specs=[whole(pltpu.SMEM)] + vmem(3),
-        out_specs=tuple(vmem(shards)),
+        out_specs=whole(pltpu.VMEM),
         compiler_params=params(8),
         cost_estimate=pl.CostEstimate(
             flops=3000 * count * rows * width,
@@ -335,46 +346,33 @@
     )(owners, grid_features, keep, received)
 
 
-def place_kernel(c, *refs):
+def place_kernel(c, arrived, *refs):
     out, sem = refs[-2:]
-    s = lax.axis_index("shard")
-    copies = []
-    for d in range(sem.shape[0]):
-        width = refs[d].shape[2]
-        columns = pl.ds(c * width, width)
-        slots = pl.ds((s ^ d) * CAP, CAP)
-        copies.append(pltpu.make_async_copy(refs[d], out.at[slots, :, columns], sem.at[d]))
-        copies[d].start()
-    for copy in copies:
-        copy.wait()
+    width = arrived.shape[2]
+    copy = pltpu.make_async_copy(arrived, out.at[:, :, pl.ds(c * width, width)], sem)
+    copy.start()
+    copy.wait()
 
 
 def run_place(c, arrived, placed):
-    shards = len(arrived)
-    _, rows, width = arrived[0].shape
-    shape = (shards * CAP, rows, CHUNKS * width)
+    slots, rows, width = arrived.shape
     return pl.pallas_call(
         functools.partial(place_kernel, c),
-        out_shape=jax.ShapeDtypeStruct(shape, jnp.bfloat16),
-        in_specs=vmem(shards) + [whole(pltpu.HBM)] * len(placed),
+        out_shape=jax.ShapeDtypeStruct((slots, rows, CHUNKS * width), jnp.bfloat16),
+        in_specs=vmem(1) + [whole(pltpu.HBM)] * len(placed),
         out_specs=whole(pltpu.HBM),
-        scratch_shapes=[pltpu.SemaphoreType.DMA((shards,))],
-        input_output_aliases={shards: 0} if placed else {},
+        scratch_shapes=[pltpu.SemaphoreType.DMA(())],
+        input_output_aliases={1: 0} if placed else {},
         compiler_params=params(4),
         cost_estimate=pl.CostEstimate(
-            flops=0, bytes_accessed=40 * CAP * shards * rows * width, transcendentals=0
+            flops=0, bytes_accessed=40 * slots * rows * width, transcendentals=0
         ),
         name="place",
-    )(*arrived, *placed)
+    )(arrived, *placed)
 
 
 def crossed(x, distance, size):
     return lax.ppermute(x, "shard", [(i, i ^ distance) for i in range(size)])
-
-
-def fetched(x, size):
-    pairs = [(2 * i + h, 2 * (i ^ (2 + h)) + h) for i in range(size) for h in range(2)]
-    return lax.ppermute(x, ("shard", "head"), pairs)
 
 
 def swapped(x, axis):
@@ -397,7 +395,7 @@
     shards = lax.axis_size("shard")
     count, rows, half = grid_features.shape
     flat = grid_features.reshape(count * rows, half)
-    far = fetched(mesh_nodes, shards)
+    far = crossed(run_pick(mesh_nodes), 2, shards)
     other = swapped(flat, "head")
     staged = run_stage(
         (
@@ -415,14 +413,16 @@
     )
     flat, gain, wq, wup, wdn, wo, wk, wv, mesh = staged
     near = crossed(mesh, 1, shards)
+    farther = crossed(far, 1, shards)
+    far_pair = swapped(far, "head")
     queries, mlp = run_mlp(flat, other, gain, wq, wup, wdn)
-    queries, mlp, far = lax.optimization_barrier((queries, mlp, far))
-    farther = swapped(far, "head")
+    queries, mlp, farther = lax.optimization_barrier((queries, mlp, farther))
+    farther_pair = swapped(farther, "head")
     blocked = (-1, BLOCK, 2 * half)
-    mine_a = run_project((mesh, near, far), wk, wv)
+    mine_a = run_project((mesh, near, far, far_pair, farther), wk, wv)
     sibling_a = swapped(mine_a, "sub")
     table = run_table(mine_a.reshape(blocked), sibling_a.reshape(blocked), 2 * shards)
-    mine_b = run_project((farther,), wk, wv)
+    mine_b = run_project((farther_pair,), wk, wv)
     sibling_b = swapped(mine_b, "sub")
     send, keep, att = run_attend(
         adjacency, queries, mine_b.reshape(blocked), sibling_b.reshape(blocked), table, mlp, wo
@@ -434,9 +434,9 @@
             send, keep = run_project_out(c, att, mlp, wo)
         received = swapped(send, "head")
         if slots is not None:
-            received, _ = lax.optimization_barrier((received, slots[0]))
+            received, _ = lax.optimization_barrier((received, slots))
         slots = run_combine(c, owners, grid_features, keep, received, shards)
-        arrived = [slots[0]] + [crossed(slots[d], d, shards) for d in range(1, shards)]
+        arrived = lax.all_to_all(slots, "shard", split_axis=0, concat_axis=0, tiled=True)
         placed = [run_place(c, arrived, placed)]
     return placed[0]
 

time: 53 us -> 64.3 us (1.21)
  waiting for transfers between devices: 17.4 us -> 25.2 us
  Pallas kernels: 16 us -> 20.8 us
  starting transfers between devices: 19.2 us -> 17.8 us
    all_to_all x0 -> x2, waiting for transfers between devices: none -> 7.89 us  [paired(): lax.all_to_all(slots, 'shard', split_axis=0, concat_axis=0, tiled=True)]
    all_to_all x0 -> x2, starting transfers between devices: none -> 7.67 us  [paired(): lax.all_to_all(slots, 'shard', split_axis=0, concat_axis=0, tiled=True)]
    ppermute x7 -> x3, starting transfers between devices: 11.4 us -> 4.75 us  [crossed(): return lax.ppermute(x, 'shard', [(i, i ^ distance) for i in range(size)])]
    ppermute x6 -> x7, waiting for transfers between devices: 6.36 us -> 12.8 us  [swapped(): return lax.ppermute(x, axis, [(0, 1), (1, 0)])]
    ppermute x7 -> x3, waiting for transfers between devices: 8.92 us -> 4.5 us  [crossed(): return lax.ppermute(x, 'shard', [(i, i ^ distance) for i in range(size)])]
    ppermute x1 -> x0, starting transfers between devices: 2.59 us -> none  [fetched(): return lax.ppermute(x, ('shard', 'head'), pairs)]
    ppermute x1 -> x0, waiting for transfers between devices: 2.14 us -> none  [fetched(): return lax.ppermute(x, ('shard', 'head'), pairs)]
    pallas_call x2 -> x3, Pallas kernels: 1.41 us -> 3.55 us  [the longest x2 2.64 us: run_combine(): pl.pallas_call(functools.partial(combine_kernel, c), out_shape=jax.ShapeD...]
  transfers between devices with their start and end apart: 14 -> 12, of which waited for: 9 -> 7; matrix products, arithmetic and copies ran while one was open for 0% -> 0% of each run, Pallas kernels for 23% -> 24%
where the time goes in v6:
time: 64.3 us; the launch traced here: 64 us
  waiting for transfers between devices  25.2 us (39%)
  Pallas kernels  20.8 us (32%)
  starting transfers between devices  17.8 us (28%)
    ppermute x7, waiting for transfers between devices, swapped(): return lax.ppermute(x, axis, [(0, 1), (1, 0)])  12.8 us
    all_to_all x2, waiting for transfers between devices, paired(): lax.all_to_all(slots, 'shard', split_axis=0, concat_axis=0, tiled=True)  7.89 us
    all_to_all x2, starting transfers between devices, paired(): lax.all_to_all(slots, 'shard', split_axis=0, concat_axis=0, tiled=True)  7.67 us
    ppermute x7, starting transfers between devices, swapped(): return lax.ppermute(x, axis, [(0, 1), (1, 0)])  5.35 us
    pallas_call x1, Pallas kernels, run_stage(): pl.pallas_call(functools.partial(stage_kernel, axes), out_shape=tuple((ja...  4.87 us
    ppermute x3, starting transfers between devices, crossed(): return lax.ppermute(x, 'shard', [(i, i ^ distance) for i in range(size)])  4.75 us
    ppermute x3, waiting for transfers between devices, crossed(): return lax.ppermute(x, 'shard', [(i, i ^ distance) for i in range(size)])  4.5 us
    pallas_call x1, Pallas kernels, run_attend(): pl.pallas_call(attend_kernel, out_shape=(part, part, jax.ShapeDtypeStruct...  3.43 us
  transfers between devices with their start and end apart: 12, of which 7 were waited for; matrix products, arithmetic and copies ran while one was open for 0% of the time, Pallas kernels for 24%

profile of v6, /device:TPU:0, one launch (start us, length us, event | category | flops | bytes accessed | tf_op | source)
XLA Modules:
  0.0 64.0 jit_solution(1791727334725786221)
XLA Ops:
  0.0 2.9 %collective-permute-start = (bf16[256,512]{1,0:T(8,128)(2,1)}, bf16[256,512]{1,0:T(8,128)(2,1)S(1)}, u32[]{:S(2)}, u32[]{:S(2)}) collective-permute-start(bf16[256,512]{1,0:T(8,128)(2,1)} %bitcast.6), channel_id=1, source_target_pairs={{0,2},{2,0},{1,3},{3,1},{4,6},{6,4},{5,7},{7,5},{8,10},{10,8},{9,1... | collective-permute-start | bytes 786440 | tf_op jit(solution)/shard_map/ppermute | solution.py:379
  2.9 0.9 %pick.1 = bf16[64,1024]{1,0:T(8,128)(2,1)S(1)} custom-call(bf16[128,1024]{1,0:T(8,128)(2,1)} %mesh.1), custom_call_target="tpu_custom_call" | custom-call | bytes 524288 | tf_op jit(solution)/shard_map/pick/pallas_call | solution.py:108
  3.9 2.7 %collective-permute-start.1 = (bf16[64,1024]{1,0:T(8,128)(2,1)S(1)}, bf16[64,1024]{1,0:T(8,128)(2,1)S(1)}, u32[]{:S(2)}, u32[]{:S(2)}) collective-permute-start(bf16[64,1024]{1,0:T(8,128)(2,1)S(1)} %pick.1), channel_id=1, source_target_pairs={{0,8},{4,12},{8,0},{12,4},{1,9},{5,13},{9,1},{13,5},{2,10},{6,14},... | collective-permute-start | bytes 393224 | tf_op jit(solution)/shard_map/ppermute | solution.py:375
  6.5 4.9 %stage.1 = (bf16[256,512]{1,0:T(8,128)(2,1)S(1)}, f32[1,1024]{1,0:T(1,128)S(1)}, bf16[1024,512]{1,0:T(8,128)(2,1)S(1)}, bf16[1024,2048]{1,0:T(8,128)(2,1)S(1)}, ...) custom-call(bf16[256,512]{1,0:T(8,128)(2,1)} %bitcast.7, ...), custom_call_target="tpu_custom_call" | custom-call | bytes 262184960 | tf_op jit(solution)/shard_map/stage/pallas_call | solution.py:145
  11.4 1.6 %collective-permute-start.5 = (bf16[128,1024]{1,0:T(8,128)(2,1)S(1)}, bf16[128,1024]{1,0:T(8,128)(2,1)S(1)}, u32[]{:S(2)}, u32[]{:S(2)}) collective-permute-start(bf16[128,1024]{1,0:T(8,128)(2,1)S(1)} %get-tuple-element.36.refs_0_), channel_id=1, source_target_pairs={{0,4},{4,0},{8,12},{12,8},{1,5},{5,1},{9,13},{13,9},{2,6},{6,2},{1... | collective-permute-start | bytes 786440 | tf_op jit(solution)/shard_map/ppermute | solution.py:375
  13.0 0.0 collective-permute-done.1.refs_2_
  13.0 0.5 collective-permute-start.2
  13.5 0.5 collective-permute-start.6
  14.0 0.0 collective-permute-done.other
  14.0 3.3 %mlp.1 = (bf16[256,512]{1,0:T(8,128)(2,1)S(1)}, f32[256,1024]{1,0:T(8,128)S(1)}) custom-call(bf16[256,512]{1,0:T(8,128)(2,1)S(1)} %get-tuple-element.25.own, bf16[256,512]{1,0:T(8,128)(2,1)S(1)} %collective-permute-done.other, f32[1,1024]{1,0:T(1,128)S(1)} %get-tuple-element.26.gain, bf16[1024,512]{1,0:T(8,128)(2,1)S(1)} %get-tuple-element.27.wq, ...), custom_call_target="tpu_custom_call" | custom-call | flops 2415919104 | bytes 9437184 | tf_op jit(solution)/shard_map/mlp/pallas_call | solution.py:81
  17.4 4.5 %collective-permute-done.2.refs_4_ = bf16[64,1024]{1,0:T(8,128)(2,1)} collective-permute-done((bf16[64,1024]{1,0:T(8,128)(2,1)S(1)}, bf16[64,1024]{1,0:T(8,128)(2,1)}, u32[]{:S(2)}, u32[]{:S(2)}) %collective-permute-start.2) | collective-permute-done | bytes 131104 | tf_op jit(solution)/shard_map/ppermute | solution.py:375
  21.9 0.5 collective-permute-start.3
  22.4 0.0 collective-permute-done.5.refs_1_
  22.4 0.0 collective-permute-done.6.refs_3_
  22.4 2.0 %project.3 = bf16[448,1024]{1,0:T(8,128)(2,1)S(1)} custom-call(bf16[128,1024]{1,0:T(8,128)(2,1)S(1)} %get-tuple-element.36.refs_0_, bf16[128,1024]{1,0:T(8,128)(2,1)S(1)} %collective-permute-done.5.refs_1_, bf16[64,1024]{1,0:T(8,128)(2,1)S(1)} %collective-permute-done.1.refs_2_, bf16[64,1024]{1,0:T(8,128)(2,1)S(1)} %collective-permute-done.6.refs_3_, ...), custom_call_target="tpu_custom_call" | custom-call | flops 187904819200 | bytes 786432000 | tf_op jit(solution)/shard_map/project/pallas_call | solution.py:168
  24.5 0.0 copy-start.1
  24.5 0.1 collective-permute-start.7
  24.5 2.6 %collective-permute-done.3.refs_0_ = bf16[64,1024]{1,0:T(8,128)(2,1)} collective-permute-done((bf16[64,1024]{1,0:T(8,128)(2,1)}, bf16[64,1024]{1,0:T(8,128)(2,1)}, u32[]{:S(2)}, u32[]{:S(2)}) %collective-permute-start.3) | collective-permute-done | bytes 131104 | tf_op jit(solution)/shard_map/ppermute | solution.py:379
  27.1 1.4 %project.2 = bf16[64,1024]{1,0:T(8,128)(2,1)S(1)} custom-call(bf16[64,1024]{1,0:T(8,128)(2,1)} %collective-permute-done.3.refs_0_, bf16[1024,512]{1,0:T(8,128)(2,1)S(1)} %get-tuple-element.34.refs_1_.refs_5_, bf16[1024,512]{1,0:T(8,128)(2,1)S(1)} %get-tuple-element.35.refs_2_.refs_6_), custom_call_target="tpu_custom_call" | custom-call | flops 26843545600 | bytes 471859200 | tf_op jit(solution)/shard_map/project/pallas_call | solution.py:168
  28.5 0.1 collective-permute-start.4
  28.6 0.0 collective-permute-done.7
  28.6 0.5 table.1.table_in
  29.1 0.8 %collective-permute-done.4 = bf16[64,1024]{1,0:T(8,128)(2,1)S(1)} collective-permute-done((bf16[64,1024]{1,0:T(8,128)(2,1)S(1)}, bf16[64,1024]{1,0:T(8,128)(2,1)S(1)}, u32[]{:S(2)}, u32[]{:S(2)}) %collective-permute-start.4) | collective-permute-done | bytes 131104 | tf_op jit(solution)/shard_map/ppermute | solution.py:379
  29.9 0.0 copy-done.1
  29.9 0.0 copy-start.2
  29.9 0.0 copy-start
  30.0 3.4 %attend.1 = (bf16[256,256]{1,0:T(8,128)(2,1)S(1)}, bf16[256,256]{1,0:T(8,128)(2,1)S(1)}, bf16[256,512]{1,0:T(8,128)(2,1)S(1)}, bf16[2,8,64,1024]{3,2,1,0:T(8,128)(2,1)S(1)}) custom-call(s32[4,8]{1,0:T(4,128)S(1)} %copy-done.1, bf16[256,512]{1,0:T(8,128)(2,1)S(1)} %get-tuple-element.32.q, ...), custom_call_target="tpu_custom_call", output_to_operand_aliasing={{3}: (4, {})} | custom-call | flops 13421772800 | bytes 41943040 | tf_op jit(solution)/shard_map/attend/pallas_call | solution.py:274
  33.4 0.6 collective-permute-start.9
  34.0 0.0 copy-done.2
  34.0 0.1 copy.15.owners
  34.1 4.9 %collective-permute-done.9.received = bf16[256,256]{1,0:T(8,128)(2,1)S(1)} collective-permute-done((bf16[256,256]{1,0:T(8,128)(2,1)S(1)}, bf16[256,256]{1,0:T(8,128)(2,1)S(1)}, u32[]{:S(2)}, u32[]{:S(2)}) %collective-permute-start.9) | collective-permute-done | bytes 131104 | tf_op jit(solution)/shard_map/ppermute | solution.py:379
  39.0 0.0 copy-done
  39.0 1.3 %combine.2 = bf16[8,64,256]{2,1,0:T(8,128)(2,1)} custom-call(s32[4,1]{1,0:T(4,128)S(1)} %copy.15.owners, bf16[4,64,512]{2,1,0:T(8,128)(2,1)S(1)} %copy-done, bf16[256,256]{1,0:T(8,128)(2,1)S(1)} %get-tuple-element.42.keep, bf16[256,256]{1,0:T(8,128)(2,1)S(1)} %collective-permute-done.9.received), custom_call_target="tpu_custom_call" | custom-call | flops 196608000 | bytes 131072000 | tf_op jit(solution)/shard_map/combine/pallas_call | solution.py:334
  40.3 4.3 %all-to-all-start.1 = ((bf16[8,64,256]{2,1,0:T(8,128)(2,1)}), bf16[8,64,256]{2,1,0:T(8,128)(2,1)S(1)}, u32[]{:S(2)}, u32[]{:S(2)}) async-start(bf16[8,64,256]{2,1,0:T(8,128)(2,1)} %combine.2), calls=%async_computation.1 | async-start | bytes 524288 | tf_op jit(solution)/shard_map/all_to_all | solution.py:439
  44.6 0.3 project_out.1
  44.9 0.6 collective-permute-start.8
  45.5 4.4 %collective-permute-done.8.received = bf16[256,256]{1,0:T(8,128)(2,1)S(1)} collective-permute-done((bf16[256,256]{1,0:T(8,128)(2,1)S(1)}, bf16[256,256]{1,0:T(8,128)(2,1)S(1)}, u32[]{:S(2)}, u32[]{:S(2)}) %collective-permute-start.8) | collective-permute-done | bytes 131104 | tf_op jit(solution)/shard_map/ppermute | solution.py:379
  49.9 1.3 %combine.3 = bf16[8,64,256]{2,1,0:T(8,128)(2,1)} custom-call(s32[4,1]{1,0:T(4,128)S(1)} %copy.15.owners, bf16[4,64,512]{2,1,0:T(8,128)(2,1)S(1)} %copy-done, bf16[256,256]{1,0:T(8,128)(2,1)S(1)} %get-tuple-element.40.keep, bf16[256,256]{1,0:T(8,128)(2,1)S(1)} %collective-permute-done.8.received), custom_call_target="tpu_custom_call" | custom-call | flops 196608000 | bytes 131072000 | tf_op jit(solution)/shard_map/combine/pallas_call | solution.py:334
  51.3 1.7 %all-to-all-done.1.arrived = bf16[8,64,256]{2,1,0:T(8,128)(2,1)S(1)} async-done(((bf16[8,64,256]{2,1,0:T(8,128)(2,1)}), bf16[8,64,256]{2,1,0:T(8,128)(2,1)S(1)}, u32[]{:S(2)}, u32[]{:S(2)}) %all-to-all-start.1) | async-done | bytes 262176 | tf_op jit(solution)/shard_map/all_to_all | solution.py:439
  53.0 3.4 %all-to-all-start = ((bf16[8,64,256]{2,1,0:T(8,128)(2,1)}), bf16[8,64,256]{2,1,0:T(8,128)(2,1)S(1)}, u32[]{:S(2)}, u32[]{:S(2)}) async-start(bf16[8,64,256]{2,1,0:T(8,128)(2,1)} %combine.3), calls=%async_computation | async-start | bytes 524288 | tf_op jit(solution)/shard_map/all_to_all | solution.py:439
  56.4 0.7 %place.2.refs_0_ = bf16[8,64,512]{2,1,0:T(8,128)(2,1)} custom-call(bf16[8,64,256]{2,1,0:T(8,128)(2,1)S(1)} %all-to-all-done.1.arrived), custom_call_target="tpu_custom_call" | custom-call | bytes 5242880 | tf_op jit(solution)/shard_map/place/pallas_call | solution.py:359
  57.1 6.2 %all-to-all-done.arrived = bf16[8,64,256]{2,1,0:T(8,128)(2,1)S(1)} async-done(((bf16[8,64,256]{2,1,0:T(8,128)(2,1)}), bf16[8,64,256]{2,1,0:T(8,128)(2,1)S(1)}, u32[]{:S(2)}, u32[]{:S(2)}) %all-to-all-start) | async-done | bytes 262176 | tf_op jit(solution)/shard_map/all_to_all | solution.py:439
  63.3 0.7 %place.3 = bf16[8,64,512]{2,1,0:T(8,128)(2,1)} custom-call(bf16[8,64,256]{2,1,0:T(8,128)(2,1)S(1)} %all-to-all-done.arrived, bf16[8,64,512]{2,1,0:T(8,128)(2,1)} %place.2.refs_0_), custom_call_target="tpu_custom_call", output_to_operand_aliasing={{}: (1, {})} | custom-call | bytes 5242880 | tf_op jit(solution)/shard_map/place/pallas_call | solution.py:359
Async XLA Ops:
  0.0 14.0 %collective-permute-start = (bf16[256,512]{1,0:T(8,128)(2,1)}, bf16[256,512]{1,0:T(8,128)(2,1)S(1)}, u32[]{:S(2)}, u32[]{:S(2)}) collective-permute-start(bf16[256,512]{1,0:T(8,128)(2,1)} %bitcast.6), channel_id=1, source_target_pairs={{0,2},{2,0},{1,3},{3,1},{4,6},{6,4},{5,7},{7,5},{8,10},{10,8},{9,1... | collective-permute-start | bytes 786440 | tf_op jit(solution)/shard_map/ppermute | solution.py:379
  3.9 9.2 %collective-permute-start.1 = (bf16[64,1024]{1,0:T(8,128)(2,1)S(1)}, bf16[64,1024]{1,0:T(8,128)(2,1)S(1)}, u32[]{:S(2)}, u32[]{:S(2)}) collective-permute-start(bf16[64,1024]{1,0:T(8,128)(2,1)S(1)} %pick.1), channel_id=1, source_target_pairs={{0,8},{4,12},{8,0},{12,4},{1,9},{5,13},{9,1},{13,5},{2,10},{6,14},... | collective-permute-start | bytes 393224 | tf_op jit(solution)/shard_map/ppermute | solution.py:375
  11.4 11.0 %collective-permute-start.5 = (bf16[128,1024]{1,0:T(8,128)(2,1)S(1)}, bf16[128,1024]{1,0:T(8,128)(2,1)S(1)}, u32[]{:S(2)}, u32[]{:S(2)}) collective-permute-start(bf16[128,1024]{1,0:T(8,128)(2,1)S(1)} %get-tuple-element.36.refs_0_), channel_id=1, source_target_pairs={{0,4},{4,0},{8,12},{12,8},{1,5},{5,1},{9,13},{13,9},{2,6},{6,2},{1... | collective-permute-start | bytes 786440 | tf_op jit(solution)/shard_map/ppermute | solution.py:375
  13.0 8.8 %collective-permute-start.2 = (bf16[64,1024]{1,0:T(8,128)(2,1)S(1)}, bf16[64,1024]{1,0:T(8,128)(2,1)}, u32[]{:S(2)}, u32[]{:S(2)}) collective-permute-start(bf16[64,1024]{1,0:T(8,128)(2,1)S(1)} %collective-permute-done.1.refs_2_), channel_id=1, source_target_pairs={{0,4},{4,0},{8,12},{12,8},{1,5},{5,1},{9,13},{13,9},{2,6},{6,2},{1... | collective-permute-start | bytes 393224 | tf_op jit(solution)/shard_map/ppermute | solution.py:375
  13.5 8.9 %collective-permute-start.6 = (bf16[64,1024]{1,0:T(8,128)(2,1)S(1)}, bf16[64,1024]{1,0:T(8,128)(2,1)S(1)}, u32[]{:S(2)}, u32[]{:S(2)}) collective-permute-start(bf16[64,1024]{1,0:T(8,128)(2,1)S(1)} %collective-permute-done.1.refs_2_), channel_id=1, source_target_pairs={{0,2},{2,0},{1,3},{3,1},{4,6},{6,4},{5,7},{7,5},{8,10},{10,8},{9,1... | collective-permute-start | bytes 393224 | tf_op jit(solution)/shard_map/ppermute | solution.py:379
  21.9 5.3 %collective-permute-start.3 = (bf16[64,1024]{1,0:T(8,128)(2,1)}, bf16[64,1024]{1,0:T(8,128)(2,1)}, u32[]{:S(2)}, u32[]{:S(2)}) collective-permute-start(bf16[64,1024]{1,0:T(8,128)(2,1)} %collective-permute-done.2.refs_4_), channel_id=1, source_target_pairs={{0,2},{2,0},{1,3},{3,1},{4,6},{6,4},{5,7},{7,5},{8,10},{10,8},{9,1... | collective-permute-start | bytes 393224 | tf_op jit(solution)/shard_map/ppermute | solution.py:379
  24.5 5.5 %copy-start.1 = (s32[4,8]{1,0:T(4,128)S(1)}, s32[4,8]{1,0:T(4,128)}, u32[]{:S(2)}) copy-start(s32[4,8]{1,0:T(4,128)} %adjacency.1) | copy-start | bytes 388
  24.5 4.1 %collective-permute-start.7 = (bf16[448,1024]{1,0:T(8,128)(2,1)S(1)}, bf16[448,1024]{1,0:T(8,128)(2,1)S(1)}, u32[]{:S(2)}, u32[]{:S(2)}) collective-permute-start(bf16[448,1024]{1,0:T(8,128)(2,1)S(1)} %project.3), channel_id=1, source_target_pairs={{0,1},{1,0},{2,3},{3,2},{4,5},{5,4},{6,7},{7,6},{8,9},{9,8},{10,11... | collective-permute-start | bytes 2752520 | tf_op jit(solution)/shard_map/ppermute | solution.py:379
  28.5 1.4 %collective-permute-start.4 = (bf16[64,1024]{1,0:T(8,128)(2,1)S(1)}, bf16[64,1024]{1,0:T(8,128)(2,1)S(1)}, u32[]{:S(2)}, u32[]{:S(2)}) collective-permute-start(bf16[64,1024]{1,0:T(8,128)(2,1)S(1)} %project.2), channel_id=1, source_target_pairs={{0,1},{1,0},{2,3},{3,2},{4,5},{5,4},{6,7},{7,6},{8,9},{9,8},{10,11... | collective-permute-start | bytes 393224 | tf_op jit(solution)/shard_map/ppermute | solution.py:379
  29.9 4.0 %copy-start.2 = (s32[4,1]{0,1:T(1,128)S(1)}, s32[4,1]{0,1:T(1,128)}, u32[]{:S(2)}) copy-start(s32[4,1]{0,1:T(1,128)} %param.12) | copy-start | bytes 52
  29.9 9.1 %copy-start = (bf16[4,64,512]{2,1,0:T(8,128)(2,1)S(1)}, bf16[4,64,512]{2,1,0:T(8,128)(2,1)}, u32[]{:S(2)}) copy-start(bf16[4,64,512]{2,1,0:T(8,128)(2,1)} %grid_features.3) | copy-start | bytes 786436
  33.4 5.6 %collective-permute-start.9 = (bf16[256,256]{1,0:T(8,128)(2,1)S(1)}, bf16[256,256]{1,0:T(8,128)(2,1)S(1)}, u32[]{:S(2)}, u32[]{:S(2)}) collective-permute-start(bf16[256,256]{1,0:T(8,128)(2,1)S(1)} %get-tuple-element.43), channel_id=1, source_target_pairs={{0,2},{2,0},{1,3},{3,1},{4,6},{6,4},{5,7},{7,5},{8,10},{10,8},{9,1... | collective-permute-start | bytes 393224 | tf_op jit(solution)/shard_map/ppermute | solution.py:379
  40.3 12.6 %all-to-all-start.1 = ((bf16[8,64,256]{2,1,0:T(8,128)(2,1)}), bf16[8,64,256]{2,1,0:T(8,128)(2,1)S(1)}, u32[]{:S(2)}, u32[]{:S(2)}) async-start(bf16[8,64,256]{2,1,0:T(8,128)(2,1)} %combine.2), calls=%async_computation.1 | async-start | bytes 524288 | tf_op jit(solution)/shard_map/all_to_all | solution.py:439
  44.9 5.0 %collective-permute-start.8 = (bf16[256,256]{1,0:T(8,128)(2,1)S(1)}, bf16[256,256]{1,0:T(8,128)(2,1)S(1)}, u32[]{:S(2)}, u32[]{:S(2)}) collective-permute-start(bf16[256,256]{1,0:T(8,128)(2,1)S(1)} %get-tuple-element.41), channel_id=1, source_target_pairs={{0,2},{2,0},{1,3},{3,1},{4,6},{6,4},{5,7},{7,5},{8,10},{10,8},{9,1... | collective-permute-start | bytes 393224 | tf_op jit(solution)/shard_map/ppermute | solution.py:379
  53.0 10.3 %all-to-all-start = ((bf16[8,64,256]{2,1,0:T(8,128)(2,1)}), bf16[8,64,256]{2,1,0:T(8,128)(2,1)S(1)}, u32[]{:S(2)}, u32[]{:S(2)}) async-start(bf16[8,64,256]{2,1,0:T(8,128)(2,1)} %combine.3), calls=%async_computation | async-start | bytes 524288 | tf_op jit(solution)/shard_map/all_to_all | solution.py:439

commit v7 on v5

--- a/solution.py
+++ b/solution.py
@@ -95,6 +95,26 @@
         ),
         name="mlp",
     )(own, other, gain, wq, wup, wdn)
+
+
+def pick_kernel(mesh, out, sem):
+    first = pl.multiple_of(lax.axis_index("head") * BLOCK, BLOCK)
+    copy = pltpu.make_async_copy(mesh.at[pl.ds(first, BLOCK), :], out, sem)
+    copy.start()
+    copy.wait()
+
+
+def run_pick(mesh):
+    return pl.pallas_call(
+        pick_kernel,
+        out_shape=jax.ShapeDtypeStruct((BLOCK, mesh.shape[1]), mesh.dtype),
+        in_specs=[whole(pltpu.HBM)],
+        out_specs=whole(pltpu.VMEM),
+        scratch_shapes=[pltpu.SemaphoreType.DMA(())],
+        compiler_params=params(4),
+        cost_estimate=pl.CostEstimate(flops=0, bytes_accessed=4 * mesh.size, transcendentals=0),
+        name="pick",
+    )(in_hbm(mesh))
 
 
 def stage_kernel(axes, *refs):
@@ -152,8 +172,8 @@
         out_specs=whole(pltpu.VMEM),
         compiler_params=params(8),
         cost_estimate=pl.CostEstimate(
-            flops=80 * rows * depth * width,
-            bytes_accessed=80 * depth * width + 80 * rows * depth,
+            flops=300 * rows * depth * width,
+            bytes_accessed=300 * depth * width + 300 * rows * depth,
             transcendentals=0,
         ),
         name="project",
@@ -223,7 +243,7 @@
             part = lax.rem(m, 2)
             core = lax.rem(m // 2, 2)
             distance = s ^ (m // 4)
-            distance = jnp.where(distance <= 1, distance, 2 + ((distance - 2) ^ h))
+            part = jnp.where(distance <= 1, part, part ^ h)
             places.append((core ^ u, distance * 2 + part))
         for g in range(half // WIDE):
             columns = slice(g * WIDE, (g + 1) * WIDE)
@@ -335,26 +355,26 @@
     )(owners, grid_features, keep, received)
 
 
-def place_kernel(c, *refs):
+def place_kernel(c, order, *refs):
     out, sem = refs[-2:]
     s = lax.axis_index("shard")
     copies = []
-    for d in range(sem.shape[0]):
-        width = refs[d].shape[2]
+    for i, d in enumerate(order):
+        width = refs[i].shape[2]
         columns = pl.ds(c * width, width)
         slots = pl.ds((s ^ d) * CAP, CAP)
-        copies.append(pltpu.make_async_copy(refs[d], out.at[slots, :, columns], sem.at[d]))
-        copies[d].start()
+        copies.append(pltpu.make_async_copy(refs[i], out.at[slots, :, columns], sem.at[i]))
+        copies[i].start()
     for copy in copies:
         copy.wait()
 
 
-def run_place(c, arrived, placed):
+def run_place(c, order, arrived, placed):
     shards = len(arrived)
     _, rows, width = arrived[0].shape
     shape = (shards * CAP, rows, CHUNKS * width)
     return pl.pallas_call(
-        functools.partial(place_kernel, c),
+        functools.partial(place_kernel, c, order),
         out_shape=jax.ShapeDtypeStruct(shape, jnp.bfloat16),
         in_specs=vmem(shards) + [whole(pltpu.HBM)] * len(placed),
         out_specs=whole(pltpu.HBM),
@@ -370,11 +390,6 @@
 
 def crossed(x, distance, size):
     return lax.ppermute(x, "shard", [(i, i ^ distance) for i in range(size)])
-
-
-def fetched(x, size):
-    pairs = [(2 * i + h, 2 * (i ^ (2 + h)) + h) for i in range(size) for h in range(2)]
-    return lax.ppermute(x, ("shard", "head"), pairs)
 
 
 def swapped(x, axis):
@@ -397,7 +412,8 @@
     shards = lax.axis_size("shard")
     count, rows, half = grid_features.shape
     flat = grid_features.reshape(count * rows, half)
-    far = fetched(mesh_nodes, shards)
+    far = crossed(run_pick(mesh_nodes), 2, shards)
+    near = crossed(mesh_nodes, 1, shards)
     other = swapped(flat, "head")
     staged = run_stage(
         (
@@ -414,15 +430,16 @@
         (None, 1, 0, 0, 1, 1, None, None, None),
     )
     flat, gain, wq, wup, wdn, wo, wk, wv, mesh = staged
-    near = crossed(mesh, 1, shards)
+    farther = crossed(far, 1, shards)
+    far_pair = swapped(far, "head")
     queries, mlp = run_mlp(flat, other, gain, wq, wup, wdn)
-    queries, mlp, far = lax.optimization_barrier((queries, mlp, far))
-    farther = swapped(far, "head")
+    queries, mlp, farther = lax.optimization_barrier((queries, mlp, farther))
+    farther_pair = swapped(farther, "head")
     blocked = (-1, BLOCK, 2 * half)
-    mine_a = run_project((mesh, near, far), wk, wv)
+    mine_a = run_project((mesh, near, far, far_pair, farther), wk, wv)
     sibling_a = swapped(mine_a, "sub")
     table = run_table(mine_a.reshape(blocked), sibling_a.reshape(blocked), 2 * shards)
-    mine_b = run_project((farther,), wk, wv)
+    mine_b = run_project((farther_pair,), wk, wv)
     sibling_b = swapped(mine_b, "sub")
     send, keep, att = run_attend(
         adjacency, queries, mine_b.reshape(blocked), sibling_b.reshape(blocked), table, mlp, wo
@@ -436,8 +453,9 @@
         if slots is not None:
             received, _ = lax.optimization_barrier((received, slots[0]))
         slots = run_combine(c, owners, grid_features, keep, received, shards)
-        arrived = [slots[0]] + [crossed(slots[d], d, shards) for d in range(1, shards)]
-        placed = [run_place(c, arrived, placed)]
+        order = (2, 3, 1, 0)
+        arrived = [crossed(slots[d], d, shards) if d else slots[d] for d in order]
+        placed = [run_place(c, order, arrived, placed)]
     return placed[0]
 
 

time: 53 us -> 50.8 us (0.958)
  waiting for transfers between devices: 17.4 us -> 13.5 us
  Pallas kernels: 16 us -> 17.8 us
    ppermute x7 -> x9, waiting for transfers between devices: 8.92 us -> 5.56 us  [crossed(): return lax.ppermute(x, 'shard', [(i, i ^ distance) for i in range(size)])]
    ppermute x1 -> x0, starting transfers between devices: 2.59 us -> none  [fetched(): return lax.ppermute(x, ('shard', 'head'), pairs)]
    ppermute x1 -> x0, waiting for transfers between devices: 2.14 us -> none  [fetched(): return lax.ppermute(x, ('shard', 'head'), pairs)]
    ppermute x6 -> x7, waiting for transfers between devices: 6.36 us -> 7.96 us  [swapped(): return lax.ppermute(x, axis, [(0, 1), (1, 0)])]
    ppermute x7 -> x9, starting transfers between devices: 11.4 us -> 12.8 us  [crossed(): return lax.ppermute(x, 'shard', [(i, i ^ distance) for i in range(size)])]
    ppermute x6 -> x7, starting transfers between devices: 5.24 us -> 6.26 us  [swapped(): return lax.ppermute(x, axis, [(0, 1), (1, 0)])]
    pallas_call x2 -> x3, Pallas kernels: 1.45 us -> 2.38 us  [the longest x2 1.47 us: run_place(): pl.pallas_call(functools.partial(place_kernel, c, order), out_shape=jax.S...]
  transfers between devices with their start and end apart: 14 -> 16, of which waited for: 9 -> 7; matrix products, arithmetic and copies ran while one was open for 0% -> 0% of each run, Pallas kernels for 23% -> 27%
where the time goes in v7:
time: 50.8 us; the launch traced here: 50.6 us
  starting transfers between devices  19.1 us (38%)
  Pallas kernels  17.8 us (35%)
  waiting for transfers between devices  13.5 us (27%)
    ppermute x9, starting transfers between devices, crossed(): return lax.ppermute(x, 'shard', [(i, i ^ distance) for i in range(size)])  12.8 us
    ppermute x7, waiting for transfers between devices, swapped(): return lax.ppermute(x, axis, [(0, 1), (1, 0)])  7.96 us
    ppermute x7, starting transfers between devices, swapped(): return lax.ppermute(x, axis, [(0, 1), (1, 0)])  6.26 us
    ppermute x9, waiting for transfers between devices, crossed(): return lax.ppermute(x, 'shard', [(i, i ^ distance) for i in range(size)])  5.56 us
    pallas_call x1, Pallas kernels, run_stage(): pl.pallas_call(functools.partial(stage_kernel, axes), out_shape=tuple((ja...  4.87 us
    pallas_call x1, Pallas kernels, run_attend(): pl.pallas_call(attend_kernel, out_shape=(part, part, jax.ShapeDtypeStruct...  3.44 us
    pallas_call x1, Pallas kernels, run_mlp(): pl.pallas_call(mlp_kernel, out_shape=(jax.ShapeDtypeStruct((rows, wq.shap...  3.33 us
    pallas_call x2, Pallas kernels, run_project(): pl.pallas_call(project_kernel, out_shape=jax.ShapeDtypeStruct((rows, 2 *...  1.59 us
  transfers between devices with their start and end apart: 16, of which 7 were waited for; matrix products, arithmetic and copies ran while one was open for 0% of the time, Pallas kernels for 27%

profile of v7, /device:TPU:0, one launch (start us, length us, event | category | flops | bytes accessed | tf_op | source)
XLA Modules:
  0.0 50.6 jit_solution(9774526007741830012)
XLA Ops:
  0.0 2.9 %collective-permute-start = (bf16[256,512]{1,0:T(8,128)(2,1)}, bf16[256,512]{1,0:T(8,128)(2,1)S(1)}, u32[]{:S(2)}, u32[]{:S(2)}) collective-permute-start(bf16[256,512]{1,0:T(8,128)(2,1)} %bitcast.8), channel_id=1, source_target_pairs={{0,2},{2,0},{1,3},{3,1},{4,6},{6,4},{5,7},{7,5},{8,10},{10,8},{9,1... | collective-permute-start | bytes 786440 | tf_op jit(solution)/shard_map/ppermute | solution.py:396
  2.9 0.9 %pick.1 = bf16[64,1024]{1,0:T(8,128)(2,1)S(1)} custom-call(bf16[128,1024]{1,0:T(8,128)(2,1)} %mesh.1), custom_call_target="tpu_custom_call" | custom-call | bytes 524288 | tf_op jit(solution)/shard_map/pick/pallas_call | solution.py:108
  3.9 2.7 %collective-permute-start.1 = (bf16[64,1024]{1,0:T(8,128)(2,1)S(1)}, bf16[64,1024]{1,0:T(8,128)(2,1)S(1)}, u32[]{:S(2)}, u32[]{:S(2)}) collective-permute-start(bf16[64,1024]{1,0:T(8,128)(2,1)S(1)} %pick.1), channel_id=1, source_target_pairs={{0,8},{4,12},{8,0},{12,4},{1,9},{5,13},{9,1},{13,5},{2,10},{6,14},... | collective-permute-start | bytes 393224 | tf_op jit(solution)/shard_map/ppermute | solution.py:392
  6.5 1.6 %collective-permute-start.5 = (bf16[128,1024]{1,0:T(8,128)(2,1)}, bf16[128,1024]{1,0:T(8,128)(2,1)S(1)}, u32[]{:S(2)}, u32[]{:S(2)}) collective-permute-start(bf16[128,1024]{1,0:T(8,128)(2,1)} %mesh.1), channel_id=1, source_target_pairs={{0,4},{4,0},{8,12},{12,8},{1,5},{5,1},{9,13},{13,9},{2,6},{6,2},{1... | collective-permute-start | bytes 786440 | tf_op jit(solution)/shard_map/ppermute | solution.py:392
  8.1 4.9 %stage.1 = (bf16[256,512]{1,0:T(8,128)(2,1)S(1)}, f32[1,1024]{1,0:T(1,128)S(1)}, bf16[1024,512]{1,0:T(8,128)(2,1)S(1)}, bf16[1024,2048]{1,0:T(8,128)(2,1)S(1)}, ...) custom-call(bf16[256,512]{1,0:T(8,128)(2,1)} %bitcast.9, ...), custom_call_target="tpu_custom_call" | custom-call | bytes 262184960 | tf_op jit(solution)/shard_map/stage/pallas_call | solution.py:145
  13.0 0.0 collective-permute-done.1.refs_2_
  13.0 0.5 %collective-permute-start.2 = (bf16[64,1024]{1,0:T(8,128)(2,1)S(1)}, bf16[64,1024]{1,0:T(8,128)(2,1)S(1)}, u32[]{:S(2)}, u32[]{:S(2)}) collective-permute-start(bf16[64,1024]{1,0:T(8,128)(2,1)S(1)} %collective-permute-done.1.refs_2_), channel_id=1, source_target_pairs={{0,4},{4,0},{8,12},{12,8},{1,5},{5,1},{9,13},{13,9},{2,6},{6,2},{1... | collective-permute-start | bytes 393224 | tf_op jit(solution)/shard_map/ppermute | solution.py:392
  13.5 0.5 %collective-permute-start.6 = (bf16[64,1024]{1,0:T(8,128)(2,1)S(1)}, bf16[64,1024]{1,0:T(8,128)(2,1)S(1)}, u32[]{:S(2)}, u32[]{:S(2)}) collective-permute-start(bf16[64,1024]{1,0:T(8,128)(2,1)S(1)} %collective-permute-done.1.refs_2_), channel_id=1, source_target_pairs={{0,2},{2,0},{1,3},{3,1},{4,6},{6,4},{5,7},{7,5},{8,10},{10,8},{9,1... | collective-permute-start | bytes 393224 | tf_op jit(solution)/shard_map/ppermute | solution.py:396
  14.0 0.0 collective-permute-done.other
  14.0 3.3 %mlp.1 = (bf16[256,512]{1,0:T(8,128)(2,1)S(1)}, f32[256,1024]{1,0:T(8,128)S(1)}) custom-call(bf16[256,512]{1,0:T(8,128)(2,1)S(1)} %get-tuple-element.33.own, bf16[256,512]{1,0:T(8,128)(2,1)S(1)} %collective-permute-done.other, f32[1,1024]{1,0:T(1,128)S(1)} %get-tuple-element.34.gain, bf16[1024,512]{1,0:T(8,128)(2,1)S(1)} %get-tuple-element.35.wq, ...), custom_call_target="tpu_custom_call" | custom-call | flops 2415919104 | bytes 9437184 | tf_op jit(solution)/shard_map/mlp/pallas_call | solution.py:81
  17.4 1.3 %collective-permute-done.2.refs_4_ = bf16[64,1024]{1,0:T(8,128)(2,1)S(1)} collective-permute-done((bf16[64,1024]{1,0:T(8,128)(2,1)S(1)}, bf16[64,1024]{1,0:T(8,128)(2,1)S(1)}, u32[]{:S(2)}, u32[]{:S(2)}) %collective-permute-start.2) | collective-permute-done | bytes 131104 | tf_op jit(solution)/shard_map/ppermute | solution.py:392
  18.7 0.5 collective-permute-start.3
  19.2 0.0 collective-permute-done.6.refs_3_
  19.2 0.0 collective-permute-done.5.refs_1_
  19.2 1.1 %project.3 = bf16[448,1024]{1,0:T(8,128)(2,1)S(1)} custom-call(bf16[128,1024]{1,0:T(8,128)(2,1)S(1)} %get-tuple-element.44.refs_0_, bf16[128,1024]{1,0:T(8,128)(2,1)S(1)} %collective-permute-done.5.refs_1_, bf16[64,1024]{1,0:T(8,128)(2,1)S(1)} %collective-permute-done.1.refs_2_, bf16[64,1024]{1,0:T(8,128)(2,1)S(1)} %collective-permute-done.6.refs_3_, ...), custom_call_target="tpu_custom_call" | custom-call | flops 70464307200 | bytes 294912000 | tf_op jit(solution)/shard_map/project/pallas_call | solution.py:168
  20.3 0.0 copy-start.1
  20.3 0.1 collective-permute-start.7
  20.4 3.3 %collective-permute-done.3.refs_0_ = bf16[64,1024]{1,0:T(8,128)(2,1)S(1)} collective-permute-done((bf16[64,1024]{1,0:T(8,128)(2,1)S(1)}, bf16[64,1024]{1,0:T(8,128)(2,1)S(1)}, u32[]{:S(2)}, u32[]{:S(2)}) %collective-permute-start.3) | collective-permute-done | bytes 131104 | tf_op jit(solution)/shard_map/ppermute | solution.py:396
  23.7 0.5 project.2
  24.2 0.1 collective-permute-start.4
  24.2 0.0 collective-permute-done.7
  24.3 0.5 table.1.table_in
  24.7 0.8 %collective-permute-done.4 = bf16[64,1024]{1,0:T(8,128)(2,1)S(1)} collective-permute-done((bf16[64,1024]{1,0:T(8,128)(2,1)S(1)}, bf16[64,1024]{1,0:T(8,128)(2,1)S(1)}, u32[]{:S(2)}, u32[]{:S(2)}) %collective-permute-start.4) | collective-permute-done | bytes 131104 | tf_op jit(solution)/shard_map/ppermute | solution.py:396
  25.6 0.0 copy-done.1
  25.6 3.4 %attend.1 = (bf16[256,256]{1,0:T(8,128)(2,1)S(1)}, bf16[256,256]{1,0:T(8,128)(2,1)S(1)}, bf16[256,512]{1,0:T(8,128)(2,1)S(1)}, bf16[2,8,64,1024]{3,2,1,0:T(8,128)(2,1)S(1)}) custom-call(s32[4,8]{1,0:T(4,128)S(1)} %copy-done.1, bf16[256,512]{1,0:T(8,128)(2,1)S(1)} %get-tuple-element.40.q, ...), custom_call_target="tpu_custom_call", output_to_operand_aliasing={{3}: (4, {})} | custom-call | flops 13421772800 | bytes 41943040 | tf_op jit(solution)/shard_map/attend/pallas_call | solution.py:274
  29.0 0.6 %collective-permute-start.9 = (bf16[256,256]{1,0:T(8,128)(2,1)S(1)}, bf16[256,256]{1,0:T(8,128)(2,1)S(1)}, u32[]{:S(2)}, u32[]{:S(2)}) collective-permute-start(bf16[256,256]{1,0:T(8,128)(2,1)S(1)} %get-tuple-element.51), channel_id=1, source_target_pairs={{0,2},{2,0},{1,3},{3,1},{4,6},{6,4},{5,7},{7,5},{8,10},{10,8},{9,1... | collective-permute-start | bytes 393224 | tf_op jit(solution)/shard_map/ppermute | solution.py:396
  29.6 0.0 copy-start.2
  29.6 0.0 copy-start
  29.6 0.3 project_out.1
  29.9 1.6 %collective-permute-start.8 = (bf16[256,256]{1,0:T(8,128)(2,1)S(1)}, bf16[256,256]{1,0:T(8,128)(2,1)S(1)}, u32[]{:S(2)}, u32[]{:S(2)}) collective-permute-start(bf16[256,256]{1,0:T(8,128)(2,1)S(1)} %get-tuple-element.49), channel_id=1, source_target_pairs={{0,2},{2,0},{1,3},{3,1},{4,6},{6,4},{5,7},{7,5},{8,10},{10,8},{9,1... | collective-permute-start | bytes 393224 | tf_op jit(solution)/shard_map/ppermute | solution.py:396
  31.5 0.0 copy-done.2
  31.5 0.1 copy.15.owners
  31.6 3.8 %collective-permute-done.9.received = bf16[256,256]{1,0:T(8,128)(2,1)S(1)} collective-permute-done((bf16[256,256]{1,0:T(8,128)(2,1)S(1)}, bf16[256,256]{1,0:T(8,128)(2,1)S(1)}, u32[]{:S(2)}, u32[]{:S(2)}) %collective-permute-start.9) | collective-permute-done | bytes 131104 | tf_op jit(solution)/shard_map/ppermute | solution.py:396
  35.4 0.0 copy-done
  35.4 0.7 %combine.2 = (bf16[2,64,256]{2,1,0:T(8,128)(2,1)S(1)}, bf16[2,64,256]{2,1,0:T(8,128)(2,1)S(1)}, bf16[2,64,256]{2,1,0:T(8,128)(2,1)S(1)}, bf16[2,64,256]{2,1,0:T(8,128)(2,1)S(1)}) custom-call(s32[4,1]{1,0:T(4,128)S(1)} %copy.15.owners, bf16[4,64,512]{2,1,0:T(8,128)(2,1)S(1)} %copy-done, bf16[256,256]{1,0:T(8,128)(2,1)S(1)} %get-tuple-element.50.keep, ...), custom_call_target="tpu_custom_call" | custom-call | flops 196608000 | bytes 131072000 | tf_op jit(solution)/shard_map/combine/pallas_call | solution.py:343
  36.1 2.1 %collective-permute-start.13 = (bf16[2,64,256]{2,1,0:T(8,128)(2,1)S(1)}, bf16[2,64,256]{2,1,0:T(8,128)(2,1)S(1)}, u32[]{:S(2)}, u32[]{:S(2)}) collective-permute-start(bf16[2,64,256]{2,1,0:T(8,128)(2,1)S(1)} %get-tuple-element.58), channel_id=1, source_target_pairs={{0,8},{4,12},{8,0},{12,4},{1,9},{5,13},{9,1},{13,5},{2,10},{6,14},... | collective-permute-start | bytes 196616 | tf_op jit(solution)/shard_map/ppermute | solution.py:392
  38.2 1.6 %collective-permute-start.14 = (bf16[2,64,256]{2,1,0:T(8,128)(2,1)S(1)}, bf16[2,64,256]{2,1,0:T(8,128)(2,1)S(1)}, u32[]{:S(2)}, u32[]{:S(2)}) collective-permute-start(bf16[2,64,256]{2,1,0:T(8,128)(2,1)S(1)} %get-tuple-element.59), channel_id=1, source_target_pairs={{0,12},{4,8},{8,4},{12,0},{1,13},{5,9},{9,5},{13,1},{2,14},{6,10},... | collective-permute-start | bytes 196616 | tf_op jit(solution)/shard_map/ppermute | solution.py:392
  39.8 0.0 collective-permute-start.15
  39.8 0.0 collective-permute-done.8.received
  39.8 0.7 %combine.3 = (bf16[2,64,256]{2,1,0:T(8,128)(2,1)S(1)}, bf16[2,64,256]{2,1,0:T(8,128)(2,1)S(1)}, bf16[2,64,256]{2,1,0:T(8,128)(2,1)S(1)}, bf16[2,64,256]{2,1,0:T(8,128)(2,1)S(1)}) custom-call(s32[4,1]{1,0:T(4,128)S(1)} %copy.15.owners, bf16[4,64,512]{2,1,0:T(8,128)(2,1)S(1)} %copy-done, bf16[256,256]{1,0:T(8,128)(2,1)S(1)} %get-tuple-element.48.keep, ...), custom_call_target="tpu_custom_call" | custom-call | flops 196608000 | bytes 131072000 | tf_op jit(solution)/shard_map/combine/pallas_call | solution.py:343
  40.5 2.9 %collective-permute-start.10 = (bf16[2,64,256]{2,1,0:T(8,128)(2,1)S(1)}, bf16[2,64,256]{2,1,0:T(8,128)(2,1)S(1)}, u32[]{:S(2)}, u32[]{:S(2)}) collective-permute-start(bf16[2,64,256]{2,1,0:T(8,128)(2,1)S(1)} %get-tuple-element.54), channel_id=1, source_target_pairs={{0,8},{4,12},{8,0},{12,4},{1,9},{5,13},{9,1},{13,5},{2,10},{6,14},... | collective-permute-start | bytes 196616 | tf_op jit(solution)/shard_map/ppermute | solution.py:392
  43.4 1.6 %collective-permute-start.11 = (bf16[2,64,256]{2,1,0:T(8,128)(2,1)S(1)}, bf16[2,64,256]{2,1,0:T(8,128)(2,1)S(1)}, u32[]{:S(2)}, u32[]{:S(2)}) collective-permute-start(bf16[2,64,256]{2,1,0:T(8,128)(2,1)S(1)} %get-tuple-element.55), channel_id=1, source_target_pairs={{0,12},{4,8},{8,4},{12,0},{1,13},{5,9},{9,5},{13,1},{2,14},{6,10},... | collective-permute-start | bytes 196616 | tf_op jit(solution)/shard_map/ppermute | solution.py:392
  44.9 0.0 collective-permute-done.13.refs_0_
  44.9 0.0 collective-permute-start.12
  44.9 0.0 collective-permute-done.14.refs_1_
  44.9 0.0 collective-permute-done.15.refs_2_
  44.9 0.7 %place.2.refs_4_ = bf16[8,64,512]{2,1,0:T(8,128)(2,1)} custom-call(bf16[2,64,256]{2,1,0:T(8,128)(2,1)S(1)} %collective-permute-done.13.refs_0_, bf16[2,64,256]{2,1,0:T(8,128)(2,1)S(1)} %collective-permute-done.14.refs_1_, bf16[2,64,256]{2,1,0:T(8,128)(2,1)S(1)} %collective-permute-done.15.refs_2_, bf16[2,64,256]{2,1,0:T(8,128)(2,1)S(1)} %get-tuple-element.52.refs_3_), custom_call_target="tpu_custom_call" | custom-call | bytes 5242880 | tf_op jit(solution)/shard_map/place/pallas_call | solution.py:376
  45.7 2.7 %collective-permute-done.10.refs_0_ = bf16[2,64,256]{2,1,0:T(8,128)(2,1)S(1)} collective-permute-done((bf16[2,64,256]{2,1,0:T(8,128)(2,1)S(1)}, bf16[2,64,256]{2,1,0:T(8,128)(2,1)S(1)}, u32[]{:S(2)}, u32[]{:S(2)}) %collective-permute-start.10) | collective-permute-done | bytes 65568 | tf_op jit(solution)/shard_map/ppermute | solution.py:392
  48.4 1.2 %collective-permute-done.11.refs_1_ = bf16[2,64,256]{2,1,0:T(8,128)(2,1)S(1)} collective-permute-done((bf16[2,64,256]{2,1,0:T(8,128)(2,1)S(1)}, bf16[2,64,256]{2,1,0:T(8,128)(2,1)S(1)}, u32[]{:S(2)}, u32[]{:S(2)}) %collective-permute-start.11) | collective-permute-done | bytes 65568 | tf_op jit(solution)/shard_map/ppermute | solution.py:392
  49.6 0.3 collective-permute-done.12.refs_2_
  49.9 0.7 %place.3 = bf16[8,64,512]{2,1,0:T(8,128)(2,1)} custom-call(bf16[2,64,256]{2,1,0:T(8,128)(2,1)S(1)} %collective-permute-done.10.refs_0_, bf16[2,64,256]{2,1,0:T(8,128)(2,1)S(1)} %collective-permute-done.11.refs_1_, bf16[2,64,256]{2,1,0:T(8,128)(2,1)S(1)} %collective-permute-done.12.refs_2_, ...), custom_call_target="tpu_custom_call", output_to_operand_aliasing={{}: (4, {})} | custom-call | bytes 5242880 | tf_op jit(solution)/shard_map/place/pallas_call | solution.py:376
Async XLA Ops:
  0.0 14.0 %collective-permute-start = (bf16[256,512]{1,0:T(8,128)(2,1)}, bf16[256,512]{1,0:T(8,128)(2,1)S(1)}, u32[]{:S(2)}, u32[]{:S(2)}) collective-permute-start(bf16[256,512]{1,0:T(8,128)(2,1)} %bitcast.8), channel_id=1, source_target_pairs={{0,2},{2,0},{1,3},{3,1},{4,6},{6,4},{5,7},{7,5},{8,10},{10,8},{9,1... | collective-permute-start | bytes 786440 | tf_op jit(solution)/shard_map/ppermute | solution.py:396
  3.9 9.1 %collective-permute-start.1 = (bf16[64,1024]{1,0:T(8,128)(2,1)S(1)}, bf16[64,1024]{1,0:T(8,128)(2,1)S(1)}, u32[]{:S(2)}, u32[]{:S(2)}) collective-permute-start(bf16[64,1024]{1,0:T(8,128)(2,1)S(1)} %pick.1), channel_id=1, source_target_pairs={{0,8},{4,12},{8,0},{12,4},{1,9},{5,13},{9,1},{13,5},{2,10},{6,14},... | collective-permute-start | bytes 393224 | tf_op jit(solution)/shard_map/ppermute | solution.py:392
  6.5 12.7 %collective-permute-start.5 = (bf16[128,1024]{1,0:T(8,128)(2,1)}, bf16[128,1024]{1,0:T(8,128)(2,1)S(1)}, u32[]{:S(2)}, u32[]{:S(2)}) collective-permute-start(bf16[128,1024]{1,0:T(8,128)(2,1)} %mesh.1), channel_id=1, source_target_pairs={{0,4},{4,0},{8,12},{12,8},{1,5},{5,1},{9,13},{13,9},{2,6},{6,2},{1... | collective-permute-start | bytes 786440 | tf_op jit(solution)/shard_map/ppermute | solution.py:392
  13.0 5.7 %collective-permute-start.2 = (bf16[64,1024]{1,0:T(8,128)(2,1)S(1)}, bf16[64,1024]{1,0:T(8,128)(2,1)S(1)}, u32[]{:S(2)}, u32[]{:S(2)}) collective-permute-start(bf16[64,1024]{1,0:T(8,128)(2,1)S(1)} %collective-permute-done.1.refs_2_), channel_id=1, source_target_pairs={{0,4},{4,0},{8,12},{12,8},{1,5},{5,1},{9,13},{13,9},{2,6},{6,2},{1... | collective-permute-start | bytes 393224 | tf_op jit(solution)/shard_map/ppermute | solution.py:392
  13.5 5.7 %collective-permute-start.6 = (bf16[64,1024]{1,0:T(8,128)(2,1)S(1)}, bf16[64,1024]{1,0:T(8,128)(2,1)S(1)}, u32[]{:S(2)}, u32[]{:S(2)}) collective-permute-start(bf16[64,1024]{1,0:T(8,128)(2,1)S(1)} %collective-permute-done.1.refs_2_), channel_id=1, source_target_pairs={{0,2},{2,0},{1,3},{3,1},{4,6},{6,4},{5,7},{7,5},{8,10},{10,8},{9,1... | collective-permute-start | bytes 393224 | tf_op jit(solution)/shard_map/ppermute | solution.py:396
  18.7 5.0 %collective-permute-start.3 = (bf16[64,1024]{1,0:T(8,128)(2,1)S(1)}, bf16[64,1024]{1,0:T(8,128)(2,1)S(1)}, u32[]{:S(2)}, u32[]{:S(2)}) collective-permute-start(bf16[64,1024]{1,0:T(8,128)(2,1)S(1)} %collective-permute-done.2.refs_4_), channel_id=1, source_target_pairs={{0,2},{2,0},{1,3},{3,1},{4,6},{6,4},{5,7},{7,5},{8,10},{10,8},{9,1... | collective-permute-start | bytes 393224 | tf_op jit(solution)/shard_map/ppermute | solution.py:396
  20.3 5.2 %copy-start.1 = (s32[4,8]{1,0:T(4,128)S(1)}, s32[4,8]{1,0:T(4,128)}, u32[]{:S(2)}) copy-start(s32[4,8]{1,0:T(4,128)} %adjacency.1) | copy-start | bytes 388
  20.3 3.9 %collective-permute-start.7 = (bf16[448,1024]{1,0:T(8,128)(2,1)S(1)}, bf16[448,1024]{1,0:T(8,128)(2,1)S(1)}, u32[]{:S(2)}, u32[]{:S(2)}) collective-permute-start(bf16[448,1024]{1,0:T(8,128)(2,1)S(1)} %project.3), channel_id=1, source_target_pairs={{0,1},{1,0},{2,3},{3,2},{4,5},{5,4},{6,7},{7,6},{8,9},{9,8},{10,11... | collective-permute-start | bytes 2752520 | tf_op jit(solution)/shard_map/ppermute | solution.py:396
  24.2 1.4 %collective-permute-start.4 = (bf16[64,1024]{1,0:T(8,128)(2,1)S(1)}, bf16[64,1024]{1,0:T(8,128)(2,1)S(1)}, u32[]{:S(2)}, u32[]{:S(2)}) collective-permute-start(bf16[64,1024]{1,0:T(8,128)(2,1)S(1)} %project.2), channel_id=1, source_target_pairs={{0,1},{1,0},{2,3},{3,2},{4,5},{5,4},{6,7},{7,6},{8,9},{9,8},{10,11... | collective-permute-start | bytes 393224 | tf_op jit(solution)/shard_map/ppermute | solution.py:396
  29.0 6.4 %collective-permute-start.9 = (bf16[256,256]{1,0:T(8,128)(2,1)S(1)}, bf16[256,256]{1,0:T(8,128)(2,1)S(1)}, u32[]{:S(2)}, u32[]{:S(2)}) collective-permute-start(bf16[256,256]{1,0:T(8,128)(2,1)S(1)} %get-tuple-element.51), channel_id=1, source_target_pairs={{0,2},{2,0},{1,3},{3,1},{4,6},{6,4},{5,7},{7,5},{8,10},{10,8},{9,1... | collective-permute-start | bytes 393224 | tf_op jit(solution)/shard_map/ppermute | solution.py:396
  29.6 1.9 %copy-start.2 = (s32[4,1]{0,1:T(1,128)S(1)}, s32[4,1]{0,1:T(1,128)}, u32[]{:S(2)}) copy-start(s32[4,1]{0,1:T(1,128)} %param.12) | copy-start | bytes 52
  29.6 5.9 %copy-start = (bf16[4,64,512]{2,1,0:T(8,128)(2,1)S(1)}, bf16[4,64,512]{2,1,0:T(8,128)(2,1)}, u32[]{:S(2)}) copy-start(bf16[4,64,512]{2,1,0:T(8,128)(2,1)} %grid_features.3) | copy-start | bytes 786436
  29.9 9.9 %collective-permute-start.8 = (bf16[256,256]{1,0:T(8,128)(2,1)S(1)}, bf16[256,256]{1,0:T(8,128)(2,1)S(1)}, u32[]{:S(2)}, u32[]{:S(2)}) collective-permute-start(bf16[256,256]{1,0:T(8,128)(2,1)S(1)} %get-tuple-element.49), channel_id=1, source_target_pairs={{0,2},{2,0},{1,3},{3,1},{4,6},{6,4},{5,7},{7,5},{8,10},{10,8},{9,1... | collective-permute-start | bytes 393224 | tf_op jit(solution)/shard_map/ppermute | solution.py:396
  36.1 8.8 %collective-permute-start.13 = (bf16[2,64,256]{2,1,0:T(8,128)(2,1)S(1)}, bf16[2,64,256]{2,1,0:T(8,128)(2,1)S(1)}, u32[]{:S(2)}, u32[]{:S(2)}) collective-permute-start(bf16[2,64,256]{2,1,0:T(8,128)(2,1)S(1)} %get-tuple-element.58), channel_id=1, source_target_pairs={{0,8},{4,12},{8,0},{12,4},{1,9},{5,13},{9,1},{13,5},{2,10},{6,14},... | collective-permute-start | bytes 196616 | tf_op jit(solution)/shard_map/ppermute | solution.py:392
  38.2 6.7 %collective-permute-start.14 = (bf16[2,64,256]{2,1,0:T(8,128)(2,1)S(1)}, bf16[2,64,256]{2,1,0:T(8,128)(2,1)S(1)}, u32[]{:S(2)}, u32[]{:S(2)}) collective-permute-start(bf16[2,64,256]{2,1,0:T(8,128)(2,1)S(1)} %get-tuple-element.59), channel_id=1, source_target_pairs={{0,12},{4,8},{8,4},{12,0},{1,13},{5,9},{9,5},{13,1},{2,14},{6,10},... | collective-permute-start | bytes 196616 | tf_op jit(solution)/shard_map/ppermute | solution.py:392
  39.8 5.2 %collective-permute-start.15 = (bf16[2,64,256]{2,1,0:T(8,128)(2,1)S(1)}, bf16[2,64,256]{2,1,0:T(8,128)(2,1)S(1)}, u32[]{:S(2)}, u32[]{:S(2)}) collective-permute-start(bf16[2,64,256]{2,1,0:T(8,128)(2,1)S(1)} %get-tuple-element.60), channel_id=1, source_target_pairs={{0,4},{4,0},{8,12},{12,8},{1,5},{5,1},{9,13},{13,9},{2,6},{6,2},{1... | collective-permute-start | bytes 196616 | tf_op jit(solution)/shard_map/ppermute | solution.py:392
  40.5 7.9 %collective-permute-start.10 = (bf16[2,64,256]{2,1,0:T(8,128)(2,1)S(1)}, bf16[2,64,256]{2,1,0:T(8,128)(2,1)S(1)}, u32[]{:S(2)}, u32[]{:S(2)}) collective-permute-start(bf16[2,64,256]{2,1,0:T(8,128)(2,1)S(1)} %get-tuple-element.54), channel_id=1, source_target_pairs={{0,8},{4,12},{8,0},{12,4},{1,9},{5,13},{9,1},{13,5},{2,10},{6,14},... | collective-permute-start | bytes 196616 | tf_op jit(solution)/shard_map/ppermute | solution.py:392
  43.4 6.2 %collective-permute-start.11 = (bf16[2,64,256]{2,1,0:T(8,128)(2,1)S(1)}, bf16[2,64,256]{2,1,0:T(8,128)(2,1)S(1)}, u32[]{:S(2)}, u32[]{:S(2)}) collective-permute-start(bf16[2,64,256]{2,1,0:T(8,128)(2,1)S(1)} %get-tuple-element.55), channel_id=1, source_target_pairs={{0,12},{4,8},{8,4},{12,0},{1,13},{5,9},{9,5},{13,1},{2,14},{6,10},... | collective-permute-start | bytes 196616 | tf_op jit(solution)/shard_map/ppermute | solution.py:392
  44.9 5.0 %collective-permute-start.12 = (bf16[2,64,256]{2,1,0:T(8,128)(2,1)S(1)}, bf16[2,64,256]{2,1,0:T(8,128)(2,1)S(1)}, u32[]{:S(2)}, u32[]{:S(2)}) collective-permute-start(bf16[2,64,256]{2,1,0:T(8,128)(2,1)S(1)} %get-tuple-element.56), channel_id=1, source_target_pairs={{0,4},{4,0},{8,12},{12,8},{1,5},{5,1},{9,13},{13,9},{2,6},{6,2},{1... | collective-permute-start | bytes 196616 | tf_op jit(solution)/shard_map/ppermute | solution.py:392

commit v8 on v7

--- a/solution.py
+++ b/solution.py
@@ -180,15 +180,9 @@
     )(*pieces, wk, wv)
 
 
-def table_kernel(mine, sibling, table, sem):
-    copies = [
-        pltpu.make_async_copy(mine, table.at[0, pl.ds(0, mine.shape[0])], sem.at[0]),
-        pltpu.make_async_copy(sibling, table.at[1, pl.ds(0, mine.shape[0])], sem.at[1]),
-    ]
-    for copy in copies:
-        copy.start()
-    for copy in copies:
-        copy.wait()
+def table_kernel(mine, sibling, table):
+    table[0, : mine.shape[0]] = mine[...]
+    table[1, : mine.shape[0]] = sibling[...]
 
 
 def run_table(mine, sibling, blocks):
@@ -197,7 +191,6 @@
         out_shape=jax.ShapeDtypeStruct((2, blocks) + mine.shape[1:], jnp.bfloat16),
         in_specs=vmem(2),
         out_specs=whole(pltpu.VMEM),
-        scratch_shapes=[pltpu.SemaphoreType.DMA((2,))],
         compiler_params=params(8),
         cost_estimate=pl.CostEstimate(
             flops=0, bytes_accessed=80 * mine.size, transcendentals=0
@@ -215,7 +208,7 @@
 
 
 def attend_kernel(
-    adjacency, q, mine, sibling, table_in, mlp, wo, send, keep, att, table, sem
+    adjacency, q, mine, sibling, table_in, mlp, wo, send, keep, att, table
 ):
     del table_in
     s = lax.axis_index("shard")
@@ -223,18 +216,13 @@
     u = lax.axis_index("sub")
     half = wo.shape[0]
     ready = table.shape[1] - mine.shape[0]
-    copies = []
     for i, part in enumerate((mine, sibling)):
-        target = table.at[i, pl.ds(ready, part.shape[0])]
-        copies.append(pltpu.make_async_copy(part, target, sem.at[i]))
-        copies[i].start()
+        table[i, ready:] = part[...]
     rows_of = lax.broadcasted_iota(jnp.int32, (WIDE, WIDE), 0) // BLOCK
     lanes_of = lax.broadcasted_iota(jnp.int32, (WIDE, WIDE), 1) // HEAD_DIM
     diagonal = rows_of == lanes_of
     lane_head = lax.broadcasted_iota(jnp.int32, (BLOCK, WIDE), 1) // HEAD_DIM
     scale = HEAD_DIM**-0.5 * math.log2(math.e)
-    for copy in copies:
-        copy.wait()
     for b in range(adjacency.shape[0]):
         rows = slice(b * BLOCK, (b + 1) * BLOCK)
         places = []
@@ -281,7 +269,6 @@
         ),
         in_specs=[whole(pltpu.SMEM)] + vmem(6),
         out_specs=tuple(vmem(4)),
-        scratch_shapes=[pltpu.SemaphoreType.DMA((2,))],
         input_output_aliases={4: 3},
         compiler_params=params(16),
         cost_estimate=pl.CostEstimate(
@@ -449,6 +436,7 @@
     for c in range(CHUNKS):
         if c > 0:
             send, keep = run_project_out(c, att, mlp, wo)
+            send, _ = lax.optimization_barrier((send, received))
         received = swapped(send, "head")
         if slots is not None:
             received, _ = lax.optimization_barrier((received, slots[0]))

time: 50.8 us -> 50.7 us (level)
  waiting for transfers between devices: 13.5 us -> 15.2 us
  starting transfers between devices: 19.1 us -> 18.1 us
  Pallas kernels: 17.8 us -> 17 us
    ppermute x7, waiting for transfers between devices: 7.96 us -> 9.22 us  [swapped(): return lax.ppermute(x, axis, [(0, 1), (1, 0)])]
    ppermute x7, starting transfers between devices: 6.26 us -> 5.14 us  [swapped(): return lax.ppermute(x, axis, [(0, 1), (1, 0)])]
  transfers between devices with their start and end apart: 16 -> 16, of which waited for: 7 -> 7; matrix products, arithmetic and copies ran while one was open for 0% -> 0% of each run, Pallas kernels for 27% -> 26%
where the time goes in v8:
time: 50.7 us; the launch traced here: 50.6 us
  starting transfers between devices  18.1 us (36%)
  Pallas kernels  17 us (34%)
  waiting for transfers between devices  15.2 us (30%)
    ppermute x9, starting transfers between devices, crossed(): return lax.ppermute(x, 'shard', [(i, i ^ distance) for i in range(size)])  12.9 us
    ppermute x7, waiting for transfers between devices, swapped(): return lax.ppermute(x, axis, [(0, 1), (1, 0)])  9.22 us
    ppermute x9, waiting for transfers between devices, crossed(): return lax.ppermute(x, 'shard', [(i, i ^ distance) for i in range(size)])  5.99 us
    ppermute x7, starting transfers between devices, swapped(): return lax.ppermute(x, axis, [(0, 1), (1, 0)])  5.14 us
    pallas_call x1, Pallas kernels, run_stage(): pl.pallas_call(functools.partial(stage_kernel, axes), out_shape=tuple((ja...  4.87 us
    pallas_call x1, Pallas kernels, run_mlp(): pl.pallas_call(mlp_kernel, out_shape=(jax.ShapeDtypeStruct((rows, wq.shap...  3.33 us
    pallas_call x1, Pallas kernels, run_attend(): pl.pallas_call(attend_kernel, out_shape=(part, part, jax.ShapeDtypeStruct...  3.05 us
    pallas_call x2, Pallas kernels, run_project(): pl.pallas_call(project_kernel, out_shape=jax.ShapeDtypeStruct((rows, 2 *...  1.59 us
  transfers between devices with their start and end apart: 16, of which 7 were waited for; matrix products, arithmetic and copies ran while one was open for 0% of the time, Pallas kernels for 26%

profile of v8, /device:TPU:0, one launch (start us, length us, event | category | flops | bytes accessed | tf_op | source)
XLA Modules:
  0.0 50.6 jit_solution(5578310613298300090)
XLA Ops:
  0.0 2.9 %collective-permute-start = (bf16[256,512]{1,0:T(8,128)(2,1)}, bf16[256,512]{1,0:T(8,128)(2,1)S(1)}, u32[]{:S(2)}, u32[]{:S(2)}) collective-permute-start(bf16[256,512]{1,0:T(8,128)(2,1)} %bitcast.8), channel_id=1, source_target_pairs={{0,2},{2,0},{1,3},{3,1},{4,6},{6,4},{5,7},{7,5},{8,10},{10,8},{9,1... | collective-permute-start | bytes 786440 | tf_op jit(solution)/shard_map/ppermute | solution.py:383
  2.9 0.9 %pick.1 = bf16[64,1024]{1,0:T(8,128)(2,1)S(1)} custom-call(bf16[128,1024]{1,0:T(8,128)(2,1)} %mesh.1), custom_call_target="tpu_custom_call" | custom-call | bytes 524288 | tf_op jit(solution)/shard_map/pick/pallas_call | solution.py:108
  3.9 2.7 %collective-permute-start.1 = (bf16[64,1024]{1,0:T(8,128)(2,1)S(1)}, bf16[64,1024]{1,0:T(8,128)(2,1)S(1)}, u32[]{:S(2)}, u32[]{:S(2)}) collective-permute-start(bf16[64,1024]{1,0:T(8,128)(2,1)S(1)} %pick.1), channel_id=1, source_target_pairs={{0,8},{4,12},{8,0},{12,4},{1,9},{5,13},{9,1},{13,5},{2,10},{6,14},... | collective-permute-start | bytes 393224 | tf_op jit(solution)/shard_map/ppermute | solution.py:379
  6.5 1.6 %collective-permute-start.5 = (bf16[128,1024]{1,0:T(8,128)(2,1)}, bf16[128,1024]{1,0:T(8,128)(2,1)S(1)}, u32[]{:S(2)}, u32[]{:S(2)}) collective-permute-start(bf16[128,1024]{1,0:T(8,128)(2,1)} %mesh.1), channel_id=1, source_target_pairs={{0,4},{4,0},{8,12},{12,8},{1,5},{5,1},{9,13},{13,9},{2,6},{6,2},{1... | collective-permute-start | bytes 786440 | tf_op jit(solution)/shard_map/ppermute | solution.py:379
  8.1 4.9 %stage.1 = (bf16[256,512]{1,0:T(8,128)(2,1)S(1)}, f32[1,1024]{1,0:T(1,128)S(1)}, bf16[1024,512]{1,0:T(8,128)(2,1)S(1)}, bf16[1024,2048]{1,0:T(8,128)(2,1)S(1)}, ...) custom-call(bf16[256,512]{1,0:T(8,128)(2,1)} %bitcast.9, ...), custom_call_target="tpu_custom_call" | custom-call | bytes 262184960 | tf_op jit(solution)/shard_map/stage/pallas_call | solution.py:145
  13.0 0.0 collective-permute-done.1.refs_2_
  13.0 0.5 %collective-permute-start.2 = (bf16[64,1024]{1,0:T(8,128)(2,1)S(1)}, bf16[64,1024]{1,0:T(8,128)(2,1)S(1)}, u32[]{:S(2)}, u32[]{:S(2)}) collective-permute-start(bf16[64,1024]{1,0:T(8,128)(2,1)S(1)} %collective-permute-done.1.refs_2_), channel_id=1, source_target_pairs={{0,4},{4,0},{8,12},{12,8},{1,5},{5,1},{9,13},{13,9},{2,6},{6,2},{1... | collective-permute-start | bytes 393224 | tf_op jit(solution)/shard_map/ppermute | solution.py:379
  13.5 0.5 %collective-permute-start.6 = (bf16[64,1024]{1,0:T(8,128)(2,1)S(1)}, bf16[64,1024]{1,0:T(8,128)(2,1)S(1)}, u32[]{:S(2)}, u32[]{:S(2)}) collective-permute-start(bf16[64,1024]{1,0:T(8,128)(2,1)S(1)} %collective-permute-done.1.refs_2_), channel_id=1, source_target_pairs={{0,2},{2,0},{1,3},{3,1},{4,6},{6,4},{5,7},{7,5},{8,10},{10,8},{9,1... | collective-permute-start | bytes 393224 | tf_op jit(solution)/shard_map/ppermute | solution.py:383
  14.0 0.0 collective-permute-done.other
  14.0 3.3 %mlp.1 = (bf16[256,512]{1,0:T(8,128)(2,1)S(1)}, f32[256,1024]{1,0:T(8,128)S(1)}) custom-call(bf16[256,512]{1,0:T(8,128)(2,1)S(1)} %get-tuple-element.34.own, bf16[256,512]{1,0:T(8,128)(2,1)S(1)} %collective-permute-done.other, f32[1,1024]{1,0:T(1,128)S(1)} %get-tuple-element.35.gain, bf16[1024,512]{1,0:T(8,128)(2,1)S(1)} %get-tuple-element.36.wq, ...), custom_call_target="tpu_custom_call" | custom-call | flops 2415919104 | bytes 9437184 | tf_op jit(solution)/shard_map/mlp/pallas_call | solution.py:81
  17.4 1.3 %collective-permute-done.2.refs_4_ = bf16[64,1024]{1,0:T(8,128)(2,1)S(1)} collective-permute-done((bf16[64,1024]{1,0:T(8,128)(2,1)S(1)}, bf16[64,1024]{1,0:T(8,128)(2,1)S(1)}, u32[]{:S(2)}, u32[]{:S(2)}) %collective-permute-start.2) | collective-permute-done | bytes 131104 | tf_op jit(solution)/shard_map/ppermute | solution.py:379
  18.7 0.5 collective-permute-start.3
  19.2 0.0 collective-permute-done.6.refs_3_
  19.2 0.0 collective-permute-done.5.refs_1_
  19.2 1.1 %project.3 = bf16[448,1024]{1,0:T(8,128)(2,1)S(1)} custom-call(bf16[128,1024]{1,0:T(8,128)(2,1)S(1)} %get-tuple-element.45.refs_0_, bf16[128,1024]{1,0:T(8,128)(2,1)S(1)} %collective-permute-done.5.refs_1_, bf16[64,1024]{1,0:T(8,128)(2,1)S(1)} %collective-permute-done.1.refs_2_, bf16[64,1024]{1,0:T(8,128)(2,1)S(1)} %collective-permute-done.6.refs_3_, ...), custom_call_target="tpu_custom_call" | custom-call | flops 70464307200 | bytes 294912000 | tf_op jit(solution)/shard_map/project/pallas_call | solution.py:168
  20.3 0.0 copy-start.1
  20.3 0.1 collective-permute-start.7
  20.4 3.3 %collective-permute-done.3.refs_0_ = bf16[64,1024]{1,0:T(8,128)(2,1)S(1)} collective-permute-done((bf16[64,1024]{1,0:T(8,128)(2,1)S(1)}, bf16[64,1024]{1,0:T(8,128)(2,1)S(1)}, u32[]{:S(2)}, u32[]{:S(2)}) %collective-permute-start.3) | collective-permute-done | bytes 131104 | tf_op jit(solution)/shard_map/ppermute | solution.py:383
  23.7 0.5 project.2
  24.2 0.1 collective-permute-start.4
  24.2 0.0 collective-permute-done.7
  24.3 0.1 table.1.table_in
  24.4 1.2 %collective-permute-done.4 = bf16[64,1024]{1,0:T(8,128)(2,1)S(1)} collective-permute-done((bf16[64,1024]{1,0:T(8,128)(2,1)S(1)}, bf16[64,1024]{1,0:T(8,128)(2,1)S(1)}, u32[]{:S(2)}, u32[]{:S(2)}) %collective-permute-start.4) | collective-permute-done | bytes 131104 | tf_op jit(solution)/shard_map/ppermute | solution.py:383
  25.6 0.0 copy-done.1
  25.6 3.1 %attend.1 = (bf16[256,256]{1,0:T(8,128)(2,1)S(1)}, bf16[256,256]{1,0:T(8,128)(2,1)S(1)}, bf16[256,512]{1,0:T(8,128)(2,1)S(1)}, bf16[2,8,64,1024]{3,2,1,0:T(8,128)(2,1)S(1)}) custom-call(s32[4,8]{1,0:T(4,128)S(1)} %copy-done.1, bf16[256,512]{1,0:T(8,128)(2,1)S(1)} %get-tuple-element.41.q, ...), custom_call_target="tpu_custom_call", output_to_operand_aliasing={{3}: (4, {})} | custom-call | flops 13421772800 | bytes 41943040 | tf_op jit(solution)/shard_map/attend/pallas_call | solution.py:262
  28.6 0.6 %collective-permute-start.8 = (bf16[256,256]{1,0:T(8,128)(2,1)S(1)}, bf16[256,256]{1,0:T(8,128)(2,1)S(1)}, u32[]{:S(2)}, u32[]{:S(2)}) collective-permute-start(bf16[256,256]{1,0:T(8,128)(2,1)S(1)} %get-tuple-element.51), channel_id=1, source_target_pairs={{0,2},{2,0},{1,3},{3,1},{4,6},{6,4},{5,7},{7,5},{8,10},{10,8},{9,1... | collective-permute-start | bytes 393224 | tf_op jit(solution)/shard_map/ppermute | solution.py:383
  29.2 0.0 copy-start.2
  29.2 0.0 copy-start
  29.2 0.3 project_out.1
  29.5 4.8 %collective-permute-done.8.received = bf16[256,256]{1,0:T(8,128)(2,1)S(1)} collective-permute-done((bf16[256,256]{1,0:T(8,128)(2,1)S(1)}, bf16[256,256]{1,0:T(8,128)(2,1)S(1)}, u32[]{:S(2)}, u32[]{:S(2)}) %collective-permute-start.8) | collective-permute-done | bytes 131104 | tf_op jit(solution)/shard_map/ppermute | solution.py:383
  34.3 0.5 collective-permute-start.9
  34.7 0.0 copy-done.2
  34.7 0.1 copy.15.owners
  34.8 0.0 copy-done
  34.8 0.7 %combine.2 = (bf16[2,64,256]{2,1,0:T(8,128)(2,1)S(1)}, bf16[2,64,256]{2,1,0:T(8,128)(2,1)S(1)}, bf16[2,64,256]{2,1,0:T(8,128)(2,1)S(1)}, bf16[2,64,256]{2,1,0:T(8,128)(2,1)S(1)}) custom-call(s32[4,1]{1,0:T(4,128)S(1)} %copy.15.owners, bf16[4,64,512]{2,1,0:T(8,128)(2,1)S(1)} %copy-done, bf16[256,256]{1,0:T(8,128)(2,1)S(1)} %get-tuple-element.53.keep, ...), custom_call_target="tpu_custom_call" | custom-call | flops 196608000 | bytes 131072000 | tf_op jit(solution)/shard_map/combine/pallas_call | solution.py:330
  35.6 3.1 %collective-permute-start.13 = (bf16[2,64,256]{2,1,0:T(8,128)(2,1)S(1)}, bf16[2,64,256]{2,1,0:T(8,128)(2,1)S(1)}, u32[]{:S(2)}, u32[]{:S(2)}) collective-permute-start(bf16[2,64,256]{2,1,0:T(8,128)(2,1)S(1)} %get-tuple-element.60), channel_id=1, source_target_pairs={{0,8},{4,12},{8,0},{12,4},{1,9},{5,13},{9,1},{13,5},{2,10},{6,14},... | collective-permute-start | bytes 196616 | tf_op jit(solution)/shard_map/ppermute | solution.py:379
  38.6 0.7 %collective-permute-start.14 = (bf16[2,64,256]{2,1,0:T(8,128)(2,1)S(1)}, bf16[2,64,256]{2,1,0:T(8,128)(2,1)S(1)}, u32[]{:S(2)}, u32[]{:S(2)}) collective-permute-start(bf16[2,64,256]{2,1,0:T(8,128)(2,1)S(1)} %get-tuple-element.61), channel_id=1, source_target_pairs={{0,12},{4,8},{8,4},{12,0},{1,13},{5,9},{9,5},{13,1},{2,14},{6,10},... | collective-permute-start | bytes 196616 | tf_op jit(solution)/shard_map/ppermute | solution.py:379
  39.3 0.0 collective-permute-start.15
  39.3 0.0 collective-permute-done.9.received
  39.3 0.7 %combine.3 = (bf16[2,64,256]{2,1,0:T(8,128)(2,1)S(1)}, bf16[2,64,256]{2,1,0:T(8,128)(2,1)S(1)}, bf16[2,64,256]{2,1,0:T(8,128)(2,1)S(1)}, bf16[2,64,256]{2,1,0:T(8,128)(2,1)S(1)}) custom-call(s32[4,1]{1,0:T(4,128)S(1)} %copy.15.owners, bf16[4,64,512]{2,1,0:T(8,128)(2,1)S(1)} %copy-done, bf16[256,256]{1,0:T(8,128)(2,1)S(1)} %get-tuple-element.49.keep, ...), custom_call_target="tpu_custom_call" | custom-call | flops 196608000 | bytes 131072000 | tf_op jit(solution)/shard_map/combine/pallas_call | solution.py:330
  40.0 3.8 %collective-permute-start.10 = (bf16[2,64,256]{2,1,0:T(8,128)(2,1)S(1)}, bf16[2,64,256]{2,1,0:T(8,128)(2,1)S(1)}, u32[]{:S(2)}, u32[]{:S(2)}) collective-permute-start(bf16[2,64,256]{2,1,0:T(8,128)(2,1)S(1)} %get-tuple-element.56), channel_id=1, source_target_pairs={{0,8},{4,12},{8,0},{12,4},{1,9},{5,13},{9,1},{13,5},{2,10},{6,14},... | collective-permute-start | bytes 196616 | tf_op jit(solution)/shard_map/ppermute | solution.py:379
  43.8 0.7 %collective-permute-start.11 = (bf16[2,64,256]{2,1,0:T(8,128)(2,1)S(1)}, bf16[2,64,256]{2,1,0:T(8,128)(2,1)S(1)}, u32[]{:S(2)}, u32[]{:S(2)}) collective-permute-start(bf16[2,64,256]{2,1,0:T(8,128)(2,1)S(1)} %get-tuple-element.57), channel_id=1, source_target_pairs={{0,12},{4,8},{8,4},{12,0},{1,13},{5,9},{9,5},{13,1},{2,14},{6,10},... | collective-permute-start | bytes 196616 | tf_op jit(solution)/shard_map/ppermute | solution.py:379
  44.5 0.0 collective-permute-done.13.refs_0_
  44.5 0.0 collective-permute-start.12
  44.5 0.3 collective-permute-done.14.refs_1_
  44.7 0.0 collective-permute-done.15.refs_2_
  44.7 0.7 %place.2.refs_4_ = bf16[8,64,512]{2,1,0:T(8,128)(2,1)} custom-call(bf16[2,64,256]{2,1,0:T(8,128)(2,1)S(1)} %collective-permute-done.13.refs_0_, bf16[2,64,256]{2,1,0:T(8,128)(2,1)S(1)} %collective-permute-done.14.refs_1_, bf16[2,64,256]{2,1,0:T(8,128)(2,1)S(1)} %collective-permute-done.15.refs_2_, bf16[2,64,256]{2,1,0:T(8,128)(2,1)S(1)} %get-tuple-element.54.refs_3_), custom_call_target="tpu_custom_call" | custom-call | bytes 5242880 | tf_op jit(solution)/shard_map/place/pallas_call | solution.py:363
  45.5 2.7 %collective-permute-done.10.refs_0_ = bf16[2,64,256]{2,1,0:T(8,128)(2,1)S(1)} collective-permute-done((bf16[2,64,256]{2,1,0:T(8,128)(2,1)S(1)}, bf16[2,64,256]{2,1,0:T(8,128)(2,1)S(1)}, u32[]{:S(2)}, u32[]{:S(2)}) %collective-permute-start.10) | collective-permute-done | bytes 65568 | tf_op jit(solution)/shard_map/ppermute | solution.py:379
  48.1 1.7 %collective-permute-done.11.refs_1_ = bf16[2,64,256]{2,1,0:T(8,128)(2,1)S(1)} collective-permute-done((bf16[2,64,256]{2,1,0:T(8,128)(2,1)S(1)}, bf16[2,64,256]{2,1,0:T(8,128)(2,1)S(1)}, u32[]{:S(2)}, u32[]{:S(2)}) %collective-permute-start.11) | collective-permute-done | bytes 65568 | tf_op jit(solution)/shard_map/ppermute | solution.py:379
  49.8 0.0 collective-permute-done.12.refs_2_
  49.8 0.7 %place.3 = bf16[8,64,512]{2,1,0:T(8,128)(2,1)} custom-call(bf16[2,64,256]{2,1,0:T(8,128)(2,1)S(1)} %collective-permute-done.10.refs_0_, bf16[2,64,256]{2,1,0:T(8,128)(2,1)S(1)} %collective-permute-done.11.refs_1_, bf16[2,64,256]{2,1,0:T(8,128)(2,1)S(1)} %collective-permute-done.12.refs_2_, ...), custom_call_target="tpu_custom_call", output_to_operand_aliasing={{}: (4, {})} | custom-call | bytes 5242880 | tf_op jit(solution)/shard_map/place/pallas_call | solution.py:363
Async XLA Ops:
  0.0 14.0 %collective-permute-start = (bf16[256,512]{1,0:T(8,128)(2,1)}, bf16[256,512]{1,0:T(8,128)(2,1)S(1)}, u32[]{:S(2)}, u32[]{:S(2)}) collective-permute-start(bf16[256,512]{1,0:T(8,128)(2,1)} %bitcast.8), channel_id=1, source_target_pairs={{0,2},{2,0},{1,3},{3,1},{4,6},{6,4},{5,7},{7,5},{8,10},{10,8},{9,1... | collective-permute-start | bytes 786440 | tf_op jit(solution)/shard_map/ppermute | solution.py:383
  3.9 9.1 %collective-permute-start.1 = (bf16[64,1024]{1,0:T(8,128)(2,1)S(1)}, bf16[64,1024]{1,0:T(8,128)(2,1)S(1)}, u32[]{:S(2)}, u32[]{:S(2)}) collective-permute-start(bf16[64,1024]{1,0:T(8,128)(2,1)S(1)} %pick.1), channel_id=1, source_target_pairs={{0,8},{4,12},{8,0},{12,4},{1,9},{5,13},{9,1},{13,5},{2,10},{6,14},... | collective-permute-start | bytes 393224 | tf_op jit(solution)/shard_map/ppermute | solution.py:379
  6.5 12.7 %collective-permute-start.5 = (bf16[128,1024]{1,0:T(8,128)(2,1)}, bf16[128,1024]{1,0:T(8,128)(2,1)S(1)}, u32[]{:S(2)}, u32[]{:S(2)}) collective-permute-start(bf16[128,1024]{1,0:T(8,128)(2,1)} %mesh.1), channel_id=1, source_target_pairs={{0,4},{4,0},{8,12},{12,8},{1,5},{5,1},{9,13},{13,9},{2,6},{6,2},{1... | collective-permute-start | bytes 786440 | tf_op jit(solution)/shard_map/ppermute | solution.py:379
  13.0 5.7 %collective-permute-start.2 = (bf16[64,1024]{1,0:T(8,128)(2,1)S(1)}, bf16[64,1024]{1,0:T(8,128)(2,1)S(1)}, u32[]{:S(2)}, u32[]{:S(2)}) collective-permute-start(bf16[64,1024]{1,0:T(8,128)(2,1)S(1)} %collective-permute-done.1.refs_2_), channel_id=1, source_target_pairs={{0,4},{4,0},{8,12},{12,8},{1,5},{5,1},{9,13},{13,9},{2,6},{6,2},{1... | collective-permute-start | bytes 393224 | tf_op jit(solution)/shard_map/ppermute | solution.py:379
  13.5 5.7 %collective-permute-start.6 = (bf16[64,1024]{1,0:T(8,128)(2,1)S(1)}, bf16[64,1024]{1,0:T(8,128)(2,1)S(1)}, u32[]{:S(2)}, u32[]{:S(2)}) collective-permute-start(bf16[64,1024]{1,0:T(8,128)(2,1)S(1)} %collective-permute-done.1.refs_2_), channel_id=1, source_target_pairs={{0,2},{2,0},{1,3},{3,1},{4,6},{6,4},{5,7},{7,5},{8,10},{10,8},{9,1... | collective-permute-start | bytes 393224 | tf_op jit(solution)/shard_map/ppermute | solution.py:383
  18.7 5.0 %collective-permute-start.3 = (bf16[64,1024]{1,0:T(8,128)(2,1)S(1)}, bf16[64,1024]{1,0:T(8,128)(2,1)S(1)}, u32[]{:S(2)}, u32[]{:S(2)}) collective-permute-start(bf16[64,1024]{1,0:T(8,128)(2,1)S(1)} %collective-permute-done.2.refs_4_), channel_id=1, source_target_pairs={{0,2},{2,0},{1,3},{3,1},{4,6},{6,4},{5,7},{7,5},{8,10},{10,8},{9,1... | collective-permute-start | bytes 393224 | tf_op jit(solution)/shard_map/ppermute | solution.py:383
  20.3 5.2 %copy-start.1 = (s32[4,8]{1,0:T(4,128)S(1)}, s32[4,8]{1,0:T(4,128)}, u32[]{:S(2)}) copy-start(s32[4,8]{1,0:T(4,128)} %adjacency.1) | copy-start | bytes 388
  20.3 3.9 %collective-permute-start.7 = (bf16[448,1024]{1,0:T(8,128)(2,1)S(1)}, bf16[448,1024]{1,0:T(8,128)(2,1)S(1)}, u32[]{:S(2)}, u32[]{:S(2)}) collective-permute-start(bf16[448,1024]{1,0:T(8,128)(2,1)S(1)} %project.3), channel_id=1, source_target_pairs={{0,1},{1,0},{2,3},{3,2},{4,5},{5,4},{6,7},{7,6},{8,9},{9,8},{10,11... | collective-permute-start | bytes 2752520 | tf_op jit(solution)/shard_map/ppermute | solution.py:383
  24.2 1.4 %collective-permute-start.4 = (bf16[64,1024]{1,0:T(8,128)(2,1)S(1)}, bf16[64,1024]{1,0:T(8,128)(2,1)S(1)}, u32[]{:S(2)}, u32[]{:S(2)}) collective-permute-start(bf16[64,1024]{1,0:T(8,128)(2,1)S(1)} %project.2), channel_id=1, source_target_pairs={{0,1},{1,0},{2,3},{3,2},{4,5},{5,4},{6,7},{7,6},{8,9},{9,8},{10,11... | collective-permute-start | bytes 393224 | tf_op jit(solution)/shard_map/ppermute | solution.py:383
  28.6 5.6 %collective-permute-start.8 = (bf16[256,256]{1,0:T(8,128)(2,1)S(1)}, bf16[256,256]{1,0:T(8,128)(2,1)S(1)}, u32[]{:S(2)}, u32[]{:S(2)}) collective-permute-start(bf16[256,256]{1,0:T(8,128)(2,1)S(1)} %get-tuple-element.51), channel_id=1, source_target_pairs={{0,2},{2,0},{1,3},{3,1},{4,6},{6,4},{5,7},{7,5},{8,10},{10,8},{9,1... | collective-permute-start | bytes 393224 | tf_op jit(solution)/shard_map/ppermute | solution.py:383
  29.2 5.6 %copy-start.2 = (s32[4,1]{0,1:T(1,128)S(1)}, s32[4,1]{0,1:T(1,128)}, u32[]{:S(2)}) copy-start(s32[4,1]{0,1:T(1,128)} %param.12) | copy-start | bytes 52
  29.2 5.6 %copy-start = (bf16[4,64,512]{2,1,0:T(8,128)(2,1)S(1)}, bf16[4,64,512]{2,1,0:T(8,128)(2,1)}, u32[]{:S(2)}) copy-start(bf16[4,64,512]{2,1,0:T(8,128)(2,1)} %grid_features.3) | copy-start | bytes 786436
  34.3 5.0 %collective-permute-start.9 = (bf16[256,256]{1,0:T(8,128)(2,1)S(1)}, bf16[256,256]{1,0:T(8,128)(2,1)S(1)}, u32[]{:S(2)}, u32[]{:S(2)}) collective-permute-start(bf16[256,256]{1,0:T(8,128)(2,1)S(1)} %get-tuple-element.52), channel_id=1, source_target_pairs={{0,2},{2,0},{1,3},{3,1},{4,6},{6,4},{5,7},{7,5},{8,10},{10,8},{9,1... | collective-permute-start | bytes 393224 | tf_op jit(solution)/shard_map/ppermute | solution.py:383
  35.6 8.9 %collective-permute-start.13 = (bf16[2,64,256]{2,1,0:T(8,128)(2,1)S(1)}, bf16[2,64,256]{2,1,0:T(8,128)(2,1)S(1)}, u32[]{:S(2)}, u32[]{:S(2)}) collective-permute-start(bf16[2,64,256]{2,1,0:T(8,128)(2,1)S(1)} %get-tuple-element.60), channel_id=1, source_target_pairs={{0,8},{4,12},{8,0},{12,4},{1,9},{5,13},{9,1},{13,5},{2,10},{6,14},... | collective-permute-start | bytes 196616 | tf_op jit(solution)/shard_map/ppermute | solution.py:379
  38.6 6.1 %collective-permute-start.14 = (bf16[2,64,256]{2,1,0:T(8,128)(2,1)S(1)}, bf16[2,64,256]{2,1,0:T(8,128)(2,1)S(1)}, u32[]{:S(2)}, u32[]{:S(2)}) collective-permute-start(bf16[2,64,256]{2,1,0:T(8,128)(2,1)S(1)} %get-tuple-element.61), channel_id=1, source_target_pairs={{0,12},{4,8},{8,4},{12,0},{1,13},{5,9},{9,5},{13,1},{2,14},{6,10},... | collective-permute-start | bytes 196616 | tf_op jit(solution)/shard_map/ppermute | solution.py:379
  39.3 5.4 %collective-permute-start.15 = (bf16[2,64,256]{2,1,0:T(8,128)(2,1)S(1)}, bf16[2,64,256]{2,1,0:T(8,128)(2,1)S(1)}, u32[]{:S(2)}, u32[]{:S(2)}) collective-permute-start(bf16[2,64,256]{2,1,0:T(8,128)(2,1)S(1)} %get-tuple-element.62), channel_id=1, source_target_pairs={{0,4},{4,0},{8,12},{12,8},{1,5},{5,1},{9,13},{13,9},{2,6},{6,2},{1... | collective-permute-start | bytes 196616 | tf_op jit(solution)/shard_map/ppermute | solution.py:379
  40.0 8.1 %collective-permute-start.10 = (bf16[2,64,256]{2,1,0:T(8,128)(2,1)S(1)}, bf16[2,64,256]{2,1,0:T(8,128)(2,1)S(1)}, u32[]{:S(2)}, u32[]{:S(2)}) collective-permute-start(bf16[2,64,256]{2,1,0:T(8,128)(2,1)S(1)} %get-tuple-element.56), channel_id=1, source_target_pairs={{0,8},{4,12},{8,0},{12,4},{1,9},{5,13},{9,1},{13,5},{2,10},{6,14},... | collective-permute-start | bytes 196616 | tf_op jit(solution)/shard_map/ppermute | solution.py:379
  43.8 6.1 %collective-permute-start.11 = (bf16[2,64,256]{2,1,0:T(8,128)(2,1)S(1)}, bf16[2,64,256]{2,1,0:T(8,128)(2,1)S(1)}, u32[]{:S(2)}, u32[]{:S(2)}) collective-permute-start(bf16[2,64,256]{2,1,0:T(8,128)(2,1)S(1)} %get-tuple-element.57), channel_id=1, source_target_pairs={{0,12},{4,8},{8,4},{12,0},{1,13},{5,9},{9,5},{13,1},{2,14},{6,10},... | collective-permute-start | bytes 196616 | tf_op jit(solution)/shard_map/ppermute | solution.py:379
  44.5 5.4 %collective-permute-start.12 = (bf16[2,64,256]{2,1,0:T(8,128)(2,1)S(1)}, bf16[2,64,256]{2,1,0:T(8,128)(2,1)S(1)}, u32[]{:S(2)}, u32[]{:S(2)}) collective-permute-start(bf16[2,64,256]{2,1,0:T(8,128)(2,1)S(1)} %get-tuple-element.58), channel_id=1, source_target_pairs={{0,4},{4,0},{8,12},{12,8},{1,5},{5,1},{9,13},{13,9},{2,6},{6,2},{1... | collective-permute-start | bytes 196616 | tf_op jit(solution)/shard_map/ppermute | solution.py:379

commit v9 on v8

--- a/solution.py
+++ b/solution.py
@@ -223,35 +223,45 @@
     diagonal = rows_of == lanes_of
     lane_head = lax.broadcasted_iota(jnp.int32, (BLOCK, WIDE), 1) // HEAD_DIM
     scale = HEAD_DIM**-0.5 * math.log2(math.e)
+    groups = half // WIDE
+    places = []
     for b in range(adjacency.shape[0]):
-        rows = slice(b * BLOCK, (b + 1) * BLOCK)
-        places = []
+        places.append([])
         for j in range(adjacency.shape[1]):
             m = adjacency[b, j]
             part = lax.rem(m, 2)
             core = lax.rem(m // 2, 2)
             distance = s ^ (m // 4)
             part = jnp.where(distance <= 1, part, part ^ h)
-            places.append((core ^ u, distance * 2 + part))
-        for g in range(half // WIDE):
-            columns = slice(g * WIDE, (g + 1) * WIDE)
-            keys = jnp.concatenate([table[i, p, :, columns] for i, p in places], axis=0)
-            vcolumns = slice(half + g * WIDE, half + (g + 1) * WIDE)
-            values = jnp.concatenate([table[i, p, :, vcolumns] for i, p in places], axis=0)
-            stacked = jnp.concatenate([q[rows, columns]] * QUAD, axis=0)
-            stacked = jnp.where(diagonal, stacked, jnp.zeros_like(stacked))
-            scores = lax.dot_general(
-                stacked, keys, (((1,), (1,)), ((), ())), preferred_element_type=jnp.float32
-            )
-            highest = jnp.max(scores, axis=-1, keepdims=True)
-            weights = jnp.exp2((scores - highest) * scale)
-            total = jnp.sum(weights, axis=-1, keepdims=True)
-            probs = (weights * (1.0 / total)).astype(jnp.bfloat16)
-            mixed = dot(probs, values)
-            merged = mixed[0:BLOCK, :]
-            for i in range(1, QUAD):
-                merged = jnp.where(lane_head == i, mixed[i * BLOCK : (i + 1) * BLOCK, :], merged)
-            att[rows, columns] = merged.astype(jnp.bfloat16)
+            places[b].append((core ^ u, distance * 2 + part))
+
+    def scores_of(step):
+        b, g = divmod(step, groups)
+        columns = slice(g * WIDE, (g + 1) * WIDE)
+        keys = jnp.concatenate([table[i, p, :, columns] for i, p in places[b]], axis=0)
+        stacked = jnp.concatenate([q[b * BLOCK : (b + 1) * BLOCK, columns]] * QUAD, axis=0)
+        stacked = jnp.where(diagonal, stacked, jnp.zeros_like(stacked))
+        return lax.dot_general(
+            stacked, keys, (((1,), (1,)), ((), ())), preferred_element_type=jnp.float32
+        )
+
+    steps = len(places) * groups
+    scores = scores_of(0)
+    for step in range(steps):
+        following = scores_of(step + 1) if step + 1 < steps else None
+        b, g = divmod(step, groups)
+        columns = slice(half + g * WIDE, half + (g + 1) * WIDE)
+        values = jnp.concatenate([table[i, p, :, columns] for i, p in places[b]], axis=0)
+        highest = jnp.max(scores, axis=-1, keepdims=True)
+        weights = jnp.exp2((scores - highest) * scale)
+        total = jnp.sum(weights, axis=-1, keepdims=True)
+        mixed = dot(weights.astype(jnp.bfloat16), values) * (1.0 / total)
+        merged = mixed[0:BLOCK, :]
+        for i in range(1, QUAD):
+            merged = jnp.where(lane_head == i, mixed[i * BLOCK : (i + 1) * BLOCK, :], merged)
+        rows = slice(b * BLOCK, (b + 1) * BLOCK)
+        att[rows, g * WIDE : (g + 1) * WIDE] = merged.astype(jnp.bfloat16)
+        scores = following
     project_out(0, att, mlp, wo, send, keep)
 
 
@@ -420,8 +430,8 @@
     farther = crossed(far, 1, shards)
     far_pair = swapped(far, "head")
     queries, mlp = run_mlp(flat, other, gain, wq, wup, wdn)
-    queries, mlp, farther = lax.optimization_barrier((queries, mlp, farther))
-    farther_pair = swapped(farther, "head")
+    queries, mlp, relayed = lax.optimization_barrier((queries, mlp, far_pair))
+    farther_pair = crossed(relayed, 1, shards)
     blocked = (-1, BLOCK, 2 * half)
     mine_a = run_project((mesh, near, far, far_pair, farther), wk, wv)
     sibling_a = swapped(mine_a, "sub")

time: 50.7 us -> 50.1 us (0.988)
  starting transfers between devices: 18.1 us -> 19.8 us
  waiting for transfers between devices: 15.2 us -> 13.5 us
  Pallas kernels: 17 us -> 16.4 us
    ppermute x7 -> x6, waiting for transfers between devices: 9.22 us -> 6.15 us  [swapped(): return lax.ppermute(x, axis, [(0, 1), (1, 0)])]
    ppermute x9 -> x10, waiting for transfers between devices: 5.99 us -> 7.38 us  [crossed(): return lax.ppermute(x, 'shard', [(i, i ^ distance) for i in range(size)])]
    ppermute x9 -> x10, starting transfers between devices: 12.9 us -> 14.1 us  [crossed(): return lax.ppermute(x, 'shard', [(i, i ^ distance) for i in range(size)])]
    pallas_call x1, Pallas kernels: 3.05 us -> 2.39 us  [run_attend(): pl.pallas_call(attend_kernel, out_shape=(part, part, jax.ShapeDtypeStruct...]
    ppermute x7 -> x6, starting transfers between devices: 5.14 us -> 5.61 us  [swapped(): return lax.ppermute(x, axis, [(0, 1), (1, 0)])]
  transfers between devices with their start and end apart: 16 -> 16, of which waited for: 7 -> 7; matrix products, arithmetic and copies ran while one was open for 0% -> 0% of each run, Pallas kernels for 26% -> 27%
where the time goes in v9:
time: 50.1 us; the launch traced here: 49.9 us
  starting transfers between devices  19.8 us (40%)
  Pallas kernels  16.4 us (33%)
  waiting for transfers between devices  13.5 us (27%)
    ppermute x10, starting transfers between devices, crossed(): return lax.ppermute(x, 'shard', [(i, i ^ distance) for i in range(size)])  14.1 us
    ppermute x10, waiting for transfers between devices, crossed(): return lax.ppermute(x, 'shard', [(i, i ^ distance) for i in range(size)])  7.38 us
    ppermute x6, waiting for transfers between devices, swapped(): return lax.ppermute(x, axis, [(0, 1), (1, 0)])  6.15 us
    ppermute x6, starting transfers between devices, swapped(): return lax.ppermute(x, axis, [(0, 1), (1, 0)])  5.61 us
    pallas_call x1, Pallas kernels, run_stage(): pl.pallas_call(functools.partial(stage_kernel, axes), out_shape=tuple((ja...  4.87 us
    pallas_call x1, Pallas kernels, run_mlp(): pl.pallas_call(mlp_kernel, out_shape=(jax.ShapeDtypeStruct((rows, wq.shap...  3.33 us
    pallas_call x1, Pallas kernels, run_attend(): pl.pallas_call(attend_kernel, out_shape=(part, part, jax.ShapeDtypeStruct...  2.39 us
    pallas_call x2, Pallas kernels, run_project(): pl.pallas_call(project_kernel, out_shape=jax.ShapeDtypeStruct((rows, 2 *...  1.59 us
  transfers between devices with their start and end apart: 16, of which 7 were waited for; matrix products, arithmetic and copies ran while one was open for 0% of the time, Pallas kernels for 27%

profile of v9, /device:TPU:0, one launch (start us, length us, event | category | flops | bytes accessed | tf_op | source)
XLA Modules:
  0.0 49.9 jit_solution(7661840548648002941)
XLA Ops:
  0.0 2.9 %collective-permute-start = (bf16[256,512]{1,0:T(8,128)(2,1)}, bf16[256,512]{1,0:T(8,128)(2,1)S(1)}, u32[]{:S(2)}, u32[]{:S(2)}) collective-permute-start(bf16[256,512]{1,0:T(8,128)(2,1)} %bitcast.8), channel_id=1, source_target_pairs={{0,2},{2,0},{1,3},{3,1},{4,6},{6,4},{5,7},{7,5},{8,10},{10,8},{9,1... | collective-permute-start | bytes 786440 | tf_op jit(solution)/shard_map/ppermute | solution.py:393
  2.9 0.9 %pick.1 = bf16[64,1024]{1,0:T(8,128)(2,1)S(1)} custom-call(bf16[128,1024]{1,0:T(8,128)(2,1)} %mesh.1), custom_call_target="tpu_custom_call" | custom-call | bytes 524288 | tf_op jit(solution)/shard_map/pick/pallas_call | solution.py:108
  3.9 2.7 %collective-permute-start.1 = (bf16[64,1024]{1,0:T(8,128)(2,1)S(1)}, bf16[64,1024]{1,0:T(8,128)(2,1)S(1)}, u32[]{:S(2)}, u32[]{:S(2)}) collective-permute-start(bf16[64,1024]{1,0:T(8,128)(2,1)S(1)} %pick.1), channel_id=1, source_target_pairs={{0,8},{4,12},{8,0},{12,4},{1,9},{5,13},{9,1},{13,5},{2,10},{6,14},... | collective-permute-start | bytes 393224 | tf_op jit(solution)/shard_map/ppermute | solution.py:389
  6.5 1.6 %collective-permute-start.5 = (bf16[128,1024]{1,0:T(8,128)(2,1)}, bf16[128,1024]{1,0:T(8,128)(2,1)S(1)}, u32[]{:S(2)}, u32[]{:S(2)}) collective-permute-start(bf16[128,1024]{1,0:T(8,128)(2,1)} %mesh.1), channel_id=1, source_target_pairs={{0,4},{4,0},{8,12},{12,8},{1,5},{5,1},{9,13},{13,9},{2,6},{6,2},{1... | collective-permute-start | bytes 786440 | tf_op jit(solution)/shard_map/ppermute | solution.py:389
  8.1 4.9 %stage.1 = (bf16[256,512]{1,0:T(8,128)(2,1)S(1)}, f32[1,1024]{1,0:T(1,128)S(1)}, bf16[1024,512]{1,0:T(8,128)(2,1)S(1)}, bf16[1024,2048]{1,0:T(8,128)(2,1)S(1)}, ...) custom-call(bf16[256,512]{1,0:T(8,128)(2,1)} %bitcast.9, ...), custom_call_target="tpu_custom_call" | custom-call | bytes 262184960 | tf_op jit(solution)/shard_map/stage/pallas_call | solution.py:145
  13.0 0.0 collective-permute-done.1.refs_2_
  13.0 0.6 %collective-permute-start.2 = (bf16[64,1024]{1,0:T(8,128)(2,1)S(1)}, bf16[64,1024]{1,0:T(8,128)(2,1)S(1)}, u32[]{:S(2)}, u32[]{:S(2)}) collective-permute-start(bf16[64,1024]{1,0:T(8,128)(2,1)S(1)} %collective-permute-done.1.refs_2_), channel_id=1, source_target_pairs={{0,2},{2,0},{1,3},{3,1},{4,6},{6,4},{5,7},{7,5},{8,10},{10,8},{9,1... | collective-permute-start | bytes 393224 | tf_op jit(solution)/shard_map/ppermute | solution.py:393
  13.6 0.4 collective-permute-start.6
  14.0 0.0 collective-permute-done.other
  14.0 3.3 %mlp.1 = (bf16[256,512]{1,0:T(8,128)(2,1)S(1)}, f32[256,1024]{1,0:T(8,128)S(1)}) custom-call(bf16[256,512]{1,0:T(8,128)(2,1)S(1)} %get-tuple-element.34.own, bf16[256,512]{1,0:T(8,128)(2,1)S(1)} %collective-permute-done.other, f32[1,1024]{1,0:T(1,128)S(1)} %get-tuple-element.35.gain, bf16[1024,512]{1,0:T(8,128)(2,1)S(1)} %get-tuple-element.36.wq, ...), custom_call_target="tpu_custom_call" | custom-call | flops 2415919104 | bytes 9437184 | tf_op jit(solution)/shard_map/mlp/pallas_call | solution.py:81
  17.4 0.6 %collective-permute-done.2.refs_3_ = bf16[64,1024]{1,0:T(8,128)(2,1)S(1)} collective-permute-done((bf16[64,1024]{1,0:T(8,128)(2,1)S(1)}, bf16[64,1024]{1,0:T(8,128)(2,1)S(1)}, u32[]{:S(2)}, u32[]{:S(2)}) %collective-permute-start.2) | collective-permute-done | bytes 131104 | tf_op jit(solution)/shard_map/ppermute | solution.py:393
  18.0 1.0 %collective-permute-start.3 = (bf16[64,1024]{1,0:T(8,128)(2,1)S(1)}, bf16[64,1024]{1,0:T(8,128)(2,1)S(1)}, u32[]{:S(2)}, u32[]{:S(2)}) collective-permute-start(bf16[64,1024]{1,0:T(8,128)(2,1)S(1)} %collective-permute-done.2.refs_3_), channel_id=1, source_target_pairs={{0,4},{4,0},{8,12},{12,8},{1,5},{5,1},{9,13},{13,9},{2,6},{6,2},{1... | collective-permute-start | bytes 393224 | tf_op jit(solution)/shard_map/ppermute | solution.py:389
  19.0 0.0 collective-permute-done.6.refs_4_
  19.0 0.0 collective-permute-done.5.refs_1_
  19.0 1.1 %project.3 = bf16[448,1024]{1,0:T(8,128)(2,1)S(1)} custom-call(bf16[128,1024]{1,0:T(8,128)(2,1)S(1)} %get-tuple-element.45.refs_0_, bf16[128,1024]{1,0:T(8,128)(2,1)S(1)} %collective-permute-done.5.refs_1_, bf16[64,1024]{1,0:T(8,128)(2,1)S(1)} %collective-permute-done.1.refs_2_, bf16[64,1024]{1,0:T(8,128)(2,1)S(1)} %collective-permute-done.2.refs_3_, ...), custom_call_target="tpu_custom_call" | custom-call | flops 70464307200 | bytes 294912000 | tf_op jit(solution)/shard_map/project/pallas_call | solution.py:168
  20.2 0.0 copy-start.1
  20.2 0.1 collective-permute-start.7
  20.2 2.7 %collective-permute-done.3.refs_0_ = bf16[64,1024]{1,0:T(8,128)(2,1)S(1)} collective-permute-done((bf16[64,1024]{1,0:T(8,128)(2,1)S(1)}, bf16[64,1024]{1,0:T(8,128)(2,1)S(1)}, u32[]{:S(2)}, u32[]{:S(2)}) %collective-permute-start.3) | collective-permute-done | bytes 131104 | tf_op jit(solution)/shard_map/ppermute | solution.py:389
  23.0 0.5 project.2
  23.5 0.1 collective-permute-start.4
  23.5 0.0 collective-permute-done.7
  23.6 0.1 table.1.table_in
  23.7 1.2 %collective-permute-done.4 = bf16[64,1024]{1,0:T(8,128)(2,1)S(1)} collective-permute-done((bf16[64,1024]{1,0:T(8,128)(2,1)S(1)}, bf16[64,1024]{1,0:T(8,128)(2,1)S(1)}, u32[]{:S(2)}, u32[]{:S(2)}) %collective-permute-start.4) | collective-permute-done | bytes 131104 | tf_op jit(solution)/shard_map/ppermute | solution.py:393
  24.9 0.0 copy-done.1
  24.9 2.4 %attend.1 = (bf16[256,256]{1,0:T(8,128)(2,1)S(1)}, bf16[256,256]{1,0:T(8,128)(2,1)S(1)}, bf16[256,512]{1,0:T(8,128)(2,1)S(1)}, bf16[2,8,64,1024]{3,2,1,0:T(8,128)(2,1)S(1)}) custom-call(s32[4,8]{1,0:T(4,128)S(1)} %copy-done.1, bf16[256,512]{1,0:T(8,128)(2,1)S(1)} %get-tuple-element.41.q, ...), custom_call_target="tpu_custom_call", output_to_operand_aliasing={{3}: (4, {})} | custom-call | flops 13421772800 | bytes 41943040 | tf_op jit(solution)/shard_map/attend/pallas_call | solution.py:272
  27.3 1.0 %collective-permute-start.8 = (bf16[256,256]{1,0:T(8,128)(2,1)S(1)}, bf16[256,256]{1,0:T(8,128)(2,1)S(1)}, u32[]{:S(2)}, u32[]{:S(2)}) collective-permute-start(bf16[256,256]{1,0:T(8,128)(2,1)S(1)} %get-tuple-element.51), channel_id=1, source_target_pairs={{0,2},{2,0},{1,3},{3,1},{4,6},{6,4},{5,7},{7,5},{8,10},{10,8},{9,1... | collective-permute-start | bytes 393224 | tf_op jit(solution)/shard_map/ppermute | solution.py:393
  28.3 0.0 copy-start.2
  28.3 0.0 copy-start
  28.3 0.3 project_out.1
  28.6 4.3 %collective-permute-done.8.received = bf16[256,256]{1,0:T(8,128)(2,1)S(1)} collective-permute-done((bf16[256,256]{1,0:T(8,128)(2,1)S(1)}, bf16[256,256]{1,0:T(8,128)(2,1)S(1)}, u32[]{:S(2)}, u32[]{:S(2)}) %collective-permute-start.8) | collective-permute-done | bytes 131104 | tf_op jit(solution)/shard_map/ppermute | solution.py:393
  32.9 0.9 %collective-permute-start.9 = (bf16[256,256]{1,0:T(8,128)(2,1)S(1)}, bf16[256,256]{1,0:T(8,128)(2,1)S(1)}, u32[]{:S(2)}, u32[]{:S(2)}) collective-permute-start(bf16[256,256]{1,0:T(8,128)(2,1)S(1)} %get-tuple-element.52), channel_id=1, source_target_pairs={{0,2},{2,0},{1,3},{3,1},{4,6},{6,4},{5,7},{7,5},{8,10},{10,8},{9,1... | collective-permute-start | bytes 393224 | tf_op jit(solution)/shard_map/ppermute | solution.py:393
  33.8 0.0 copy-done.2
  33.8 0.1 copy.15.owners
  33.9 0.0 copy-done
  33.9 0.7 %combine.2 = (bf16[2,64,256]{2,1,0:T(8,128)(2,1)S(1)}, bf16[2,64,256]{2,1,0:T(8,128)(2,1)S(1)}, bf16[2,64,256]{2,1,0:T(8,128)(2,1)S(1)}, bf16[2,64,256]{2,1,0:T(8,128)(2,1)S(1)}) custom-call(s32[4,1]{1,0:T(4,128)S(1)} %copy.15.owners, bf16[4,64,512]{2,1,0:T(8,128)(2,1)S(1)} %copy-done, bf16[256,256]{1,0:T(8,128)(2,1)S(1)} %get-tuple-element.53.keep, ...), custom_call_target="tpu_custom_call" | custom-call | flops 196608000 | bytes 131072000 | tf_op jit(solution)/shard_map/combine/pallas_call | solution.py:340
  34.6 3.3 %collective-permute-start.13 = (bf16[2,64,256]{2,1,0:T(8,128)(2,1)S(1)}, bf16[2,64,256]{2,1,0:T(8,128)(2,1)S(1)}, u32[]{:S(2)}, u32[]{:S(2)}) collective-permute-start(bf16[2,64,256]{2,1,0:T(8,128)(2,1)S(1)} %get-tuple-element.60), channel_id=1, source_target_pairs={{0,8},{4,12},{8,0},{12,4},{1,9},{5,13},{9,1},{13,5},{2,10},{6,14},... | collective-permute-start | bytes 196616 | tf_op jit(solution)/shard_map/ppermute | solution.py:389
  37.9 0.7 %collective-permute-start.14 = (bf16[2,64,256]{2,1,0:T(8,128)(2,1)S(1)}, bf16[2,64,256]{2,1,0:T(8,128)(2,1)S(1)}, u32[]{:S(2)}, u32[]{:S(2)}) collective-permute-start(bf16[2,64,256]{2,1,0:T(8,128)(2,1)S(1)} %get-tuple-element.61), channel_id=1, source_target_pairs={{0,12},{4,8},{8,4},{12,0},{1,13},{5,9},{9,5},{13,1},{2,14},{6,10},... | collective-permute-start | bytes 196616 | tf_op jit(solution)/shard_map/ppermute | solution.py:389
  38.6 0.0 collective-permute-start.15
  38.6 0.0 collective-permute-done.9.received
  38.6 0.7 %combine.3 = (bf16[2,64,256]{2,1,0:T(8,128)(2,1)S(1)}, bf16[2,64,256]{2,1,0:T(8,128)(2,1)S(1)}, bf16[2,64,256]{2,1,0:T(8,128)(2,1)S(1)}, bf16[2,64,256]{2,1,0:T(8,128)(2,1)S(1)}) custom-call(s32[4,1]{1,0:T(4,128)S(1)} %copy.15.owners, bf16[4,64,512]{2,1,0:T(8,128)(2,1)S(1)} %copy-done, bf16[256,256]{1,0:T(8,128)(2,1)S(1)} %get-tuple-element.49.keep, ...), custom_call_target="tpu_custom_call" | custom-call | flops 196608000 | bytes 131072000 | tf_op jit(solution)/shard_map/combine/pallas_call | solution.py:340
  39.3 3.8 %collective-permute-start.10 = (bf16[2,64,256]{2,1,0:T(8,128)(2,1)S(1)}, bf16[2,64,256]{2,1,0:T(8,128)(2,1)S(1)}, u32[]{:S(2)}, u32[]{:S(2)}) collective-permute-start(bf16[2,64,256]{2,1,0:T(8,128)(2,1)S(1)} %get-tuple-element.56), channel_id=1, source_target_pairs={{0,8},{4,12},{8,0},{12,4},{1,9},{5,13},{9,1},{13,5},{2,10},{6,14},... | collective-permute-start | bytes 196616 | tf_op jit(solution)/shard_map/ppermute | solution.py:389
  43.1 0.7 %collective-permute-start.11 = (bf16[2,64,256]{2,1,0:T(8,128)(2,1)S(1)}, bf16[2,64,256]{2,1,0:T(8,128)(2,1)S(1)}, u32[]{:S(2)}, u32[]{:S(2)}) collective-permute-start(bf16[2,64,256]{2,1,0:T(8,128)(2,1)S(1)} %get-tuple-element.57), channel_id=1, source_target_pairs={{0,12},{4,8},{8,4},{12,0},{1,13},{5,9},{9,5},{13,1},{2,14},{6,10},... | collective-permute-start | bytes 196616 | tf_op jit(solution)/shard_map/ppermute | solution.py:389
  43.8 0.0 collective-permute-done.13.refs_0_
  43.8 0.0 collective-permute-start.12
  43.8 0.3 collective-permute-done.14.refs_1_
  44.1 0.0 collective-permute-done.15.refs_2_
  44.1 0.7 %place.2.refs_4_ = bf16[8,64,512]{2,1,0:T(8,128)(2,1)} custom-call(bf16[2,64,256]{2,1,0:T(8,128)(2,1)S(1)} %collective-permute-done.13.refs_0_, bf16[2,64,256]{2,1,0:T(8,128)(2,1)S(1)} %collective-permute-done.14.refs_1_, bf16[2,64,256]{2,1,0:T(8,128)(2,1)S(1)} %collective-permute-done.15.refs_2_, bf16[2,64,256]{2,1,0:T(8,128)(2,1)S(1)} %get-tuple-element.54.refs_3_), custom_call_target="tpu_custom_call" | custom-call | bytes 5242880 | tf_op jit(solution)/shard_map/place/pallas_call | solution.py:373
  44.8 2.7 %collective-permute-done.10.refs_0_ = bf16[2,64,256]{2,1,0:T(8,128)(2,1)S(1)} collective-permute-done((bf16[2,64,256]{2,1,0:T(8,128)(2,1)S(1)}, bf16[2,64,256]{2,1,0:T(8,128)(2,1)S(1)}, u32[]{:S(2)}, u32[]{:S(2)}) %collective-permute-start.10) | collective-permute-done | bytes 65568 | tf_op jit(solution)/shard_map/ppermute | solution.py:389
  47.5 1.7 %collective-permute-done.11.refs_1_ = bf16[2,64,256]{2,1,0:T(8,128)(2,1)S(1)} collective-permute-done((bf16[2,64,256]{2,1,0:T(8,128)(2,1)S(1)}, bf16[2,64,256]{2,1,0:T(8,128)(2,1)S(1)}, u32[]{:S(2)}, u32[]{:S(2)}) %collective-permute-start.11) | collective-permute-done | bytes 65568 | tf_op jit(solution)/shard_map/ppermute | solution.py:389
  49.2 0.0 collective-permute-done.12.refs_2_
  49.2 0.7 %place.3 = bf16[8,64,512]{2,1,0:T(8,128)(2,1)} custom-call(bf16[2,64,256]{2,1,0:T(8,128)(2,1)S(1)} %collective-permute-done.10.refs_0_, bf16[2,64,256]{2,1,0:T(8,128)(2,1)S(1)} %collective-permute-done.11.refs_1_, bf16[2,64,256]{2,1,0:T(8,128)(2,1)S(1)} %collective-permute-done.12.refs_2_, ...), custom_call_target="tpu_custom_call", output_to_operand_aliasing={{}: (4, {})} | custom-call | bytes 5242880 | tf_op jit(solution)/shard_map/place/pallas_call | solution.py:373
Async XLA Ops:
  0.0 14.0 %collective-permute-start = (bf16[256,512]{1,0:T(8,128)(2,1)}, bf16[256,512]{1,0:T(8,128)(2,1)S(1)}, u32[]{:S(2)}, u32[]{:S(2)}) collective-permute-start(bf16[256,512]{1,0:T(8,128)(2,1)} %bitcast.8), channel_id=1, source_target_pairs={{0,2},{2,0},{1,3},{3,1},{4,6},{6,4},{5,7},{7,5},{8,10},{10,8},{9,1... | collective-permute-start | bytes 786440 | tf_op jit(solution)/shard_map/ppermute | solution.py:393
  3.9 9.1 %collective-permute-start.1 = (bf16[64,1024]{1,0:T(8,128)(2,1)S(1)}, bf16[64,1024]{1,0:T(8,128)(2,1)S(1)}, u32[]{:S(2)}, u32[]{:S(2)}) collective-permute-start(bf16[64,1024]{1,0:T(8,128)(2,1)S(1)} %pick.1), channel_id=1, source_target_pairs={{0,8},{4,12},{8,0},{12,4},{1,9},{5,13},{9,1},{13,5},{2,10},{6,14},... | collective-permute-start | bytes 393224 | tf_op jit(solution)/shard_map/ppermute | solution.py:389
  6.5 12.5 %collective-permute-start.5 = (bf16[128,1024]{1,0:T(8,128)(2,1)}, bf16[128,1024]{1,0:T(8,128)(2,1)S(1)}, u32[]{:S(2)}, u32[]{:S(2)}) collective-permute-start(bf16[128,1024]{1,0:T(8,128)(2,1)} %mesh.1), channel_id=1, source_target_pairs={{0,4},{4,0},{8,12},{12,8},{1,5},{5,1},{9,13},{13,9},{2,6},{6,2},{1... | collective-permute-start | bytes 786440 | tf_op jit(solution)/shard_map/ppermute | solution.py:389
  13.0 5.0 %collective-permute-start.2 = (bf16[64,1024]{1,0:T(8,128)(2,1)S(1)}, bf16[64,1024]{1,0:T(8,128)(2,1)S(1)}, u32[]{:S(2)}, u32[]{:S(2)}) collective-permute-start(bf16[64,1024]{1,0:T(8,128)(2,1)S(1)} %collective-permute-done.1.refs_2_), channel_id=1, source_target_pairs={{0,2},{2,0},{1,3},{3,1},{4,6},{6,4},{5,7},{7,5},{8,10},{10,8},{9,1... | collective-permute-start | bytes 393224 | tf_op jit(solution)/shard_map/ppermute | solution.py:393
  13.6 5.4 %collective-permute-start.6 = (bf16[64,1024]{1,0:T(8,128)(2,1)S(1)}, bf16[64,1024]{1,0:T(8,128)(2,1)S(1)}, u32[]{:S(2)}, u32[]{:S(2)}) collective-permute-start(bf16[64,1024]{1,0:T(8,128)(2,1)S(1)} %collective-permute-done.1.refs_2_), channel_id=1, source_target_pairs={{0,4},{4,0},{8,12},{12,8},{1,5},{5,1},{9,13},{13,9},{2,6},{6,2},{1... | collective-permute-start | bytes 393224 | tf_op jit(solution)/shard_map/ppermute | solution.py:389
  18.0 5.0 %collective-permute-start.3 = (bf16[64,1024]{1,0:T(8,128)(2,1)S(1)}, bf16[64,1024]{1,0:T(8,128)(2,1)S(1)}, u32[]{:S(2)}, u32[]{:S(2)}) collective-permute-start(bf16[64,1024]{1,0:T(8,128)(2,1)S(1)} %collective-permute-done.2.refs_3_), channel_id=1, source_target_pairs={{0,4},{4,0},{8,12},{12,8},{1,5},{5,1},{9,13},{13,9},{2,6},{6,2},{1... | collective-permute-start | bytes 393224 | tf_op jit(solution)/shard_map/ppermute | solution.py:389
  20.2 4.7 %copy-start.1 = (s32[4,8]{1,0:T(4,128)S(1)}, s32[4,8]{1,0:T(4,128)}, u32[]{:S(2)}) copy-start(s32[4,8]{1,0:T(4,128)} %adjacency.1) | copy-start | bytes 388
  20.2 3.4 %collective-permute-start.7 = (bf16[448,1024]{1,0:T(8,128)(2,1)S(1)}, bf16[448,1024]{1,0:T(8,128)(2,1)S(1)}, u32[]{:S(2)}, u32[]{:S(2)}) collective-permute-start(bf16[448,1024]{1,0:T(8,128)(2,1)S(1)} %project.3), channel_id=1, source_target_pairs={{0,1},{1,0},{2,3},{3,2},{4,5},{5,4},{6,7},{7,6},{8,9},{9,8},{10,11... | collective-permute-start | bytes 2752520 | tf_op jit(solution)/shard_map/ppermute | solution.py:393
  23.5 1.4 %collective-permute-start.4 = (bf16[64,1024]{1,0:T(8,128)(2,1)S(1)}, bf16[64,1024]{1,0:T(8,128)(2,1)S(1)}, u32[]{:S(2)}, u32[]{:S(2)}) collective-permute-start(bf16[64,1024]{1,0:T(8,128)(2,1)S(1)} %project.2), channel_id=1, source_target_pairs={{0,1},{1,0},{2,3},{3,2},{4,5},{5,4},{6,7},{7,6},{8,9},{9,8},{10,11... | collective-permute-start | bytes 393224 | tf_op jit(solution)/shard_map/ppermute | solution.py:393
  27.3 5.6 %collective-permute-start.8 = (bf16[256,256]{1,0:T(8,128)(2,1)S(1)}, bf16[256,256]{1,0:T(8,128)(2,1)S(1)}, u32[]{:S(2)}, u32[]{:S(2)}) collective-permute-start(bf16[256,256]{1,0:T(8,128)(2,1)S(1)} %get-tuple-element.51), channel_id=1, source_target_pairs={{0,2},{2,0},{1,3},{3,1},{4,6},{6,4},{5,7},{7,5},{8,10},{10,8},{9,1... | collective-permute-start | bytes 393224 | tf_op jit(solution)/shard_map/ppermute | solution.py:393
  28.3 5.6 %copy-start.2 = (s32[4,1]{0,1:T(1,128)S(1)}, s32[4,1]{0,1:T(1,128)}, u32[]{:S(2)}) copy-start(s32[4,1]{0,1:T(1,128)} %param.12) | copy-start | bytes 52
  28.3 5.6 %copy-start = (bf16[4,64,512]{2,1,0:T(8,128)(2,1)S(1)}, bf16[4,64,512]{2,1,0:T(8,128)(2,1)}, u32[]{:S(2)}) copy-start(bf16[4,64,512]{2,1,0:T(8,128)(2,1)} %grid_features.3) | copy-start | bytes 786436
  32.9 5.7 %collective-permute-start.9 = (bf16[256,256]{1,0:T(8,128)(2,1)S(1)}, bf16[256,256]{1,0:T(8,128)(2,1)S(1)}, u32[]{:S(2)}, u32[]{:S(2)}) collective-permute-start(bf16[256,256]{1,0:T(8,128)(2,1)S(1)} %get-tuple-element.52), channel_id=1, source_target_pairs={{0,2},{2,0},{1,3},{3,1},{4,6},{6,4},{5,7},{7,5},{8,10},{10,8},{9,1... | collective-permute-start | bytes 393224 | tf_op jit(solution)/shard_map/ppermute | solution.py:393
  34.6 9.2 %collective-permute-start.13 = (bf16[2,64,256]{2,1,0:T(8,128)(2,1)S(1)}, bf16[2,64,256]{2,1,0:T(8,128)(2,1)S(1)}, u32[]{:S(2)}, u32[]{:S(2)}) collective-permute-start(bf16[2,64,256]{2,1,0:T(8,128)(2,1)S(1)} %get-tuple-element.60), channel_id=1, source_target_pairs={{0,8},{4,12},{8,0},{12,4},{1,9},{5,13},{9,1},{13,5},{2,10},{6,14},... | collective-permute-start | bytes 196616 | tf_op jit(solution)/shard_map/ppermute | solution.py:389
  37.9 6.1 %collective-permute-start.14 = (bf16[2,64,256]{2,1,0:T(8,128)(2,1)S(1)}, bf16[2,64,256]{2,1,0:T(8,128)(2,1)S(1)}, u32[]{:S(2)}, u32[]{:S(2)}) collective-permute-start(bf16[2,64,256]{2,1,0:T(8,128)(2,1)S(1)} %get-tuple-element.61), channel_id=1, source_target_pairs={{0,12},{4,8},{8,4},{12,0},{1,13},{5,9},{9,5},{13,1},{2,14},{6,10},... | collective-permute-start | bytes 196616 | tf_op jit(solution)/shard_map/ppermute | solution.py:389
  38.6 5.4 %collective-permute-start.15 = (bf16[2,64,256]{2,1,0:T(8,128)(2,1)S(1)}, bf16[2,64,256]{2,1,0:T(8,128)(2,1)S(1)}, u32[]{:S(2)}, u32[]{:S(2)}) collective-permute-start(bf16[2,64,256]{2,1,0:T(8,128)(2,1)S(1)} %get-tuple-element.62), channel_id=1, source_target_pairs={{0,4},{4,0},{8,12},{12,8},{1,5},{5,1},{9,13},{13,9},{2,6},{6,2},{1... | collective-permute-start | bytes 196616 | tf_op jit(solution)/shard_map/ppermute | solution.py:389
  39.3 8.1 %collective-permute-start.10 = (bf16[2,64,256]{2,1,0:T(8,128)(2,1)S(1)}, bf16[2,64,256]{2,1,0:T(8,128)(2,1)S(1)}, u32[]{:S(2)}, u32[]{:S(2)}) collective-permute-start(bf16[2,64,256]{2,1,0:T(8,128)(2,1)S(1)} %get-tuple-element.56), channel_id=1, source_target_pairs={{0,8},{4,12},{8,0},{12,4},{1,9},{5,13},{9,1},{13,5},{2,10},{6,14},... | collective-permute-start | bytes 196616 | tf_op jit(solution)/shard_map/ppermute | solution.py:389
  43.1 6.1 %collective-permute-start.11 = (bf16[2,64,256]{2,1,0:T(8,128)(2,1)S(1)}, bf16[2,64,256]{2,1,0:T(8,128)(2,1)S(1)}, u32[]{:S(2)}, u32[]{:S(2)}) collective-permute-start(bf16[2,64,256]{2,1,0:T(8,128)(2,1)S(1)} %get-tuple-element.57), channel_id=1, source_target_pairs={{0,12},{4,8},{8,4},{12,0},{1,13},{5,9},{9,5},{13,1},{2,14},{6,10},... | collective-permute-start | bytes 196616 | tf_op jit(solution)/shard_map/ppermute | solution.py:389
  43.8 5.4 %collective-permute-start.12 = (bf16[2,64,256]{2,1,0:T(8,128)(2,1)S(1)}, bf16[2,64,256]{2,1,0:T(8,128)(2,1)S(1)}, u32[]{:S(2)}, u32[]{:S(2)}) collective-permute-start(bf16[2,64,256]{2,1,0:T(8,128)(2,1)S(1)} %get-tuple-element.58), channel_id=1, source_target_pairs={{0,4},{4,0},{8,12},{12,8},{1,5},{5,1},{9,13},{13,9},{2,6},{6,2},{1... | collective-permute-start | bytes 196616 | tf_op jit(solution)/shard_map/ppermute | solution.py:389

commit v10 on v9

--- a/solution.py
+++ b/solution.py
@@ -14,7 +14,7 @@
 BLOCK = 64
 QUAD = 4
 WIDE = QUAD * HEAD_DIM
-CHUNKS = 2
+WIDTHS = (128, 128, 256)
 MIB = 1 << 20
 
 
@@ -199,11 +199,15 @@
     )(mine, sibling)
 
 
+def columns_of(c):
+    return slice(sum(WIDTHS[:c]), sum(WIDTHS[: c + 1]))
+
+
 def project_out(c, att, mlp, wo, send, keep):
-    width = send.shape[1]
     half = att.shape[1]
+    chunk = columns_of(c)
     for out, first in ((send, 0), (keep, half)):
-        span = slice(first + c * width, first + (c + 1) * width)
+        span = slice(first + chunk.start, first + chunk.stop)
         out[...] = (mlp[:, span] + dot(att[...], wo[:, span])).astype(jnp.bfloat16)
 
 
@@ -267,7 +271,7 @@
 
 def run_attend(adjacency, q, mine, sibling, table, mlp, wo):
     rows, half = q.shape
-    part = jax.ShapeDtypeStruct((rows, half // CHUNKS), jnp.bfloat16)
+    part = jax.ShapeDtypeStruct((rows, WIDTHS[0]), jnp.bfloat16)
     blocks = table.shape[0] * table.shape[1]
     send, keep, att, _ = pl.pallas_call(
         attend_kernel,
@@ -293,7 +297,7 @@
 
 def run_project_out(c, att, mlp, wo):
     rows, half = att.shape
-    part = jax.ShapeDtypeStruct((rows, half // CHUNKS), jnp.bfloat16)
+    part = jax.ShapeDtypeStruct((rows, WIDTHS[c]), jnp.bfloat16)
     return pl.pallas_call(
         functools.partial(project_out, c),
         out_shape=(part, part),
@@ -309,14 +313,15 @@
     )(att, mlp, wo)
 
 
-def combine_kernel(c, owners, grid_features, keep, received, *outs):
+def combine_kernel(chunks, distances, owners, grid_features, *refs):
     s = lax.axis_index("shard")
+    keeps, refs = refs[: len(chunks)], refs[len(chunks) :]
+    swaps, outs = refs[: len(chunks)], refs[len(chunks) :]
     count = grid_features.shape[0]
-    width = keep.shape[1]
     names = [owners[t, 0] for t in range(count)]
-    for d, out in enumerate(outs):
-        for j in range(CAP):
-            out[j] = jnp.zeros(out.shape[1:], jnp.bfloat16)
+    first = columns_of(chunks[0]).start
+    for d, out in zip(distances, outs):
+        out[...] = jnp.zeros(out.shape, jnp.bfloat16)
         seen = jnp.int32(0)
         for t in range(count):
             hit = names[t] == s ^ d
@@ -325,40 +330,42 @@
             @pl.when(hit)
             def _():
                 rows = slice(t * BLOCK, (t + 1) * BLOCK)
-                partials = keep[rows, :].astype(jnp.float32)
-                partials = partials + received[rows, :].astype(jnp.float32)
-                residual = grid_features[t, :, c * width : (c + 1) * width]
-                out[rank] = (residual.astype(jnp.float32) + partials).astype(jnp.bfloat16)
+                for c, keep, swap in zip(chunks, keeps, swaps):
+                    columns = columns_of(c)
+                    partials = keep[rows, :].astype(jnp.float32)
+                    partials = partials + swap[rows, :].astype(jnp.float32)
+                    residual = grid_features[t, :, columns].astype(jnp.float32)
+                    place = slice(columns.start - first, columns.stop - first)
+                    out[rank, :, place] = (residual + partials).astype(jnp.bfloat16)
 
             seen = seen + hit.astype(jnp.int32)
 
 
-def run_combine(c, owners, grid_features, keep, received, shards):
+def run_combine(chunks, distances, owners, grid_features, keeps, swaps):
     count, rows, _ = grid_features.shape
-    width = keep.shape[1]
+    width = sum(WIDTHS[c] for c in chunks)
     slot = jax.ShapeDtypeStruct((CAP, rows, width), jnp.bfloat16)
     return pl.pallas_call(
-        functools.partial(combine_kernel, c),
-        out_shape=(slot,) * shards,
-        in_specs=[whole(pltpu.SMEM)] + vmem(3),
-        out_specs=tuple(vmem(shards)),
+        functools.partial(combine_kernel, chunks, distances),
+        out_shape=(slot,) * len(distances),
+        in_specs=[whole(pltpu.SMEM)] + vmem(1 + 2 * len(chunks)),
+        out_specs=tuple(vmem(len(distances))),
         compiler_params=params(8),
         cost_estimate=pl.CostEstimate(
             flops=3000 * count * rows * width,
-            bytes_accessed=400 * rows * width * (3 * count + CAP * shards),
+            bytes_accessed=400 * rows * width * (3 * count + CAP * len(distances)),
             transcendentals=0,
         ),
         name="combine",
-    )(owners, grid_features, keep, received)
-
-
-def place_kernel(c, order, *refs):
+    )(owners, grid_features, *keeps, *swaps)
+
+
+def place_kernel(spots, *refs):
     out, sem = refs[-2:]
     s = lax.axis_index("shard")
     copies = []
-    for i, d in enumerate(order):
-        width = refs[i].shape[2]
-        columns = pl.ds(c * width, width)
+    for i, (d, first) in enumerate(spots):
+        columns = pl.ds(first, refs[i].shape[2])
         slots = pl.ds((s ^ d) * CAP, CAP)
         copies.append(pltpu.make_async_copy(refs[i], out.at[slots, :, columns], sem.at[i]))
         copies[i].start()
@@ -366,20 +373,17 @@
         copy.wait()
 
 
-def run_place(c, order, arrived, placed):
-    shards = len(arrived)
-    _, rows, width = arrived[0].shape
-    shape = (shards * CAP, rows, CHUNKS * width)
-    return pl.pallas_call(
-        functools.partial(place_kernel, c, order),
+def run_place(spots, arrived, placed, shape):
+    return pl.pallas_call(
+        functools.partial(place_kernel, spots),
         out_shape=jax.ShapeDtypeStruct(shape, jnp.bfloat16),
-        in_specs=vmem(shards) + [whole(pltpu.HBM)] * len(placed),
+        in_specs=vmem(len(arrived)) + [whole(pltpu.HBM)] * len(placed),
         out_specs=whole(pltpu.HBM),
-        scratch_shapes=[pltpu.SemaphoreType.DMA((shards,))],
-        input_output_aliases={shards: 0} if placed else {},
+        scratch_shapes=[pltpu.SemaphoreType.DMA((len(arrived),))],
+        input_output_aliases={len(arrived): 0} if placed else {},
         compiler_params=params(4),
         cost_estimate=pl.CostEstimate(
-            flops=0, bytes_accessed=40 * CAP * shards * rows * width, transcendentals=0
+            flops=400000 * sum(part.size for part in arrived), bytes_accessed=0, transcendentals=0
         ),
         name="place",
     )(*arrived, *placed)
@@ -441,19 +445,28 @@
     send, keep, att = run_attend(
         adjacency, queries, mine_b.reshape(blocked), sibling_b.reshape(blocked), table, mlp, wo
     )
-    placed = []
-    slots = None
-    for c in range(CHUNKS):
+    keeps, swaps, slots, placed = [], [], [], []
+    shape = (shards * CAP, rows, half)
+    for c in range(len(WIDTHS)):
         if c > 0:
             send, keep = run_project_out(c, att, mlp, wo)
-            send, _ = lax.optimization_barrier((send, received))
         received = swapped(send, "head")
-        if slots is not None:
-            received, _ = lax.optimization_barrier((received, slots[0]))
-        slots = run_combine(c, owners, grid_features, keep, received, shards)
-        order = (2, 3, 1, 0)
-        arrived = [crossed(slots[d], d, shards) if d else slots[d] for d in order]
-        placed = [run_place(c, order, arrived, placed)]
+        if c > 0:
+            received, _ = lax.optimization_barrier((received, slots[c - 1][0]))
+        slots.append(run_combine((c,), (2, 3), owners, grid_features, (keep,), (received,)))
+        keeps.append(keep)
+        swaps.append(received)
+    every = tuple(range(len(WIDTHS)))
+    swaps[-1], _ = lax.optimization_barrier((swaps[-1], slots[-1][0]))
+    near_slots, own_slots = run_combine(every, (1, 0), owners, grid_features, keeps, swaps)
+    for c in every:
+        first = columns_of(c).start
+        spots = [(2, first), (3, first)]
+        arrived = [crossed(slot, d, shards) for d, slot in zip((2, 3), slots[c])]
+        if c == len(WIDTHS) - 1:
+            spots += [(1, 0), (0, 0)]
+            arrived += [crossed(near_slots, 1, shards), own_slots]
+        placed = [run_place(spots, arrived, placed, shape)]
     return placed[0]
 
 
@@ -570,7 +583,7 @@
 def local(grid_features, owners, adjacency, mesh_nodes, *parameters):
     sizes = [lax.axis_size(axis) for axis in ("shard", "head", "sub")]
     small = grid_features.shape[:2] == (4, BLOCK) and mesh_nodes.shape[0] == 2 * BLOCK
-    if sizes == [4, 2, 2] and small:
+    if sizes == [4, 2, 2] and small and grid_features.shape[2] == 512:
         return paired(grid_features, owners, adjacency, mesh_nodes, *parameters)
     return general(grid_features, owners, adjacency, mesh_nodes, *parameters)
 

time: 50.1 us -> 54.7 us (1.092)
  starting transfers between devices: 19.8 us -> 24.5 us
  waiting for transfers between devices: 13.5 us -> 9.97 us
  Pallas kernels: 16.4 us -> 18.5 us
  local copies, waits for them, and re-layouts: 0.11 us -> 1.34 us
    ppermute x10 -> x11, starting transfers between devices: 14.1 us -> 17.3 us  [crossed(): return lax.ppermute(x, 'shard', [(i, i ^ distance) for i in range(size)])]
    ppermute x6 -> x7, waiting for transfers between devices: 6.15 us -> 4.08 us  [swapped(): return lax.ppermute(x, axis, [(0, 1), (1, 0)])]
    pallas_call x4 -> x7, Pallas kernels: 2.86 us -> 4.63 us  [the longest x4 2.56 us: run_combine(): pl.pallas_call(functools.partial(combine_kernel, chunks, distances), out_...]
    ppermute x6 -> x7, starting transfers between devices: 5.61 us -> 7.17 us  [swapped(): return lax.ppermute(x, axis, [(0, 1), (1, 0)])]
    ppermute x10 -> x11, waiting for transfers between devices: 7.38 us -> 5.89 us  [crossed(): return lax.ppermute(x, 'shard', [(i, i ^ distance) for i in range(size)])]
    unnamed x7 -> x11, local copies, waits for them, and re-layouts: 0.11 us -> 1.34 us
  transfers between devices with their start and end apart: 16 -> 18, of which waited for: 7 -> 6; matrix products, arithmetic and copies ran while one was open for 0% -> 0% of each run, Pallas kernels for 27% -> 28%
where the time goes in v10:
time: 54.7 us; the launch traced here: 54.5 us
  starting transfers between devices  24.5 us (45%)
  Pallas kernels  18.5 us (34%)
  waiting for transfers between devices  9.97 us (18%)
  local copies, waits for them, and re-layouts  1.34 us (2%)
    ppermute x11, starting transfers between devices, crossed(): return lax.ppermute(x, 'shard', [(i, i ^ distance) for i in range(size)])  17.3 us
    ppermute x7, starting transfers between devices, swapped(): return lax.ppermute(x, axis, [(0, 1), (1, 0)])  7.17 us
    ppermute x11, waiting for transfers between devices, crossed(): return lax.ppermute(x, 'shard', [(i, i ^ distance) for i in range(size)])  5.89 us
    pallas_call x1, Pallas kernels, run_stage(): pl.pallas_call(functools.partial(stage_kernel, axes), out_shape=tuple((ja...  4.87 us
    ppermute x7, waiting for transfers between devices, swapped(): return lax.ppermute(x, axis, [(0, 1), (1, 0)])  4.08 us
    pallas_call x1, Pallas kernels, run_mlp(): pl.pallas_call(mlp_kernel, out_shape=(jax.ShapeDtypeStruct((rows, wq.shap...  3.33 us
    pallas_call x4, Pallas kernels, run_combine(): pl.pallas_call(functools.partial(combine_kernel, chunks, distances), out_...  2.56 us
    pallas_call x1, Pallas kernels, run_attend(): pl.pallas_call(attend_kernel, out_shape=(part, part, jax.ShapeDtypeStruct...  2.45 us
  transfers between devices with their start and end apart: 18, of which 6 were waited for; matrix products, arithmetic and copies ran while one was open for 0% of the time, Pallas kernels for 28%

profile of v10, /device:TPU:0, one launch (start us, length us, event | category | flops | bytes accessed | tf_op | source)
XLA Modules:
  0.0 54.5 jit_solution(4229583401129331217)
XLA Ops:
  0.0 2.9 %collective-permute-start = (bf16[256,512]{1,0:T(8,128)(2,1)}, bf16[256,512]{1,0:T(8,128)(2,1)S(1)}, u32[]{:S(2)}, u32[]{:S(2)}) collective-permute-start(bf16[256,512]{1,0:T(8,128)(2,1)} %bitcast.6), channel_id=1, source_target_pairs={{0,2},{2,0},{1,3},{3,1},{4,6},{6,4},{5,7},{7,5},{8,10},{10,8},{9,1... | collective-permute-start | bytes 786440 | tf_op jit(solution)/shard_map/ppermute | solution.py:397
  2.9 0.9 %pick.1 = bf16[64,1024]{1,0:T(8,128)(2,1)S(1)} custom-call(bf16[128,1024]{1,0:T(8,128)(2,1)} %mesh.1), custom_call_target="tpu_custom_call" | custom-call | bytes 524288 | tf_op jit(solution)/shard_map/pick/pallas_call | solution.py:108
  3.9 2.7 %collective-permute-start.1 = (bf16[64,1024]{1,0:T(8,128)(2,1)S(1)}, bf16[64,1024]{1,0:T(8,128)(2,1)S(1)}, u32[]{:S(2)}, u32[]{:S(2)}) collective-permute-start(bf16[64,1024]{1,0:T(8,128)(2,1)S(1)} %pick.1), channel_id=1, source_target_pairs={{0,8},{4,12},{8,0},{12,4},{1,9},{5,13},{9,1},{13,5},{2,10},{6,14},... | collective-permute-start | bytes 393224 | tf_op jit(solution)/shard_map/ppermute | solution.py:393
  6.5 1.6 %collective-permute-start.5 = (bf16[128,1024]{1,0:T(8,128)(2,1)}, bf16[128,1024]{1,0:T(8,128)(2,1)S(1)}, u32[]{:S(2)}, u32[]{:S(2)}) collective-permute-start(bf16[128,1024]{1,0:T(8,128)(2,1)} %mesh.1), channel_id=1, source_target_pairs={{0,4},{4,0},{8,12},{12,8},{1,5},{5,1},{9,13},{13,9},{2,6},{6,2},{1... | collective-permute-start | bytes 786440 | tf_op jit(solution)/shard_map/ppermute | solution.py:393
  8.1 4.9 %stage.1 = (bf16[256,512]{1,0:T(8,128)(2,1)S(1)}, f32[1,1024]{1,0:T(1,128)S(1)}, bf16[1024,512]{1,0:T(8,128)(2,1)S(1)}, bf16[1024,2048]{1,0:T(8,128)(2,1)S(1)}, ...) custom-call(bf16[256,512]{1,0:T(8,128)(2,1)} %bitcast.7, ...), custom_call_target="tpu_custom_call" | custom-call | bytes 262184960 | tf_op jit(solution)/shard_map/stage/pallas_call | solution.py:145
  13.0 0.0 collective-permute-done.1.refs_2_
  13.0 0.6 %collective-permute-start.2 = (bf16[64,1024]{1,0:T(8,128)(2,1)S(1)}, bf16[64,1024]{1,0:T(8,128)(2,1)S(1)}, u32[]{:S(2)}, u32[]{:S(2)}) collective-permute-start(bf16[64,1024]{1,0:T(8,128)(2,1)S(1)} %collective-permute-done.1.refs_2_), channel_id=1, source_target_pairs={{0,2},{2,0},{1,3},{3,1},{4,6},{6,4},{5,7},{7,5},{8,10},{10,8},{9,1... | collective-permute-start | bytes 393224 | tf_op jit(solution)/shard_map/ppermute | solution.py:397
  13.6 0.4 collective-permute-start.6
  14.0 0.0 collective-permute-done.other
  14.0 3.3 %mlp.1 = (bf16[256,512]{1,0:T(8,128)(2,1)S(1)}, f32[256,1024]{1,0:T(8,128)S(1)}) custom-call(bf16[256,512]{1,0:T(8,128)(2,1)S(1)} %get-tuple-element.37.own, bf16[256,512]{1,0:T(8,128)(2,1)S(1)} %collective-permute-done.other, f32[1,1024]{1,0:T(1,128)S(1)} %get-tuple-element.38.gain, bf16[1024,512]{1,0:T(8,128)(2,1)S(1)} %get-tuple-element.39.wq, ...), custom_call_target="tpu_custom_call" | custom-call | flops 2415919104 | bytes 9437184 | tf_op jit(solution)/shard_map/mlp/pallas_call | solution.py:81
  17.4 0.0 copy-start.1
  17.4 0.6 %collective-permute-done.2.refs_3_ = bf16[64,1024]{1,0:T(8,128)(2,1)S(1)} collective-permute-done((bf16[64,1024]{1,0:T(8,128)(2,1)S(1)}, bf16[64,1024]{1,0:T(8,128)(2,1)S(1)}, u32[]{:S(2)}, u32[]{:S(2)}) %collective-permute-start.2) | collective-permute-done | bytes 131104 | tf_op jit(solution)/shard_map/ppermute | solution.py:397
  18.0 1.0 %collective-permute-start.3 = (bf16[64,1024]{1,0:T(8,128)(2,1)S(1)}, bf16[64,1024]{1,0:T(8,128)(2,1)S(1)}, u32[]{:S(2)}, u32[]{:S(2)}) collective-permute-start(bf16[64,1024]{1,0:T(8,128)(2,1)S(1)} %collective-permute-done.2.refs_3_), channel_id=1, source_target_pairs={{0,4},{4,0},{8,12},{12,8},{1,5},{5,1},{9,13},{13,9},{2,6},{6,2},{1... | collective-permute-start | bytes 393224 | tf_op jit(solution)/shard_map/ppermute | solution.py:393
  19.0 0.0 collective-permute-done.6.refs_4_
  19.0 0.0 collective-permute-done.5.refs_1_
  19.0 1.1 %project.3 = bf16[448,1024]{1,0:T(8,128)(2,1)S(1)} custom-call(bf16[128,1024]{1,0:T(8,128)(2,1)S(1)} %get-tuple-element.48.refs_0_, bf16[128,1024]{1,0:T(8,128)(2,1)S(1)} %collective-permute-done.5.refs_1_, bf16[64,1024]{1,0:T(8,128)(2,1)S(1)} %collective-permute-done.1.refs_2_, bf16[64,1024]{1,0:T(8,128)(2,1)S(1)} %collective-permute-done.2.refs_3_, ...), custom_call_target="tpu_custom_call" | custom-call | flops 70464307200 | bytes 294912000 | tf_op jit(solution)/shard_map/project/pallas_call | solution.py:168
  20.2 0.0 copy-done.1
  20.2 0.0 copy-start.4
  20.2 0.0 copy-start.3
  20.2 0.1 collective-permute-start.7
  20.3 2.7 %collective-permute-done.3.refs_0_ = bf16[64,1024]{1,0:T(8,128)(2,1)S(1)} collective-permute-done((bf16[64,1024]{1,0:T(8,128)(2,1)S(1)}, bf16[64,1024]{1,0:T(8,128)(2,1)S(1)}, u32[]{:S(2)}, u32[]{:S(2)}) %collective-permute-start.3) | collective-permute-done | bytes 131104 | tf_op jit(solution)/shard_map/ppermute | solution.py:393
  23.0 0.5 project.2
  23.5 0.1 collective-permute-start.4
  23.5 0.0 copy-done.4
  23.6 0.1 copy.17.owners
  23.6 0.0 collective-permute-done.7
  23.6 0.1 table.1.table_in
  23.8 1.1 %collective-permute-done.4 = bf16[64,1024]{1,0:T(8,128)(2,1)S(1)} collective-permute-done((bf16[64,1024]{1,0:T(8,128)(2,1)S(1)}, bf16[64,1024]{1,0:T(8,128)(2,1)S(1)}, u32[]{:S(2)}, u32[]{:S(2)}) %collective-permute-start.4) | collective-permute-done | bytes 131104 | tf_op jit(solution)/shard_map/ppermute | solution.py:397
  24.9 0.0 copy-done.3
  24.9 0.0 copy-start.2
  24.9 1.2 %copy-done.2 = f32[256,1024]{1,0:T(8,128)S(1)} copy-done((f32[256,1024]{1,0:T(8,128)S(1)}, f32[256,1024]{1,0:T(8,128)}, u32[]{:S(2)}) %copy-start.2) | copy-done | bytes 1048600
  26.1 2.5 %attend.1 = (bf16[256,128]{1,0:T(8,128)(2,1)S(1)}, bf16[256,128]{1,0:T(8,128)(2,1)S(1)}, bf16[256,512]{1,0:T(8,128)(2,1)S(1)}, bf16[2,8,64,1024]{3,2,1,0:T(8,128)(2,1)S(1)}) custom-call(s32[4,8]{1,0:T(4,128)S(1)} %copy-done.3, bf16[256,512]{1,0:T(8,128)(2,1)S(1)} %get-tuple-element.44.q, ...), custom_call_target="tpu_custom_call", output_to_operand_aliasing={{3}: (4, {})} | custom-call | flops 13421772800 | bytes 41943040 | tf_op jit(solution)/shard_map/attend/pallas_call | solution.py:276
  28.6 1.0 %collective-permute-start.10 = (bf16[256,128]{1,0:T(8,128)(2,1)S(1)}, bf16[256,128]{1,0:T(8,128)(2,1)S(1)}, u32[]{:S(2)}, u32[]{:S(2)}) collective-permute-start(bf16[256,128]{1,0:T(8,128)(2,1)S(1)} %get-tuple-element.57), channel_id=1, source_target_pairs={{0,2},{2,0},{1,3},{3,1},{4,6},{6,4},{5,7},{7,5},{8,10},{10,8},{9,1... | collective-permute-start | bytes 196616 | tf_op jit(solution)/shard_map/ppermute | solution.py:397
  29.6 0.0 copy-start
  29.6 0.3 project_out.3
  29.9 1.1 %collective-permute-start.9 = (bf16[256,128]{1,0:T(8,128)(2,1)S(1)}, bf16[256,128]{1,0:T(8,128)(2,1)S(1)}, u32[]{:S(2)}, u32[]{:S(2)}) collective-permute-start(bf16[256,128]{1,0:T(8,128)(2,1)S(1)} %get-tuple-element.55), channel_id=1, source_target_pairs={{0,2},{2,0},{1,3},{3,1},{4,6},{6,4},{5,7},{7,5},{8,10},{10,8},{9,1... | collective-permute-start | bytes 196616 | tf_op jit(solution)/shard_map/ppermute | solution.py:397
  31.0 2.3 %collective-permute-done.10.refs_1_.refs_3_ = bf16[256,128]{1,0:T(8,128)(2,1)S(1)} collective-permute-done((bf16[256,128]{1,0:T(8,128)(2,1)S(1)}, bf16[256,128]{1,0:T(8,128)(2,1)S(1)}, u32[]{:S(2)}, u32[]{:S(2)}) %collective-permute-start.10) | collective-permute-done | bytes 65568 | tf_op jit(solution)/shard_map/ppermute | solution.py:397
  33.4 0.0 copy-done
  33.4 0.6 %combine.4 = (bf16[2,64,128]{2,1,0:T(8,128)(2,1)S(1)}, bf16[2,64,128]{2,1,0:T(8,128)(2,1)S(1)}) custom-call(s32[4,1]{1,0:T(4,128)S(1)} %copy.17.owners, bf16[4,64,512]{2,1,0:T(8,128)(2,1)S(1)} %copy-done, bf16[256,128]{1,0:T(8,128)(2,1)S(1)} %get-tuple-element.56.refs_0_, bf16[256,128]{1,0:T(8,128)(2,1)S(1)} %collective-permute-done.10.refs_1_.refs_3_), custom_call_target="tpu_custom_call" | custom-call | flops 98304000 | bytes 52428800 | tf_op jit(solution)/shard_map/combine/pallas_call | solution.py:348
  34.0 2.3 %collective-permute-start.16 = (bf16[2,64,128]{2,1,0:T(8,128)(2,1)S(1)}, bf16[2,64,128]{2,1,0:T(8,128)(2,1)S(1)}, u32[]{:S(2)}, u32[]{:S(2)}) collective-permute-start(bf16[2,64,128]{2,1,0:T(8,128)(2,1)S(1)} %get-tuple-element.58), channel_id=1, source_target_pairs={{0,8},{4,12},{8,0},{12,4},{1,9},{5,13},{9,1},{13,5},{2,10},{6,14},... | collective-permute-start | bytes 98312 | tf_op jit(solution)/shard_map/ppermute | solution.py:393
  36.3 1.5 %collective-permute-start.17 = (bf16[2,64,128]{2,1,0:T(8,128)(2,1)S(1)}, bf16[2,64,128]{2,1,0:T(8,128)(2,1)S(1)}, u32[]{:S(2)}, u32[]{:S(2)}) collective-permute-start(bf16[2,64,128]{2,1,0:T(8,128)(2,1)S(1)} %get-tuple-element.68), channel_id=1, source_target_pairs={{0,12},{4,8},{8,4},{12,0},{1,13},{5,9},{9,5},{13,1},{2,14},{6,10},... | collective-permute-start | bytes 98312 | tf_op jit(solution)/shard_map/ppermute | solution.py:393
  37.8 0.3 project_out.2
  38.1 1.3 %collective-permute-start.8 = (bf16[256,256]{1,0:T(8,128)(2,1)S(1)}, bf16[256,256]{1,0:T(8,128)(2,1)S(1)}, u32[]{:S(2)}, u32[]{:S(2)}) collective-permute-start(bf16[256,256]{1,0:T(8,128)(2,1)S(1)} %get-tuple-element.53), channel_id=1, source_target_pairs={{0,2},{2,0},{1,3},{3,1},{4,6},{6,4},{5,7},{7,5},{8,10},{10,8},{9,1... | collective-permute-start | bytes 393224 | tf_op jit(solution)/shard_map/ppermute | solution.py:397
  39.4 0.0 collective-permute-done.9.refs_1_.refs_4_
  39.4 0.6 %combine.5 = (bf16[2,64,128]{2,1,0:T(8,128)(2,1)S(1)}, bf16[2,64,128]{2,1,0:T(8,128)(2,1)S(1)}) custom-call(s32[4,1]{1,0:T(4,128)S(1)} %copy.17.owners, bf16[4,64,512]{2,1,0:T(8,128)(2,1)S(1)} %copy-done, bf16[256,128]{1,0:T(8,128)(2,1)S(1)} %get-tuple-element.54.refs_0_.refs_1_, bf16[256,128]{1,0:T(8,128)(2,1)S(1)} %collective-permute-done.9.refs_1_.refs_4_), custom_call_target="tpu_custom_call" | custom-call | flops 98304000 | bytes 52428800 | tf_op jit(solution)/shard_map/combine/pallas_call | solution.py:348
  40.1 0.8 %collective-permute-start.14 = (bf16[2,64,128]{2,1,0:T(8,128)(2,1)S(1)}, bf16[2,64,128]{2,1,0:T(8,128)(2,1)S(1)}, u32[]{:S(2)}, u32[]{:S(2)}) collective-permute-start(bf16[2,64,128]{2,1,0:T(8,128)(2,1)S(1)} %get-tuple-element.60), channel_id=1, source_target_pairs={{0,8},{4,12},{8,0},{12,4},{1,9},{5,13},{9,1},{13,5},{2,10},{6,14},... | collective-permute-start | bytes 98312 | tf_op jit(solution)/shard_map/ppermute | solution.py:393
  40.8 2.5 %collective-permute-start.15 = (bf16[2,64,128]{2,1,0:T(8,128)(2,1)S(1)}, bf16[2,64,128]{2,1,0:T(8,128)(2,1)S(1)}, u32[]{:S(2)}, u32[]{:S(2)}) collective-permute-start(bf16[2,64,128]{2,1,0:T(8,128)(2,1)S(1)} %get-tuple-element.67), channel_id=1, source_target_pairs={{0,12},{4,8},{8,4},{12,0},{1,13},{5,9},{9,5},{13,1},{2,14},{6,10},... | collective-permute-start | bytes 98312 | tf_op jit(solution)/shard_map/ppermute | solution.py:393
  43.4 0.0 collective-permute-done.16.refs_0_
  43.4 0.0 collective-permute-done.17.refs_1_
  43.4 0.6 %place.3.refs_2_ = bf16[8,64,512]{2,1,0:T(8,128)(2,1)} custom-call(bf16[2,64,128]{2,1,0:T(8,128)(2,1)S(1)} %collective-permute-done.16.refs_0_, bf16[2,64,128]{2,1,0:T(8,128)(2,1)S(1)} %collective-permute-done.17.refs_1_), custom_call_target="tpu_custom_call" | custom-call | flops 13107200000 | tf_op jit(solution)/shard_map/place/pallas_call | solution.py:377
  44.0 0.0 collective-permute-done.8.refs_1_.refs_5_
  44.0 0.6 %combine.6 = (bf16[2,64,256]{2,1,0:T(8,128)(2,1)S(1)}, bf16[2,64,256]{2,1,0:T(8,128)(2,1)S(1)}) custom-call(s32[4,1]{1,0:T(4,128)S(1)} %copy.17.owners, bf16[4,64,512]{2,1,0:T(8,128)(2,1)S(1)} %copy-done, bf16[256,256]{1,0:T(8,128)(2,1)S(1)} %get-tuple-element.52.refs_0_.refs_2_, bf16[256,256]{1,0:T(8,128)(2,1)S(1)} %collective-permute-done.8.refs_1_.refs_5_), custom_call_target="tpu_custom_call" | custom-call | flops 196608000 | bytes 104857600 | tf_op jit(solution)/shard_map/combine/pallas_call | solution.py:348
  44.7 2.0 %collective-permute-start.11 = (bf16[2,64,256]{2,1,0:T(8,128)(2,1)S(1)}, bf16[2,64,256]{2,1,0:T(8,128)(2,1)S(1)}, u32[]{:S(2)}, u32[]{:S(2)}) collective-permute-start(bf16[2,64,256]{2,1,0:T(8,128)(2,1)S(1)} %get-tuple-element.62), channel_id=1, source_target_pairs={{0,8},{4,12},{8,0},{12,4},{1,9},{5,13},{9,1},{13,5},{2,10},{6,14},... | collective-permute-start | bytes 196616 | tf_op jit(solution)/shard_map/ppermute | solution.py:393
  46.7 0.7 %combine.7 = (bf16[2,64,512]{2,1,0:T(8,128)(2,1)S(1)}, bf16[2,64,512]{2,1,0:T(8,128)(2,1)S(1)}) custom-call(s32[4,1]{1,0:T(4,128)S(1)} %copy.17.owners, bf16[4,64,512]{2,1,0:T(8,128)(2,1)S(1)} %copy-done, bf16[256,128]{1,0:T(8,128)(2,1)S(1)} %get-tuple-element.56.refs_0_, bf16[256,128]{1,0:T(8,128)(2,1)S(1)} %get-tuple-element.54.refs_0_.refs_1_, ...), custom_call_target="tpu_custom_call" | custom-call | flops 393216000 | bytes 209715200 | tf_op jit(solution)/shard_map/combine/pallas_call | solution.py:348
  47.3 0.2 collective-permute-start.13
  47.5 2.3 %collective-permute-start.12 = (bf16[2,64,256]{2,1,0:T(8,128)(2,1)S(1)}, bf16[2,64,256]{2,1,0:T(8,128)(2,1)S(1)}, u32[]{:S(2)}, u32[]{:S(2)}) collective-permute-start(bf16[2,64,256]{2,1,0:T(8,128)(2,1)S(1)} %get-tuple-element.63), channel_id=1, source_target_pairs={{0,12},{4,8},{8,4},{12,0},{1,13},{5,9},{9,5},{13,1},{2,14},{6,10},... | collective-permute-start | bytes 196616 | tf_op jit(solution)/shard_map/ppermute | solution.py:393
  49.9 0.0 collective-permute-done.14.refs_0_
  49.9 0.0 collective-permute-done.15.refs_1_
  49.9 0.6 %place.4.refs_4_ = bf16[8,64,512]{2,1,0:T(8,128)(2,1)} custom-call(bf16[2,64,128]{2,1,0:T(8,128)(2,1)S(1)} %collective-permute-done.14.refs_0_, bf16[2,64,128]{2,1,0:T(8,128)(2,1)S(1)} %collective-permute-done.15.refs_1_, bf16[8,64,512]{2,1,0:T(8,128)(2,1)} %place.3.refs_2_), custom_call_target="tpu_custom_call", output_to_operand_aliasing={{}: (2, {})} | custom-call | flops 13107200000 | tf_op jit(solution)/shard_map/place/pallas_call | solution.py:377
  50.5 0.5 collective-permute-done.11.refs_0_
  51.0 2.7 %collective-permute-done.12.refs_1_ = bf16[2,64,256]{2,1,0:T(8,128)(2,1)S(1)} collective-permute-done((bf16[2,64,256]{2,1,0:T(8,128)(2,1)S(1)}, bf16[2,64,256]{2,1,0:T(8,128)(2,1)S(1)}, u32[]{:S(2)}, u32[]{:S(2)}) %collective-permute-start.12) | collective-permute-done | bytes 65568 | tf_op jit(solution)/shard_map/ppermute | solution.py:393
  53.7 0.0 collective-permute-done.13.refs_2_
  53.7 0.8 %place.5 = bf16[8,64,512]{2,1,0:T(8,128)(2,1)} custom-call(bf16[2,64,256]{2,1,0:T(8,128)(2,1)S(1)} %collective-permute-done.11.refs_0_, bf16[2,64,256]{2,1,0:T(8,128)(2,1)S(1)} %collective-permute-done.12.refs_1_, bf16[2,64,512]{2,1,0:T(8,128)(2,1)S(1)} %collective-permute-done.13.refs_2_, ...), custom_call_target="tpu_custom_call", output_to_operand_aliasing={{}: (4, {})} | custom-call | flops 78643200000 | tf_op jit(solution)/shard_map/place/pallas_call | solution.py:377
Async XLA Ops:
  0.0 14.0 %collective-permute-start = (bf16[256,512]{1,0:T(8,128)(2,1)}, bf16[256,512]{1,0:T(8,128)(2,1)S(1)}, u32[]{:S(2)}, u32[]{:S(2)}) collective-permute-start(bf16[256,512]{1,0:T(8,128)(2,1)} %bitcast.6), channel_id=1, source_target_pairs={{0,2},{2,0},{1,3},{3,1},{4,6},{6,4},{5,7},{7,5},{8,10},{10,8},{9,1... | collective-permute-start | bytes 786440 | tf_op jit(solution)/shard_map/ppermute | solution.py:397
  3.9 9.1 %collective-permute-start.1 = (bf16[64,1024]{1,0:T(8,128)(2,1)S(1)}, bf16[64,1024]{1,0:T(8,128)(2,1)S(1)}, u32[]{:S(2)}, u32[]{:S(2)}) collective-permute-start(bf16[64,1024]{1,0:T(8,128)(2,1)S(1)} %pick.1), channel_id=1, source_target_pairs={{0,8},{4,12},{8,0},{12,4},{1,9},{5,13},{9,1},{13,5},{2,10},{6,14},... | collective-permute-start | bytes 393224 | tf_op jit(solution)/shard_map/ppermute | solution.py:393
  6.5 12.5 %collective-permute-start.5 = (bf16[128,1024]{1,0:T(8,128)(2,1)}, bf16[128,1024]{1,0:T(8,128)(2,1)S(1)}, u32[]{:S(2)}, u32[]{:S(2)}) collective-permute-start(bf16[128,1024]{1,0:T(8,128)(2,1)} %mesh.1), channel_id=1, source_target_pairs={{0,4},{4,0},{8,12},{12,8},{1,5},{5,1},{9,13},{13,9},{2,6},{6,2},{1... | collective-permute-start | bytes 786440 | tf_op jit(solution)/shard_map/ppermute | solution.py:393
  13.0 5.0 %collective-permute-start.2 = (bf16[64,1024]{1,0:T(8,128)(2,1)S(1)}, bf16[64,1024]{1,0:T(8,128)(2,1)S(1)}, u32[]{:S(2)}, u32[]{:S(2)}) collective-permute-start(bf16[64,1024]{1,0:T(8,128)(2,1)S(1)} %collective-permute-done.1.refs_2_), channel_id=1, source_target_pairs={{0,2},{2,0},{1,3},{3,1},{4,6},{6,4},{5,7},{7,5},{8,10},{10,8},{9,1... | collective-permute-start | bytes 393224 | tf_op jit(solution)/shard_map/ppermute | solution.py:397
  13.6 5.5 %collective-permute-start.6 = (bf16[64,1024]{1,0:T(8,128)(2,1)S(1)}, bf16[64,1024]{1,0:T(8,128)(2,1)S(1)}, u32[]{:S(2)}, u32[]{:S(2)}) collective-permute-start(bf16[64,1024]{1,0:T(8,128)(2,1)S(1)} %collective-permute-done.1.refs_2_), channel_id=1, source_target_pairs={{0,4},{4,0},{8,12},{12,8},{1,5},{5,1},{9,13},{13,9},{2,6},{6,2},{1... | collective-permute-start | bytes 393224 | tf_op jit(solution)/shard_map/ppermute | solution.py:393
  17.4 2.8 %copy-start.1 = (f32[256,1024]{1,0:T(8,128)}, f32[256,1024]{1,0:T(8,128)S(1)}, u32[]{:S(2)}) copy-start(f32[256,1024]{1,0:T(8,128)S(1)} %get-tuple-element.49.mlp) | copy-start | bytes 3145732
  18.0 5.0 %collective-permute-start.3 = (bf16[64,1024]{1,0:T(8,128)(2,1)S(1)}, bf16[64,1024]{1,0:T(8,128)(2,1)S(1)}, u32[]{:S(2)}, u32[]{:S(2)}) collective-permute-start(bf16[64,1024]{1,0:T(8,128)(2,1)S(1)} %collective-permute-done.2.refs_3_), channel_id=1, source_target_pairs={{0,4},{4,0},{8,12},{12,8},{1,5},{5,1},{9,13},{13,9},{2,6},{6,2},{1... | collective-permute-start | bytes 393224 | tf_op jit(solution)/shard_map/ppermute | solution.py:393
  20.2 3.4 %copy-start.4 = (s32[4,1]{0,1:T(1,128)S(1)}, s32[4,1]{0,1:T(1,128)}, u32[]{:S(2)}) copy-start(s32[4,1]{0,1:T(1,128)} %param.12) | copy-start | bytes 52
  20.2 4.7 %copy-start.3 = (s32[4,8]{1,0:T(4,128)S(1)}, s32[4,8]{1,0:T(4,128)}, u32[]{:S(2)}) copy-start(s32[4,8]{1,0:T(4,128)} %adjacency.1) | copy-start | bytes 388
  20.2 3.4 %collective-permute-start.7 = (bf16[448,1024]{1,0:T(8,128)(2,1)S(1)}, bf16[448,1024]{1,0:T(8,128)(2,1)S(1)}, u32[]{:S(2)}, u32[]{:S(2)}) collective-permute-start(bf16[448,1024]{1,0:T(8,128)(2,1)S(1)} %project.3), channel_id=1, source_target_pairs={{0,1},{1,0},{2,3},{3,2},{4,5},{5,4},{6,7},{7,6},{8,9},{9,8},{10,11... | collective-permute-start | bytes 2752520 | tf_op jit(solution)/shard_map/ppermute | solution.py:397
  23.5 1.4 %collective-permute-start.4 = (bf16[64,1024]{1,0:T(8,128)(2,1)S(1)}, bf16[64,1024]{1,0:T(8,128)(2,1)S(1)}, u32[]{:S(2)}, u32[]{:S(2)}) collective-permute-start(bf16[64,1024]{1,0:T(8,128)(2,1)S(1)} %project.2), channel_id=1, source_target_pairs={{0,1},{1,0},{2,3},{3,2},{4,5},{5,4},{6,7},{7,6},{8,9},{9,8},{10,11... | collective-permute-start | bytes 393224 | tf_op jit(solution)/shard_map/ppermute | solution.py:397
  24.9 1.2 %copy-start.2 = (f32[256,1024]{1,0:T(8,128)S(1)}, f32[256,1024]{1,0:T(8,128)}, u32[]{:S(2)}) copy-start(f32[256,1024]{1,0:T(8,128)} %copy-done.1) | copy-start | bytes 3145732
  28.6 4.8 %collective-permute-start.10 = (bf16[256,128]{1,0:T(8,128)(2,1)S(1)}, bf16[256,128]{1,0:T(8,128)(2,1)S(1)}, u32[]{:S(2)}, u32[]{:S(2)}) collective-permute-start(bf16[256,128]{1,0:T(8,128)(2,1)S(1)} %get-tuple-element.57), channel_id=1, source_target_pairs={{0,2},{2,0},{1,3},{3,1},{4,6},{6,4},{5,7},{7,5},{8,10},{10,8},{9,1... | collective-permute-start | bytes 196616 | tf_op jit(solution)/shard_map/ppermute | solution.py:397
  29.6 3.8 %copy-start = (bf16[4,64,512]{2,1,0:T(8,128)(2,1)S(1)}, bf16[4,64,512]{2,1,0:T(8,128)(2,1)}, u32[]{:S(2)}) copy-start(bf16[4,64,512]{2,1,0:T(8,128)(2,1)} %grid_features.7) | copy-start | bytes 786436
  29.9 9.5 %collective-permute-start.9 = (bf16[256,128]{1,0:T(8,128)(2,1)S(1)}, bf16[256,128]{1,0:T(8,128)(2,1)S(1)}, u32[]{:S(2)}, u32[]{:S(2)}) collective-permute-start(bf16[256,128]{1,0:T(8,128)(2,1)S(1)} %get-tuple-element.55), channel_id=1, source_target_pairs={{0,2},{2,0},{1,3},{3,1},{4,6},{6,4},{5,7},{7,5},{8,10},{10,8},{9,1... | collective-permute-start | bytes 196616 | tf_op jit(solution)/shard_map/ppermute | solution.py:397
  34.0 9.3 %collective-permute-start.16 = (bf16[2,64,128]{2,1,0:T(8,128)(2,1)S(1)}, bf16[2,64,128]{2,1,0:T(8,128)(2,1)S(1)}, u32[]{:S(2)}, u32[]{:S(2)}) collective-permute-start(bf16[2,64,128]{2,1,0:T(8,128)(2,1)S(1)} %get-tuple-element.58), channel_id=1, source_target_pairs={{0,8},{4,12},{8,0},{12,4},{1,9},{5,13},{9,1},{13,5},{2,10},{6,14},... | collective-permute-start | bytes 98312 | tf_op jit(solution)/shard_map/ppermute | solution.py:393
  36.3 7.1 %collective-permute-start.17 = (bf16[2,64,128]{2,1,0:T(8,128)(2,1)S(1)}, bf16[2,64,128]{2,1,0:T(8,128)(2,1)S(1)}, u32[]{:S(2)}, u32[]{:S(2)}) collective-permute-start(bf16[2,64,128]{2,1,0:T(8,128)(2,1)S(1)} %get-tuple-element.68), channel_id=1, source_target_pairs={{0,12},{4,8},{8,4},{12,0},{1,13},{5,9},{9,5},{13,1},{2,14},{6,10},... | collective-permute-start | bytes 98312 | tf_op jit(solution)/shard_map/ppermute | solution.py:393
  38.1 5.9 %collective-permute-start.8 = (bf16[256,256]{1,0:T(8,128)(2,1)S(1)}, bf16[256,256]{1,0:T(8,128)(2,1)S(1)}, u32[]{:S(2)}, u32[]{:S(2)}) collective-permute-start(bf16[256,256]{1,0:T(8,128)(2,1)S(1)} %get-tuple-element.53), channel_id=1, source_target_pairs={{0,2},{2,0},{1,3},{3,1},{4,6},{6,4},{5,7},{7,5},{8,10},{10,8},{9,1... | collective-permute-start | bytes 393224 | tf_op jit(solution)/shard_map/ppermute | solution.py:397
  40.1 9.8 %collective-permute-start.14 = (bf16[2,64,128]{2,1,0:T(8,128)(2,1)S(1)}, bf16[2,64,128]{2,1,0:T(8,128)(2,1)S(1)}, u32[]{:S(2)}, u32[]{:S(2)}) collective-permute-start(bf16[2,64,128]{2,1,0:T(8,128)(2,1)S(1)} %get-tuple-element.60), channel_id=1, source_target_pairs={{0,8},{4,12},{8,0},{12,4},{1,9},{5,13},{9,1},{13,5},{2,10},{6,14},... | collective-permute-start | bytes 98312 | tf_op jit(solution)/shard_map/ppermute | solution.py:393
  40.8 9.1 %collective-permute-start.15 = (bf16[2,64,128]{2,1,0:T(8,128)(2,1)S(1)}, bf16[2,64,128]{2,1,0:T(8,128)(2,1)S(1)}, u32[]{:S(2)}, u32[]{:S(2)}) collective-permute-start(bf16[2,64,128]{2,1,0:T(8,128)(2,1)S(1)} %get-tuple-element.67), channel_id=1, source_target_pairs={{0,12},{4,8},{8,4},{12,0},{1,13},{5,9},{9,5},{13,1},{2,14},{6,10},... | collective-permute-start | bytes 98312 | tf_op jit(solution)/shard_map/ppermute | solution.py:393
  44.7 6.3 %collective-permute-start.11 = (bf16[2,64,256]{2,1,0:T(8,128)(2,1)S(1)}, bf16[2,64,256]{2,1,0:T(8,128)(2,1)S(1)}, u32[]{:S(2)}, u32[]{:S(2)}) collective-permute-start(bf16[2,64,256]{2,1,0:T(8,128)(2,1)S(1)} %get-tuple-element.62), channel_id=1, source_target_pairs={{0,8},{4,12},{8,0},{12,4},{1,9},{5,13},{9,1},{13,5},{2,10},{6,14},... | collective-permute-start | bytes 196616 | tf_op jit(solution)/shard_map/ppermute | solution.py:393
  47.3 6.4 %collective-permute-start.13 = (bf16[2,64,512]{2,1,0:T(8,128)(2,1)S(1)}, bf16[2,64,512]{2,1,0:T(8,128)(2,1)S(1)}, u32[]{:S(2)}, u32[]{:S(2)}) collective-permute-start(bf16[2,64,512]{2,1,0:T(8,128)(2,1)S(1)} %get-tuple-element.65), channel_id=1, source_target_pairs={{0,4},{4,0},{8,12},{12,8},{1,5},{5,1},{9,13},{13,9},{2,6},{6,2},{1... | collective-permute-start | bytes 393224 | tf_op jit(solution)/shard_map/ppermute | solution.py:393
  47.5 6.2 %collective-permute-start.12 = (bf16[2,64,256]{2,1,0:T(8,128)(2,1)S(1)}, bf16[2,64,256]{2,1,0:T(8,128)(2,1)S(1)}, u32[]{:S(2)}, u32[]{:S(2)}) collective-permute-start(bf16[2,64,256]{2,1,0:T(8,128)(2,1)S(1)} %get-tuple-element.63), channel_id=1, source_target_pairs={{0,12},{4,8},{8,4},{12,0},{1,13},{5,9},{9,5},{13,1},{2,14},{6,10},... | collective-permute-start | bytes 196616 | tf_op jit(solution)/shard_map/ppermute | solution.py:393

commit v11 on v10

--- a/solution.py
+++ b/solution.py
@@ -14,7 +14,7 @@
 BLOCK = 64
 QUAD = 4
 WIDE = QUAD * HEAD_DIM
-WIDTHS = (128, 128, 256)
+WIDTHS = (128, 384)
 MIB = 1 << 20
 
 
@@ -352,7 +352,7 @@
         out_specs=tuple(vmem(len(distances))),
         compiler_params=params(8),
         cost_estimate=pl.CostEstimate(
-            flops=3000 * count * rows * width,
+            flops=300000 * count * rows * width,
             bytes_accessed=400 * rows * width * (3 * count + CAP * len(distances)),
             transcendentals=0,
         ),

time: 54.7 us -> 50.2 us (0.918)
  starting transfers between devices: 24.5 us -> 20.1 us
  waiting for transfers between devices: 9.97 us -> 11.4 us
  Pallas kernels: 18.5 us -> 17.1 us
    ppermute x11 -> x9, starting transfers between devices: 17.3 us -> 14.2 us  [crossed(): return lax.ppermute(x, 'shard', [(i, i ^ distance) for i in range(size)])]
    ppermute x11 -> x9, waiting for transfers between devices: 5.89 us -> 7.58 us  [crossed(): return lax.ppermute(x, 'shard', [(i, i ^ distance) for i in range(size)])]
    ppermute x7 -> x6, starting transfers between devices: 7.17 us -> 5.84 us  [swapped(): return lax.ppermute(x, axis, [(0, 1), (1, 0)])]
    pallas_call x3 -> x2, Pallas kernels: 2.06 us -> 1.44 us  [run_place(): pl.pallas_call(functools.partial(place_kernel, spots), out_shape=jax.Shap...]
    pallas_call x4 -> x3, Pallas kernels: 2.56 us -> 1.95 us  [run_combine(): pl.pallas_call(functools.partial(combine_kernel, chunks, distances), out_...]
    ppermute x7 -> x6, waiting for transfers between devices: 4.08 us -> 3.84 us  [swapped(): return lax.ppermute(x, axis, [(0, 1), (1, 0)])]
  transfers between devices with their start and end apart: 18 -> 15, of which waited for: 6 -> 7; matrix products, arithmetic and copies ran while one was open for 0% -> 0% of each run, Pallas kernels for 28% -> 28%
where the time goes in v11:
time: 50.2 us; the launch traced here: 50.1 us
  starting transfers between devices  20.1 us (40%)
  Pallas kernels  17.1 us (34%)
  waiting for transfers between devices  11.4 us (23%)
  local copies, waits for them, and re-layouts  1.34 us (3%)
    ppermute x9, starting transfers between devices, crossed(): return lax.ppermute(x, 'shard', [(i, i ^ distance) for i in range(size)])  14.2 us
    ppermute x9, waiting for transfers between devices, crossed(): return lax.ppermute(x, 'shard', [(i, i ^ distance) for i in range(size)])  7.58 us
    ppermute x6, starting transfers between devices, swapped(): return lax.ppermute(x, axis, [(0, 1), (1, 0)])  5.84 us
    pallas_call x1, Pallas kernels, run_stage(): pl.pallas_call(functools.partial(stage_kernel, axes), out_shape=tuple((ja...  4.87 us
    ppermute x6, waiting for transfers between devices, swapped(): return lax.ppermute(x, axis, [(0, 1), (1, 0)])  3.84 us
    pallas_call x1, Pallas kernels, run_mlp(): pl.pallas_call(mlp_kernel, out_shape=(jax.ShapeDtypeStruct((rows, wq.shap...  3.33 us
    pallas_call x1, Pallas kernels, run_attend(): pl.pallas_call(attend_kernel, out_shape=(part, part, jax.ShapeDtypeStruct...  2.45 us
    pallas_call x3, Pallas kernels, run_combine(): pl.pallas_call(functools.partial(combine_kernel, chunks, distances), out_...  1.95 us
  transfers between devices with their start and end apart: 15, of which 7 were waited for; matrix products, arithmetic and copies ran while one was open for 0% of the time, Pallas kernels for 28%

profile of v11, /device:TPU:0, one launch (start us, length us, event | category | flops | bytes accessed | tf_op | source)
XLA Modules:
  0.0 50.1 jit_solution(3518404716810381184)
XLA Ops:
  0.0 2.9 %collective-permute-start = (bf16[256,512]{1,0:T(8,128)(2,1)}, bf16[256,512]{1,0:T(8,128)(2,1)S(1)}, u32[]{:S(2)}, u32[]{:S(2)}) collective-permute-start(bf16[256,512]{1,0:T(8,128)(2,1)} %bitcast.8), channel_id=1, source_target_pairs={{0,2},{2,0},{1,3},{3,1},{4,6},{6,4},{5,7},{7,5},{8,10},{10,8},{9,1... | collective-permute-start | bytes 786440 | tf_op jit(solution)/shard_map/ppermute | solution.py:397
  2.9 0.9 %pick.1 = bf16[64,1024]{1,0:T(8,128)(2,1)S(1)} custom-call(bf16[128,1024]{1,0:T(8,128)(2,1)} %mesh.1), custom_call_target="tpu_custom_call" | custom-call | bytes 524288 | tf_op jit(solution)/shard_map/pick/pallas_call | solution.py:108
  3.9 2.7 %collective-permute-start.1 = (bf16[64,1024]{1,0:T(8,128)(2,1)S(1)}, bf16[64,1024]{1,0:T(8,128)(2,1)S(1)}, u32[]{:S(2)}, u32[]{:S(2)}) collective-permute-start(bf16[64,1024]{1,0:T(8,128)(2,1)S(1)} %pick.1), channel_id=1, source_target_pairs={{0,8},{4,12},{8,0},{12,4},{1,9},{5,13},{9,1},{13,5},{2,10},{6,14},... | collective-permute-start | bytes 393224 | tf_op jit(solution)/shard_map/ppermute | solution.py:393
  6.5 1.6 %collective-permute-start.5 = (bf16[128,1024]{1,0:T(8,128)(2,1)}, bf16[128,1024]{1,0:T(8,128)(2,1)S(1)}, u32[]{:S(2)}, u32[]{:S(2)}) collective-permute-start(bf16[128,1024]{1,0:T(8,128)(2,1)} %mesh.1), channel_id=1, source_target_pairs={{0,4},{4,0},{8,12},{12,8},{1,5},{5,1},{9,13},{13,9},{2,6},{6,2},{1... | collective-permute-start | bytes 786440 | tf_op jit(solution)/shard_map/ppermute | solution.py:393
  8.1 4.9 %stage.1 = (bf16[256,512]{1,0:T(8,128)(2,1)S(1)}, f32[1,1024]{1,0:T(1,128)S(1)}, bf16[1024,512]{1,0:T(8,128)(2,1)S(1)}, bf16[1024,2048]{1,0:T(8,128)(2,1)S(1)}, ...) custom-call(bf16[256,512]{1,0:T(8,128)(2,1)} %bitcast.9, ...), custom_call_target="tpu_custom_call" | custom-call | bytes 262184960 | tf_op jit(solution)/shard_map/stage/pallas_call | solution.py:145
  13.0 0.0 collective-permute-done.1.refs_2_
  13.0 0.6 %collective-permute-start.2 = (bf16[64,1024]{1,0:T(8,128)(2,1)S(1)}, bf16[64,1024]{1,0:T(8,128)(2,1)S(1)}, u32[]{:S(2)}, u32[]{:S(2)}) collective-permute-start(bf16[64,1024]{1,0:T(8,128)(2,1)S(1)} %collective-permute-done.1.refs_2_), channel_id=1, source_target_pairs={{0,2},{2,0},{1,3},{3,1},{4,6},{6,4},{5,7},{7,5},{8,10},{10,8},{9,1... | collective-permute-start | bytes 393224 | tf_op jit(solution)/shard_map/ppermute | solution.py:397
  13.6 0.4 collective-permute-start.6
  14.0 0.0 collective-permute-done.other
  14.0 3.3 %mlp.1 = (bf16[256,512]{1,0:T(8,128)(2,1)S(1)}, f32[256,1024]{1,0:T(8,128)S(1)}) custom-call(bf16[256,512]{1,0:T(8,128)(2,1)S(1)} %get-tuple-element.32.own, bf16[256,512]{1,0:T(8,128)(2,1)S(1)} %collective-permute-done.other, f32[1,1024]{1,0:T(1,128)S(1)} %get-tuple-element.33.gain, bf16[1024,512]{1,0:T(8,128)(2,1)S(1)} %get-tuple-element.34.wq, ...), custom_call_target="tpu_custom_call" | custom-call | flops 2415919104 | bytes 9437184 | tf_op jit(solution)/shard_map/mlp/pallas_call | solution.py:81
  17.4 0.0 copy-start.1
  17.4 0.6 %collective-permute-done.2.refs_3_ = bf16[64,1024]{1,0:T(8,128)(2,1)S(1)} collective-permute-done((bf16[64,1024]{1,0:T(8,128)(2,1)S(1)}, bf16[64,1024]{1,0:T(8,128)(2,1)S(1)}, u32[]{:S(2)}, u32[]{:S(2)}) %collective-permute-start.2) | collective-permute-done | bytes 131104 | tf_op jit(solution)/shard_map/ppermute | solution.py:397
  18.0 1.0 %collective-permute-start.3 = (bf16[64,1024]{1,0:T(8,128)(2,1)S(1)}, bf16[64,1024]{1,0:T(8,128)(2,1)S(1)}, u32[]{:S(2)}, u32[]{:S(2)}) collective-permute-start(bf16[64,1024]{1,0:T(8,128)(2,1)S(1)} %collective-permute-done.2.refs_3_), channel_id=1, source_target_pairs={{0,4},{4,0},{8,12},{12,8},{1,5},{5,1},{9,13},{13,9},{2,6},{6,2},{1... | collective-permute-start | bytes 393224 | tf_op jit(solution)/shard_map/ppermute | solution.py:393
  19.0 0.0 collective-permute-done.6.refs_4_
  19.0 0.0 collective-permute-done.5.refs_1_
  19.0 1.1 %project.3 = bf16[448,1024]{1,0:T(8,128)(2,1)S(1)} custom-call(bf16[128,1024]{1,0:T(8,128)(2,1)S(1)} %get-tuple-element.43.refs_0_, bf16[128,1024]{1,0:T(8,128)(2,1)S(1)} %collective-permute-done.5.refs_1_, bf16[64,1024]{1,0:T(8,128)(2,1)S(1)} %collective-permute-done.1.refs_2_, bf16[64,1024]{1,0:T(8,128)(2,1)S(1)} %collective-permute-done.2.refs_3_, ...), custom_call_target="tpu_custom_call" | custom-call | flops 70464307200 | bytes 294912000 | tf_op jit(solution)/shard_map/project/pallas_call | solution.py:168
  20.2 0.0 copy-done.1
  20.2 0.0 copy-start.4
  20.2 0.0 copy-start.3
  20.2 0.1 collective-permute-start.7
  20.3 2.7 %collective-permute-done.3.refs_0_ = bf16[64,1024]{1,0:T(8,128)(2,1)S(1)} collective-permute-done((bf16[64,1024]{1,0:T(8,128)(2,1)S(1)}, bf16[64,1024]{1,0:T(8,128)(2,1)S(1)}, u32[]{:S(2)}, u32[]{:S(2)}) %collective-permute-start.3) | collective-permute-done | bytes 131104 | tf_op jit(solution)/shard_map/ppermute | solution.py:393
  23.0 0.5 project.2
  23.5 0.1 collective-permute-start.4
  23.5 0.0 copy-done.4
  23.6 0.1 copy.15.owners
  23.6 0.0 collective-permute-done.7
  23.6 0.1 table.1.table_in
  23.8 1.1 %collective-permute-done.4 = bf16[64,1024]{1,0:T(8,128)(2,1)S(1)} collective-permute-done((bf16[64,1024]{1,0:T(8,128)(2,1)S(1)}, bf16[64,1024]{1,0:T(8,128)(2,1)S(1)}, u32[]{:S(2)}, u32[]{:S(2)}) %collective-permute-start.4) | collective-permute-done | bytes 131104 | tf_op jit(solution)/shard_map/ppermute | solution.py:397
  24.9 0.0 copy-done.3
  24.9 0.0 copy-start.2
  24.9 1.2 %copy-done.2 = f32[256,1024]{1,0:T(8,128)S(1)} copy-done((f32[256,1024]{1,0:T(8,128)S(1)}, f32[256,1024]{1,0:T(8,128)}, u32[]{:S(2)}) %copy-start.2) | copy-done | bytes 1048600
  26.1 2.5 %attend.1 = (bf16[256,128]{1,0:T(8,128)(2,1)S(1)}, bf16[256,128]{1,0:T(8,128)(2,1)S(1)}, bf16[256,512]{1,0:T(8,128)(2,1)S(1)}, bf16[2,8,64,1024]{3,2,1,0:T(8,128)(2,1)S(1)}) custom-call(s32[4,8]{1,0:T(4,128)S(1)} %copy-done.3, bf16[256,512]{1,0:T(8,128)(2,1)S(1)} %get-tuple-element.39.q, ...), custom_call_target="tpu_custom_call", output_to_operand_aliasing={{3}: (4, {})} | custom-call | flops 13421772800 | bytes 41943040 | tf_op jit(solution)/shard_map/attend/pallas_call | solution.py:276
  28.6 1.0 %collective-permute-start.9 = (bf16[256,128]{1,0:T(8,128)(2,1)S(1)}, bf16[256,128]{1,0:T(8,128)(2,1)S(1)}, u32[]{:S(2)}, u32[]{:S(2)}) collective-permute-start(bf16[256,128]{1,0:T(8,128)(2,1)S(1)} %get-tuple-element.50), channel_id=1, source_target_pairs={{0,2},{2,0},{1,3},{3,1},{4,6},{6,4},{5,7},{7,5},{8,10},{10,8},{9,1... | collective-permute-start | bytes 196616 | tf_op jit(solution)/shard_map/ppermute | solution.py:397
  29.6 0.0 copy-start
  29.6 0.4 project_out.1
  30.0 1.1 %collective-permute-start.8 = (bf16[256,384]{1,0:T(8,128)(2,1)S(1)}, bf16[256,384]{1,0:T(8,128)(2,1)S(1)}, u32[]{:S(2)}, u32[]{:S(2)}) collective-permute-start(bf16[256,384]{1,0:T(8,128)(2,1)S(1)} %get-tuple-element.48), channel_id=1, source_target_pairs={{0,2},{2,0},{1,3},{3,1},{4,6},{6,4},{5,7},{7,5},{8,10},{10,8},{9,1... | collective-permute-start | bytes 589832 | tf_op jit(solution)/shard_map/ppermute | solution.py:397
  31.2 2.1 %collective-permute-done.9.refs_1_.refs_2_ = bf16[256,128]{1,0:T(8,128)(2,1)S(1)} collective-permute-done((bf16[256,128]{1,0:T(8,128)(2,1)S(1)}, bf16[256,128]{1,0:T(8,128)(2,1)S(1)}, u32[]{:S(2)}, u32[]{:S(2)}) %collective-permute-start.9) | collective-permute-done | bytes 65568 | tf_op jit(solution)/shard_map/ppermute | solution.py:397
  33.3 0.0 copy-done
  33.3 0.6 %combine.3 = (bf16[2,64,128]{2,1,0:T(8,128)(2,1)S(1)}, bf16[2,64,128]{2,1,0:T(8,128)(2,1)S(1)}) custom-call(s32[4,1]{1,0:T(4,128)S(1)} %copy.15.owners, bf16[4,64,512]{2,1,0:T(8,128)(2,1)S(1)} %copy-done, bf16[256,128]{1,0:T(8,128)(2,1)S(1)} %get-tuple-element.49.refs_0_, bf16[256,128]{1,0:T(8,128)(2,1)S(1)} %collective-permute-done.9.refs_1_.refs_2_), custom_call_target="tpu_custom_call" | custom-call | flops 9830400000 | bytes 52428800 | tf_op jit(solution)/shard_map/combine/pallas_call | solution.py:348
  33.9 2.4 %collective-permute-start.13 = (bf16[2,64,128]{2,1,0:T(8,128)(2,1)S(1)}, bf16[2,64,128]{2,1,0:T(8,128)(2,1)S(1)}, u32[]{:S(2)}, u32[]{:S(2)}) collective-permute-start(bf16[2,64,128]{2,1,0:T(8,128)(2,1)S(1)} %get-tuple-element.51), channel_id=1, source_target_pairs={{0,8},{4,12},{8,0},{12,4},{1,9},{5,13},{9,1},{13,5},{2,10},{6,14},... | collective-permute-start | bytes 98312 | tf_op jit(solution)/shard_map/ppermute | solution.py:393
  36.3 1.6 %collective-permute-start.14 = (bf16[2,64,128]{2,1,0:T(8,128)(2,1)S(1)}, bf16[2,64,128]{2,1,0:T(8,128)(2,1)S(1)}, u32[]{:S(2)}, u32[]{:S(2)}) collective-permute-start(bf16[2,64,128]{2,1,0:T(8,128)(2,1)S(1)} %get-tuple-element.58), channel_id=1, source_target_pairs={{0,12},{4,8},{8,4},{12,0},{1,13},{5,9},{9,5},{13,1},{2,14},{6,10},... | collective-permute-start | bytes 98312 | tf_op jit(solution)/shard_map/ppermute | solution.py:393
  37.9 0.0 collective-permute-done.8.refs_1_.refs_3_
  37.9 0.7 %combine.4 = (bf16[2,64,384]{2,1,0:T(8,128)(2,1)S(1)}, bf16[2,64,384]{2,1,0:T(8,128)(2,1)S(1)}) custom-call(s32[4,1]{1,0:T(4,128)S(1)} %copy.15.owners, bf16[4,64,512]{2,1,0:T(8,128)(2,1)S(1)} %copy-done, bf16[256,384]{1,0:T(8,128)(2,1)S(1)} %get-tuple-element.47.refs_0_.refs_1_, bf16[256,384]{1,0:T(8,128)(2,1)S(1)} %collective-permute-done.8.refs_1_.refs_3_), custom_call_target="tpu_custom_call" | custom-call | flops 29491200000 | bytes 157286400 | tf_op jit(solution)/shard_map/combine/pallas_call | solution.py:348
  38.6 2.1 %collective-permute-start.10 = (bf16[2,64,384]{2,1,0:T(8,128)(2,1)S(1)}, bf16[2,64,384]{2,1,0:T(8,128)(2,1)S(1)}, u32[]{:S(2)}, u32[]{:S(2)}) collective-permute-start(bf16[2,64,384]{2,1,0:T(8,128)(2,1)S(1)} %get-tuple-element.53), channel_id=1, source_target_pairs={{0,8},{4,12},{8,0},{12,4},{1,9},{5,13},{9,1},{13,5},{2,10},{6,14},... | collective-permute-start | bytes 294920 | tf_op jit(solution)/shard_map/ppermute | solution.py:393
  40.7 0.7 %combine.5 = (bf16[2,64,512]{2,1,0:T(8,128)(2,1)S(1)}, bf16[2,64,512]{2,1,0:T(8,128)(2,1)S(1)}) custom-call(s32[4,1]{1,0:T(4,128)S(1)} %copy.15.owners, bf16[4,64,512]{2,1,0:T(8,128)(2,1)S(1)} %copy-done, bf16[256,128]{1,0:T(8,128)(2,1)S(1)} %get-tuple-element.49.refs_0_, bf16[256,384]{1,0:T(8,128)(2,1)S(1)} %get-tuple-element.47.refs_0_.refs_1_, ...), custom_call_target="tpu_custom_call" | custom-call | flops 39321600000 | bytes 209715200 | tf_op jit(solution)/shard_map/combine/pallas_call | solution.py:348
  41.4 1.2 %collective-permute-start.12 = (bf16[2,64,512]{2,1,0:T(8,128)(2,1)S(1)}, bf16[2,64,512]{2,1,0:T(8,128)(2,1)S(1)}, u32[]{:S(2)}, u32[]{:S(2)}) collective-permute-start(bf16[2,64,512]{2,1,0:T(8,128)(2,1)S(1)} %get-tuple-element.56), channel_id=1, source_target_pairs={{0,4},{4,0},{8,12},{12,8},{1,5},{5,1},{9,13},{13,9},{2,6},{6,2},{1... | collective-permute-start | bytes 393224 | tf_op jit(solution)/shard_map/ppermute | solution.py:393
  42.6 1.2 %collective-permute-start.11 = (bf16[2,64,384]{2,1,0:T(8,128)(2,1)S(1)}, bf16[2,64,384]{2,1,0:T(8,128)(2,1)S(1)}, u32[]{:S(2)}, u32[]{:S(2)}) collective-permute-start(bf16[2,64,384]{2,1,0:T(8,128)(2,1)S(1)} %get-tuple-element.54), channel_id=1, source_target_pairs={{0,12},{4,8},{8,4},{12,0},{1,13},{5,9},{9,5},{13,1},{2,14},{6,10},... | collective-permute-start | bytes 294920 | tf_op jit(solution)/shard_map/ppermute | solution.py:393
  43.8 0.0 collective-permute-done.13.refs_0_
  43.8 0.0 collective-permute-done.14.refs_1_
  43.8 0.6 %place.2.refs_4_ = bf16[8,64,512]{2,1,0:T(8,128)(2,1)} custom-call(bf16[2,64,128]{2,1,0:T(8,128)(2,1)S(1)} %collective-permute-done.13.refs_0_, bf16[2,64,128]{2,1,0:T(8,128)(2,1)S(1)} %collective-permute-done.14.refs_1_), custom_call_target="tpu_custom_call" | custom-call | flops 13107200000 | tf_op jit(solution)/shard_map/place/pallas_call | solution.py:377
  44.4 3.1 %collective-permute-done.10.refs_0_ = bf16[2,64,384]{2,1,0:T(8,128)(2,1)S(1)} collective-permute-done((bf16[2,64,384]{2,1,0:T(8,128)(2,1)S(1)}, bf16[2,64,384]{2,1,0:T(8,128)(2,1)S(1)}, u32[]{:S(2)}, u32[]{:S(2)}) %collective-permute-start.10) | collective-permute-done | bytes 98336 | tf_op jit(solution)/shard_map/ppermute | solution.py:393
  47.5 1.6 %collective-permute-done.11.refs_1_ = bf16[2,64,384]{2,1,0:T(8,128)(2,1)S(1)} collective-permute-done((bf16[2,64,384]{2,1,0:T(8,128)(2,1)S(1)}, bf16[2,64,384]{2,1,0:T(8,128)(2,1)S(1)}, u32[]{:S(2)}, u32[]{:S(2)}) %collective-permute-start.11) | collective-permute-done | bytes 98336 | tf_op jit(solution)/shard_map/ppermute | solution.py:393
  49.1 0.2 collective-permute-done.12.refs_2_
  49.3 0.8 %place.3 = bf16[8,64,512]{2,1,0:T(8,128)(2,1)} custom-call(bf16[2,64,384]{2,1,0:T(8,128)(2,1)S(1)} %collective-permute-done.10.refs_0_, bf16[2,64,384]{2,1,0:T(8,128)(2,1)S(1)} %collective-permute-done.11.refs_1_, bf16[2,64,512]{2,1,0:T(8,128)(2,1)S(1)} %collective-permute-done.12.refs_2_, ...), custom_call_target="tpu_custom_call", output_to_operand_aliasing={{}: (4, {})} | custom-call | flops 91750400000 | tf_op jit(solution)/shard_map/place/pallas_call | solution.py:377
Async XLA Ops:
  0.0 14.0 %collective-permute-start = (bf16[256,512]{1,0:T(8,128)(2,1)}, bf16[256,512]{1,0:T(8,128)(2,1)S(1)}, u32[]{:S(2)}, u32[]{:S(2)}) collective-permute-start(bf16[256,512]{1,0:T(8,128)(2,1)} %bitcast.8), channel_id=1, source_target_pairs={{0,2},{2,0},{1,3},{3,1},{4,6},{6,4},{5,7},{7,5},{8,10},{10,8},{9,1... | collective-permute-start | bytes 786440 | tf_op jit(solution)/shard_map/ppermute | solution.py:397
  3.9 9.1 %collective-permute-start.1 = (bf16[64,1024]{1,0:T(8,128)(2,1)S(1)}, bf16[64,1024]{1,0:T(8,128)(2,1)S(1)}, u32[]{:S(2)}, u32[]{:S(2)}) collective-permute-start(bf16[64,1024]{1,0:T(8,128)(2,1)S(1)} %pick.1), channel_id=1, source_target_pairs={{0,8},{4,12},{8,0},{12,4},{1,9},{5,13},{9,1},{13,5},{2,10},{6,14},... | collective-permute-start | bytes 393224 | tf_op jit(solution)/shard_map/ppermute | solution.py:393
  6.5 12.5 %collective-permute-start.5 = (bf16[128,1024]{1,0:T(8,128)(2,1)}, bf16[128,1024]{1,0:T(8,128)(2,1)S(1)}, u32[]{:S(2)}, u32[]{:S(2)}) collective-permute-start(bf16[128,1024]{1,0:T(8,128)(2,1)} %mesh.1), channel_id=1, source_target_pairs={{0,4},{4,0},{8,12},{12,8},{1,5},{5,1},{9,13},{13,9},{2,6},{6,2},{1... | collective-permute-start | bytes 786440 | tf_op jit(solution)/shard_map/ppermute | solution.py:393
  13.0 5.0 %collective-permute-start.2 = (bf16[64,1024]{1,0:T(8,128)(2,1)S(1)}, bf16[64,1024]{1,0:T(8,128)(2,1)S(1)}, u32[]{:S(2)}, u32[]{:S(2)}) collective-permute-start(bf16[64,1024]{1,0:T(8,128)(2,1)S(1)} %collective-permute-done.1.refs_2_), channel_id=1, source_target_pairs={{0,2},{2,0},{1,3},{3,1},{4,6},{6,4},{5,7},{7,5},{8,10},{10,8},{9,1... | collective-permute-start | bytes 393224 | tf_op jit(solution)/shard_map/ppermute | solution.py:397
  13.6 5.5 %collective-permute-start.6 = (bf16[64,1024]{1,0:T(8,128)(2,1)S(1)}, bf16[64,1024]{1,0:T(8,128)(2,1)S(1)}, u32[]{:S(2)}, u32[]{:S(2)}) collective-permute-start(bf16[64,1024]{1,0:T(8,128)(2,1)S(1)} %collective-permute-done.1.refs_2_), channel_id=1, source_target_pairs={{0,4},{4,0},{8,12},{12,8},{1,5},{5,1},{9,13},{13,9},{2,6},{6,2},{1... | collective-permute-start | bytes 393224 | tf_op jit(solution)/shard_map/ppermute | solution.py:393
  17.4 2.8 %copy-start.1 = (f32[256,1024]{1,0:T(8,128)}, f32[256,1024]{1,0:T(8,128)S(1)}, u32[]{:S(2)}) copy-start(f32[256,1024]{1,0:T(8,128)S(1)} %get-tuple-element.44.mlp) | copy-start | bytes 3145732
  18.0 5.0 %collective-permute-start.3 = (bf16[64,1024]{1,0:T(8,128)(2,1)S(1)}, bf16[64,1024]{1,0:T(8,128)(2,1)S(1)}, u32[]{:S(2)}, u32[]{:S(2)}) collective-permute-start(bf16[64,1024]{1,0:T(8,128)(2,1)S(1)} %collective-permute-done.2.refs_3_), channel_id=1, source_target_pairs={{0,4},{4,0},{8,12},{12,8},{1,5},{5,1},{9,13},{13,9},{2,6},{6,2},{1... | collective-permute-start | bytes 393224 | tf_op jit(solution)/shard_map/ppermute | solution.py:393
  20.2 3.4 %copy-start.4 = (s32[4,1]{0,1:T(1,128)S(1)}, s32[4,1]{0,1:T(1,128)}, u32[]{:S(2)}) copy-start(s32[4,1]{0,1:T(1,128)} %param.12) | copy-start | bytes 52
  20.2 4.7 %copy-start.3 = (s32[4,8]{1,0:T(4,128)S(1)}, s32[4,8]{1,0:T(4,128)}, u32[]{:S(2)}) copy-start(s32[4,8]{1,0:T(4,128)} %adjacency.1) | copy-start | bytes 388
  20.2 3.4 %collective-permute-start.7 = (bf16[448,1024]{1,0:T(8,128)(2,1)S(1)}, bf16[448,1024]{1,0:T(8,128)(2,1)S(1)}, u32[]{:S(2)}, u32[]{:S(2)}) collective-permute-start(bf16[448,1024]{1,0:T(8,128)(2,1)S(1)} %project.3), channel_id=1, source_target_pairs={{0,1},{1,0},{2,3},{3,2},{4,5},{5,4},{6,7},{7,6},{8,9},{9,8},{10,11... | collective-permute-start | bytes 2752520 | tf_op jit(solution)/shard_map/ppermute | solution.py:397
  23.5 1.4 %collective-permute-start.4 = (bf16[64,1024]{1,0:T(8,128)(2,1)S(1)}, bf16[64,1024]{1,0:T(8,128)(2,1)S(1)}, u32[]{:S(2)}, u32[]{:S(2)}) collective-permute-start(bf16[64,1024]{1,0:T(8,128)(2,1)S(1)} %project.2), channel_id=1, source_target_pairs={{0,1},{1,0},{2,3},{3,2},{4,5},{5,4},{6,7},{7,6},{8,9},{9,8},{10,11... | collective-permute-start | bytes 393224 | tf_op jit(solution)/shard_map/ppermute | solution.py:397
  24.9 1.2 %copy-start.2 = (f32[256,1024]{1,0:T(8,128)S(1)}, f32[256,1024]{1,0:T(8,128)}, u32[]{:S(2)}) copy-start(f32[256,1024]{1,0:T(8,128)} %copy-done.1) | copy-start | bytes 3145732
  28.6 4.7 %collective-permute-start.9 = (bf16[256,128]{1,0:T(8,128)(2,1)S(1)}, bf16[256,128]{1,0:T(8,128)(2,1)S(1)}, u32[]{:S(2)}, u32[]{:S(2)}) collective-permute-start(bf16[256,128]{1,0:T(8,128)(2,1)S(1)} %get-tuple-element.50), channel_id=1, source_target_pairs={{0,2},{2,0},{1,3},{3,1},{4,6},{6,4},{5,7},{7,5},{8,10},{10,8},{9,1... | collective-permute-start | bytes 196616 | tf_op jit(solution)/shard_map/ppermute | solution.py:397
  29.6 3.7 %copy-start = (bf16[4,64,512]{2,1,0:T(8,128)(2,1)S(1)}, bf16[4,64,512]{2,1,0:T(8,128)(2,1)}, u32[]{:S(2)}) copy-start(bf16[4,64,512]{2,1,0:T(8,128)(2,1)} %grid_features.5) | copy-start | bytes 786436
  30.0 7.9 %collective-permute-start.8 = (bf16[256,384]{1,0:T(8,128)(2,1)S(1)}, bf16[256,384]{1,0:T(8,128)(2,1)S(1)}, u32[]{:S(2)}, u32[]{:S(2)}) collective-permute-start(bf16[256,384]{1,0:T(8,128)(2,1)S(1)} %get-tuple-element.48), channel_id=1, source_target_pairs={{0,2},{2,0},{1,3},{3,1},{4,6},{6,4},{5,7},{7,5},{8,10},{10,8},{9,1... | collective-permute-start | bytes 589832 | tf_op jit(solution)/shard_map/ppermute | solution.py:397
  33.9 9.9 %collective-permute-start.13 = (bf16[2,64,128]{2,1,0:T(8,128)(2,1)S(1)}, bf16[2,64,128]{2,1,0:T(8,128)(2,1)S(1)}, u32[]{:S(2)}, u32[]{:S(2)}) collective-permute-start(bf16[2,64,128]{2,1,0:T(8,128)(2,1)S(1)} %get-tuple-element.51), channel_id=1, source_target_pairs={{0,8},{4,12},{8,0},{12,4},{1,9},{5,13},{9,1},{13,5},{2,10},{6,14},... | collective-permute-start | bytes 98312 | tf_op jit(solution)/shard_map/ppermute | solution.py:393
  36.3 7.5 %collective-permute-start.14 = (bf16[2,64,128]{2,1,0:T(8,128)(2,1)S(1)}, bf16[2,64,128]{2,1,0:T(8,128)(2,1)S(1)}, u32[]{:S(2)}, u32[]{:S(2)}) collective-permute-start(bf16[2,64,128]{2,1,0:T(8,128)(2,1)S(1)} %get-tuple-element.58), channel_id=1, source_target_pairs={{0,12},{4,8},{8,4},{12,0},{1,13},{5,9},{9,5},{13,1},{2,14},{6,10},... | collective-permute-start | bytes 98312 | tf_op jit(solution)/shard_map/ppermute | solution.py:393
  38.6 8.9 %collective-permute-start.10 = (bf16[2,64,384]{2,1,0:T(8,128)(2,1)S(1)}, bf16[2,64,384]{2,1,0:T(8,128)(2,1)S(1)}, u32[]{:S(2)}, u32[]{:S(2)}) collective-permute-start(bf16[2,64,384]{2,1,0:T(8,128)(2,1)S(1)} %get-tuple-element.53), channel_id=1, source_target_pairs={{0,8},{4,12},{8,0},{12,4},{1,9},{5,13},{9,1},{13,5},{2,10},{6,14},... | collective-permute-start | bytes 294920 | tf_op jit(solution)/shard_map/ppermute | solution.py:393
  41.4 7.9 %collective-permute-start.12 = (bf16[2,64,512]{2,1,0:T(8,128)(2,1)S(1)}, bf16[2,64,512]{2,1,0:T(8,128)(2,1)S(1)}, u32[]{:S(2)}, u32[]{:S(2)}) collective-permute-start(bf16[2,64,512]{2,1,0:T(8,128)(2,1)S(1)} %get-tuple-element.56), channel_id=1, source_target_pairs={{0,4},{4,0},{8,12},{12,8},{1,5},{5,1},{9,13},{13,9},{2,6},{6,2},{1... | collective-permute-start | bytes 393224 | tf_op jit(solution)/shard_map/ppermute | solution.py:393
  42.6 6.5 %collective-permute-start.11 = (bf16[2,64,384]{2,1,0:T(8,128)(2,1)S(1)}, bf16[2,64,384]{2,1,0:T(8,128)(2,1)S(1)}, u32[]{:S(2)}, u32[]{:S(2)}) collective-permute-start(bf16[2,64,384]{2,1,0:T(8,128)(2,1)S(1)} %get-tuple-element.54), channel_id=1, source_target_pairs={{0,12},{4,8},{8,4},{12,0},{1,13},{5,9},{9,5},{13,1},{2,14},{6,10},... | collective-permute-start | bytes 294920 | tf_op jit(solution)/shard_map/ppermute | solution.py:393

commit v12 on v11

--- a/solution.py
+++ b/solution.py
@@ -125,6 +125,10 @@
         if axis is None:
             copies.append(pltpu.make_async_copy(source, target, sem.at[len(copies)]))
             continue
+        if axis == "rest":
+            span = pl.ds(pl.multiple_of((1 - h) * BLOCK, BLOCK), BLOCK)
+            copies.append(pltpu.make_async_copy(source.at[span, :], target, sem.at[len(copies)]))
+            continue
         half = source.shape[axis] // 2
         for part, head in enumerate((1 - h, h)):
             span = pl.ds(pl.multiple_of(head * half, half), half)
@@ -144,7 +148,10 @@
     size = sum(2 * array.size for array in arrays)
     return pl.pallas_call(
         functools.partial(stage_kernel, axes),
-        out_shape=tuple(jax.ShapeDtypeStruct(array.shape, array.dtype) for array in arrays),
+        out_shape=tuple(
+            jax.ShapeDtypeStruct((BLOCK,) + array.shape[1:] if axis == "rest" else array.shape, array.dtype)
+            for array, axis in zip(arrays, axes)
+        ),
         in_specs=[whole(pltpu.HBM)] * len(arrays),
         out_specs=tuple(vmem(len(arrays))),
         scratch_shapes=[pltpu.SemaphoreType.DMA((2 * len(arrays),))],
@@ -352,7 +359,7 @@
         out_specs=tuple(vmem(len(distances))),
         compiler_params=params(8),
         cost_estimate=pl.CostEstimate(
-            flops=300000 * count * rows * width,
+            flops=60000 * count * rows * width,
             bytes_accessed=400 * rows * width * (3 * count + CAP * len(distances)),
             transcendentals=0,
         ),
@@ -427,20 +434,22 @@
             key_weight,
             value_weight,
             mesh_nodes,
-        ),
-        (None, 1, 0, 0, 1, 1, None, None, None),
-    )
-    flat, gain, wq, wup, wdn, wo, wk, wv, mesh = staged
+            mesh_nodes,
+        ),
+        (None, 1, 0, 0, 1, 1, None, None, None, "rest"),
+    )
+    flat, gain, wq, wup, wdn, wo, wk, wv, mesh, rest = staged
+    straight = crossed(rest, 3, shards)
+    far, _ = lax.optimization_barrier((far, rest))
     farther = crossed(far, 1, shards)
     far_pair = swapped(far, "head")
     queries, mlp = run_mlp(flat, other, gain, wq, wup, wdn)
-    queries, mlp, relayed = lax.optimization_barrier((queries, mlp, far_pair))
-    farther_pair = crossed(relayed, 1, shards)
+    queries, mlp, far_pair, near = lax.optimization_barrier((queries, mlp, far_pair, near))
     blocked = (-1, BLOCK, 2 * half)
-    mine_a = run_project((mesh, near, far, far_pair, farther), wk, wv)
+    mine_a = run_project((mesh, near, far, far_pair), wk, wv)
     sibling_a = swapped(mine_a, "sub")
     table = run_table(mine_a.reshape(blocked), sibling_a.reshape(blocked), 2 * shards)
-    mine_b = run_project((farther_pair,), wk, wv)
+    mine_b = run_project((farther, straight), wk, wv)
     sibling_b = swapped(mine_b, "sub")
     send, keep, att = run_attend(
         adjacency, queries, mine_b.reshape(blocked), sibling_b.reshape(blocked), table, mlp, wo

time: 50.2 us -> 47.1 us (0.938)
  local copies, waits for them, and re-layouts: 1.34 us -> 0.11 us
  starting transfers between devices: 20.1 us -> 19.1 us
  waiting for transfers between devices: 11.4 us -> 10.7 us
    unnamed x11 -> x7, local copies, waits for them, and re-layouts: 1.34 us -> 0.11 us
    ppermute x9, waiting for transfers between devices: 7.58 us -> 6.55 us  [crossed(): return lax.ppermute(x, 'shard', [(i, i ^ distance) for i in range(size)])]
    ppermute x9, starting transfers between devices: 14.2 us -> 13.5 us  [crossed(): return lax.ppermute(x, 'shard', [(i, i ^ distance) for i in range(size)])]
  transfers between devices with their start and end apart: 15 -> 15, of which waited for: 7 -> 7; matrix products, arithmetic and copies ran while one was open for 0% -> 0% of each run, Pallas kernels for 28% -> 29%
where the time goes in v12:
time: 47.1 us; the launch traced here: 47 us
  starting transfers between devices  19.1 us (41%)
  Pallas kernels  17 us (36%)
  waiting for transfers between devices  10.7 us (23%)
    ppermute x9, starting transfers between devices, crossed(): return lax.ppermute(x, 'shard', [(i, i ^ distance) for i in range(size)])  13.5 us
    ppermute x9, waiting for transfers between devices, crossed(): return lax.ppermute(x, 'shard', [(i, i ^ distance) for i in range(size)])  6.55 us
    ppermute x6, starting transfers between devices, swapped(): return lax.ppermute(x, axis, [(0, 1), (1, 0)])  5.64 us
    pallas_call x1, Pallas kernels, run_stage(): pl.pallas_call(functools.partial(stage_kernel, axes), out_shape=tuple((ja...  4.92 us
    ppermute x6, waiting for transfers between devices, swapped(): return lax.ppermute(x, axis, [(0, 1), (1, 0)])  4.16 us
    pallas_call x1, Pallas kernels, run_mlp(): pl.pallas_call(mlp_kernel, out_shape=(jax.ShapeDtypeStruct((rows, wq.shap...  3.33 us
    pallas_call x1, Pallas kernels, run_attend(): pl.pallas_call(attend_kernel, out_shape=(part, part, jax.ShapeDtypeStruct...  2.46 us
    pallas_call x3, Pallas kernels, run_combine(): pl.pallas_call(functools.partial(combine_kernel, chunks, distances), out_...  1.95 us
  transfers between devices with their start and end apart: 15, of which 7 were waited for; matrix products, arithmetic and copies ran while one was open for 0% of the time, Pallas kernels for 29%

profile of v12, /device:TPU:0, one launch (start us, length us, event | category | flops | bytes accessed | tf_op | source)
XLA Modules:
  0.0 47.0 jit_solution(5573146394694256942)
XLA Ops:
  0.0 2.9 %collective-permute-start = (bf16[256,512]{1,0:T(8,128)(2,1)}, bf16[256,512]{1,0:T(8,128)(2,1)S(1)}, u32[]{:S(2)}, u32[]{:S(2)}) collective-permute-start(bf16[256,512]{1,0:T(8,128)(2,1)} %bitcast.8), channel_id=1, source_target_pairs={{0,2},{2,0},{1,3},{3,1},{4,6},{6,4},{5,7},{7,5},{8,10},{10,8},{9,1... | collective-permute-start | bytes 786440 | tf_op jit(solution)/shard_map/ppermute | solution.py:404
  2.9 0.9 %pick.1 = bf16[64,1024]{1,0:T(8,128)(2,1)S(1)} custom-call(bf16[128,1024]{1,0:T(8,128)(2,1)} %mesh.1), custom_call_target="tpu_custom_call" | custom-call | bytes 524288 | tf_op jit(solution)/shard_map/pick/pallas_call | solution.py:108
  3.9 2.7 %collective-permute-start.1 = (bf16[64,1024]{1,0:T(8,128)(2,1)S(1)}, bf16[64,1024]{1,0:T(8,128)(2,1)S(1)}, u32[]{:S(2)}, u32[]{:S(2)}) collective-permute-start(bf16[64,1024]{1,0:T(8,128)(2,1)S(1)} %pick.1), channel_id=1, source_target_pairs={{0,8},{4,12},{8,0},{12,4},{1,9},{5,13},{9,1},{13,5},{2,10},{6,14},... | collective-permute-start | bytes 393224 | tf_op jit(solution)/shard_map/ppermute | solution.py:400
  6.5 1.6 %collective-permute-start.3 = (bf16[128,1024]{1,0:T(8,128)(2,1)}, bf16[128,1024]{1,0:T(8,128)(2,1)S(1)}, u32[]{:S(2)}, u32[]{:S(2)}) collective-permute-start(bf16[128,1024]{1,0:T(8,128)(2,1)} %mesh.1), channel_id=1, source_target_pairs={{0,4},{4,0},{8,12},{12,8},{1,5},{5,1},{9,13},{13,9},{2,6},{6,2},{1... | collective-permute-start | bytes 786440 | tf_op jit(solution)/shard_map/ppermute | solution.py:400
  8.1 4.9 %stage.1 = (bf16[256,512]{1,0:T(8,128)(2,1)S(1)}, f32[1,1024]{1,0:T(1,128)S(1)}, bf16[1024,512]{1,0:T(8,128)(2,1)S(1)}, bf16[1024,2048]{1,0:T(8,128)(2,1)S(1)}, ...) custom-call(bf16[256,512]{1,0:T(8,128)(2,1)} %bitcast.9, ...), custom_call_target="tpu_custom_call" | custom-call | bytes 267427840 | tf_op jit(solution)/shard_map/stage/pallas_call | solution.py:149
  13.0 0.3 collective-permute-start.5
  13.3 0.0 collective-permute-done.1.refs_2_
  13.3 0.4 collective-permute-start.2
  13.7 0.8 %collective-permute-start.4 = (bf16[64,1024]{1,0:T(8,128)(2,1)S(1)}, bf16[64,1024]{1,0:T(8,128)(2,1)S(1)}, u32[]{:S(2)}, u32[]{:S(2)}) collective-permute-start(bf16[64,1024]{1,0:T(8,128)(2,1)S(1)} %collective-permute-done.1.refs_2_), channel_id=1, source_target_pairs={{0,4},{4,0},{8,12},{12,8},{1,5},{5,1},{9,13},{13,9},{2,6},{6,2},{1... | collective-permute-start | bytes 393224 | tf_op jit(solution)/shard_map/ppermute | solution.py:400
  14.5 0.0 collective-permute-done.other
  14.5 3.3 %mlp.1 = (bf16[256,512]{1,0:T(8,128)(2,1)S(1)}, f32[256,1024]{1,0:T(8,128)S(1)}) custom-call(bf16[256,512]{1,0:T(8,128)(2,1)S(1)} %get-tuple-element.35.own, bf16[256,512]{1,0:T(8,128)(2,1)S(1)} %collective-permute-done.other, f32[1,1024]{1,0:T(1,128)S(1)} %get-tuple-element.36.gain, bf16[1024,512]{1,0:T(8,128)(2,1)S(1)} %get-tuple-element.37.wq, ...), custom_call_target="tpu_custom_call" | custom-call | flops 2415919104 | bytes 9437184 | tf_op jit(solution)/shard_map/mlp/pallas_call | solution.py:81
  17.9 0.4 collective-permute-done.2.refs_3_
  18.3 0.0 collective-permute-done.3.refs_1_
  18.3 1.0 %project.3 = bf16[384,1024]{1,0:T(8,128)(2,1)S(1)} custom-call(bf16[128,1024]{1,0:T(8,128)(2,1)S(1)} %get-tuple-element.47.refs_0_, bf16[128,1024]{1,0:T(8,128)(2,1)S(1)} %collective-permute-done.3.refs_1_, bf16[64,1024]{1,0:T(8,128)(2,1)S(1)} %collective-permute-done.1.refs_2_, bf16[64,1024]{1,0:T(8,128)(2,1)S(1)} %collective-permute-done.2.refs_3_, ...), custom_call_target="tpu_custom_call" | custom-call | flops 60397977600 | bytes 275251200 | tf_op jit(solution)/shard_map/project/pallas_call | solution.py:175
  19.3 0.0 copy-start.1
  19.3 0.1 collective-permute-start.7
  19.4 1.4 %collective-permute-done.5.refs_1_ = bf16[64,1024]{1,0:T(8,128)(2,1)S(1)} collective-permute-done((bf16[64,1024]{1,0:T(8,128)(2,1)S(1)}, bf16[64,1024]{1,0:T(8,128)(2,1)S(1)}, u32[]{:S(2)}, u32[]{:S(2)}) %collective-permute-start.5) | collective-permute-done | bytes 131104 | tf_op jit(solution)/shard_map/ppermute | solution.py:400
  20.8 0.7 %collective-permute-done.4.refs_0_ = bf16[64,1024]{1,0:T(8,128)(2,1)S(1)} collective-permute-done((bf16[64,1024]{1,0:T(8,128)(2,1)S(1)}, bf16[64,1024]{1,0:T(8,128)(2,1)S(1)}, u32[]{:S(2)}, u32[]{:S(2)}) %collective-permute-start.4) | collective-permute-done | bytes 131104 | tf_op jit(solution)/shard_map/ppermute | solution.py:400
  21.5 0.4 project.2
  22.0 0.1 collective-permute-start.6
  22.0 0.0 collective-permute-done.7
  22.1 0.1 table.1.table_in
  22.2 1.4 %collective-permute-done.6 = bf16[128,1024]{1,0:T(8,128)(2,1)S(1)} collective-permute-done((bf16[128,1024]{1,0:T(8,128)(2,1)S(1)}, bf16[128,1024]{1,0:T(8,128)(2,1)S(1)}, u32[]{:S(2)}, u32[]{:S(2)}) %collective-permute-start.6) | collective-permute-done | bytes 262176 | tf_op jit(solution)/shard_map/ppermute | solution.py:404
  23.6 0.0 copy-done.1
  23.6 2.5 %attend.1 = (bf16[256,128]{1,0:T(8,128)(2,1)S(1)}, bf16[256,128]{1,0:T(8,128)(2,1)S(1)}, bf16[256,512]{1,0:T(8,128)(2,1)S(1)}, bf16[2,8,64,1024]{3,2,1,0:T(8,128)(2,1)S(1)}) custom-call(s32[4,8]{1,0:T(4,128)S(1)} %copy-done.1, bf16[256,512]{1,0:T(8,128)(2,1)S(1)} %get-tuple-element.44.q, ...), custom_call_target="tpu_custom_call", output_to_operand_aliasing={{3}: (4, {})} | custom-call | flops 13421772800 | bytes 41943040 | tf_op jit(solution)/shard_map/attend/pallas_call | solution.py:283
  26.0 0.7 %collective-permute-start.9 = (bf16[256,128]{1,0:T(8,128)(2,1)S(1)}, bf16[256,128]{1,0:T(8,128)(2,1)S(1)}, u32[]{:S(2)}, u32[]{:S(2)}) collective-permute-start(bf16[256,128]{1,0:T(8,128)(2,1)S(1)} %get-tuple-element.56), channel_id=1, source_target_pairs={{0,2},{2,0},{1,3},{3,1},{4,6},{6,4},{5,7},{7,5},{8,10},{10,8},{9,1... | collective-permute-start | bytes 196616 | tf_op jit(solution)/shard_map/ppermute | solution.py:404
  26.7 0.0 copy-start.2
  26.7 0.0 copy-start
  26.7 0.4 project_out.1
  27.1 1.5 %collective-permute-start.8 = (bf16[256,384]{1,0:T(8,128)(2,1)S(1)}, bf16[256,384]{1,0:T(8,128)(2,1)S(1)}, u32[]{:S(2)}, u32[]{:S(2)}) collective-permute-start(bf16[256,384]{1,0:T(8,128)(2,1)S(1)} %get-tuple-element.54), channel_id=1, source_target_pairs={{0,2},{2,0},{1,3},{3,1},{4,6},{6,4},{5,7},{7,5},{8,10},{10,8},{9,1... | collective-permute-start | bytes 589832 | tf_op jit(solution)/shard_map/ppermute | solution.py:404
  28.6 0.0 copy-done.2
  28.6 0.1 copy.15.owners
  28.7 2.3 %collective-permute-done.9.refs_1_.refs_2_ = bf16[256,128]{1,0:T(8,128)(2,1)S(1)} collective-permute-done((bf16[256,128]{1,0:T(8,128)(2,1)S(1)}, bf16[256,128]{1,0:T(8,128)(2,1)S(1)}, u32[]{:S(2)}, u32[]{:S(2)}) %collective-permute-start.9) | collective-permute-done | bytes 65568 | tf_op jit(solution)/shard_map/ppermute | solution.py:404
  31.1 0.0 copy-done
  31.1 0.6 %combine.3 = (bf16[2,64,128]{2,1,0:T(8,128)(2,1)S(1)}, bf16[2,64,128]{2,1,0:T(8,128)(2,1)S(1)}) custom-call(s32[4,1]{1,0:T(4,128)S(1)} %copy.15.owners, bf16[4,64,512]{2,1,0:T(8,128)(2,1)S(1)} %copy-done, bf16[256,128]{1,0:T(8,128)(2,1)S(1)} %get-tuple-element.55.refs_0_, bf16[256,128]{1,0:T(8,128)(2,1)S(1)} %collective-permute-done.9.refs_1_.refs_2_), custom_call_target="tpu_custom_call" | custom-call | flops 1966080000 | bytes 52428800 | tf_op jit(solution)/shard_map/combine/pallas_call | solution.py:355
  31.7 0.9 %collective-permute-start.13 = (bf16[2,64,128]{2,1,0:T(8,128)(2,1)S(1)}, bf16[2,64,128]{2,1,0:T(8,128)(2,1)S(1)}, u32[]{:S(2)}, u32[]{:S(2)}) collective-permute-start(bf16[2,64,128]{2,1,0:T(8,128)(2,1)S(1)} %get-tuple-element.57), channel_id=1, source_target_pairs={{0,8},{4,12},{8,0},{12,4},{1,9},{5,13},{9,1},{13,5},{2,10},{6,14},... | collective-permute-start | bytes 98312 | tf_op jit(solution)/shard_map/ppermute | solution.py:400
  32.6 2.7 %collective-permute-start.14 = (bf16[2,64,128]{2,1,0:T(8,128)(2,1)S(1)}, bf16[2,64,128]{2,1,0:T(8,128)(2,1)S(1)}, u32[]{:S(2)}, u32[]{:S(2)}) collective-permute-start(bf16[2,64,128]{2,1,0:T(8,128)(2,1)S(1)} %get-tuple-element.64), channel_id=1, source_target_pairs={{0,12},{4,8},{8,4},{12,0},{1,13},{5,9},{9,5},{13,1},{2,14},{6,10},... | collective-permute-start | bytes 98312 | tf_op jit(solution)/shard_map/ppermute | solution.py:400
  35.3 0.0 collective-permute-done.8.refs_1_.refs_3_
  35.3 0.7 %combine.4 = (bf16[2,64,384]{2,1,0:T(8,128)(2,1)S(1)}, bf16[2,64,384]{2,1,0:T(8,128)(2,1)S(1)}) custom-call(s32[4,1]{1,0:T(4,128)S(1)} %copy.15.owners, bf16[4,64,512]{2,1,0:T(8,128)(2,1)S(1)} %copy-done, bf16[256,384]{1,0:T(8,128)(2,1)S(1)} %get-tuple-element.53.refs_0_.refs_1_, bf16[256,384]{1,0:T(8,128)(2,1)S(1)} %collective-permute-done.8.refs_1_.refs_3_), custom_call_target="tpu_custom_call" | custom-call | flops 5898240000 | bytes 157286400 | tf_op jit(solution)/shard_map/combine/pallas_call | solution.py:355
  36.0 1.0 %collective-permute-start.10 = (bf16[2,64,384]{2,1,0:T(8,128)(2,1)S(1)}, bf16[2,64,384]{2,1,0:T(8,128)(2,1)S(1)}, u32[]{:S(2)}, u32[]{:S(2)}) collective-permute-start(bf16[2,64,384]{2,1,0:T(8,128)(2,1)S(1)} %get-tuple-element.59), channel_id=1, source_target_pairs={{0,8},{4,12},{8,0},{12,4},{1,9},{5,13},{9,1},{13,5},{2,10},{6,14},... | collective-permute-start | bytes 294920 | tf_op jit(solution)/shard_map/ppermute | solution.py:400
  37.0 0.7 %combine.5 = (bf16[2,64,512]{2,1,0:T(8,128)(2,1)S(1)}, bf16[2,64,512]{2,1,0:T(8,128)(2,1)S(1)}) custom-call(s32[4,1]{1,0:T(4,128)S(1)} %copy.15.owners, bf16[4,64,512]{2,1,0:T(8,128)(2,1)S(1)} %copy-done, bf16[256,128]{1,0:T(8,128)(2,1)S(1)} %get-tuple-element.55.refs_0_, bf16[256,384]{1,0:T(8,128)(2,1)S(1)} %get-tuple-element.53.refs_0_.refs_1_, ...), custom_call_target="tpu_custom_call" | custom-call | flops 7864320000 | bytes 209715200 | tf_op jit(solution)/shard_map/combine/pallas_call | solution.py:355
  37.7 1.4 %collective-permute-start.12 = (bf16[2,64,512]{2,1,0:T(8,128)(2,1)S(1)}, bf16[2,64,512]{2,1,0:T(8,128)(2,1)S(1)}, u32[]{:S(2)}, u32[]{:S(2)}) collective-permute-start(bf16[2,64,512]{2,1,0:T(8,128)(2,1)S(1)} %get-tuple-element.62), channel_id=1, source_target_pairs={{0,4},{4,0},{8,12},{12,8},{1,5},{5,1},{9,13},{13,9},{2,6},{6,2},{1... | collective-permute-start | bytes 393224 | tf_op jit(solution)/shard_map/ppermute | solution.py:400
  39.1 2.1 %collective-permute-start.11 = (bf16[2,64,384]{2,1,0:T(8,128)(2,1)S(1)}, bf16[2,64,384]{2,1,0:T(8,128)(2,1)S(1)}, u32[]{:S(2)}, u32[]{:S(2)}) collective-permute-start(bf16[2,64,384]{2,1,0:T(8,128)(2,1)S(1)} %get-tuple-element.60), channel_id=1, source_target_pairs={{0,12},{4,8},{8,4},{12,0},{1,13},{5,9},{9,5},{13,1},{2,14},{6,10},... | collective-permute-start | bytes 294920 | tf_op jit(solution)/shard_map/ppermute | solution.py:400
  41.2 0.0 collective-permute-done.13.refs_0_
  41.2 0.0 collective-permute-done.14.refs_1_
  41.2 0.6 %place.2.refs_4_ = bf16[8,64,512]{2,1,0:T(8,128)(2,1)} custom-call(bf16[2,64,128]{2,1,0:T(8,128)(2,1)S(1)} %collective-permute-done.13.refs_0_, bf16[2,64,128]{2,1,0:T(8,128)(2,1)S(1)} %collective-permute-done.14.refs_1_), custom_call_target="tpu_custom_call" | custom-call | flops 13107200000 | tf_op jit(solution)/shard_map/place/pallas_call | solution.py:384
  41.8 2.8 %collective-permute-done.10.refs_0_ = bf16[2,64,384]{2,1,0:T(8,128)(2,1)S(1)} collective-permute-done((bf16[2,64,384]{2,1,0:T(8,128)(2,1)S(1)}, bf16[2,64,384]{2,1,0:T(8,128)(2,1)S(1)}, u32[]{:S(2)}, u32[]{:S(2)}) %collective-permute-start.10) | collective-permute-done | bytes 98336 | tf_op jit(solution)/shard_map/ppermute | solution.py:400
  44.6 1.5 %collective-permute-done.11.refs_1_ = bf16[2,64,384]{2,1,0:T(8,128)(2,1)S(1)} collective-permute-done((bf16[2,64,384]{2,1,0:T(8,128)(2,1)S(1)}, bf16[2,64,384]{2,1,0:T(8,128)(2,1)S(1)}, u32[]{:S(2)}, u32[]{:S(2)}) %collective-permute-start.11) | collective-permute-done | bytes 98336 | tf_op jit(solution)/shard_map/ppermute | solution.py:400
  46.2 0.0 collective-permute-done.12.refs_2_
  46.2 0.8 %place.3 = bf16[8,64,512]{2,1,0:T(8,128)(2,1)} custom-call(bf16[2,64,384]{2,1,0:T(8,128)(2,1)S(1)} %collective-permute-done.10.refs_0_, bf16[2,64,384]{2,1,0:T(8,128)(2,1)S(1)} %collective-permute-done.11.refs_1_, bf16[2,64,512]{2,1,0:T(8,128)(2,1)S(1)} %collective-permute-done.12.refs_2_, ...), custom_call_target="tpu_custom_call", output_to_operand_aliasing={{}: (4, {})} | custom-call | flops 91750400000 | tf_op jit(solution)/shard_map/place/pallas_call | solution.py:384
Async XLA Ops:
  0.0 14.5 %collective-permute-start = (bf16[256,512]{1,0:T(8,128)(2,1)}, bf16[256,512]{1,0:T(8,128)(2,1)S(1)}, u32[]{:S(2)}, u32[]{:S(2)}) collective-permute-start(bf16[256,512]{1,0:T(8,128)(2,1)} %bitcast.8), channel_id=1, source_target_pairs={{0,2},{2,0},{1,3},{3,1},{4,6},{6,4},{5,7},{7,5},{8,10},{10,8},{9,1... | collective-permute-start | bytes 786440 | tf_op jit(solution)/shard_map/ppermute | solution.py:404
  3.9 9.4 %collective-permute-start.1 = (bf16[64,1024]{1,0:T(8,128)(2,1)S(1)}, bf16[64,1024]{1,0:T(8,128)(2,1)S(1)}, u32[]{:S(2)}, u32[]{:S(2)}) collective-permute-start(bf16[64,1024]{1,0:T(8,128)(2,1)S(1)} %pick.1), channel_id=1, source_target_pairs={{0,8},{4,12},{8,0},{12,4},{1,9},{5,13},{9,1},{13,5},{2,10},{6,14},... | collective-permute-start | bytes 393224 | tf_op jit(solution)/shard_map/ppermute | solution.py:400
  6.5 11.8 %collective-permute-start.3 = (bf16[128,1024]{1,0:T(8,128)(2,1)}, bf16[128,1024]{1,0:T(8,128)(2,1)S(1)}, u32[]{:S(2)}, u32[]{:S(2)}) collective-permute-start(bf16[128,1024]{1,0:T(8,128)(2,1)} %mesh.1), channel_id=1, source_target_pairs={{0,4},{4,0},{8,12},{12,8},{1,5},{5,1},{9,13},{13,9},{2,6},{6,2},{1... | collective-permute-start | bytes 786440 | tf_op jit(solution)/shard_map/ppermute | solution.py:400
  13.0 7.8 %collective-permute-start.5 = (bf16[64,1024]{1,0:T(8,128)(2,1)S(1)}, bf16[64,1024]{1,0:T(8,128)(2,1)S(1)}, u32[]{:S(2)}, u32[]{:S(2)}) collective-permute-start(bf16[64,1024]{1,0:T(8,128)(2,1)S(1)} %get-tuple-element.42), channel_id=1, source_target_pairs={{0,12},{4,8},{8,4},{12,0},{1,13},{5,9},{9,5},{13,1},{2,14},{6,10},... | collective-permute-start | bytes 393224 | tf_op jit(solution)/shard_map/ppermute | solution.py:400
  13.3 5.0 %collective-permute-start.2 = (bf16[64,1024]{1,0:T(8,128)(2,1)S(1)}, bf16[64,1024]{1,0:T(8,128)(2,1)S(1)}, u32[]{:S(2)}, u32[]{:S(2)}) collective-permute-start(bf16[64,1024]{1,0:T(8,128)(2,1)S(1)} %collective-permute-done.1.refs_2_), channel_id=1, source_target_pairs={{0,2},{2,0},{1,3},{3,1},{4,6},{6,4},{5,7},{7,5},{8,10},{10,8},{9,1... | collective-permute-start | bytes 393224 | tf_op jit(solution)/shard_map/ppermute | solution.py:404
  13.7 7.8 %collective-permute-start.4 = (bf16[64,1024]{1,0:T(8,128)(2,1)S(1)}, bf16[64,1024]{1,0:T(8,128)(2,1)S(1)}, u32[]{:S(2)}, u32[]{:S(2)}) collective-permute-start(bf16[64,1024]{1,0:T(8,128)(2,1)S(1)} %collective-permute-done.1.refs_2_), channel_id=1, source_target_pairs={{0,4},{4,0},{8,12},{12,8},{1,5},{5,1},{9,13},{13,9},{2,6},{6,2},{1... | collective-permute-start | bytes 393224 | tf_op jit(solution)/shard_map/ppermute | solution.py:400
  19.3 4.3 %copy-start.1 = (s32[4,8]{1,0:T(4,128)S(1)}, s32[4,8]{1,0:T(4,128)}, u32[]{:S(2)}) copy-start(s32[4,8]{1,0:T(4,128)} %adjacency.1) | copy-start | bytes 388
  19.3 2.8 %collective-permute-start.7 = (bf16[384,1024]{1,0:T(8,128)(2,1)S(1)}, bf16[384,1024]{1,0:T(8,128)(2,1)S(1)}, u32[]{:S(2)}, u32[]{:S(2)}) collective-permute-start(bf16[384,1024]{1,0:T(8,128)(2,1)S(1)} %project.3), channel_id=1, source_target_pairs={{0,1},{1,0},{2,3},{3,2},{4,5},{5,4},{6,7},{7,6},{8,9},{9,8},{10,11... | collective-permute-start | bytes 2359304 | tf_op jit(solution)/shard_map/ppermute | solution.py:404
  22.0 1.6 %collective-permute-start.6 = (bf16[128,1024]{1,0:T(8,128)(2,1)S(1)}, bf16[128,1024]{1,0:T(8,128)(2,1)S(1)}, u32[]{:S(2)}, u32[]{:S(2)}) collective-permute-start(bf16[128,1024]{1,0:T(8,128)(2,1)S(1)} %project.2), channel_id=1, source_target_pairs={{0,1},{1,0},{2,3},{3,2},{4,5},{5,4},{6,7},{7,6},{8,9},{9,8},{10,11... | collective-permute-start | bytes 786440 | tf_op jit(solution)/shard_map/ppermute | solution.py:404
  26.0 5.0 %collective-permute-start.9 = (bf16[256,128]{1,0:T(8,128)(2,1)S(1)}, bf16[256,128]{1,0:T(8,128)(2,1)S(1)}, u32[]{:S(2)}, u32[]{:S(2)}) collective-permute-start(bf16[256,128]{1,0:T(8,128)(2,1)S(1)} %get-tuple-element.56), channel_id=1, source_target_pairs={{0,2},{2,0},{1,3},{3,1},{4,6},{6,4},{5,7},{7,5},{8,10},{10,8},{9,1... | collective-permute-start | bytes 196616 | tf_op jit(solution)/shard_map/ppermute | solution.py:404
  26.7 1.9 %copy-start.2 = (s32[4,1]{0,1:T(1,128)S(1)}, s32[4,1]{0,1:T(1,128)}, u32[]{:S(2)}) copy-start(s32[4,1]{0,1:T(1,128)} %param.12) | copy-start | bytes 52
  26.7 4.4 %copy-start = (bf16[4,64,512]{2,1,0:T(8,128)(2,1)S(1)}, bf16[4,64,512]{2,1,0:T(8,128)(2,1)}, u32[]{:S(2)}) copy-start(bf16[4,64,512]{2,1,0:T(8,128)(2,1)} %grid_features.5) | copy-start | bytes 786436
  27.1 8.2 %collective-permute-start.8 = (bf16[256,384]{1,0:T(8,128)(2,1)S(1)}, bf16[256,384]{1,0:T(8,128)(2,1)S(1)}, u32[]{:S(2)}, u32[]{:S(2)}) collective-permute-start(bf16[256,384]{1,0:T(8,128)(2,1)S(1)} %get-tuple-element.54), channel_id=1, source_target_pairs={{0,2},{2,0},{1,3},{3,1},{4,6},{6,4},{5,7},{7,5},{8,10},{10,8},{9,1... | collective-permute-start | bytes 589832 | tf_op jit(solution)/shard_map/ppermute | solution.py:404
  31.7 9.5 %collective-permute-start.13 = (bf16[2,64,128]{2,1,0:T(8,128)(2,1)S(1)}, bf16[2,64,128]{2,1,0:T(8,128)(2,1)S(1)}, u32[]{:S(2)}, u32[]{:S(2)}) collective-permute-start(bf16[2,64,128]{2,1,0:T(8,128)(2,1)S(1)} %get-tuple-element.57), channel_id=1, source_target_pairs={{0,8},{4,12},{8,0},{12,4},{1,9},{5,13},{9,1},{13,5},{2,10},{6,14},... | collective-permute-start | bytes 98312 | tf_op jit(solution)/shard_map/ppermute | solution.py:400
  32.6 8.6 %collective-permute-start.14 = (bf16[2,64,128]{2,1,0:T(8,128)(2,1)S(1)}, bf16[2,64,128]{2,1,0:T(8,128)(2,1)S(1)}, u32[]{:S(2)}, u32[]{:S(2)}) collective-permute-start(bf16[2,64,128]{2,1,0:T(8,128)(2,1)S(1)} %get-tuple-element.64), channel_id=1, source_target_pairs={{0,12},{4,8},{8,4},{12,0},{1,13},{5,9},{9,5},{13,1},{2,14},{6,10},... | collective-permute-start | bytes 98312 | tf_op jit(solution)/shard_map/ppermute | solution.py:400
  36.0 8.6 %collective-permute-start.10 = (bf16[2,64,384]{2,1,0:T(8,128)(2,1)S(1)}, bf16[2,64,384]{2,1,0:T(8,128)(2,1)S(1)}, u32[]{:S(2)}, u32[]{:S(2)}) collective-permute-start(bf16[2,64,384]{2,1,0:T(8,128)(2,1)S(1)} %get-tuple-element.59), channel_id=1, source_target_pairs={{0,8},{4,12},{8,0},{12,4},{1,9},{5,13},{9,1},{13,5},{2,10},{6,14},... | collective-permute-start | bytes 294920 | tf_op jit(solution)/shard_map/ppermute | solution.py:400
  37.7 8.5 %collective-permute-start.12 = (bf16[2,64,512]{2,1,0:T(8,128)(2,1)S(1)}, bf16[2,64,512]{2,1,0:T(8,128)(2,1)S(1)}, u32[]{:S(2)}, u32[]{:S(2)}) collective-permute-start(bf16[2,64,512]{2,1,0:T(8,128)(2,1)S(1)} %get-tuple-element.62), channel_id=1, source_target_pairs={{0,4},{4,0},{8,12},{12,8},{1,5},{5,1},{9,13},{13,9},{2,6},{6,2},{1... | collective-permute-start | bytes 393224 | tf_op jit(solution)/shard_map/ppermute | solution.py:400
  39.1 7.1 %collective-permute-start.11 = (bf16[2,64,384]{2,1,0:T(8,128)(2,1)S(1)}, bf16[2,64,384]{2,1,0:T(8,128)(2,1)S(1)}, u32[]{:S(2)}, u32[]{:S(2)}) collective-permute-start(bf16[2,64,384]{2,1,0:T(8,128)(2,1)S(1)} %get-tuple-element.60), channel_id=1, source_target_pairs={{0,12},{4,8},{8,4},{12,0},{1,13},{5,9},{9,5},{13,1},{2,14},{6,10},... | collective-permute-start | bytes 294920 | tf_op jit(solution)/shard_map/ppermute | solution.py:400

commit v13 on v12

--- a/solution.py
+++ b/solution.py
@@ -31,6 +31,10 @@
 
 def in_hbm(x):
     return pltpu.with_memory_space_constraint(x, pltpu.HBM)
+
+
+def in_vmem(x):
+    return pltpu.with_memory_space_constraint(x, pltpu.VMEM)
 
 
 def whole(space):
@@ -121,25 +125,34 @@
     sources, targets, sem = refs[: len(axes)], refs[len(axes) : -1], refs[-1]
     h = lax.axis_index("head")
     copies = []
+
+    def add(source, target):
+        pieces = 2 if source.shape[0] >= 512 else 1
+        rows = source.shape[0] // pieces
+        for piece in range(pieces):
+            span = pl.ds(piece * rows, rows)
+            copies.append(
+                pltpu.make_async_copy(
+                    source.at[span, :], target.at[span, :], sem.at[len(copies)]
+                )
+            )
+            copies[-1].start()
+
     for source, target, axis in zip(sources, targets, axes):
         if axis is None:
-            copies.append(pltpu.make_async_copy(source, target, sem.at[len(copies)]))
+            add(source, target)
             continue
         if axis == "rest":
-            span = pl.ds(pl.multiple_of((1 - h) * BLOCK, BLOCK), BLOCK)
-            copies.append(pltpu.make_async_copy(source.at[span, :], target, sem.at[len(copies)]))
+            add(source.at[pl.ds(pl.multiple_of((1 - h) * BLOCK, BLOCK), BLOCK), :], target)
             continue
         half = source.shape[axis] // 2
         for part, head in enumerate((1 - h, h)):
             span = pl.ds(pl.multiple_of(head * half, half), half)
             place = pl.ds(part * half, half)
             if axis == 0:
-                pair = (source.at[span, :], target.at[place, :])
+                add(source.at[span, :], target.at[place, :])
             else:
-                pair = (source.at[:, span], target.at[:, place])
-            copies.append(pltpu.make_async_copy(*pair, sem.at[len(copies)]))
-    for copy in copies:
-        copy.start()
+                add(source.at[:, span], target.at[:, place])
     for copy in copies:
         copy.wait()
 
@@ -154,9 +167,11 @@
         ),
         in_specs=[whole(pltpu.HBM)] * len(arrays),
         out_specs=tuple(vmem(len(arrays))),
-        scratch_shapes=[pltpu.SemaphoreType.DMA((2 * len(arrays),))],
+        scratch_shapes=[pltpu.SemaphoreType.DMA((4 * len(arrays),))],
         compiler_params=params(16),
-        cost_estimate=pl.CostEstimate(flops=0, bytes_accessed=20 * size, transcendentals=0),
+        cost_estimate=pl.CostEstimate(
+            flops=2000 * size, bytes_accessed=20 * size, transcendentals=0
+        ),
         name="stage",
     )(*(in_hbm(array) for array in arrays))
 
@@ -184,7 +199,7 @@
             transcendentals=0,
         ),
         name="project",
-    )(*pieces, wk, wv)
+    )(*pieces, in_vmem(wk), in_vmem(wv))
 
 
 def table_kernel(mine, sibling, table):
@@ -420,25 +435,24 @@
     shards = lax.axis_size("shard")
     count, rows, half = grid_features.shape
     flat = grid_features.reshape(count * rows, half)
-    far = crossed(run_pick(mesh_nodes), 2, shards)
-    near = crossed(mesh_nodes, 1, shards)
-    other = swapped(flat, "head")
-    staged = run_stage(
+    half_unit = run_pick(mesh_nodes)
+    far = crossed(half_unit, 2, shards)
+    waiting, _ = lax.optimization_barrier((mesh_nodes, half_unit))
+    near = crossed(waiting, 1, shards)
+    waiting, _ = lax.optimization_barrier((flat, half_unit))
+    other = swapped(waiting, "head")
+    flat, gain, wq, wup, wdn, mesh, rest = run_stage(
         (
             flat,
             norm_gain.reshape(1, -1),
             query_weight,
             up_weight,
             down_weight,
-            output_weight,
-            key_weight,
-            value_weight,
             mesh_nodes,
             mesh_nodes,
         ),
-        (None, 1, 0, 0, 1, 1, None, None, None, "rest"),
-    )
-    flat, gain, wq, wup, wdn, wo, wk, wv, mesh, rest = staged
+        (None, 1, 0, 0, 1, None, "rest"),
+    )
     straight = crossed(rest, 3, shards)
     far, _ = lax.optimization_barrier((far, rest))
     farther = crossed(far, 1, shards)
@@ -446,10 +460,12 @@
     queries, mlp = run_mlp(flat, other, gain, wq, wup, wdn)
     queries, mlp, far_pair, near = lax.optimization_barrier((queries, mlp, far_pair, near))
     blocked = (-1, BLOCK, 2 * half)
-    mine_a = run_project((mesh, near, far, far_pair), wk, wv)
+    mine_a = run_project((mesh, near, far, far_pair), key_weight, value_weight)
     sibling_a = swapped(mine_a, "sub")
+    unstaged, _ = lax.optimization_barrier((output_weight, mine_a))
+    (wo,) = run_stage((unstaged,), (1,))
     table = run_table(mine_a.reshape(blocked), sibling_a.reshape(blocked), 2 * shards)
-    mine_b = run_project((farther, straight), wk, wv)
+    mine_b = run_project((farther, straight), key_weight, value_weight)
     sibling_b = swapped(mine_b, "sub")
     send, keep, att = run_attend(
         adjacency, queries, mine_b.reshape(blocked), sibling_b.reshape(blocked), table, mlp, wo

time: 47.1 us -> 47.1 us (level)
  starting transfers between devices: 19.1 us -> 18.1 us
  waiting for transfers between devices: 10.7 us -> 11.2 us
    ppermute x9, waiting for transfers between devices: 6.55 us -> 8 us  [crossed(): return lax.ppermute(x, 'shard', [(i, i ^ distance) for i in range(size)])]
    ppermute x6, starting transfers between devices: 5.64 us -> 4.27 us  [swapped(): return lax.ppermute(x, axis, [(0, 1), (1, 0)])]
    ppermute x6, waiting for transfers between devices: 4.16 us -> 3.24 us  [swapped(): return lax.ppermute(x, axis, [(0, 1), (1, 0)])]
    pallas_call x1 -> x2, Pallas kernels: 4.92 us -> 5.33 us  [run_stage(): pl.pallas_call(functools.partial(stage_kernel, axes), out_shape=tuple((ja...]
  transfers between devices with their start and end apart: 15 -> 15, of which waited for: 7 -> 10; matrix products, arithmetic and copies ran while one was open for 0% -> 0% of each run, Pallas kernels for 29% -> 28%
where the time goes in v13:
time: 47.1 us; the launch traced here: 47 us
  starting transfers between devices  18.1 us (38%)
  Pallas kernels  17.3 us (37%)
  waiting for transfers between devices  11.2 us (24%)
    ppermute x9, starting transfers between devices, crossed(): return lax.ppermute(x, 'shard', [(i, i ^ distance) for i in range(size)])  13.8 us
    ppermute x9, waiting for transfers between devices, crossed(): return lax.ppermute(x, 'shard', [(i, i ^ distance) for i in range(size)])  8 us
    pallas_call x2, Pallas kernels, run_stage(): pl.pallas_call(functools.partial(stage_kernel, axes), out_shape=tuple((ja...  5.33 us
    ppermute x6, starting transfers between devices, swapped(): return lax.ppermute(x, axis, [(0, 1), (1, 0)])  4.27 us
    pallas_call x1, Pallas kernels, run_mlp(): pl.pallas_call(mlp_kernel, out_shape=(jax.ShapeDtypeStruct((rows, wq.shap...  3.33 us
    ppermute x6, waiting for transfers between devices, swapped(): return lax.ppermute(x, axis, [(0, 1), (1, 0)])  3.24 us
    pallas_call x1, Pallas kernels, run_attend(): pl.pallas_call(attend_kernel, out_shape=(part, part, jax.ShapeDtypeStruct...  2.43 us
    pallas_call x3, Pallas kernels, run_combine(): pl.pallas_call(functools.partial(combine_kernel, chunks, distances), out_...  1.95 us
  transfers between devices with their start and end apart: 15, of which 10 were waited for; matrix products, arithmetic and copies ran while one was open for 0% of the time, Pallas kernels for 28%

profile of v13, /device:TPU:0, one launch (start us, length us, event | category | flops | bytes accessed | tf_op | source)
XLA Modules:
  0.0 47.0 jit_solution(4597645039992645216)
XLA Ops:
  0.0 0.9 %pick.1 = bf16[64,1024]{1,0:T(8,128)(2,1)S(1)} custom-call(bf16[128,1024]{1,0:T(8,128)(2,1)} %mesh.1), custom_call_target="tpu_custom_call" | custom-call | bytes 524288 | tf_op jit(solution)/shard_map/pick/pallas_call | solution.py:112
  0.9 4.1 %collective-permute-start.1 = (bf16[64,1024]{1,0:T(8,128)(2,1)S(1)}, bf16[64,1024]{1,0:T(8,128)(2,1)S(1)}, u32[]{:S(2)}, u32[]{:S(2)}) collective-permute-start(bf16[64,1024]{1,0:T(8,128)(2,1)S(1)} %pick.1), channel_id=1, source_target_pairs={{0,8},{4,12},{8,0},{12,4},{1,9},{5,13},{9,1},{13,5},{2,10},{6,14},... | collective-permute-start | bytes 393224 | tf_op jit(solution)/shard_map/ppermute | solution.py:415
  5.0 1.5 %collective-permute-start = (bf16[256,512]{1,0:T(8,128)(2,1)}, bf16[256,512]{1,0:T(8,128)(2,1)S(1)}, u32[]{:S(2)}, u32[]{:S(2)}) collective-permute-start(bf16[256,512]{1,0:T(8,128)(2,1)} %bitcast.8), channel_id=1, source_target_pairs={{0,2},{2,0},{1,3},{3,1},{4,6},{6,4},{5,7},{7,5},{8,10},{10,8},{9,1... | collective-permute-start | bytes 786440 | tf_op jit(solution)/shard_map/ppermute | solution.py:419
  6.5 1.6 %collective-permute-start.3 = (bf16[128,1024]{1,0:T(8,128)(2,1)}, bf16[128,1024]{1,0:T(8,128)(2,1)S(1)}, u32[]{:S(2)}, u32[]{:S(2)}) collective-permute-start(bf16[128,1024]{1,0:T(8,128)(2,1)} %mesh.1), channel_id=1, source_target_pairs={{0,4},{4,0},{8,12},{12,8},{1,5},{5,1},{9,13},{13,9},{2,6},{6,2},{1... | collective-permute-start | bytes 786440 | tf_op jit(solution)/shard_map/ppermute | solution.py:415
  8.1 4.1 %stage.2 = (bf16[256,512]{1,0:T(8,128)(2,1)S(1)}, f32[1,1024]{1,0:T(1,128)S(1)}, bf16[1024,512]{1,0:T(8,128)(2,1)S(1)}, bf16[1024,2048]{1,0:T(8,128)(2,1)S(1)}, ...) custom-call(bf16[256,512]{1,0:T(8,128)(2,1)} %bitcast.9, ...), custom_call_target="tpu_custom_call" | custom-call | flops 20451328000 | bytes 204513280 | tf_op jit(solution)/shard_map/stage/pallas_call | solution.py:162
  12.2 0.3 collective-permute-start.5
  12.5 0.0 collective-permute-done.1.refs_2_
  12.5 0.5 %collective-permute-start.2 = (bf16[64,1024]{1,0:T(8,128)(2,1)S(1)}, bf16[64,1024]{1,0:T(8,128)(2,1)S(1)}, u32[]{:S(2)}, u32[]{:S(2)}) collective-permute-start(bf16[64,1024]{1,0:T(8,128)(2,1)S(1)} %collective-permute-done.1.refs_2_), channel_id=1, source_target_pairs={{0,2},{2,0},{1,3},{3,1},{4,6},{6,4},{5,7},{7,5},{8,10},{10,8},{9,1... | collective-permute-start | bytes 393224 | tf_op jit(solution)/shard_map/ppermute | solution.py:419
  13.0 0.7 %collective-permute-start.4 = (bf16[64,1024]{1,0:T(8,128)(2,1)S(1)}, bf16[64,1024]{1,0:T(8,128)(2,1)S(1)}, u32[]{:S(2)}, u32[]{:S(2)}) collective-permute-start(bf16[64,1024]{1,0:T(8,128)(2,1)S(1)} %collective-permute-done.1.refs_2_), channel_id=1, source_target_pairs={{0,4},{4,0},{8,12},{12,8},{1,5},{5,1},{9,13},{13,9},{2,6},{6,2},{1... | collective-permute-start | bytes 393224 | tf_op jit(solution)/shard_map/ppermute | solution.py:415
  13.7 0.0 collective-permute-done.other
  13.7 0.0 copy-start
  13.7 0.0 copy-start.1
  13.7 3.3 %mlp.1 = (bf16[256,512]{1,0:T(8,128)(2,1)S(1)}, f32[256,1024]{1,0:T(8,128)S(1)}) custom-call(bf16[256,512]{1,0:T(8,128)(2,1)S(1)} %get-tuple-element.35.own, bf16[256,512]{1,0:T(8,128)(2,1)S(1)} %collective-permute-done.other, f32[1,1024]{1,0:T(1,128)S(1)} %get-tuple-element.37.gain, bf16[1024,512]{1,0:T(8,128)(2,1)S(1)} %get-tuple-element.38.wq, ...), custom_call_target="tpu_custom_call" | custom-call | flops 2415919104 | bytes 9437184 | tf_op jit(solution)/shard_map/mlp/pallas_call | solution.py:85
  17.1 0.4 collective-permute-done.2.refs_3_
  17.5 1.2 %collective-permute-done.3.refs_1_ = bf16[128,1024]{1,0:T(8,128)(2,1)S(1)} collective-permute-done((bf16[128,1024]{1,0:T(8,128)(2,1)}, bf16[128,1024]{1,0:T(8,128)(2,1)S(1)}, u32[]{:S(2)}, u32[]{:S(2)}) %collective-permute-start.3) | collective-permute-done | bytes 262176 | tf_op jit(solution)/shard_map/ppermute | solution.py:415
  18.7 0.0 copy-done
  18.7 0.0 copy-done.1
  18.7 1.0 %project.3 = bf16[384,1024]{1,0:T(8,128)(2,1)S(1)} custom-call(bf16[128,1024]{1,0:T(8,128)(2,1)S(1)} %get-tuple-element.47.refs_0_, bf16[128,1024]{1,0:T(8,128)(2,1)S(1)} %collective-permute-done.3.refs_1_, bf16[64,1024]{1,0:T(8,128)(2,1)S(1)} %collective-permute-done.1.refs_2_, bf16[64,1024]{1,0:T(8,128)(2,1)S(1)} %collective-permute-done.2.refs_3_, ...), custom_call_target="tpu_custom_call" | custom-call | flops 60397977600 | bytes 275251200 | tf_op jit(solution)/shard_map/project/pallas_call | solution.py:190
  19.7 0.1 collective-permute-start.7
  19.8 0.2 collective-permute-done.5.refs_1_
  20.0 1.5 %collective-permute-done.4.refs_0_ = bf16[64,1024]{1,0:T(8,128)(2,1)S(1)} collective-permute-done((bf16[64,1024]{1,0:T(8,128)(2,1)S(1)}, bf16[64,1024]{1,0:T(8,128)(2,1)S(1)}, u32[]{:S(2)}, u32[]{:S(2)}) %collective-permute-start.4) | collective-permute-done | bytes 131104 | tf_op jit(solution)/shard_map/ppermute | solution.py:415
  21.5 0.4 project.2
  21.9 0.0 copy-start.3
  21.9 0.1 collective-permute-start.6
  22.0 1.2 %stage.3.wo = bf16[512,1024]{1,0:T(8,128)(2,1)S(1)} custom-call(bf16[512,1024]{1,0:T(8,128)(2,1)} %refs_0_), custom_call_target="tpu_custom_call" | custom-call | flops 2097152000 | bytes 20971520 | tf_op jit(solution)/shard_map/stage/pallas_call | solution.py:162
  23.3 0.0 collective-permute-done.7
  23.3 0.1 table.1.table_in
  23.4 0.2 collective-permute-done.6
  23.5 0.0 copy-done.3
  23.5 2.4 %attend.1 = (bf16[256,128]{1,0:T(8,128)(2,1)S(1)}, bf16[256,128]{1,0:T(8,128)(2,1)S(1)}, bf16[256,512]{1,0:T(8,128)(2,1)S(1)}, bf16[2,8,64,1024]{3,2,1,0:T(8,128)(2,1)S(1)}) custom-call(s32[4,8]{1,0:T(4,128)S(1)} %copy-done.3, bf16[256,512]{1,0:T(8,128)(2,1)S(1)} %get-tuple-element.46.q, ...), custom_call_target="tpu_custom_call", output_to_operand_aliasing={{3}: (4, {})} | custom-call | flops 13421772800 | bytes 41943040 | tf_op jit(solution)/shard_map/attend/pallas_call | solution.py:298
  26.0 0.7 %collective-permute-start.9 = (bf16[256,128]{1,0:T(8,128)(2,1)S(1)}, bf16[256,128]{1,0:T(8,128)(2,1)S(1)}, u32[]{:S(2)}, u32[]{:S(2)}) collective-permute-start(bf16[256,128]{1,0:T(8,128)(2,1)S(1)} %get-tuple-element.56), channel_id=1, source_target_pairs={{0,2},{2,0},{1,3},{3,1},{4,6},{6,4},{5,7},{7,5},{8,10},{10,8},{9,1... | collective-permute-start | bytes 196616 | tf_op jit(solution)/shard_map/ppermute | solution.py:419
  26.6 0.0 copy-start.4
  26.6 0.0 copy-start.2
  26.6 0.4 project_out.1
  27.1 1.5 %collective-permute-start.8 = (bf16[256,384]{1,0:T(8,128)(2,1)S(1)}, bf16[256,384]{1,0:T(8,128)(2,1)S(1)}, u32[]{:S(2)}, u32[]{:S(2)}) collective-permute-start(bf16[256,384]{1,0:T(8,128)(2,1)S(1)} %get-tuple-element.54), channel_id=1, source_target_pairs={{0,2},{2,0},{1,3},{3,1},{4,6},{6,4},{5,7},{7,5},{8,10},{10,8},{9,1... | collective-permute-start | bytes 589832 | tf_op jit(solution)/shard_map/ppermute | solution.py:419
  28.6 0.0 copy-done.4
  28.6 0.1 copy.15.owners
  28.7 2.3 %collective-permute-done.9.refs_1_.refs_2_ = bf16[256,128]{1,0:T(8,128)(2,1)S(1)} collective-permute-done((bf16[256,128]{1,0:T(8,128)(2,1)S(1)}, bf16[256,128]{1,0:T(8,128)(2,1)S(1)}, u32[]{:S(2)}, u32[]{:S(2)}) %collective-permute-start.9) | collective-permute-done | bytes 65568 | tf_op jit(solution)/shard_map/ppermute | solution.py:419
  30.9 0.0 copy-done.2
  31.0 0.6 %combine.3 = (bf16[2,64,128]{2,1,0:T(8,128)(2,1)S(1)}, bf16[2,64,128]{2,1,0:T(8,128)(2,1)S(1)}) custom-call(s32[4,1]{1,0:T(4,128)S(1)} %copy.15.owners, bf16[4,64,512]{2,1,0:T(8,128)(2,1)S(1)} %copy-done.2, bf16[256,128]{1,0:T(8,128)(2,1)S(1)} %get-tuple-element.55.refs_0_, bf16[256,128]{1,0:T(8,128)(2,1)S(1)} %collective-permute-done.9.refs_1_.refs_2_), custom_call_target="tpu_custom_call" | custom-call | flops 1966080000 | bytes 52428800 | tf_op jit(solution)/shard_map/combine/pallas_call | solution.py:370
  31.6 0.2 collective-permute-start.13
  31.8 2.4 %collective-permute-start.14 = (bf16[2,64,128]{2,1,0:T(8,128)(2,1)S(1)}, bf16[2,64,128]{2,1,0:T(8,128)(2,1)S(1)}, u32[]{:S(2)}, u32[]{:S(2)}) collective-permute-start(bf16[2,64,128]{2,1,0:T(8,128)(2,1)S(1)} %get-tuple-element.64), channel_id=1, source_target_pairs={{0,12},{4,8},{8,4},{12,0},{1,13},{5,9},{9,5},{13,1},{2,14},{6,10},... | collective-permute-start | bytes 98312 | tf_op jit(solution)/shard_map/ppermute | solution.py:415
  34.2 0.4 collective-permute-done.8.refs_1_.refs_3_
  34.6 0.7 %combine.4 = (bf16[2,64,384]{2,1,0:T(8,128)(2,1)S(1)}, bf16[2,64,384]{2,1,0:T(8,128)(2,1)S(1)}) custom-call(s32[4,1]{1,0:T(4,128)S(1)} %copy.15.owners, bf16[4,64,512]{2,1,0:T(8,128)(2,1)S(1)} %copy-done.2, bf16[256,384]{1,0:T(8,128)(2,1)S(1)} %get-tuple-element.53.refs_0_.refs_1_, bf16[256,384]{1,0:T(8,128)(2,1)S(1)} %collective-permute-done.8.refs_1_.refs_3_), custom_call_target="tpu_custom_call" | custom-call | flops 5898240000 | bytes 157286400 | tf_op jit(solution)/shard_map/combine/pallas_call | solution.py:370
  35.3 1.6 %collective-permute-start.10 = (bf16[2,64,384]{2,1,0:T(8,128)(2,1)S(1)}, bf16[2,64,384]{2,1,0:T(8,128)(2,1)S(1)}, u32[]{:S(2)}, u32[]{:S(2)}) collective-permute-start(bf16[2,64,384]{2,1,0:T(8,128)(2,1)S(1)} %get-tuple-element.59), channel_id=1, source_target_pairs={{0,8},{4,12},{8,0},{12,4},{1,9},{5,13},{9,1},{13,5},{2,10},{6,14},... | collective-permute-start | bytes 294920 | tf_op jit(solution)/shard_map/ppermute | solution.py:415
  36.9 0.7 %combine.5 = (bf16[2,64,512]{2,1,0:T(8,128)(2,1)S(1)}, bf16[2,64,512]{2,1,0:T(8,128)(2,1)S(1)}) custom-call(s32[4,1]{1,0:T(4,128)S(1)} %copy.15.owners, bf16[4,64,512]{2,1,0:T(8,128)(2,1)S(1)} %copy-done.2, bf16[256,128]{1,0:T(8,128)(2,1)S(1)} %get-tuple-element.55.refs_0_, bf16[256,384]{1,0:T(8,128)(2,1)S(1)} %get-tuple-element.53.refs_0_.refs_1_, ...), custom_call_target="tpu_custom_call" | custom-call | flops 7864320000 | bytes 209715200 | tf_op jit(solution)/shard_map/combine/pallas_call | solution.py:370
  37.6 1.5 %collective-permute-start.12 = (bf16[2,64,512]{2,1,0:T(8,128)(2,1)S(1)}, bf16[2,64,512]{2,1,0:T(8,128)(2,1)S(1)}, u32[]{:S(2)}, u32[]{:S(2)}) collective-permute-start(bf16[2,64,512]{2,1,0:T(8,128)(2,1)S(1)} %get-tuple-element.62), channel_id=1, source_target_pairs={{0,4},{4,0},{8,12},{12,8},{1,5},{5,1},{9,13},{13,9},{2,6},{6,2},{1... | collective-permute-start | bytes 393224 | tf_op jit(solution)/shard_map/ppermute | solution.py:415
  39.1 1.3 %collective-permute-start.11 = (bf16[2,64,384]{2,1,0:T(8,128)(2,1)S(1)}, bf16[2,64,384]{2,1,0:T(8,128)(2,1)S(1)}, u32[]{:S(2)}, u32[]{:S(2)}) collective-permute-start(bf16[2,64,384]{2,1,0:T(8,128)(2,1)S(1)} %get-tuple-element.60), channel_id=1, source_target_pairs={{0,12},{4,8},{8,4},{12,0},{1,13},{5,9},{9,5},{13,1},{2,14},{6,10},... | collective-permute-start | bytes 294920 | tf_op jit(solution)/shard_map/ppermute | solution.py:415
  40.5 0.0 collective-permute-done.13.refs_0_
  40.5 0.0 collective-permute-done.14.refs_1_
  40.5 0.6 %place.2.refs_4_ = bf16[8,64,512]{2,1,0:T(8,128)(2,1)} custom-call(bf16[2,64,128]{2,1,0:T(8,128)(2,1)S(1)} %collective-permute-done.13.refs_0_, bf16[2,64,128]{2,1,0:T(8,128)(2,1)S(1)} %collective-permute-done.14.refs_1_), custom_call_target="tpu_custom_call" | custom-call | flops 13107200000 | tf_op jit(solution)/shard_map/place/pallas_call | solution.py:399
  41.1 2.4 %collective-permute-done.10.refs_0_ = bf16[2,64,384]{2,1,0:T(8,128)(2,1)S(1)} collective-permute-done((bf16[2,64,384]{2,1,0:T(8,128)(2,1)S(1)}, bf16[2,64,384]{2,1,0:T(8,128)(2,1)S(1)}, u32[]{:S(2)}, u32[]{:S(2)}) %collective-permute-start.10) | collective-permute-done | bytes 98336 | tf_op jit(solution)/shard_map/ppermute | solution.py:415
  43.5 2.4 %collective-permute-done.11.refs_1_ = bf16[2,64,384]{2,1,0:T(8,128)(2,1)S(1)} collective-permute-done((bf16[2,64,384]{2,1,0:T(8,128)(2,1)S(1)}, bf16[2,64,384]{2,1,0:T(8,128)(2,1)S(1)}, u32[]{:S(2)}, u32[]{:S(2)}) %collective-permute-start.11) | collective-permute-done | bytes 98336 | tf_op jit(solution)/shard_map/ppermute | solution.py:415
  45.9 0.3 collective-permute-done.12.refs_2_
  46.2 0.8 %place.3 = bf16[8,64,512]{2,1,0:T(8,128)(2,1)} custom-call(bf16[2,64,384]{2,1,0:T(8,128)(2,1)S(1)} %collective-permute-done.10.refs_0_, bf16[2,64,384]{2,1,0:T(8,128)(2,1)S(1)} %collective-permute-done.11.refs_1_, bf16[2,64,512]{2,1,0:T(8,128)(2,1)S(1)} %collective-permute-done.12.refs_2_, ...), custom_call_target="tpu_custom_call", output_to_operand_aliasing={{}: (4, {})} | custom-call | flops 91750400000 | tf_op jit(solution)/shard_map/place/pallas_call | solution.py:399
Async XLA Ops:
  0.9 11.6 %collective-permute-start.1 = (bf16[64,1024]{1,0:T(8,128)(2,1)S(1)}, bf16[64,1024]{1,0:T(8,128)(2,1)S(1)}, u32[]{:S(2)}, u32[]{:S(2)}) collective-permute-start(bf16[64,1024]{1,0:T(8,128)(2,1)S(1)} %pick.1), channel_id=1, source_target_pairs={{0,8},{4,12},{8,0},{12,4},{1,9},{5,13},{9,1},{13,5},{2,10},{6,14},... | collective-permute-start | bytes 393224 | tf_op jit(solution)/shard_map/ppermute | solution.py:415
  5.0 8.7 %collective-permute-start = (bf16[256,512]{1,0:T(8,128)(2,1)}, bf16[256,512]{1,0:T(8,128)(2,1)S(1)}, u32[]{:S(2)}, u32[]{:S(2)}) collective-permute-start(bf16[256,512]{1,0:T(8,128)(2,1)} %bitcast.8), channel_id=1, source_target_pairs={{0,2},{2,0},{1,3},{3,1},{4,6},{6,4},{5,7},{7,5},{8,10},{10,8},{9,1... | collective-permute-start | bytes 786440 | tf_op jit(solution)/shard_map/ppermute | solution.py:419
  6.5 12.2 %collective-permute-start.3 = (bf16[128,1024]{1,0:T(8,128)(2,1)}, bf16[128,1024]{1,0:T(8,128)(2,1)S(1)}, u32[]{:S(2)}, u32[]{:S(2)}) collective-permute-start(bf16[128,1024]{1,0:T(8,128)(2,1)} %mesh.1), channel_id=1, source_target_pairs={{0,4},{4,0},{8,12},{12,8},{1,5},{5,1},{9,13},{13,9},{2,6},{6,2},{1... | collective-permute-start | bytes 786440 | tf_op jit(solution)/shard_map/ppermute | solution.py:415
  12.2 7.8 %collective-permute-start.5 = (bf16[64,1024]{1,0:T(8,128)(2,1)S(1)}, bf16[64,1024]{1,0:T(8,128)(2,1)S(1)}, u32[]{:S(2)}, u32[]{:S(2)}) collective-permute-start(bf16[64,1024]{1,0:T(8,128)(2,1)S(1)} %get-tuple-element.43), channel_id=1, source_target_pairs={{0,12},{4,8},{8,4},{12,0},{1,13},{5,9},{9,5},{13,1},{2,14},{6,10},... | collective-permute-start | bytes 393224 | tf_op jit(solution)/shard_map/ppermute | solution.py:415
  12.5 5.0 %collective-permute-start.2 = (bf16[64,1024]{1,0:T(8,128)(2,1)S(1)}, bf16[64,1024]{1,0:T(8,128)(2,1)S(1)}, u32[]{:S(2)}, u32[]{:S(2)}) collective-permute-start(bf16[64,1024]{1,0:T(8,128)(2,1)S(1)} %collective-permute-done.1.refs_2_), channel_id=1, source_target_pairs={{0,2},{2,0},{1,3},{3,1},{4,6},{6,4},{5,7},{7,5},{8,10},{10,8},{9,1... | collective-permute-start | bytes 393224 | tf_op jit(solution)/shard_map/ppermute | solution.py:419
  13.0 8.5 %collective-permute-start.4 = (bf16[64,1024]{1,0:T(8,128)(2,1)S(1)}, bf16[64,1024]{1,0:T(8,128)(2,1)S(1)}, u32[]{:S(2)}, u32[]{:S(2)}) collective-permute-start(bf16[64,1024]{1,0:T(8,128)(2,1)S(1)} %collective-permute-done.1.refs_2_), channel_id=1, source_target_pairs={{0,4},{4,0},{8,12},{12,8},{1,5},{5,1},{9,13},{13,9},{2,6},{6,2},{1... | collective-permute-start | bytes 393224 | tf_op jit(solution)/shard_map/ppermute | solution.py:415
  13.7 5.0 %copy-start = (bf16[1024,512]{1,0:T(8,128)(2,1)S(1)}, bf16[1024,512]{1,0:T(8,128)(2,1)}, u32[]{:S(2)}) copy-start(bf16[1024,512]{1,0:T(8,128)(2,1)} %refs_4_.3) | copy-start | bytes 3145732
  13.7 5.0 %copy-start.1 = (bf16[1024,512]{1,0:T(8,128)(2,1)S(1)}, bf16[1024,512]{1,0:T(8,128)(2,1)}, u32[]{:S(2)}) copy-start(bf16[1024,512]{1,0:T(8,128)(2,1)} %refs_5_.3) | copy-start | bytes 3145732
  19.7 3.6 %collective-permute-start.7 = (bf16[384,1024]{1,0:T(8,128)(2,1)S(1)}, bf16[384,1024]{1,0:T(8,128)(2,1)S(1)}, u32[]{:S(2)}, u32[]{:S(2)}) collective-permute-start(bf16[384,1024]{1,0:T(8,128)(2,1)S(1)} %project.3), channel_id=1, source_target_pairs={{0,1},{1,0},{2,3},{3,2},{4,5},{5,4},{6,7},{7,6},{8,9},{9,8},{10,11... | collective-permute-start | bytes 2359304 | tf_op jit(solution)/shard_map/ppermute | solution.py:419
  21.9 1.6 %copy-start.3 = (s32[4,8]{1,0:T(4,128)S(1)}, s32[4,8]{1,0:T(4,128)}, u32[]{:S(2)}) copy-start(s32[4,8]{1,0:T(4,128)} %adjacency.1) | copy-start | bytes 388
  21.9 1.6 %collective-permute-start.6 = (bf16[128,1024]{1,0:T(8,128)(2,1)S(1)}, bf16[128,1024]{1,0:T(8,128)(2,1)S(1)}, u32[]{:S(2)}, u32[]{:S(2)}) collective-permute-start(bf16[128,1024]{1,0:T(8,128)(2,1)S(1)} %project.2), channel_id=1, source_target_pairs={{0,1},{1,0},{2,3},{3,2},{4,5},{5,4},{6,7},{7,6},{8,9},{9,8},{10,11... | collective-permute-start | bytes 786440 | tf_op jit(solution)/shard_map/ppermute | solution.py:419
  26.0 5.0 %collective-permute-start.9 = (bf16[256,128]{1,0:T(8,128)(2,1)S(1)}, bf16[256,128]{1,0:T(8,128)(2,1)S(1)}, u32[]{:S(2)}, u32[]{:S(2)}) collective-permute-start(bf16[256,128]{1,0:T(8,128)(2,1)S(1)} %get-tuple-element.56), channel_id=1, source_target_pairs={{0,2},{2,0},{1,3},{3,1},{4,6},{6,4},{5,7},{7,5},{8,10},{10,8},{9,1... | collective-permute-start | bytes 196616 | tf_op jit(solution)/shard_map/ppermute | solution.py:419
  26.6 1.9 %copy-start.4 = (s32[4,1]{0,1:T(1,128)S(1)}, s32[4,1]{0,1:T(1,128)}, u32[]{:S(2)}) copy-start(s32[4,1]{0,1:T(1,128)} %param.12) | copy-start | bytes 52
  26.6 4.3 %copy-start.2 = (bf16[4,64,512]{2,1,0:T(8,128)(2,1)S(1)}, bf16[4,64,512]{2,1,0:T(8,128)(2,1)}, u32[]{:S(2)}) copy-start(bf16[4,64,512]{2,1,0:T(8,128)(2,1)} %grid_features.5) | copy-start | bytes 786436
  27.1 7.5 %collective-permute-start.8 = (bf16[256,384]{1,0:T(8,128)(2,1)S(1)}, bf16[256,384]{1,0:T(8,128)(2,1)S(1)}, u32[]{:S(2)}, u32[]{:S(2)}) collective-permute-start(bf16[256,384]{1,0:T(8,128)(2,1)S(1)} %get-tuple-element.54), channel_id=1, source_target_pairs={{0,2},{2,0},{1,3},{3,1},{4,6},{6,4},{5,7},{7,5},{8,10},{10,8},{9,1... | collective-permute-start | bytes 589832 | tf_op jit(solution)/shard_map/ppermute | solution.py:419
  31.6 8.9 %collective-permute-start.13 = (bf16[2,64,128]{2,1,0:T(8,128)(2,1)S(1)}, bf16[2,64,128]{2,1,0:T(8,128)(2,1)S(1)}, u32[]{:S(2)}, u32[]{:S(2)}) collective-permute-start(bf16[2,64,128]{2,1,0:T(8,128)(2,1)S(1)} %get-tuple-element.57), channel_id=1, source_target_pairs={{0,8},{4,12},{8,0},{12,4},{1,9},{5,13},{9,1},{13,5},{2,10},{6,14},... | collective-permute-start | bytes 98312 | tf_op jit(solution)/shard_map/ppermute | solution.py:415
  31.8 8.7 %collective-permute-start.14 = (bf16[2,64,128]{2,1,0:T(8,128)(2,1)S(1)}, bf16[2,64,128]{2,1,0:T(8,128)(2,1)S(1)}, u32[]{:S(2)}, u32[]{:S(2)}) collective-permute-start(bf16[2,64,128]{2,1,0:T(8,128)(2,1)S(1)} %get-tuple-element.64), channel_id=1, source_target_pairs={{0,12},{4,8},{8,4},{12,0},{1,13},{5,9},{9,5},{13,1},{2,14},{6,10},... | collective-permute-start | bytes 98312 | tf_op jit(solution)/shard_map/ppermute | solution.py:415
  35.3 8.2 %collective-permute-start.10 = (bf16[2,64,384]{2,1,0:T(8,128)(2,1)S(1)}, bf16[2,64,384]{2,1,0:T(8,128)(2,1)S(1)}, u32[]{:S(2)}, u32[]{:S(2)}) collective-permute-start(bf16[2,64,384]{2,1,0:T(8,128)(2,1)S(1)} %get-tuple-element.59), channel_id=1, source_target_pairs={{0,8},{4,12},{8,0},{12,4},{1,9},{5,13},{9,1},{13,5},{2,10},{6,14},... | collective-permute-start | bytes 294920 | tf_op jit(solution)/shard_map/ppermute | solution.py:415
  37.6 8.6 %collective-permute-start.12 = (bf16[2,64,512]{2,1,0:T(8,128)(2,1)S(1)}, bf16[2,64,512]{2,1,0:T(8,128)(2,1)S(1)}, u32[]{:S(2)}, u32[]{:S(2)}) collective-permute-start(bf16[2,64,512]{2,1,0:T(8,128)(2,1)S(1)} %get-tuple-element.62), channel_id=1, source_target_pairs={{0,4},{4,0},{8,12},{12,8},{1,5},{5,1},{9,13},{13,9},{2,6},{6,2},{1... | collective-permute-start | bytes 393224 | tf_op jit(solution)/shard_map/ppermute | solution.py:415
  39.1 6.8 %collective-permute-start.11 = (bf16[2,64,384]{2,1,0:T(8,128)(2,1)S(1)}, bf16[2,64,384]{2,1,0:T(8,128)(2,1)S(1)}, u32[]{:S(2)}, u32[]{:S(2)}) collective-permute-start(bf16[2,64,384]{2,1,0:T(8,128)(2,1)S(1)} %get-tuple-element.60), channel_id=1, source_target_pairs={{0,12},{4,8},{8,4},{12,0},{1,13},{5,9},{9,5},{13,1},{2,14},{6,10},... | collective-permute-start | bytes 294920 | tf_op jit(solution)/shard_map/ppermute | solution.py:415

commit v14 on v13

--- a/solution.py
+++ b/solution.py
@@ -228,9 +228,16 @@
 def project_out(c, att, mlp, wo, send, keep):
     half = att.shape[1]
     chunk = columns_of(c)
-    for out, first in ((send, 0), (keep, half)):
-        span = slice(first + chunk.start, first + chunk.stop)
-        out[...] = (mlp[:, span] + dot(att[...], wo[:, span])).astype(jnp.bfloat16)
+    h = lax.axis_index("head")
+
+    def write(head):
+        for out, first, place in ((send, 0, 1 - head), (keep, half, head)):
+            extra = mlp[:, first + chunk.start : first + chunk.stop]
+            span = slice(place * half + chunk.start, place * half + chunk.stop)
+            out[...] = (extra + dot(att[...], wo[:, span])).astype(jnp.bfloat16)
+
+    for head in range(2):
+        pl.when(h == head)(functools.partial(write, head))
 
 
 def attend_kernel(
@@ -258,7 +265,7 @@
             part = lax.rem(m, 2)
             core = lax.rem(m // 2, 2)
             distance = s ^ (m // 4)
-            part = jnp.where(distance <= 1, part, part ^ h)
+            part = jnp.where(distance == 0, part, part ^ h)
             places[b].append((core ^ u, distance * 2 + part))
 
     def scores_of(step):
@@ -313,7 +320,7 @@
             transcendentals=rows * 8 * BLOCK * half // HEAD_DIM,
         ),
         name="attend",
-    )(adjacency, q, mine, sibling, table, mlp, wo)
+    )(adjacency, q, mine, sibling, table, mlp, in_vmem(wo))
     return send, keep, att
 
 
@@ -332,7 +339,7 @@
             transcendentals=0,
         ),
         name="project_out",
-    )(att, mlp, wo)
+    )(att, mlp, in_vmem(wo))
 
 
 def combine_kernel(chunks, distances, owners, grid_features, *refs):
@@ -437,8 +444,7 @@
     flat = grid_features.reshape(count * rows, half)
     half_unit = run_pick(mesh_nodes)
     far = crossed(half_unit, 2, shards)
-    waiting, _ = lax.optimization_barrier((mesh_nodes, half_unit))
-    near = crossed(waiting, 1, shards)
+    near = crossed(half_unit, 1, shards)
     waiting, _ = lax.optimization_barrier((flat, half_unit))
     other = swapped(waiting, "head")
     flat, gain, wq, wup, wdn, mesh, rest = run_stage(
@@ -454,27 +460,27 @@
         (None, 1, 0, 0, 1, None, "rest"),
     )
     straight = crossed(rest, 3, shards)
-    far, _ = lax.optimization_barrier((far, rest))
+    near, _ = lax.optimization_barrier((near, rest))
+    near_pair = swapped(near, "head")
+    far, _, _ = lax.optimization_barrier((far, near, rest))
     farther = crossed(far, 1, shards)
     far_pair = swapped(far, "head")
     queries, mlp = run_mlp(flat, other, gain, wq, wup, wdn)
-    queries, mlp, far_pair, near = lax.optimization_barrier((queries, mlp, far_pair, near))
+    queries, mlp, far_pair = lax.optimization_barrier((queries, mlp, far_pair))
     blocked = (-1, BLOCK, 2 * half)
-    mine_a = run_project((mesh, near, far, far_pair), key_weight, value_weight)
+    mine_a = run_project((mesh, near, near_pair, far, far_pair), key_weight, value_weight)
     sibling_a = swapped(mine_a, "sub")
-    unstaged, _ = lax.optimization_barrier((output_weight, mine_a))
-    (wo,) = run_stage((unstaged,), (1,))
     table = run_table(mine_a.reshape(blocked), sibling_a.reshape(blocked), 2 * shards)
     mine_b = run_project((farther, straight), key_weight, value_weight)
     sibling_b = swapped(mine_b, "sub")
     send, keep, att = run_attend(
-        adjacency, queries, mine_b.reshape(blocked), sibling_b.reshape(blocked), table, mlp, wo
+        adjacency, queries, mine_b.reshape(blocked), sibling_b.reshape(blocked), table, mlp, output_weight
     )
     keeps, swaps, slots, placed = [], [], [], []
     shape = (shards * CAP, rows, half)
     for c in range(len(WIDTHS)):
         if c > 0:
-            send, keep = run_project_out(c, att, mlp, wo)
+            send, keep = run_project_out(c, att, mlp, output_weight)
         received = swapped(send, "head")
         if c > 0:
             received, _ = lax.optimization_barrier((received, slots[c - 1][0]))

time: 47.1 us -> 49.4 us (1.049)
  starting transfers between devices: 18.1 us -> 23.5 us
  waiting for transfers between devices: 11.2 us -> 9.21 us
  Pallas kernels: 17.3 us -> 16.2 us
    ppermute x9, starting transfers between devices: 13.8 us -> 17.2 us  [crossed(): return lax.ppermute(x, 'shard', [(i, i ^ distance) for i in range(size)])]
    ppermute x9, waiting for transfers between devices: 8 us -> 5.77 us  [crossed(): return lax.ppermute(x, 'shard', [(i, i ^ distance) for i in range(size)])]
    ppermute x6 -> x7, starting transfers between devices: 4.27 us -> 6.28 us  [swapped(): return lax.ppermute(x, axis, [(0, 1), (1, 0)])]
    pallas_call x2 -> x1, Pallas kernels: 5.33 us -> 4.1 us  [run_stage(): pl.pallas_call(functools.partial(stage_kernel, axes), out_shape=tuple((ja...]
    ppermute x6 -> x7, waiting for transfers between devices: 3.24 us -> 3.44 us  [swapped(): return lax.ppermute(x, axis, [(0, 1), (1, 0)])]
  transfers between devices with their start and end apart: 15 -> 16, of which waited for: 10 -> 5; matrix products, arithmetic and copies ran while one was open for 0% -> 0% of each run, Pallas kernels for 28% -> 24%
where the time goes in v14:
time: 49.4 us; the launch traced here: 49.2 us
  starting transfers between devices  23.5 us (48%)
  Pallas kernels  16.2 us (33%)
  waiting for transfers between devices  9.21 us (19%)
    ppermute x9, starting transfers between devices, crossed(): return lax.ppermute(x, 'shard', [(i, i ^ distance) for i in range(size)])  17.2 us
    ppermute x7, starting transfers between devices, swapped(): return lax.ppermute(x, axis, [(0, 1), (1, 0)])  6.28 us
    ppermute x9, waiting for transfers between devices, crossed(): return lax.ppermute(x, 'shard', [(i, i ^ distance) for i in range(size)])  5.77 us
    pallas_call x1, Pallas kernels, run_stage(): pl.pallas_call(functools.partial(stage_kernel, axes), out_shape=tuple((ja...  4.1 us
    ppermute x7, waiting for transfers between devices, swapped(): return lax.ppermute(x, axis, [(0, 1), (1, 0)])  3.44 us
    pallas_call x1, Pallas kernels, run_mlp(): pl.pallas_call(mlp_kernel, out_shape=(jax.ShapeDtypeStruct((rows, wq.shap...  3.33 us
    pallas_call x1, Pallas kernels, run_attend(): pl.pallas_call(attend_kernel, out_shape=(part, part, jax.ShapeDtypeStruct...  2.52 us
    pallas_call x3, Pallas kernels, run_combine(): pl.pallas_call(functools.partial(combine_kernel, chunks, distances), out_...  1.95 us
  transfers between devices with their start and end apart: 16, of which 5 were waited for; matrix products, arithmetic and copies ran while one was open for 0% of the time, Pallas kernels for 24%

profile of v14, /device:TPU:0, one launch (start us, length us, event | category | flops | bytes accessed | tf_op | source)
XLA Modules:
  0.0 49.2 jit_solution(1569785442625202937)
XLA Ops:
  0.0 0.9 %pick.1 = bf16[64,1024]{1,0:T(8,128)(2,1)S(1)} custom-call(bf16[128,1024]{1,0:T(8,128)(2,1)} %mesh.1), custom_call_target="tpu_custom_call" | custom-call | bytes 524288 | tf_op jit(solution)/shard_map/pick/pallas_call | solution.py:112
  0.9 3.1 %collective-permute-start.2 = (bf16[64,1024]{1,0:T(8,128)(2,1)S(1)}, bf16[64,1024]{1,0:T(8,128)(2,1)S(1)}, u32[]{:S(2)}, u32[]{:S(2)}) collective-permute-start(bf16[64,1024]{1,0:T(8,128)(2,1)S(1)} %pick.1), channel_id=1, source_target_pairs={{0,4},{4,0},{8,12},{12,8},{1,5},{5,1},{9,13},{13,9},{2,6},{6,2},{1... | collective-permute-start | bytes 393224 | tf_op jit(solution)/shard_map/ppermute | solution.py:422
  4.0 2.6 %collective-permute-start.1 = (bf16[64,1024]{1,0:T(8,128)(2,1)S(1)}, bf16[64,1024]{1,0:T(8,128)(2,1)S(1)}, u32[]{:S(2)}, u32[]{:S(2)}) collective-permute-start(bf16[64,1024]{1,0:T(8,128)(2,1)S(1)} %pick.1), channel_id=1, source_target_pairs={{0,8},{4,12},{8,0},{12,4},{1,9},{5,13},{9,1},{13,5},{2,10},{6,14},... | collective-permute-start | bytes 393224 | tf_op jit(solution)/shard_map/ppermute | solution.py:422
  6.6 1.5 %collective-permute-start = (bf16[256,512]{1,0:T(8,128)(2,1)}, bf16[256,512]{1,0:T(8,128)(2,1)S(1)}, u32[]{:S(2)}, u32[]{:S(2)}) collective-permute-start(bf16[256,512]{1,0:T(8,128)(2,1)} %bitcast.8), channel_id=1, source_target_pairs={{0,2},{2,0},{1,3},{3,1},{4,6},{6,4},{5,7},{7,5},{8,10},{10,8},{9,1... | collective-permute-start | bytes 786440 | tf_op jit(solution)/shard_map/ppermute | solution.py:426
  8.1 4.1 %stage.1 = (bf16[256,512]{1,0:T(8,128)(2,1)S(1)}, f32[1,1024]{1,0:T(1,128)S(1)}, bf16[1024,512]{1,0:T(8,128)(2,1)S(1)}, bf16[1024,2048]{1,0:T(8,128)(2,1)S(1)}, ...) custom-call(bf16[256,512]{1,0:T(8,128)(2,1)} %bitcast.9, ...), custom_call_target="tpu_custom_call" | custom-call | flops 20451328000 | bytes 204513280 | tf_op jit(solution)/shard_map/stage/pallas_call | solution.py:162
  12.2 0.3 collective-permute-start.5
  12.5 0.0 collective-permute-done.2.refs_1_
  12.5 0.4 collective-permute-start.7
  12.9 0.0 collective-permute-done.1.refs_3_
  12.9 1.6 %collective-permute-start.3 = (bf16[64,1024]{1,0:T(8,128)(2,1)S(1)}, bf16[64,1024]{1,0:T(8,128)(2,1)S(1)}, u32[]{:S(2)}, u32[]{:S(2)}) collective-permute-start(bf16[64,1024]{1,0:T(8,128)(2,1)S(1)} %collective-permute-done.1.refs_3_), channel_id=1, source_target_pairs={{0,2},{2,0},{1,3},{3,1},{4,6},{6,4},{5,7},{7,5},{8,10},{10,8},{9,1... | collective-permute-start | bytes 393224 | tf_op jit(solution)/shard_map/ppermute | solution.py:426
  14.5 2.4 %collective-permute-start.4 = (bf16[64,1024]{1,0:T(8,128)(2,1)S(1)}, bf16[64,1024]{1,0:T(8,128)(2,1)S(1)}, u32[]{:S(2)}, u32[]{:S(2)}) collective-permute-start(bf16[64,1024]{1,0:T(8,128)(2,1)S(1)} %collective-permute-done.1.refs_3_), channel_id=1, source_target_pairs={{0,4},{4,0},{8,12},{12,8},{1,5},{5,1},{9,13},{13,9},{2,6},{6,2},{1... | collective-permute-start | bytes 393224 | tf_op jit(solution)/shard_map/ppermute | solution.py:422
  16.9 0.0 collective-permute-done.other
  16.9 0.0 copy-start
  16.9 0.0 copy-start.1
  16.9 3.3 %mlp.1 = (bf16[256,512]{1,0:T(8,128)(2,1)S(1)}, f32[256,1024]{1,0:T(8,128)S(1)}) custom-call(bf16[256,512]{1,0:T(8,128)(2,1)S(1)} %get-tuple-element.33.own, bf16[256,512]{1,0:T(8,128)(2,1)S(1)} %collective-permute-done.other, f32[1,1024]{1,0:T(1,128)S(1)} %get-tuple-element.35.gain, bf16[1024,512]{1,0:T(8,128)(2,1)S(1)} %get-tuple-element.36.wq, ...), custom_call_target="tpu_custom_call" | custom-call | flops 2415919104 | bytes 9437184 | tf_op jit(solution)/shard_map/mlp/pallas_call | solution.py:85
  20.3 0.0 collective-permute-done.3.refs_4_
  20.3 0.0 collective-permute-done.7.refs_2_
  20.3 0.0 copy-done
  20.3 0.0 copy-done.1
  20.3 1.0 %project.3 = bf16[384,1024]{1,0:T(8,128)(2,1)S(1)} custom-call(bf16[128,1024]{1,0:T(8,128)(2,1)S(1)} %get-tuple-element.45.refs_0_, bf16[64,1024]{1,0:T(8,128)(2,1)S(1)} %collective-permute-done.2.refs_1_, bf16[64,1024]{1,0:T(8,128)(2,1)S(1)} %collective-permute-done.7.refs_2_, bf16[64,1024]{1,0:T(8,128)(2,1)S(1)} %collective-permute-done.1.refs_3_, ...), custom_call_target="tpu_custom_call" | custom-call | flops 60397977600 | bytes 275251200 | tf_op jit(solution)/shard_map/project/pallas_call | solution.py:190
  21.3 0.0 copy-start.2
  21.3 0.0 copy-start.4
  21.3 0.1 collective-permute-start.8
  21.4 0.0 collective-permute-done.5.refs_1_
  21.4 0.0 collective-permute-done.4.refs_0_
  21.4 0.4 project.2
  21.9 0.5 %collective-permute-start.6 = (bf16[128,1024]{1,0:T(8,128)(2,1)S(1)}, bf16[128,1024]{1,0:T(8,128)(2,1)S(1)}, u32[]{:S(2)}, u32[]{:S(2)}) collective-permute-start(bf16[128,1024]{1,0:T(8,128)(2,1)S(1)} %project.2), channel_id=1, source_target_pairs={{0,1},{1,0},{2,3},{3,2},{4,5},{5,4},{6,7},{7,6},{8,9},{9,8},{10,11... | collective-permute-start | bytes 786440 | tf_op jit(solution)/shard_map/ppermute | solution.py:426
  22.4 1.3 %collective-permute-done.8 = bf16[384,1024]{1,0:T(8,128)(2,1)S(1)} collective-permute-done((bf16[384,1024]{1,0:T(8,128)(2,1)S(1)}, bf16[384,1024]{1,0:T(8,128)(2,1)S(1)}, u32[]{:S(2)}, u32[]{:S(2)}) %collective-permute-start.8) | collective-permute-done | bytes 786464 | tf_op jit(solution)/shard_map/ppermute | solution.py:426
  23.7 0.1 table.1.table_in
  23.8 0.3 collective-permute-done.6
  24.1 0.0 copy-done.2
  24.1 0.0 copy-done.4
  24.1 2.5 %attend.1 = (bf16[256,128]{1,0:T(8,128)(2,1)S(1)}, bf16[256,128]{1,0:T(8,128)(2,1)S(1)}, bf16[256,512]{1,0:T(8,128)(2,1)S(1)}, bf16[2,8,64,1024]{3,2,1,0:T(8,128)(2,1)S(1)}) custom-call(s32[4,8]{1,0:T(4,128)S(1)} %copy-done.4, bf16[256,512]{1,0:T(8,128)(2,1)S(1)} %get-tuple-element.44.q, ...), custom_call_target="tpu_custom_call", output_to_operand_aliasing={{3}: (4, {})} | custom-call | flops 13421772800 | bytes 41943040 | tf_op jit(solution)/shard_map/attend/pallas_call | solution.py:305
  26.6 1.2 %collective-permute-start.10 = (bf16[256,128]{1,0:T(8,128)(2,1)S(1)}, bf16[256,128]{1,0:T(8,128)(2,1)S(1)}, u32[]{:S(2)}, u32[]{:S(2)}) collective-permute-start(bf16[256,128]{1,0:T(8,128)(2,1)S(1)} %get-tuple-element.52), channel_id=1, source_target_pairs={{0,2},{2,0},{1,3},{3,1},{4,6},{6,4},{5,7},{7,5},{8,10},{10,8},{9,1... | collective-permute-start | bytes 196616 | tf_op jit(solution)/shard_map/ppermute | solution.py:426
  27.8 0.0 copy-start.5
  27.8 0.0 copy-start.3
  27.8 0.4 project_out.1
  28.2 1.0 %collective-permute-start.9 = (bf16[256,384]{1,0:T(8,128)(2,1)S(1)}, bf16[256,384]{1,0:T(8,128)(2,1)S(1)}, u32[]{:S(2)}, u32[]{:S(2)}) collective-permute-start(bf16[256,384]{1,0:T(8,128)(2,1)S(1)} %get-tuple-element.50), channel_id=1, source_target_pairs={{0,2},{2,0},{1,3},{3,1},{4,6},{6,4},{5,7},{7,5},{8,10},{10,8},{9,1... | collective-permute-start | bytes 589832 | tf_op jit(solution)/shard_map/ppermute | solution.py:426
  29.2 0.0 copy-done.5
  29.2 0.1 copy.15.owners
  29.3 1.9 %collective-permute-done.10.refs_1_.refs_2_ = bf16[256,128]{1,0:T(8,128)(2,1)S(1)} collective-permute-done((bf16[256,128]{1,0:T(8,128)(2,1)S(1)}, bf16[256,128]{1,0:T(8,128)(2,1)S(1)}, u32[]{:S(2)}, u32[]{:S(2)}) %collective-permute-start.10) | collective-permute-done | bytes 65568 | tf_op jit(solution)/shard_map/ppermute | solution.py:426
  31.2 0.0 copy-done.3
  31.2 0.6 %combine.3 = (bf16[2,64,128]{2,1,0:T(8,128)(2,1)S(1)}, bf16[2,64,128]{2,1,0:T(8,128)(2,1)S(1)}) custom-call(s32[4,1]{1,0:T(4,128)S(1)} %copy.15.owners, bf16[4,64,512]{2,1,0:T(8,128)(2,1)S(1)} %copy-done.3, bf16[256,128]{1,0:T(8,128)(2,1)S(1)} %get-tuple-element.51.refs_0_, bf16[256,128]{1,0:T(8,128)(2,1)S(1)} %collective-permute-done.10.refs_1_.refs_2_), custom_call_target="tpu_custom_call" | custom-call | flops 1966080000 | bytes 52428800 | tf_op jit(solution)/shard_map/combine/pallas_call | solution.py:377
  31.8 4.3 %collective-permute-start.14 = (bf16[2,64,128]{2,1,0:T(8,128)(2,1)S(1)}, bf16[2,64,128]{2,1,0:T(8,128)(2,1)S(1)}, u32[]{:S(2)}, u32[]{:S(2)}) collective-permute-start(bf16[2,64,128]{2,1,0:T(8,128)(2,1)S(1)} %get-tuple-element.53), channel_id=1, source_target_pairs={{0,8},{4,12},{8,0},{12,4},{1,9},{5,13},{9,1},{13,5},{2,10},{6,14},... | collective-permute-start | bytes 98312 | tf_op jit(solution)/shard_map/ppermute | solution.py:422
  36.2 0.0 collective-permute-start.15
  36.2 0.0 collective-permute-done.9.refs_1_.refs_3_
  36.2 0.7 %combine.4 = (bf16[2,64,384]{2,1,0:T(8,128)(2,1)S(1)}, bf16[2,64,384]{2,1,0:T(8,128)(2,1)S(1)}) custom-call(s32[4,1]{1,0:T(4,128)S(1)} %copy.15.owners, bf16[4,64,512]{2,1,0:T(8,128)(2,1)S(1)} %copy-done.3, bf16[256,384]{1,0:T(8,128)(2,1)S(1)} %get-tuple-element.49.refs_0_.refs_1_, bf16[256,384]{1,0:T(8,128)(2,1)S(1)} %collective-permute-done.9.refs_1_.refs_3_), custom_call_target="tpu_custom_call" | custom-call | flops 5898240000 | bytes 157286400 | tf_op jit(solution)/shard_map/combine/pallas_call | solution.py:377
  36.8 2.8 %collective-permute-start.11 = (bf16[2,64,384]{2,1,0:T(8,128)(2,1)S(1)}, bf16[2,64,384]{2,1,0:T(8,128)(2,1)S(1)}, u32[]{:S(2)}, u32[]{:S(2)}) collective-permute-start(bf16[2,64,384]{2,1,0:T(8,128)(2,1)S(1)} %get-tuple-element.55), channel_id=1, source_target_pairs={{0,8},{4,12},{8,0},{12,4},{1,9},{5,13},{9,1},{13,5},{2,10},{6,14},... | collective-permute-start | bytes 294920 | tf_op jit(solution)/shard_map/ppermute | solution.py:422
  39.6 0.7 %combine.5 = (bf16[2,64,512]{2,1,0:T(8,128)(2,1)S(1)}, bf16[2,64,512]{2,1,0:T(8,128)(2,1)S(1)}) custom-call(s32[4,1]{1,0:T(4,128)S(1)} %copy.15.owners, bf16[4,64,512]{2,1,0:T(8,128)(2,1)S(1)} %copy-done.3, bf16[256,128]{1,0:T(8,128)(2,1)S(1)} %get-tuple-element.51.refs_0_, bf16[256,384]{1,0:T(8,128)(2,1)S(1)} %get-tuple-element.49.refs_0_.refs_1_, ...), custom_call_target="tpu_custom_call" | custom-call | flops 7864320000 | bytes 209715200 | tf_op jit(solution)/shard_map/combine/pallas_call | solution.py:377
  40.3 1.7 %collective-permute-start.13 = (bf16[2,64,512]{2,1,0:T(8,128)(2,1)S(1)}, bf16[2,64,512]{2,1,0:T(8,128)(2,1)S(1)}, u32[]{:S(2)}, u32[]{:S(2)}) collective-permute-start(bf16[2,64,512]{2,1,0:T(8,128)(2,1)S(1)} %get-tuple-element.58), channel_id=1, source_target_pairs={{0,4},{4,0},{8,12},{12,8},{1,5},{5,1},{9,13},{13,9},{2,6},{6,2},{1... | collective-permute-start | bytes 393224 | tf_op jit(solution)/shard_map/ppermute | solution.py:422
  42.0 0.0 collective-permute-start.12
  42.0 0.0 collective-permute-done.14.refs_0_
  42.0 0.0 collective-permute-done.15.refs_1_
  42.1 0.6 %place.2.refs_4_ = bf16[8,64,512]{2,1,0:T(8,128)(2,1)} custom-call(bf16[2,64,128]{2,1,0:T(8,128)(2,1)S(1)} %collective-permute-done.14.refs_0_, bf16[2,64,128]{2,1,0:T(8,128)(2,1)S(1)} %collective-permute-done.15.refs_1_), custom_call_target="tpu_custom_call" | custom-call | flops 13107200000 | tf_op jit(solution)/shard_map/place/pallas_call | solution.py:406
  42.7 1.0 %collective-permute-done.11.refs_0_ = bf16[2,64,384]{2,1,0:T(8,128)(2,1)S(1)} collective-permute-done((bf16[2,64,384]{2,1,0:T(8,128)(2,1)S(1)}, bf16[2,64,384]{2,1,0:T(8,128)(2,1)S(1)}, u32[]{:S(2)}, u32[]{:S(2)}) %collective-permute-start.11) | collective-permute-done | bytes 98336 | tf_op jit(solution)/shard_map/ppermute | solution.py:422
  43.7 4.8 %collective-permute-done.12.refs_1_ = bf16[2,64,384]{2,1,0:T(8,128)(2,1)S(1)} collective-permute-done((bf16[2,64,384]{2,1,0:T(8,128)(2,1)S(1)}, bf16[2,64,384]{2,1,0:T(8,128)(2,1)S(1)}, u32[]{:S(2)}, u32[]{:S(2)}) %collective-permute-start.12) | collective-permute-done | bytes 98336 | tf_op jit(solution)/shard_map/ppermute | solution.py:422
  48.4 0.0 collective-permute-done.13.refs_2_
  48.4 0.8 %place.3 = bf16[8,64,512]{2,1,0:T(8,128)(2,1)} custom-call(bf16[2,64,384]{2,1,0:T(8,128)(2,1)S(1)} %collective-permute-done.11.refs_0_, bf16[2,64,384]{2,1,0:T(8,128)(2,1)S(1)} %collective-permute-done.12.refs_1_, bf16[2,64,512]{2,1,0:T(8,128)(2,1)S(1)} %collective-permute-done.13.refs_2_, ...), custom_call_target="tpu_custom_call", output_to_operand_aliasing={{}: (4, {})} | custom-call | flops 91750400000 | tf_op jit(solution)/shard_map/place/pallas_call | solution.py:406
Async XLA Ops:
  0.9 11.6 %collective-permute-start.2 = (bf16[64,1024]{1,0:T(8,128)(2,1)S(1)}, bf16[64,1024]{1,0:T(8,128)(2,1)S(1)}, u32[]{:S(2)}, u32[]{:S(2)}) collective-permute-start(bf16[64,1024]{1,0:T(8,128)(2,1)S(1)} %pick.1), channel_id=1, source_target_pairs={{0,4},{4,0},{8,12},{12,8},{1,5},{5,1},{9,13},{13,9},{2,6},{6,2},{1... | collective-permute-start | bytes 393224 | tf_op jit(solution)/shard_map/ppermute | solution.py:422
  4.0 8.9 %collective-permute-start.1 = (bf16[64,1024]{1,0:T(8,128)(2,1)S(1)}, bf16[64,1024]{1,0:T(8,128)(2,1)S(1)}, u32[]{:S(2)}, u32[]{:S(2)}) collective-permute-start(bf16[64,1024]{1,0:T(8,128)(2,1)S(1)} %pick.1), channel_id=1, source_target_pairs={{0,8},{4,12},{8,0},{12,4},{1,9},{5,13},{9,1},{13,5},{2,10},{6,14},... | collective-permute-start | bytes 393224 | tf_op jit(solution)/shard_map/ppermute | solution.py:422
  6.6 10.3 %collective-permute-start = (bf16[256,512]{1,0:T(8,128)(2,1)}, bf16[256,512]{1,0:T(8,128)(2,1)S(1)}, u32[]{:S(2)}, u32[]{:S(2)}) collective-permute-start(bf16[256,512]{1,0:T(8,128)(2,1)} %bitcast.8), channel_id=1, source_target_pairs={{0,2},{2,0},{1,3},{3,1},{4,6},{6,4},{5,7},{7,5},{8,10},{10,8},{9,1... | collective-permute-start | bytes 786440 | tf_op jit(solution)/shard_map/ppermute | solution.py:426
  12.2 9.2 %collective-permute-start.5 = (bf16[64,1024]{1,0:T(8,128)(2,1)S(1)}, bf16[64,1024]{1,0:T(8,128)(2,1)S(1)}, u32[]{:S(2)}, u32[]{:S(2)}) collective-permute-start(bf16[64,1024]{1,0:T(8,128)(2,1)S(1)} %get-tuple-element.41), channel_id=1, source_target_pairs={{0,12},{4,8},{8,4},{12,0},{1,13},{5,9},{9,5},{13,1},{2,14},{6,10},... | collective-permute-start | bytes 393224 | tf_op jit(solution)/shard_map/ppermute | solution.py:422
  12.5 7.8 %collective-permute-start.7 = (bf16[64,1024]{1,0:T(8,128)(2,1)S(1)}, bf16[64,1024]{1,0:T(8,128)(2,1)S(1)}, u32[]{:S(2)}, u32[]{:S(2)}) collective-permute-start(bf16[64,1024]{1,0:T(8,128)(2,1)S(1)} %collective-permute-done.2.refs_1_), channel_id=1, source_target_pairs={{0,2},{2,0},{1,3},{3,1},{4,6},{6,4},{5,7},{7,5},{8,10},{10,8},{9,1... | collective-permute-start | bytes 393224 | tf_op jit(solution)/shard_map/ppermute | solution.py:426
  12.9 7.4 %collective-permute-start.3 = (bf16[64,1024]{1,0:T(8,128)(2,1)S(1)}, bf16[64,1024]{1,0:T(8,128)(2,1)S(1)}, u32[]{:S(2)}, u32[]{:S(2)}) collective-permute-start(bf16[64,1024]{1,0:T(8,128)(2,1)S(1)} %collective-permute-done.1.refs_3_), channel_id=1, source_target_pairs={{0,2},{2,0},{1,3},{3,1},{4,6},{6,4},{5,7},{7,5},{8,10},{10,8},{9,1... | collective-permute-start | bytes 393224 | tf_op jit(solution)/shard_map/ppermute | solution.py:426
  14.5 6.9 %collective-permute-start.4 = (bf16[64,1024]{1,0:T(8,128)(2,1)S(1)}, bf16[64,1024]{1,0:T(8,128)(2,1)S(1)}, u32[]{:S(2)}, u32[]{:S(2)}) collective-permute-start(bf16[64,1024]{1,0:T(8,128)(2,1)S(1)} %collective-permute-done.1.refs_3_), channel_id=1, source_target_pairs={{0,4},{4,0},{8,12},{12,8},{1,5},{5,1},{9,13},{13,9},{2,6},{6,2},{1... | collective-permute-start | bytes 393224 | tf_op jit(solution)/shard_map/ppermute | solution.py:422
  16.9 3.4 %copy-start = (bf16[1024,512]{1,0:T(8,128)(2,1)S(1)}, bf16[1024,512]{1,0:T(8,128)(2,1)}, u32[]{:S(2)}) copy-start(bf16[1024,512]{1,0:T(8,128)(2,1)} %refs_5_.3) | copy-start | bytes 3145732
  16.9 3.4 %copy-start.1 = (bf16[1024,512]{1,0:T(8,128)(2,1)S(1)}, bf16[1024,512]{1,0:T(8,128)(2,1)}, u32[]{:S(2)}) copy-start(bf16[1024,512]{1,0:T(8,128)(2,1)} %refs_6_.3) | copy-start | bytes 3145732
  21.3 2.8 %copy-start.2 = (bf16[512,1024]{1,0:T(8,128)(2,1)S(1)}, bf16[512,1024]{1,0:T(8,128)(2,1)}, u32[]{:S(2)}) copy-start(bf16[512,1024]{1,0:T(8,128)(2,1)} %wo.3) | copy-start | bytes 3145732
  21.3 2.7 %copy-start.4 = (s32[4,8]{1,0:T(4,128)S(1)}, s32[4,8]{1,0:T(4,128)}, u32[]{:S(2)}) copy-start(s32[4,8]{1,0:T(4,128)} %adjacency.1) | copy-start | bytes 388
  21.3 2.4 %collective-permute-start.8 = (bf16[384,1024]{1,0:T(8,128)(2,1)S(1)}, bf16[384,1024]{1,0:T(8,128)(2,1)S(1)}, u32[]{:S(2)}, u32[]{:S(2)}) collective-permute-start(bf16[384,1024]{1,0:T(8,128)(2,1)S(1)} %project.3), channel_id=1, source_target_pairs={{0,1},{1,0},{2,3},{3,2},{4,5},{5,4},{6,7},{7,6},{8,9},{9,8},{10,11... | collective-permute-start | bytes 2359304 | tf_op jit(solution)/shard_map/ppermute | solution.py:426
  21.9 2.2 %collective-permute-start.6 = (bf16[128,1024]{1,0:T(8,128)(2,1)S(1)}, bf16[128,1024]{1,0:T(8,128)(2,1)S(1)}, u32[]{:S(2)}, u32[]{:S(2)}) collective-permute-start(bf16[128,1024]{1,0:T(8,128)(2,1)S(1)} %project.2), channel_id=1, source_target_pairs={{0,1},{1,0},{2,3},{3,2},{4,5},{5,4},{6,7},{7,6},{8,9},{9,8},{10,11... | collective-permute-start | bytes 786440 | tf_op jit(solution)/shard_map/ppermute | solution.py:426
  26.6 4.6 %collective-permute-start.10 = (bf16[256,128]{1,0:T(8,128)(2,1)S(1)}, bf16[256,128]{1,0:T(8,128)(2,1)S(1)}, u32[]{:S(2)}, u32[]{:S(2)}) collective-permute-start(bf16[256,128]{1,0:T(8,128)(2,1)S(1)} %get-tuple-element.52), channel_id=1, source_target_pairs={{0,2},{2,0},{1,3},{3,1},{4,6},{6,4},{5,7},{7,5},{8,10},{10,8},{9,1... | collective-permute-start | bytes 196616 | tf_op jit(solution)/shard_map/ppermute | solution.py:426
  27.8 1.4 %copy-start.5 = (s32[4,1]{0,1:T(1,128)S(1)}, s32[4,1]{0,1:T(1,128)}, u32[]{:S(2)}) copy-start(s32[4,1]{0,1:T(1,128)} %param.12) | copy-start | bytes 52
  27.8 3.4 %copy-start.3 = (bf16[4,64,512]{2,1,0:T(8,128)(2,1)S(1)}, bf16[4,64,512]{2,1,0:T(8,128)(2,1)}, u32[]{:S(2)}) copy-start(bf16[4,64,512]{2,1,0:T(8,128)(2,1)} %grid_features.5) | copy-start | bytes 786436
  28.2 8.0 %collective-permute-start.9 = (bf16[256,384]{1,0:T(8,128)(2,1)S(1)}, bf16[256,384]{1,0:T(8,128)(2,1)S(1)}, u32[]{:S(2)}, u32[]{:S(2)}) collective-permute-start(bf16[256,384]{1,0:T(8,128)(2,1)S(1)} %get-tuple-element.50), channel_id=1, source_target_pairs={{0,2},{2,0},{1,3},{3,1},{4,6},{6,4},{5,7},{7,5},{8,10},{10,8},{9,1... | collective-permute-start | bytes 589832 | tf_op jit(solution)/shard_map/ppermute | solution.py:426
  31.8 10.2 %collective-permute-start.14 = (bf16[2,64,128]{2,1,0:T(8,128)(2,1)S(1)}, bf16[2,64,128]{2,1,0:T(8,128)(2,1)S(1)}, u32[]{:S(2)}, u32[]{:S(2)}) collective-permute-start(bf16[2,64,128]{2,1,0:T(8,128)(2,1)S(1)} %get-tuple-element.53), channel_id=1, source_target_pairs={{0,8},{4,12},{8,0},{12,4},{1,9},{5,13},{9,1},{13,5},{2,10},{6,14},... | collective-permute-start | bytes 98312 | tf_op jit(solution)/shard_map/ppermute | solution.py:422
  36.2 5.9 %collective-permute-start.15 = (bf16[2,64,128]{2,1,0:T(8,128)(2,1)S(1)}, bf16[2,64,128]{2,1,0:T(8,128)(2,1)S(1)}, u32[]{:S(2)}, u32[]{:S(2)}) collective-permute-start(bf16[2,64,128]{2,1,0:T(8,128)(2,1)S(1)} %get-tuple-element.60), channel_id=1, source_target_pairs={{0,12},{4,8},{8,4},{12,0},{1,13},{5,9},{9,5},{13,1},{2,14},{6,10},... | collective-permute-start | bytes 98312 | tf_op jit(solution)/shard_map/ppermute | solution.py:422
  36.8 6.8 %collective-permute-start.11 = (bf16[2,64,384]{2,1,0:T(8,128)(2,1)S(1)}, bf16[2,64,384]{2,1,0:T(8,128)(2,1)S(1)}, u32[]{:S(2)}, u32[]{:S(2)}) collective-permute-start(bf16[2,64,384]{2,1,0:T(8,128)(2,1)S(1)} %get-tuple-element.55), channel_id=1, source_target_pairs={{0,8},{4,12},{8,0},{12,4},{1,9},{5,13},{9,1},{13,5},{2,10},{6,14},... | collective-permute-start | bytes 294920 | tf_op jit(solution)/shard_map/ppermute | solution.py:422
  40.3 8.2 %collective-permute-start.13 = (bf16[2,64,512]{2,1,0:T(8,128)(2,1)S(1)}, bf16[2,64,512]{2,1,0:T(8,128)(2,1)S(1)}, u32[]{:S(2)}, u32[]{:S(2)}) collective-permute-start(bf16[2,64,512]{2,1,0:T(8,128)(2,1)S(1)} %get-tuple-element.58), channel_id=1, source_target_pairs={{0,4},{4,0},{8,12},{12,8},{1,5},{5,1},{9,13},{13,9},{2,6},{6,2},{1... | collective-permute-start | bytes 393224 | tf_op jit(solution)/shard_map/ppermute | solution.py:422
  42.0 6.4 %collective-permute-start.12 = (bf16[2,64,384]{2,1,0:T(8,128)(2,1)S(1)}, bf16[2,64,384]{2,1,0:T(8,128)(2,1)S(1)}, u32[]{:S(2)}, u32[]{:S(2)}) collective-permute-start(bf16[2,64,384]{2,1,0:T(8,128)(2,1)S(1)} %get-tuple-element.56), channel_id=1, source_target_pairs={{0,12},{4,8},{8,4},{12,0},{1,13},{5,9},{9,5},{13,1},{2,14},{6,10},... | collective-permute-start | bytes 294920 | tf_op jit(solution)/shard_map/ppermute | solution.py:422

commit v15 on v14

--- a/solution.py
+++ b/solution.py
@@ -49,10 +49,15 @@
     return pltpu.CompilerParams(vmem_limit_bytes=mib * MIB)
 
 
-def mlp_kernel(own, other, gain, wq, wup, wdn, q_out, mlp_out, normed_s):
+def mlp_kernel(own, other, gain, wq, wup, wdn, q_out, mlp_out, normed_s, wdn_s, sem):
     half = own.shape[1]
     units = wup.shape[1]
     chunk = units // 4
+    copies = []
+    for c in range(units // chunk):
+        span = pl.ds(c * chunk, chunk)
+        copies.append(pltpu.make_async_copy(wdn.at[span, :], wdn_s.at[span, :], sem.at[c]))
+        copies[c].start()
     x_other = other[...].astype(jnp.float32)
     x_own = own[...].astype(jnp.float32)
 
@@ -71,7 +76,8 @@
     for c in range(units // chunk):
         span = slice(c * chunk, (c + 1) * chunk)
         hidden = gelu(dot(normed, wup[:, span])).astype(jnp.bfloat16)
-        term = dot(hidden, wdn[span, :])
+        copies[c].wait()
+        term = dot(hidden, wdn_s[span, :])
         if c == 0:
             mlp_out[...] = term
         else:
@@ -88,9 +94,13 @@
             jax.ShapeDtypeStruct((rows, wq.shape[1]), jnp.bfloat16),
             jax.ShapeDtypeStruct((rows, width), jnp.float32),
         ),
-        in_specs=vmem(6),
+        in_specs=vmem(5) + [whole(pltpu.HBM)],
         out_specs=tuple(vmem(2)),
-        scratch_shapes=[pltpu.VMEM((rows, width), jnp.bfloat16)],
+        scratch_shapes=[
+            pltpu.VMEM((rows, width), jnp.bfloat16),
+            pltpu.VMEM(wdn.shape, jnp.bfloat16),
+            pltpu.SemaphoreType.DMA((4,)),
+        ],
         compiler_params=params(16),
         cost_estimate=pl.CostEstimate(
             flops=2 * rows * width * (wq.shape[1] + 2 * units),
@@ -98,7 +108,7 @@
             transcendentals=rows * units,
         ),
         name="mlp",
-    )(own, other, gain, wq, wup, wdn)
+    )(own, other, gain, wq, wup, in_hbm(wdn))
 
 
 def pick_kernel(mesh, out, sem):
@@ -231,10 +241,9 @@
     h = lax.axis_index("head")
 
     def write(head):
-        for out, first, place in ((send, 0, 1 - head), (keep, half, head)):
-            extra = mlp[:, first + chunk.start : first + chunk.stop]
+        for out, place in ((send, 1 - head), (keep, head)):
             span = slice(place * half + chunk.start, place * half + chunk.stop)
-            out[...] = (extra + dot(att[...], wo[:, span])).astype(jnp.bfloat16)
+            out[...] = (mlp[:, span] + dot(att[...], wo[:, span])).astype(jnp.bfloat16)
 
     for head in range(2):
         pl.when(h == head)(functools.partial(write, head))
@@ -447,17 +456,16 @@
     near = crossed(half_unit, 1, shards)
     waiting, _ = lax.optimization_barrier((flat, half_unit))
     other = swapped(waiting, "head")
-    flat, gain, wq, wup, wdn, mesh, rest = run_stage(
+    flat, gain, wq, wup, mesh, rest = run_stage(
         (
             flat,
             norm_gain.reshape(1, -1),
             query_weight,
             up_weight,
-            down_weight,
             mesh_nodes,
             mesh_nodes,
         ),
-        (None, 1, 0, 0, 1, None, "rest"),
+        (None, 1, 0, 0, None, "rest"),
     )
     straight = crossed(rest, 3, shards)
     near, _ = lax.optimization_barrier((near, rest))
@@ -465,7 +473,7 @@
     far, _, _ = lax.optimization_barrier((far, near, rest))
     farther = crossed(far, 1, shards)
     far_pair = swapped(far, "head")
-    queries, mlp = run_mlp(flat, other, gain, wq, wup, wdn)
+    queries, mlp = run_mlp(flat, other, gain, wq, wup, down_weight)
     queries, mlp, far_pair = lax.optimization_barrier((queries, mlp, far_pair))
     blocked = (-1, BLOCK, 2 * half)
     mine_a = run_project((mesh, near, near_pair, far, far_pair), key_weight, value_weight)

time: 49.4 us -> 50.8 us (1.028)
  waiting for transfers between devices: 9.21 us -> 10.7 us
    pallas_call x1, Pallas kernels: 4.1 us -> 2.87 us  [run_stage(): pl.pallas_call(functools.partial(stage_kernel, axes), out_shape=tuple((ja...]
    ppermute x9, waiting for transfers between devices: 5.77 us -> 6.87 us  [crossed(): return lax.ppermute(x, 'shard', [(i, i ^ distance) for i in range(size)])]
    pallas_call x1, Pallas kernels: 3.33 us -> 4.22 us  [run_mlp(): pl.pallas_call(mlp_kernel, out_shape=(jax.ShapeDtypeStruct((rows, wq.shap...]
  transfers between devices with their start and end apart: 16 -> 16, of which waited for: 5 -> 6; matrix products, arithmetic and copies ran while one was open for 0% -> 0% of each run, Pallas kernels for 24% -> 23%
where the time goes in v15:
time: 50.8 us; the launch traced here: 50.6 us
  starting transfers between devices  23.7 us (47%)
  Pallas kernels  15.9 us (31%)
  waiting for transfers between devices  10.7 us (21%)
    ppermute x9, starting transfers between devices, crossed(): return lax.ppermute(x, 'shard', [(i, i ^ distance) for i in range(size)])  17.6 us
    ppermute x9, waiting for transfers between devices, crossed(): return lax.ppermute(x, 'shard', [(i, i ^ distance) for i in range(size)])  6.87 us
    ppermute x7, starting transfers between devices, swapped(): return lax.ppermute(x, axis, [(0, 1), (1, 0)])  6.15 us
    pallas_call x1, Pallas kernels, run_mlp(): pl.pallas_call(mlp_kernel, out_shape=(jax.ShapeDtypeStruct((rows, wq.shap...  4.22 us
    ppermute x7, waiting for transfers between devices, swapped(): return lax.ppermute(x, axis, [(0, 1), (1, 0)])  3.87 us
    pallas_call x1, Pallas kernels, run_stage(): pl.pallas_call(functools.partial(stage_kernel, axes), out_shape=tuple((ja...  2.87 us
    pallas_call x1, Pallas kernels, run_attend(): pl.pallas_call(attend_kernel, out_shape=(part, part, jax.ShapeDtypeStruct...  2.52 us
    pallas_call x3, Pallas kernels, run_combine(): pl.pallas_call(functools.partial(combine_kernel, chunks, distances), out_...  1.95 us
  transfers between devices with their start and end apart: 16, of which 6 were waited for; matrix products, arithmetic and copies ran while one was open for 0% of the time, Pallas kernels for 23%

profile of v15, /device:TPU:0, one launch (start us, length us, event | category | flops | bytes accessed | tf_op | source)
XLA Modules:
  0.0 50.6 jit_solution(16231803849794988952)
XLA Ops:
  0.0 0.9 %pick.1 = bf16[64,1024]{1,0:T(8,128)(2,1)S(1)} custom-call(bf16[128,1024]{1,0:T(8,128)(2,1)} %mesh.1), custom_call_target="tpu_custom_call" | custom-call | bytes 524288 | tf_op jit(solution)/shard_map/pick/pallas_call | solution.py:122
  0.9 3.1 %collective-permute-start.2 = (bf16[64,1024]{1,0:T(8,128)(2,1)S(1)}, bf16[64,1024]{1,0:T(8,128)(2,1)S(1)}, u32[]{:S(2)}, u32[]{:S(2)}) collective-permute-start(bf16[64,1024]{1,0:T(8,128)(2,1)S(1)} %pick.1), channel_id=1, source_target_pairs={{0,4},{4,0},{8,12},{12,8},{1,5},{5,1},{9,13},{13,9},{2,6},{6,2},{1... | collective-permute-start | bytes 393224 | tf_op jit(solution)/shard_map/ppermute | solution.py:431
  4.0 2.6 %collective-permute-start.1 = (bf16[64,1024]{1,0:T(8,128)(2,1)S(1)}, bf16[64,1024]{1,0:T(8,128)(2,1)S(1)}, u32[]{:S(2)}, u32[]{:S(2)}) collective-permute-start(bf16[64,1024]{1,0:T(8,128)(2,1)S(1)} %pick.1), channel_id=1, source_target_pairs={{0,8},{4,12},{8,0},{12,4},{1,9},{5,13},{9,1},{13,5},{2,10},{6,14},... | collective-permute-start | bytes 393224 | tf_op jit(solution)/shard_map/ppermute | solution.py:431
  6.6 1.5 %collective-permute-start = (bf16[256,512]{1,0:T(8,128)(2,1)}, bf16[256,512]{1,0:T(8,128)(2,1)S(1)}, u32[]{:S(2)}, u32[]{:S(2)}) collective-permute-start(bf16[256,512]{1,0:T(8,128)(2,1)} %bitcast.8), channel_id=1, source_target_pairs={{0,2},{2,0},{1,3},{3,1},{4,6},{6,4},{5,7},{7,5},{8,10},{10,8},{9,1... | collective-permute-start | bytes 786440 | tf_op jit(solution)/shard_map/ppermute | solution.py:435
  8.1 2.9 %stage.1 = (bf16[256,512]{1,0:T(8,128)(2,1)S(1)}, f32[1,1024]{1,0:T(1,128)S(1)}, bf16[1024,512]{1,0:T(8,128)(2,1)S(1)}, bf16[1024,2048]{1,0:T(8,128)(2,1)S(1)}, ...) custom-call(bf16[256,512]{1,0:T(8,128)(2,1)} %bitcast.9, f32[1,1024]{1,0:T(1,128)} %bitcast.12, ...), custom_call_target="tpu_custom_call" | custom-call | flops 12062720000 | bytes 120627200 | tf_op jit(solution)/shard_map/stage/pallas_call | solution.py:172
  11.0 0.3 collective-permute-start.5
  11.3 0.0 collective-permute-done.2.refs_1_
  11.3 0.4 collective-permute-start.7
  11.7 1.1 %collective-permute-done.1.refs_3_ = bf16[64,1024]{1,0:T(8,128)(2,1)S(1)} collective-permute-done((bf16[64,1024]{1,0:T(8,128)(2,1)S(1)}, bf16[64,1024]{1,0:T(8,128)(2,1)S(1)}, u32[]{:S(2)}, u32[]{:S(2)}) %collective-permute-start.1) | collective-permute-done | bytes 131104 | tf_op jit(solution)/shard_map/ppermute | solution.py:431
  12.8 1.5 %collective-permute-start.3 = (bf16[64,1024]{1,0:T(8,128)(2,1)S(1)}, bf16[64,1024]{1,0:T(8,128)(2,1)S(1)}, u32[]{:S(2)}, u32[]{:S(2)}) collective-permute-start(bf16[64,1024]{1,0:T(8,128)(2,1)S(1)} %collective-permute-done.1.refs_3_), channel_id=1, source_target_pairs={{0,2},{2,0},{1,3},{3,1},{4,6},{6,4},{5,7},{7,5},{8,10},{10,8},{9,1... | collective-permute-start | bytes 393224 | tf_op jit(solution)/shard_map/ppermute | solution.py:435
  14.3 3.6 %collective-permute-start.4 = (bf16[64,1024]{1,0:T(8,128)(2,1)S(1)}, bf16[64,1024]{1,0:T(8,128)(2,1)S(1)}, u32[]{:S(2)}, u32[]{:S(2)}) collective-permute-start(bf16[64,1024]{1,0:T(8,128)(2,1)S(1)} %collective-permute-done.1.refs_3_), channel_id=1, source_target_pairs={{0,4},{4,0},{8,12},{12,8},{1,5},{5,1},{9,13},{13,9},{2,6},{6,2},{1... | collective-permute-start | bytes 393224 | tf_op jit(solution)/shard_map/ppermute | solution.py:431
  17.9 0.0 collective-permute-done.other
  17.9 0.0 copy-start
  17.9 0.0 copy-start.1
  17.9 4.2 %mlp.1 = (bf16[256,512]{1,0:T(8,128)(2,1)S(1)}, f32[256,1024]{1,0:T(8,128)S(1)}) custom-call(bf16[256,512]{1,0:T(8,128)(2,1)S(1)} %get-tuple-element.32.own, bf16[256,512]{1,0:T(8,128)(2,1)S(1)} %collective-permute-done.other, f32[1,1024]{1,0:T(1,128)S(1)} %get-tuple-element.34.gain, bf16[1024,512]{1,0:T(8,128)(2,1)S(1)} %get-tuple-element.35.wq, ...), custom_call_target="tpu_custom_call" | custom-call | flops 2415919104 | bytes 9437184 | tf_op jit(solution)/shard_map/mlp/pallas_call | solution.py:91
  22.1 0.0 collective-permute-done.3.refs_4_
  22.2 0.0 collective-permute-done.7.refs_2_
  22.2 0.0 copy-done
  22.2 0.0 copy-done.1
  22.2 1.0 %project.3 = bf16[384,1024]{1,0:T(8,128)(2,1)S(1)} custom-call(bf16[128,1024]{1,0:T(8,128)(2,1)S(1)} %get-tuple-element.43.refs_0_, bf16[64,1024]{1,0:T(8,128)(2,1)S(1)} %collective-permute-done.2.refs_1_, bf16[64,1024]{1,0:T(8,128)(2,1)S(1)} %collective-permute-done.7.refs_2_, bf16[64,1024]{1,0:T(8,128)(2,1)S(1)} %collective-permute-done.1.refs_3_, ...), custom_call_target="tpu_custom_call" | custom-call | flops 60397977600 | bytes 275251200 | tf_op jit(solution)/shard_map/project/pallas_call | solution.py:200
  23.2 0.0 copy-start.2
  23.2 0.0 copy-start.4
  23.2 0.1 collective-permute-start.8
  23.3 0.0 collective-permute-done.5.refs_1_
  23.3 0.0 collective-permute-done.4.refs_0_
  23.3 0.4 project.2
  23.7 0.5 %collective-permute-start.6 = (bf16[128,1024]{1,0:T(8,128)(2,1)S(1)}, bf16[128,1024]{1,0:T(8,128)(2,1)S(1)}, u32[]{:S(2)}, u32[]{:S(2)}) collective-permute-start(bf16[128,1024]{1,0:T(8,128)(2,1)S(1)} %project.2), channel_id=1, source_target_pairs={{0,1},{1,0},{2,3},{3,2},{4,5},{5,4},{6,7},{7,6},{8,9},{9,8},{10,11... | collective-permute-start | bytes 786440 | tf_op jit(solution)/shard_map/ppermute | solution.py:435
  24.3 1.3 %collective-permute-done.8 = bf16[384,1024]{1,0:T(8,128)(2,1)S(1)} collective-permute-done((bf16[384,1024]{1,0:T(8,128)(2,1)S(1)}, bf16[384,1024]{1,0:T(8,128)(2,1)S(1)}, u32[]{:S(2)}, u32[]{:S(2)}) %collective-permute-start.8) | collective-permute-done | bytes 786464 | tf_op jit(solution)/shard_map/ppermute | solution.py:435
  25.5 0.1 table.1.table_in
  25.7 0.3 collective-permute-done.6
  25.9 0.0 copy-done.2
  25.9 0.0 copy-done.4
  25.9 2.5 %attend.1 = (bf16[256,128]{1,0:T(8,128)(2,1)S(1)}, bf16[256,128]{1,0:T(8,128)(2,1)S(1)}, bf16[256,512]{1,0:T(8,128)(2,1)S(1)}, bf16[2,8,64,1024]{3,2,1,0:T(8,128)(2,1)S(1)}) custom-call(s32[4,8]{1,0:T(4,128)S(1)} %copy-done.4, bf16[256,512]{1,0:T(8,128)(2,1)S(1)} %get-tuple-element.42.q, ...), custom_call_target="tpu_custom_call", output_to_operand_aliasing={{3}: (4, {})} | custom-call | flops 13421772800 | bytes 41943040 | tf_op jit(solution)/shard_map/attend/pallas_call | solution.py:314
  28.5 0.6 %collective-permute-start.10 = (bf16[256,128]{1,0:T(8,128)(2,1)S(1)}, bf16[256,128]{1,0:T(8,128)(2,1)S(1)}, u32[]{:S(2)}, u32[]{:S(2)}) collective-permute-start(bf16[256,128]{1,0:T(8,128)(2,1)S(1)} %get-tuple-element.50), channel_id=1, source_target_pairs={{0,2},{2,0},{1,3},{3,1},{4,6},{6,4},{5,7},{7,5},{8,10},{10,8},{9,1... | collective-permute-start | bytes 196616 | tf_op jit(solution)/shard_map/ppermute | solution.py:435
  29.1 0.0 copy-start.5
  29.1 0.0 copy-start.3
  29.1 0.4 project_out.1
  29.5 1.5 %collective-permute-start.9 = (bf16[256,384]{1,0:T(8,128)(2,1)S(1)}, bf16[256,384]{1,0:T(8,128)(2,1)S(1)}, u32[]{:S(2)}, u32[]{:S(2)}) collective-permute-start(bf16[256,384]{1,0:T(8,128)(2,1)S(1)} %get-tuple-element.48), channel_id=1, source_target_pairs={{0,2},{2,0},{1,3},{3,1},{4,6},{6,4},{5,7},{7,5},{8,10},{10,8},{9,1... | collective-permute-start | bytes 589832 | tf_op jit(solution)/shard_map/ppermute | solution.py:435
  31.1 0.0 copy-done.5
  31.1 0.1 copy.15.owners
  31.1 2.3 %collective-permute-done.10.refs_1_.refs_2_ = bf16[256,128]{1,0:T(8,128)(2,1)S(1)} collective-permute-done((bf16[256,128]{1,0:T(8,128)(2,1)S(1)}, bf16[256,128]{1,0:T(8,128)(2,1)S(1)}, u32[]{:S(2)}, u32[]{:S(2)}) %collective-permute-start.10) | collective-permute-done | bytes 65568 | tf_op jit(solution)/shard_map/ppermute | solution.py:435
  33.5 0.0 copy-done.3
  33.5 0.6 %combine.3 = (bf16[2,64,128]{2,1,0:T(8,128)(2,1)S(1)}, bf16[2,64,128]{2,1,0:T(8,128)(2,1)S(1)}) custom-call(s32[4,1]{1,0:T(4,128)S(1)} %copy.15.owners, bf16[4,64,512]{2,1,0:T(8,128)(2,1)S(1)} %copy-done.3, bf16[256,128]{1,0:T(8,128)(2,1)S(1)} %get-tuple-element.49.refs_0_, bf16[256,128]{1,0:T(8,128)(2,1)S(1)} %collective-permute-done.10.refs_1_.refs_2_), custom_call_target="tpu_custom_call" | custom-call | flops 1966080000 | bytes 52428800 | tf_op jit(solution)/shard_map/combine/pallas_call | solution.py:386
  34.1 3.5 %collective-permute-start.14 = (bf16[2,64,128]{2,1,0:T(8,128)(2,1)S(1)}, bf16[2,64,128]{2,1,0:T(8,128)(2,1)S(1)}, u32[]{:S(2)}, u32[]{:S(2)}) collective-permute-start(bf16[2,64,128]{2,1,0:T(8,128)(2,1)S(1)} %get-tuple-element.51), channel_id=1, source_target_pairs={{0,8},{4,12},{8,0},{12,4},{1,9},{5,13},{9,1},{13,5},{2,10},{6,14},... | collective-permute-start | bytes 98312 | tf_op jit(solution)/shard_map/ppermute | solution.py:431
  37.6 0.0 collective-permute-start.15
  37.6 0.0 collective-permute-done.9.refs_1_.refs_3_
  37.6 0.6 %combine.4 = (bf16[2,64,384]{2,1,0:T(8,128)(2,1)S(1)}, bf16[2,64,384]{2,1,0:T(8,128)(2,1)S(1)}) custom-call(s32[4,1]{1,0:T(4,128)S(1)} %copy.15.owners, bf16[4,64,512]{2,1,0:T(8,128)(2,1)S(1)} %copy-done.3, bf16[256,384]{1,0:T(8,128)(2,1)S(1)} %get-tuple-element.47.refs_0_.refs_1_, bf16[256,384]{1,0:T(8,128)(2,1)S(1)} %collective-permute-done.9.refs_1_.refs_3_), custom_call_target="tpu_custom_call" | custom-call | flops 5898240000 | bytes 157286400 | tf_op jit(solution)/shard_map/combine/pallas_call | solution.py:386
  38.2 2.8 %collective-permute-start.11 = (bf16[2,64,384]{2,1,0:T(8,128)(2,1)S(1)}, bf16[2,64,384]{2,1,0:T(8,128)(2,1)S(1)}, u32[]{:S(2)}, u32[]{:S(2)}) collective-permute-start(bf16[2,64,384]{2,1,0:T(8,128)(2,1)S(1)} %get-tuple-element.53), channel_id=1, source_target_pairs={{0,8},{4,12},{8,0},{12,4},{1,9},{5,13},{9,1},{13,5},{2,10},{6,14},... | collective-permute-start | bytes 294920 | tf_op jit(solution)/shard_map/ppermute | solution.py:431
  41.0 0.7 %combine.5 = (bf16[2,64,512]{2,1,0:T(8,128)(2,1)S(1)}, bf16[2,64,512]{2,1,0:T(8,128)(2,1)S(1)}) custom-call(s32[4,1]{1,0:T(4,128)S(1)} %copy.15.owners, bf16[4,64,512]{2,1,0:T(8,128)(2,1)S(1)} %copy-done.3, bf16[256,128]{1,0:T(8,128)(2,1)S(1)} %get-tuple-element.49.refs_0_, bf16[256,384]{1,0:T(8,128)(2,1)S(1)} %get-tuple-element.47.refs_0_.refs_1_, ...), custom_call_target="tpu_custom_call" | custom-call | flops 7864320000 | bytes 209715200 | tf_op jit(solution)/shard_map/combine/pallas_call | solution.py:386
  41.7 1.7 %collective-permute-start.13 = (bf16[2,64,512]{2,1,0:T(8,128)(2,1)S(1)}, bf16[2,64,512]{2,1,0:T(8,128)(2,1)S(1)}, u32[]{:S(2)}, u32[]{:S(2)}) collective-permute-start(bf16[2,64,512]{2,1,0:T(8,128)(2,1)S(1)} %get-tuple-element.56), channel_id=1, source_target_pairs={{0,4},{4,0},{8,12},{12,8},{1,5},{5,1},{9,13},{13,9},{2,6},{6,2},{1... | collective-permute-start | bytes 393224 | tf_op jit(solution)/shard_map/ppermute | solution.py:431
  43.4 0.0 collective-permute-start.12
  43.4 0.0 collective-permute-done.14.refs_0_
  43.4 0.0 collective-permute-done.15.refs_1_
  43.4 0.7 %place.2.refs_4_ = bf16[8,64,512]{2,1,0:T(8,128)(2,1)} custom-call(bf16[2,64,128]{2,1,0:T(8,128)(2,1)S(1)} %collective-permute-done.14.refs_0_, bf16[2,64,128]{2,1,0:T(8,128)(2,1)S(1)} %collective-permute-done.15.refs_1_), custom_call_target="tpu_custom_call" | custom-call | flops 13107200000 | tf_op jit(solution)/shard_map/place/pallas_call | solution.py:415
  44.1 1.6 %collective-permute-done.11.refs_0_ = bf16[2,64,384]{2,1,0:T(8,128)(2,1)S(1)} collective-permute-done((bf16[2,64,384]{2,1,0:T(8,128)(2,1)S(1)}, bf16[2,64,384]{2,1,0:T(8,128)(2,1)S(1)}, u32[]{:S(2)}, u32[]{:S(2)}) %collective-permute-start.11) | collective-permute-done | bytes 98336 | tf_op jit(solution)/shard_map/ppermute | solution.py:431
  45.7 4.1 %collective-permute-done.12.refs_1_ = bf16[2,64,384]{2,1,0:T(8,128)(2,1)S(1)} collective-permute-done((bf16[2,64,384]{2,1,0:T(8,128)(2,1)S(1)}, bf16[2,64,384]{2,1,0:T(8,128)(2,1)S(1)}, u32[]{:S(2)}, u32[]{:S(2)}) %collective-permute-start.12) | collective-permute-done | bytes 98336 | tf_op jit(solution)/shard_map/ppermute | solution.py:431
  49.8 0.0 collective-permute-done.13.refs_2_
  49.8 0.8 %place.3 = bf16[8,64,512]{2,1,0:T(8,128)(2,1)} custom-call(bf16[2,64,384]{2,1,0:T(8,128)(2,1)S(1)} %collective-permute-done.11.refs_0_, bf16[2,64,384]{2,1,0:T(8,128)(2,1)S(1)} %collective-permute-done.12.refs_1_, bf16[2,64,512]{2,1,0:T(8,128)(2,1)S(1)} %collective-permute-done.13.refs_2_, ...), custom_call_target="tpu_custom_call", output_to_operand_aliasing={{}: (4, {})} | custom-call | flops 91750400000 | tf_op jit(solution)/shard_map/place/pallas_call | solution.py:415
Async XLA Ops:
  0.9 10.3 %collective-permute-start.2 = (bf16[64,1024]{1,0:T(8,128)(2,1)S(1)}, bf16[64,1024]{1,0:T(8,128)(2,1)S(1)}, u32[]{:S(2)}, u32[]{:S(2)}) collective-permute-start(bf16[64,1024]{1,0:T(8,128)(2,1)S(1)} %pick.1), channel_id=1, source_target_pairs={{0,4},{4,0},{8,12},{12,8},{1,5},{5,1},{9,13},{13,9},{2,6},{6,2},{1... | collective-permute-start | bytes 393224 | tf_op jit(solution)/shard_map/ppermute | solution.py:431
  4.0 8.8 %collective-permute-start.1 = (bf16[64,1024]{1,0:T(8,128)(2,1)S(1)}, bf16[64,1024]{1,0:T(8,128)(2,1)S(1)}, u32[]{:S(2)}, u32[]{:S(2)}) collective-permute-start(bf16[64,1024]{1,0:T(8,128)(2,1)S(1)} %pick.1), channel_id=1, source_target_pairs={{0,8},{4,12},{8,0},{12,4},{1,9},{5,13},{9,1},{13,5},{2,10},{6,14},... | collective-permute-start | bytes 393224 | tf_op jit(solution)/shard_map/ppermute | solution.py:431
  6.6 11.3 %collective-permute-start = (bf16[256,512]{1,0:T(8,128)(2,1)}, bf16[256,512]{1,0:T(8,128)(2,1)S(1)}, u32[]{:S(2)}, u32[]{:S(2)}) collective-permute-start(bf16[256,512]{1,0:T(8,128)(2,1)} %bitcast.8), channel_id=1, source_target_pairs={{0,2},{2,0},{1,3},{3,1},{4,6},{6,4},{5,7},{7,5},{8,10},{10,8},{9,1... | collective-permute-start | bytes 786440 | tf_op jit(solution)/shard_map/ppermute | solution.py:435
  11.0 12.3 %collective-permute-start.5 = (bf16[64,1024]{1,0:T(8,128)(2,1)S(1)}, bf16[64,1024]{1,0:T(8,128)(2,1)S(1)}, u32[]{:S(2)}, u32[]{:S(2)}) collective-permute-start(bf16[64,1024]{1,0:T(8,128)(2,1)S(1)} %get-tuple-element.39), channel_id=1, source_target_pairs={{0,12},{4,8},{8,4},{12,0},{1,13},{5,9},{9,5},{13,1},{2,14},{6,10},... | collective-permute-start | bytes 393224 | tf_op jit(solution)/shard_map/ppermute | solution.py:431
  11.3 10.9 %collective-permute-start.7 = (bf16[64,1024]{1,0:T(8,128)(2,1)S(1)}, bf16[64,1024]{1,0:T(8,128)(2,1)S(1)}, u32[]{:S(2)}, u32[]{:S(2)}) collective-permute-start(bf16[64,1024]{1,0:T(8,128)(2,1)S(1)} %collective-permute-done.2.refs_1_), channel_id=1, source_target_pairs={{0,2},{2,0},{1,3},{3,1},{4,6},{6,4},{5,7},{7,5},{8,10},{10,8},{9,1... | collective-permute-start | bytes 393224 | tf_op jit(solution)/shard_map/ppermute | solution.py:435
  12.8 9.4 %collective-permute-start.3 = (bf16[64,1024]{1,0:T(8,128)(2,1)S(1)}, bf16[64,1024]{1,0:T(8,128)(2,1)S(1)}, u32[]{:S(2)}, u32[]{:S(2)}) collective-permute-start(bf16[64,1024]{1,0:T(8,128)(2,1)S(1)} %collective-permute-done.1.refs_3_), channel_id=1, source_target_pairs={{0,2},{2,0},{1,3},{3,1},{4,6},{6,4},{5,7},{7,5},{8,10},{10,8},{9,1... | collective-permute-start | bytes 393224 | tf_op jit(solution)/shard_map/ppermute | solution.py:435
  14.3 9.0 %collective-permute-start.4 = (bf16[64,1024]{1,0:T(8,128)(2,1)S(1)}, bf16[64,1024]{1,0:T(8,128)(2,1)S(1)}, u32[]{:S(2)}, u32[]{:S(2)}) collective-permute-start(bf16[64,1024]{1,0:T(8,128)(2,1)S(1)} %collective-permute-done.1.refs_3_), channel_id=1, source_target_pairs={{0,4},{4,0},{8,12},{12,8},{1,5},{5,1},{9,13},{13,9},{2,6},{6,2},{1... | collective-permute-start | bytes 393224 | tf_op jit(solution)/shard_map/ppermute | solution.py:431
  17.9 4.3 %copy-start = (bf16[1024,512]{1,0:T(8,128)(2,1)S(1)}, bf16[1024,512]{1,0:T(8,128)(2,1)}, u32[]{:S(2)}) copy-start(bf16[1024,512]{1,0:T(8,128)(2,1)} %refs_5_.3) | copy-start | bytes 3145732
  17.9 4.3 %copy-start.1 = (bf16[1024,512]{1,0:T(8,128)(2,1)S(1)}, bf16[1024,512]{1,0:T(8,128)(2,1)}, u32[]{:S(2)}) copy-start(bf16[1024,512]{1,0:T(8,128)(2,1)} %refs_6_.1) | copy-start | bytes 3145732
  23.2 2.8 %copy-start.2 = (bf16[512,1024]{1,0:T(8,128)(2,1)S(1)}, bf16[512,1024]{1,0:T(8,128)(2,1)}, u32[]{:S(2)}) copy-start(bf16[512,1024]{1,0:T(8,128)(2,1)} %wo.3) | copy-start | bytes 3145732
  23.2 2.7 %copy-start.4 = (s32[4,8]{1,0:T(4,128)S(1)}, s32[4,8]{1,0:T(4,128)}, u32[]{:S(2)}) copy-start(s32[4,8]{1,0:T(4,128)} %adjacency.1) | copy-start | bytes 388
  23.2 2.4 %collective-permute-start.8 = (bf16[384,1024]{1,0:T(8,128)(2,1)S(1)}, bf16[384,1024]{1,0:T(8,128)(2,1)S(1)}, u32[]{:S(2)}, u32[]{:S(2)}) collective-permute-start(bf16[384,1024]{1,0:T(8,128)(2,1)S(1)} %project.3), channel_id=1, source_target_pairs={{0,1},{1,0},{2,3},{3,2},{4,5},{5,4},{6,7},{7,6},{8,9},{9,8},{10,11... | collective-permute-start | bytes 2359304 | tf_op jit(solution)/shard_map/ppermute | solution.py:435
  23.7 2.2 %collective-permute-start.6 = (bf16[128,1024]{1,0:T(8,128)(2,1)S(1)}, bf16[128,1024]{1,0:T(8,128)(2,1)S(1)}, u32[]{:S(2)}, u32[]{:S(2)}) collective-permute-start(bf16[128,1024]{1,0:T(8,128)(2,1)S(1)} %project.2), channel_id=1, source_target_pairs={{0,1},{1,0},{2,3},{3,2},{4,5},{5,4},{6,7},{7,6},{8,9},{9,8},{10,11... | collective-permute-start | bytes 786440 | tf_op jit(solution)/shard_map/ppermute | solution.py:435
  28.5 5.0 %collective-permute-start.10 = (bf16[256,128]{1,0:T(8,128)(2,1)S(1)}, bf16[256,128]{1,0:T(8,128)(2,1)S(1)}, u32[]{:S(2)}, u32[]{:S(2)}) collective-permute-start(bf16[256,128]{1,0:T(8,128)(2,1)S(1)} %get-tuple-element.50), channel_id=1, source_target_pairs={{0,2},{2,0},{1,3},{3,1},{4,6},{6,4},{5,7},{7,5},{8,10},{10,8},{9,1... | collective-permute-start | bytes 196616 | tf_op jit(solution)/shard_map/ppermute | solution.py:435
  29.1 2.0 %copy-start.5 = (s32[4,1]{0,1:T(1,128)S(1)}, s32[4,1]{0,1:T(1,128)}, u32[]{:S(2)}) copy-start(s32[4,1]{0,1:T(1,128)} %param.12) | copy-start | bytes 52
  29.1 4.4 %copy-start.3 = (bf16[4,64,512]{2,1,0:T(8,128)(2,1)S(1)}, bf16[4,64,512]{2,1,0:T(8,128)(2,1)}, u32[]{:S(2)}) copy-start(bf16[4,64,512]{2,1,0:T(8,128)(2,1)} %grid_features.5) | copy-start | bytes 786436
  29.5 8.1 %collective-permute-start.9 = (bf16[256,384]{1,0:T(8,128)(2,1)S(1)}, bf16[256,384]{1,0:T(8,128)(2,1)S(1)}, u32[]{:S(2)}, u32[]{:S(2)}) collective-permute-start(bf16[256,384]{1,0:T(8,128)(2,1)S(1)} %get-tuple-element.48), channel_id=1, source_target_pairs={{0,2},{2,0},{1,3},{3,1},{4,6},{6,4},{5,7},{7,5},{8,10},{10,8},{9,1... | collective-permute-start | bytes 589832 | tf_op jit(solution)/shard_map/ppermute | solution.py:435
  34.1 9.3 %collective-permute-start.14 = (bf16[2,64,128]{2,1,0:T(8,128)(2,1)S(1)}, bf16[2,64,128]{2,1,0:T(8,128)(2,1)S(1)}, u32[]{:S(2)}, u32[]{:S(2)}) collective-permute-start(bf16[2,64,128]{2,1,0:T(8,128)(2,1)S(1)} %get-tuple-element.51), channel_id=1, source_target_pairs={{0,8},{4,12},{8,0},{12,4},{1,9},{5,13},{9,1},{13,5},{2,10},{6,14},... | collective-permute-start | bytes 98312 | tf_op jit(solution)/shard_map/ppermute | solution.py:431
  37.6 5.9 %collective-permute-start.15 = (bf16[2,64,128]{2,1,0:T(8,128)(2,1)S(1)}, bf16[2,64,128]{2,1,0:T(8,128)(2,1)S(1)}, u32[]{:S(2)}, u32[]{:S(2)}) collective-permute-start(bf16[2,64,128]{2,1,0:T(8,128)(2,1)S(1)} %get-tuple-element.58), channel_id=1, source_target_pairs={{0,12},{4,8},{8,4},{12,0},{1,13},{5,9},{9,5},{13,1},{2,14},{6,10},... | collective-permute-start | bytes 98312 | tf_op jit(solution)/shard_map/ppermute | solution.py:431
  38.2 7.5 %collective-permute-start.11 = (bf16[2,64,384]{2,1,0:T(8,128)(2,1)S(1)}, bf16[2,64,384]{2,1,0:T(8,128)(2,1)S(1)}, u32[]{:S(2)}, u32[]{:S(2)}) collective-permute-start(bf16[2,64,384]{2,1,0:T(8,128)(2,1)S(1)} %get-tuple-element.53), channel_id=1, source_target_pairs={{0,8},{4,12},{8,0},{12,4},{1,9},{5,13},{9,1},{13,5},{2,10},{6,14},... | collective-permute-start | bytes 294920 | tf_op jit(solution)/shard_map/ppermute | solution.py:431
  41.7 8.1 %collective-permute-start.13 = (bf16[2,64,512]{2,1,0:T(8,128)(2,1)S(1)}, bf16[2,64,512]{2,1,0:T(8,128)(2,1)S(1)}, u32[]{:S(2)}, u32[]{:S(2)}) collective-permute-start(bf16[2,64,512]{2,1,0:T(8,128)(2,1)S(1)} %get-tuple-element.56), channel_id=1, source_target_pairs={{0,4},{4,0},{8,12},{12,8},{1,5},{5,1},{9,13},{13,9},{2,6},{6,2},{1... | collective-permute-start | bytes 393224 | tf_op jit(solution)/shard_map/ppermute | solution.py:431
  43.4 6.4 %collective-permute-start.12 = (bf16[2,64,384]{2,1,0:T(8,128)(2,1)S(1)}, bf16[2,64,384]{2,1,0:T(8,128)(2,1)S(1)}, u32[]{:S(2)}, u32[]{:S(2)}) collective-permute-start(bf16[2,64,384]{2,1,0:T(8,128)(2,1)S(1)} %get-tuple-element.54), channel_id=1, source_target_pairs={{0,12},{4,8},{8,4},{12,0},{1,13},{5,9},{9,5},{13,1},{2,14},{6,10},... | collective-permute-start | bytes 294920 | tf_op jit(solution)/shard_map/ppermute | solution.py:431

commit v16 on v14

--- a/solution.py
+++ b/solution.py
@@ -265,7 +265,7 @@
             part = lax.rem(m, 2)
             core = lax.rem(m // 2, 2)
             distance = s ^ (m // 4)
-            part = jnp.where(distance == 0, part, part ^ h)
+            part = jnp.where(distance <= 1, part, part ^ h)
             places[b].append((core ^ u, distance * 2 + part))
 
     def scores_of(step):
@@ -444,7 +444,8 @@
     flat = grid_features.reshape(count * rows, half)
     half_unit = run_pick(mesh_nodes)
     far = crossed(half_unit, 2, shards)
-    near = crossed(half_unit, 1, shards)
+    waiting, _ = lax.optimization_barrier((mesh_nodes, half_unit))
+    near = crossed(waiting, 1, shards)
     waiting, _ = lax.optimization_barrier((flat, half_unit))
     other = swapped(waiting, "head")
     flat, gain, wq, wup, wdn, mesh, rest = run_stage(
@@ -460,15 +461,13 @@
         (None, 1, 0, 0, 1, None, "rest"),
     )
     straight = crossed(rest, 3, shards)
-    near, _ = lax.optimization_barrier((near, rest))
-    near_pair = swapped(near, "head")
-    far, _, _ = lax.optimization_barrier((far, near, rest))
+    far, _ = lax.optimization_barrier((far, rest))
     farther = crossed(far, 1, shards)
     far_pair = swapped(far, "head")
     queries, mlp = run_mlp(flat, other, gain, wq, wup, wdn)
-    queries, mlp, far_pair = lax.optimization_barrier((queries, mlp, far_pair))
+    queries, mlp, far_pair, near = lax.optimization_barrier((queries, mlp, far_pair, near))
     blocked = (-1, BLOCK, 2 * half)
-    mine_a = run_project((mesh, near, near_pair, far, far_pair), key_weight, value_weight)
+    mine_a = run_project((mesh, near, far, far_pair), key_weight, value_weight)
     sibling_a = swapped(mine_a, "sub")
     table = run_table(mine_a.reshape(blocked), sibling_a.reshape(blocked), 2 * shards)
     mine_b = run_project((farther, straight), key_weight, value_weight)

time: 49.4 us -> 47.1 us (0.953)
  starting transfers between devices: 23.5 us -> 18.1 us
  waiting for transfers between devices: 9.21 us -> 12.4 us
    ppermute x9, starting transfers between devices: 17.2 us -> 13.8 us  [crossed(): return lax.ppermute(x, 'shard', [(i, i ^ distance) for i in range(size)])]
    ppermute x9, waiting for transfers between devices: 5.77 us -> 7.93 us  [crossed(): return lax.ppermute(x, 'shard', [(i, i ^ distance) for i in range(size)])]
    ppermute x7 -> x6, starting transfers between devices: 6.28 us -> 4.27 us  [swapped(): return lax.ppermute(x, axis, [(0, 1), (1, 0)])]
    ppermute x7 -> x6, waiting for transfers between devices: 3.44 us -> 4.42 us  [swapped(): return lax.ppermute(x, axis, [(0, 1), (1, 0)])]
  transfers between devices with their start and end apart: 16 -> 15, of which waited for: 5 -> 11; matrix products, arithmetic and copies ran while one was open for 0% -> 0% of each run, Pallas kernels for 24% -> 26%
where the time goes in v16:
time: 47.1 us; the launch traced here: 46.9 us
  starting transfers between devices  18.1 us (38%)
  Pallas kernels  16.2 us (34%)
  waiting for transfers between devices  12.4 us (26%)
    ppermute x9, starting transfers between devices, crossed(): return lax.ppermute(x, 'shard', [(i, i ^ distance) for i in range(size)])  13.8 us
    ppermute x9, waiting for transfers between devices, crossed(): return lax.ppermute(x, 'shard', [(i, i ^ distance) for i in range(size)])  7.93 us
    ppermute x6, waiting for transfers between devices, swapped(): return lax.ppermute(x, axis, [(0, 1), (1, 0)])  4.42 us
    ppermute x6, starting transfers between devices, swapped(): return lax.ppermute(x, axis, [(0, 1), (1, 0)])  4.27 us
    pallas_call x1, Pallas kernels, run_stage(): pl.pallas_call(functools.partial(stage_kernel, axes), out_shape=tuple((ja...  4.1 us
    pallas_call x1, Pallas kernels, run_mlp(): pl.pallas_call(mlp_kernel, out_shape=(jax.ShapeDtypeStruct((rows, wq.shap...  3.33 us
    pallas_call x1, Pallas kernels, run_attend(): pl.pallas_call(attend_kernel, out_shape=(part, part, jax.ShapeDtypeStruct...  2.52 us
    pallas_call x3, Pallas kernels, run_combine(): pl.pallas_call(functools.partial(combine_kernel, chunks, distances), out_...  1.95 us
  transfers between devices with their start and end apart: 15, of which 11 were waited for; matrix products, arithmetic and copies ran while one was open for 0% of the time, Pallas kernels for 26%

profile of v16, /device:TPU:0, one launch (start us, length us, event | category | flops | bytes accessed | tf_op | source)
XLA Modules:
  0.0 46.9 jit_solution(1689792333506826172)
XLA Ops:
  0.0 0.9 %pick.1 = bf16[64,1024]{1,0:T(8,128)(2,1)S(1)} custom-call(bf16[128,1024]{1,0:T(8,128)(2,1)} %mesh.1), custom_call_target="tpu_custom_call" | custom-call | bytes 524288 | tf_op jit(solution)/shard_map/pick/pallas_call | solution.py:112
  0.9 4.1 %collective-permute-start.1 = (bf16[64,1024]{1,0:T(8,128)(2,1)S(1)}, bf16[64,1024]{1,0:T(8,128)(2,1)S(1)}, u32[]{:S(2)}, u32[]{:S(2)}) collective-permute-start(bf16[64,1024]{1,0:T(8,128)(2,1)S(1)} %pick.1), channel_id=1, source_target_pairs={{0,8},{4,12},{8,0},{12,4},{1,9},{5,13},{9,1},{13,5},{2,10},{6,14},... | collective-permute-start | bytes 393224 | tf_op jit(solution)/shard_map/ppermute | solution.py:422
  5.0 1.5 %collective-permute-start = (bf16[256,512]{1,0:T(8,128)(2,1)}, bf16[256,512]{1,0:T(8,128)(2,1)S(1)}, u32[]{:S(2)}, u32[]{:S(2)}) collective-permute-start(bf16[256,512]{1,0:T(8,128)(2,1)} %bitcast.8), channel_id=1, source_target_pairs={{0,2},{2,0},{1,3},{3,1},{4,6},{6,4},{5,7},{7,5},{8,10},{10,8},{9,1... | collective-permute-start | bytes 786440 | tf_op jit(solution)/shard_map/ppermute | solution.py:426
  6.5 1.6 %collective-permute-start.3 = (bf16[128,1024]{1,0:T(8,128)(2,1)}, bf16[128,1024]{1,0:T(8,128)(2,1)S(1)}, u32[]{:S(2)}, u32[]{:S(2)}) collective-permute-start(bf16[128,1024]{1,0:T(8,128)(2,1)} %mesh.1), channel_id=1, source_target_pairs={{0,4},{4,0},{8,12},{12,8},{1,5},{5,1},{9,13},{13,9},{2,6},{6,2},{1... | collective-permute-start | bytes 786440 | tf_op jit(solution)/shard_map/ppermute | solution.py:422
  8.1 4.1 %stage.1 = (bf16[256,512]{1,0:T(8,128)(2,1)S(1)}, f32[1,1024]{1,0:T(1,128)S(1)}, bf16[1024,512]{1,0:T(8,128)(2,1)S(1)}, bf16[1024,2048]{1,0:T(8,128)(2,1)S(1)}, ...) custom-call(bf16[256,512]{1,0:T(8,128)(2,1)} %bitcast.9, ...), custom_call_target="tpu_custom_call" | custom-call | flops 20451328000 | bytes 204513280 | tf_op jit(solution)/shard_map/stage/pallas_call | solution.py:162
  12.2 0.3 collective-permute-start.5
  12.5 0.0 collective-permute-done.1.refs_2_
  12.5 0.5 %collective-permute-start.2 = (bf16[64,1024]{1,0:T(8,128)(2,1)S(1)}, bf16[64,1024]{1,0:T(8,128)(2,1)S(1)}, u32[]{:S(2)}, u32[]{:S(2)}) collective-permute-start(bf16[64,1024]{1,0:T(8,128)(2,1)S(1)} %collective-permute-done.1.refs_2_), channel_id=1, source_target_pairs={{0,2},{2,0},{1,3},{3,1},{4,6},{6,4},{5,7},{7,5},{8,10},{10,8},{9,1... | collective-permute-start | bytes 393224 | tf_op jit(solution)/shard_map/ppermute | solution.py:426
  13.0 0.7 %collective-permute-start.4 = (bf16[64,1024]{1,0:T(8,128)(2,1)S(1)}, bf16[64,1024]{1,0:T(8,128)(2,1)S(1)}, u32[]{:S(2)}, u32[]{:S(2)}) collective-permute-start(bf16[64,1024]{1,0:T(8,128)(2,1)S(1)} %collective-permute-done.1.refs_2_), channel_id=1, source_target_pairs={{0,4},{4,0},{8,12},{12,8},{1,5},{5,1},{9,13},{13,9},{2,6},{6,2},{1... | collective-permute-start | bytes 393224 | tf_op jit(solution)/shard_map/ppermute | solution.py:422
  13.7 0.0 collective-permute-done.other
  13.7 0.0 copy-start
  13.7 0.0 copy-start.1
  13.7 3.3 %mlp.1 = (bf16[256,512]{1,0:T(8,128)(2,1)S(1)}, f32[256,1024]{1,0:T(8,128)S(1)}) custom-call(bf16[256,512]{1,0:T(8,128)(2,1)S(1)} %get-tuple-element.34.own, bf16[256,512]{1,0:T(8,128)(2,1)S(1)} %collective-permute-done.other, f32[1,1024]{1,0:T(1,128)S(1)} %get-tuple-element.36.gain, bf16[1024,512]{1,0:T(8,128)(2,1)S(1)} %get-tuple-element.37.wq, ...), custom_call_target="tpu_custom_call" | custom-call | flops 2415919104 | bytes 9437184 | tf_op jit(solution)/shard_map/mlp/pallas_call | solution.py:85
  17.1 0.4 collective-permute-done.2.refs_3_
  17.5 1.2 %collective-permute-done.3.refs_1_ = bf16[128,1024]{1,0:T(8,128)(2,1)S(1)} collective-permute-done((bf16[128,1024]{1,0:T(8,128)(2,1)}, bf16[128,1024]{1,0:T(8,128)(2,1)S(1)}, u32[]{:S(2)}, u32[]{:S(2)}) %collective-permute-start.3) | collective-permute-done | bytes 262176 | tf_op jit(solution)/shard_map/ppermute | solution.py:422
  18.7 0.0 copy-done
  18.7 0.0 copy-done.1
  18.7 1.0 %project.3 = bf16[384,1024]{1,0:T(8,128)(2,1)S(1)} custom-call(bf16[128,1024]{1,0:T(8,128)(2,1)S(1)} %get-tuple-element.46.refs_0_, bf16[128,1024]{1,0:T(8,128)(2,1)S(1)} %collective-permute-done.3.refs_1_, bf16[64,1024]{1,0:T(8,128)(2,1)S(1)} %collective-permute-done.1.refs_2_, bf16[64,1024]{1,0:T(8,128)(2,1)S(1)} %collective-permute-done.2.refs_3_, ...), custom_call_target="tpu_custom_call" | custom-call | flops 60397977600 | bytes 275251200 | tf_op jit(solution)/shard_map/project/pallas_call | solution.py:190
  19.7 0.0 copy-start.2
  19.7 0.0 copy-start.4
  19.7 0.1 collective-permute-start.7
  19.8 0.2 collective-permute-done.5.refs_1_
  20.0 1.5 %collective-permute-done.4.refs_0_ = bf16[64,1024]{1,0:T(8,128)(2,1)S(1)} collective-permute-done((bf16[64,1024]{1,0:T(8,128)(2,1)S(1)}, bf16[64,1024]{1,0:T(8,128)(2,1)S(1)}, u32[]{:S(2)}, u32[]{:S(2)}) %collective-permute-start.4) | collective-permute-done | bytes 131104 | tf_op jit(solution)/shard_map/ppermute | solution.py:422
  21.5 0.4 project.2
  21.9 0.1 collective-permute-start.6
  22.0 0.1 collective-permute-done.7
  22.1 0.1 table.1.table_in
  22.2 1.4 %collective-permute-done.6 = bf16[128,1024]{1,0:T(8,128)(2,1)S(1)} collective-permute-done((bf16[128,1024]{1,0:T(8,128)(2,1)S(1)}, bf16[128,1024]{1,0:T(8,128)(2,1)S(1)}, u32[]{:S(2)}, u32[]{:S(2)}) %collective-permute-start.6) | collective-permute-done | bytes 262176 | tf_op jit(solution)/shard_map/ppermute | solution.py:426
  23.5 0.0 copy-done.2
  23.5 0.0 copy-done.4
  23.5 2.5 %attend.1 = (bf16[256,128]{1,0:T(8,128)(2,1)S(1)}, bf16[256,128]{1,0:T(8,128)(2,1)S(1)}, bf16[256,512]{1,0:T(8,128)(2,1)S(1)}, bf16[2,8,64,1024]{3,2,1,0:T(8,128)(2,1)S(1)}) custom-call(s32[4,8]{1,0:T(4,128)S(1)} %copy-done.4, bf16[256,512]{1,0:T(8,128)(2,1)S(1)} %get-tuple-element.45.q, ...), custom_call_target="tpu_custom_call", output_to_operand_aliasing={{3}: (4, {})} | custom-call | flops 13421772800 | bytes 41943040 | tf_op jit(solution)/shard_map/attend/pallas_call | solution.py:305
  26.1 0.7 %collective-permute-start.9 = (bf16[256,128]{1,0:T(8,128)(2,1)S(1)}, bf16[256,128]{1,0:T(8,128)(2,1)S(1)}, u32[]{:S(2)}, u32[]{:S(2)}) collective-permute-start(bf16[256,128]{1,0:T(8,128)(2,1)S(1)} %get-tuple-element.54), channel_id=1, source_target_pairs={{0,2},{2,0},{1,3},{3,1},{4,6},{6,4},{5,7},{7,5},{8,10},{10,8},{9,1... | collective-permute-start | bytes 196616 | tf_op jit(solution)/shard_map/ppermute | solution.py:426
  26.7 0.0 copy-start.5
  26.7 0.0 copy-start.3
  26.7 0.4 project_out.1
  27.2 1.5 %collective-permute-start.8 = (bf16[256,384]{1,0:T(8,128)(2,1)S(1)}, bf16[256,384]{1,0:T(8,128)(2,1)S(1)}, u32[]{:S(2)}, u32[]{:S(2)}) collective-permute-start(bf16[256,384]{1,0:T(8,128)(2,1)S(1)} %get-tuple-element.52), channel_id=1, source_target_pairs={{0,2},{2,0},{1,3},{3,1},{4,6},{6,4},{5,7},{7,5},{8,10},{10,8},{9,1... | collective-permute-start | bytes 589832 | tf_op jit(solution)/shard_map/ppermute | solution.py:426
  28.7 0.0 copy-done.5
  28.7 0.1 copy.15.owners
  28.7 2.3 %collective-permute-done.9.refs_1_.refs_2_ = bf16[256,128]{1,0:T(8,128)(2,1)S(1)} collective-permute-done((bf16[256,128]{1,0:T(8,128)(2,1)S(1)}, bf16[256,128]{1,0:T(8,128)(2,1)S(1)}, u32[]{:S(2)}, u32[]{:S(2)}) %collective-permute-start.9) | collective-permute-done | bytes 65568 | tf_op jit(solution)/shard_map/ppermute | solution.py:426
  31.1 0.0 copy-done.3
  31.1 0.6 %combine.3 = (bf16[2,64,128]{2,1,0:T(8,128)(2,1)S(1)}, bf16[2,64,128]{2,1,0:T(8,128)(2,1)S(1)}) custom-call(s32[4,1]{1,0:T(4,128)S(1)} %copy.15.owners, bf16[4,64,512]{2,1,0:T(8,128)(2,1)S(1)} %copy-done.3, bf16[256,128]{1,0:T(8,128)(2,1)S(1)} %get-tuple-element.53.refs_0_, bf16[256,128]{1,0:T(8,128)(2,1)S(1)} %collective-permute-done.9.refs_1_.refs_2_), custom_call_target="tpu_custom_call" | custom-call | flops 1966080000 | bytes 52428800 | tf_op jit(solution)/shard_map/combine/pallas_call | solution.py:377
  31.7 0.2 collective-permute-start.13
  31.9 2.5 %collective-permute-start.14 = (bf16[2,64,128]{2,1,0:T(8,128)(2,1)S(1)}, bf16[2,64,128]{2,1,0:T(8,128)(2,1)S(1)}, u32[]{:S(2)}, u32[]{:S(2)}) collective-permute-start(bf16[2,64,128]{2,1,0:T(8,128)(2,1)S(1)} %get-tuple-element.62), channel_id=1, source_target_pairs={{0,12},{4,8},{8,4},{12,0},{1,13},{5,9},{9,5},{13,1},{2,14},{6,10},... | collective-permute-start | bytes 98312 | tf_op jit(solution)/shard_map/ppermute | solution.py:422
  34.3 0.3 collective-permute-done.8.refs_1_.refs_3_
  34.6 0.7 %combine.4 = (bf16[2,64,384]{2,1,0:T(8,128)(2,1)S(1)}, bf16[2,64,384]{2,1,0:T(8,128)(2,1)S(1)}) custom-call(s32[4,1]{1,0:T(4,128)S(1)} %copy.15.owners, bf16[4,64,512]{2,1,0:T(8,128)(2,1)S(1)} %copy-done.3, bf16[256,384]{1,0:T(8,128)(2,1)S(1)} %get-tuple-element.51.refs_0_.refs_1_, bf16[256,384]{1,0:T(8,128)(2,1)S(1)} %collective-permute-done.8.refs_1_.refs_3_), custom_call_target="tpu_custom_call" | custom-call | flops 5898240000 | bytes 157286400 | tf_op jit(solution)/shard_map/combine/pallas_call | solution.py:377
  35.3 1.8 %collective-permute-start.10 = (bf16[2,64,384]{2,1,0:T(8,128)(2,1)S(1)}, bf16[2,64,384]{2,1,0:T(8,128)(2,1)S(1)}, u32[]{:S(2)}, u32[]{:S(2)}) collective-permute-start(bf16[2,64,384]{2,1,0:T(8,128)(2,1)S(1)} %get-tuple-element.57), channel_id=1, source_target_pairs={{0,8},{4,12},{8,0},{12,4},{1,9},{5,13},{9,1},{13,5},{2,10},{6,14},... | collective-permute-start | bytes 294920 | tf_op jit(solution)/shard_map/ppermute | solution.py:422
  37.0 0.7 %combine.5 = (bf16[2,64,512]{2,1,0:T(8,128)(2,1)S(1)}, bf16[2,64,512]{2,1,0:T(8,128)(2,1)S(1)}) custom-call(s32[4,1]{1,0:T(4,128)S(1)} %copy.15.owners, bf16[4,64,512]{2,1,0:T(8,128)(2,1)S(1)} %copy-done.3, bf16[256,128]{1,0:T(8,128)(2,1)S(1)} %get-tuple-element.53.refs_0_, bf16[256,384]{1,0:T(8,128)(2,1)S(1)} %get-tuple-element.51.refs_0_.refs_1_, ...), custom_call_target="tpu_custom_call" | custom-call | flops 7864320000 | bytes 209715200 | tf_op jit(solution)/shard_map/combine/pallas_call | solution.py:377
  37.7 1.4 %collective-permute-start.12 = (bf16[2,64,512]{2,1,0:T(8,128)(2,1)S(1)}, bf16[2,64,512]{2,1,0:T(8,128)(2,1)S(1)}, u32[]{:S(2)}, u32[]{:S(2)}) collective-permute-start(bf16[2,64,512]{2,1,0:T(8,128)(2,1)S(1)} %get-tuple-element.60), channel_id=1, source_target_pairs={{0,4},{4,0},{8,12},{12,8},{1,5},{5,1},{9,13},{13,9},{2,6},{6,2},{1... | collective-permute-start | bytes 393224 | tf_op jit(solution)/shard_map/ppermute | solution.py:422
  39.1 1.3 %collective-permute-start.11 = (bf16[2,64,384]{2,1,0:T(8,128)(2,1)S(1)}, bf16[2,64,384]{2,1,0:T(8,128)(2,1)S(1)}, u32[]{:S(2)}, u32[]{:S(2)}) collective-permute-start(bf16[2,64,384]{2,1,0:T(8,128)(2,1)S(1)} %get-tuple-element.58), channel_id=1, source_target_pairs={{0,12},{4,8},{8,4},{12,0},{1,13},{5,9},{9,5},{13,1},{2,14},{6,10},... | collective-permute-start | bytes 294920 | tf_op jit(solution)/shard_map/ppermute | solution.py:422
  40.5 0.0 collective-permute-done.13.refs_0_
  40.5 0.0 collective-permute-done.14.refs_1_
  40.5 0.6 %place.2.refs_4_ = bf16[8,64,512]{2,1,0:T(8,128)(2,1)} custom-call(bf16[2,64,128]{2,1,0:T(8,128)(2,1)S(1)} %collective-permute-done.13.refs_0_, bf16[2,64,128]{2,1,0:T(8,128)(2,1)S(1)} %collective-permute-done.14.refs_1_), custom_call_target="tpu_custom_call" | custom-call | flops 13107200000 | tf_op jit(solution)/shard_map/place/pallas_call | solution.py:406
  41.1 2.2 %collective-permute-done.10.refs_0_ = bf16[2,64,384]{2,1,0:T(8,128)(2,1)S(1)} collective-permute-done((bf16[2,64,384]{2,1,0:T(8,128)(2,1)S(1)}, bf16[2,64,384]{2,1,0:T(8,128)(2,1)S(1)}, u32[]{:S(2)}, u32[]{:S(2)}) %collective-permute-start.10) | collective-permute-done | bytes 98336 | tf_op jit(solution)/shard_map/ppermute | solution.py:422
  43.3 2.7 %collective-permute-done.11.refs_1_ = bf16[2,64,384]{2,1,0:T(8,128)(2,1)S(1)} collective-permute-done((bf16[2,64,384]{2,1,0:T(8,128)(2,1)S(1)}, bf16[2,64,384]{2,1,0:T(8,128)(2,1)S(1)}, u32[]{:S(2)}, u32[]{:S(2)}) %collective-permute-start.11) | collective-permute-done | bytes 98336 | tf_op jit(solution)/shard_map/ppermute | solution.py:422
  46.0 0.1 collective-permute-done.12.refs_2_
  46.1 0.8 %place.3 = bf16[8,64,512]{2,1,0:T(8,128)(2,1)} custom-call(bf16[2,64,384]{2,1,0:T(8,128)(2,1)S(1)} %collective-permute-done.10.refs_0_, bf16[2,64,384]{2,1,0:T(8,128)(2,1)S(1)} %collective-permute-done.11.refs_1_, bf16[2,64,512]{2,1,0:T(8,128)(2,1)S(1)} %collective-permute-done.12.refs_2_, ...), custom_call_target="tpu_custom_call", output_to_operand_aliasing={{}: (4, {})} | custom-call | flops 91750400000 | tf_op jit(solution)/shard_map/place/pallas_call | solution.py:406
Async XLA Ops:
  0.9 11.6 %collective-permute-start.1 = (bf16[64,1024]{1,0:T(8,128)(2,1)S(1)}, bf16[64,1024]{1,0:T(8,128)(2,1)S(1)}, u32[]{:S(2)}, u32[]{:S(2)}) collective-permute-start(bf16[64,1024]{1,0:T(8,128)(2,1)S(1)} %pick.1), channel_id=1, source_target_pairs={{0,8},{4,12},{8,0},{12,4},{1,9},{5,13},{9,1},{13,5},{2,10},{6,14},... | collective-permute-start | bytes 393224 | tf_op jit(solution)/shard_map/ppermute | solution.py:422
  5.0 8.7 %collective-permute-start = (bf16[256,512]{1,0:T(8,128)(2,1)}, bf16[256,512]{1,0:T(8,128)(2,1)S(1)}, u32[]{:S(2)}, u32[]{:S(2)}) collective-permute-start(bf16[256,512]{1,0:T(8,128)(2,1)} %bitcast.8), channel_id=1, source_target_pairs={{0,2},{2,0},{1,3},{3,1},{4,6},{6,4},{5,7},{7,5},{8,10},{10,8},{9,1... | collective-permute-start | bytes 786440 | tf_op jit(solution)/shard_map/ppermute | solution.py:426
  6.5 12.2 %collective-permute-start.3 = (bf16[128,1024]{1,0:T(8,128)(2,1)}, bf16[128,1024]{1,0:T(8,128)(2,1)S(1)}, u32[]{:S(2)}, u32[]{:S(2)}) collective-permute-start(bf16[128,1024]{1,0:T(8,128)(2,1)} %mesh.1), channel_id=1, source_target_pairs={{0,4},{4,0},{8,12},{12,8},{1,5},{5,1},{9,13},{13,9},{2,6},{6,2},{1... | collective-permute-start | bytes 786440 | tf_op jit(solution)/shard_map/ppermute | solution.py:422
  12.2 7.8 %collective-permute-start.5 = (bf16[64,1024]{1,0:T(8,128)(2,1)S(1)}, bf16[64,1024]{1,0:T(8,128)(2,1)S(1)}, u32[]{:S(2)}, u32[]{:S(2)}) collective-permute-start(bf16[64,1024]{1,0:T(8,128)(2,1)S(1)} %get-tuple-element.42), channel_id=1, source_target_pairs={{0,12},{4,8},{8,4},{12,0},{1,13},{5,9},{9,5},{13,1},{2,14},{6,10},... | collective-permute-start | bytes 393224 | tf_op jit(solution)/shard_map/ppermute | solution.py:422
  12.5 5.0 %collective-permute-start.2 = (bf16[64,1024]{1,0:T(8,128)(2,1)S(1)}, bf16[64,1024]{1,0:T(8,128)(2,1)S(1)}, u32[]{:S(2)}, u32[]{:S(2)}) collective-permute-start(bf16[64,1024]{1,0:T(8,128)(2,1)S(1)} %collective-permute-done.1.refs_2_), channel_id=1, source_target_pairs={{0,2},{2,0},{1,3},{3,1},{4,6},{6,4},{5,7},{7,5},{8,10},{10,8},{9,1... | collective-permute-start | bytes 393224 | tf_op jit(solution)/shard_map/ppermute | solution.py:426
  13.0 8.5 %collective-permute-start.4 = (bf16[64,1024]{1,0:T(8,128)(2,1)S(1)}, bf16[64,1024]{1,0:T(8,128)(2,1)S(1)}, u32[]{:S(2)}, u32[]{:S(2)}) collective-permute-start(bf16[64,1024]{1,0:T(8,128)(2,1)S(1)} %collective-permute-done.1.refs_2_), channel_id=1, source_target_pairs={{0,4},{4,0},{8,12},{12,8},{1,5},{5,1},{9,13},{13,9},{2,6},{6,2},{1... | collective-permute-start | bytes 393224 | tf_op jit(solution)/shard_map/ppermute | solution.py:422
  13.7 5.0 %copy-start = (bf16[1024,512]{1,0:T(8,128)(2,1)S(1)}, bf16[1024,512]{1,0:T(8,128)(2,1)}, u32[]{:S(2)}) copy-start(bf16[1024,512]{1,0:T(8,128)(2,1)} %refs_4_.3) | copy-start | bytes 3145732
  13.7 5.0 %copy-start.1 = (bf16[1024,512]{1,0:T(8,128)(2,1)S(1)}, bf16[1024,512]{1,0:T(8,128)(2,1)}, u32[]{:S(2)}) copy-start(bf16[1024,512]{1,0:T(8,128)(2,1)} %refs_5_.3) | copy-start | bytes 3145732
  19.7 3.8 %copy-start.2 = (bf16[512,1024]{1,0:T(8,128)(2,1)S(1)}, bf16[512,1024]{1,0:T(8,128)(2,1)}, u32[]{:S(2)}) copy-start(bf16[512,1024]{1,0:T(8,128)(2,1)} %wo.3) | copy-start | bytes 3145732
  19.7 3.8 %copy-start.4 = (s32[4,8]{1,0:T(4,128)S(1)}, s32[4,8]{1,0:T(4,128)}, u32[]{:S(2)}) copy-start(s32[4,8]{1,0:T(4,128)} %adjacency.1) | copy-start | bytes 388
  19.7 2.4 %collective-permute-start.7 = (bf16[384,1024]{1,0:T(8,128)(2,1)S(1)}, bf16[384,1024]{1,0:T(8,128)(2,1)S(1)}, u32[]{:S(2)}, u32[]{:S(2)}) collective-permute-start(bf16[384,1024]{1,0:T(8,128)(2,1)S(1)} %project.3), channel_id=1, source_target_pairs={{0,1},{1,0},{2,3},{3,2},{4,5},{5,4},{6,7},{7,6},{8,9},{9,8},{10,11... | collective-permute-start | bytes 2359304 | tf_op jit(solution)/shard_map/ppermute | solution.py:426
  21.9 1.6 %collective-permute-start.6 = (bf16[128,1024]{1,0:T(8,128)(2,1)S(1)}, bf16[128,1024]{1,0:T(8,128)(2,1)S(1)}, u32[]{:S(2)}, u32[]{:S(2)}) collective-permute-start(bf16[128,1024]{1,0:T(8,128)(2,1)S(1)} %project.2), channel_id=1, source_target_pairs={{0,1},{1,0},{2,3},{3,2},{4,5},{5,4},{6,7},{7,6},{8,9},{9,8},{10,11... | collective-permute-start | bytes 786440 | tf_op jit(solution)/shard_map/ppermute | solution.py:426
  26.1 5.0 %collective-permute-start.9 = (bf16[256,128]{1,0:T(8,128)(2,1)S(1)}, bf16[256,128]{1,0:T(8,128)(2,1)S(1)}, u32[]{:S(2)}, u32[]{:S(2)}) collective-permute-start(bf16[256,128]{1,0:T(8,128)(2,1)S(1)} %get-tuple-element.54), channel_id=1, source_target_pairs={{0,2},{2,0},{1,3},{3,1},{4,6},{6,4},{5,7},{7,5},{8,10},{10,8},{9,1... | collective-permute-start | bytes 196616 | tf_op jit(solution)/shard_map/ppermute | solution.py:426
  26.7 1.9 %copy-start.5 = (s32[4,1]{0,1:T(1,128)S(1)}, s32[4,1]{0,1:T(1,128)}, u32[]{:S(2)}) copy-start(s32[4,1]{0,1:T(1,128)} %param.12) | copy-start | bytes 52
  26.7 4.4 %copy-start.3 = (bf16[4,64,512]{2,1,0:T(8,128)(2,1)S(1)}, bf16[4,64,512]{2,1,0:T(8,128)(2,1)}, u32[]{:S(2)}) copy-start(bf16[4,64,512]{2,1,0:T(8,128)(2,1)} %grid_features.5) | copy-start | bytes 786436
  27.2 7.4 %collective-permute-start.8 = (bf16[256,384]{1,0:T(8,128)(2,1)S(1)}, bf16[256,384]{1,0:T(8,128)(2,1)S(1)}, u32[]{:S(2)}, u32[]{:S(2)}) collective-permute-start(bf16[256,384]{1,0:T(8,128)(2,1)S(1)} %get-tuple-element.52), channel_id=1, source_target_pairs={{0,2},{2,0},{1,3},{3,1},{4,6},{6,4},{5,7},{7,5},{8,10},{10,8},{9,1... | collective-permute-start | bytes 589832 | tf_op jit(solution)/shard_map/ppermute | solution.py:426
  31.7 8.7 %collective-permute-start.13 = (bf16[2,64,128]{2,1,0:T(8,128)(2,1)S(1)}, bf16[2,64,128]{2,1,0:T(8,128)(2,1)S(1)}, u32[]{:S(2)}, u32[]{:S(2)}) collective-permute-start(bf16[2,64,128]{2,1,0:T(8,128)(2,1)S(1)} %get-tuple-element.55), channel_id=1, source_target_pairs={{0,8},{4,12},{8,0},{12,4},{1,9},{5,13},{9,1},{13,5},{2,10},{6,14},... | collective-permute-start | bytes 98312 | tf_op jit(solution)/shard_map/ppermute | solution.py:422
  31.9 8.6 %collective-permute-start.14 = (bf16[2,64,128]{2,1,0:T(8,128)(2,1)S(1)}, bf16[2,64,128]{2,1,0:T(8,128)(2,1)S(1)}, u32[]{:S(2)}, u32[]{:S(2)}) collective-permute-start(bf16[2,64,128]{2,1,0:T(8,128)(2,1)S(1)} %get-tuple-element.62), channel_id=1, source_target_pairs={{0,12},{4,8},{8,4},{12,0},{1,13},{5,9},{9,5},{13,1},{2,14},{6,10},... | collective-permute-start | bytes 98312 | tf_op jit(solution)/shard_map/ppermute | solution.py:422
  35.3 8.1 %collective-permute-start.10 = (bf16[2,64,384]{2,1,0:T(8,128)(2,1)S(1)}, bf16[2,64,384]{2,1,0:T(8,128)(2,1)S(1)}, u32[]{:S(2)}, u32[]{:S(2)}) collective-permute-start(bf16[2,64,384]{2,1,0:T(8,128)(2,1)S(1)} %get-tuple-element.57), channel_id=1, source_target_pairs={{0,8},{4,12},{8,0},{12,4},{1,9},{5,13},{9,1},{13,5},{2,10},{6,14},... | collective-permute-start | bytes 294920 | tf_op jit(solution)/shard_map/ppermute | solution.py:422
  37.7 8.4 %collective-permute-start.12 = (bf16[2,64,512]{2,1,0:T(8,128)(2,1)S(1)}, bf16[2,64,512]{2,1,0:T(8,128)(2,1)S(1)}, u32[]{:S(2)}, u32[]{:S(2)}) collective-permute-start(bf16[2,64,512]{2,1,0:T(8,128)(2,1)S(1)} %get-tuple-element.60), channel_id=1, source_target_pairs={{0,4},{4,0},{8,12},{12,8},{1,5},{5,1},{9,13},{13,9},{2,6},{6,2},{1... | collective-permute-start | bytes 393224 | tf_op jit(solution)/shard_map/ppermute | solution.py:422
  39.1 6.9 %collective-permute-start.11 = (bf16[2,64,384]{2,1,0:T(8,128)(2,1)S(1)}, bf16[2,64,384]{2,1,0:T(8,128)(2,1)S(1)}, u32[]{:S(2)}, u32[]{:S(2)}) collective-permute-start(bf16[2,64,384]{2,1,0:T(8,128)(2,1)S(1)} %get-tuple-element.58), channel_id=1, source_target_pairs={{0,12},{4,8},{8,4},{12,0},{1,13},{5,9},{9,5},{13,1},{2,14},{6,10},... | collective-permute-start | bytes 294920 | tf_op jit(solution)/shard_map/ppermute | solution.py:422

commit v17 on v16

--- a/solution.py
+++ b/solution.py
@@ -101,26 +101,6 @@
     )(own, other, gain, wq, wup, wdn)
 
 
-def pick_kernel(mesh, out, sem):
-    first = pl.multiple_of(lax.axis_index("head") * BLOCK, BLOCK)
-    copy = pltpu.make_async_copy(mesh.at[pl.ds(first, BLOCK), :], out, sem)
-    copy.start()
-    copy.wait()
-
-
-def run_pick(mesh):
-    return pl.pallas_call(
-        pick_kernel,
-        out_shape=jax.ShapeDtypeStruct((BLOCK, mesh.shape[1]), mesh.dtype),
-        in_specs=[whole(pltpu.HBM)],
-        out_specs=whole(pltpu.VMEM),
-        scratch_shapes=[pltpu.SemaphoreType.DMA(())],
-        compiler_params=params(4),
-        cost_estimate=pl.CostEstimate(flops=0, bytes_accessed=4 * mesh.size, transcendentals=0),
-        name="pick",
-    )(in_hbm(mesh))
-
-
 def stage_kernel(axes, *refs):
     sources, targets, sem = refs[: len(axes)], refs[len(axes) : -1], refs[-1]
     h = lax.axis_index("head")
@@ -142,9 +122,6 @@
         if axis is None:
             add(source, target)
             continue
-        if axis == "rest":
-            add(source.at[pl.ds(pl.multiple_of((1 - h) * BLOCK, BLOCK), BLOCK), :], target)
-            continue
         half = source.shape[axis] // 2
         for part, head in enumerate((1 - h, h)):
             span = pl.ds(pl.multiple_of(head * half, half), half)
@@ -161,10 +138,7 @@
     size = sum(2 * array.size for array in arrays)
     return pl.pallas_call(
         functools.partial(stage_kernel, axes),
-        out_shape=tuple(
-            jax.ShapeDtypeStruct((BLOCK,) + array.shape[1:] if axis == "rest" else array.shape, array.dtype)
-            for array, axis in zip(arrays, axes)
-        ),
+        out_shape=tuple(jax.ShapeDtypeStruct(array.shape, array.dtype) for array in arrays),
         in_specs=[whole(pltpu.HBM)] * len(arrays),
         out_specs=tuple(vmem(len(arrays))),
         scratch_shapes=[pltpu.SemaphoreType.DMA((4 * len(arrays),))],
@@ -177,21 +151,36 @@
 
 
 def project_kernel(*refs):
-    pieces, (wk, wv, out) = refs[:-3], refs[-3:]
+    *pieces, first, second, wk, wv, out, rows_s = refs
     width = wk.shape[1]
-    rows = jnp.concatenate([piece[...] for piece in pieces], axis=0)
-    out[:, :width] = dot(rows, wk[...]).astype(jnp.bfloat16)
-    out[:, width:] = dot(rows, wv[...]).astype(jnp.bfloat16)
+    fixed = sum(piece.shape[0] for piece in pieces)
+    start = 0
+    for piece in pieces:
+        rows_s[start : start + piece.shape[0], :] = piece[...]
+        start += piece.shape[0]
+    same = lax.axis_index("head") == lax.axis_index("sub")
+
+    @pl.when(same)
+    def _():
+        rows_s[fixed:, :] = first[...]
+
+    @pl.when(jnp.logical_not(same))
+    def _():
+        rows_s[fixed:, :] = second[...]
+
+    out[:, :width] = dot(rows_s[...], wk[...]).astype(jnp.bfloat16)
+    out[:, width:] = dot(rows_s[...], wv[...]).astype(jnp.bfloat16)
 
 
 def run_project(pieces, wk, wv):
-    rows = sum(piece.shape[0] for piece in pieces)
+    rows = sum(piece.shape[0] for piece in pieces[:-1])
     depth, width = wk.shape
     return pl.pallas_call(
         project_kernel,
         out_shape=jax.ShapeDtypeStruct((rows, 2 * width), jnp.bfloat16),
         in_specs=vmem(len(pieces) + 2),
         out_specs=whole(pltpu.VMEM),
+        scratch_shapes=[pltpu.VMEM((rows, depth), jnp.bfloat16)],
         compiler_params=params(8),
         cost_estimate=pl.CostEstimate(
             flops=300 * rows * depth * width,
@@ -245,7 +234,6 @@
 ):
     del table_in
     s = lax.axis_index("shard")
-    h = lax.axis_index("head")
     u = lax.axis_index("sub")
     half = wo.shape[0]
     ready = table.shape[1] - mine.shape[0]
@@ -265,7 +253,6 @@
             part = lax.rem(m, 2)
             core = lax.rem(m // 2, 2)
             distance = s ^ (m // 4)
-            part = jnp.where(distance <= 1, part, part ^ h)
             places[b].append((core ^ u, distance * 2 + part))
 
     def scores_of(step):
@@ -422,6 +409,19 @@
     return lax.ppermute(x, "shard", [(i, i ^ distance) for i in range(size)])
 
 
+def fetched(x, distance, same, size):
+    pairs = []
+    for i in range(size):
+        for h in range(2):
+            u = h if same else 1 - h
+            pairs.append((4 * i + 2 * h + u, 4 * (i ^ distance) + 2 * h + u))
+    return lax.ppermute(x, ("shard", "head", "sub"), pairs)
+
+
+def handed(x):
+    return lax.ppermute(x, ("head", "sub"), [(0, 2), (3, 1)])
+
+
 def swapped(x, axis):
     return lax.ppermute(x, axis, [(0, 1), (1, 0)])
 
@@ -442,13 +442,10 @@
     shards = lax.axis_size("shard")
     count, rows, half = grid_features.shape
     flat = grid_features.reshape(count * rows, half)
-    half_unit = run_pick(mesh_nodes)
-    far = crossed(half_unit, 2, shards)
-    waiting, _ = lax.optimization_barrier((mesh_nodes, half_unit))
-    near = crossed(waiting, 1, shards)
-    waiting, _ = lax.optimization_barrier((flat, half_unit))
-    other = swapped(waiting, "head")
-    flat, gain, wq, wup, wdn, mesh, rest = run_stage(
+    far = fetched(mesh_nodes, 2, True, shards)
+    near = crossed(mesh_nodes, 1, shards)
+    other = swapped(flat, "head")
+    flat, gain, wq, wup, wdn, mesh = run_stage(
         (
             flat,
             norm_gain.reshape(1, -1),
@@ -456,18 +453,17 @@
             up_weight,
             down_weight,
             mesh_nodes,
-            mesh_nodes,
-        ),
-        (None, 1, 0, 0, 1, None, "rest"),
-    )
-    straight = crossed(rest, 3, shards)
-    far, _ = lax.optimization_barrier((far, rest))
-    farther = crossed(far, 1, shards)
-    far_pair = swapped(far, "head")
+        ),
+        (None, 1, 0, 0, 1, None),
+    )
+    straight = fetched(mesh, 3, False, shards)
+    far, _ = lax.optimization_barrier((far, mesh))
+    farther = fetched(far, 1, True, shards)
+    passed = handed(far)
     queries, mlp = run_mlp(flat, other, gain, wq, wup, wdn)
-    queries, mlp, far_pair, near = lax.optimization_barrier((queries, mlp, far_pair, near))
+    queries, mlp, passed, near = lax.optimization_barrier((queries, mlp, passed, near))
     blocked = (-1, BLOCK, 2 * half)
-    mine_a = run_project((mesh, near, far, far_pair), key_weight, value_weight)
+    mine_a = run_project((mesh, near, far, passed), key_weight, value_weight)
     sibling_a = swapped(mine_a, "sub")
     table = run_table(mine_a.reshape(blocked), sibling_a.reshape(blocked), 2 * shards)
     mine_b = run_project((farther, straight), key_weight, value_weight)

time: 47.1 us -> 51 us (1.083)
  starting transfers between devices: 18.1 us -> 22.5 us
  Pallas kernels: 16.2 us -> 15.4 us
    ppermute x0 -> x4, starting transfers between devices: none -> 11.1 us  [the longest x3 8.97 us: fetched(): return lax.ppermute(x, ('shard', 'head', 'sub'), pairs)]
    ppermute x9 -> x6, starting transfers between devices: 13.8 us -> 8.61 us  [crossed(): return lax.ppermute(x, 'shard', [(i, i ^ distance) for i in range(size)])]
    ppermute x9 -> x6, waiting for transfers between devices: 7.93 us -> 3.74 us  [crossed(): return lax.ppermute(x, 'shard', [(i, i ^ distance) for i in range(size)])]
    ppermute x0 -> x4, waiting for transfers between devices: none -> 3.96 us  [the longest x3 3.96 us: fetched(): return lax.ppermute(x, ('shard', 'head', 'sub'), pairs)]
    ppermute x6 -> x5, starting transfers between devices: 4.27 us -> 2.72 us  [swapped(): return lax.ppermute(x, axis, [(0, 1), (1, 0)])]
    pallas_call x1 -> x0, Pallas kernels: 0.91 us -> none  [run_pick(): pl.pallas_call(pick_kernel, out_shape=jax.ShapeDtypeStruct((BLOCK, mesh.s...]
    ppermute x6 -> x5, waiting for transfers between devices: 4.42 us -> 4.76 us  [swapped(): return lax.ppermute(x, axis, [(0, 1), (1, 0)])]
  transfers between devices with their start and end apart: 15 -> 15, of which waited for: 11 -> 7; matrix products, arithmetic and copies ran while one was open for 0% -> 0% of each run, Pallas kernels for 26% -> 24%
where the time goes in v17:
time: 51 us; the launch traced here: 50.8 us
  starting transfers between devices  22.5 us (44%)
  Pallas kernels  15.4 us (30%)
  waiting for transfers between devices  12.5 us (25%)
    ppermute x3, starting transfers between devices, fetched(): return lax.ppermute(x, ('shard', 'head', 'sub'), pairs)  8.97 us
    ppermute x6, starting transfers between devices, crossed(): return lax.ppermute(x, 'shard', [(i, i ^ distance) for i in range(size)])  8.61 us
    ppermute x5, waiting for transfers between devices, swapped(): return lax.ppermute(x, axis, [(0, 1), (1, 0)])  4.76 us
    pallas_call x1, Pallas kernels, run_stage(): pl.pallas_call(functools.partial(stage_kernel, axes), out_shape=tuple((ja...  4.04 us
    ppermute x3, waiting for transfers between devices, fetched(): return lax.ppermute(x, ('shard', 'head', 'sub'), pairs)  3.96 us
    ppermute x6, waiting for transfers between devices, crossed(): return lax.ppermute(x, 'shard', [(i, i ^ distance) for i in range(size)])  3.74 us
    pallas_call x1, Pallas kernels, run_mlp(): pl.pallas_call(mlp_kernel, out_shape=(jax.ShapeDtypeStruct((rows, wq.shap...  3.33 us
    ppermute x5, starting transfers between devices, swapped(): return lax.ppermute(x, axis, [(0, 1), (1, 0)])  2.72 us
  transfers between devices with their start and end apart: 15, of which 7 were waited for; matrix products, arithmetic and copies ran while one was open for 0% of the time, Pallas kernels for 24%

profile of v17, /device:TPU:0, one launch (start us, length us, event | category | flops | bytes accessed | tf_op | source)
XLA Modules:
  0.0 50.8 jit_solution(12378137828908799546)
XLA Ops:
  0.0 5.9 %collective-permute-start.1 = (bf16[128,1024]{1,0:T(8,128)(2,1)}, bf16[128,1024]{1,0:T(8,128)(2,1)S(1)}, u32[]{:S(2)}, u32[]{:S(2)}) collective-permute-start(bf16[128,1024]{1,0:T(8,128)(2,1)} %refs_5_.2), channel_id=1, source_target_pairs={{0,8},{3,11},{4,12},{7,15},{8,0},{11,3},{12,4},{15,7},{16,24},{19,... | collective-permute-start | bytes 786440 | tf_op jit(solution)/shard_map/ppermute | solution.py:418
  5.9 1.6 %collective-permute-start.3 = (bf16[128,1024]{1,0:T(8,128)(2,1)}, bf16[128,1024]{1,0:T(8,128)(2,1)S(1)}, u32[]{:S(2)}, u32[]{:S(2)}) collective-permute-start(bf16[128,1024]{1,0:T(8,128)(2,1)} %refs_5_.2), channel_id=1, source_target_pairs={{0,4},{4,0},{8,12},{12,8},{1,5},{5,1},{9,13},{13,9},{2,6},{6,2},{1... | collective-permute-start | bytes 786440 | tf_op jit(solution)/shard_map/ppermute | solution.py:409
  7.6 0.0 collective-permute-start
  7.6 4.0 %stage.1 = (bf16[256,512]{1,0:T(8,128)(2,1)S(1)}, f32[1,1024]{1,0:T(1,128)S(1)}, bf16[1024,512]{1,0:T(8,128)(2,1)S(1)}, bf16[1024,2048]{1,0:T(8,128)(2,1)S(1)}, ...) custom-call(bf16[256,512]{1,0:T(8,128)(2,1)} %bitcast.9, f32[1,1024]{1,0:T(1,128)} %bitcast.12, ...), custom_call_target="tpu_custom_call" | custom-call | flops 19927040000 | bytes 199270400 | tf_op jit(solution)/shard_map/stage/pallas_call | solution.py:139
  11.6 1.8 %collective-permute-done.1.refs_2_ = bf16[128,1024]{1,0:T(8,128)(2,1)S(1)} collective-permute-done((bf16[128,1024]{1,0:T(8,128)(2,1)}, bf16[128,1024]{1,0:T(8,128)(2,1)S(1)}, u32[]{:S(2)}, u32[]{:S(2)}) %collective-permute-start.1) | collective-permute-done | bytes 262176 | tf_op jit(solution)/shard_map/ppermute | solution.py:418
  13.4 2.2 %collective-permute-start.2 = (bf16[128,1024]{1,0:T(8,128)(2,1)S(1)}, bf16[128,1024]{1,0:T(8,128)(2,1)S(1)}, u32[]{:S(2)}, u32[]{:S(2)}) collective-permute-start(bf16[128,1024]{1,0:T(8,128)(2,1)S(1)} %collective-permute-done.1.refs_2_), channel_id=1, source_target_pairs={{0,2},{3,1},{4,6},{7,5},{8,10},{11,9},{12,14},{15,13},{16,18},{19,... | collective-permute-start | bytes 786440 | tf_op jit(solution)/shard_map/ppermute | solution.py:422
  15.6 0.7 %collective-permute-start.5 = (bf16[128,1024]{1,0:T(8,128)(2,1)S(1)}, bf16[128,1024]{1,0:T(8,128)(2,1)S(1)}, u32[]{:S(2)}, u32[]{:S(2)}) collective-permute-start(bf16[128,1024]{1,0:T(8,128)(2,1)S(1)} %get-tuple-element.38.refs_0_), channel_id=1, source_target_pairs={{1,13},{2,14},{5,9},{6,10},{9,5},{10,6},{13,1},{14,2},{17,29},{18,... | collective-permute-start | bytes 786440 | tf_op jit(solution)/shard_map/ppermute | solution.py:418
  16.3 2.4 %collective-permute-start.4 = (bf16[128,1024]{1,0:T(8,128)(2,1)S(1)}, bf16[128,1024]{1,0:T(8,128)(2,1)S(1)}, u32[]{:S(2)}, u32[]{:S(2)}) collective-permute-start(bf16[128,1024]{1,0:T(8,128)(2,1)S(1)} %collective-permute-done.1.refs_2_), channel_id=1, source_target_pairs={{0,4},{3,7},{4,0},{7,3},{8,12},{11,15},{12,8},{15,11},{16,20},{19,... | collective-permute-start | bytes 786440 | tf_op jit(solution)/shard_map/ppermute | solution.py:418
  18.6 0.0 collective-permute-done.other
  18.7 0.0 copy-start
  18.7 0.0 copy-start.1
  18.7 3.3 %mlp.1 = (bf16[256,512]{1,0:T(8,128)(2,1)S(1)}, f32[256,1024]{1,0:T(8,128)S(1)}) custom-call(bf16[256,512]{1,0:T(8,128)(2,1)S(1)} %get-tuple-element.31.own, bf16[256,512]{1,0:T(8,128)(2,1)S(1)} %collective-permute-done.other, f32[1,1024]{1,0:T(1,128)S(1)} %get-tuple-element.32.gain, bf16[1024,512]{1,0:T(8,128)(2,1)S(1)} %get-tuple-element.33.wq, ...), custom_call_target="tpu_custom_call" | custom-call | flops 2415919104 | bytes 9437184 | tf_op jit(solution)/shard_map/mlp/pallas_call | solution.py:85
  22.0 0.0 collective-permute-done.3.refs_1_
  22.0 0.0 collective-permute-done.2.refs_3_
  22.0 0.0 copy-done
  22.0 0.0 copy-done.1
  22.1 1.1 %project.3 = bf16[384,1024]{1,0:T(8,128)(2,1)S(1)} custom-call(bf16[128,1024]{1,0:T(8,128)(2,1)S(1)} %get-tuple-element.38.refs_0_, bf16[128,1024]{1,0:T(8,128)(2,1)S(1)} %collective-permute-done.3.refs_1_, bf16[128,1024]{1,0:T(8,128)(2,1)S(1)} %collective-permute-done.1.refs_2_, bf16[128,1024]{1,0:T(8,128)(2,1)S(1)} %collective-permute-done.2.refs_3_, ...), custom_call_target="tpu_custom_call" | custom-call | flops 60397977600 | bytes 275251200 | tf_op jit(solution)/shard_map/project/pallas_call | solution.py:178
  23.1 0.0 copy-start.2
  23.1 0.0 copy-start.4
  23.1 0.1 collective-permute-start.7
  23.2 0.0 collective-permute-done.5.refs_1_
  23.2 2.2 %collective-permute-done.4.refs_0_ = bf16[128,1024]{1,0:T(8,128)(2,1)S(1)} collective-permute-done((bf16[128,1024]{1,0:T(8,128)(2,1)S(1)}, bf16[128,1024]{1,0:T(8,128)(2,1)S(1)}, u32[]{:S(2)}, u32[]{:S(2)}) %collective-permute-start.4) | collective-permute-done | bytes 262176 | tf_op jit(solution)/shard_map/ppermute | solution.py:418
  25.4 0.5 project.2
  25.9 0.1 collective-permute-start.6
  26.0 0.0 collective-permute-done.7
  26.0 0.1 table.1.table_in
  26.1 1.4 %collective-permute-done.6 = bf16[128,1024]{1,0:T(8,128)(2,1)S(1)} collective-permute-done((bf16[128,1024]{1,0:T(8,128)(2,1)S(1)}, bf16[128,1024]{1,0:T(8,128)(2,1)S(1)}, u32[]{:S(2)}, u32[]{:S(2)}) %collective-permute-start.6) | collective-permute-done | bytes 262176 | tf_op jit(solution)/shard_map/ppermute | solution.py:426
  27.5 0.0 copy-done.2
  27.5 0.0 copy-done.4
  27.5 2.5 %attend.1 = (bf16[256,128]{1,0:T(8,128)(2,1)S(1)}, bf16[256,128]{1,0:T(8,128)(2,1)S(1)}, bf16[256,512]{1,0:T(8,128)(2,1)S(1)}, bf16[2,8,64,1024]{3,2,1,0:T(8,128)(2,1)S(1)}) custom-call(s32[4,8]{1,0:T(4,128)S(1)} %copy-done.4, bf16[256,512]{1,0:T(8,128)(2,1)S(1)} %get-tuple-element.40.q, ...), custom_call_target="tpu_custom_call", output_to_operand_aliasing={{3}: (4, {})} | custom-call | flops 13421772800 | bytes 41943040 | tf_op jit(solution)/shard_map/attend/pallas_call | solution.py:292
  30.1 2.5 %collective-permute-start.9 = (bf16[256,128]{1,0:T(8,128)(2,1)S(1)}, bf16[256,128]{1,0:T(8,128)(2,1)S(1)}, u32[]{:S(2)}, u32[]{:S(2)}) collective-permute-start(bf16[256,128]{1,0:T(8,128)(2,1)S(1)} %get-tuple-element.48), channel_id=1, source_target_pairs={{0,2},{2,0},{1,3},{3,1},{4,6},{6,4},{5,7},{7,5},{8,10},{10,8},{9,1... | collective-permute-start | bytes 196616 | tf_op jit(solution)/shard_map/ppermute | solution.py:426
  32.5 0.0 copy-start.5
  32.5 0.0 copy-start.3
  32.5 0.4 project_out.1
  33.0 0.1 collective-permute-start.8
  33.1 0.1 copy-done.5
  33.2 0.1 copy.15.owners
  33.3 1.7 %collective-permute-done.9.refs_1_.refs_2_ = bf16[256,128]{1,0:T(8,128)(2,1)S(1)} collective-permute-done((bf16[256,128]{1,0:T(8,128)(2,1)S(1)}, bf16[256,128]{1,0:T(8,128)(2,1)S(1)}, u32[]{:S(2)}, u32[]{:S(2)}) %collective-permute-start.9) | collective-permute-done | bytes 65568 | tf_op jit(solution)/shard_map/ppermute | solution.py:426
  35.0 0.0 copy-done.3
  35.0 0.6 %combine.3 = (bf16[2,64,128]{2,1,0:T(8,128)(2,1)S(1)}, bf16[2,64,128]{2,1,0:T(8,128)(2,1)S(1)}) custom-call(s32[4,1]{1,0:T(4,128)S(1)} %copy.15.owners, bf16[4,64,512]{2,1,0:T(8,128)(2,1)S(1)} %copy-done.3, bf16[256,128]{1,0:T(8,128)(2,1)S(1)} %get-tuple-element.47.refs_0_, bf16[256,128]{1,0:T(8,128)(2,1)S(1)} %collective-permute-done.9.refs_1_.refs_2_), custom_call_target="tpu_custom_call" | custom-call | flops 1966080000 | bytes 52428800 | tf_op jit(solution)/shard_map/combine/pallas_call | solution.py:364
  35.6 0.8 %collective-permute-start.13 = (bf16[2,64,128]{2,1,0:T(8,128)(2,1)S(1)}, bf16[2,64,128]{2,1,0:T(8,128)(2,1)S(1)}, u32[]{:S(2)}, u32[]{:S(2)}) collective-permute-start(bf16[2,64,128]{2,1,0:T(8,128)(2,1)S(1)} %get-tuple-element.49), channel_id=1, source_target_pairs={{0,8},{4,12},{8,0},{12,4},{1,9},{5,13},{9,1},{13,5},{2,10},{6,14},... | collective-permute-start | bytes 98312 | tf_op jit(solution)/shard_map/ppermute | solution.py:409
  36.4 1.7 %collective-permute-start.14 = (bf16[2,64,128]{2,1,0:T(8,128)(2,1)S(1)}, bf16[2,64,128]{2,1,0:T(8,128)(2,1)S(1)}, u32[]{:S(2)}, u32[]{:S(2)}) collective-permute-start(bf16[2,64,128]{2,1,0:T(8,128)(2,1)S(1)} %get-tuple-element.56), channel_id=1, source_target_pairs={{0,12},{4,8},{8,4},{12,0},{1,13},{5,9},{9,5},{13,1},{2,14},{6,10},... | collective-permute-start | bytes 98312 | tf_op jit(solution)/shard_map/ppermute | solution.py:409
  38.1 1.6 %collective-permute-done.8.refs_1_.refs_3_ = bf16[256,384]{1,0:T(8,128)(2,1)S(1)} collective-permute-done((bf16[256,384]{1,0:T(8,128)(2,1)S(1)}, bf16[256,384]{1,0:T(8,128)(2,1)S(1)}, u32[]{:S(2)}, u32[]{:S(2)}) %collective-permute-start.8) | collective-permute-done | bytes 196640 | tf_op jit(solution)/shard_map/ppermute | solution.py:426
  39.7 0.7 %combine.4 = (bf16[2,64,384]{2,1,0:T(8,128)(2,1)S(1)}, bf16[2,64,384]{2,1,0:T(8,128)(2,1)S(1)}) custom-call(s32[4,1]{1,0:T(4,128)S(1)} %copy.15.owners, bf16[4,64,512]{2,1,0:T(8,128)(2,1)S(1)} %copy-done.3, bf16[256,384]{1,0:T(8,128)(2,1)S(1)} %get-tuple-element.45.refs_0_.refs_1_, bf16[256,384]{1,0:T(8,128)(2,1)S(1)} %collective-permute-done.8.refs_1_.refs_3_), custom_call_target="tpu_custom_call" | custom-call | flops 5898240000 | bytes 157286400 | tf_op jit(solution)/shard_map/combine/pallas_call | solution.py:364
  40.4 0.3 collective-permute-start.10
  40.6 0.6 %combine.5 = (bf16[2,64,512]{2,1,0:T(8,128)(2,1)S(1)}, bf16[2,64,512]{2,1,0:T(8,128)(2,1)S(1)}) custom-call(s32[4,1]{1,0:T(4,128)S(1)} %copy.15.owners, bf16[4,64,512]{2,1,0:T(8,128)(2,1)S(1)} %copy-done.3, bf16[256,128]{1,0:T(8,128)(2,1)S(1)} %get-tuple-element.47.refs_0_, bf16[256,384]{1,0:T(8,128)(2,1)S(1)} %get-tuple-element.45.refs_0_.refs_1_, ...), custom_call_target="tpu_custom_call" | custom-call | flops 7864320000 | bytes 209715200 | tf_op jit(solution)/shard_map/combine/pallas_call | solution.py:364
  41.3 1.1 %collective-permute-start.12 = (bf16[2,64,512]{2,1,0:T(8,128)(2,1)S(1)}, bf16[2,64,512]{2,1,0:T(8,128)(2,1)S(1)}, u32[]{:S(2)}, u32[]{:S(2)}) collective-permute-start(bf16[2,64,512]{2,1,0:T(8,128)(2,1)S(1)} %get-tuple-element.54), channel_id=1, source_target_pairs={{0,4},{4,0},{8,12},{12,8},{1,5},{5,1},{9,13},{13,9},{2,6},{6,2},{1... | collective-permute-start | bytes 393224 | tf_op jit(solution)/shard_map/ppermute | solution.py:409
  42.4 3.1 %collective-permute-start.11 = (bf16[2,64,384]{2,1,0:T(8,128)(2,1)S(1)}, bf16[2,64,384]{2,1,0:T(8,128)(2,1)S(1)}, u32[]{:S(2)}, u32[]{:S(2)}) collective-permute-start(bf16[2,64,384]{2,1,0:T(8,128)(2,1)S(1)} %get-tuple-element.52), channel_id=1, source_target_pairs={{0,12},{4,8},{8,4},{12,0},{1,13},{5,9},{9,5},{13,1},{2,14},{6,10},... | collective-permute-start | bytes 294920 | tf_op jit(solution)/shard_map/ppermute | solution.py:409
  45.6 0.0 collective-permute-done.13.refs_0_
  45.6 0.0 collective-permute-done.14.refs_1_
  45.6 0.6 %place.2.refs_4_ = bf16[8,64,512]{2,1,0:T(8,128)(2,1)} custom-call(bf16[2,64,128]{2,1,0:T(8,128)(2,1)S(1)} %collective-permute-done.13.refs_0_, bf16[2,64,128]{2,1,0:T(8,128)(2,1)S(1)} %collective-permute-done.14.refs_1_), custom_call_target="tpu_custom_call" | custom-call | flops 13107200000 | tf_op jit(solution)/shard_map/place/pallas_call | solution.py:393
  46.2 2.0 %collective-permute-done.10.refs_0_ = bf16[2,64,384]{2,1,0:T(8,128)(2,1)S(1)} collective-permute-done((bf16[2,64,384]{2,1,0:T(8,128)(2,1)S(1)}, bf16[2,64,384]{2,1,0:T(8,128)(2,1)S(1)}, u32[]{:S(2)}, u32[]{:S(2)}) %collective-permute-start.10) | collective-permute-done | bytes 98336 | tf_op jit(solution)/shard_map/ppermute | solution.py:409
  48.2 1.8 %collective-permute-done.11.refs_1_ = bf16[2,64,384]{2,1,0:T(8,128)(2,1)S(1)} collective-permute-done((bf16[2,64,384]{2,1,0:T(8,128)(2,1)S(1)}, bf16[2,64,384]{2,1,0:T(8,128)(2,1)S(1)}, u32[]{:S(2)}, u32[]{:S(2)}) %collective-permute-start.11) | collective-permute-done | bytes 98336 | tf_op jit(solution)/shard_map/ppermute | solution.py:409
  50.0 0.0 collective-permute-done.12.refs_2_
  50.0 0.8 %place.3 = bf16[8,64,512]{2,1,0:T(8,128)(2,1)} custom-call(bf16[2,64,384]{2,1,0:T(8,128)(2,1)S(1)} %collective-permute-done.10.refs_0_, bf16[2,64,384]{2,1,0:T(8,128)(2,1)S(1)} %collective-permute-done.11.refs_1_, bf16[2,64,512]{2,1,0:T(8,128)(2,1)S(1)} %collective-permute-done.12.refs_2_, ...), custom_call_target="tpu_custom_call", output_to_operand_aliasing={{}: (4, {})} | custom-call | flops 91750400000 | tf_op jit(solution)/shard_map/place/pallas_call | solution.py:393
Async XLA Ops:
  0.0 13.4 %collective-permute-start.1 = (bf16[128,1024]{1,0:T(8,128)(2,1)}, bf16[128,1024]{1,0:T(8,128)(2,1)S(1)}, u32[]{:S(2)}, u32[]{:S(2)}) collective-permute-start(bf16[128,1024]{1,0:T(8,128)(2,1)} %refs_5_.2), channel_id=1, source_target_pairs={{0,8},{3,11},{4,12},{7,15},{8,0},{11,3},{12,4},{15,7},{16,24},{19,... | collective-permute-start | bytes 786440 | tf_op jit(solution)/shard_map/ppermute | solution.py:418
  5.9 16.1 %collective-permute-start.3 = (bf16[128,1024]{1,0:T(8,128)(2,1)}, bf16[128,1024]{1,0:T(8,128)(2,1)S(1)}, u32[]{:S(2)}, u32[]{:S(2)}) collective-permute-start(bf16[128,1024]{1,0:T(8,128)(2,1)} %refs_5_.2), channel_id=1, source_target_pairs={{0,4},{4,0},{8,12},{12,8},{1,5},{5,1},{9,13},{13,9},{2,6},{6,2},{1... | collective-permute-start | bytes 786440 | tf_op jit(solution)/shard_map/ppermute | solution.py:409
  7.6 11.1 %collective-permute-start = (bf16[256,512]{1,0:T(8,128)(2,1)}, bf16[256,512]{1,0:T(8,128)(2,1)S(1)}, u32[]{:S(2)}, u32[]{:S(2)}) collective-permute-start(bf16[256,512]{1,0:T(8,128)(2,1)} %bitcast.8), channel_id=1, source_target_pairs={{0,2},{2,0},{1,3},{3,1},{4,6},{6,4},{5,7},{7,5},{8,10},{10,8},{9,1... | collective-permute-start | bytes 786440 | tf_op jit(solution)/shard_map/ppermute | solution.py:426
  13.4 8.6 %collective-permute-start.2 = (bf16[128,1024]{1,0:T(8,128)(2,1)S(1)}, bf16[128,1024]{1,0:T(8,128)(2,1)S(1)}, u32[]{:S(2)}, u32[]{:S(2)}) collective-permute-start(bf16[128,1024]{1,0:T(8,128)(2,1)S(1)} %collective-permute-done.1.refs_2_), channel_id=1, source_target_pairs={{0,2},{3,1},{4,6},{7,5},{8,10},{11,9},{12,14},{15,13},{16,18},{19,... | collective-permute-start | bytes 786440 | tf_op jit(solution)/shard_map/ppermute | solution.py:422
  15.6 7.6 %collective-permute-start.5 = (bf16[128,1024]{1,0:T(8,128)(2,1)S(1)}, bf16[128,1024]{1,0:T(8,128)(2,1)S(1)}, u32[]{:S(2)}, u32[]{:S(2)}) collective-permute-start(bf16[128,1024]{1,0:T(8,128)(2,1)S(1)} %get-tuple-element.38.refs_0_), channel_id=1, source_target_pairs={{1,13},{2,14},{5,9},{6,10},{9,5},{10,6},{13,1},{14,2},{17,29},{18,... | collective-permute-start | bytes 786440 | tf_op jit(solution)/shard_map/ppermute | solution.py:418
  16.3 9.2 %collective-permute-start.4 = (bf16[128,1024]{1,0:T(8,128)(2,1)S(1)}, bf16[128,1024]{1,0:T(8,128)(2,1)S(1)}, u32[]{:S(2)}, u32[]{:S(2)}) collective-permute-start(bf16[128,1024]{1,0:T(8,128)(2,1)S(1)} %collective-permute-done.1.refs_2_), channel_id=1, source_target_pairs={{0,4},{3,7},{4,0},{7,3},{8,12},{11,15},{12,8},{15,11},{16,20},{19,... | collective-permute-start | bytes 786440 | tf_op jit(solution)/shard_map/ppermute | solution.py:418
  18.7 3.4 %copy-start = (bf16[1024,512]{1,0:T(8,128)(2,1)S(1)}, bf16[1024,512]{1,0:T(8,128)(2,1)}, u32[]{:S(2)}) copy-start(bf16[1024,512]{1,0:T(8,128)(2,1)} %refs_4_.3) | copy-start | bytes 3145732
  18.7 3.4 %copy-start.1 = (bf16[1024,512]{1,0:T(8,128)(2,1)S(1)}, bf16[1024,512]{1,0:T(8,128)(2,1)}, u32[]{:S(2)}) copy-start(bf16[1024,512]{1,0:T(8,128)(2,1)} %refs_5_.3) | copy-start | bytes 3145732
  23.1 4.4 %copy-start.2 = (bf16[512,1024]{1,0:T(8,128)(2,1)S(1)}, bf16[512,1024]{1,0:T(8,128)(2,1)}, u32[]{:S(2)}) copy-start(bf16[512,1024]{1,0:T(8,128)(2,1)} %wo.3) | copy-start | bytes 3145732
  23.1 4.4 %copy-start.4 = (s32[4,8]{1,0:T(4,128)S(1)}, s32[4,8]{1,0:T(4,128)}, u32[]{:S(2)}) copy-start(s32[4,8]{1,0:T(4,128)} %adjacency.1) | copy-start | bytes 388
  23.1 2.9 %collective-permute-start.7 = (bf16[384,1024]{1,0:T(8,128)(2,1)S(1)}, bf16[384,1024]{1,0:T(8,128)(2,1)S(1)}, u32[]{:S(2)}, u32[]{:S(2)}) collective-permute-start(bf16[384,1024]{1,0:T(8,128)(2,1)S(1)} %project.3), channel_id=1, source_target_pairs={{0,1},{1,0},{2,3},{3,2},{4,5},{5,4},{6,7},{7,6},{8,9},{9,8},{10,11... | collective-permute-start | bytes 2359304 | tf_op jit(solution)/shard_map/ppermute | solution.py:426
  25.9 1.6 %collective-permute-start.6 = (bf16[128,1024]{1,0:T(8,128)(2,1)S(1)}, bf16[128,1024]{1,0:T(8,128)(2,1)S(1)}, u32[]{:S(2)}, u32[]{:S(2)}) collective-permute-start(bf16[128,1024]{1,0:T(8,128)(2,1)S(1)} %project.2), channel_id=1, source_target_pairs={{0,1},{1,0},{2,3},{3,2},{4,5},{5,4},{6,7},{7,6},{8,9},{9,8},{10,11... | collective-permute-start | bytes 786440 | tf_op jit(solution)/shard_map/ppermute | solution.py:426
  30.1 4.9 %collective-permute-start.9 = (bf16[256,128]{1,0:T(8,128)(2,1)S(1)}, bf16[256,128]{1,0:T(8,128)(2,1)S(1)}, u32[]{:S(2)}, u32[]{:S(2)}) collective-permute-start(bf16[256,128]{1,0:T(8,128)(2,1)S(1)} %get-tuple-element.48), channel_id=1, source_target_pairs={{0,2},{2,0},{1,3},{3,1},{4,6},{6,4},{5,7},{7,5},{8,10},{10,8},{9,1... | collective-permute-start | bytes 196616 | tf_op jit(solution)/shard_map/ppermute | solution.py:426
  32.5 0.7 %copy-start.5 = (s32[4,1]{0,1:T(1,128)S(1)}, s32[4,1]{0,1:T(1,128)}, u32[]{:S(2)}) copy-start(s32[4,1]{0,1:T(1,128)} %param.12) | copy-start | bytes 52
  32.5 2.5 %copy-start.3 = (bf16[4,64,512]{2,1,0:T(8,128)(2,1)S(1)}, bf16[4,64,512]{2,1,0:T(8,128)(2,1)}, u32[]{:S(2)}) copy-start(bf16[4,64,512]{2,1,0:T(8,128)(2,1)} %grid_features.5) | copy-start | bytes 786436
  33.0 6.7 %collective-permute-start.8 = (bf16[256,384]{1,0:T(8,128)(2,1)S(1)}, bf16[256,384]{1,0:T(8,128)(2,1)S(1)}, u32[]{:S(2)}, u32[]{:S(2)}) collective-permute-start(bf16[256,384]{1,0:T(8,128)(2,1)S(1)} %get-tuple-element.46), channel_id=1, source_target_pairs={{0,2},{2,0},{1,3},{3,1},{4,6},{6,4},{5,7},{7,5},{8,10},{10,8},{9,1... | collective-permute-start | bytes 589832 | tf_op jit(solution)/shard_map/ppermute | solution.py:426
  35.6 9.9 %collective-permute-start.13 = (bf16[2,64,128]{2,1,0:T(8,128)(2,1)S(1)}, bf16[2,64,128]{2,1,0:T(8,128)(2,1)S(1)}, u32[]{:S(2)}, u32[]{:S(2)}) collective-permute-start(bf16[2,64,128]{2,1,0:T(8,128)(2,1)S(1)} %get-tuple-element.49), channel_id=1, source_target_pairs={{0,8},{4,12},{8,0},{12,4},{1,9},{5,13},{9,1},{13,5},{2,10},{6,14},... | collective-permute-start | bytes 98312 | tf_op jit(solution)/shard_map/ppermute | solution.py:409
  36.4 9.2 %collective-permute-start.14 = (bf16[2,64,128]{2,1,0:T(8,128)(2,1)S(1)}, bf16[2,64,128]{2,1,0:T(8,128)(2,1)S(1)}, u32[]{:S(2)}, u32[]{:S(2)}) collective-permute-start(bf16[2,64,128]{2,1,0:T(8,128)(2,1)S(1)} %get-tuple-element.56), channel_id=1, source_target_pairs={{0,12},{4,8},{8,4},{12,0},{1,13},{5,9},{9,5},{13,1},{2,14},{6,10},... | collective-permute-start | bytes 98312 | tf_op jit(solution)/shard_map/ppermute | solution.py:409
  40.4 7.8 %collective-permute-start.10 = (bf16[2,64,384]{2,1,0:T(8,128)(2,1)S(1)}, bf16[2,64,384]{2,1,0:T(8,128)(2,1)S(1)}, u32[]{:S(2)}, u32[]{:S(2)}) collective-permute-start(bf16[2,64,384]{2,1,0:T(8,128)(2,1)S(1)} %get-tuple-element.51), channel_id=1, source_target_pairs={{0,8},{4,12},{8,0},{12,4},{1,9},{5,13},{9,1},{13,5},{2,10},{6,14},... | collective-permute-start | bytes 294920 | tf_op jit(solution)/shard_map/ppermute | solution.py:409
  41.3 8.7 %collective-permute-start.12 = (bf16[2,64,512]{2,1,0:T(8,128)(2,1)S(1)}, bf16[2,64,512]{2,1,0:T(8,128)(2,1)S(1)}, u32[]{:S(2)}, u32[]{:S(2)}) collective-permute-start(bf16[2,64,512]{2,1,0:T(8,128)(2,1)S(1)} %get-tuple-element.54), channel_id=1, source_target_pairs={{0,4},{4,0},{8,12},{12,8},{1,5},{5,1},{9,13},{13,9},{2,6},{6,2},{1... | collective-permute-start | bytes 393224 | tf_op jit(solution)/shard_map/ppermute | solution.py:409
  42.4 7.5 %collective-permute-start.11 = (bf16[2,64,384]{2,1,0:T(8,128)(2,1)S(1)}, bf16[2,64,384]{2,1,0:T(8,128)(2,1)S(1)}, u32[]{:S(2)}, u32[]{:S(2)}) collective-permute-start(bf16[2,64,384]{2,1,0:T(8,128)(2,1)S(1)} %get-tuple-element.52), channel_id=1, source_target_pairs={{0,12},{4,8},{8,4},{12,0},{1,13},{5,9},{9,5},{13,1},{2,14},{6,10},... | collective-permute-start | bytes 294920 | tf_op jit(solution)/shard_map/ppermute | solution.py:409

commit v18 on v16

--- a/solution.py
+++ b/solution.py
@@ -345,29 +345,29 @@
 def combine_kernel(chunks, distances, owners, grid_features, *refs):
     s = lax.axis_index("shard")
     keeps, refs = refs[: len(chunks)], refs[len(chunks) :]
-    swaps, outs = refs[: len(chunks)], refs[len(chunks) :]
+    swaps, outs, ready = refs[: len(chunks)], refs[len(chunks) : -1], refs[-1]
     count = grid_features.shape[0]
+    first = columns_of(chunks[0]).start
     names = [owners[t, 0] for t in range(count)]
-    first = columns_of(chunks[0]).start
+    ranks = []
+    for t in range(count):
+        same = [(names[e] == names[t]).astype(jnp.int32) for e in range(t)]
+        ranks.append(sum(same, jnp.int32(0)))
+    for c, keep, swap in zip(chunks, keeps, swaps):
+        columns = columns_of(c)
+        place = slice(columns.start - first, columns.stop - first)
+        for t in range(count):
+            rows = slice(t * BLOCK, (t + 1) * BLOCK)
+            partials = keep[rows, :].astype(jnp.float32) + swap[rows, :].astype(jnp.float32)
+            residual = grid_features[t, :, columns].astype(jnp.float32)
+            ready[t, :, place] = (residual + partials).astype(jnp.bfloat16)
+    ready[count] = jnp.zeros(ready.shape[1:], jnp.bfloat16)
     for d, out in zip(distances, outs):
-        out[...] = jnp.zeros(out.shape, jnp.bfloat16)
-        seen = jnp.int32(0)
-        for t in range(count):
-            hit = names[t] == s ^ d
-            rank = seen
-
-            @pl.when(hit)
-            def _():
-                rows = slice(t * BLOCK, (t + 1) * BLOCK)
-                for c, keep, swap in zip(chunks, keeps, swaps):
-                    columns = columns_of(c)
-                    partials = keep[rows, :].astype(jnp.float32)
-                    partials = partials + swap[rows, :].astype(jnp.float32)
-                    residual = grid_features[t, :, columns].astype(jnp.float32)
-                    place = slice(columns.start - first, columns.stop - first)
-                    out[rank, :, place] = (residual + partials).astype(jnp.bfloat16)
-
-            seen = seen + hit.astype(jnp.int32)
+        for j in range(CAP):
+            index = jnp.int32(count)
+            for t in range(count):
+                index = jnp.where((names[t] == s ^ d) & (ranks[t] == j), t, index)
+            out[j] = ready[index]
 
 
 def run_combine(chunks, distances, owners, grid_features, keeps, swaps):
@@ -379,6 +379,7 @@
         out_shape=(slot,) * len(distances),
         in_specs=[whole(pltpu.SMEM)] + vmem(1 + 2 * len(chunks)),
         out_specs=tuple(vmem(len(distances))),
+        scratch_shapes=[pltpu.VMEM((count + 1, rows, width), jnp.bfloat16)],
         compiler_params=params(8),
         cost_estimate=pl.CostEstimate(
             flops=60000 * count * rows * width,
@@ -493,9 +494,12 @@
         first = columns_of(c).start
         spots = [(2, first), (3, first)]
         arrived = [crossed(slot, d, shards) for d, slot in zip((2, 3), slots[c])]
+        if c == 0:
+            spots.append((0, 0))
+            arrived.append(own_slots)
         if c == len(WIDTHS) - 1:
-            spots += [(1, 0), (0, 0)]
-            arrived += [crossed(near_slots, 1, shards), own_slots]
+            spots.append((1, 0))
+            arrived.append(crossed(near_slots, 1, shards))
         placed = [run_place(spots, arrived, placed, shape)]
     return placed[0]
 

time: 47.1 us -> 47 us (level)
  no operation moved by 1% of the time
where the time goes in v18:
time: 47 us; the launch traced here: 46.9 us
  starting transfers between devices  18.1 us (39%)
  Pallas kernels  16.2 us (34%)
  waiting for transfers between devices  12.3 us (26%)
    ppermute x9, starting transfers between devices, crossed(): return lax.ppermute(x, 'shard', [(i, i ^ distance) for i in range(size)])  13.8 us
    ppermute x9, waiting for transfers between devices, crossed(): return lax.ppermute(x, 'shard', [(i, i ^ distance) for i in range(size)])  7.83 us
    ppermute x6, waiting for transfers between devices, swapped(): return lax.ppermute(x, axis, [(0, 1), (1, 0)])  4.45 us
    ppermute x6, starting transfers between devices, swapped(): return lax.ppermute(x, axis, [(0, 1), (1, 0)])  4.27 us
    pallas_call x1, Pallas kernels, run_stage(): pl.pallas_call(functools.partial(stage_kernel, axes), out_shape=tuple((ja...  4.1 us
    pallas_call x1, Pallas kernels, run_mlp(): pl.pallas_call(mlp_kernel, out_shape=(jax.ShapeDtypeStruct((rows, wq.shap...  3.33 us
    pallas_call x1, Pallas kernels, run_attend(): pl.pallas_call(attend_kernel, out_shape=(part, part, jax.ShapeDtypeStruct...  2.52 us
    pallas_call x3, Pallas kernels, run_combine(): pl.pallas_call(functools.partial(combine_kernel, chunks, distances), out_...  1.95 us
  transfers between devices with their start and end apart: 15, of which 11 were waited for; matrix products, arithmetic and copies ran while one was open for 0% of the time, Pallas kernels for 26%

profile of v18, /device:TPU:0, one launch (start us, length us, event | category | flops | bytes accessed | tf_op | source)
XLA Modules:
  0.0 46.9 jit_solution(7547758090254798363)
XLA Ops:
  0.0 0.9 %pick.1 = bf16[64,1024]{1,0:T(8,128)(2,1)S(1)} custom-call(bf16[128,1024]{1,0:T(8,128)(2,1)} %mesh.1), custom_call_target="tpu_custom_call" | custom-call | bytes 524288 | tf_op jit(solution)/shard_map/pick/pallas_call | solution.py:112
  0.9 4.1 %collective-permute-start.1 = (bf16[64,1024]{1,0:T(8,128)(2,1)S(1)}, bf16[64,1024]{1,0:T(8,128)(2,1)S(1)}, u32[]{:S(2)}, u32[]{:S(2)}) collective-permute-start(bf16[64,1024]{1,0:T(8,128)(2,1)S(1)} %pick.1), channel_id=1, source_target_pairs={{0,8},{4,12},{8,0},{12,4},{1,9},{5,13},{9,1},{13,5},{2,10},{6,14},... | collective-permute-start | bytes 393224 | tf_op jit(solution)/shard_map/ppermute | solution.py:423
  5.0 1.5 %collective-permute-start = (bf16[256,512]{1,0:T(8,128)(2,1)}, bf16[256,512]{1,0:T(8,128)(2,1)S(1)}, u32[]{:S(2)}, u32[]{:S(2)}) collective-permute-start(bf16[256,512]{1,0:T(8,128)(2,1)} %bitcast.8), channel_id=1, source_target_pairs={{0,2},{2,0},{1,3},{3,1},{4,6},{6,4},{5,7},{7,5},{8,10},{10,8},{9,1... | collective-permute-start | bytes 786440 | tf_op jit(solution)/shard_map/ppermute | solution.py:427
  6.5 1.6 %collective-permute-start.3 = (bf16[128,1024]{1,0:T(8,128)(2,1)}, bf16[128,1024]{1,0:T(8,128)(2,1)S(1)}, u32[]{:S(2)}, u32[]{:S(2)}) collective-permute-start(bf16[128,1024]{1,0:T(8,128)(2,1)} %mesh.1), channel_id=1, source_target_pairs={{0,4},{4,0},{8,12},{12,8},{1,5},{5,1},{9,13},{13,9},{2,6},{6,2},{1... | collective-permute-start | bytes 786440 | tf_op jit(solution)/shard_map/ppermute | solution.py:423
  8.1 4.1 %stage.1 = (bf16[256,512]{1,0:T(8,128)(2,1)S(1)}, f32[1,1024]{1,0:T(1,128)S(1)}, bf16[1024,512]{1,0:T(8,128)(2,1)S(1)}, bf16[1024,2048]{1,0:T(8,128)(2,1)S(1)}, ...) custom-call(bf16[256,512]{1,0:T(8,128)(2,1)} %bitcast.9, ...), custom_call_target="tpu_custom_call" | custom-call | flops 20451328000 | bytes 204513280 | tf_op jit(solution)/shard_map/stage/pallas_call | solution.py:162
  12.2 0.3 collective-permute-start.5
  12.5 0.0 collective-permute-done.1.refs_2_
  12.5 0.5 %collective-permute-start.2 = (bf16[64,1024]{1,0:T(8,128)(2,1)S(1)}, bf16[64,1024]{1,0:T(8,128)(2,1)S(1)}, u32[]{:S(2)}, u32[]{:S(2)}) collective-permute-start(bf16[64,1024]{1,0:T(8,128)(2,1)S(1)} %collective-permute-done.1.refs_2_), channel_id=1, source_target_pairs={{0,2},{2,0},{1,3},{3,1},{4,6},{6,4},{5,7},{7,5},{8,10},{10,8},{9,1... | collective-permute-start | bytes 393224 | tf_op jit(solution)/shard_map/ppermute | solution.py:427
  13.0 0.7 %collective-permute-start.4 = (bf16[64,1024]{1,0:T(8,128)(2,1)S(1)}, bf16[64,1024]{1,0:T(8,128)(2,1)S(1)}, u32[]{:S(2)}, u32[]{:S(2)}) collective-permute-start(bf16[64,1024]{1,0:T(8,128)(2,1)S(1)} %collective-permute-done.1.refs_2_), channel_id=1, source_target_pairs={{0,4},{4,0},{8,12},{12,8},{1,5},{5,1},{9,13},{13,9},{2,6},{6,2},{1... | collective-permute-start | bytes 393224 | tf_op jit(solution)/shard_map/ppermute | solution.py:423
  13.7 0.0 collective-permute-done.other
  13.7 0.0 copy-start
  13.7 0.0 copy-start.1
  13.7 3.3 %mlp.1 = (bf16[256,512]{1,0:T(8,128)(2,1)S(1)}, f32[256,1024]{1,0:T(8,128)S(1)}) custom-call(bf16[256,512]{1,0:T(8,128)(2,1)S(1)} %get-tuple-element.34.own, bf16[256,512]{1,0:T(8,128)(2,1)S(1)} %collective-permute-done.other, f32[1,1024]{1,0:T(1,128)S(1)} %get-tuple-element.36.gain, bf16[1024,512]{1,0:T(8,128)(2,1)S(1)} %get-tuple-element.37.wq, ...), custom_call_target="tpu_custom_call" | custom-call | flops 2415919104 | bytes 9437184 | tf_op jit(solution)/shard_map/mlp/pallas_call | solution.py:85
  17.1 0.4 collective-permute-done.2.refs_3_
  17.5 1.2 %collective-permute-done.3.refs_1_ = bf16[128,1024]{1,0:T(8,128)(2,1)S(1)} collective-permute-done((bf16[128,1024]{1,0:T(8,128)(2,1)}, bf16[128,1024]{1,0:T(8,128)(2,1)S(1)}, u32[]{:S(2)}, u32[]{:S(2)}) %collective-permute-start.3) | collective-permute-done | bytes 262176 | tf_op jit(solution)/shard_map/ppermute | solution.py:423
  18.7 0.0 copy-done
  18.7 0.0 copy-done.1
  18.7 1.0 %project.3 = bf16[384,1024]{1,0:T(8,128)(2,1)S(1)} custom-call(bf16[128,1024]{1,0:T(8,128)(2,1)S(1)} %get-tuple-element.46.refs_0_, bf16[128,1024]{1,0:T(8,128)(2,1)S(1)} %collective-permute-done.3.refs_1_, bf16[64,1024]{1,0:T(8,128)(2,1)S(1)} %collective-permute-done.1.refs_2_, bf16[64,1024]{1,0:T(8,128)(2,1)S(1)} %collective-permute-done.2.refs_3_, ...), custom_call_target="tpu_custom_call" | custom-call | flops 60397977600 | bytes 275251200 | tf_op jit(solution)/shard_map/project/pallas_call | solution.py:190
  19.7 0.0 copy-start.2
  19.7 0.0 copy-start.4
  19.7 0.1 collective-permute-start.7
  19.8 0.2 collective-permute-done.5.refs_1_
  20.0 1.5 %collective-permute-done.4.refs_0_ = bf16[64,1024]{1,0:T(8,128)(2,1)S(1)} collective-permute-done((bf16[64,1024]{1,0:T(8,128)(2,1)S(1)}, bf16[64,1024]{1,0:T(8,128)(2,1)S(1)}, u32[]{:S(2)}, u32[]{:S(2)}) %collective-permute-start.4) | collective-permute-done | bytes 131104 | tf_op jit(solution)/shard_map/ppermute | solution.py:423
  21.5 0.4 project.2
  21.9 0.1 collective-permute-start.6
  22.0 0.1 collective-permute-done.7
  22.1 0.1 table.1.table_in
  22.2 1.4 %collective-permute-done.6 = bf16[128,1024]{1,0:T(8,128)(2,1)S(1)} collective-permute-done((bf16[128,1024]{1,0:T(8,128)(2,1)S(1)}, bf16[128,1024]{1,0:T(8,128)(2,1)S(1)}, u32[]{:S(2)}, u32[]{:S(2)}) %collective-permute-start.6) | collective-permute-done | bytes 262176 | tf_op jit(solution)/shard_map/ppermute | solution.py:427
  23.5 0.0 copy-done.2
  23.5 0.0 copy-done.4
  23.5 2.5 %attend.1 = (bf16[256,128]{1,0:T(8,128)(2,1)S(1)}, bf16[256,128]{1,0:T(8,128)(2,1)S(1)}, bf16[256,512]{1,0:T(8,128)(2,1)S(1)}, bf16[2,8,64,1024]{3,2,1,0:T(8,128)(2,1)S(1)}) custom-call(s32[4,8]{1,0:T(4,128)S(1)} %copy-done.4, bf16[256,512]{1,0:T(8,128)(2,1)S(1)} %get-tuple-element.45.q, ...), custom_call_target="tpu_custom_call", output_to_operand_aliasing={{3}: (4, {})} | custom-call | flops 13421772800 | bytes 41943040 | tf_op jit(solution)/shard_map/attend/pallas_call | solution.py:305
  26.1 0.7 %collective-permute-start.9 = (bf16[256,128]{1,0:T(8,128)(2,1)S(1)}, bf16[256,128]{1,0:T(8,128)(2,1)S(1)}, u32[]{:S(2)}, u32[]{:S(2)}) collective-permute-start(bf16[256,128]{1,0:T(8,128)(2,1)S(1)} %get-tuple-element.54), channel_id=1, source_target_pairs={{0,2},{2,0},{1,3},{3,1},{4,6},{6,4},{5,7},{7,5},{8,10},{10,8},{9,1... | collective-permute-start | bytes 196616 | tf_op jit(solution)/shard_map/ppermute | solution.py:427
  26.7 0.0 copy-start.5
  26.7 0.0 copy-start.3
  26.7 0.4 project_out.1
  27.2 1.5 %collective-permute-start.8 = (bf16[256,384]{1,0:T(8,128)(2,1)S(1)}, bf16[256,384]{1,0:T(8,128)(2,1)S(1)}, u32[]{:S(2)}, u32[]{:S(2)}) collective-permute-start(bf16[256,384]{1,0:T(8,128)(2,1)S(1)} %get-tuple-element.52), channel_id=1, source_target_pairs={{0,2},{2,0},{1,3},{3,1},{4,6},{6,4},{5,7},{7,5},{8,10},{10,8},{9,1... | collective-permute-start | bytes 589832 | tf_op jit(solution)/shard_map/ppermute | solution.py:427
  28.7 0.0 copy-done.5
  28.7 0.1 copy.15.owners
  28.7 2.3 %collective-permute-done.9.refs_1_.refs_2_ = bf16[256,128]{1,0:T(8,128)(2,1)S(1)} collective-permute-done((bf16[256,128]{1,0:T(8,128)(2,1)S(1)}, bf16[256,128]{1,0:T(8,128)(2,1)S(1)}, u32[]{:S(2)}, u32[]{:S(2)}) %collective-permute-start.9) | collective-permute-done | bytes 65568 | tf_op jit(solution)/shard_map/ppermute | solution.py:427
  31.1 0.0 copy-done.3
  31.1 0.6 %combine.3 = (bf16[2,64,128]{2,1,0:T(8,128)(2,1)S(1)}, bf16[2,64,128]{2,1,0:T(8,128)(2,1)S(1)}) custom-call(s32[4,1]{1,0:T(4,128)S(1)} %copy.15.owners, bf16[4,64,512]{2,1,0:T(8,128)(2,1)S(1)} %copy-done.3, bf16[256,128]{1,0:T(8,128)(2,1)S(1)} %get-tuple-element.53.refs_0_, bf16[256,128]{1,0:T(8,128)(2,1)S(1)} %collective-permute-done.9.refs_1_.refs_2_), custom_call_target="tpu_custom_call" | custom-call | flops 1966080000 | bytes 52428800 | tf_op jit(solution)/shard_map/combine/pallas_call | solution.py:377
  31.7 0.2 collective-permute-start.13
  31.9 2.5 %collective-permute-start.14 = (bf16[2,64,128]{2,1,0:T(8,128)(2,1)S(1)}, bf16[2,64,128]{2,1,0:T(8,128)(2,1)S(1)}, u32[]{:S(2)}, u32[]{:S(2)}) collective-permute-start(bf16[2,64,128]{2,1,0:T(8,128)(2,1)S(1)} %get-tuple-element.61), channel_id=1, source_target_pairs={{0,12},{4,8},{8,4},{12,0},{1,13},{5,9},{9,5},{13,1},{2,14},{6,10},... | collective-permute-start | bytes 98312 | tf_op jit(solution)/shard_map/ppermute | solution.py:423
  34.3 0.3 collective-permute-done.8.refs_1_.refs_3_
  34.6 0.7 %combine.4 = (bf16[2,64,384]{2,1,0:T(8,128)(2,1)S(1)}, bf16[2,64,384]{2,1,0:T(8,128)(2,1)S(1)}) custom-call(s32[4,1]{1,0:T(4,128)S(1)} %copy.15.owners, bf16[4,64,512]{2,1,0:T(8,128)(2,1)S(1)} %copy-done.3, bf16[256,384]{1,0:T(8,128)(2,1)S(1)} %get-tuple-element.51.refs_0_.refs_1_, bf16[256,384]{1,0:T(8,128)(2,1)S(1)} %collective-permute-done.8.refs_1_.refs_3_), custom_call_target="tpu_custom_call" | custom-call | flops 5898240000 | bytes 157286400 | tf_op jit(solution)/shard_map/combine/pallas_call | solution.py:377
  35.3 1.7 %collective-permute-start.10 = (bf16[2,64,384]{2,1,0:T(8,128)(2,1)S(1)}, bf16[2,64,384]{2,1,0:T(8,128)(2,1)S(1)}, u32[]{:S(2)}, u32[]{:S(2)}) collective-permute-start(bf16[2,64,384]{2,1,0:T(8,128)(2,1)S(1)} %get-tuple-element.57), channel_id=1, source_target_pairs={{0,8},{4,12},{8,0},{12,4},{1,9},{5,13},{9,1},{13,5},{2,10},{6,14},... | collective-permute-start | bytes 294920 | tf_op jit(solution)/shard_map/ppermute | solution.py:423
  37.0 0.7 %combine.5 = (bf16[2,64,512]{2,1,0:T(8,128)(2,1)S(1)}, bf16[2,64,512]{2,1,0:T(8,128)(2,1)S(1)}) custom-call(s32[4,1]{1,0:T(4,128)S(1)} %copy.15.owners, bf16[4,64,512]{2,1,0:T(8,128)(2,1)S(1)} %copy-done.3, bf16[256,128]{1,0:T(8,128)(2,1)S(1)} %get-tuple-element.53.refs_0_, bf16[256,384]{1,0:T(8,128)(2,1)S(1)} %get-tuple-element.51.refs_0_.refs_1_, ...), custom_call_target="tpu_custom_call" | custom-call | flops 7864320000 | bytes 209715200 | tf_op jit(solution)/shard_map/combine/pallas_call | solution.py:377
  37.7 1.4 %collective-permute-start.12 = (bf16[2,64,512]{2,1,0:T(8,128)(2,1)S(1)}, bf16[2,64,512]{2,1,0:T(8,128)(2,1)S(1)}, u32[]{:S(2)}, u32[]{:S(2)}) collective-permute-start(bf16[2,64,512]{2,1,0:T(8,128)(2,1)S(1)} %get-tuple-element.60), channel_id=1, source_target_pairs={{0,4},{4,0},{8,12},{12,8},{1,5},{5,1},{9,13},{13,9},{2,6},{6,2},{1... | collective-permute-start | bytes 393224 | tf_op jit(solution)/shard_map/ppermute | solution.py:423
  39.1 1.3 %collective-permute-start.11 = (bf16[2,64,384]{2,1,0:T(8,128)(2,1)S(1)}, bf16[2,64,384]{2,1,0:T(8,128)(2,1)S(1)}, u32[]{:S(2)}, u32[]{:S(2)}) collective-permute-start(bf16[2,64,384]{2,1,0:T(8,128)(2,1)S(1)} %get-tuple-element.58), channel_id=1, source_target_pairs={{0,12},{4,8},{8,4},{12,0},{1,13},{5,9},{9,5},{13,1},{2,14},{6,10},... | collective-permute-start | bytes 294920 | tf_op jit(solution)/shard_map/ppermute | solution.py:423
  40.5 0.0 collective-permute-done.13.refs_0_
  40.5 0.0 collective-permute-done.14.refs_1_
  40.5 0.7 %place.2.refs_3_ = bf16[8,64,512]{2,1,0:T(8,128)(2,1)} custom-call(bf16[2,64,128]{2,1,0:T(8,128)(2,1)S(1)} %collective-permute-done.13.refs_0_, bf16[2,64,128]{2,1,0:T(8,128)(2,1)S(1)} %collective-permute-done.14.refs_1_, bf16[2,64,512]{2,1,0:T(8,128)(2,1)S(1)} %get-tuple-element.62.refs_2_), custom_call_target="tpu_custom_call" | custom-call | flops 39321600000 | tf_op jit(solution)/shard_map/place/pallas_call | solution.py:407
  41.2 2.2 %collective-permute-done.10.refs_0_ = bf16[2,64,384]{2,1,0:T(8,128)(2,1)S(1)} collective-permute-done((bf16[2,64,384]{2,1,0:T(8,128)(2,1)S(1)}, bf16[2,64,384]{2,1,0:T(8,128)(2,1)S(1)}, u32[]{:S(2)}, u32[]{:S(2)}) %collective-permute-start.10) | collective-permute-done | bytes 98336 | tf_op jit(solution)/shard_map/ppermute | solution.py:423
  43.4 2.6 %collective-permute-done.11.refs_1_ = bf16[2,64,384]{2,1,0:T(8,128)(2,1)S(1)} collective-permute-done((bf16[2,64,384]{2,1,0:T(8,128)(2,1)S(1)}, bf16[2,64,384]{2,1,0:T(8,128)(2,1)S(1)}, u32[]{:S(2)}, u32[]{:S(2)}) %collective-permute-start.11) | collective-permute-done | bytes 98336 | tf_op jit(solution)/shard_map/ppermute | solution.py:423
  46.0 0.1 collective-permute-done.12.refs_2_
  46.1 0.7 %place.3 = bf16[8,64,512]{2,1,0:T(8,128)(2,1)} custom-call(bf16[2,64,384]{2,1,0:T(8,128)(2,1)S(1)} %collective-permute-done.10.refs_0_, bf16[2,64,384]{2,1,0:T(8,128)(2,1)S(1)} %collective-permute-done.11.refs_1_, bf16[2,64,512]{2,1,0:T(8,128)(2,1)S(1)} %collective-permute-done.12.refs_2_, ...), custom_call_target="tpu_custom_call", output_to_operand_aliasing={{}: (3, {})} | custom-call | flops 65536000000 | tf_op jit(solution)/shard_map/place/pallas_call | solution.py:407
Async XLA Ops:
  0.9 11.6 %collective-permute-start.1 = (bf16[64,1024]{1,0:T(8,128)(2,1)S(1)}, bf16[64,1024]{1,0:T(8,128)(2,1)S(1)}, u32[]{:S(2)}, u32[]{:S(2)}) collective-permute-start(bf16[64,1024]{1,0:T(8,128)(2,1)S(1)} %pick.1), channel_id=1, source_target_pairs={{0,8},{4,12},{8,0},{12,4},{1,9},{5,13},{9,1},{13,5},{2,10},{6,14},... | collective-permute-start | bytes 393224 | tf_op jit(solution)/shard_map/ppermute | solution.py:423
  5.0 8.7 %collective-permute-start = (bf16[256,512]{1,0:T(8,128)(2,1)}, bf16[256,512]{1,0:T(8,128)(2,1)S(1)}, u32[]{:S(2)}, u32[]{:S(2)}) collective-permute-start(bf16[256,512]{1,0:T(8,128)(2,1)} %bitcast.8), channel_id=1, source_target_pairs={{0,2},{2,0},{1,3},{3,1},{4,6},{6,4},{5,7},{7,5},{8,10},{10,8},{9,1... | collective-permute-start | bytes 786440 | tf_op jit(solution)/shard_map/ppermute | solution.py:427
  6.5 12.2 %collective-permute-start.3 = (bf16[128,1024]{1,0:T(8,128)(2,1)}, bf16[128,1024]{1,0:T(8,128)(2,1)S(1)}, u32[]{:S(2)}, u32[]{:S(2)}) collective-permute-start(bf16[128,1024]{1,0:T(8,128)(2,1)} %mesh.1), channel_id=1, source_target_pairs={{0,4},{4,0},{8,12},{12,8},{1,5},{5,1},{9,13},{13,9},{2,6},{6,2},{1... | collective-permute-start | bytes 786440 | tf_op jit(solution)/shard_map/ppermute | solution.py:423
  12.2 7.8 %collective-permute-start.5 = (bf16[64,1024]{1,0:T(8,128)(2,1)S(1)}, bf16[64,1024]{1,0:T(8,128)(2,1)S(1)}, u32[]{:S(2)}, u32[]{:S(2)}) collective-permute-start(bf16[64,1024]{1,0:T(8,128)(2,1)S(1)} %get-tuple-element.42), channel_id=1, source_target_pairs={{0,12},{4,8},{8,4},{12,0},{1,13},{5,9},{9,5},{13,1},{2,14},{6,10},... | collective-permute-start | bytes 393224 | tf_op jit(solution)/shard_map/ppermute | solution.py:423
  12.5 5.0 %collective-permute-start.2 = (bf16[64,1024]{1,0:T(8,128)(2,1)S(1)}, bf16[64,1024]{1,0:T(8,128)(2,1)S(1)}, u32[]{:S(2)}, u32[]{:S(2)}) collective-permute-start(bf16[64,1024]{1,0:T(8,128)(2,1)S(1)} %collective-permute-done.1.refs_2_), channel_id=1, source_target_pairs={{0,2},{2,0},{1,3},{3,1},{4,6},{6,4},{5,7},{7,5},{8,10},{10,8},{9,1... | collective-permute-start | bytes 393224 | tf_op jit(solution)/shard_map/ppermute | solution.py:427
  13.0 8.5 %collective-permute-start.4 = (bf16[64,1024]{1,0:T(8,128)(2,1)S(1)}, bf16[64,1024]{1,0:T(8,128)(2,1)S(1)}, u32[]{:S(2)}, u32[]{:S(2)}) collective-permute-start(bf16[64,1024]{1,0:T(8,128)(2,1)S(1)} %collective-permute-done.1.refs_2_), channel_id=1, source_target_pairs={{0,4},{4,0},{8,12},{12,8},{1,5},{5,1},{9,13},{13,9},{2,6},{6,2},{1... | collective-permute-start | bytes 393224 | tf_op jit(solution)/shard_map/ppermute | solution.py:423
  13.7 5.0 %copy-start = (bf16[1024,512]{1,0:T(8,128)(2,1)S(1)}, bf16[1024,512]{1,0:T(8,128)(2,1)}, u32[]{:S(2)}) copy-start(bf16[1024,512]{1,0:T(8,128)(2,1)} %refs_4_.3) | copy-start | bytes 3145732
  13.7 5.0 %copy-start.1 = (bf16[1024,512]{1,0:T(8,128)(2,1)S(1)}, bf16[1024,512]{1,0:T(8,128)(2,1)}, u32[]{:S(2)}) copy-start(bf16[1024,512]{1,0:T(8,128)(2,1)} %refs_5_.3) | copy-start | bytes 3145732
  19.7 3.8 %copy-start.2 = (bf16[512,1024]{1,0:T(8,128)(2,1)S(1)}, bf16[512,1024]{1,0:T(8,128)(2,1)}, u32[]{:S(2)}) copy-start(bf16[512,1024]{1,0:T(8,128)(2,1)} %wo.3) | copy-start | bytes 3145732
  19.7 3.8 %copy-start.4 = (s32[4,8]{1,0:T(4,128)S(1)}, s32[4,8]{1,0:T(4,128)}, u32[]{:S(2)}) copy-start(s32[4,8]{1,0:T(4,128)} %adjacency.1) | copy-start | bytes 388
  19.7 2.4 %collective-permute-start.7 = (bf16[384,1024]{1,0:T(8,128)(2,1)S(1)}, bf16[384,1024]{1,0:T(8,128)(2,1)S(1)}, u32[]{:S(2)}, u32[]{:S(2)}) collective-permute-start(bf16[384,1024]{1,0:T(8,128)(2,1)S(1)} %project.3), channel_id=1, source_target_pairs={{0,1},{1,0},{2,3},{3,2},{4,5},{5,4},{6,7},{7,6},{8,9},{9,8},{10,11... | collective-permute-start | bytes 2359304 | tf_op jit(solution)/shard_map/ppermute | solution.py:427
  21.9 1.6 %collective-permute-start.6 = (bf16[128,1024]{1,0:T(8,128)(2,1)S(1)}, bf16[128,1024]{1,0:T(8,128)(2,1)S(1)}, u32[]{:S(2)}, u32[]{:S(2)}) collective-permute-start(bf16[128,1024]{1,0:T(8,128)(2,1)S(1)} %project.2), channel_id=1, source_target_pairs={{0,1},{1,0},{2,3},{3,2},{4,5},{5,4},{6,7},{7,6},{8,9},{9,8},{10,11... | collective-permute-start | bytes 786440 | tf_op jit(solution)/shard_map/ppermute | solution.py:427
  26.1 5.0 %collective-permute-start.9 = (bf16[256,128]{1,0:T(8,128)(2,1)S(1)}, bf16[256,128]{1,0:T(8,128)(2,1)S(1)}, u32[]{:S(2)}, u32[]{:S(2)}) collective-permute-start(bf16[256,128]{1,0:T(8,128)(2,1)S(1)} %get-tuple-element.54), channel_id=1, source_target_pairs={{0,2},{2,0},{1,3},{3,1},{4,6},{6,4},{5,7},{7,5},{8,10},{10,8},{9,1... | collective-permute-start | bytes 196616 | tf_op jit(solution)/shard_map/ppermute | solution.py:427
  26.7 1.9 %copy-start.5 = (s32[4,1]{0,1:T(1,128)S(1)}, s32[4,1]{0,1:T(1,128)}, u32[]{:S(2)}) copy-start(s32[4,1]{0,1:T(1,128)} %param.12) | copy-start | bytes 52
  26.7 4.4 %copy-start.3 = (bf16[4,64,512]{2,1,0:T(8,128)(2,1)S(1)}, bf16[4,64,512]{2,1,0:T(8,128)(2,1)}, u32[]{:S(2)}) copy-start(bf16[4,64,512]{2,1,0:T(8,128)(2,1)} %grid_features.5) | copy-start | bytes 786436
  27.2 7.4 %collective-permute-start.8 = (bf16[256,384]{1,0:T(8,128)(2,1)S(1)}, bf16[256,384]{1,0:T(8,128)(2,1)S(1)}, u32[]{:S(2)}, u32[]{:S(2)}) collective-permute-start(bf16[256,384]{1,0:T(8,128)(2,1)S(1)} %get-tuple-element.52), channel_id=1, source_target_pairs={{0,2},{2,0},{1,3},{3,1},{4,6},{6,4},{5,7},{7,5},{8,10},{10,8},{9,1... | collective-permute-start | bytes 589832 | tf_op jit(solution)/shard_map/ppermute | solution.py:427
  31.7 8.8 %collective-permute-start.13 = (bf16[2,64,128]{2,1,0:T(8,128)(2,1)S(1)}, bf16[2,64,128]{2,1,0:T(8,128)(2,1)S(1)}, u32[]{:S(2)}, u32[]{:S(2)}) collective-permute-start(bf16[2,64,128]{2,1,0:T(8,128)(2,1)S(1)} %get-tuple-element.55), channel_id=1, source_target_pairs={{0,8},{4,12},{8,0},{12,4},{1,9},{5,13},{9,1},{13,5},{2,10},{6,14},... | collective-permute-start | bytes 98312 | tf_op jit(solution)/shard_map/ppermute | solution.py:423
  31.9 8.6 %collective-permute-start.14 = (bf16[2,64,128]{2,1,0:T(8,128)(2,1)S(1)}, bf16[2,64,128]{2,1,0:T(8,128)(2,1)S(1)}, u32[]{:S(2)}, u32[]{:S(2)}) collective-permute-start(bf16[2,64,128]{2,1,0:T(8,128)(2,1)S(1)} %get-tuple-element.61), channel_id=1, source_target_pairs={{0,12},{4,8},{8,4},{12,0},{1,13},{5,9},{9,5},{13,1},{2,14},{6,10},... | collective-permute-start | bytes 98312 | tf_op jit(solution)/shard_map/ppermute | solution.py:423
  35.3 8.2 %collective-permute-start.10 = (bf16[2,64,384]{2,1,0:T(8,128)(2,1)S(1)}, bf16[2,64,384]{2,1,0:T(8,128)(2,1)S(1)}, u32[]{:S(2)}, u32[]{:S(2)}) collective-permute-start(bf16[2,64,384]{2,1,0:T(8,128)(2,1)S(1)} %get-tuple-element.57), channel_id=1, source_target_pairs={{0,8},{4,12},{8,0},{12,4},{1,9},{5,13},{9,1},{13,5},{2,10},{6,14},... | collective-permute-start | bytes 294920 | tf_op jit(solution)/shard_map/ppermute | solution.py:423
  37.7 8.4 %collective-permute-start.12 = (bf16[2,64,512]{2,1,0:T(8,128)(2,1)S(1)}, bf16[2,64,512]{2,1,0:T(8,128)(2,1)S(1)}, u32[]{:S(2)}, u32[]{:S(2)}) collective-permute-start(bf16[2,64,512]{2,1,0:T(8,128)(2,1)S(1)} %get-tuple-element.60), channel_id=1, source_target_pairs={{0,4},{4,0},{8,12},{12,8},{1,5},{5,1},{9,13},{13,9},{2,6},{6,2},{1... | collective-permute-start | bytes 393224 | tf_op jit(solution)/shard_map/ppermute | solution.py:423
  39.1 6.9 %collective-permute-start.11 = (bf16[2,64,384]{2,1,0:T(8,128)(2,1)S(1)}, bf16[2,64,384]{2,1,0:T(8,128)(2,1)S(1)}, u32[]{:S(2)}, u32[]{:S(2)}) collective-permute-start(bf16[2,64,384]{2,1,0:T(8,128)(2,1)S(1)} %get-tuple-element.58), channel_id=1, source_target_pairs={{0,12},{4,8},{8,4},{12,0},{1,13},{5,9},{9,5},{13,1},{2,14},{6,10},... | collective-permute-start | bytes 294920 | tf_op jit(solution)/shard_map/ppermute | solution.py:423

commit v19 on v18

--- a/solution.py
+++ b/solution.py
@@ -342,44 +342,62 @@
     )(att, mlp, in_vmem(wo))
 
 
-def combine_kernel(chunks, distances, owners, grid_features, *refs):
+def plan_kernel(owners, masks):
     s = lax.axis_index("shard")
+    count = owners.shape[0]
+    names = [owners[t, 0] for t in range(count)]
+    for t in range(count):
+        same = [(names[e] == names[t]).astype(jnp.int32) for e in range(t)]
+        rank = sum(same, jnp.int32(0))
+        for d in range(masks.shape[0]):
+            for j in range(CAP):
+                hit = (names[t] == s ^ d) & (rank == j)
+                masks[d, j, t] = jnp.full(masks.shape[3:], hit.astype(jnp.float32))
+
+
+def run_plan(owners, shards):
+    return pl.pallas_call(
+        plan_kernel,
+        out_shape=jax.ShapeDtypeStruct((shards, CAP, owners.shape[0], 8, 128), jnp.float32),
+        in_specs=[whole(pltpu.SMEM)],
+        out_specs=whole(pltpu.VMEM),
+        compiler_params=params(4),
+        cost_estimate=pl.CostEstimate(flops=0, bytes_accessed=1 << 18, transcendentals=0),
+        name="plan",
+    )(owners)
+
+
+def combine_kernel(chunks, distances, masks, grid_features, *refs):
     keeps, refs = refs[: len(chunks)], refs[len(chunks) :]
-    swaps, outs, ready = refs[: len(chunks)], refs[len(chunks) : -1], refs[-1]
+    swaps, outs = refs[: len(chunks)], refs[len(chunks) :]
     count = grid_features.shape[0]
     first = columns_of(chunks[0]).start
-    names = [owners[t, 0] for t in range(count)]
-    ranks = []
-    for t in range(count):
-        same = [(names[e] == names[t]).astype(jnp.int32) for e in range(t)]
-        ranks.append(sum(same, jnp.int32(0)))
     for c, keep, swap in zip(chunks, keeps, swaps):
         columns = columns_of(c)
         place = slice(columns.start - first, columns.stop - first)
+        updated = []
         for t in range(count):
             rows = slice(t * BLOCK, (t + 1) * BLOCK)
             partials = keep[rows, :].astype(jnp.float32) + swap[rows, :].astype(jnp.float32)
-            residual = grid_features[t, :, columns].astype(jnp.float32)
-            ready[t, :, place] = (residual + partials).astype(jnp.bfloat16)
-    ready[count] = jnp.zeros(ready.shape[1:], jnp.bfloat16)
-    for d, out in zip(distances, outs):
-        for j in range(CAP):
-            index = jnp.int32(count)
-            for t in range(count):
-                index = jnp.where((names[t] == s ^ d) & (ranks[t] == j), t, index)
-            out[j] = ready[index]
-
-
-def run_combine(chunks, distances, owners, grid_features, keeps, swaps):
+            updated.append(grid_features[t, :, columns].astype(jnp.float32) + partials)
+        for d, out in zip(distances, outs):
+            for j in range(CAP):
+                chosen = jnp.zeros_like(updated[0])
+                for t in range(count):
+                    row = jnp.concatenate([masks[d, j, t, 0:1, :]] * (WIDTHS[c] // 128), axis=1)
+                    chosen = jnp.where(jnp.broadcast_to(row, chosen.shape) > 0.5, updated[t], chosen)
+                out[j, :, place] = chosen.astype(jnp.bfloat16)
+
+
+def run_combine(chunks, distances, masks, grid_features, keeps, swaps):
     count, rows, _ = grid_features.shape
     width = sum(WIDTHS[c] for c in chunks)
     slot = jax.ShapeDtypeStruct((CAP, rows, width), jnp.bfloat16)
     return pl.pallas_call(
         functools.partial(combine_kernel, chunks, distances),
         out_shape=(slot,) * len(distances),
-        in_specs=[whole(pltpu.SMEM)] + vmem(1 + 2 * len(chunks)),
+        in_specs=vmem(2 + 2 * len(chunks)),
         out_specs=tuple(vmem(len(distances))),
-        scratch_shapes=[pltpu.VMEM((count + 1, rows, width), jnp.bfloat16)],
         compiler_params=params(8),
         cost_estimate=pl.CostEstimate(
             flops=60000 * count * rows * width,
@@ -387,7 +405,7 @@
             transcendentals=0,
         ),
         name="combine",
-    )(owners, grid_features, *keeps, *swaps)
+    )(masks, grid_features, *keeps, *swaps)
 
 
 def place_kernel(spots, *refs):
@@ -470,6 +488,8 @@
     blocked = (-1, BLOCK, 2 * half)
     mine_a = run_project((mesh, near, far, far_pair), key_weight, value_weight)
     sibling_a = swapped(mine_a, "sub")
+    named, _ = lax.optimization_barrier((owners, mine_a))
+    masks = run_plan(named, shards)
     table = run_table(mine_a.reshape(blocked), sibling_a.reshape(blocked), 2 * shards)
     mine_b = run_project((farther, straight), key_weight, value_weight)
     sibling_b = swapped(mine_b, "sub")
@@ -484,12 +504,12 @@
         received = swapped(send, "head")
         if c > 0:
             received, _ = lax.optimization_barrier((received, slots[c - 1][0]))
-        slots.append(run_combine((c,), (2, 3), owners, grid_features, (keep,), (received,)))
+        slots.append(run_combine((c,), (2, 3), masks, grid_features, (keep,), (received,)))
         keeps.append(keep)
         swaps.append(received)
     every = tuple(range(len(WIDTHS)))
     swaps[-1], _ = lax.optimization_barrier((swaps[-1], slots[-1][0]))
-    near_slots, own_slots = run_combine(every, (1, 0), owners, grid_features, keeps, swaps)
+    near_slots, own_slots = run_combine(every, (1, 0), masks, grid_features, keeps, swaps)
     for c in every:
         first = columns_of(c).start
         spots = [(2, first), (3, first)]

time: 47 us -> 46 us (0.979)
  Pallas kernels: 16.2 us -> 15.2 us
    pallas_call x3, Pallas kernels: 1.95 us -> 0.35 us  [run_combine(): pl.pallas_call(functools.partial(combine_kernel, chunks, distances), out_...]
    pallas_call x0 -> x1, Pallas kernels: none -> 0.62 us  [run_plan(): pl.pallas_call(plan_kernel, out_shape=jax.ShapeDtypeStruct((shards, CAP,...]
  transfers between devices with their start and end apart: 15 -> 15, of which waited for: 11 -> 10; matrix products, arithmetic and copies ran while one was open for 0% -> 0% of each run, Pallas kernels for 26% -> 24%
where the time goes in v19:
time: 46 us; the launch traced here: 45.8 us
  starting transfers between devices  18.1 us (39%)
  Pallas kernels  15.2 us (33%)
  waiting for transfers between devices  12.2 us (27%)
    ppermute x9, starting transfers between devices, crossed(): return lax.ppermute(x, 'shard', [(i, i ^ distance) for i in range(size)])  13.8 us
    ppermute x9, waiting for transfers between devices, crossed(): return lax.ppermute(x, 'shard', [(i, i ^ distance) for i in range(size)])  7.85 us
    ppermute x6, waiting for transfers between devices, swapped(): return lax.ppermute(x, axis, [(0, 1), (1, 0)])  4.39 us
    ppermute x6, starting transfers between devices, swapped(): return lax.ppermute(x, axis, [(0, 1), (1, 0)])  4.27 us
    pallas_call x1, Pallas kernels, run_stage(): pl.pallas_call(functools.partial(stage_kernel, axes), out_shape=tuple((ja...  4.1 us
    pallas_call x1, Pallas kernels, run_mlp(): pl.pallas_call(mlp_kernel, out_shape=(jax.ShapeDtypeStruct((rows, wq.shap...  3.33 us
    pallas_call x1, Pallas kernels, run_attend(): pl.pallas_call(attend_kernel, out_shape=(part, part, jax.ShapeDtypeStruct...  2.52 us
    pallas_call x2, Pallas kernels, run_place(): pl.pallas_call(functools.partial(place_kernel, spots), out_shape=jax.Shap...  1.45 us
  transfers between devices with their start and end apart: 15, of which 10 were waited for; matrix products, arithmetic and copies ran while one was open for 0% of the time, Pallas kernels for 24%

profile of v19, /device:TPU:0, one launch (start us, length us, event | category | flops | bytes accessed | tf_op | source)
XLA Modules:
  0.0 45.8 jit_solution(2974001119225748638)
XLA Ops:
  0.0 0.9 %pick.1 = bf16[64,1024]{1,0:T(8,128)(2,1)S(1)} custom-call(bf16[128,1024]{1,0:T(8,128)(2,1)} %mesh.1), custom_call_target="tpu_custom_call" | custom-call | bytes 524288 | tf_op jit(solution)/shard_map/pick/pallas_call | solution.py:112
  0.9 4.1 %collective-permute-start.1 = (bf16[64,1024]{1,0:T(8,128)(2,1)S(1)}, bf16[64,1024]{1,0:T(8,128)(2,1)S(1)}, u32[]{:S(2)}, u32[]{:S(2)}) collective-permute-start(bf16[64,1024]{1,0:T(8,128)(2,1)S(1)} %pick.1), channel_id=1, source_target_pairs={{0,8},{4,12},{8,0},{12,4},{1,9},{5,13},{9,1},{13,5},{2,10},{6,14},... | collective-permute-start | bytes 393224 | tf_op jit(solution)/shard_map/ppermute | solution.py:441
  5.0 1.5 %collective-permute-start = (bf16[256,512]{1,0:T(8,128)(2,1)}, bf16[256,512]{1,0:T(8,128)(2,1)S(1)}, u32[]{:S(2)}, u32[]{:S(2)}) collective-permute-start(bf16[256,512]{1,0:T(8,128)(2,1)} %bitcast.8), channel_id=1, source_target_pairs={{0,2},{2,0},{1,3},{3,1},{4,6},{6,4},{5,7},{7,5},{8,10},{10,8},{9,1... | collective-permute-start | bytes 786440 | tf_op jit(solution)/shard_map/ppermute | solution.py:445
  6.5 1.6 %collective-permute-start.3 = (bf16[128,1024]{1,0:T(8,128)(2,1)}, bf16[128,1024]{1,0:T(8,128)(2,1)S(1)}, u32[]{:S(2)}, u32[]{:S(2)}) collective-permute-start(bf16[128,1024]{1,0:T(8,128)(2,1)} %mesh.1), channel_id=1, source_target_pairs={{0,4},{4,0},{8,12},{12,8},{1,5},{5,1},{9,13},{13,9},{2,6},{6,2},{1... | collective-permute-start | bytes 786440 | tf_op jit(solution)/shard_map/ppermute | solution.py:441
  8.1 4.1 %stage.1 = (bf16[256,512]{1,0:T(8,128)(2,1)S(1)}, f32[1,1024]{1,0:T(1,128)S(1)}, bf16[1024,512]{1,0:T(8,128)(2,1)S(1)}, bf16[1024,2048]{1,0:T(8,128)(2,1)S(1)}, ...) custom-call(bf16[256,512]{1,0:T(8,128)(2,1)} %bitcast.9, ...), custom_call_target="tpu_custom_call" | custom-call | flops 20451328000 | bytes 204513280 | tf_op jit(solution)/shard_map/stage/pallas_call | solution.py:162
  12.2 0.3 collective-permute-start.5
  12.5 0.0 collective-permute-done.1.refs_2_
  12.5 0.5 %collective-permute-start.2 = (bf16[64,1024]{1,0:T(8,128)(2,1)S(1)}, bf16[64,1024]{1,0:T(8,128)(2,1)S(1)}, u32[]{:S(2)}, u32[]{:S(2)}) collective-permute-start(bf16[64,1024]{1,0:T(8,128)(2,1)S(1)} %collective-permute-done.1.refs_2_), channel_id=1, source_target_pairs={{0,2},{2,0},{1,3},{3,1},{4,6},{6,4},{5,7},{7,5},{8,10},{10,8},{9,1... | collective-permute-start | bytes 393224 | tf_op jit(solution)/shard_map/ppermute | solution.py:445
  13.0 0.7 %collective-permute-start.4 = (bf16[64,1024]{1,0:T(8,128)(2,1)S(1)}, bf16[64,1024]{1,0:T(8,128)(2,1)S(1)}, u32[]{:S(2)}, u32[]{:S(2)}) collective-permute-start(bf16[64,1024]{1,0:T(8,128)(2,1)S(1)} %collective-permute-done.1.refs_2_), channel_id=1, source_target_pairs={{0,4},{4,0},{8,12},{12,8},{1,5},{5,1},{9,13},{13,9},{2,6},{6,2},{1... | collective-permute-start | bytes 393224 | tf_op jit(solution)/shard_map/ppermute | solution.py:441
  13.7 0.0 collective-permute-done.other
  13.7 0.0 copy-start
  13.7 0.0 copy-start.1
  13.7 3.3 %mlp.1 = (bf16[256,512]{1,0:T(8,128)(2,1)S(1)}, f32[256,1024]{1,0:T(8,128)S(1)}) custom-call(bf16[256,512]{1,0:T(8,128)(2,1)S(1)} %get-tuple-element.36.own, bf16[256,512]{1,0:T(8,128)(2,1)S(1)} %collective-permute-done.other, f32[1,1024]{1,0:T(1,128)S(1)} %get-tuple-element.38.gain, bf16[1024,512]{1,0:T(8,128)(2,1)S(1)} %get-tuple-element.39.wq, ...), custom_call_target="tpu_custom_call" | custom-call | flops 2415919104 | bytes 9437184 | tf_op jit(solution)/shard_map/mlp/pallas_call | solution.py:85
  17.1 0.4 collective-permute-done.2.refs_3_
  17.5 1.2 %collective-permute-done.3.refs_1_ = bf16[128,1024]{1,0:T(8,128)(2,1)S(1)} collective-permute-done((bf16[128,1024]{1,0:T(8,128)(2,1)}, bf16[128,1024]{1,0:T(8,128)(2,1)S(1)}, u32[]{:S(2)}, u32[]{:S(2)}) %collective-permute-start.3) | collective-permute-done | bytes 262176 | tf_op jit(solution)/shard_map/ppermute | solution.py:441
  18.7 0.0 copy-done
  18.7 0.0 copy-done.1
  18.7 1.0 %project.2 = bf16[384,1024]{1,0:T(8,128)(2,1)S(1)} custom-call(bf16[128,1024]{1,0:T(8,128)(2,1)S(1)} %get-tuple-element.35.refs_0_, bf16[128,1024]{1,0:T(8,128)(2,1)S(1)} %collective-permute-done.3.refs_1_, bf16[64,1024]{1,0:T(8,128)(2,1)S(1)} %collective-permute-done.1.refs_2_, bf16[64,1024]{1,0:T(8,128)(2,1)S(1)} %collective-permute-done.2.refs_3_, ...), custom_call_target="tpu_custom_call" | custom-call | flops 60397977600 | bytes 275251200 | tf_op jit(solution)/shard_map/project/pallas_call | solution.py:190
  19.7 0.0 copy-start.2
  19.7 0.0 copy-start.4
  19.7 0.1 collective-permute-start.7
  19.8 0.2 collective-permute-done.5.refs_1_
  20.0 1.5 %collective-permute-done.4.refs_0_ = bf16[64,1024]{1,0:T(8,128)(2,1)S(1)} collective-permute-done((bf16[64,1024]{1,0:T(8,128)(2,1)S(1)}, bf16[64,1024]{1,0:T(8,128)(2,1)S(1)}, u32[]{:S(2)}, u32[]{:S(2)}) %collective-permute-start.4) | collective-permute-done | bytes 131104 | tf_op jit(solution)/shard_map/ppermute | solution.py:441
  21.5 0.4 project.3
  21.9 0.1 collective-permute-start.6
  22.0 0.1 collective-permute-done.7
  22.1 0.1 table.1.table_in
  22.2 1.4 %collective-permute-done.6 = bf16[128,1024]{1,0:T(8,128)(2,1)S(1)} collective-permute-done((bf16[128,1024]{1,0:T(8,128)(2,1)S(1)}, bf16[128,1024]{1,0:T(8,128)(2,1)S(1)}, u32[]{:S(2)}, u32[]{:S(2)}) %collective-permute-start.6) | collective-permute-done | bytes 262176 | tf_op jit(solution)/shard_map/ppermute | solution.py:445
  23.5 0.0 copy-done.2
  23.5 0.0 copy-done.4
  23.5 2.5 %attend.1 = (bf16[256,128]{1,0:T(8,128)(2,1)S(1)}, bf16[256,128]{1,0:T(8,128)(2,1)S(1)}, bf16[256,512]{1,0:T(8,128)(2,1)S(1)}, bf16[2,8,64,1024]{3,2,1,0:T(8,128)(2,1)S(1)}) custom-call(s32[4,8]{1,0:T(4,128)S(1)} %copy-done.4, bf16[256,512]{1,0:T(8,128)(2,1)S(1)} %get-tuple-element.50.q, ...), custom_call_target="tpu_custom_call", output_to_operand_aliasing={{3}: (4, {})} | custom-call | flops 13421772800 | bytes 41943040 | tf_op jit(solution)/shard_map/attend/pallas_call | solution.py:305
  26.1 0.7 %collective-permute-start.9 = (bf16[256,128]{1,0:T(8,128)(2,1)S(1)}, bf16[256,128]{1,0:T(8,128)(2,1)S(1)}, u32[]{:S(2)}, u32[]{:S(2)}) collective-permute-start(bf16[256,128]{1,0:T(8,128)(2,1)S(1)} %get-tuple-element.56), channel_id=1, source_target_pairs={{0,2},{2,0},{1,3},{3,1},{4,6},{6,4},{5,7},{7,5},{8,10},{10,8},{9,1... | collective-permute-start | bytes 196616 | tf_op jit(solution)/shard_map/ppermute | solution.py:445
  26.7 0.0 copy-start.5
  26.7 0.0 copy-start.3
  26.7 0.4 project_out.1
  27.2 1.5 %collective-permute-start.8 = (bf16[256,384]{1,0:T(8,128)(2,1)S(1)}, bf16[256,384]{1,0:T(8,128)(2,1)S(1)}, u32[]{:S(2)}, u32[]{:S(2)}) collective-permute-start(bf16[256,384]{1,0:T(8,128)(2,1)S(1)} %get-tuple-element.54), channel_id=1, source_target_pairs={{0,2},{2,0},{1,3},{3,1},{4,6},{6,4},{5,7},{7,5},{8,10},{10,8},{9,1... | collective-permute-start | bytes 589832 | tf_op jit(solution)/shard_map/ppermute | solution.py:445
  28.7 0.0 copy-done.5
  28.7 0.1 copy.14.owners
  28.7 0.6 %plan.1.masks = f32[4,2,4,8,128]{4,3,2,1,0:T(8,128)S(1)} custom-call(s32[4,1]{1,0:T(4,128)S(1)} %copy.14.owners), custom_call_target="tpu_custom_call" | custom-call | bytes 262144 | tf_op jit(solution)/shard_map/plan/pallas_call | solution.py:359
  29.4 1.7 %collective-permute-done.9.refs_1_.refs_2_ = bf16[256,128]{1,0:T(8,128)(2,1)S(1)} collective-permute-done((bf16[256,128]{1,0:T(8,128)(2,1)S(1)}, bf16[256,128]{1,0:T(8,128)(2,1)S(1)}, u32[]{:S(2)}, u32[]{:S(2)}) %collective-permute-start.9) | collective-permute-done | bytes 65568 | tf_op jit(solution)/shard_map/ppermute | solution.py:445
  31.1 0.0 copy-done.3
  31.1 0.2 collective-permute-start.13
  31.3 2.5 %collective-permute-start.14 = (bf16[2,64,128]{2,1,0:T(8,128)(2,1)S(1)}, bf16[2,64,128]{2,1,0:T(8,128)(2,1)S(1)}, u32[]{:S(2)}, u32[]{:S(2)}) collective-permute-start(bf16[2,64,128]{2,1,0:T(8,128)(2,1)S(1)} %get-tuple-element.63), channel_id=1, source_target_pairs={{0,12},{4,8},{8,4},{12,0},{1,13},{5,9},{9,5},{13,1},{2,14},{6,10},... | collective-permute-start | bytes 98312 | tf_op jit(solution)/shard_map/ppermute | solution.py:441
  33.8 0.8 %collective-permute-done.8.refs_1_.refs_3_ = bf16[256,384]{1,0:T(8,128)(2,1)S(1)} collective-permute-done((bf16[256,384]{1,0:T(8,128)(2,1)S(1)}, bf16[256,384]{1,0:T(8,128)(2,1)S(1)}, u32[]{:S(2)}, u32[]{:S(2)}) %collective-permute-start.8) | collective-permute-done | bytes 196640 | tf_op jit(solution)/shard_map/ppermute | solution.py:445
  34.6 0.1 combine.4
  34.7 1.2 %collective-permute-start.10 = (bf16[2,64,384]{2,1,0:T(8,128)(2,1)S(1)}, bf16[2,64,384]{2,1,0:T(8,128)(2,1)S(1)}, u32[]{:S(2)}, u32[]{:S(2)}) collective-permute-start(bf16[2,64,384]{2,1,0:T(8,128)(2,1)S(1)} %get-tuple-element.59), channel_id=1, source_target_pairs={{0,8},{4,12},{8,0},{12,4},{1,9},{5,13},{9,1},{13,5},{2,10},{6,14},... | collective-permute-start | bytes 294920 | tf_op jit(solution)/shard_map/ppermute | solution.py:441
  35.9 0.2 combine.5
  36.1 2.0 %collective-permute-start.12 = (bf16[2,64,512]{2,1,0:T(8,128)(2,1)S(1)}, bf16[2,64,512]{2,1,0:T(8,128)(2,1)S(1)}, u32[]{:S(2)}, u32[]{:S(2)}) collective-permute-start(bf16[2,64,512]{2,1,0:T(8,128)(2,1)S(1)} %get-tuple-element.62), channel_id=1, source_target_pairs={{0,4},{4,0},{8,12},{12,8},{1,5},{5,1},{9,13},{13,9},{2,6},{6,2},{1... | collective-permute-start | bytes 393224 | tf_op jit(solution)/shard_map/ppermute | solution.py:441
  38.1 1.3 %collective-permute-start.11 = (bf16[2,64,384]{2,1,0:T(8,128)(2,1)S(1)}, bf16[2,64,384]{2,1,0:T(8,128)(2,1)S(1)}, u32[]{:S(2)}, u32[]{:S(2)}) collective-permute-start(bf16[2,64,384]{2,1,0:T(8,128)(2,1)S(1)} %get-tuple-element.60), channel_id=1, source_target_pairs={{0,12},{4,8},{8,4},{12,0},{1,13},{5,9},{9,5},{13,1},{2,14},{6,10},... | collective-permute-start | bytes 294920 | tf_op jit(solution)/shard_map/ppermute | solution.py:441
  39.4 0.0 collective-permute-done.13.refs_0_
  39.4 0.0 collective-permute-done.14.refs_1_
  39.4 0.7 %place.2.refs_3_ = bf16[8,64,512]{2,1,0:T(8,128)(2,1)} custom-call(bf16[2,64,128]{2,1,0:T(8,128)(2,1)S(1)} %collective-permute-done.13.refs_0_, bf16[2,64,128]{2,1,0:T(8,128)(2,1)S(1)} %collective-permute-done.14.refs_1_, bf16[2,64,512]{2,1,0:T(8,128)(2,1)S(1)} %get-tuple-element.64.refs_2_), custom_call_target="tpu_custom_call" | custom-call | flops 39321600000 | tf_op jit(solution)/shard_map/place/pallas_call | solution.py:425
  40.1 2.5 %collective-permute-done.10.refs_0_ = bf16[2,64,384]{2,1,0:T(8,128)(2,1)S(1)} collective-permute-done((bf16[2,64,384]{2,1,0:T(8,128)(2,1)S(1)}, bf16[2,64,384]{2,1,0:T(8,128)(2,1)S(1)}, u32[]{:S(2)}, u32[]{:S(2)}) %collective-permute-start.10) | collective-permute-done | bytes 98336 | tf_op jit(solution)/shard_map/ppermute | solution.py:441
  42.7 2.4 %collective-permute-done.11.refs_1_ = bf16[2,64,384]{2,1,0:T(8,128)(2,1)S(1)} collective-permute-done((bf16[2,64,384]{2,1,0:T(8,128)(2,1)S(1)}, bf16[2,64,384]{2,1,0:T(8,128)(2,1)S(1)}, u32[]{:S(2)}, u32[]{:S(2)}) %collective-permute-start.11) | collective-permute-done | bytes 98336 | tf_op jit(solution)/shard_map/ppermute | solution.py:441
  45.1 0.0 collective-permute-done.12.refs_2_
  45.1 0.7 %place.3 = bf16[8,64,512]{2,1,0:T(8,128)(2,1)} custom-call(bf16[2,64,384]{2,1,0:T(8,128)(2,1)S(1)} %collective-permute-done.10.refs_0_, bf16[2,64,384]{2,1,0:T(8,128)(2,1)S(1)} %collective-permute-done.11.refs_1_, bf16[2,64,512]{2,1,0:T(8,128)(2,1)S(1)} %collective-permute-done.12.refs_2_, ...), custom_call_target="tpu_custom_call", output_to_operand_aliasing={{}: (3, {})} | custom-call | flops 65536000000 | tf_op jit(solution)/shard_map/place/pallas_call | solution.py:425
  (1 shorter events, 0.0 us)
Async XLA Ops:
  0.9 11.6 %collective-permute-start.1 = (bf16[64,1024]{1,0:T(8,128)(2,1)S(1)}, bf16[64,1024]{1,0:T(8,128)(2,1)S(1)}, u32[]{:S(2)}, u32[]{:S(2)}) collective-permute-start(bf16[64,1024]{1,0:T(8,128)(2,1)S(1)} %pick.1), channel_id=1, source_target_pairs={{0,8},{4,12},{8,0},{12,4},{1,9},{5,13},{9,1},{13,5},{2,10},{6,14},... | collective-permute-start | bytes 393224 | tf_op jit(solution)/shard_map/ppermute | solution.py:441
  5.0 8.7 %collective-permute-start = (bf16[256,512]{1,0:T(8,128)(2,1)}, bf16[256,512]{1,0:T(8,128)(2,1)S(1)}, u32[]{:S(2)}, u32[]{:S(2)}) collective-permute-start(bf16[256,512]{1,0:T(8,128)(2,1)} %bitcast.8), channel_id=1, source_target_pairs={{0,2},{2,0},{1,3},{3,1},{4,6},{6,4},{5,7},{7,5},{8,10},{10,8},{9,1... | collective-permute-start | bytes 786440 | tf_op jit(solution)/shard_map/ppermute | solution.py:445
  6.5 12.2 %collective-permute-start.3 = (bf16[128,1024]{1,0:T(8,128)(2,1)}, bf16[128,1024]{1,0:T(8,128)(2,1)S(1)}, u32[]{:S(2)}, u32[]{:S(2)}) collective-permute-start(bf16[128,1024]{1,0:T(8,128)(2,1)} %mesh.1), channel_id=1, source_target_pairs={{0,4},{4,0},{8,12},{12,8},{1,5},{5,1},{9,13},{13,9},{2,6},{6,2},{1... | collective-permute-start | bytes 786440 | tf_op jit(solution)/shard_map/ppermute | solution.py:441
  12.2 7.8 %collective-permute-start.5 = (bf16[64,1024]{1,0:T(8,128)(2,1)S(1)}, bf16[64,1024]{1,0:T(8,128)(2,1)S(1)}, u32[]{:S(2)}, u32[]{:S(2)}) collective-permute-start(bf16[64,1024]{1,0:T(8,128)(2,1)S(1)} %get-tuple-element.44), channel_id=1, source_target_pairs={{0,12},{4,8},{8,4},{12,0},{1,13},{5,9},{9,5},{13,1},{2,14},{6,10},... | collective-permute-start | bytes 393224 | tf_op jit(solution)/shard_map/ppermute | solution.py:441
  12.5 5.0 %collective-permute-start.2 = (bf16[64,1024]{1,0:T(8,128)(2,1)S(1)}, bf16[64,1024]{1,0:T(8,128)(2,1)S(1)}, u32[]{:S(2)}, u32[]{:S(2)}) collective-permute-start(bf16[64,1024]{1,0:T(8,128)(2,1)S(1)} %collective-permute-done.1.refs_2_), channel_id=1, source_target_pairs={{0,2},{2,0},{1,3},{3,1},{4,6},{6,4},{5,7},{7,5},{8,10},{10,8},{9,1... | collective-permute-start | bytes 393224 | tf_op jit(solution)/shard_map/ppermute | solution.py:445
  13.0 8.5 %collective-permute-start.4 = (bf16[64,1024]{1,0:T(8,128)(2,1)S(1)}, bf16[64,1024]{1,0:T(8,128)(2,1)S(1)}, u32[]{:S(2)}, u32[]{:S(2)}) collective-permute-start(bf16[64,1024]{1,0:T(8,128)(2,1)S(1)} %collective-permute-done.1.refs_2_), channel_id=1, source_target_pairs={{0,4},{4,0},{8,12},{12,8},{1,5},{5,1},{9,13},{13,9},{2,6},{6,2},{1... | collective-permute-start | bytes 393224 | tf_op jit(solution)/shard_map/ppermute | solution.py:441
  13.7 5.0 %copy-start = (bf16[1024,512]{1,0:T(8,128)(2,1)S(1)}, bf16[1024,512]{1,0:T(8,128)(2,1)}, u32[]{:S(2)}) copy-start(bf16[1024,512]{1,0:T(8,128)(2,1)} %refs_2_.3) | copy-start | bytes 3145732
  13.7 5.0 %copy-start.1 = (bf16[1024,512]{1,0:T(8,128)(2,1)S(1)}, bf16[1024,512]{1,0:T(8,128)(2,1)}, u32[]{:S(2)}) copy-start(bf16[1024,512]{1,0:T(8,128)(2,1)} %refs_3_.3) | copy-start | bytes 3145732
  19.7 3.8 %copy-start.2 = (bf16[512,1024]{1,0:T(8,128)(2,1)S(1)}, bf16[512,1024]{1,0:T(8,128)(2,1)}, u32[]{:S(2)}) copy-start(bf16[512,1024]{1,0:T(8,128)(2,1)} %wo.3) | copy-start | bytes 3145732
  19.7 3.8 %copy-start.4 = (s32[4,8]{1,0:T(4,128)S(1)}, s32[4,8]{1,0:T(4,128)}, u32[]{:S(2)}) copy-start(s32[4,8]{1,0:T(4,128)} %adjacency.1) | copy-start | bytes 388
  19.7 2.4 %collective-permute-start.7 = (bf16[384,1024]{1,0:T(8,128)(2,1)S(1)}, bf16[384,1024]{1,0:T(8,128)(2,1)S(1)}, u32[]{:S(2)}, u32[]{:S(2)}) collective-permute-start(bf16[384,1024]{1,0:T(8,128)(2,1)S(1)} %project.2), channel_id=1, source_target_pairs={{0,1},{1,0},{2,3},{3,2},{4,5},{5,4},{6,7},{7,6},{8,9},{9,8},{10,11... | collective-permute-start | bytes 2359304 | tf_op jit(solution)/shard_map/ppermute | solution.py:445
  21.9 1.6 %collective-permute-start.6 = (bf16[128,1024]{1,0:T(8,128)(2,1)S(1)}, bf16[128,1024]{1,0:T(8,128)(2,1)S(1)}, u32[]{:S(2)}, u32[]{:S(2)}) collective-permute-start(bf16[128,1024]{1,0:T(8,128)(2,1)S(1)} %project.3), channel_id=1, source_target_pairs={{0,1},{1,0},{2,3},{3,2},{4,5},{5,4},{6,7},{7,6},{8,9},{9,8},{10,11... | collective-permute-start | bytes 786440 | tf_op jit(solution)/shard_map/ppermute | solution.py:445
  26.1 5.0 %collective-permute-start.9 = (bf16[256,128]{1,0:T(8,128)(2,1)S(1)}, bf16[256,128]{1,0:T(8,128)(2,1)S(1)}, u32[]{:S(2)}, u32[]{:S(2)}) collective-permute-start(bf16[256,128]{1,0:T(8,128)(2,1)S(1)} %get-tuple-element.56), channel_id=1, source_target_pairs={{0,2},{2,0},{1,3},{3,1},{4,6},{6,4},{5,7},{7,5},{8,10},{10,8},{9,1... | collective-permute-start | bytes 196616 | tf_op jit(solution)/shard_map/ppermute | solution.py:445
  26.7 1.9 %copy-start.5 = (s32[4,1]{0,1:T(1,128)S(1)}, s32[4,1]{0,1:T(1,128)}, u32[]{:S(2)}) copy-start(s32[4,1]{0,1:T(1,128)} %param.12) | copy-start | bytes 52
  26.7 4.4 %copy-start.3 = (bf16[4,64,512]{2,1,0:T(8,128)(2,1)S(1)}, bf16[4,64,512]{2,1,0:T(8,128)(2,1)}, u32[]{:S(2)}) copy-start(bf16[4,64,512]{2,1,0:T(8,128)(2,1)} %grid_features.5) | copy-start | bytes 786436
  27.2 7.4 %collective-permute-start.8 = (bf16[256,384]{1,0:T(8,128)(2,1)S(1)}, bf16[256,384]{1,0:T(8,128)(2,1)S(1)}, u32[]{:S(2)}, u32[]{:S(2)}) collective-permute-start(bf16[256,384]{1,0:T(8,128)(2,1)S(1)} %get-tuple-element.54), channel_id=1, source_target_pairs={{0,2},{2,0},{1,3},{3,1},{4,6},{6,4},{5,7},{7,5},{8,10},{10,8},{9,1... | collective-permute-start | bytes 589832 | tf_op jit(solution)/shard_map/ppermute | solution.py:445
  31.1 8.3 %collective-permute-start.13 = (bf16[2,64,128]{2,1,0:T(8,128)(2,1)S(1)}, bf16[2,64,128]{2,1,0:T(8,128)(2,1)S(1)}, u32[]{:S(2)}, u32[]{:S(2)}) collective-permute-start(bf16[2,64,128]{2,1,0:T(8,128)(2,1)S(1)} %get-tuple-element.57), channel_id=1, source_target_pairs={{0,8},{4,12},{8,0},{12,4},{1,9},{5,13},{9,1},{13,5},{2,10},{6,14},... | collective-permute-start | bytes 98312 | tf_op jit(solution)/shard_map/ppermute | solution.py:441
  31.3 8.1 %collective-permute-start.14 = (bf16[2,64,128]{2,1,0:T(8,128)(2,1)S(1)}, bf16[2,64,128]{2,1,0:T(8,128)(2,1)S(1)}, u32[]{:S(2)}, u32[]{:S(2)}) collective-permute-start(bf16[2,64,128]{2,1,0:T(8,128)(2,1)S(1)} %get-tuple-element.63), channel_id=1, source_target_pairs={{0,12},{4,8},{8,4},{12,0},{1,13},{5,9},{9,5},{13,1},{2,14},{6,10},... | collective-permute-start | bytes 98312 | tf_op jit(solution)/shard_map/ppermute | solution.py:441
  34.7 8.0 %collective-permute-start.10 = (bf16[2,64,384]{2,1,0:T(8,128)(2,1)S(1)}, bf16[2,64,384]{2,1,0:T(8,128)(2,1)S(1)}, u32[]{:S(2)}, u32[]{:S(2)}) collective-permute-start(bf16[2,64,384]{2,1,0:T(8,128)(2,1)S(1)} %get-tuple-element.59), channel_id=1, source_target_pairs={{0,8},{4,12},{8,0},{12,4},{1,9},{5,13},{9,1},{13,5},{2,10},{6,14},... | collective-permute-start | bytes 294920 | tf_op jit(solution)/shard_map/ppermute | solution.py:441
  36.1 9.0 %collective-permute-start.12 = (bf16[2,64,512]{2,1,0:T(8,128)(2,1)S(1)}, bf16[2,64,512]{2,1,0:T(8,128)(2,1)S(1)}, u32[]{:S(2)}, u32[]{:S(2)}) collective-permute-start(bf16[2,64,512]{2,1,0:T(8,128)(2,1)S(1)} %get-tuple-element.62), channel_id=1, source_target_pairs={{0,4},{4,0},{8,12},{12,8},{1,5},{5,1},{9,13},{13,9},{2,6},{6,2},{1... | collective-permute-start | bytes 393224 | tf_op jit(solution)/shard_map/ppermute | solution.py:441
  38.1 7.0 %collective-permute-start.11 = (bf16[2,64,384]{2,1,0:T(8,128)(2,1)S(1)}, bf16[2,64,384]{2,1,0:T(8,128)(2,1)S(1)}, u32[]{:S(2)}, u32[]{:S(2)}) collective-permute-start(bf16[2,64,384]{2,1,0:T(8,128)(2,1)S(1)} %get-tuple-element.60), channel_id=1, source_target_pairs={{0,12},{4,8},{8,4},{12,0},{1,13},{5,9},{9,5},{13,1},{2,14},{6,10},... | collective-permute-start | bytes 294920 | tf_op jit(solution)/shard_map/ppermute | solution.py:441

commit v20 on v19

--- a/solution.py
+++ b/solution.py
@@ -14,7 +14,8 @@
 BLOCK = 64
 QUAD = 4
 WIDE = QUAD * HEAD_DIM
-WIDTHS = (128, 384)
+TILE = 128
+CHUNKS = ((0, 96), (96, 256))
 MIB = 1 << 20
 
 
@@ -221,27 +222,39 @@
     )(mine, sibling)
 
 
-def columns_of(c):
-    return slice(sum(WIDTHS[:c]), sum(WIDTHS[: c + 1]))
+def pieces_of(c):
+    low, high = CHUNKS[c]
+    pieces = []
+    for tile in range(low // BLOCK, -(-high // BLOCK)):
+        first, last = max(low, tile * BLOCK), min(high, (tile + 1) * BLOCK)
+        rows = slice(first - tile * BLOCK, last - tile * BLOCK)
+        pieces.append((tile, rows, slice(first - low, last - low)))
+    return pieces
 
 
 def project_out(c, att, mlp, wo, send, keep):
     half = att.shape[1]
-    chunk = columns_of(c)
     h = lax.axis_index("head")
+    pieces = pieces_of(c)
+    start, stop = pieces[0][0] * TILE, (pieces[-1][0] + 1) * TILE
 
     def write(head):
         for out, first, place in ((send, 0, 1 - head), (keep, half, head)):
-            extra = mlp[:, first + chunk.start : first + chunk.stop]
-            span = slice(place * half + chunk.start, place * half + chunk.stop)
-            out[...] = (extra + dot(att[...], wo[:, span])).astype(jnp.bfloat16)
+            extra = mlp[:, first + start : first + stop]
+            total = extra + dot(att[...], wo[:, place * half + start : place * half + stop])
+            total = total.astype(jnp.bfloat16)
+            for tile, rows, spot in pieces:
+                columns = slice(tile * TILE - start, (tile + 1) * TILE - start)
+                for t in range(out.shape[0]):
+                    block = slice(t * BLOCK + rows.start, t * BLOCK + rows.stop)
+                    out[t, spot, :] = total[block, columns]
 
     for head in range(2):
         pl.when(h == head)(functools.partial(write, head))
 
 
 def attend_kernel(
-    adjacency, q, mine, sibling, table_in, mlp, wo, send, keep, att, table
+    adjacency, q, mine, sibling, table_in, mlp, wo, send, keep, att, table, stacked_s, near_s, sem
 ):
     del table_in
     s = lax.axis_index("shard")
@@ -249,6 +262,8 @@
     u = lax.axis_index("sub")
     half = wo.shape[0]
     ready = table.shape[1] - mine.shape[0]
+    copy = pltpu.make_async_copy(adjacency, near_s, sem)
+    copy.start()
     for i, part in enumerate((mine, sibling)):
         table[i, ready:] = part[...]
     rows_of = lax.broadcasted_iota(jnp.int32, (WIDE, WIDE), 0) // BLOCK
@@ -257,11 +272,18 @@
     lane_head = lax.broadcasted_iota(jnp.int32, (BLOCK, WIDE), 1) // HEAD_DIM
     scale = HEAD_DIM**-0.5 * math.log2(math.e)
     groups = half // WIDE
+    steps = near_s.shape[0] * groups
+    for step in range(steps):
+        b, g = divmod(step, groups)
+        columns = slice(g * WIDE, (g + 1) * WIDE)
+        stacked = jnp.concatenate([q[b * BLOCK : (b + 1) * BLOCK, columns]] * QUAD, axis=0)
+        stacked_s[step] = jnp.where(diagonal, stacked, jnp.zeros_like(stacked))
+    copy.wait()
     places = []
-    for b in range(adjacency.shape[0]):
+    for b in range(near_s.shape[0]):
         places.append([])
-        for j in range(adjacency.shape[1]):
-            m = adjacency[b, j]
+        for j in range(near_s.shape[1]):
+            m = near_s[b, j]
             part = lax.rem(m, 2)
             core = lax.rem(m // 2, 2)
             distance = s ^ (m // 4)
@@ -272,13 +294,10 @@
         b, g = divmod(step, groups)
         columns = slice(g * WIDE, (g + 1) * WIDE)
         keys = jnp.concatenate([table[i, p, :, columns] for i, p in places[b]], axis=0)
-        stacked = jnp.concatenate([q[b * BLOCK : (b + 1) * BLOCK, columns]] * QUAD, axis=0)
-        stacked = jnp.where(diagonal, stacked, jnp.zeros_like(stacked))
         return lax.dot_general(
-            stacked, keys, (((1,), (1,)), ((), ())), preferred_element_type=jnp.float32
+            stacked_s[step], keys, (((1,), (1,)), ((), ())), preferred_element_type=jnp.float32
         )
 
-    steps = len(places) * groups
     scores = scores_of(0)
     for step in range(steps):
         following = scores_of(step + 1) if step + 1 < steps else None
@@ -300,7 +319,8 @@
 
 def run_attend(adjacency, q, mine, sibling, table, mlp, wo):
     rows, half = q.shape
-    part = jax.ShapeDtypeStruct((rows, WIDTHS[0]), jnp.bfloat16)
+    size = CHUNKS[0][1] - CHUNKS[0][0]
+    part = jax.ShapeDtypeStruct((rows // BLOCK, size, TILE), jnp.bfloat16)
     blocks = table.shape[0] * table.shape[1]
     send, keep, att, _ = pl.pallas_call(
         attend_kernel,
@@ -310,8 +330,13 @@
             jax.ShapeDtypeStruct(q.shape, jnp.bfloat16),
             jax.ShapeDtypeStruct(table.shape, jnp.bfloat16),
         ),
-        in_specs=[whole(pltpu.SMEM)] + vmem(6),
+        in_specs=[whole(pl.ANY)] + vmem(6),
         out_specs=tuple(vmem(4)),
+        scratch_shapes=[
+            pltpu.VMEM((rows // BLOCK * (half // WIDE), WIDE, WIDE), jnp.bfloat16),
+            pltpu.SMEM(adjacency.shape, jnp.int32),
+            pltpu.SemaphoreType.DMA(()),
+        ],
         input_output_aliases={4: 3},
         compiler_params=params(16),
         cost_estimate=pl.CostEstimate(
@@ -326,7 +351,8 @@
 
 def run_project_out(c, att, mlp, wo):
     rows, half = att.shape
-    part = jax.ShapeDtypeStruct((rows, WIDTHS[c]), jnp.bfloat16)
+    size = CHUNKS[c][1] - CHUNKS[c][0]
+    part = jax.ShapeDtypeStruct((rows // BLOCK, size, TILE), jnp.bfloat16)
     return pl.pallas_call(
         functools.partial(project_out, c),
         out_shape=(part, part),
@@ -371,27 +397,30 @@
     keeps, refs = refs[: len(chunks)], refs[len(chunks) :]
     swaps, outs = refs[: len(chunks)], refs[len(chunks) :]
     count = grid_features.shape[0]
-    first = columns_of(chunks[0]).start
+    first = CHUNKS[chunks[0]][0]
     for c, keep, swap in zip(chunks, keeps, swaps):
-        columns = columns_of(c)
-        place = slice(columns.start - first, columns.stop - first)
+        low, high = CHUNKS[c]
         updated = []
         for t in range(count):
-            rows = slice(t * BLOCK, (t + 1) * BLOCK)
-            partials = keep[rows, :].astype(jnp.float32) + swap[rows, :].astype(jnp.float32)
-            updated.append(grid_features[t, :, columns].astype(jnp.float32) + partials)
+            residual = [
+                grid_features[t, rows, tile * TILE : (tile + 1) * TILE]
+                for tile, rows, _ in pieces_of(c)
+            ]
+            residual = jnp.concatenate(residual, axis=0).astype(jnp.float32)
+            partials = keep[t].astype(jnp.float32) + swap[t].astype(jnp.float32)
+            updated.append(residual + partials)
         for d, out in zip(distances, outs):
             for j in range(CAP):
                 chosen = jnp.zeros_like(updated[0])
                 for t in range(count):
-                    row = jnp.concatenate([masks[d, j, t, 0:1, :]] * (WIDTHS[c] // 128), axis=1)
-                    chosen = jnp.where(jnp.broadcast_to(row, chosen.shape) > 0.5, updated[t], chosen)
-                out[j, :, place] = chosen.astype(jnp.bfloat16)
+                    mask = jnp.broadcast_to(masks[d, j, t, 0:1, :], chosen.shape)
+                    chosen = jnp.where(mask > 0.5, updated[t], chosen)
+                out[j, low - first : high - first, :] = chosen.astype(jnp.bfloat16)
 
 
 def run_combine(chunks, distances, masks, grid_features, keeps, swaps):
-    count, rows, _ = grid_features.shape
-    width = sum(WIDTHS[c] for c in chunks)
+    count = grid_features.shape[0]
+    rows, width = CHUNKS[chunks[-1]][1] - CHUNKS[chunks[0]][0], TILE
     slot = jax.ShapeDtypeStruct((CAP, rows, width), jnp.bfloat16)
     return pl.pallas_call(
         functools.partial(combine_kernel, chunks, distances),
@@ -412,22 +441,30 @@
     out, sem = refs[-2:]
     s = lax.axis_index("shard")
     copies = []
-    for i, (d, first) in enumerate(spots):
-        columns = pl.ds(first, refs[i].shape[2])
+    for ref, (d, chunks) in zip(refs, spots):
+        first = CHUNKS[chunks[0]][0]
         slots = pl.ds((s ^ d) * CAP, CAP)
-        copies.append(pltpu.make_async_copy(refs[i], out.at[slots, :, columns], sem.at[i]))
-        copies[i].start()
+        for c in chunks:
+            shift = CHUNKS[c][0] - first
+            for tile, rows, spot in pieces_of(c):
+                size = rows.stop - rows.start
+                source = ref.at[:, pl.ds(spot.start + shift, size), :]
+                columns = pl.ds(tile * TILE, TILE)
+                target = out.at[slots, pl.ds(rows.start, size), columns]
+                copies.append(pltpu.make_async_copy(source, target, sem.at[len(copies)]))
+                copies[-1].start()
     for copy in copies:
         copy.wait()
 
 
 def run_place(spots, arrived, placed, shape):
+    count = sum(len(pieces_of(c)) for _, chunks in spots for c in chunks)
     return pl.pallas_call(
         functools.partial(place_kernel, spots),
         out_shape=jax.ShapeDtypeStruct(shape, jnp.bfloat16),
         in_specs=vmem(len(arrived)) + [whole(pltpu.HBM)] * len(placed),
         out_specs=whole(pltpu.HBM),
-        scratch_shapes=[pltpu.SemaphoreType.DMA((len(arrived),))],
+        scratch_shapes=[pltpu.SemaphoreType.DMA((count,))],
         input_output_aliases={len(arrived): 0} if placed else {},
         compiler_params=params(4),
         cost_estimate=pl.CostEstimate(
@@ -488,17 +525,18 @@
     blocked = (-1, BLOCK, 2 * half)
     mine_a = run_project((mesh, near, far, far_pair), key_weight, value_weight)
     sibling_a = swapped(mine_a, "sub")
-    named, _ = lax.optimization_barrier((owners, mine_a))
-    masks = run_plan(named, shards)
     table = run_table(mine_a.reshape(blocked), sibling_a.reshape(blocked), 2 * shards)
     mine_b = run_project((farther, straight), key_weight, value_weight)
     sibling_b = swapped(mine_b, "sub")
     send, keep, att = run_attend(
         adjacency, queries, mine_b.reshape(blocked), sibling_b.reshape(blocked), table, mlp, output_weight
     )
+    named, _ = lax.optimization_barrier((owners, att))
+    masks = run_plan(named, shards)
     keeps, swaps, slots, placed = [], [], [], []
     shape = (shards * CAP, rows, half)
-    for c in range(len(WIDTHS)):
+    every = tuple(range(len(CHUNKS)))
+    for c in every:
         if c > 0:
             send, keep = run_project_out(c, att, mlp, output_weight)
         received = swapped(send, "head")
@@ -507,18 +545,16 @@
         slots.append(run_combine((c,), (2, 3), masks, grid_features, (keep,), (received,)))
         keeps.append(keep)
         swaps.append(received)
-    every = tuple(range(len(WIDTHS)))
     swaps[-1], _ = lax.optimization_barrier((swaps[-1], slots[-1][0]))
     near_slots, own_slots = run_combine(every, (1, 0), masks, grid_features, keeps, swaps)
     for c in every:
-        first = columns_of(c).start
-        spots = [(2, first), (3, first)]
+        spots = [(2, (c,)), (3, (c,))]
         arrived = [crossed(slot, d, shards) for d, slot in zip((2, 3), slots[c])]
         if c == 0:
-            spots.append((0, 0))
+            spots.append((0, every))
             arrived.append(own_slots)
-        if c == len(WIDTHS) - 1:
-            spots.append((1, 0))
+        if c == every[-1]:
+            spots.append((1, every))
             arrived.append(crossed(near_slots, 1, shards))
         placed = [run_place(spots, arrived, placed, shape)]
     return placed[0]

time: 46 us -> 45.4 us (0.987)
  waiting for transfers between devices: 12.2 us -> 11.4 us
    ppermute x9, waiting for transfers between devices: 7.85 us -> 7.36 us  [crossed(): return lax.ppermute(x, 'shard', [(i, i ^ distance) for i in range(size)])]
  transfers between devices with their start and end apart: 15 -> 15, of which waited for: 10 -> 10; matrix products, arithmetic and copies ran while one was open for 0% -> 0% of each run, Pallas kernels for 24% -> 25%
where the time goes in v20:
time: 45.4 us; the launch traced here: 45.3 us
  starting transfers between devices  18.1 us (40%)
  Pallas kernels  15.3 us (34%)
  waiting for transfers between devices  11.4 us (25%)
    ppermute x9, starting transfers between devices, crossed(): return lax.ppermute(x, 'shard', [(i, i ^ distance) for i in range(size)])  13.8 us
    ppermute x9, waiting for transfers between devices, crossed(): return lax.ppermute(x, 'shard', [(i, i ^ distance) for i in range(size)])  7.36 us
    ppermute x6, starting transfers between devices, swapped(): return lax.ppermute(x, axis, [(0, 1), (1, 0)])  4.27 us
    pallas_call x1, Pallas kernels, run_stage(): pl.pallas_call(functools.partial(stage_kernel, axes), out_shape=tuple((ja...  4.1 us
    ppermute x6, waiting for transfers between devices, swapped(): return lax.ppermute(x, axis, [(0, 1), (1, 0)])  4.03 us
    pallas_call x1, Pallas kernels, run_mlp(): pl.pallas_call(mlp_kernel, out_shape=(jax.ShapeDtypeStruct((rows, wq.shap...  3.33 us
    pallas_call x1, Pallas kernels, run_attend(): pl.pallas_call(attend_kernel, out_shape=(part, part, jax.ShapeDtypeStruct...  2.51 us
    pallas_call x2, Pallas kernels, run_place(): pl.pallas_call(functools.partial(place_kernel, spots), out_shape=jax.Shap...  1.56 us
  transfers between devices with their start and end apart: 15, of which 10 were waited for; matrix products, arithmetic and copies ran while one was open for 0% of the time, Pallas kernels for 25%

profile of v20, /device:TPU:0, one launch (start us, length us, event | category | flops | bytes accessed | tf_op | source)
XLA Modules:
  0.0 45.3 jit_solution(6408320057979497067)
XLA Ops:
  0.0 0.9 %pick.1 = bf16[64,1024]{1,0:T(8,128)(2,1)S(1)} custom-call(bf16[128,1024]{1,0:T(8,128)(2,1)} %mesh.1), custom_call_target="tpu_custom_call" | custom-call | bytes 524288 | tf_op jit(solution)/shard_map/pick/pallas_call | solution.py:113
  0.9 4.1 %collective-permute-start.1 = (bf16[64,1024]{1,0:T(8,128)(2,1)S(1)}, bf16[64,1024]{1,0:T(8,128)(2,1)S(1)}, u32[]{:S(2)}, u32[]{:S(2)}) collective-permute-start(bf16[64,1024]{1,0:T(8,128)(2,1)S(1)} %pick.1), channel_id=1, source_target_pairs={{0,8},{4,12},{8,0},{12,4},{1,9},{5,13},{9,1},{13,5},{2,10},{6,14},... | collective-permute-start | bytes 393224 | tf_op jit(solution)/shard_map/ppermute | solution.py:478
  5.0 1.5 %collective-permute-start = (bf16[256,512]{1,0:T(8,128)(2,1)}, bf16[256,512]{1,0:T(8,128)(2,1)S(1)}, u32[]{:S(2)}, u32[]{:S(2)}) collective-permute-start(bf16[256,512]{1,0:T(8,128)(2,1)} %bitcast.8), channel_id=1, source_target_pairs={{0,2},{2,0},{1,3},{3,1},{4,6},{6,4},{5,7},{7,5},{8,10},{10,8},{9,1... | collective-permute-start | bytes 786440 | tf_op jit(solution)/shard_map/ppermute | solution.py:482
  6.5 1.6 %collective-permute-start.3 = (bf16[128,1024]{1,0:T(8,128)(2,1)}, bf16[128,1024]{1,0:T(8,128)(2,1)S(1)}, u32[]{:S(2)}, u32[]{:S(2)}) collective-permute-start(bf16[128,1024]{1,0:T(8,128)(2,1)} %mesh.1), channel_id=1, source_target_pairs={{0,4},{4,0},{8,12},{12,8},{1,5},{5,1},{9,13},{13,9},{2,6},{6,2},{1... | collective-permute-start | bytes 786440 | tf_op jit(solution)/shard_map/ppermute | solution.py:478
  8.1 4.1 %stage.1 = (bf16[256,512]{1,0:T(8,128)(2,1)S(1)}, f32[1,1024]{1,0:T(1,128)S(1)}, bf16[1024,512]{1,0:T(8,128)(2,1)S(1)}, bf16[1024,2048]{1,0:T(8,128)(2,1)S(1)}, ...) custom-call(bf16[256,512]{1,0:T(8,128)(2,1)} %bitcast.9, ...), custom_call_target="tpu_custom_call" | custom-call | flops 20451328000 | bytes 204513280 | tf_op jit(solution)/shard_map/stage/pallas_call | solution.py:163
  12.2 0.3 collective-permute-start.5
  12.5 0.0 collective-permute-done.1.refs_2_
  12.5 0.5 %collective-permute-start.2 = (bf16[64,1024]{1,0:T(8,128)(2,1)S(1)}, bf16[64,1024]{1,0:T(8,128)(2,1)S(1)}, u32[]{:S(2)}, u32[]{:S(2)}) collective-permute-start(bf16[64,1024]{1,0:T(8,128)(2,1)S(1)} %collective-permute-done.1.refs_2_), channel_id=1, source_target_pairs={{0,2},{2,0},{1,3},{3,1},{4,6},{6,4},{5,7},{7,5},{8,10},{10,8},{9,1... | collective-permute-start | bytes 393224 | tf_op jit(solution)/shard_map/ppermute | solution.py:482
  13.0 0.7 %collective-permute-start.4 = (bf16[64,1024]{1,0:T(8,128)(2,1)S(1)}, bf16[64,1024]{1,0:T(8,128)(2,1)S(1)}, u32[]{:S(2)}, u32[]{:S(2)}) collective-permute-start(bf16[64,1024]{1,0:T(8,128)(2,1)S(1)} %collective-permute-done.1.refs_2_), channel_id=1, source_target_pairs={{0,4},{4,0},{8,12},{12,8},{1,5},{5,1},{9,13},{13,9},{2,6},{6,2},{1... | collective-permute-start | bytes 393224 | tf_op jit(solution)/shard_map/ppermute | solution.py:478
  13.7 0.0 collective-permute-done.other
  13.7 0.0 copy-start
  13.7 0.0 copy-start.1
  13.7 3.3 %mlp.1 = (bf16[256,512]{1,0:T(8,128)(2,1)S(1)}, f32[256,1024]{1,0:T(8,128)S(1)}) custom-call(bf16[256,512]{1,0:T(8,128)(2,1)S(1)} %get-tuple-element.35.own, bf16[256,512]{1,0:T(8,128)(2,1)S(1)} %collective-permute-done.other, f32[1,1024]{1,0:T(1,128)S(1)} %get-tuple-element.37.gain, bf16[1024,512]{1,0:T(8,128)(2,1)S(1)} %get-tuple-element.38.wq, ...), custom_call_target="tpu_custom_call" | custom-call | flops 2415919104 | bytes 9437184 | tf_op jit(solution)/shard_map/mlp/pallas_call | solution.py:86
  17.1 0.4 collective-permute-done.2.refs_3_
  17.5 1.2 %collective-permute-done.3.refs_1_ = bf16[128,1024]{1,0:T(8,128)(2,1)S(1)} collective-permute-done((bf16[128,1024]{1,0:T(8,128)(2,1)}, bf16[128,1024]{1,0:T(8,128)(2,1)S(1)}, u32[]{:S(2)}, u32[]{:S(2)}) %collective-permute-start.3) | collective-permute-done | bytes 262176 | tf_op jit(solution)/shard_map/ppermute | solution.py:478
  18.7 0.0 copy-done
  18.7 0.0 copy-done.1
  18.7 1.0 %project.3 = bf16[384,1024]{1,0:T(8,128)(2,1)S(1)} custom-call(bf16[128,1024]{1,0:T(8,128)(2,1)S(1)} %get-tuple-element.47.refs_0_, bf16[128,1024]{1,0:T(8,128)(2,1)S(1)} %collective-permute-done.3.refs_1_, bf16[64,1024]{1,0:T(8,128)(2,1)S(1)} %collective-permute-done.1.refs_2_, bf16[64,1024]{1,0:T(8,128)(2,1)S(1)} %collective-permute-done.2.refs_3_, ...), custom_call_target="tpu_custom_call" | custom-call | flops 60397977600 | bytes 275251200 | tf_op jit(solution)/shard_map/project/pallas_call | solution.py:191
  19.7 0.0 copy-start.2
  19.7 0.0 copy-start.4
  19.7 0.1 collective-permute-start.7
  19.8 0.2 collective-permute-done.5.refs_1_
  20.0 1.5 %collective-permute-done.4.refs_0_ = bf16[64,1024]{1,0:T(8,128)(2,1)S(1)} collective-permute-done((bf16[64,1024]{1,0:T(8,128)(2,1)S(1)}, bf16[64,1024]{1,0:T(8,128)(2,1)S(1)}, u32[]{:S(2)}, u32[]{:S(2)}) %collective-permute-start.4) | collective-permute-done | bytes 131104 | tf_op jit(solution)/shard_map/ppermute | solution.py:478
  21.5 0.4 project.2
  21.9 0.1 collective-permute-start.6
  22.0 0.1 collective-permute-done.7
  22.1 0.1 table.1.table_in
  22.2 1.4 %collective-permute-done.6 = bf16[128,1024]{1,0:T(8,128)(2,1)S(1)} collective-permute-done((bf16[128,1024]{1,0:T(8,128)(2,1)S(1)}, bf16[128,1024]{1,0:T(8,128)(2,1)S(1)}, u32[]{:S(2)}, u32[]{:S(2)}) %collective-permute-start.6) | collective-permute-done | bytes 262176 | tf_op jit(solution)/shard_map/ppermute | solution.py:482
  23.5 0.0 copy-done.2
  23.5 0.0 copy-done.4
  23.5 2.5 %attend.1 = (bf16[4,96,128]{2,1,0:T(8,128)(2,1)S(1)}, bf16[4,96,128]{2,1,0:T(8,128)(2,1)S(1)}, bf16[256,512]{1,0:T(8,128)(2,1)S(1)}, bf16[2,8,64,1024]{3,2,1,0:T(8,128)(2,1)S(1)}) custom-call(s32[4,8]{1,0:T(4,128)S(1)} %copy-done.4, bf16[256,512]{1,0:T(8,128)(2,1)S(1)} %get-tuple-element.46.q, ...), custom_call_target="tpu_custom_call", output_to_operand_aliasing={{3}: (4, {})} | custom-call | flops 13421772800 | bytes 41943040 | tf_op jit(solution)/shard_map/attend/pallas_call | solution.py:325
  26.0 0.6 %collective-permute-start.9 = (bf16[4,96,128]{2,1,0:T(8,128)(2,1)S(1)}, bf16[4,96,128]{2,1,0:T(8,128)(2,1)S(1)}, u32[]{:S(2)}, u32[]{:S(2)}) collective-permute-start(bf16[4,96,128]{2,1,0:T(8,128)(2,1)S(1)} %get-tuple-element.56), channel_id=1, source_target_pairs={{0,2},{2,0},{1,3},{3,1},{4,6},{6,4},{5,7},{7,5},{8,10},{10,8},{9,1... | collective-permute-start | bytes 294920 | tf_op jit(solution)/shard_map/ppermute | solution.py:482
  26.7 0.0 copy-start.5
  26.7 0.0 copy-start.3
  26.7 0.4 project_out.1
  27.1 0.2 copy-done.5
  27.3 0.1 copy.14.owners
  27.4 0.6 %plan.1.masks = f32[4,2,4,8,128]{4,3,2,1,0:T(8,128)S(1)} custom-call(s32[4,1]{1,0:T(4,128)S(1)} %copy.14.owners), custom_call_target="tpu_custom_call" | custom-call | bytes 262144 | tf_op jit(solution)/shard_map/plan/pallas_call | solution.py:385
  28.1 1.5 %collective-permute-start.8 = (bf16[4,160,128]{2,1,0:T(8,128)(2,1)S(1)}, bf16[4,160,128]{2,1,0:T(8,128)(2,1)S(1)}, u32[]{:S(2)}, u32[]{:S(2)}) collective-permute-start(bf16[4,160,128]{2,1,0:T(8,128)(2,1)S(1)} %get-tuple-element.54), channel_id=1, source_target_pairs={{0,2},{2,0},{1,3},{3,1},{4,6},{6,4},{5,7},{7,5},{8,10},{10,8},{9,1... | collective-permute-start | bytes 491528 | tf_op jit(solution)/shard_map/ppermute | solution.py:482
  29.6 1.8 %collective-permute-done.9.refs_1_.refs_2_ = bf16[4,96,128]{2,1,0:T(8,128)(2,1)S(1)} collective-permute-done((bf16[4,96,128]{2,1,0:T(8,128)(2,1)S(1)}, bf16[4,96,128]{2,1,0:T(8,128)(2,1)S(1)}, u32[]{:S(2)}, u32[]{:S(2)}) %collective-permute-start.9) | collective-permute-done | bytes 98336 | tf_op jit(solution)/shard_map/ppermute | solution.py:482
  31.3 0.0 copy-done.3
  31.3 0.1 combine.3
  31.4 0.5 %collective-permute-start.13 = (bf16[2,96,128]{2,1,0:T(8,128)(2,1)S(1)}, bf16[2,96,128]{2,1,0:T(8,128)(2,1)S(1)}, u32[]{:S(2)}, u32[]{:S(2)}) collective-permute-start(bf16[2,96,128]{2,1,0:T(8,128)(2,1)S(1)} %get-tuple-element.57), channel_id=1, source_target_pairs={{0,8},{4,12},{8,0},{12,4},{1,9},{5,13},{9,1},{13,5},{2,10},{6,14},... | collective-permute-start | bytes 147464 | tf_op jit(solution)/shard_map/ppermute | solution.py:478
  31.9 2.1 %collective-permute-start.14 = (bf16[2,96,128]{2,1,0:T(8,128)(2,1)S(1)}, bf16[2,96,128]{2,1,0:T(8,128)(2,1)S(1)}, u32[]{:S(2)}, u32[]{:S(2)}) collective-permute-start(bf16[2,96,128]{2,1,0:T(8,128)(2,1)S(1)} %get-tuple-element.63), channel_id=1, source_target_pairs={{0,12},{4,8},{8,4},{12,0},{1,13},{5,9},{9,5},{13,1},{2,14},{6,10},... | collective-permute-start | bytes 147464 | tf_op jit(solution)/shard_map/ppermute | solution.py:478
  34.0 0.5 %collective-permute-done.8.refs_1_.refs_3_ = bf16[4,160,128]{2,1,0:T(8,128)(2,1)S(1)} collective-permute-done((bf16[4,160,128]{2,1,0:T(8,128)(2,1)S(1)}, bf16[4,160,128]{2,1,0:T(8,128)(2,1)S(1)}, u32[]{:S(2)}, u32[]{:S(2)}) %collective-permute-start.8) | collective-permute-done | bytes 163872 | tf_op jit(solution)/shard_map/ppermute | solution.py:482
  34.5 0.1 combine.4
  34.6 1.6 %collective-permute-start.10 = (bf16[2,160,128]{2,1,0:T(8,128)(2,1)S(1)}, bf16[2,160,128]{2,1,0:T(8,128)(2,1)S(1)}, u32[]{:S(2)}, u32[]{:S(2)}) collective-permute-start(bf16[2,160,128]{2,1,0:T(8,128)(2,1)S(1)} %get-tuple-element.59), channel_id=1, source_target_pairs={{0,8},{4,12},{8,0},{12,4},{1,9},{5,13},{9,1},{13,5},{2,10},{6,14},... | collective-permute-start | bytes 245768 | tf_op jit(solution)/shard_map/ppermute | solution.py:478
  36.1 0.2 combine.5
  36.3 1.6 %collective-permute-start.12 = (bf16[2,256,128]{2,1,0:T(8,128)(2,1)S(1)}, bf16[2,256,128]{2,1,0:T(8,128)(2,1)S(1)}, u32[]{:S(2)}, u32[]{:S(2)}) collective-permute-start(bf16[2,256,128]{2,1,0:T(8,128)(2,1)S(1)} %get-tuple-element.62), channel_id=1, source_target_pairs={{0,4},{4,0},{8,12},{12,8},{1,5},{5,1},{9,13},{13,9},{2,6},{6,2},{1... | collective-permute-start | bytes 393224 | tf_op jit(solution)/shard_map/ppermute | solution.py:478
  37.9 1.4 %collective-permute-start.11 = (bf16[2,160,128]{2,1,0:T(8,128)(2,1)S(1)}, bf16[2,160,128]{2,1,0:T(8,128)(2,1)S(1)}, u32[]{:S(2)}, u32[]{:S(2)}) collective-permute-start(bf16[2,160,128]{2,1,0:T(8,128)(2,1)S(1)} %get-tuple-element.60), channel_id=1, source_target_pairs={{0,12},{4,8},{8,4},{12,0},{1,13},{5,9},{9,5},{13,1},{2,14},{6,10},... | collective-permute-start | bytes 245768 | tf_op jit(solution)/shard_map/ppermute | solution.py:478
  39.3 0.0 collective-permute-done.13.refs_0_
  39.3 0.0 collective-permute-done.14.refs_1_
  39.3 0.8 %place.2.refs_3_ = bf16[8,64,512]{2,1,0:T(8,128)(2,1)} custom-call(bf16[2,96,128]{2,1,0:T(8,128)(2,1)S(1)} %collective-permute-done.13.refs_0_, bf16[2,96,128]{2,1,0:T(8,128)(2,1)S(1)} %collective-permute-done.14.refs_1_, bf16[2,256,128]{2,1,0:T(8,128)(2,1)S(1)} %get-tuple-element.64.refs_2_), custom_call_target="tpu_custom_call" | custom-call | flops 45875200000 | tf_op jit(solution)/shard_map/place/pallas_call | solution.py:462
  40.0 3.2 %collective-permute-done.10.refs_0_ = bf16[2,160,128]{2,1,0:T(8,128)(2,1)S(1)} collective-permute-done((bf16[2,160,128]{2,1,0:T(8,128)(2,1)S(1)}, bf16[2,160,128]{2,1,0:T(8,128)(2,1)S(1)}, u32[]{:S(2)}, u32[]{:S(2)}) %collective-permute-start.10) | collective-permute-done | bytes 81952 | tf_op jit(solution)/shard_map/ppermute | solution.py:478
  43.2 1.3 %collective-permute-done.11.refs_1_ = bf16[2,160,128]{2,1,0:T(8,128)(2,1)S(1)} collective-permute-done((bf16[2,160,128]{2,1,0:T(8,128)(2,1)S(1)}, bf16[2,160,128]{2,1,0:T(8,128)(2,1)S(1)}, u32[]{:S(2)}, u32[]{:S(2)}) %collective-permute-start.11) | collective-permute-done | bytes 81952 | tf_op jit(solution)/shard_map/ppermute | solution.py:478
  44.5 0.0 collective-permute-done.12.refs_2_
  44.5 0.8 %place.3 = bf16[8,64,512]{2,1,0:T(8,128)(2,1)} custom-call(bf16[2,160,128]{2,1,0:T(8,128)(2,1)S(1)} %collective-permute-done.10.refs_0_, bf16[2,160,128]{2,1,0:T(8,128)(2,1)S(1)} %collective-permute-done.11.refs_1_, bf16[2,256,128]{2,1,0:T(8,128)(2,1)S(1)} %collective-permute-done.12.refs_2_, ...), custom_call_target="tpu_custom_call", output_to_operand_aliasing={{}: (3, {})} | custom-call | flops 58982400000 | tf_op jit(solution)/shard_map/place/pallas_call | solution.py:462
Async XLA Ops:
  0.9 11.6 %collective-permute-start.1 = (bf16[64,1024]{1,0:T(8,128)(2,1)S(1)}, bf16[64,1024]{1,0:T(8,128)(2,1)S(1)}, u32[]{:S(2)}, u32[]{:S(2)}) collective-permute-start(bf16[64,1024]{1,0:T(8,128)(2,1)S(1)} %pick.1), channel_id=1, source_target_pairs={{0,8},{4,12},{8,0},{12,4},{1,9},{5,13},{9,1},{13,5},{2,10},{6,14},... | collective-permute-start | bytes 393224 | tf_op jit(solution)/shard_map/ppermute | solution.py:478
  5.0 8.7 %collective-permute-start = (bf16[256,512]{1,0:T(8,128)(2,1)}, bf16[256,512]{1,0:T(8,128)(2,1)S(1)}, u32[]{:S(2)}, u32[]{:S(2)}) collective-permute-start(bf16[256,512]{1,0:T(8,128)(2,1)} %bitcast.8), channel_id=1, source_target_pairs={{0,2},{2,0},{1,3},{3,1},{4,6},{6,4},{5,7},{7,5},{8,10},{10,8},{9,1... | collective-permute-start | bytes 786440 | tf_op jit(solution)/shard_map/ppermute | solution.py:482
  6.5 12.2 %collective-permute-start.3 = (bf16[128,1024]{1,0:T(8,128)(2,1)}, bf16[128,1024]{1,0:T(8,128)(2,1)S(1)}, u32[]{:S(2)}, u32[]{:S(2)}) collective-permute-start(bf16[128,1024]{1,0:T(8,128)(2,1)} %mesh.1), channel_id=1, source_target_pairs={{0,4},{4,0},{8,12},{12,8},{1,5},{5,1},{9,13},{13,9},{2,6},{6,2},{1... | collective-permute-start | bytes 786440 | tf_op jit(solution)/shard_map/ppermute | solution.py:478
  12.2 7.8 %collective-permute-start.5 = (bf16[64,1024]{1,0:T(8,128)(2,1)S(1)}, bf16[64,1024]{1,0:T(8,128)(2,1)S(1)}, u32[]{:S(2)}, u32[]{:S(2)}) collective-permute-start(bf16[64,1024]{1,0:T(8,128)(2,1)S(1)} %get-tuple-element.43), channel_id=1, source_target_pairs={{0,12},{4,8},{8,4},{12,0},{1,13},{5,9},{9,5},{13,1},{2,14},{6,10},... | collective-permute-start | bytes 393224 | tf_op jit(solution)/shard_map/ppermute | solution.py:478
  12.5 5.0 %collective-permute-start.2 = (bf16[64,1024]{1,0:T(8,128)(2,1)S(1)}, bf16[64,1024]{1,0:T(8,128)(2,1)S(1)}, u32[]{:S(2)}, u32[]{:S(2)}) collective-permute-start(bf16[64,1024]{1,0:T(8,128)(2,1)S(1)} %collective-permute-done.1.refs_2_), channel_id=1, source_target_pairs={{0,2},{2,0},{1,3},{3,1},{4,6},{6,4},{5,7},{7,5},{8,10},{10,8},{9,1... | collective-permute-start | bytes 393224 | tf_op jit(solution)/shard_map/ppermute | solution.py:482
  13.0 8.5 %collective-permute-start.4 = (bf16[64,1024]{1,0:T(8,128)(2,1)S(1)}, bf16[64,1024]{1,0:T(8,128)(2,1)S(1)}, u32[]{:S(2)}, u32[]{:S(2)}) collective-permute-start(bf16[64,1024]{1,0:T(8,128)(2,1)S(1)} %collective-permute-done.1.refs_2_), channel_id=1, source_target_pairs={{0,4},{4,0},{8,12},{12,8},{1,5},{5,1},{9,13},{13,9},{2,6},{6,2},{1... | collective-permute-start | bytes 393224 | tf_op jit(solution)/shard_map/ppermute | solution.py:478
  13.7 5.0 %copy-start = (bf16[1024,512]{1,0:T(8,128)(2,1)S(1)}, bf16[1024,512]{1,0:T(8,128)(2,1)}, u32[]{:S(2)}) copy-start(bf16[1024,512]{1,0:T(8,128)(2,1)} %refs_4_.3) | copy-start | bytes 3145732
  13.7 5.0 %copy-start.1 = (bf16[1024,512]{1,0:T(8,128)(2,1)S(1)}, bf16[1024,512]{1,0:T(8,128)(2,1)}, u32[]{:S(2)}) copy-start(bf16[1024,512]{1,0:T(8,128)(2,1)} %refs_5_.3) | copy-start | bytes 3145732
  19.7 3.8 %copy-start.2 = (bf16[512,1024]{1,0:T(8,128)(2,1)S(1)}, bf16[512,1024]{1,0:T(8,128)(2,1)}, u32[]{:S(2)}) copy-start(bf16[512,1024]{1,0:T(8,128)(2,1)} %wo.3) | copy-start | bytes 3145732
  19.7 3.8 %copy-start.4 = (s32[4,8]{1,0:T(4,128)S(1)}, s32[4,8]{1,0:T(4,128)}, u32[]{:S(2)}) copy-start(s32[4,8]{1,0:T(4,128)} %adjacency.1) | copy-start | bytes 388
  19.7 2.4 %collective-permute-start.7 = (bf16[384,1024]{1,0:T(8,128)(2,1)S(1)}, bf16[384,1024]{1,0:T(8,128)(2,1)S(1)}, u32[]{:S(2)}, u32[]{:S(2)}) collective-permute-start(bf16[384,1024]{1,0:T(8,128)(2,1)S(1)} %project.3), channel_id=1, source_target_pairs={{0,1},{1,0},{2,3},{3,2},{4,5},{5,4},{6,7},{7,6},{8,9},{9,8},{10,11... | collective-permute-start | bytes 2359304 | tf_op jit(solution)/shard_map/ppermute | solution.py:482
  21.9 1.6 %collective-permute-start.6 = (bf16[128,1024]{1,0:T(8,128)(2,1)S(1)}, bf16[128,1024]{1,0:T(8,128)(2,1)S(1)}, u32[]{:S(2)}, u32[]{:S(2)}) collective-permute-start(bf16[128,1024]{1,0:T(8,128)(2,1)S(1)} %project.2), channel_id=1, source_target_pairs={{0,1},{1,0},{2,3},{3,2},{4,5},{5,4},{6,7},{7,6},{8,9},{9,8},{10,11... | collective-permute-start | bytes 786440 | tf_op jit(solution)/shard_map/ppermute | solution.py:482
  26.0 5.3 %collective-permute-start.9 = (bf16[4,96,128]{2,1,0:T(8,128)(2,1)S(1)}, bf16[4,96,128]{2,1,0:T(8,128)(2,1)S(1)}, u32[]{:S(2)}, u32[]{:S(2)}) collective-permute-start(bf16[4,96,128]{2,1,0:T(8,128)(2,1)S(1)} %get-tuple-element.56), channel_id=1, source_target_pairs={{0,2},{2,0},{1,3},{3,1},{4,6},{6,4},{5,7},{7,5},{8,10},{10,8},{9,1... | collective-permute-start | bytes 294920 | tf_op jit(solution)/shard_map/ppermute | solution.py:482
  26.7 0.7 %copy-start.5 = (s32[4,1]{0,1:T(1,128)S(1)}, s32[4,1]{0,1:T(1,128)}, u32[]{:S(2)}) copy-start(s32[4,1]{0,1:T(1,128)} %param.12) | copy-start | bytes 52
  26.7 4.6 %copy-start.3 = (bf16[4,64,512]{2,1,0:T(8,128)(2,1)S(1)}, bf16[4,64,512]{2,1,0:T(8,128)(2,1)}, u32[]{:S(2)}) copy-start(bf16[4,64,512]{2,1,0:T(8,128)(2,1)} %grid_features.5) | copy-start | bytes 786436
  28.1 6.4 %collective-permute-start.8 = (bf16[4,160,128]{2,1,0:T(8,128)(2,1)S(1)}, bf16[4,160,128]{2,1,0:T(8,128)(2,1)S(1)}, u32[]{:S(2)}, u32[]{:S(2)}) collective-permute-start(bf16[4,160,128]{2,1,0:T(8,128)(2,1)S(1)} %get-tuple-element.54), channel_id=1, source_target_pairs={{0,2},{2,0},{1,3},{3,1},{4,6},{6,4},{5,7},{7,5},{8,10},{10,8},{9,1... | collective-permute-start | bytes 491528 | tf_op jit(solution)/shard_map/ppermute | solution.py:482
  31.4 7.9 %collective-permute-start.13 = (bf16[2,96,128]{2,1,0:T(8,128)(2,1)S(1)}, bf16[2,96,128]{2,1,0:T(8,128)(2,1)S(1)}, u32[]{:S(2)}, u32[]{:S(2)}) collective-permute-start(bf16[2,96,128]{2,1,0:T(8,128)(2,1)S(1)} %get-tuple-element.57), channel_id=1, source_target_pairs={{0,8},{4,12},{8,0},{12,4},{1,9},{5,13},{9,1},{13,5},{2,10},{6,14},... | collective-permute-start | bytes 147464 | tf_op jit(solution)/shard_map/ppermute | solution.py:478
  31.9 7.4 %collective-permute-start.14 = (bf16[2,96,128]{2,1,0:T(8,128)(2,1)S(1)}, bf16[2,96,128]{2,1,0:T(8,128)(2,1)S(1)}, u32[]{:S(2)}, u32[]{:S(2)}) collective-permute-start(bf16[2,96,128]{2,1,0:T(8,128)(2,1)S(1)} %get-tuple-element.63), channel_id=1, source_target_pairs={{0,12},{4,8},{8,4},{12,0},{1,13},{5,9},{9,5},{13,1},{2,14},{6,10},... | collective-permute-start | bytes 147464 | tf_op jit(solution)/shard_map/ppermute | solution.py:478
  34.6 8.6 %collective-permute-start.10 = (bf16[2,160,128]{2,1,0:T(8,128)(2,1)S(1)}, bf16[2,160,128]{2,1,0:T(8,128)(2,1)S(1)}, u32[]{:S(2)}, u32[]{:S(2)}) collective-permute-start(bf16[2,160,128]{2,1,0:T(8,128)(2,1)S(1)} %get-tuple-element.59), channel_id=1, source_target_pairs={{0,8},{4,12},{8,0},{12,4},{1,9},{5,13},{9,1},{13,5},{2,10},{6,14},... | collective-permute-start | bytes 245768 | tf_op jit(solution)/shard_map/ppermute | solution.py:478
  36.3 8.2 %collective-permute-start.12 = (bf16[2,256,128]{2,1,0:T(8,128)(2,1)S(1)}, bf16[2,256,128]{2,1,0:T(8,128)(2,1)S(1)}, u32[]{:S(2)}, u32[]{:S(2)}) collective-permute-start(bf16[2,256,128]{2,1,0:T(8,128)(2,1)S(1)} %get-tuple-element.62), channel_id=1, source_target_pairs={{0,4},{4,0},{8,12},{12,8},{1,5},{5,1},{9,13},{13,9},{2,6},{6,2},{1... | collective-permute-start | bytes 393224 | tf_op jit(solution)/shard_map/ppermute | solution.py:478
  37.9 6.6 %collective-permute-start.11 = (bf16[2,160,128]{2,1,0:T(8,128)(2,1)S(1)}, bf16[2,160,128]{2,1,0:T(8,128)(2,1)S(1)}, u32[]{:S(2)}, u32[]{:S(2)}) collective-permute-start(bf16[2,160,128]{2,1,0:T(8,128)(2,1)S(1)} %get-tuple-element.60), channel_id=1, source_target_pairs={{0,12},{4,8},{8,4},{12,0},{1,13},{5,9},{9,5},{13,1},{2,14},{6,10},... | collective-permute-start | bytes 245768 | tf_op jit(solution)/shard_map/ppermute | solution.py:478

commit v21 on v20

--- a/solution.py
+++ b/solution.py
@@ -15,7 +15,7 @@
 QUAD = 4
 WIDE = QUAD * HEAD_DIM
 TILE = 128
-CHUNKS = ((0, 96), (96, 256))
+CHUNKS = ((0, 80), (80, 256))
 MIB = 1 << 20
 
 
@@ -388,7 +388,9 @@
         in_specs=[whole(pltpu.SMEM)],
         out_specs=whole(pltpu.VMEM),
         compiler_params=params(4),
-        cost_estimate=pl.CostEstimate(flops=0, bytes_accessed=1 << 18, transcendentals=0),
+        cost_estimate=pl.CostEstimate(
+            flops=100000000, bytes_accessed=1 << 18, transcendentals=0
+        ),
         name="plan",
     )(owners)
 
@@ -531,8 +533,6 @@
     send, keep, att = run_attend(
         adjacency, queries, mine_b.reshape(blocked), sibling_b.reshape(blocked), table, mlp, output_weight
     )
-    named, _ = lax.optimization_barrier((owners, att))
-    masks = run_plan(named, shards)
     keeps, swaps, slots, placed = [], [], [], []
     shape = (shards * CAP, rows, half)
     every = tuple(range(len(CHUNKS)))
@@ -540,11 +540,15 @@
         if c > 0:
             send, keep = run_project_out(c, att, mlp, output_weight)
         received = swapped(send, "head")
+        swaps.append(received)
+        keeps.append(keep)
+    named, _ = lax.optimization_barrier((owners, keep))
+    masks = run_plan(named, shards)
+    for c in every:
+        received = swaps[c]
         if c > 0:
             received, _ = lax.optimization_barrier((received, slots[c - 1][0]))
-        slots.append(run_combine((c,), (2, 3), masks, grid_features, (keep,), (received,)))
-        keeps.append(keep)
-        swaps.append(received)
+        slots.append(run_combine((c,), (2, 3), masks, grid_features, (keeps[c],), (received,)))
     swaps[-1], _ = lax.optimization_barrier((swaps[-1], slots[-1][0]))
     near_slots, own_slots = run_combine(every, (1, 0), masks, grid_features, keeps, swaps)
     for c in every:

time: 45.4 us -> 45.7 us (level)
  transfers between devices with their start and end apart: 15 -> 15, of which waited for: 10 -> 10; matrix products, arithmetic and copies ran while one was open for 0% -> 0% of each run, Pallas kernels for 25% -> 24%
where the time goes in v21:
time: 45.7 us; the launch traced here: 45.6 us
  starting transfers between devices  18 us (39%)
  Pallas kernels  15.4 us (34%)
  waiting for transfers between devices  11.8 us (26%)
    ppermute x9, starting transfers between devices, crossed(): return lax.ppermute(x, 'shard', [(i, i ^ distance) for i in range(size)])  13.8 us
    ppermute x9, waiting for transfers between devices, crossed(): return lax.ppermute(x, 'shard', [(i, i ^ distance) for i in range(size)])  7.66 us
    ppermute x6, starting transfers between devices, swapped(): return lax.ppermute(x, axis, [(0, 1), (1, 0)])  4.21 us
    ppermute x6, waiting for transfers between devices, swapped(): return lax.ppermute(x, axis, [(0, 1), (1, 0)])  4.11 us
    pallas_call x1, Pallas kernels, run_stage(): pl.pallas_call(functools.partial(stage_kernel, axes), out_shape=tuple((ja...  4.1 us
    pallas_call x1, Pallas kernels, run_mlp(): pl.pallas_call(mlp_kernel, out_shape=(jax.ShapeDtypeStruct((rows, wq.shap...  3.33 us
    pallas_call x1, Pallas kernels, run_attend(): pl.pallas_call(attend_kernel, out_shape=(part, part, jax.ShapeDtypeStruct...  2.51 us
    pallas_call x2, Pallas kernels, run_place(): pl.pallas_call(functools.partial(place_kernel, spots), out_shape=jax.Shap...  1.56 us
  transfers between devices with their start and end apart: 15, of which 10 were waited for; matrix products, arithmetic and copies ran while one was open for 0% of the time, Pallas kernels for 24%

profile of v21, /device:TPU:0, one launch (start us, length us, event | category | flops | bytes accessed | tf_op | source)
XLA Modules:
  0.0 45.6 jit_solution(6568767454615212736)
XLA Ops:
  0.0 0.9 %pick.1 = bf16[64,1024]{1,0:T(8,128)(2,1)S(1)} custom-call(bf16[128,1024]{1,0:T(8,128)(2,1)} %mesh.1), custom_call_target="tpu_custom_call" | custom-call | bytes 524288 | tf_op jit(solution)/shard_map/pick/pallas_call | solution.py:113
  0.9 4.1 %collective-permute-start.1 = (bf16[64,1024]{1,0:T(8,128)(2,1)S(1)}, bf16[64,1024]{1,0:T(8,128)(2,1)S(1)}, u32[]{:S(2)}, u32[]{:S(2)}) collective-permute-start(bf16[64,1024]{1,0:T(8,128)(2,1)S(1)} %pick.1), channel_id=1, source_target_pairs={{0,8},{4,12},{8,0},{12,4},{1,9},{5,13},{9,1},{13,5},{2,10},{6,14},... | collective-permute-start | bytes 393224 | tf_op jit(solution)/shard_map/ppermute | solution.py:480
  5.0 1.5 %collective-permute-start = (bf16[256,512]{1,0:T(8,128)(2,1)}, bf16[256,512]{1,0:T(8,128)(2,1)S(1)}, u32[]{:S(2)}, u32[]{:S(2)}) collective-permute-start(bf16[256,512]{1,0:T(8,128)(2,1)} %bitcast.8), channel_id=1, source_target_pairs={{0,2},{2,0},{1,3},{3,1},{4,6},{6,4},{5,7},{7,5},{8,10},{10,8},{9,1... | collective-permute-start | bytes 786440 | tf_op jit(solution)/shard_map/ppermute | solution.py:484
  6.5 1.6 %collective-permute-start.3 = (bf16[128,1024]{1,0:T(8,128)(2,1)}, bf16[128,1024]{1,0:T(8,128)(2,1)S(1)}, u32[]{:S(2)}, u32[]{:S(2)}) collective-permute-start(bf16[128,1024]{1,0:T(8,128)(2,1)} %mesh.1), channel_id=1, source_target_pairs={{0,4},{4,0},{8,12},{12,8},{1,5},{5,1},{9,13},{13,9},{2,6},{6,2},{1... | collective-permute-start | bytes 786440 | tf_op jit(solution)/shard_map/ppermute | solution.py:480
  8.1 4.1 %stage.1 = (bf16[256,512]{1,0:T(8,128)(2,1)S(1)}, f32[1,1024]{1,0:T(1,128)S(1)}, bf16[1024,512]{1,0:T(8,128)(2,1)S(1)}, bf16[1024,2048]{1,0:T(8,128)(2,1)S(1)}, ...) custom-call(bf16[256,512]{1,0:T(8,128)(2,1)} %bitcast.9, ...), custom_call_target="tpu_custom_call" | custom-call | flops 20451328000 | bytes 204513280 | tf_op jit(solution)/shard_map/stage/pallas_call | solution.py:163
  12.2 0.3 collective-permute-start.5
  12.5 0.0 collective-permute-done.1.refs_2_
  12.5 0.5 %collective-permute-start.2 = (bf16[64,1024]{1,0:T(8,128)(2,1)S(1)}, bf16[64,1024]{1,0:T(8,128)(2,1)S(1)}, u32[]{:S(2)}, u32[]{:S(2)}) collective-permute-start(bf16[64,1024]{1,0:T(8,128)(2,1)S(1)} %collective-permute-done.1.refs_2_), channel_id=1, source_target_pairs={{0,2},{2,0},{1,3},{3,1},{4,6},{6,4},{5,7},{7,5},{8,10},{10,8},{9,1... | collective-permute-start | bytes 393224 | tf_op jit(solution)/shard_map/ppermute | solution.py:484
  13.0 0.7 %collective-permute-start.4 = (bf16[64,1024]{1,0:T(8,128)(2,1)S(1)}, bf16[64,1024]{1,0:T(8,128)(2,1)S(1)}, u32[]{:S(2)}, u32[]{:S(2)}) collective-permute-start(bf16[64,1024]{1,0:T(8,128)(2,1)S(1)} %collective-permute-done.1.refs_2_), channel_id=1, source_target_pairs={{0,4},{4,0},{8,12},{12,8},{1,5},{5,1},{9,13},{13,9},{2,6},{6,2},{1... | collective-permute-start | bytes 393224 | tf_op jit(solution)/shard_map/ppermute | solution.py:480
  13.7 0.0 collective-permute-done.other
  13.7 0.0 copy-start
  13.7 0.0 copy-start.1
  13.7 3.3 %mlp.1 = (bf16[256,512]{1,0:T(8,128)(2,1)S(1)}, f32[256,1024]{1,0:T(8,128)S(1)}) custom-call(bf16[256,512]{1,0:T(8,128)(2,1)S(1)} %get-tuple-element.35.own, bf16[256,512]{1,0:T(8,128)(2,1)S(1)} %collective-permute-done.other, f32[1,1024]{1,0:T(1,128)S(1)} %get-tuple-element.37.gain, bf16[1024,512]{1,0:T(8,128)(2,1)S(1)} %get-tuple-element.38.wq, ...), custom_call_target="tpu_custom_call" | custom-call | flops 2415919104 | bytes 9437184 | tf_op jit(solution)/shard_map/mlp/pallas_call | solution.py:86
  17.1 0.4 collective-permute-done.2.refs_3_
  17.5 1.2 %collective-permute-done.3.refs_1_ = bf16[128,1024]{1,0:T(8,128)(2,1)S(1)} collective-permute-done((bf16[128,1024]{1,0:T(8,128)(2,1)}, bf16[128,1024]{1,0:T(8,128)(2,1)S(1)}, u32[]{:S(2)}, u32[]{:S(2)}) %collective-permute-start.3) | collective-permute-done | bytes 262176 | tf_op jit(solution)/shard_map/ppermute | solution.py:480
  18.7 0.0 copy-done
  18.7 0.0 copy-done.1
  18.7 1.0 %project.3 = bf16[384,1024]{1,0:T(8,128)(2,1)S(1)} custom-call(bf16[128,1024]{1,0:T(8,128)(2,1)S(1)} %get-tuple-element.47.refs_0_, bf16[128,1024]{1,0:T(8,128)(2,1)S(1)} %collective-permute-done.3.refs_1_, bf16[64,1024]{1,0:T(8,128)(2,1)S(1)} %collective-permute-done.1.refs_2_, bf16[64,1024]{1,0:T(8,128)(2,1)S(1)} %collective-permute-done.2.refs_3_, ...), custom_call_target="tpu_custom_call" | custom-call | flops 60397977600 | bytes 275251200 | tf_op jit(solution)/shard_map/project/pallas_call | solution.py:191
  19.7 0.0 copy-start.2
  19.7 0.0 copy-start.4
  19.7 0.1 collective-permute-start.7
  19.8 0.2 collective-permute-done.5.refs_1_
  20.0 1.5 %collective-permute-done.4.refs_0_ = bf16[64,1024]{1,0:T(8,128)(2,1)S(1)} collective-permute-done((bf16[64,1024]{1,0:T(8,128)(2,1)S(1)}, bf16[64,1024]{1,0:T(8,128)(2,1)S(1)}, u32[]{:S(2)}, u32[]{:S(2)}) %collective-permute-start.4) | collective-permute-done | bytes 131104 | tf_op jit(solution)/shard_map/ppermute | solution.py:480
  21.5 0.4 project.2
  21.9 0.1 collective-permute-start.6
  22.0 0.1 collective-permute-done.7
  22.1 0.1 table.1.table_in
  22.2 1.4 %collective-permute-done.6 = bf16[128,1024]{1,0:T(8,128)(2,1)S(1)} collective-permute-done((bf16[128,1024]{1,0:T(8,128)(2,1)S(1)}, bf16[128,1024]{1,0:T(8,128)(2,1)S(1)}, u32[]{:S(2)}, u32[]{:S(2)}) %collective-permute-start.6) | collective-permute-done | bytes 262176 | tf_op jit(solution)/shard_map/ppermute | solution.py:484
  23.5 0.0 copy-done.2
  23.5 0.0 copy-done.4
  23.5 2.5 %attend.1 = (bf16[4,80,128]{2,1,0:T(8,128)(2,1)S(1)}, bf16[4,80,128]{2,1,0:T(8,128)(2,1)S(1)}, bf16[256,512]{1,0:T(8,128)(2,1)S(1)}, bf16[2,8,64,1024]{3,2,1,0:T(8,128)(2,1)S(1)}) custom-call(s32[4,8]{1,0:T(4,128)S(1)} %copy-done.4, bf16[256,512]{1,0:T(8,128)(2,1)S(1)} %get-tuple-element.46.q, ...), custom_call_target="tpu_custom_call", output_to_operand_aliasing={{3}: (4, {})} | custom-call | flops 13421772800 | bytes 41943040 | tf_op jit(solution)/shard_map/attend/pallas_call | solution.py:325
  26.1 0.6 %collective-permute-start.9 = (bf16[4,80,128]{2,1,0:T(8,128)(2,1)S(1)}, bf16[4,80,128]{2,1,0:T(8,128)(2,1)S(1)}, u32[]{:S(2)}, u32[]{:S(2)}) collective-permute-start(bf16[4,80,128]{2,1,0:T(8,128)(2,1)S(1)} %get-tuple-element.56), channel_id=1, source_target_pairs={{0,2},{2,0},{1,3},{3,1},{4,6},{6,4},{5,7},{7,5},{8,10},{10,8},{9,1... | collective-permute-start | bytes 245768 | tf_op jit(solution)/shard_map/ppermute | solution.py:484
  26.7 0.0 copy-start.5
  26.7 0.0 copy-start.3
  26.7 0.4 project_out.1
  27.1 0.2 copy-done.5
  27.3 0.1 copy.14.owners
  27.4 1.4 %collective-permute-start.8 = (bf16[4,176,128]{2,1,0:T(8,128)(2,1)S(1)}, bf16[4,176,128]{2,1,0:T(8,128)(2,1)S(1)}, u32[]{:S(2)}, u32[]{:S(2)}) collective-permute-start(bf16[4,176,128]{2,1,0:T(8,128)(2,1)S(1)} %get-tuple-element.54), channel_id=1, source_target_pairs={{0,2},{2,0},{1,3},{3,1},{4,6},{6,4},{5,7},{7,5},{8,10},{10,8},{9,1... | collective-permute-start | bytes 540680 | tf_op jit(solution)/shard_map/ppermute | solution.py:484
  28.9 0.6 %plan.1.masks = f32[4,2,4,8,128]{4,3,2,1,0:T(8,128)S(1)} custom-call(s32[4,1]{1,0:T(4,128)S(1)} %copy.14.owners), custom_call_target="tpu_custom_call" | custom-call | flops 100000000 | bytes 262144 | tf_op jit(solution)/shard_map/plan/pallas_call | solution.py:385
  29.5 1.8 %collective-permute-done.9.refs_1_.refs_2_ = bf16[4,80,128]{2,1,0:T(8,128)(2,1)S(1)} collective-permute-done((bf16[4,80,128]{2,1,0:T(8,128)(2,1)S(1)}, bf16[4,80,128]{2,1,0:T(8,128)(2,1)S(1)}, u32[]{:S(2)}, u32[]{:S(2)}) %collective-permute-start.9) | collective-permute-done | bytes 81952 | tf_op jit(solution)/shard_map/ppermute | solution.py:484
  31.3 0.0 copy-done.3
  31.3 0.1 combine.3
  31.4 0.1 collective-permute-start.13
  31.5 2.4 %collective-permute-start.14 = (bf16[2,80,128]{2,1,0:T(8,128)(2,1)S(1)}, bf16[2,80,128]{2,1,0:T(8,128)(2,1)S(1)}, u32[]{:S(2)}, u32[]{:S(2)}) collective-permute-start(bf16[2,80,128]{2,1,0:T(8,128)(2,1)S(1)} %get-tuple-element.63), channel_id=1, source_target_pairs={{0,12},{4,8},{8,4},{12,0},{1,13},{5,9},{9,5},{13,1},{2,14},{6,10},... | collective-permute-start | bytes 122888 | tf_op jit(solution)/shard_map/ppermute | solution.py:480
  34.0 0.5 %collective-permute-done.8.refs_1_.refs_3_ = bf16[4,176,128]{2,1,0:T(8,128)(2,1)S(1)} collective-permute-done((bf16[4,176,128]{2,1,0:T(8,128)(2,1)S(1)}, bf16[4,176,128]{2,1,0:T(8,128)(2,1)S(1)}, u32[]{:S(2)}, u32[]{:S(2)}) %collective-permute-start.8) | collective-permute-done | bytes 180256 | tf_op jit(solution)/shard_map/ppermute | solution.py:484
  34.5 0.1 combine.4
  34.6 1.5 %collective-permute-start.10 = (bf16[2,176,128]{2,1,0:T(8,128)(2,1)S(1)}, bf16[2,176,128]{2,1,0:T(8,128)(2,1)S(1)}, u32[]{:S(2)}, u32[]{:S(2)}) collective-permute-start(bf16[2,176,128]{2,1,0:T(8,128)(2,1)S(1)} %get-tuple-element.59), channel_id=1, source_target_pairs={{0,8},{4,12},{8,0},{12,4},{1,9},{5,13},{9,1},{13,5},{2,10},{6,14},... | collective-permute-start | bytes 270344 | tf_op jit(solution)/shard_map/ppermute | solution.py:480
  36.1 0.2 combine.5
  36.3 1.6 %collective-permute-start.12 = (bf16[2,256,128]{2,1,0:T(8,128)(2,1)S(1)}, bf16[2,256,128]{2,1,0:T(8,128)(2,1)S(1)}, u32[]{:S(2)}, u32[]{:S(2)}) collective-permute-start(bf16[2,256,128]{2,1,0:T(8,128)(2,1)S(1)} %get-tuple-element.62), channel_id=1, source_target_pairs={{0,4},{4,0},{8,12},{12,8},{1,5},{5,1},{9,13},{13,9},{2,6},{6,2},{1... | collective-permute-start | bytes 393224 | tf_op jit(solution)/shard_map/ppermute | solution.py:480
  37.9 1.4 %collective-permute-start.11 = (bf16[2,176,128]{2,1,0:T(8,128)(2,1)S(1)}, bf16[2,176,128]{2,1,0:T(8,128)(2,1)S(1)}, u32[]{:S(2)}, u32[]{:S(2)}) collective-permute-start(bf16[2,176,128]{2,1,0:T(8,128)(2,1)S(1)} %get-tuple-element.60), channel_id=1, source_target_pairs={{0,12},{4,8},{8,4},{12,0},{1,13},{5,9},{9,5},{13,1},{2,14},{6,10},... | collective-permute-start | bytes 270344 | tf_op jit(solution)/shard_map/ppermute | solution.py:480
  39.3 0.0 collective-permute-done.13.refs_0_
  39.3 0.0 collective-permute-done.14.refs_1_
  39.3 0.8 %place.2.refs_3_ = bf16[8,64,512]{2,1,0:T(8,128)(2,1)} custom-call(bf16[2,80,128]{2,1,0:T(8,128)(2,1)S(1)} %collective-permute-done.13.refs_0_, bf16[2,80,128]{2,1,0:T(8,128)(2,1)S(1)} %collective-permute-done.14.refs_1_, bf16[2,256,128]{2,1,0:T(8,128)(2,1)S(1)} %get-tuple-element.64.refs_2_), custom_call_target="tpu_custom_call" | custom-call | flops 42598400000 | tf_op jit(solution)/shard_map/place/pallas_call | solution.py:464
  40.1 2.5 %collective-permute-done.10.refs_0_ = bf16[2,176,128]{2,1,0:T(8,128)(2,1)S(1)} collective-permute-done((bf16[2,176,128]{2,1,0:T(8,128)(2,1)S(1)}, bf16[2,176,128]{2,1,0:T(8,128)(2,1)S(1)}, u32[]{:S(2)}, u32[]{:S(2)}) %collective-permute-start.10) | collective-permute-done | bytes 90144 | tf_op jit(solution)/shard_map/ppermute | solution.py:480
  42.5 2.3 %collective-permute-done.11.refs_1_ = bf16[2,176,128]{2,1,0:T(8,128)(2,1)S(1)} collective-permute-done((bf16[2,176,128]{2,1,0:T(8,128)(2,1)S(1)}, bf16[2,176,128]{2,1,0:T(8,128)(2,1)S(1)}, u32[]{:S(2)}, u32[]{:S(2)}) %collective-permute-start.11) | collective-permute-done | bytes 90144 | tf_op jit(solution)/shard_map/ppermute | solution.py:480
  44.8 0.0 collective-permute-done.12.refs_2_
  44.8 0.8 %place.3 = bf16[8,64,512]{2,1,0:T(8,128)(2,1)} custom-call(bf16[2,176,128]{2,1,0:T(8,128)(2,1)S(1)} %collective-permute-done.10.refs_0_, bf16[2,176,128]{2,1,0:T(8,128)(2,1)S(1)} %collective-permute-done.11.refs_1_, bf16[2,256,128]{2,1,0:T(8,128)(2,1)S(1)} %collective-permute-done.12.refs_2_, ...), custom_call_target="tpu_custom_call", output_to_operand_aliasing={{}: (3, {})} | custom-call | flops 62259200000 | tf_op jit(solution)/shard_map/place/pallas_call | solution.py:464
Async XLA Ops:
  0.9 11.6 %collective-permute-start.1 = (bf16[64,1024]{1,0:T(8,128)(2,1)S(1)}, bf16[64,1024]{1,0:T(8,128)(2,1)S(1)}, u32[]{:S(2)}, u32[]{:S(2)}) collective-permute-start(bf16[64,1024]{1,0:T(8,128)(2,1)S(1)} %pick.1), channel_id=1, source_target_pairs={{0,8},{4,12},{8,0},{12,4},{1,9},{5,13},{9,1},{13,5},{2,10},{6,14},... | collective-permute-start | bytes 393224 | tf_op jit(solution)/shard_map/ppermute | solution.py:480
  5.0 8.7 %collective-permute-start = (bf16[256,512]{1,0:T(8,128)(2,1)}, bf16[256,512]{1,0:T(8,128)(2,1)S(1)}, u32[]{:S(2)}, u32[]{:S(2)}) collective-permute-start(bf16[256,512]{1,0:T(8,128)(2,1)} %bitcast.8), channel_id=1, source_target_pairs={{0,2},{2,0},{1,3},{3,1},{4,6},{6,4},{5,7},{7,5},{8,10},{10,8},{9,1... | collective-permute-start | bytes 786440 | tf_op jit(solution)/shard_map/ppermute | solution.py:484
  6.5 12.2 %collective-permute-start.3 = (bf16[128,1024]{1,0:T(8,128)(2,1)}, bf16[128,1024]{1,0:T(8,128)(2,1)S(1)}, u32[]{:S(2)}, u32[]{:S(2)}) collective-permute-start(bf16[128,1024]{1,0:T(8,128)(2,1)} %mesh.1), channel_id=1, source_target_pairs={{0,4},{4,0},{8,12},{12,8},{1,5},{5,1},{9,13},{13,9},{2,6},{6,2},{1... | collective-permute-start | bytes 786440 | tf_op jit(solution)/shard_map/ppermute | solution.py:480
  12.2 7.8 %collective-permute-start.5 = (bf16[64,1024]{1,0:T(8,128)(2,1)S(1)}, bf16[64,1024]{1,0:T(8,128)(2,1)S(1)}, u32[]{:S(2)}, u32[]{:S(2)}) collective-permute-start(bf16[64,1024]{1,0:T(8,128)(2,1)S(1)} %get-tuple-element.43), channel_id=1, source_target_pairs={{0,12},{4,8},{8,4},{12,0},{1,13},{5,9},{9,5},{13,1},{2,14},{6,10},... | collective-permute-start | bytes 393224 | tf_op jit(solution)/shard_map/ppermute | solution.py:480
  12.5 5.0 %collective-permute-start.2 = (bf16[64,1024]{1,0:T(8,128)(2,1)S(1)}, bf16[64,1024]{1,0:T(8,128)(2,1)S(1)}, u32[]{:S(2)}, u32[]{:S(2)}) collective-permute-start(bf16[64,1024]{1,0:T(8,128)(2,1)S(1)} %collective-permute-done.1.refs_2_), channel_id=1, source_target_pairs={{0,2},{2,0},{1,3},{3,1},{4,6},{6,4},{5,7},{7,5},{8,10},{10,8},{9,1... | collective-permute-start | bytes 393224 | tf_op jit(solution)/shard_map/ppermute | solution.py:484
  13.0 8.5 %collective-permute-start.4 = (bf16[64,1024]{1,0:T(8,128)(2,1)S(1)}, bf16[64,1024]{1,0:T(8,128)(2,1)S(1)}, u32[]{:S(2)}, u32[]{:S(2)}) collective-permute-start(bf16[64,1024]{1,0:T(8,128)(2,1)S(1)} %collective-permute-done.1.refs_2_), channel_id=1, source_target_pairs={{0,4},{4,0},{8,12},{12,8},{1,5},{5,1},{9,13},{13,9},{2,6},{6,2},{1... | collective-permute-start | bytes 393224 | tf_op jit(solution)/shard_map/ppermute | solution.py:480
  13.7 5.0 %copy-start = (bf16[1024,512]{1,0:T(8,128)(2,1)S(1)}, bf16[1024,512]{1,0:T(8,128)(2,1)}, u32[]{:S(2)}) copy-start(bf16[1024,512]{1,0:T(8,128)(2,1)} %refs_4_.3) | copy-start | bytes 3145732
  13.7 5.0 %copy-start.1 = (bf16[1024,512]{1,0:T(8,128)(2,1)S(1)}, bf16[1024,512]{1,0:T(8,128)(2,1)}, u32[]{:S(2)}) copy-start(bf16[1024,512]{1,0:T(8,128)(2,1)} %refs_5_.3) | copy-start | bytes 3145732
  19.7 3.8 %copy-start.2 = (bf16[512,1024]{1,0:T(8,128)(2,1)S(1)}, bf16[512,1024]{1,0:T(8,128)(2,1)}, u32[]{:S(2)}) copy-start(bf16[512,1024]{1,0:T(8,128)(2,1)} %wo.3) | copy-start | bytes 3145732
  19.7 3.8 %copy-start.4 = (s32[4,8]{1,0:T(4,128)S(1)}, s32[4,8]{1,0:T(4,128)}, u32[]{:S(2)}) copy-start(s32[4,8]{1,0:T(4,128)} %adjacency.1) | copy-start | bytes 388
  19.7 2.4 %collective-permute-start.7 = (bf16[384,1024]{1,0:T(8,128)(2,1)S(1)}, bf16[384,1024]{1,0:T(8,128)(2,1)S(1)}, u32[]{:S(2)}, u32[]{:S(2)}) collective-permute-start(bf16[384,1024]{1,0:T(8,128)(2,1)S(1)} %project.3), channel_id=1, source_target_pairs={{0,1},{1,0},{2,3},{3,2},{4,5},{5,4},{6,7},{7,6},{8,9},{9,8},{10,11... | collective-permute-start | bytes 2359304 | tf_op jit(solution)/shard_map/ppermute | solution.py:484
  21.9 1.6 %collective-permute-start.6 = (bf16[128,1024]{1,0:T(8,128)(2,1)S(1)}, bf16[128,1024]{1,0:T(8,128)(2,1)S(1)}, u32[]{:S(2)}, u32[]{:S(2)}) collective-permute-start(bf16[128,1024]{1,0:T(8,128)(2,1)S(1)} %project.2), channel_id=1, source_target_pairs={{0,1},{1,0},{2,3},{3,2},{4,5},{5,4},{6,7},{7,6},{8,9},{9,8},{10,11... | collective-permute-start | bytes 786440 | tf_op jit(solution)/shard_map/ppermute | solution.py:484
  26.1 5.3 %collective-permute-start.9 = (bf16[4,80,128]{2,1,0:T(8,128)(2,1)S(1)}, bf16[4,80,128]{2,1,0:T(8,128)(2,1)S(1)}, u32[]{:S(2)}, u32[]{:S(2)}) collective-permute-start(bf16[4,80,128]{2,1,0:T(8,128)(2,1)S(1)} %get-tuple-element.56), channel_id=1, source_target_pairs={{0,2},{2,0},{1,3},{3,1},{4,6},{6,4},{5,7},{7,5},{8,10},{10,8},{9,1... | collective-permute-start | bytes 245768 | tf_op jit(solution)/shard_map/ppermute | solution.py:484
  26.7 0.7 %copy-start.5 = (s32[4,1]{0,1:T(1,128)S(1)}, s32[4,1]{0,1:T(1,128)}, u32[]{:S(2)}) copy-start(s32[4,1]{0,1:T(1,128)} %param.12) | copy-start | bytes 52
  26.7 4.6 %copy-start.3 = (bf16[4,64,512]{2,1,0:T(8,128)(2,1)S(1)}, bf16[4,64,512]{2,1,0:T(8,128)(2,1)}, u32[]{:S(2)}) copy-start(bf16[4,64,512]{2,1,0:T(8,128)(2,1)} %grid_features.5) | copy-start | bytes 786436
  27.4 7.0 %collective-permute-start.8 = (bf16[4,176,128]{2,1,0:T(8,128)(2,1)S(1)}, bf16[4,176,128]{2,1,0:T(8,128)(2,1)S(1)}, u32[]{:S(2)}, u32[]{:S(2)}) collective-permute-start(bf16[4,176,128]{2,1,0:T(8,128)(2,1)S(1)} %get-tuple-element.54), channel_id=1, source_target_pairs={{0,2},{2,0},{1,3},{3,1},{4,6},{6,4},{5,7},{7,5},{8,10},{10,8},{9,1... | collective-permute-start | bytes 540680 | tf_op jit(solution)/shard_map/ppermute | solution.py:484
  31.4 7.9 %collective-permute-start.13 = (bf16[2,80,128]{2,1,0:T(8,128)(2,1)S(1)}, bf16[2,80,128]{2,1,0:T(8,128)(2,1)S(1)}, u32[]{:S(2)}, u32[]{:S(2)}) collective-permute-start(bf16[2,80,128]{2,1,0:T(8,128)(2,1)S(1)} %get-tuple-element.57), channel_id=1, source_target_pairs={{0,8},{4,12},{8,0},{12,4},{1,9},{5,13},{9,1},{13,5},{2,10},{6,14},... | collective-permute-start | bytes 122888 | tf_op jit(solution)/shard_map/ppermute | solution.py:480
  31.5 7.8 %collective-permute-start.14 = (bf16[2,80,128]{2,1,0:T(8,128)(2,1)S(1)}, bf16[2,80,128]{2,1,0:T(8,128)(2,1)S(1)}, u32[]{:S(2)}, u32[]{:S(2)}) collective-permute-start(bf16[2,80,128]{2,1,0:T(8,128)(2,1)S(1)} %get-tuple-element.63), channel_id=1, source_target_pairs={{0,12},{4,8},{8,4},{12,0},{1,13},{5,9},{9,5},{13,1},{2,14},{6,10},... | collective-permute-start | bytes 122888 | tf_op jit(solution)/shard_map/ppermute | solution.py:480
  34.6 7.9 %collective-permute-start.10 = (bf16[2,176,128]{2,1,0:T(8,128)(2,1)S(1)}, bf16[2,176,128]{2,1,0:T(8,128)(2,1)S(1)}, u32[]{:S(2)}, u32[]{:S(2)}) collective-permute-start(bf16[2,176,128]{2,1,0:T(8,128)(2,1)S(1)} %get-tuple-element.59), channel_id=1, source_target_pairs={{0,8},{4,12},{8,0},{12,4},{1,9},{5,13},{9,1},{13,5},{2,10},{6,14},... | collective-permute-start | bytes 270344 | tf_op jit(solution)/shard_map/ppermute | solution.py:480
  36.3 8.5 %collective-permute-start.12 = (bf16[2,256,128]{2,1,0:T(8,128)(2,1)S(1)}, bf16[2,256,128]{2,1,0:T(8,128)(2,1)S(1)}, u32[]{:S(2)}, u32[]{:S(2)}) collective-permute-start(bf16[2,256,128]{2,1,0:T(8,128)(2,1)S(1)} %get-tuple-element.62), channel_id=1, source_target_pairs={{0,4},{4,0},{8,12},{12,8},{1,5},{5,1},{9,13},{13,9},{2,6},{6,2},{1... | collective-permute-start | bytes 393224 | tf_op jit(solution)/shard_map/ppermute | solution.py:480
  37.9 6.9 %collective-permute-start.11 = (bf16[2,176,128]{2,1,0:T(8,128)(2,1)S(1)}, bf16[2,176,128]{2,1,0:T(8,128)(2,1)S(1)}, u32[]{:S(2)}, u32[]{:S(2)}) collective-permute-start(bf16[2,176,128]{2,1,0:T(8,128)(2,1)S(1)} %get-tuple-element.60), channel_id=1, source_target_pairs={{0,12},{4,8},{8,4},{12,0},{1,13},{5,9},{9,5},{13,1},{2,14},{6,10},... | collective-permute-start | bytes 270344 | tf_op jit(solution)/shard_map/ppermute | solution.py:480

commit v22 on v21

--- a/solution.py
+++ b/solution.py
@@ -15,7 +15,7 @@
 QUAD = 4
 WIDE = QUAD * HEAD_DIM
 TILE = 128
-CHUNKS = ((0, 80), (80, 256))
+CHUNKS = ((0, 96), (96, 256))
 MIB = 1 << 20
 
 
@@ -305,9 +305,9 @@
         columns = slice(half + g * WIDE, half + (g + 1) * WIDE)
         values = jnp.concatenate([table[i, p, :, columns] for i, p in places[b]], axis=0)
         highest = jnp.max(scores, axis=-1, keepdims=True)
-        weights = jnp.exp2((scores - highest) * scale)
-        total = jnp.sum(weights, axis=-1, keepdims=True)
-        mixed = dot(weights.astype(jnp.bfloat16), values) * (1.0 / total)
+        weights = jnp.exp2(((scores - highest) * scale).astype(jnp.bfloat16))
+        total = jnp.sum(weights.astype(jnp.float32), axis=-1, keepdims=True)
+        mixed = dot(weights, values) * (1.0 / total)
         merged = mixed[0:BLOCK, :]
         for i in range(1, QUAD):
             merged = jnp.where(lane_head == i, mixed[i * BLOCK : (i + 1) * BLOCK, :], merged)

time: 45.7 us -> 45.7 us (level)
  no operation moved by 1% of the time
where the time goes in v22:
time: 45.7 us; the launch traced here: 45.5 us
  starting transfers between devices  18 us (39%)
  Pallas kernels  15.4 us (34%)
  waiting for transfers between devices  11.6 us (25%)
    ppermute x9, starting transfers between devices, crossed(): return lax.ppermute(x, 'shard', [(i, i ^ distance) for i in range(size)])  13.8 us
    ppermute x9, waiting for transfers between devices, crossed(): return lax.ppermute(x, 'shard', [(i, i ^ distance) for i in range(size)])  7.52 us
    ppermute x6, starting transfers between devices, swapped(): return lax.ppermute(x, axis, [(0, 1), (1, 0)])  4.21 us
    pallas_call x1, Pallas kernels, run_stage(): pl.pallas_call(functools.partial(stage_kernel, axes), out_shape=tuple((ja...  4.1 us
    ppermute x6, waiting for transfers between devices, swapped(): return lax.ppermute(x, axis, [(0, 1), (1, 0)])  4.08 us
    pallas_call x1, Pallas kernels, run_mlp(): pl.pallas_call(mlp_kernel, out_shape=(jax.ShapeDtypeStruct((rows, wq.shap...  3.33 us
    pallas_call x1, Pallas kernels, run_attend(): pl.pallas_call(attend_kernel, out_shape=(part, part, jax.ShapeDtypeStruct...  2.58 us
    pallas_call x2, Pallas kernels, run_place(): pl.pallas_call(functools.partial(place_kernel, spots), out_shape=jax.Shap...  1.55 us
  transfers between devices with their start and end apart: 15, of which 10 were waited for; matrix products, arithmetic and copies ran while one was open for 0% of the time, Pallas kernels for 24%

profile of v22, /device:TPU:0, one launch (start us, length us, event | category | flops | bytes accessed | tf_op | source)
XLA Modules:
  0.0 45.5 jit_solution(16014489689507436441)
XLA Ops:
  0.0 0.9 %pick.1 = bf16[64,1024]{1,0:T(8,128)(2,1)S(1)} custom-call(bf16[128,1024]{1,0:T(8,128)(2,1)} %mesh.1), custom_call_target="tpu_custom_call" | custom-call | bytes 524288 | tf_op jit(solution)/shard_map/pick/pallas_call | solution.py:113
  0.9 4.1 %collective-permute-start.1 = (bf16[64,1024]{1,0:T(8,128)(2,1)S(1)}, bf16[64,1024]{1,0:T(8,128)(2,1)S(1)}, u32[]{:S(2)}, u32[]{:S(2)}) collective-permute-start(bf16[64,1024]{1,0:T(8,128)(2,1)S(1)} %pick.1), channel_id=1, source_target_pairs={{0,8},{4,12},{8,0},{12,4},{1,9},{5,13},{9,1},{13,5},{2,10},{6,14},... | collective-permute-start | bytes 393224 | tf_op jit(solution)/shard_map/ppermute | solution.py:480
  5.0 1.5 %collective-permute-start = (bf16[256,512]{1,0:T(8,128)(2,1)}, bf16[256,512]{1,0:T(8,128)(2,1)S(1)}, u32[]{:S(2)}, u32[]{:S(2)}) collective-permute-start(bf16[256,512]{1,0:T(8,128)(2,1)} %bitcast.8), channel_id=1, source_target_pairs={{0,2},{2,0},{1,3},{3,1},{4,6},{6,4},{5,7},{7,5},{8,10},{10,8},{9,1... | collective-permute-start | bytes 786440 | tf_op jit(solution)/shard_map/ppermute | solution.py:484
  6.5 1.6 %collective-permute-start.3 = (bf16[128,1024]{1,0:T(8,128)(2,1)}, bf16[128,1024]{1,0:T(8,128)(2,1)S(1)}, u32[]{:S(2)}, u32[]{:S(2)}) collective-permute-start(bf16[128,1024]{1,0:T(8,128)(2,1)} %mesh.1), channel_id=1, source_target_pairs={{0,4},{4,0},{8,12},{12,8},{1,5},{5,1},{9,13},{13,9},{2,6},{6,2},{1... | collective-permute-start | bytes 786440 | tf_op jit(solution)/shard_map/ppermute | solution.py:480
  8.1 4.1 %stage.1 = (bf16[256,512]{1,0:T(8,128)(2,1)S(1)}, f32[1,1024]{1,0:T(1,128)S(1)}, bf16[1024,512]{1,0:T(8,128)(2,1)S(1)}, bf16[1024,2048]{1,0:T(8,128)(2,1)S(1)}, ...) custom-call(bf16[256,512]{1,0:T(8,128)(2,1)} %bitcast.9, ...), custom_call_target="tpu_custom_call" | custom-call | flops 20451328000 | bytes 204513280 | tf_op jit(solution)/shard_map/stage/pallas_call | solution.py:163
  12.2 0.3 collective-permute-start.5
  12.5 0.0 collective-permute-done.1.refs_2_
  12.5 0.5 %collective-permute-start.2 = (bf16[64,1024]{1,0:T(8,128)(2,1)S(1)}, bf16[64,1024]{1,0:T(8,128)(2,1)S(1)}, u32[]{:S(2)}, u32[]{:S(2)}) collective-permute-start(bf16[64,1024]{1,0:T(8,128)(2,1)S(1)} %collective-permute-done.1.refs_2_), channel_id=1, source_target_pairs={{0,2},{2,0},{1,3},{3,1},{4,6},{6,4},{5,7},{7,5},{8,10},{10,8},{9,1... | collective-permute-start | bytes 393224 | tf_op jit(solution)/shard_map/ppermute | solution.py:484
  13.0 0.7 %collective-permute-start.4 = (bf16[64,1024]{1,0:T(8,128)(2,1)S(1)}, bf16[64,1024]{1,0:T(8,128)(2,1)S(1)}, u32[]{:S(2)}, u32[]{:S(2)}) collective-permute-start(bf16[64,1024]{1,0:T(8,128)(2,1)S(1)} %collective-permute-done.1.refs_2_), channel_id=1, source_target_pairs={{0,4},{4,0},{8,12},{12,8},{1,5},{5,1},{9,13},{13,9},{2,6},{6,2},{1... | collective-permute-start | bytes 393224 | tf_op jit(solution)/shard_map/ppermute | solution.py:480
  13.7 0.0 collective-permute-done.other
  13.7 0.0 copy-start
  13.7 0.0 copy-start.1
  13.7 3.3 %mlp.1 = (bf16[256,512]{1,0:T(8,128)(2,1)S(1)}, f32[256,1024]{1,0:T(8,128)S(1)}) custom-call(bf16[256,512]{1,0:T(8,128)(2,1)S(1)} %get-tuple-element.35.own, bf16[256,512]{1,0:T(8,128)(2,1)S(1)} %collective-permute-done.other, f32[1,1024]{1,0:T(1,128)S(1)} %get-tuple-element.37.gain, bf16[1024,512]{1,0:T(8,128)(2,1)S(1)} %get-tuple-element.38.wq, ...), custom_call_target="tpu_custom_call" | custom-call | flops 2415919104 | bytes 9437184 | tf_op jit(solution)/shard_map/mlp/pallas_call | solution.py:86
  17.1 0.4 collective-permute-done.2.refs_3_
  17.5 1.2 %collective-permute-done.3.refs_1_ = bf16[128,1024]{1,0:T(8,128)(2,1)S(1)} collective-permute-done((bf16[128,1024]{1,0:T(8,128)(2,1)}, bf16[128,1024]{1,0:T(8,128)(2,1)S(1)}, u32[]{:S(2)}, u32[]{:S(2)}) %collective-permute-start.3) | collective-permute-done | bytes 262176 | tf_op jit(solution)/shard_map/ppermute | solution.py:480
  18.7 0.0 copy-done
  18.7 0.0 copy-done.1
  18.7 1.0 %project.3 = bf16[384,1024]{1,0:T(8,128)(2,1)S(1)} custom-call(bf16[128,1024]{1,0:T(8,128)(2,1)S(1)} %get-tuple-element.47.refs_0_, bf16[128,1024]{1,0:T(8,128)(2,1)S(1)} %collective-permute-done.3.refs_1_, bf16[64,1024]{1,0:T(8,128)(2,1)S(1)} %collective-permute-done.1.refs_2_, bf16[64,1024]{1,0:T(8,128)(2,1)S(1)} %collective-permute-done.2.refs_3_, ...), custom_call_target="tpu_custom_call" | custom-call | flops 60397977600 | bytes 275251200 | tf_op jit(solution)/shard_map/project/pallas_call | solution.py:191
  19.7 0.0 copy-start.2
  19.7 0.0 copy-start.4
  19.7 0.1 collective-permute-start.7
  19.8 0.2 collective-permute-done.5.refs_1_
  20.0 1.5 %collective-permute-done.4.refs_0_ = bf16[64,1024]{1,0:T(8,128)(2,1)S(1)} collective-permute-done((bf16[64,1024]{1,0:T(8,128)(2,1)S(1)}, bf16[64,1024]{1,0:T(8,128)(2,1)S(1)}, u32[]{:S(2)}, u32[]{:S(2)}) %collective-permute-start.4) | collective-permute-done | bytes 131104 | tf_op jit(solution)/shard_map/ppermute | solution.py:480
  21.5 0.4 project.2
  21.9 0.1 collective-permute-start.6
  22.0 0.1 collective-permute-done.7
  22.1 0.1 table.1.table_in
  22.2 1.4 %collective-permute-done.6 = bf16[128,1024]{1,0:T(8,128)(2,1)S(1)} collective-permute-done((bf16[128,1024]{1,0:T(8,128)(2,1)S(1)}, bf16[128,1024]{1,0:T(8,128)(2,1)S(1)}, u32[]{:S(2)}, u32[]{:S(2)}) %collective-permute-start.6) | collective-permute-done | bytes 262176 | tf_op jit(solution)/shard_map/ppermute | solution.py:484
  23.5 0.0 copy-done.2
  23.5 0.0 copy-done.4
  23.5 2.6 %attend.1 = (bf16[4,96,128]{2,1,0:T(8,128)(2,1)S(1)}, bf16[4,96,128]{2,1,0:T(8,128)(2,1)S(1)}, bf16[256,512]{1,0:T(8,128)(2,1)S(1)}, bf16[2,8,64,1024]{3,2,1,0:T(8,128)(2,1)S(1)}) custom-call(s32[4,8]{1,0:T(4,128)S(1)} %copy-done.4, bf16[256,512]{1,0:T(8,128)(2,1)S(1)} %get-tuple-element.46.q, ...), custom_call_target="tpu_custom_call", output_to_operand_aliasing={{3}: (4, {})} | custom-call | flops 13421772800 | bytes 41943040 | tf_op jit(solution)/shard_map/attend/pallas_call | solution.py:325
  26.1 0.7 %collective-permute-start.9 = (bf16[4,96,128]{2,1,0:T(8,128)(2,1)S(1)}, bf16[4,96,128]{2,1,0:T(8,128)(2,1)S(1)}, u32[]{:S(2)}, u32[]{:S(2)}) collective-permute-start(bf16[4,96,128]{2,1,0:T(8,128)(2,1)S(1)} %get-tuple-element.56), channel_id=1, source_target_pairs={{0,2},{2,0},{1,3},{3,1},{4,6},{6,4},{5,7},{7,5},{8,10},{10,8},{9,1... | collective-permute-start | bytes 294920 | tf_op jit(solution)/shard_map/ppermute | solution.py:484
  26.8 0.0 copy-start.5
  26.8 0.0 copy-start.3
  26.8 0.4 project_out.1
  27.2 0.2 copy-done.5
  27.4 0.1 copy.14.owners
  27.5 1.4 %collective-permute-start.8 = (bf16[4,160,128]{2,1,0:T(8,128)(2,1)S(1)}, bf16[4,160,128]{2,1,0:T(8,128)(2,1)S(1)}, u32[]{:S(2)}, u32[]{:S(2)}) collective-permute-start(bf16[4,160,128]{2,1,0:T(8,128)(2,1)S(1)} %get-tuple-element.54), channel_id=1, source_target_pairs={{0,2},{2,0},{1,3},{3,1},{4,6},{6,4},{5,7},{7,5},{8,10},{10,8},{9,1... | collective-permute-start | bytes 491528 | tf_op jit(solution)/shard_map/ppermute | solution.py:484
  29.0 0.6 %plan.1.masks = f32[4,2,4,8,128]{4,3,2,1,0:T(8,128)S(1)} custom-call(s32[4,1]{1,0:T(4,128)S(1)} %copy.14.owners), custom_call_target="tpu_custom_call" | custom-call | flops 100000000 | bytes 262144 | tf_op jit(solution)/shard_map/plan/pallas_call | solution.py:385
  29.6 2.2 %collective-permute-done.9.refs_1_.refs_2_ = bf16[4,96,128]{2,1,0:T(8,128)(2,1)S(1)} collective-permute-done((bf16[4,96,128]{2,1,0:T(8,128)(2,1)S(1)}, bf16[4,96,128]{2,1,0:T(8,128)(2,1)S(1)}, u32[]{:S(2)}, u32[]{:S(2)}) %collective-permute-start.9) | collective-permute-done | bytes 98336 | tf_op jit(solution)/shard_map/ppermute | solution.py:484
  31.8 0.0 copy-done.3
  31.8 0.1 combine.3
  31.9 0.2 collective-permute-start.13
  32.1 2.5 %collective-permute-start.14 = (bf16[2,96,128]{2,1,0:T(8,128)(2,1)S(1)}, bf16[2,96,128]{2,1,0:T(8,128)(2,1)S(1)}, u32[]{:S(2)}, u32[]{:S(2)}) collective-permute-start(bf16[2,96,128]{2,1,0:T(8,128)(2,1)S(1)} %get-tuple-element.63), channel_id=1, source_target_pairs={{0,12},{4,8},{8,4},{12,0},{1,13},{5,9},{9,5},{13,1},{2,14},{6,10},... | collective-permute-start | bytes 147464 | tf_op jit(solution)/shard_map/ppermute | solution.py:480
  34.5 0.0 collective-permute-done.8.refs_1_.refs_3_
  34.5 0.1 combine.4
  34.7 2.0 %collective-permute-start.10 = (bf16[2,160,128]{2,1,0:T(8,128)(2,1)S(1)}, bf16[2,160,128]{2,1,0:T(8,128)(2,1)S(1)}, u32[]{:S(2)}, u32[]{:S(2)}) collective-permute-start(bf16[2,160,128]{2,1,0:T(8,128)(2,1)S(1)} %get-tuple-element.59), channel_id=1, source_target_pairs={{0,8},{4,12},{8,0},{12,4},{1,9},{5,13},{9,1},{13,5},{2,10},{6,14},... | collective-permute-start | bytes 245768 | tf_op jit(solution)/shard_map/ppermute | solution.py:480
  36.6 0.2 combine.5
  36.8 1.2 %collective-permute-start.12 = (bf16[2,256,128]{2,1,0:T(8,128)(2,1)S(1)}, bf16[2,256,128]{2,1,0:T(8,128)(2,1)S(1)}, u32[]{:S(2)}, u32[]{:S(2)}) collective-permute-start(bf16[2,256,128]{2,1,0:T(8,128)(2,1)S(1)} %get-tuple-element.62), channel_id=1, source_target_pairs={{0,4},{4,0},{8,12},{12,8},{1,5},{5,1},{9,13},{13,9},{2,6},{6,2},{1... | collective-permute-start | bytes 393224 | tf_op jit(solution)/shard_map/ppermute | solution.py:480
  38.0 1.3 %collective-permute-start.11 = (bf16[2,160,128]{2,1,0:T(8,128)(2,1)S(1)}, bf16[2,160,128]{2,1,0:T(8,128)(2,1)S(1)}, u32[]{:S(2)}, u32[]{:S(2)}) collective-permute-start(bf16[2,160,128]{2,1,0:T(8,128)(2,1)S(1)} %get-tuple-element.60), channel_id=1, source_target_pairs={{0,12},{4,8},{8,4},{12,0},{1,13},{5,9},{9,5},{13,1},{2,14},{6,10},... | collective-permute-start | bytes 245768 | tf_op jit(solution)/shard_map/ppermute | solution.py:480
  39.3 0.0 collective-permute-done.13.refs_0_
  39.3 0.0 collective-permute-done.14.refs_1_
  39.4 0.8 %place.2.refs_3_ = bf16[8,64,512]{2,1,0:T(8,128)(2,1)} custom-call(bf16[2,96,128]{2,1,0:T(8,128)(2,1)S(1)} %collective-permute-done.13.refs_0_, bf16[2,96,128]{2,1,0:T(8,128)(2,1)S(1)} %collective-permute-done.14.refs_1_, bf16[2,256,128]{2,1,0:T(8,128)(2,1)S(1)} %get-tuple-element.64.refs_2_), custom_call_target="tpu_custom_call" | custom-call | flops 45875200000 | tf_op jit(solution)/shard_map/place/pallas_call | solution.py:464
  40.1 3.3 %collective-permute-done.10.refs_0_ = bf16[2,160,128]{2,1,0:T(8,128)(2,1)S(1)} collective-permute-done((bf16[2,160,128]{2,1,0:T(8,128)(2,1)S(1)}, bf16[2,160,128]{2,1,0:T(8,128)(2,1)S(1)}, u32[]{:S(2)}, u32[]{:S(2)}) %collective-permute-start.10) | collective-permute-done | bytes 81952 | tf_op jit(solution)/shard_map/ppermute | solution.py:480
  43.4 1.2 %collective-permute-done.11.refs_1_ = bf16[2,160,128]{2,1,0:T(8,128)(2,1)S(1)} collective-permute-done((bf16[2,160,128]{2,1,0:T(8,128)(2,1)S(1)}, bf16[2,160,128]{2,1,0:T(8,128)(2,1)S(1)}, u32[]{:S(2)}, u32[]{:S(2)}) %collective-permute-start.11) | collective-permute-done | bytes 81952 | tf_op jit(solution)/shard_map/ppermute | solution.py:480
  44.5 0.2 collective-permute-done.12.refs_2_
  44.7 0.8 %place.3 = bf16[8,64,512]{2,1,0:T(8,128)(2,1)} custom-call(bf16[2,160,128]{2,1,0:T(8,128)(2,1)S(1)} %collective-permute-done.10.refs_0_, bf16[2,160,128]{2,1,0:T(8,128)(2,1)S(1)} %collective-permute-done.11.refs_1_, bf16[2,256,128]{2,1,0:T(8,128)(2,1)S(1)} %collective-permute-done.12.refs_2_, ...), custom_call_target="tpu_custom_call", output_to_operand_aliasing={{}: (3, {})} | custom-call | flops 58982400000 | tf_op jit(solution)/shard_map/place/pallas_call | solution.py:464
Async XLA Ops:
  0.9 11.6 %collective-permute-start.1 = (bf16[64,1024]{1,0:T(8,128)(2,1)S(1)}, bf16[64,1024]{1,0:T(8,128)(2,1)S(1)}, u32[]{:S(2)}, u32[]{:S(2)}) collective-permute-start(bf16[64,1024]{1,0:T(8,128)(2,1)S(1)} %pick.1), channel_id=1, source_target_pairs={{0,8},{4,12},{8,0},{12,4},{1,9},{5,13},{9,1},{13,5},{2,10},{6,14},... | collective-permute-start | bytes 393224 | tf_op jit(solution)/shard_map/ppermute | solution.py:480
  5.0 8.7 %collective-permute-start = (bf16[256,512]{1,0:T(8,128)(2,1)}, bf16[256,512]{1,0:T(8,128)(2,1)S(1)}, u32[]{:S(2)}, u32[]{:S(2)}) collective-permute-start(bf16[256,512]{1,0:T(8,128)(2,1)} %bitcast.8), channel_id=1, source_target_pairs={{0,2},{2,0},{1,3},{3,1},{4,6},{6,4},{5,7},{7,5},{8,10},{10,8},{9,1... | collective-permute-start | bytes 786440 | tf_op jit(solution)/shard_map/ppermute | solution.py:484
  6.5 12.2 %collective-permute-start.3 = (bf16[128,1024]{1,0:T(8,128)(2,1)}, bf16[128,1024]{1,0:T(8,128)(2,1)S(1)}, u32[]{:S(2)}, u32[]{:S(2)}) collective-permute-start(bf16[128,1024]{1,0:T(8,128)(2,1)} %mesh.1), channel_id=1, source_target_pairs={{0,4},{4,0},{8,12},{12,8},{1,5},{5,1},{9,13},{13,9},{2,6},{6,2},{1... | collective-permute-start | bytes 786440 | tf_op jit(solution)/shard_map/ppermute | solution.py:480
  12.2 7.8 %collective-permute-start.5 = (bf16[64,1024]{1,0:T(8,128)(2,1)S(1)}, bf16[64,1024]{1,0:T(8,128)(2,1)S(1)}, u32[]{:S(2)}, u32[]{:S(2)}) collective-permute-start(bf16[64,1024]{1,0:T(8,128)(2,1)S(1)} %get-tuple-element.43), channel_id=1, source_target_pairs={{0,12},{4,8},{8,4},{12,0},{1,13},{5,9},{9,5},{13,1},{2,14},{6,10},... | collective-permute-start | bytes 393224 | tf_op jit(solution)/shard_map/ppermute | solution.py:480
  12.5 5.0 %collective-permute-start.2 = (bf16[64,1024]{1,0:T(8,128)(2,1)S(1)}, bf16[64,1024]{1,0:T(8,128)(2,1)S(1)}, u32[]{:S(2)}, u32[]{:S(2)}) collective-permute-start(bf16[64,1024]{1,0:T(8,128)(2,1)S(1)} %collective-permute-done.1.refs_2_), channel_id=1, source_target_pairs={{0,2},{2,0},{1,3},{3,1},{4,6},{6,4},{5,7},{7,5},{8,10},{10,8},{9,1... | collective-permute-start | bytes 393224 | tf_op jit(solution)/shard_map/ppermute | solution.py:484
  13.0 8.5 %collective-permute-start.4 = (bf16[64,1024]{1,0:T(8,128)(2,1)S(1)}, bf16[64,1024]{1,0:T(8,128)(2,1)S(1)}, u32[]{:S(2)}, u32[]{:S(2)}) collective-permute-start(bf16[64,1024]{1,0:T(8,128)(2,1)S(1)} %collective-permute-done.1.refs_2_), channel_id=1, source_target_pairs={{0,4},{4,0},{8,12},{12,8},{1,5},{5,1},{9,13},{13,9},{2,6},{6,2},{1... | collective-permute-start | bytes 393224 | tf_op jit(solution)/shard_map/ppermute | solution.py:480
  13.7 5.0 %copy-start = (bf16[1024,512]{1,0:T(8,128)(2,1)S(1)}, bf16[1024,512]{1,0:T(8,128)(2,1)}, u32[]{:S(2)}) copy-start(bf16[1024,512]{1,0:T(8,128)(2,1)} %refs_4_.3) | copy-start | bytes 3145732
  13.7 5.0 %copy-start.1 = (bf16[1024,512]{1,0:T(8,128)(2,1)S(1)}, bf16[1024,512]{1,0:T(8,128)(2,1)}, u32[]{:S(2)}) copy-start(bf16[1024,512]{1,0:T(8,128)(2,1)} %refs_5_.3) | copy-start | bytes 3145732
  19.7 3.8 %copy-start.2 = (bf16[512,1024]{1,0:T(8,128)(2,1)S(1)}, bf16[512,1024]{1,0:T(8,128)(2,1)}, u32[]{:S(2)}) copy-start(bf16[512,1024]{1,0:T(8,128)(2,1)} %wo.3) | copy-start | bytes 3145732
  19.7 3.8 %copy-start.4 = (s32[4,8]{1,0:T(4,128)S(1)}, s32[4,8]{1,0:T(4,128)}, u32[]{:S(2)}) copy-start(s32[4,8]{1,0:T(4,128)} %adjacency.1) | copy-start | bytes 388
  19.7 2.4 %collective-permute-start.7 = (bf16[384,1024]{1,0:T(8,128)(2,1)S(1)}, bf16[384,1024]{1,0:T(8,128)(2,1)S(1)}, u32[]{:S(2)}, u32[]{:S(2)}) collective-permute-start(bf16[384,1024]{1,0:T(8,128)(2,1)S(1)} %project.3), channel_id=1, source_target_pairs={{0,1},{1,0},{2,3},{3,2},{4,5},{5,4},{6,7},{7,6},{8,9},{9,8},{10,11... | collective-permute-start | bytes 2359304 | tf_op jit(solution)/shard_map/ppermute | solution.py:484
  21.9 1.6 %collective-permute-start.6 = (bf16[128,1024]{1,0:T(8,128)(2,1)S(1)}, bf16[128,1024]{1,0:T(8,128)(2,1)S(1)}, u32[]{:S(2)}, u32[]{:S(2)}) collective-permute-start(bf16[128,1024]{1,0:T(8,128)(2,1)S(1)} %project.2), channel_id=1, source_target_pairs={{0,1},{1,0},{2,3},{3,2},{4,5},{5,4},{6,7},{7,6},{8,9},{9,8},{10,11... | collective-permute-start | bytes 786440 | tf_op jit(solution)/shard_map/ppermute | solution.py:484
  26.1 5.7 %collective-permute-start.9 = (bf16[4,96,128]{2,1,0:T(8,128)(2,1)S(1)}, bf16[4,96,128]{2,1,0:T(8,128)(2,1)S(1)}, u32[]{:S(2)}, u32[]{:S(2)}) collective-permute-start(bf16[4,96,128]{2,1,0:T(8,128)(2,1)S(1)} %get-tuple-element.56), channel_id=1, source_target_pairs={{0,2},{2,0},{1,3},{3,1},{4,6},{6,4},{5,7},{7,5},{8,10},{10,8},{9,1... | collective-permute-start | bytes 294920 | tf_op jit(solution)/shard_map/ppermute | solution.py:484
  26.8 0.7 %copy-start.5 = (s32[4,1]{0,1:T(1,128)S(1)}, s32[4,1]{0,1:T(1,128)}, u32[]{:S(2)}) copy-start(s32[4,1]{0,1:T(1,128)} %param.12) | copy-start | bytes 52
  26.8 5.0 %copy-start.3 = (bf16[4,64,512]{2,1,0:T(8,128)(2,1)S(1)}, bf16[4,64,512]{2,1,0:T(8,128)(2,1)}, u32[]{:S(2)}) copy-start(bf16[4,64,512]{2,1,0:T(8,128)(2,1)} %grid_features.5) | copy-start | bytes 786436
  27.5 7.0 %collective-permute-start.8 = (bf16[4,160,128]{2,1,0:T(8,128)(2,1)S(1)}, bf16[4,160,128]{2,1,0:T(8,128)(2,1)S(1)}, u32[]{:S(2)}, u32[]{:S(2)}) collective-permute-start(bf16[4,160,128]{2,1,0:T(8,128)(2,1)S(1)} %get-tuple-element.54), channel_id=1, source_target_pairs={{0,2},{2,0},{1,3},{3,1},{4,6},{6,4},{5,7},{7,5},{8,10},{10,8},{9,1... | collective-permute-start | bytes 491528 | tf_op jit(solution)/shard_map/ppermute | solution.py:484
  31.9 7.5 %collective-permute-start.13 = (bf16[2,96,128]{2,1,0:T(8,128)(2,1)S(1)}, bf16[2,96,128]{2,1,0:T(8,128)(2,1)S(1)}, u32[]{:S(2)}, u32[]{:S(2)}) collective-permute-start(bf16[2,96,128]{2,1,0:T(8,128)(2,1)S(1)} %get-tuple-element.57), channel_id=1, source_target_pairs={{0,8},{4,12},{8,0},{12,4},{1,9},{5,13},{9,1},{13,5},{2,10},{6,14},... | collective-permute-start | bytes 147464 | tf_op jit(solution)/shard_map/ppermute | solution.py:480
  32.1 7.3 %collective-permute-start.14 = (bf16[2,96,128]{2,1,0:T(8,128)(2,1)S(1)}, bf16[2,96,128]{2,1,0:T(8,128)(2,1)S(1)}, u32[]{:S(2)}, u32[]{:S(2)}) collective-permute-start(bf16[2,96,128]{2,1,0:T(8,128)(2,1)S(1)} %get-tuple-element.63), channel_id=1, source_target_pairs={{0,12},{4,8},{8,4},{12,0},{1,13},{5,9},{9,5},{13,1},{2,14},{6,10},... | collective-permute-start | bytes 147464 | tf_op jit(solution)/shard_map/ppermute | solution.py:480
  34.7 8.7 %collective-permute-start.10 = (bf16[2,160,128]{2,1,0:T(8,128)(2,1)S(1)}, bf16[2,160,128]{2,1,0:T(8,128)(2,1)S(1)}, u32[]{:S(2)}, u32[]{:S(2)}) collective-permute-start(bf16[2,160,128]{2,1,0:T(8,128)(2,1)S(1)} %get-tuple-element.59), channel_id=1, source_target_pairs={{0,8},{4,12},{8,0},{12,4},{1,9},{5,13},{9,1},{13,5},{2,10},{6,14},... | collective-permute-start | bytes 245768 | tf_op jit(solution)/shard_map/ppermute | solution.py:480
  36.8 7.9 %collective-permute-start.12 = (bf16[2,256,128]{2,1,0:T(8,128)(2,1)S(1)}, bf16[2,256,128]{2,1,0:T(8,128)(2,1)S(1)}, u32[]{:S(2)}, u32[]{:S(2)}) collective-permute-start(bf16[2,256,128]{2,1,0:T(8,128)(2,1)S(1)} %get-tuple-element.62), channel_id=1, source_target_pairs={{0,4},{4,0},{8,12},{12,8},{1,5},{5,1},{9,13},{13,9},{2,6},{6,2},{1... | collective-permute-start | bytes 393224 | tf_op jit(solution)/shard_map/ppermute | solution.py:480
  38.0 6.6 %collective-permute-start.11 = (bf16[2,160,128]{2,1,0:T(8,128)(2,1)S(1)}, bf16[2,160,128]{2,1,0:T(8,128)(2,1)S(1)}, u32[]{:S(2)}, u32[]{:S(2)}) collective-permute-start(bf16[2,160,128]{2,1,0:T(8,128)(2,1)S(1)} %get-tuple-element.60), channel_id=1, source_target_pairs={{0,12},{4,8},{8,4},{12,0},{1,13},{5,9},{9,5},{13,1},{2,14},{6,10},... | collective-permute-start | bytes 245768 | tf_op jit(solution)/shard_map/ppermute | solution.py:480

commit v23 on v21

--- a/solution.py
+++ b/solution.py
@@ -15,7 +15,7 @@
 QUAD = 4
 WIDE = QUAD * HEAD_DIM
 TILE = 128
-CHUNKS = ((0, 80), (80, 256))
+CHUNKS = ((0, 96), (96, 256))
 MIB = 1 << 20
 
 
@@ -370,8 +370,8 @@
 
 def plan_kernel(owners, masks):
     s = lax.axis_index("shard")
-    count = owners.shape[0]
-    names = [owners[t, 0] for t in range(count)]
+    count = owners.shape[1]
+    names = [owners[0, t] for t in range(count)]
     for t in range(count):
         same = [(names[e] == names[t]).astype(jnp.int32) for e in range(t)]
         rank = sum(same, jnp.int32(0))
@@ -384,7 +384,7 @@
 def run_plan(owners, shards):
     return pl.pallas_call(
         plan_kernel,
-        out_shape=jax.ShapeDtypeStruct((shards, CAP, owners.shape[0], 8, 128), jnp.float32),
+        out_shape=jax.ShapeDtypeStruct((shards, CAP, owners.shape[1], 8, 128), jnp.float32),
         in_specs=[whole(pltpu.SMEM)],
         out_specs=whole(pltpu.VMEM),
         compiler_params=params(4),
@@ -543,7 +543,7 @@
         swaps.append(received)
         keeps.append(keep)
     named, _ = lax.optimization_barrier((owners, keep))
-    masks = run_plan(named, shards)
+    masks = run_plan(named.T, shards)
     for c in every:
         received = swaps[c]
         if c > 0:
@@ -552,15 +552,15 @@
     swaps[-1], _ = lax.optimization_barrier((swaps[-1], slots[-1][0]))
     near_slots, own_slots = run_combine(every, (1, 0), masks, grid_features, keeps, swaps)
     for c in every:
-        spots = [(2, (c,)), (3, (c,))]
-        arrived = [crossed(slot, d, shards) for d, slot in zip((2, 3), slots[c])]
+        moved = {d: crossed(slot, d, shards) for d, slot in zip((2, 3), slots[c])}
         if c == 0:
-            spots.append((0, every))
-            arrived.append(own_slots)
-        if c == every[-1]:
-            spots.append((1, every))
-            arrived.append(crossed(near_slots, 1, shards))
-        placed = [run_place(spots, arrived, placed, shape)]
+            groups = [[(2, (c,)), (3, (c,)), (0, every)]]
+            moved[0] = own_slots
+        else:
+            groups = [[(1, every), (2, (c,))], [(3, (c,))]]
+            moved[1] = crossed(near_slots, 1, shards)
+        for spots in groups:
+            placed = [run_place(spots, [moved[d] for d, _ in spots], placed, shape)]
     return placed[0]
 
 

time: 45.7 us -> 46.2 us (1.011)
  Pallas kernels: 15.4 us -> 15.9 us
    pallas_call x2 -> x3, Pallas kernels: 1.56 us -> 2.17 us  [run_place(): pl.pallas_call(functools.partial(place_kernel, spots), out_shape=jax.Shap...]
  transfers between devices with their start and end apart: 15 -> 15, of which waited for: 10 -> 9; matrix products, arithmetic and copies ran while one was open for 0% -> 0% of each run, Pallas kernels for 24% -> 26%
where the time goes in v23:
time: 46.2 us; the launch traced here: 46.1 us
  starting transfers between devices  18.1 us (39%)
  Pallas kernels  15.9 us (34%)
  waiting for transfers between devices  11.9 us (26%)
    ppermute x9, starting transfers between devices, crossed(): return lax.ppermute(x, 'shard', [(i, i ^ distance) for i in range(size)])  13.8 us
    ppermute x9, waiting for transfers between devices, crossed(): return lax.ppermute(x, 'shard', [(i, i ^ distance) for i in range(size)])  7.52 us
    ppermute x6, waiting for transfers between devices, swapped(): return lax.ppermute(x, axis, [(0, 1), (1, 0)])  4.34 us
    ppermute x6, starting transfers between devices, swapped(): return lax.ppermute(x, axis, [(0, 1), (1, 0)])  4.27 us
    pallas_call x1, Pallas kernels, run_stage(): pl.pallas_call(functools.partial(stage_kernel, axes), out_shape=tuple((ja...  4.1 us
    pallas_call x1, Pallas kernels, run_mlp(): pl.pallas_call(mlp_kernel, out_shape=(jax.ShapeDtypeStruct((rows, wq.shap...  3.33 us
    pallas_call x1, Pallas kernels, run_attend(): pl.pallas_call(attend_kernel, out_shape=(part, part, jax.ShapeDtypeStruct...  2.51 us
    pallas_call x3, Pallas kernels, run_place(): pl.pallas_call(functools.partial(place_kernel, spots), out_shape=jax.Shap...  2.17 us
  transfers between devices with their start and end apart: 15, of which 9 were waited for; matrix products, arithmetic and copies ran while one was open for 0% of the time, Pallas kernels for 26%

profile of v23, /device:TPU:0, one launch (start us, length us, event | category | flops | bytes accessed | tf_op | source)
XLA Modules:
  0.0 46.1 jit_solution(1689409039189853087)
XLA Ops:
  0.0 0.9 %pick.1 = bf16[64,1024]{1,0:T(8,128)(2,1)S(1)} custom-call(bf16[128,1024]{1,0:T(8,128)(2,1)} %mesh.1), custom_call_target="tpu_custom_call" | custom-call | bytes 524288 | tf_op jit(solution)/shard_map/pick/pallas_call | solution.py:113
  0.9 4.1 %collective-permute-start.1 = (bf16[64,1024]{1,0:T(8,128)(2,1)S(1)}, bf16[64,1024]{1,0:T(8,128)(2,1)S(1)}, u32[]{:S(2)}, u32[]{:S(2)}) collective-permute-start(bf16[64,1024]{1,0:T(8,128)(2,1)S(1)} %pick.1), channel_id=1, source_target_pairs={{0,8},{4,12},{8,0},{12,4},{1,9},{5,13},{9,1},{13,5},{2,10},{6,14},... | collective-permute-start | bytes 393224 | tf_op jit(solution)/shard_map/ppermute | solution.py:480
  5.0 1.5 %collective-permute-start = (bf16[256,512]{1,0:T(8,128)(2,1)}, bf16[256,512]{1,0:T(8,128)(2,1)S(1)}, u32[]{:S(2)}, u32[]{:S(2)}) collective-permute-start(bf16[256,512]{1,0:T(8,128)(2,1)} %bitcast.9), channel_id=1, source_target_pairs={{0,2},{2,0},{1,3},{3,1},{4,6},{6,4},{5,7},{7,5},{8,10},{10,8},{9,1... | collective-permute-start | bytes 786440 | tf_op jit(solution)/shard_map/ppermute | solution.py:484
  6.5 1.6 %collective-permute-start.3 = (bf16[128,1024]{1,0:T(8,128)(2,1)}, bf16[128,1024]{1,0:T(8,128)(2,1)S(1)}, u32[]{:S(2)}, u32[]{:S(2)}) collective-permute-start(bf16[128,1024]{1,0:T(8,128)(2,1)} %mesh.1), channel_id=1, source_target_pairs={{0,4},{4,0},{8,12},{12,8},{1,5},{5,1},{9,13},{13,9},{2,6},{6,2},{1... | collective-permute-start | bytes 786440 | tf_op jit(solution)/shard_map/ppermute | solution.py:480
  8.1 4.1 %stage.1 = (bf16[256,512]{1,0:T(8,128)(2,1)S(1)}, f32[1,1024]{1,0:T(1,128)S(1)}, bf16[1024,512]{1,0:T(8,128)(2,1)S(1)}, bf16[1024,2048]{1,0:T(8,128)(2,1)S(1)}, ...) custom-call(bf16[256,512]{1,0:T(8,128)(2,1)} %bitcast.10, ...), custom_call_target="tpu_custom_call" | custom-call | flops 20451328000 | bytes 204513280 | tf_op jit(solution)/shard_map/stage/pallas_call | solution.py:163
  12.2 0.3 collective-permute-start.5
  12.5 0.0 collective-permute-done.1.refs_2_
  12.5 0.5 %collective-permute-start.2 = (bf16[64,1024]{1,0:T(8,128)(2,1)S(1)}, bf16[64,1024]{1,0:T(8,128)(2,1)S(1)}, u32[]{:S(2)}, u32[]{:S(2)}) collective-permute-start(bf16[64,1024]{1,0:T(8,128)(2,1)S(1)} %collective-permute-done.1.refs_2_), channel_id=1, source_target_pairs={{0,2},{2,0},{1,3},{3,1},{4,6},{6,4},{5,7},{7,5},{8,10},{10,8},{9,1... | collective-permute-start | bytes 393224 | tf_op jit(solution)/shard_map/ppermute | solution.py:484
  13.0 0.7 %collective-permute-start.4 = (bf16[64,1024]{1,0:T(8,128)(2,1)S(1)}, bf16[64,1024]{1,0:T(8,128)(2,1)S(1)}, u32[]{:S(2)}, u32[]{:S(2)}) collective-permute-start(bf16[64,1024]{1,0:T(8,128)(2,1)S(1)} %collective-permute-done.1.refs_2_), channel_id=1, source_target_pairs={{0,4},{4,0},{8,12},{12,8},{1,5},{5,1},{9,13},{13,9},{2,6},{6,2},{1... | collective-permute-start | bytes 393224 | tf_op jit(solution)/shard_map/ppermute | solution.py:480
  13.7 0.0 collective-permute-done.other
  13.7 0.0 copy-start
  13.7 0.0 copy-start.1
  13.7 3.3 %mlp.1 = (bf16[256,512]{1,0:T(8,128)(2,1)S(1)}, f32[256,1024]{1,0:T(8,128)S(1)}) custom-call(bf16[256,512]{1,0:T(8,128)(2,1)S(1)} %get-tuple-element.35.own, bf16[256,512]{1,0:T(8,128)(2,1)S(1)} %collective-permute-done.other, f32[1,1024]{1,0:T(1,128)S(1)} %get-tuple-element.37.gain, bf16[1024,512]{1,0:T(8,128)(2,1)S(1)} %get-tuple-element.38.wq, ...), custom_call_target="tpu_custom_call" | custom-call | flops 2415919104 | bytes 9437184 | tf_op jit(solution)/shard_map/mlp/pallas_call | solution.py:86
  17.1 0.4 collective-permute-done.2.refs_3_
  17.5 1.2 %collective-permute-done.3.refs_1_ = bf16[128,1024]{1,0:T(8,128)(2,1)S(1)} collective-permute-done((bf16[128,1024]{1,0:T(8,128)(2,1)}, bf16[128,1024]{1,0:T(8,128)(2,1)S(1)}, u32[]{:S(2)}, u32[]{:S(2)}) %collective-permute-start.3) | collective-permute-done | bytes 262176 | tf_op jit(solution)/shard_map/ppermute | solution.py:480
  18.7 0.0 copy-done
  18.7 0.0 copy-done.1
  18.7 1.0 %project.3 = bf16[384,1024]{1,0:T(8,128)(2,1)S(1)} custom-call(bf16[128,1024]{1,0:T(8,128)(2,1)S(1)} %get-tuple-element.47.refs_0_, bf16[128,1024]{1,0:T(8,128)(2,1)S(1)} %collective-permute-done.3.refs_1_, bf16[64,1024]{1,0:T(8,128)(2,1)S(1)} %collective-permute-done.1.refs_2_, bf16[64,1024]{1,0:T(8,128)(2,1)S(1)} %collective-permute-done.2.refs_3_, ...), custom_call_target="tpu_custom_call" | custom-call | flops 60397977600 | bytes 275251200 | tf_op jit(solution)/shard_map/project/pallas_call | solution.py:191
  19.7 0.0 copy-start.2
  19.7 0.0 copy-start.4
  19.7 0.1 collective-permute-start.7
  19.8 0.2 collective-permute-done.5.refs_1_
  20.0 1.5 %collective-permute-done.4.refs_0_ = bf16[64,1024]{1,0:T(8,128)(2,1)S(1)} collective-permute-done((bf16[64,1024]{1,0:T(8,128)(2,1)S(1)}, bf16[64,1024]{1,0:T(8,128)(2,1)S(1)}, u32[]{:S(2)}, u32[]{:S(2)}) %collective-permute-start.4) | collective-permute-done | bytes 131104 | tf_op jit(solution)/shard_map/ppermute | solution.py:480
  21.5 0.4 project.2
  21.9 0.1 collective-permute-start.6
  22.0 0.1 collective-permute-done.7
  22.1 0.1 table.1.table_in
  22.2 1.4 %collective-permute-done.6 = bf16[128,1024]{1,0:T(8,128)(2,1)S(1)} collective-permute-done((bf16[128,1024]{1,0:T(8,128)(2,1)S(1)}, bf16[128,1024]{1,0:T(8,128)(2,1)S(1)}, u32[]{:S(2)}, u32[]{:S(2)}) %collective-permute-start.6) | collective-permute-done | bytes 262176 | tf_op jit(solution)/shard_map/ppermute | solution.py:484
  23.5 0.0 copy-done.2
  23.5 0.0 copy-done.4
  23.5 2.5 %attend.1 = (bf16[4,96,128]{2,1,0:T(8,128)(2,1)S(1)}, bf16[4,96,128]{2,1,0:T(8,128)(2,1)S(1)}, bf16[256,512]{1,0:T(8,128)(2,1)S(1)}, bf16[2,8,64,1024]{3,2,1,0:T(8,128)(2,1)S(1)}) custom-call(s32[4,8]{1,0:T(4,128)S(1)} %copy-done.4, bf16[256,512]{1,0:T(8,128)(2,1)S(1)} %get-tuple-element.46.q, ...), custom_call_target="tpu_custom_call", output_to_operand_aliasing={{3}: (4, {})} | custom-call | flops 13421772800 | bytes 41943040 | tf_op jit(solution)/shard_map/attend/pallas_call | solution.py:325
  26.0 0.6 %collective-permute-start.9 = (bf16[4,96,128]{2,1,0:T(8,128)(2,1)S(1)}, bf16[4,96,128]{2,1,0:T(8,128)(2,1)S(1)}, u32[]{:S(2)}, u32[]{:S(2)}) collective-permute-start(bf16[4,96,128]{2,1,0:T(8,128)(2,1)S(1)} %get-tuple-element.56), channel_id=1, source_target_pairs={{0,2},{2,0},{1,3},{3,1},{4,6},{6,4},{5,7},{7,5},{8,10},{10,8},{9,1... | collective-permute-start | bytes 294920 | tf_op jit(solution)/shard_map/ppermute | solution.py:484
  26.7 0.0 copy-start.5
  26.7 0.0 copy-start.3
  26.7 0.4 project_out.1
  27.1 1.5 %collective-permute-start.8 = (bf16[4,160,128]{2,1,0:T(8,128)(2,1)S(1)}, bf16[4,160,128]{2,1,0:T(8,128)(2,1)S(1)}, u32[]{:S(2)}, u32[]{:S(2)}) collective-permute-start(bf16[4,160,128]{2,1,0:T(8,128)(2,1)S(1)} %get-tuple-element.54), channel_id=1, source_target_pairs={{0,2},{2,0},{1,3},{3,1},{4,6},{6,4},{5,7},{7,5},{8,10},{10,8},{9,1... | collective-permute-start | bytes 491528 | tf_op jit(solution)/shard_map/ppermute | solution.py:484
  28.7 0.0 copy-done.5
  28.7 0.6 %plan.1.masks = f32[4,2,4,8,128]{4,3,2,1,0:T(8,128)S(1)} custom-call(s32[1,4]{1,0:T(1,128)S(1)} %bitcast.13), custom_call_target="tpu_custom_call" | custom-call | flops 100000000 | bytes 262144 | tf_op jit(solution)/shard_map/plan/pallas_call | solution.py:385
  29.3 2.5 %collective-permute-done.9.refs_1_.refs_2_ = bf16[4,96,128]{2,1,0:T(8,128)(2,1)S(1)} collective-permute-done((bf16[4,96,128]{2,1,0:T(8,128)(2,1)S(1)}, bf16[4,96,128]{2,1,0:T(8,128)(2,1)S(1)}, u32[]{:S(2)}, u32[]{:S(2)}) %collective-permute-start.9) | collective-permute-done | bytes 98336 | tf_op jit(solution)/shard_map/ppermute | solution.py:484
  31.8 0.0 copy-done.3
  31.8 0.1 combine.3
  31.8 0.4 collective-permute-start.13
  32.3 2.2 %collective-permute-start.14 = (bf16[2,96,128]{2,1,0:T(8,128)(2,1)S(1)}, bf16[2,96,128]{2,1,0:T(8,128)(2,1)S(1)}, u32[]{:S(2)}, u32[]{:S(2)}) collective-permute-start(bf16[2,96,128]{2,1,0:T(8,128)(2,1)S(1)} %get-tuple-element.63), channel_id=1, source_target_pairs={{0,12},{4,8},{8,4},{12,0},{1,13},{5,9},{9,5},{13,1},{2,14},{6,10},... | collective-permute-start | bytes 147464 | tf_op jit(solution)/shard_map/ppermute | solution.py:480
  34.4 0.0 collective-permute-done.8.refs_1_.refs_3_
  34.5 0.1 combine.4
  34.6 2.0 %collective-permute-start.12 = (bf16[2,160,128]{2,1,0:T(8,128)(2,1)S(1)}, bf16[2,160,128]{2,1,0:T(8,128)(2,1)S(1)}, u32[]{:S(2)}, u32[]{:S(2)}) collective-permute-start(bf16[2,160,128]{2,1,0:T(8,128)(2,1)S(1)} %get-tuple-element.60), channel_id=1, source_target_pairs={{0,8},{4,12},{8,0},{12,4},{1,9},{5,13},{9,1},{13,5},{2,10},{6,14},... | collective-permute-start | bytes 245768 | tf_op jit(solution)/shard_map/ppermute | solution.py:480
  36.6 0.2 combine.5
  36.7 1.2 %collective-permute-start.11 = (bf16[2,256,128]{2,1,0:T(8,128)(2,1)S(1)}, bf16[2,256,128]{2,1,0:T(8,128)(2,1)S(1)}, u32[]{:S(2)}, u32[]{:S(2)}) collective-permute-start(bf16[2,256,128]{2,1,0:T(8,128)(2,1)S(1)} %get-tuple-element.62), channel_id=1, source_target_pairs={{0,4},{4,0},{8,12},{12,8},{1,5},{5,1},{9,13},{13,9},{2,6},{6,2},{1... | collective-permute-start | bytes 393224 | tf_op jit(solution)/shard_map/ppermute | solution.py:480
  37.9 1.4 %collective-permute-start.10 = (bf16[2,160,128]{2,1,0:T(8,128)(2,1)S(1)}, bf16[2,160,128]{2,1,0:T(8,128)(2,1)S(1)}, u32[]{:S(2)}, u32[]{:S(2)}) collective-permute-start(bf16[2,160,128]{2,1,0:T(8,128)(2,1)S(1)} %get-tuple-element.59), channel_id=1, source_target_pairs={{0,12},{4,8},{8,4},{12,0},{1,13},{5,9},{9,5},{13,1},{2,14},{6,10},... | collective-permute-start | bytes 245768 | tf_op jit(solution)/shard_map/ppermute | solution.py:480
  39.3 0.0 collective-permute-done.13.refs_0_
  39.3 0.0 collective-permute-done.14.refs_1_
  39.3 0.8 %place.3.refs_2_ = bf16[8,64,512]{2,1,0:T(8,128)(2,1)} custom-call(bf16[2,96,128]{2,1,0:T(8,128)(2,1)S(1)} %collective-permute-done.13.refs_0_, bf16[2,96,128]{2,1,0:T(8,128)(2,1)S(1)} %collective-permute-done.14.refs_1_, bf16[2,256,128]{2,1,0:T(8,128)(2,1)S(1)} %get-tuple-element.64.refs_2_), custom_call_target="tpu_custom_call" | custom-call | flops 45875200000 | tf_op jit(solution)/shard_map/place/pallas_call | solution.py:464
  40.0 3.3 %collective-permute-done.12.refs_1_ = bf16[2,160,128]{2,1,0:T(8,128)(2,1)S(1)} collective-permute-done((bf16[2,160,128]{2,1,0:T(8,128)(2,1)S(1)}, bf16[2,160,128]{2,1,0:T(8,128)(2,1)S(1)}, u32[]{:S(2)}, u32[]{:S(2)}) %collective-permute-start.12) | collective-permute-done | bytes 81952 | tf_op jit(solution)/shard_map/ppermute | solution.py:480
  43.3 1.3 %collective-permute-done.11.refs_0_ = bf16[2,256,128]{2,1,0:T(8,128)(2,1)S(1)} collective-permute-done((bf16[2,256,128]{2,1,0:T(8,128)(2,1)S(1)}, bf16[2,256,128]{2,1,0:T(8,128)(2,1)S(1)}, u32[]{:S(2)}, u32[]{:S(2)}) %collective-permute-start.11) | collective-permute-done | bytes 131104 | tf_op jit(solution)/shard_map/ppermute | solution.py:480
  44.6 0.7 %place.4.refs_1_ = bf16[8,64,512]{2,1,0:T(8,128)(2,1)} custom-call(bf16[2,256,128]{2,1,0:T(8,128)(2,1)S(1)} %collective-permute-done.11.refs_0_, bf16[2,160,128]{2,1,0:T(8,128)(2,1)S(1)} %collective-permute-done.12.refs_1_, bf16[8,64,512]{2,1,0:T(8,128)(2,1)} %place.3.refs_2_), custom_call_target="tpu_custom_call", output_to_operand_aliasing={{}: (2, {})} | custom-call | flops 42598400000 | tf_op jit(solution)/shard_map/place/pallas_call | solution.py:464
  45.4 0.0 collective-permute-done.10.refs_0_
  45.4 0.7 %place.5 = bf16[8,64,512]{2,1,0:T(8,128)(2,1)} custom-call(bf16[2,160,128]{2,1,0:T(8,128)(2,1)S(1)} %collective-permute-done.10.refs_0_, bf16[8,64,512]{2,1,0:T(8,128)(2,1)} %place.4.refs_1_), custom_call_target="tpu_custom_call", output_to_operand_aliasing={{}: (1, {})} | custom-call | flops 16384000000 | tf_op jit(solution)/shard_map/place/pallas_call | solution.py:464
Async XLA Ops:
  0.9 11.6 %collective-permute-start.1 = (bf16[64,1024]{1,0:T(8,128)(2,1)S(1)}, bf16[64,1024]{1,0:T(8,128)(2,1)S(1)}, u32[]{:S(2)}, u32[]{:S(2)}) collective-permute-start(bf16[64,1024]{1,0:T(8,128)(2,1)S(1)} %pick.1), channel_id=1, source_target_pairs={{0,8},{4,12},{8,0},{12,4},{1,9},{5,13},{9,1},{13,5},{2,10},{6,14},... | collective-permute-start | bytes 393224 | tf_op jit(solution)/shard_map/ppermute | solution.py:480
  5.0 8.7 %collective-permute-start = (bf16[256,512]{1,0:T(8,128)(2,1)}, bf16[256,512]{1,0:T(8,128)(2,1)S(1)}, u32[]{:S(2)}, u32[]{:S(2)}) collective-permute-start(bf16[256,512]{1,0:T(8,128)(2,1)} %bitcast.9), channel_id=1, source_target_pairs={{0,2},{2,0},{1,3},{3,1},{4,6},{6,4},{5,7},{7,5},{8,10},{10,8},{9,1... | collective-permute-start | bytes 786440 | tf_op jit(solution)/shard_map/ppermute | solution.py:484
  6.5 12.2 %collective-permute-start.3 = (bf16[128,1024]{1,0:T(8,128)(2,1)}, bf16[128,1024]{1,0:T(8,128)(2,1)S(1)}, u32[]{:S(2)}, u32[]{:S(2)}) collective-permute-start(bf16[128,1024]{1,0:T(8,128)(2,1)} %mesh.1), channel_id=1, source_target_pairs={{0,4},{4,0},{8,12},{12,8},{1,5},{5,1},{9,13},{13,9},{2,6},{6,2},{1... | collective-permute-start | bytes 786440 | tf_op jit(solution)/shard_map/ppermute | solution.py:480
  12.2 7.8 %collective-permute-start.5 = (bf16[64,1024]{1,0:T(8,128)(2,1)S(1)}, bf16[64,1024]{1,0:T(8,128)(2,1)S(1)}, u32[]{:S(2)}, u32[]{:S(2)}) collective-permute-start(bf16[64,1024]{1,0:T(8,128)(2,1)S(1)} %get-tuple-element.43), channel_id=1, source_target_pairs={{0,12},{4,8},{8,4},{12,0},{1,13},{5,9},{9,5},{13,1},{2,14},{6,10},... | collective-permute-start | bytes 393224 | tf_op jit(solution)/shard_map/ppermute | solution.py:480
  12.5 5.0 %collective-permute-start.2 = (bf16[64,1024]{1,0:T(8,128)(2,1)S(1)}, bf16[64,1024]{1,0:T(8,128)(2,1)S(1)}, u32[]{:S(2)}, u32[]{:S(2)}) collective-permute-start(bf16[64,1024]{1,0:T(8,128)(2,1)S(1)} %collective-permute-done.1.refs_2_), channel_id=1, source_target_pairs={{0,2},{2,0},{1,3},{3,1},{4,6},{6,4},{5,7},{7,5},{8,10},{10,8},{9,1... | collective-permute-start | bytes 393224 | tf_op jit(solution)/shard_map/ppermute | solution.py:484
  13.0 8.5 %collective-permute-start.4 = (bf16[64,1024]{1,0:T(8,128)(2,1)S(1)}, bf16[64,1024]{1,0:T(8,128)(2,1)S(1)}, u32[]{:S(2)}, u32[]{:S(2)}) collective-permute-start(bf16[64,1024]{1,0:T(8,128)(2,1)S(1)} %collective-permute-done.1.refs_2_), channel_id=1, source_target_pairs={{0,4},{4,0},{8,12},{12,8},{1,5},{5,1},{9,13},{13,9},{2,6},{6,2},{1... | collective-permute-start | bytes 393224 | tf_op jit(solution)/shard_map/ppermute | solution.py:480
  13.7 5.0 %copy-start = (bf16[1024,512]{1,0:T(8,128)(2,1)S(1)}, bf16[1024,512]{1,0:T(8,128)(2,1)}, u32[]{:S(2)}) copy-start(bf16[1024,512]{1,0:T(8,128)(2,1)} %refs_4_.3) | copy-start | bytes 3145732
  13.7 5.0 %copy-start.1 = (bf16[1024,512]{1,0:T(8,128)(2,1)S(1)}, bf16[1024,512]{1,0:T(8,128)(2,1)}, u32[]{:S(2)}) copy-start(bf16[1024,512]{1,0:T(8,128)(2,1)} %refs_5_.3) | copy-start | bytes 3145732
  19.7 3.8 %copy-start.2 = (bf16[512,1024]{1,0:T(8,128)(2,1)S(1)}, bf16[512,1024]{1,0:T(8,128)(2,1)}, u32[]{:S(2)}) copy-start(bf16[512,1024]{1,0:T(8,128)(2,1)} %wo.3) | copy-start | bytes 3145732
  19.7 3.8 %copy-start.4 = (s32[4,8]{1,0:T(4,128)S(1)}, s32[4,8]{1,0:T(4,128)}, u32[]{:S(2)}) copy-start(s32[4,8]{1,0:T(4,128)} %adjacency.1) | copy-start | bytes 388
  19.7 2.4 %collective-permute-start.7 = (bf16[384,1024]{1,0:T(8,128)(2,1)S(1)}, bf16[384,1024]{1,0:T(8,128)(2,1)S(1)}, u32[]{:S(2)}, u32[]{:S(2)}) collective-permute-start(bf16[384,1024]{1,0:T(8,128)(2,1)S(1)} %project.3), channel_id=1, source_target_pairs={{0,1},{1,0},{2,3},{3,2},{4,5},{5,4},{6,7},{7,6},{8,9},{9,8},{10,11... | collective-permute-start | bytes 2359304 | tf_op jit(solution)/shard_map/ppermute | solution.py:484
  21.9 1.6 %collective-permute-start.6 = (bf16[128,1024]{1,0:T(8,128)(2,1)S(1)}, bf16[128,1024]{1,0:T(8,128)(2,1)S(1)}, u32[]{:S(2)}, u32[]{:S(2)}) collective-permute-start(bf16[128,1024]{1,0:T(8,128)(2,1)S(1)} %project.2), channel_id=1, source_target_pairs={{0,1},{1,0},{2,3},{3,2},{4,5},{5,4},{6,7},{7,6},{8,9},{9,8},{10,11... | collective-permute-start | bytes 786440 | tf_op jit(solution)/shard_map/ppermute | solution.py:484
  26.0 5.7 %collective-permute-start.9 = (bf16[4,96,128]{2,1,0:T(8,128)(2,1)S(1)}, bf16[4,96,128]{2,1,0:T(8,128)(2,1)S(1)}, u32[]{:S(2)}, u32[]{:S(2)}) collective-permute-start(bf16[4,96,128]{2,1,0:T(8,128)(2,1)S(1)} %get-tuple-element.56), channel_id=1, source_target_pairs={{0,2},{2,0},{1,3},{3,1},{4,6},{6,4},{5,7},{7,5},{8,10},{10,8},{9,1... | collective-permute-start | bytes 294920 | tf_op jit(solution)/shard_map/ppermute | solution.py:484
  26.7 2.0 %copy-start.5 = (s32[4,1]{0,1:T(1,128)S(1)}, s32[4,1]{0,1:T(1,128)}, u32[]{:S(2)}) copy-start(s32[4,1]{0,1:T(1,128)} %param.12) | copy-start | bytes 52
  26.7 5.1 %copy-start.3 = (bf16[4,64,512]{2,1,0:T(8,128)(2,1)S(1)}, bf16[4,64,512]{2,1,0:T(8,128)(2,1)}, u32[]{:S(2)}) copy-start(bf16[4,64,512]{2,1,0:T(8,128)(2,1)} %grid_features.5) | copy-start | bytes 786436
  27.1 7.3 %collective-permute-start.8 = (bf16[4,160,128]{2,1,0:T(8,128)(2,1)S(1)}, bf16[4,160,128]{2,1,0:T(8,128)(2,1)S(1)}, u32[]{:S(2)}, u32[]{:S(2)}) collective-permute-start(bf16[4,160,128]{2,1,0:T(8,128)(2,1)S(1)} %get-tuple-element.54), channel_id=1, source_target_pairs={{0,2},{2,0},{1,3},{3,1},{4,6},{6,4},{5,7},{7,5},{8,10},{10,8},{9,1... | collective-permute-start | bytes 491528 | tf_op jit(solution)/shard_map/ppermute | solution.py:484
  31.8 7.4 %collective-permute-start.13 = (bf16[2,96,128]{2,1,0:T(8,128)(2,1)S(1)}, bf16[2,96,128]{2,1,0:T(8,128)(2,1)S(1)}, u32[]{:S(2)}, u32[]{:S(2)}) collective-permute-start(bf16[2,96,128]{2,1,0:T(8,128)(2,1)S(1)} %get-tuple-element.57), channel_id=1, source_target_pairs={{0,8},{4,12},{8,0},{12,4},{1,9},{5,13},{9,1},{13,5},{2,10},{6,14},... | collective-permute-start | bytes 147464 | tf_op jit(solution)/shard_map/ppermute | solution.py:480
  32.3 7.0 %collective-permute-start.14 = (bf16[2,96,128]{2,1,0:T(8,128)(2,1)S(1)}, bf16[2,96,128]{2,1,0:T(8,128)(2,1)S(1)}, u32[]{:S(2)}, u32[]{:S(2)}) collective-permute-start(bf16[2,96,128]{2,1,0:T(8,128)(2,1)S(1)} %get-tuple-element.63), channel_id=1, source_target_pairs={{0,12},{4,8},{8,4},{12,0},{1,13},{5,9},{9,5},{13,1},{2,14},{6,10},... | collective-permute-start | bytes 147464 | tf_op jit(solution)/shard_map/ppermute | solution.py:480
  34.6 8.7 %collective-permute-start.12 = (bf16[2,160,128]{2,1,0:T(8,128)(2,1)S(1)}, bf16[2,160,128]{2,1,0:T(8,128)(2,1)S(1)}, u32[]{:S(2)}, u32[]{:S(2)}) collective-permute-start(bf16[2,160,128]{2,1,0:T(8,128)(2,1)S(1)} %get-tuple-element.60), channel_id=1, source_target_pairs={{0,8},{4,12},{8,0},{12,4},{1,9},{5,13},{9,1},{13,5},{2,10},{6,14},... | collective-permute-start | bytes 245768 | tf_op jit(solution)/shard_map/ppermute | solution.py:480
  36.7 7.9 %collective-permute-start.11 = (bf16[2,256,128]{2,1,0:T(8,128)(2,1)S(1)}, bf16[2,256,128]{2,1,0:T(8,128)(2,1)S(1)}, u32[]{:S(2)}, u32[]{:S(2)}) collective-permute-start(bf16[2,256,128]{2,1,0:T(8,128)(2,1)S(1)} %get-tuple-element.62), channel_id=1, source_target_pairs={{0,4},{4,0},{8,12},{12,8},{1,5},{5,1},{9,13},{13,9},{2,6},{6,2},{1... | collective-permute-start | bytes 393224 | tf_op jit(solution)/shard_map/ppermute | solution.py:480
  37.9 7.5 %collective-permute-start.10 = (bf16[2,160,128]{2,1,0:T(8,128)(2,1)S(1)}, bf16[2,160,128]{2,1,0:T(8,128)(2,1)S(1)}, u32[]{:S(2)}, u32[]{:S(2)}) collective-permute-start(bf16[2,160,128]{2,1,0:T(8,128)(2,1)S(1)} %get-tuple-element.59), channel_id=1, source_target_pairs={{0,12},{4,8},{8,4},{12,0},{1,13},{5,9},{9,5},{13,1},{2,14},{6,10},... | collective-permute-start | bytes 245768 | tf_op jit(solution)/shard_map/ppermute | solution.py:480

commit v24 on v21

--- a/solution.py
+++ b/solution.py
@@ -15,7 +15,7 @@
 QUAD = 4
 WIDE = QUAD * HEAD_DIM
 TILE = 128
-CHUNKS = ((0, 80), (80, 256))
+CHUNKS = ((0, 96), (96, 256))
 MIB = 1 << 20
 
 
@@ -370,8 +370,8 @@
 
 def plan_kernel(owners, masks):
     s = lax.axis_index("shard")
-    count = owners.shape[0]
-    names = [owners[t, 0] for t in range(count)]
+    count = owners.shape[1]
+    names = [owners[0, t] for t in range(count)]
     for t in range(count):
         same = [(names[e] == names[t]).astype(jnp.int32) for e in range(t)]
         rank = sum(same, jnp.int32(0))
@@ -384,7 +384,7 @@
 def run_plan(owners, shards):
     return pl.pallas_call(
         plan_kernel,
-        out_shape=jax.ShapeDtypeStruct((shards, CAP, owners.shape[0], 8, 128), jnp.float32),
+        out_shape=jax.ShapeDtypeStruct((shards, CAP, owners.shape[1], 8, 128), jnp.float32),
         in_specs=[whole(pltpu.SMEM)],
         out_specs=whole(pltpu.VMEM),
         compiler_params=params(4),
@@ -502,8 +502,7 @@
     flat = grid_features.reshape(count * rows, half)
     half_unit = run_pick(mesh_nodes)
     far = crossed(half_unit, 2, shards)
-    waiting, _ = lax.optimization_barrier((mesh_nodes, half_unit))
-    near = crossed(waiting, 1, shards)
+    near = crossed(mesh_nodes, 1, shards)
     waiting, _ = lax.optimization_barrier((flat, half_unit))
     other = swapped(waiting, "head")
     flat, gain, wq, wup, wdn, mesh, rest = run_stage(
@@ -543,7 +542,7 @@
         swaps.append(received)
         keeps.append(keep)
     named, _ = lax.optimization_barrier((owners, keep))
-    masks = run_plan(named, shards)
+    masks = run_plan(named.T, shards)
     for c in every:
         received = swaps[c]
         if c > 0:

time: 45.7 us -> 45.7 us (level)
  starting transfers between devices: 18 us -> 21 us
  waiting for transfers between devices: 11.8 us -> 8.96 us
    ppermute x9, waiting for transfers between devices: 7.66 us -> 4.59 us  [crossed(): return lax.ppermute(x, 'shard', [(i, i ^ distance) for i in range(size)])]
    ppermute x9, starting transfers between devices: 13.8 us -> 15.5 us  [crossed(): return lax.ppermute(x, 'shard', [(i, i ^ distance) for i in range(size)])]
    ppermute x6, starting transfers between devices: 4.21 us -> 5.49 us  [swapped(): return lax.ppermute(x, axis, [(0, 1), (1, 0)])]
  transfers between devices with their start and end apart: 15 -> 15, of which waited for: 10 -> 7; matrix products, arithmetic and copies ran while one was open for 0% -> 0% of each run, Pallas kernels for 24% -> 26%
where the time goes in v24:
time: 45.7 us; the launch traced here: 45.5 us
  starting transfers between devices  21 us (46%)
  Pallas kernels  15.3 us (33%)
  waiting for transfers between devices  8.96 us (20%)
    ppermute x9, starting transfers between devices, crossed(): return lax.ppermute(x, 'shard', [(i, i ^ distance) for i in range(size)])  15.5 us
    ppermute x6, starting transfers between devices, swapped(): return lax.ppermute(x, axis, [(0, 1), (1, 0)])  5.49 us
    ppermute x9, waiting for transfers between devices, crossed(): return lax.ppermute(x, 'shard', [(i, i ^ distance) for i in range(size)])  4.59 us
    ppermute x6, waiting for transfers between devices, swapped(): return lax.ppermute(x, axis, [(0, 1), (1, 0)])  4.37 us
    pallas_call x1, Pallas kernels, run_stage(): pl.pallas_call(functools.partial(stage_kernel, axes), out_shape=tuple((ja...  4.1 us
    pallas_call x1, Pallas kernels, run_mlp(): pl.pallas_call(mlp_kernel, out_shape=(jax.ShapeDtypeStruct((rows, wq.shap...  3.34 us
    pallas_call x1, Pallas kernels, run_attend(): pl.pallas_call(attend_kernel, out_shape=(part, part, jax.ShapeDtypeStruct...  2.51 us
    pallas_call x2, Pallas kernels, run_place(): pl.pallas_call(functools.partial(place_kernel, spots), out_shape=jax.Shap...  1.56 us
  transfers between devices with their start and end apart: 15, of which 7 were waited for; matrix products, arithmetic and copies ran while one was open for 0% of the time, Pallas kernels for 26%

profile of v24, /device:TPU:0, one launch (start us, length us, event | category | flops | bytes accessed | tf_op | source)
XLA Modules:
  0.0 45.5 jit_solution(7265970916626850221)
XLA Ops:
  0.0 3.0 %collective-permute-start.3 = (bf16[128,1024]{1,0:T(8,128)(2,1)}, bf16[128,1024]{1,0:T(8,128)(2,1)S(1)}, u32[]{:S(2)}, u32[]{:S(2)}) collective-permute-start(bf16[128,1024]{1,0:T(8,128)(2,1)} %mesh.1), channel_id=1, source_target_pairs={{0,4},{4,0},{8,12},{12,8},{1,5},{5,1},{9,13},{13,9},{2,6},{6,2},{1... | collective-permute-start | bytes 786440 | tf_op jit(solution)/shard_map/ppermute | solution.py:480
  3.0 0.9 %pick.1 = bf16[64,1024]{1,0:T(8,128)(2,1)S(1)} custom-call(bf16[128,1024]{1,0:T(8,128)(2,1)} %mesh.1), custom_call_target="tpu_custom_call" | custom-call | bytes 524288 | tf_op jit(solution)/shard_map/pick/pallas_call | solution.py:113
  4.0 2.7 %collective-permute-start.1 = (bf16[64,1024]{1,0:T(8,128)(2,1)S(1)}, bf16[64,1024]{1,0:T(8,128)(2,1)S(1)}, u32[]{:S(2)}, u32[]{:S(2)}) collective-permute-start(bf16[64,1024]{1,0:T(8,128)(2,1)S(1)} %pick.1), channel_id=1, source_target_pairs={{0,8},{4,12},{8,0},{12,4},{1,9},{5,13},{9,1},{13,5},{2,10},{6,14},... | collective-permute-start | bytes 393224 | tf_op jit(solution)/shard_map/ppermute | solution.py:480
  6.6 1.5 %collective-permute-start = (bf16[256,512]{1,0:T(8,128)(2,1)}, bf16[256,512]{1,0:T(8,128)(2,1)S(1)}, u32[]{:S(2)}, u32[]{:S(2)}) collective-permute-start(bf16[256,512]{1,0:T(8,128)(2,1)} %bitcast.9), channel_id=1, source_target_pairs={{0,2},{2,0},{1,3},{3,1},{4,6},{6,4},{5,7},{7,5},{8,10},{10,8},{9,1... | collective-permute-start | bytes 786440 | tf_op jit(solution)/shard_map/ppermute | solution.py:484
  8.1 4.1 %stage.1 = (bf16[256,512]{1,0:T(8,128)(2,1)S(1)}, f32[1,1024]{1,0:T(1,128)S(1)}, bf16[1024,512]{1,0:T(8,128)(2,1)S(1)}, bf16[1024,2048]{1,0:T(8,128)(2,1)S(1)}, ...) custom-call(bf16[256,512]{1,0:T(8,128)(2,1)} %bitcast.10, ...), custom_call_target="tpu_custom_call" | custom-call | flops 20451328000 | bytes 204513280 | tf_op jit(solution)/shard_map/stage/pallas_call | solution.py:163
  12.2 0.3 collective-permute-start.5
  12.5 0.0 collective-permute-done.1.refs_2_
  12.5 1.4 %collective-permute-start.2 = (bf16[64,1024]{1,0:T(8,128)(2,1)S(1)}, bf16[64,1024]{1,0:T(8,128)(2,1)S(1)}, u32[]{:S(2)}, u32[]{:S(2)}) collective-permute-start(bf16[64,1024]{1,0:T(8,128)(2,1)S(1)} %collective-permute-done.1.refs_2_), channel_id=1, source_target_pairs={{0,2},{2,0},{1,3},{3,1},{4,6},{6,4},{5,7},{7,5},{8,10},{10,8},{9,1... | collective-permute-start | bytes 393224 | tf_op jit(solution)/shard_map/ppermute | solution.py:484
  13.9 2.7 %collective-permute-start.4 = (bf16[64,1024]{1,0:T(8,128)(2,1)S(1)}, bf16[64,1024]{1,0:T(8,128)(2,1)S(1)}, u32[]{:S(2)}, u32[]{:S(2)}) collective-permute-start(bf16[64,1024]{1,0:T(8,128)(2,1)S(1)} %collective-permute-done.1.refs_2_), channel_id=1, source_target_pairs={{0,4},{4,0},{8,12},{12,8},{1,5},{5,1},{9,13},{13,9},{2,6},{6,2},{1... | collective-permute-start | bytes 393224 | tf_op jit(solution)/shard_map/ppermute | solution.py:480
  16.7 0.0 collective-permute-done.other
  16.7 0.0 copy-start
  16.7 0.0 copy-start.1
  16.7 3.3 %mlp.1 = (bf16[256,512]{1,0:T(8,128)(2,1)S(1)}, f32[256,1024]{1,0:T(8,128)S(1)}) custom-call(bf16[256,512]{1,0:T(8,128)(2,1)S(1)} %get-tuple-element.34.own, bf16[256,512]{1,0:T(8,128)(2,1)S(1)} %collective-permute-done.other, f32[1,1024]{1,0:T(1,128)S(1)} %get-tuple-element.36.gain, bf16[1024,512]{1,0:T(8,128)(2,1)S(1)} %get-tuple-element.37.wq, ...), custom_call_target="tpu_custom_call" | custom-call | flops 2415919104 | bytes 9437184 | tf_op jit(solution)/shard_map/mlp/pallas_call | solution.py:86
  20.1 0.0 collective-permute-done.2.refs_3_
  20.1 0.0 collective-permute-done.3.refs_1_
  20.1 0.0 copy-done
  20.1 0.0 copy-done.1
  20.1 1.0 %project.3 = bf16[384,1024]{1,0:T(8,128)(2,1)S(1)} custom-call(bf16[128,1024]{1,0:T(8,128)(2,1)S(1)} %get-tuple-element.45.refs_0_, bf16[128,1024]{1,0:T(8,128)(2,1)S(1)} %collective-permute-done.3.refs_1_, bf16[64,1024]{1,0:T(8,128)(2,1)S(1)} %collective-permute-done.1.refs_2_, bf16[64,1024]{1,0:T(8,128)(2,1)S(1)} %collective-permute-done.2.refs_3_, ...), custom_call_target="tpu_custom_call" | custom-call | flops 60397977600 | bytes 275251200 | tf_op jit(solution)/shard_map/project/pallas_call | solution.py:191
  21.1 0.0 copy-start.2
  21.1 0.0 copy-start.4
  21.1 0.1 collective-permute-start.7
  21.2 0.0 collective-permute-done.5.refs_1_
  21.2 0.2 collective-permute-done.4.refs_0_
  21.4 0.4 project.2
  21.8 0.3 collective-permute-start.6
  22.2 1.3 %collective-permute-done.7 = bf16[384,1024]{1,0:T(8,128)(2,1)S(1)} collective-permute-done((bf16[384,1024]{1,0:T(8,128)(2,1)S(1)}, bf16[384,1024]{1,0:T(8,128)(2,1)S(1)}, u32[]{:S(2)}, u32[]{:S(2)}) %collective-permute-start.7) | collective-permute-done | bytes 786464 | tf_op jit(solution)/shard_map/ppermute | solution.py:484
  23.5 0.1 table.1.table_in
  23.6 0.3 collective-permute-done.6
  23.8 0.0 copy-done.2
  23.8 0.0 copy-done.4
  23.8 2.5 %attend.1 = (bf16[4,96,128]{2,1,0:T(8,128)(2,1)S(1)}, bf16[4,96,128]{2,1,0:T(8,128)(2,1)S(1)}, bf16[256,512]{1,0:T(8,128)(2,1)S(1)}, bf16[2,8,64,1024]{3,2,1,0:T(8,128)(2,1)S(1)}) custom-call(s32[4,8]{1,0:T(4,128)S(1)} %copy-done.4, bf16[256,512]{1,0:T(8,128)(2,1)S(1)} %get-tuple-element.44.q, ...), custom_call_target="tpu_custom_call", output_to_operand_aliasing={{3}: (4, {})} | custom-call | flops 13421772800 | bytes 41943040 | tf_op jit(solution)/shard_map/attend/pallas_call | solution.py:325
  26.4 0.6 %collective-permute-start.9 = (bf16[4,96,128]{2,1,0:T(8,128)(2,1)S(1)}, bf16[4,96,128]{2,1,0:T(8,128)(2,1)S(1)}, u32[]{:S(2)}, u32[]{:S(2)}) collective-permute-start(bf16[4,96,128]{2,1,0:T(8,128)(2,1)S(1)} %get-tuple-element.54), channel_id=1, source_target_pairs={{0,2},{2,0},{1,3},{3,1},{4,6},{6,4},{5,7},{7,5},{8,10},{10,8},{9,1... | collective-permute-start | bytes 294920 | tf_op jit(solution)/shard_map/ppermute | solution.py:484
  26.9 0.0 copy-start.5
  26.9 0.0 copy-start.3
  26.9 0.4 project_out.1
  27.4 1.6 %collective-permute-start.8 = (bf16[4,160,128]{2,1,0:T(8,128)(2,1)S(1)}, bf16[4,160,128]{2,1,0:T(8,128)(2,1)S(1)}, u32[]{:S(2)}, u32[]{:S(2)}) collective-permute-start(bf16[4,160,128]{2,1,0:T(8,128)(2,1)S(1)} %get-tuple-element.52), channel_id=1, source_target_pairs={{0,2},{2,0},{1,3},{3,1},{4,6},{6,4},{5,7},{7,5},{8,10},{10,8},{9,1... | collective-permute-start | bytes 491528 | tf_op jit(solution)/shard_map/ppermute | solution.py:484
  29.0 0.0 copy-done.5
  29.0 0.6 %plan.1.masks = f32[4,2,4,8,128]{4,3,2,1,0:T(8,128)S(1)} custom-call(s32[1,4]{1,0:T(1,128)S(1)} %bitcast.13), custom_call_target="tpu_custom_call" | custom-call | flops 100000000 | bytes 262144 | tf_op jit(solution)/shard_map/plan/pallas_call | solution.py:385
  29.6 2.5 %collective-permute-done.9.refs_1_.refs_2_ = bf16[4,96,128]{2,1,0:T(8,128)(2,1)S(1)} collective-permute-done((bf16[4,96,128]{2,1,0:T(8,128)(2,1)S(1)}, bf16[4,96,128]{2,1,0:T(8,128)(2,1)S(1)}, u32[]{:S(2)}, u32[]{:S(2)}) %collective-permute-start.9) | collective-permute-done | bytes 98336 | tf_op jit(solution)/shard_map/ppermute | solution.py:484
  32.1 0.0 copy-done.3
  32.1 0.1 combine.3
  32.1 0.3 collective-permute-start.13
  32.4 2.0 %collective-permute-start.14 = (bf16[2,96,128]{2,1,0:T(8,128)(2,1)S(1)}, bf16[2,96,128]{2,1,0:T(8,128)(2,1)S(1)}, u32[]{:S(2)}, u32[]{:S(2)}) collective-permute-start(bf16[2,96,128]{2,1,0:T(8,128)(2,1)S(1)} %get-tuple-element.61), channel_id=1, source_target_pairs={{0,12},{4,8},{8,4},{12,0},{1,13},{5,9},{9,5},{13,1},{2,14},{6,10},... | collective-permute-start | bytes 147464 | tf_op jit(solution)/shard_map/ppermute | solution.py:480
  34.4 0.3 collective-permute-done.8.refs_1_.refs_3_
  34.8 0.1 combine.4
  34.9 1.7 %collective-permute-start.10 = (bf16[2,160,128]{2,1,0:T(8,128)(2,1)S(1)}, bf16[2,160,128]{2,1,0:T(8,128)(2,1)S(1)}, u32[]{:S(2)}, u32[]{:S(2)}) collective-permute-start(bf16[2,160,128]{2,1,0:T(8,128)(2,1)S(1)} %get-tuple-element.57), channel_id=1, source_target_pairs={{0,8},{4,12},{8,0},{12,4},{1,9},{5,13},{9,1},{13,5},{2,10},{6,14},... | collective-permute-start | bytes 245768 | tf_op jit(solution)/shard_map/ppermute | solution.py:480
  36.5 0.2 combine.5
  36.7 1.2 %collective-permute-start.12 = (bf16[2,256,128]{2,1,0:T(8,128)(2,1)S(1)}, bf16[2,256,128]{2,1,0:T(8,128)(2,1)S(1)}, u32[]{:S(2)}, u32[]{:S(2)}) collective-permute-start(bf16[2,256,128]{2,1,0:T(8,128)(2,1)S(1)} %get-tuple-element.60), channel_id=1, source_target_pairs={{0,4},{4,0},{8,12},{12,8},{1,5},{5,1},{9,13},{13,9},{2,6},{6,2},{1... | collective-permute-start | bytes 393224 | tf_op jit(solution)/shard_map/ppermute | solution.py:480
  37.9 1.7 %collective-permute-start.11 = (bf16[2,160,128]{2,1,0:T(8,128)(2,1)S(1)}, bf16[2,160,128]{2,1,0:T(8,128)(2,1)S(1)}, u32[]{:S(2)}, u32[]{:S(2)}) collective-permute-start(bf16[2,160,128]{2,1,0:T(8,128)(2,1)S(1)} %get-tuple-element.58), channel_id=1, source_target_pairs={{0,12},{4,8},{8,4},{12,0},{1,13},{5,9},{9,5},{13,1},{2,14},{6,10},... | collective-permute-start | bytes 245768 | tf_op jit(solution)/shard_map/ppermute | solution.py:480
  39.6 0.0 collective-permute-done.13.refs_0_
  39.6 0.0 collective-permute-done.14.refs_1_
  39.6 0.8 %place.2.refs_3_ = bf16[8,64,512]{2,1,0:T(8,128)(2,1)} custom-call(bf16[2,96,128]{2,1,0:T(8,128)(2,1)S(1)} %collective-permute-done.13.refs_0_, bf16[2,96,128]{2,1,0:T(8,128)(2,1)S(1)} %collective-permute-done.14.refs_1_, bf16[2,256,128]{2,1,0:T(8,128)(2,1)S(1)} %get-tuple-element.62.refs_2_), custom_call_target="tpu_custom_call" | custom-call | flops 45875200000 | tf_op jit(solution)/shard_map/place/pallas_call | solution.py:464
  40.3 2.9 %collective-permute-done.10.refs_0_ = bf16[2,160,128]{2,1,0:T(8,128)(2,1)S(1)} collective-permute-done((bf16[2,160,128]{2,1,0:T(8,128)(2,1)S(1)}, bf16[2,160,128]{2,1,0:T(8,128)(2,1)S(1)}, u32[]{:S(2)}, u32[]{:S(2)}) %collective-permute-start.10) | collective-permute-done | bytes 81952 | tf_op jit(solution)/shard_map/ppermute | solution.py:480
  43.3 1.4 %collective-permute-done.11.refs_1_ = bf16[2,160,128]{2,1,0:T(8,128)(2,1)S(1)} collective-permute-done((bf16[2,160,128]{2,1,0:T(8,128)(2,1)S(1)}, bf16[2,160,128]{2,1,0:T(8,128)(2,1)S(1)}, u32[]{:S(2)}, u32[]{:S(2)}) %collective-permute-start.11) | collective-permute-done | bytes 81952 | tf_op jit(solution)/shard_map/ppermute | solution.py:480
  44.7 0.0 collective-permute-done.12.refs_2_
  44.7 0.8 %place.3 = bf16[8,64,512]{2,1,0:T(8,128)(2,1)} custom-call(bf16[2,160,128]{2,1,0:T(8,128)(2,1)S(1)} %collective-permute-done.10.refs_0_, bf16[2,160,128]{2,1,0:T(8,128)(2,1)S(1)} %collective-permute-done.11.refs_1_, bf16[2,256,128]{2,1,0:T(8,128)(2,1)S(1)} %collective-permute-done.12.refs_2_, ...), custom_call_target="tpu_custom_call", output_to_operand_aliasing={{}: (3, {})} | custom-call | flops 58982400000 | tf_op jit(solution)/shard_map/place/pallas_call | solution.py:464
Async XLA Ops:
  0.0 20.1 %collective-permute-start.3 = (bf16[128,1024]{1,0:T(8,128)(2,1)}, bf16[128,1024]{1,0:T(8,128)(2,1)S(1)}, u32[]{:S(2)}, u32[]{:S(2)}) collective-permute-start(bf16[128,1024]{1,0:T(8,128)(2,1)} %mesh.1), channel_id=1, source_target_pairs={{0,4},{4,0},{8,12},{12,8},{1,5},{5,1},{9,13},{13,9},{2,6},{6,2},{1... | collective-permute-start | bytes 786440 | tf_op jit(solution)/shard_map/ppermute | solution.py:480
  4.0 8.5 %collective-permute-start.1 = (bf16[64,1024]{1,0:T(8,128)(2,1)S(1)}, bf16[64,1024]{1,0:T(8,128)(2,1)S(1)}, u32[]{:S(2)}, u32[]{:S(2)}) collective-permute-start(bf16[64,1024]{1,0:T(8,128)(2,1)S(1)} %pick.1), channel_id=1, source_target_pairs={{0,8},{4,12},{8,0},{12,4},{1,9},{5,13},{9,1},{13,5},{2,10},{6,14},... | collective-permute-start | bytes 393224 | tf_op jit(solution)/shard_map/ppermute | solution.py:480
  6.6 10.1 %collective-permute-start = (bf16[256,512]{1,0:T(8,128)(2,1)}, bf16[256,512]{1,0:T(8,128)(2,1)S(1)}, u32[]{:S(2)}, u32[]{:S(2)}) collective-permute-start(bf16[256,512]{1,0:T(8,128)(2,1)} %bitcast.9), channel_id=1, source_target_pairs={{0,2},{2,0},{1,3},{3,1},{4,6},{6,4},{5,7},{7,5},{8,10},{10,8},{9,1... | collective-permute-start | bytes 786440 | tf_op jit(solution)/shard_map/ppermute | solution.py:484
  12.2 9.0 %collective-permute-start.5 = (bf16[64,1024]{1,0:T(8,128)(2,1)S(1)}, bf16[64,1024]{1,0:T(8,128)(2,1)S(1)}, u32[]{:S(2)}, u32[]{:S(2)}) collective-permute-start(bf16[64,1024]{1,0:T(8,128)(2,1)S(1)} %get-tuple-element.42), channel_id=1, source_target_pairs={{0,12},{4,8},{8,4},{12,0},{1,13},{5,9},{9,5},{13,1},{2,14},{6,10},... | collective-permute-start | bytes 393224 | tf_op jit(solution)/shard_map/ppermute | solution.py:480
  12.5 7.5 %collective-permute-start.2 = (bf16[64,1024]{1,0:T(8,128)(2,1)S(1)}, bf16[64,1024]{1,0:T(8,128)(2,1)S(1)}, u32[]{:S(2)}, u32[]{:S(2)}) collective-permute-start(bf16[64,1024]{1,0:T(8,128)(2,1)S(1)} %collective-permute-done.1.refs_2_), channel_id=1, source_target_pairs={{0,2},{2,0},{1,3},{3,1},{4,6},{6,4},{5,7},{7,5},{8,10},{10,8},{9,1... | collective-permute-start | bytes 393224 | tf_op jit(solution)/shard_map/ppermute | solution.py:484
  13.9 7.5 %collective-permute-start.4 = (bf16[64,1024]{1,0:T(8,128)(2,1)S(1)}, bf16[64,1024]{1,0:T(8,128)(2,1)S(1)}, u32[]{:S(2)}, u32[]{:S(2)}) collective-permute-start(bf16[64,1024]{1,0:T(8,128)(2,1)S(1)} %collective-permute-done.1.refs_2_), channel_id=1, source_target_pairs={{0,4},{4,0},{8,12},{12,8},{1,5},{5,1},{9,13},{13,9},{2,6},{6,2},{1... | collective-permute-start | bytes 393224 | tf_op jit(solution)/shard_map/ppermute | solution.py:480
  16.7 3.4 %copy-start = (bf16[1024,512]{1,0:T(8,128)(2,1)S(1)}, bf16[1024,512]{1,0:T(8,128)(2,1)}, u32[]{:S(2)}) copy-start(bf16[1024,512]{1,0:T(8,128)(2,1)} %refs_4_.3) | copy-start | bytes 3145732
  16.7 3.4 %copy-start.1 = (bf16[1024,512]{1,0:T(8,128)(2,1)S(1)}, bf16[1024,512]{1,0:T(8,128)(2,1)}, u32[]{:S(2)}) copy-start(bf16[1024,512]{1,0:T(8,128)(2,1)} %refs_5_.3) | copy-start | bytes 3145732
  21.1 2.8 %copy-start.2 = (bf16[512,1024]{1,0:T(8,128)(2,1)S(1)}, bf16[512,1024]{1,0:T(8,128)(2,1)}, u32[]{:S(2)}) copy-start(bf16[512,1024]{1,0:T(8,128)(2,1)} %wo.3) | copy-start | bytes 3145732
  21.1 2.7 %copy-start.4 = (s32[4,8]{1,0:T(4,128)S(1)}, s32[4,8]{1,0:T(4,128)}, u32[]{:S(2)}) copy-start(s32[4,8]{1,0:T(4,128)} %adjacency.1) | copy-start | bytes 388
  21.1 2.4 %collective-permute-start.7 = (bf16[384,1024]{1,0:T(8,128)(2,1)S(1)}, bf16[384,1024]{1,0:T(8,128)(2,1)S(1)}, u32[]{:S(2)}, u32[]{:S(2)}) collective-permute-start(bf16[384,1024]{1,0:T(8,128)(2,1)S(1)} %project.3), channel_id=1, source_target_pairs={{0,1},{1,0},{2,3},{3,2},{4,5},{5,4},{6,7},{7,6},{8,9},{9,8},{10,11... | collective-permute-start | bytes 2359304 | tf_op jit(solution)/shard_map/ppermute | solution.py:484
  21.8 2.0 %collective-permute-start.6 = (bf16[128,1024]{1,0:T(8,128)(2,1)S(1)}, bf16[128,1024]{1,0:T(8,128)(2,1)S(1)}, u32[]{:S(2)}, u32[]{:S(2)}) collective-permute-start(bf16[128,1024]{1,0:T(8,128)(2,1)S(1)} %project.2), channel_id=1, source_target_pairs={{0,1},{1,0},{2,3},{3,2},{4,5},{5,4},{6,7},{7,6},{8,9},{9,8},{10,11... | collective-permute-start | bytes 786440 | tf_op jit(solution)/shard_map/ppermute | solution.py:484
  26.4 5.7 %collective-permute-start.9 = (bf16[4,96,128]{2,1,0:T(8,128)(2,1)S(1)}, bf16[4,96,128]{2,1,0:T(8,128)(2,1)S(1)}, u32[]{:S(2)}, u32[]{:S(2)}) collective-permute-start(bf16[4,96,128]{2,1,0:T(8,128)(2,1)S(1)} %get-tuple-element.54), channel_id=1, source_target_pairs={{0,2},{2,0},{1,3},{3,1},{4,6},{6,4},{5,7},{7,5},{8,10},{10,8},{9,1... | collective-permute-start | bytes 294920 | tf_op jit(solution)/shard_map/ppermute | solution.py:484
  26.9 2.0 %copy-start.5 = (s32[4,1]{0,1:T(1,128)S(1)}, s32[4,1]{0,1:T(1,128)}, u32[]{:S(2)}) copy-start(s32[4,1]{0,1:T(1,128)} %param.12) | copy-start | bytes 52
  26.9 5.1 %copy-start.3 = (bf16[4,64,512]{2,1,0:T(8,128)(2,1)S(1)}, bf16[4,64,512]{2,1,0:T(8,128)(2,1)}, u32[]{:S(2)}) copy-start(bf16[4,64,512]{2,1,0:T(8,128)(2,1)} %grid_features.5) | copy-start | bytes 786436
  27.4 7.4 %collective-permute-start.8 = (bf16[4,160,128]{2,1,0:T(8,128)(2,1)S(1)}, bf16[4,160,128]{2,1,0:T(8,128)(2,1)S(1)}, u32[]{:S(2)}, u32[]{:S(2)}) collective-permute-start(bf16[4,160,128]{2,1,0:T(8,128)(2,1)S(1)} %get-tuple-element.52), channel_id=1, source_target_pairs={{0,2},{2,0},{1,3},{3,1},{4,6},{6,4},{5,7},{7,5},{8,10},{10,8},{9,1... | collective-permute-start | bytes 491528 | tf_op jit(solution)/shard_map/ppermute | solution.py:484
  32.1 7.4 %collective-permute-start.13 = (bf16[2,96,128]{2,1,0:T(8,128)(2,1)S(1)}, bf16[2,96,128]{2,1,0:T(8,128)(2,1)S(1)}, u32[]{:S(2)}, u32[]{:S(2)}) collective-permute-start(bf16[2,96,128]{2,1,0:T(8,128)(2,1)S(1)} %get-tuple-element.55), channel_id=1, source_target_pairs={{0,8},{4,12},{8,0},{12,4},{1,9},{5,13},{9,1},{13,5},{2,10},{6,14},... | collective-permute-start | bytes 147464 | tf_op jit(solution)/shard_map/ppermute | solution.py:480
  32.4 7.2 %collective-permute-start.14 = (bf16[2,96,128]{2,1,0:T(8,128)(2,1)S(1)}, bf16[2,96,128]{2,1,0:T(8,128)(2,1)S(1)}, u32[]{:S(2)}, u32[]{:S(2)}) collective-permute-start(bf16[2,96,128]{2,1,0:T(8,128)(2,1)S(1)} %get-tuple-element.61), channel_id=1, source_target_pairs={{0,12},{4,8},{8,4},{12,0},{1,13},{5,9},{9,5},{13,1},{2,14},{6,10},... | collective-permute-start | bytes 147464 | tf_op jit(solution)/shard_map/ppermute | solution.py:480
  34.9 8.4 %collective-permute-start.10 = (bf16[2,160,128]{2,1,0:T(8,128)(2,1)S(1)}, bf16[2,160,128]{2,1,0:T(8,128)(2,1)S(1)}, u32[]{:S(2)}, u32[]{:S(2)}) collective-permute-start(bf16[2,160,128]{2,1,0:T(8,128)(2,1)S(1)} %get-tuple-element.57), channel_id=1, source_target_pairs={{0,8},{4,12},{8,0},{12,4},{1,9},{5,13},{9,1},{13,5},{2,10},{6,14},... | collective-permute-start | bytes 245768 | tf_op jit(solution)/shard_map/ppermute | solution.py:480
  36.7 8.0 %collective-permute-start.12 = (bf16[2,256,128]{2,1,0:T(8,128)(2,1)S(1)}, bf16[2,256,128]{2,1,0:T(8,128)(2,1)S(1)}, u32[]{:S(2)}, u32[]{:S(2)}) collective-permute-start(bf16[2,256,128]{2,1,0:T(8,128)(2,1)S(1)} %get-tuple-element.60), channel_id=1, source_target_pairs={{0,4},{4,0},{8,12},{12,8},{1,5},{5,1},{9,13},{13,9},{2,6},{6,2},{1... | collective-permute-start | bytes 393224 | tf_op jit(solution)/shard_map/ppermute | solution.py:480
  37.9 6.8 %collective-permute-start.11 = (bf16[2,160,128]{2,1,0:T(8,128)(2,1)S(1)}, bf16[2,160,128]{2,1,0:T(8,128)(2,1)S(1)}, u32[]{:S(2)}, u32[]{:S(2)}) collective-permute-start(bf16[2,160,128]{2,1,0:T(8,128)(2,1)S(1)} %get-tuple-element.58), channel_id=1, source_target_pairs={{0,12},{4,8},{8,4},{12,0},{1,13},{5,9},{9,5},{13,1},{2,14},{6,10},... | collective-permute-start | bytes 245768 | tf_op jit(solution)/shard_map/ppermute | solution.py:480

commit v25 on v24

--- a/solution.py
+++ b/solution.py
@@ -50,10 +50,20 @@
     return pltpu.CompilerParams(vmem_limit_bytes=mib * MIB)
 
 
-def mlp_kernel(own, other, gain, wq, wup, wdn, q_out, mlp_out, normed_s):
+def add_units(normed, wup, wdn, out, span, fresh):
+    chunk = 512
+    for start in range(span.start, span.stop, chunk):
+        units = slice(start, start + chunk)
+        hidden = gelu(dot(normed, wup[:, units])).astype(jnp.bfloat16)
+        term = dot(hidden, wdn[units, :])
+        if fresh and start == span.start:
+            out[...] = term
+        else:
+            out[...] += term
+
+
+def mlp_kernel(split, own, other, gain, wq, wup, wdn, q_out, normed_out, sum_out):
     half = own.shape[1]
-    units = wup.shape[1]
-    chunk = units // 4
     x_other = other[...].astype(jnp.float32)
     x_own = own[...].astype(jnp.float32)
 
@@ -65,41 +75,56 @@
     x_other = x_other - average
     x_own = x_own - average
     factor = lax.rsqrt(mean(x_other * x_other, x_own * x_own) + epsilon)
-    normed_s[:, :half] = (x_other * factor * gain[:, :half]).astype(jnp.bfloat16)
-    normed_s[:, half:] = (x_own * factor * gain[:, half:]).astype(jnp.bfloat16)
-    normed = normed_s[...]
+    normed_out[:, :half] = (x_other * factor * gain[:, :half]).astype(jnp.bfloat16)
+    normed_out[:, half:] = (x_own * factor * gain[:, half:]).astype(jnp.bfloat16)
+    normed = normed_out[...]
     q_out[...] = dot(normed, wq[...]).astype(jnp.bfloat16)
-    for c in range(units // chunk):
-        span = slice(c * chunk, (c + 1) * chunk)
-        hidden = gelu(dot(normed, wup[:, span])).astype(jnp.bfloat16)
-        term = dot(hidden, wdn[span, :])
-        if c == 0:
-            mlp_out[...] = term
-        else:
-            mlp_out[...] += term
-
-
-def run_mlp(own, other, gain, wq, wup, wdn):
+    add_units(normed, wup, wdn, sum_out, slice(0, split), True)
+
+
+def mlp_rest_kernel(split, normed, wup, wdn, sum_in, sum_out):
+    sum_out[...] = sum_in[...]
+    add_units(normed[...], wup, wdn, sum_out, slice(split, wup.shape[1]), False)
+
+
+def run_mlp(split, own, other, gain, wq, wup, wdn):
     rows = own.shape[0]
     width = wq.shape[0]
-    units = wup.shape[1]
-    return pl.pallas_call(
-        mlp_kernel,
+    return pl.pallas_call(
+        functools.partial(mlp_kernel, split),
         out_shape=(
             jax.ShapeDtypeStruct((rows, wq.shape[1]), jnp.bfloat16),
+            jax.ShapeDtypeStruct((rows, width), jnp.bfloat16),
             jax.ShapeDtypeStruct((rows, width), jnp.float32),
         ),
         in_specs=vmem(6),
-        out_specs=tuple(vmem(2)),
-        scratch_shapes=[pltpu.VMEM((rows, width), jnp.bfloat16)],
+        out_specs=tuple(vmem(3)),
         compiler_params=params(16),
         cost_estimate=pl.CostEstimate(
-            flops=2 * rows * width * (wq.shape[1] + 2 * units),
-            bytes_accessed=2 * width * (wq.shape[1] + 2 * units),
-            transcendentals=rows * units,
+            flops=2 * rows * width * (wq.shape[1] + 4 * split),
+            bytes_accessed=2 * width * (wq.shape[1] + 4 * split),
+            transcendentals=2 * rows * split,
         ),
         name="mlp",
     )(own, other, gain, wq, wup, wdn)
+
+
+def run_mlp_rest(split, normed, wup, wdn, total):
+    rows, width = normed.shape
+    units = wup.shape[1] - split
+    return pl.pallas_call(
+        functools.partial(mlp_rest_kernel, split),
+        out_shape=jax.ShapeDtypeStruct((rows, width), jnp.float32),
+        in_specs=vmem(4),
+        out_specs=whole(pltpu.VMEM),
+        compiler_params=params(16),
+        cost_estimate=pl.CostEstimate(
+            flops=4 * rows * width * units,
+            bytes_accessed=4 * width * units,
+            transcendentals=rows * units,
+        ),
+        name="mlp_rest",
+    )(normed, wup, wdn, total)
 
 
 def pick_kernel(mesh, out, sem):
@@ -521,7 +546,8 @@
     far, _ = lax.optimization_barrier((far, rest))
     farther = crossed(far, 1, shards)
     far_pair = swapped(far, "head")
-    queries, mlp = run_mlp(flat, other, gain, wq, wup, wdn)
+    split = up_weight.shape[1] // 2
+    queries, normed, mlp = run_mlp(split, flat, other, gain, wq, wup, wdn)
     queries, mlp, far_pair, near = lax.optimization_barrier((queries, mlp, far_pair, near))
     blocked = (-1, BLOCK, 2 * half)
     mine_a = run_project((mesh, near, far, far_pair), key_weight, value_weight)
@@ -529,6 +555,8 @@
     table = run_table(mine_a.reshape(blocked), sibling_a.reshape(blocked), 2 * shards)
     mine_b = run_project((farther, straight), key_weight, value_weight)
     sibling_b = swapped(mine_b, "sub")
+    normed, _ = lax.optimization_barrier((normed, mine_b))
+    mlp = run_mlp_rest(split, normed, wup, wdn, mlp)
     send, keep, att = run_attend(
         adjacency, queries, mine_b.reshape(blocked), sibling_b.reshape(blocked), table, mlp, output_weight
     )

time: 45.7 us -> 46 us (level)
    ppermute x6, waiting for transfers between devices: 4.37 us -> 2.72 us  [swapped(): return lax.ppermute(x, axis, [(0, 1), (1, 0)])]
    ppermute x9, waiting for transfers between devices: 4.59 us -> 6.1 us  [crossed(): return lax.ppermute(x, 'shard', [(i, i ^ distance) for i in range(size)])]
    ppermute x9, starting transfers between devices: 15.5 us -> 16 us  [crossed(): return lax.ppermute(x, 'shard', [(i, i ^ distance) for i in range(size)])]
    pallas_call x1 -> x2, Pallas kernels: 3.34 us -> 3.56 us  [the longest x1 2.05 us: run_mlp(): pl.pallas_call(functools.partial(mlp_kernel, split), out_shape=(jax.Shape...]
  transfers between devices with their start and end apart: 15 -> 15, of which waited for: 7 -> 6; matrix products, arithmetic and copies ran while one was open for 0% -> 0% of each run, Pallas kernels for 26% -> 27%
where the time goes in v25:
time: 46 us; the launch traced here: 45.9 us
  starting transfers between devices  21.2 us (46%)
  Pallas kernels  15.6 us (34%)
  waiting for transfers between devices  8.82 us (19%)
    ppermute x9, starting transfers between devices, crossed(): return lax.ppermute(x, 'shard', [(i, i ^ distance) for i in range(size)])  16 us
    ppermute x9, waiting for transfers between devices, crossed(): return lax.ppermute(x, 'shard', [(i, i ^ distance) for i in range(size)])  6.1 us
    ppermute x6, starting transfers between devices, swapped(): return lax.ppermute(x, axis, [(0, 1), (1, 0)])  5.21 us
    pallas_call x1, Pallas kernels, run_stage(): pl.pallas_call(functools.partial(stage_kernel, axes), out_shape=tuple((ja...  4.1 us
    ppermute x6, waiting for transfers between devices, swapped(): return lax.ppermute(x, axis, [(0, 1), (1, 0)])  2.72 us
    pallas_call x1, Pallas kernels, run_attend(): pl.pallas_call(attend_kernel, out_shape=(part, part, jax.ShapeDtypeStruct...  2.51 us
    pallas_call x1, Pallas kernels, run_mlp(): pl.pallas_call(functools.partial(mlp_kernel, split), out_shape=(jax.Shape...  2.05 us
    pallas_call x2, Pallas kernels, run_place(): pl.pallas_call(functools.partial(place_kernel, spots), out_shape=jax.Shap...  1.56 us
  transfers between devices with their start and end apart: 15, of which 6 were waited for; matrix products, arithmetic and copies ran while one was open for 0% of the time, Pallas kernels for 27%

profile of v25, /device:TPU:0, one launch (start us, length us, event | category | flops | bytes accessed | tf_op | source)
XLA Modules:
  0.0 45.9 jit_solution(10559530244624363037)
XLA Ops:
  0.0 3.0 %collective-permute-start.3 = (bf16[128,1024]{1,0:T(8,128)(2,1)}, bf16[128,1024]{1,0:T(8,128)(2,1)S(1)}, u32[]{:S(2)}, u32[]{:S(2)}) collective-permute-start(bf16[128,1024]{1,0:T(8,128)(2,1)} %mesh.1), channel_id=1, source_target_pairs={{0,4},{4,0},{8,12},{12,8},{1,5},{5,1},{9,13},{13,9},{2,6},{6,2},{1... | collective-permute-start | bytes 786440 | tf_op jit(solution)/shard_map/ppermute | solution.py:505
  3.0 0.9 %pick.1 = bf16[64,1024]{1,0:T(8,128)(2,1)S(1)} custom-call(bf16[128,1024]{1,0:T(8,128)(2,1)} %mesh.1), custom_call_target="tpu_custom_call" | custom-call | bytes 524288 | tf_op jit(solution)/shard_map/pick/pallas_call | solution.py:138
  4.0 2.7 %collective-permute-start.1 = (bf16[64,1024]{1,0:T(8,128)(2,1)S(1)}, bf16[64,1024]{1,0:T(8,128)(2,1)S(1)}, u32[]{:S(2)}, u32[]{:S(2)}) collective-permute-start(bf16[64,1024]{1,0:T(8,128)(2,1)S(1)} %pick.1), channel_id=1, source_target_pairs={{0,8},{4,12},{8,0},{12,4},{1,9},{5,13},{9,1},{13,5},{2,10},{6,14},... | collective-permute-start | bytes 393224 | tf_op jit(solution)/shard_map/ppermute | solution.py:505
  6.6 1.5 %collective-permute-start = (bf16[256,512]{1,0:T(8,128)(2,1)}, bf16[256,512]{1,0:T(8,128)(2,1)S(1)}, u32[]{:S(2)}, u32[]{:S(2)}) collective-permute-start(bf16[256,512]{1,0:T(8,128)(2,1)} %bitcast.9), channel_id=1, source_target_pairs={{0,2},{2,0},{1,3},{3,1},{4,6},{6,4},{5,7},{7,5},{8,10},{10,8},{9,1... | collective-permute-start | bytes 786440 | tf_op jit(solution)/shard_map/ppermute | solution.py:509
  8.1 4.1 %stage.1 = (bf16[256,512]{1,0:T(8,128)(2,1)S(1)}, f32[1,1024]{1,0:T(1,128)S(1)}, bf16[1024,512]{1,0:T(8,128)(2,1)S(1)}, bf16[1024,2048]{1,0:T(8,128)(2,1)S(1)}, ...) custom-call(bf16[256,512]{1,0:T(8,128)(2,1)} %bitcast.10, ...), custom_call_target="tpu_custom_call" | custom-call | flops 20451328000 | bytes 204513280 | tf_op jit(solution)/shard_map/stage/pallas_call | solution.py:188
  12.2 0.3 collective-permute-start.5
  12.5 0.0 collective-permute-done.1.refs_2_
  12.5 1.4 %collective-permute-start.2 = (bf16[64,1024]{1,0:T(8,128)(2,1)S(1)}, bf16[64,1024]{1,0:T(8,128)(2,1)S(1)}, u32[]{:S(2)}, u32[]{:S(2)}) collective-permute-start(bf16[64,1024]{1,0:T(8,128)(2,1)S(1)} %collective-permute-done.1.refs_2_), channel_id=1, source_target_pairs={{0,2},{2,0},{1,3},{3,1},{4,6},{6,4},{5,7},{7,5},{8,10},{10,8},{9,1... | collective-permute-start | bytes 393224 | tf_op jit(solution)/shard_map/ppermute | solution.py:509
  13.9 2.7 %collective-permute-start.4 = (bf16[64,1024]{1,0:T(8,128)(2,1)S(1)}, bf16[64,1024]{1,0:T(8,128)(2,1)S(1)}, u32[]{:S(2)}, u32[]{:S(2)}) collective-permute-start(bf16[64,1024]{1,0:T(8,128)(2,1)S(1)} %collective-permute-done.1.refs_2_), channel_id=1, source_target_pairs={{0,4},{4,0},{8,12},{12,8},{1,5},{5,1},{9,13},{13,9},{2,6},{6,2},{1... | collective-permute-start | bytes 393224 | tf_op jit(solution)/shard_map/ppermute | solution.py:505
  16.7 0.0 collective-permute-done.other
  16.7 0.0 copy-start
  16.7 0.0 copy-start.1
  16.7 2.1 %mlp.1 = (bf16[256,512]{1,0:T(8,128)(2,1)S(1)}, bf16[256,1024]{1,0:T(8,128)(2,1)S(1)}, f32[256,1024]{1,0:T(8,128)S(1)}) custom-call(bf16[256,512]{1,0:T(8,128)(2,1)S(1)} %get-tuple-element.36.own, bf16[256,512]{1,0:T(8,128)(2,1)S(1)} %collective-permute-done.other, f32[1,1024]{1,0:T(1,128)S(1)} %get-tuple-element.38.gain, ...), custom_call_target="tpu_custom_call" | custom-call | flops 2415919104 | bytes 9437184 | tf_op jit(solution)/shard_map/mlp/pallas_call | solution.py:93
  18.8 0.0 collective-permute-done.2.refs_3_
  18.8 0.0 collective-permute-done.3.refs_1_
  18.8 0.0 copy-done
  18.8 0.0 copy-done.1
  18.8 1.0 %project.3 = bf16[384,1024]{1,0:T(8,128)(2,1)S(1)} custom-call(bf16[128,1024]{1,0:T(8,128)(2,1)S(1)} %get-tuple-element.47.refs_0_, bf16[128,1024]{1,0:T(8,128)(2,1)S(1)} %collective-permute-done.3.refs_1_, bf16[64,1024]{1,0:T(8,128)(2,1)S(1)} %collective-permute-done.1.refs_2_, bf16[64,1024]{1,0:T(8,128)(2,1)S(1)} %collective-permute-done.2.refs_3_, ...), custom_call_target="tpu_custom_call" | custom-call | flops 60397977600 | bytes 275251200 | tf_op jit(solution)/shard_map/project/pallas_call | solution.py:216
  19.8 0.1 collective-permute-start.7
  19.9 0.1 collective-permute-done.5.refs_1_
  20.0 1.4 %collective-permute-done.4.refs_0_ = bf16[64,1024]{1,0:T(8,128)(2,1)S(1)} collective-permute-done((bf16[64,1024]{1,0:T(8,128)(2,1)S(1)}, bf16[64,1024]{1,0:T(8,128)(2,1)S(1)}, u32[]{:S(2)}, u32[]{:S(2)}) %collective-permute-start.4) | collective-permute-done | bytes 131104 | tf_op jit(solution)/shard_map/ppermute | solution.py:505
  21.4 0.4 project.2
  21.8 0.1 collective-permute-start.6
  21.9 0.0 copy-start.2
  21.9 0.0 copy-start.4
  21.9 1.5 %mlp_rest.1.mlp = f32[256,1024]{1,0:T(8,128)S(1)} custom-call(bf16[256,1024]{1,0:T(8,128)(2,1)S(1)} %get-tuple-element.51.normed, bf16[1024,2048]{1,0:T(8,128)(2,1)S(1)} %get-tuple-element.40.wup, bf16[2048,1024]{1,0:T(8,128)(2,1)S(1)} %get-tuple-element.41.wdn, f32[256,1024]{1,0:T(8,128)S(1)} %get-tuple-element.52.sum_in), custom_call_target="tpu_custom_call" | custom-call | flops 1073741824 | bytes 4194304 | tf_op jit(solution)/shard_map/mlp_rest/pallas_call | solution.py:115
  23.5 0.0 collective-permute-done.7
  23.5 0.1 table.1.table_in
  23.6 0.0 collective-permute-done.6
  23.6 0.0 copy-done.2
  23.6 0.0 copy-done.4
  23.6 2.5 %attend.1 = (bf16[4,96,128]{2,1,0:T(8,128)(2,1)S(1)}, bf16[4,96,128]{2,1,0:T(8,128)(2,1)S(1)}, bf16[256,512]{1,0:T(8,128)(2,1)S(1)}, bf16[2,8,64,1024]{3,2,1,0:T(8,128)(2,1)S(1)}) custom-call(s32[4,8]{1,0:T(4,128)S(1)} %copy-done.4, bf16[256,512]{1,0:T(8,128)(2,1)S(1)} %get-tuple-element.46.q, ...), custom_call_target="tpu_custom_call", output_to_operand_aliasing={{3}: (4, {})} | custom-call | flops 13421772800 | bytes 41943040 | tf_op jit(solution)/shard_map/attend/pallas_call | solution.py:350
  26.1 0.6 %collective-permute-start.9 = (bf16[4,96,128]{2,1,0:T(8,128)(2,1)S(1)}, bf16[4,96,128]{2,1,0:T(8,128)(2,1)S(1)}, u32[]{:S(2)}, u32[]{:S(2)}) collective-permute-start(bf16[4,96,128]{2,1,0:T(8,128)(2,1)S(1)} %get-tuple-element.58), channel_id=1, source_target_pairs={{0,2},{2,0},{1,3},{3,1},{4,6},{6,4},{5,7},{7,5},{8,10},{10,8},{9,1... | collective-permute-start | bytes 294920 | tf_op jit(solution)/shard_map/ppermute | solution.py:509
  26.7 0.0 copy-start.5
  26.7 0.0 copy-start.3
  26.7 0.4 project_out.1
  27.1 1.6 %collective-permute-start.8 = (bf16[4,160,128]{2,1,0:T(8,128)(2,1)S(1)}, bf16[4,160,128]{2,1,0:T(8,128)(2,1)S(1)}, u32[]{:S(2)}, u32[]{:S(2)}) collective-permute-start(bf16[4,160,128]{2,1,0:T(8,128)(2,1)S(1)} %get-tuple-element.56), channel_id=1, source_target_pairs={{0,2},{2,0},{1,3},{3,1},{4,6},{6,4},{5,7},{7,5},{8,10},{10,8},{9,1... | collective-permute-start | bytes 491528 | tf_op jit(solution)/shard_map/ppermute | solution.py:509
  28.7 0.0 copy-done.5
  28.7 0.6 %plan.1.masks = f32[4,2,4,8,128]{4,3,2,1,0:T(8,128)S(1)} custom-call(s32[1,4]{1,0:T(1,128)S(1)} %bitcast.13), custom_call_target="tpu_custom_call" | custom-call | flops 100000000 | bytes 262144 | tf_op jit(solution)/shard_map/plan/pallas_call | solution.py:410
  29.3 2.5 %collective-permute-done.9.refs_1_.refs_2_ = bf16[4,96,128]{2,1,0:T(8,128)(2,1)S(1)} collective-permute-done((bf16[4,96,128]{2,1,0:T(8,128)(2,1)S(1)}, bf16[4,96,128]{2,1,0:T(8,128)(2,1)S(1)}, u32[]{:S(2)}, u32[]{:S(2)}) %collective-permute-start.9) | collective-permute-done | bytes 98336 | tf_op jit(solution)/shard_map/ppermute | solution.py:509
  31.8 0.0 copy-done.3
  31.8 0.1 combine.3
  31.9 1.0 %collective-permute-start.13 = (bf16[2,96,128]{2,1,0:T(8,128)(2,1)S(1)}, bf16[2,96,128]{2,1,0:T(8,128)(2,1)S(1)}, u32[]{:S(2)}, u32[]{:S(2)}) collective-permute-start(bf16[2,96,128]{2,1,0:T(8,128)(2,1)S(1)} %get-tuple-element.59), channel_id=1, source_target_pairs={{0,8},{4,12},{8,0},{12,4},{1,9},{5,13},{9,1},{13,5},{2,10},{6,14},... | collective-permute-start | bytes 147464 | tf_op jit(solution)/shard_map/ppermute | solution.py:505
  32.9 1.7 %collective-permute-start.14 = (bf16[2,96,128]{2,1,0:T(8,128)(2,1)S(1)}, bf16[2,96,128]{2,1,0:T(8,128)(2,1)S(1)}, u32[]{:S(2)}, u32[]{:S(2)}) collective-permute-start(bf16[2,96,128]{2,1,0:T(8,128)(2,1)S(1)} %get-tuple-element.65), channel_id=1, source_target_pairs={{0,12},{4,8},{8,4},{12,0},{1,13},{5,9},{9,5},{13,1},{2,14},{6,10},... | collective-permute-start | bytes 147464 | tf_op jit(solution)/shard_map/ppermute | solution.py:505
  34.6 0.3 collective-permute-done.8.refs_1_.refs_3_
  34.9 0.1 combine.4
  35.0 1.0 %collective-permute-start.10 = (bf16[2,160,128]{2,1,0:T(8,128)(2,1)S(1)}, bf16[2,160,128]{2,1,0:T(8,128)(2,1)S(1)}, u32[]{:S(2)}, u32[]{:S(2)}) collective-permute-start(bf16[2,160,128]{2,1,0:T(8,128)(2,1)S(1)} %get-tuple-element.61), channel_id=1, source_target_pairs={{0,8},{4,12},{8,0},{12,4},{1,9},{5,13},{9,1},{13,5},{2,10},{6,14},... | collective-permute-start | bytes 245768 | tf_op jit(solution)/shard_map/ppermute | solution.py:505
  36.0 0.2 combine.5
  36.2 1.5 %collective-permute-start.12 = (bf16[2,256,128]{2,1,0:T(8,128)(2,1)S(1)}, bf16[2,256,128]{2,1,0:T(8,128)(2,1)S(1)}, u32[]{:S(2)}, u32[]{:S(2)}) collective-permute-start(bf16[2,256,128]{2,1,0:T(8,128)(2,1)S(1)} %get-tuple-element.64), channel_id=1, source_target_pairs={{0,4},{4,0},{8,12},{12,8},{1,5},{5,1},{9,13},{13,9},{2,6},{6,2},{1... | collective-permute-start | bytes 393224 | tf_op jit(solution)/shard_map/ppermute | solution.py:505
  37.7 2.0 %collective-permute-start.11 = (bf16[2,160,128]{2,1,0:T(8,128)(2,1)S(1)}, bf16[2,160,128]{2,1,0:T(8,128)(2,1)S(1)}, u32[]{:S(2)}, u32[]{:S(2)}) collective-permute-start(bf16[2,160,128]{2,1,0:T(8,128)(2,1)S(1)} %get-tuple-element.62), channel_id=1, source_target_pairs={{0,12},{4,8},{8,4},{12,0},{1,13},{5,9},{9,5},{13,1},{2,14},{6,10},... | collective-permute-start | bytes 245768 | tf_op jit(solution)/shard_map/ppermute | solution.py:505
  39.7 0.0 collective-permute-done.13.refs_0_
  39.7 0.0 collective-permute-done.14.refs_1_
  39.7 0.8 %place.2.refs_3_ = bf16[8,64,512]{2,1,0:T(8,128)(2,1)} custom-call(bf16[2,96,128]{2,1,0:T(8,128)(2,1)S(1)} %collective-permute-done.13.refs_0_, bf16[2,96,128]{2,1,0:T(8,128)(2,1)S(1)} %collective-permute-done.14.refs_1_, bf16[2,256,128]{2,1,0:T(8,128)(2,1)S(1)} %get-tuple-element.66.refs_2_), custom_call_target="tpu_custom_call" | custom-call | flops 45875200000 | tf_op jit(solution)/shard_map/place/pallas_call | solution.py:489
  40.5 2.3 %collective-permute-done.10.refs_0_ = bf16[2,160,128]{2,1,0:T(8,128)(2,1)S(1)} collective-permute-done((bf16[2,160,128]{2,1,0:T(8,128)(2,1)S(1)}, bf16[2,160,128]{2,1,0:T(8,128)(2,1)S(1)}, u32[]{:S(2)}, u32[]{:S(2)}) %collective-permute-start.10) | collective-permute-done | bytes 81952 | tf_op jit(solution)/shard_map/ppermute | solution.py:505
  42.7 2.3 %collective-permute-done.11.refs_1_ = bf16[2,160,128]{2,1,0:T(8,128)(2,1)S(1)} collective-permute-done((bf16[2,160,128]{2,1,0:T(8,128)(2,1)S(1)}, bf16[2,160,128]{2,1,0:T(8,128)(2,1)S(1)}, u32[]{:S(2)}, u32[]{:S(2)}) %collective-permute-start.11) | collective-permute-done | bytes 81952 | tf_op jit(solution)/shard_map/ppermute | solution.py:505
  45.1 0.0 collective-permute-done.12.refs_2_
  45.1 0.8 %place.3 = bf16[8,64,512]{2,1,0:T(8,128)(2,1)} custom-call(bf16[2,160,128]{2,1,0:T(8,128)(2,1)S(1)} %collective-permute-done.10.refs_0_, bf16[2,160,128]{2,1,0:T(8,128)(2,1)S(1)} %collective-permute-done.11.refs_1_, bf16[2,256,128]{2,1,0:T(8,128)(2,1)S(1)} %collective-permute-done.12.refs_2_, ...), custom_call_target="tpu_custom_call", output_to_operand_aliasing={{}: (3, {})} | custom-call | flops 58982400000 | tf_op jit(solution)/shard_map/place/pallas_call | solution.py:489
Async XLA Ops:
  0.0 18.8 %collective-permute-start.3 = (bf16[128,1024]{1,0:T(8,128)(2,1)}, bf16[128,1024]{1,0:T(8,128)(2,1)S(1)}, u32[]{:S(2)}, u32[]{:S(2)}) collective-permute-start(bf16[128,1024]{1,0:T(8,128)(2,1)} %mesh.1), channel_id=1, source_target_pairs={{0,4},{4,0},{8,12},{12,8},{1,5},{5,1},{9,13},{13,9},{2,6},{6,2},{1... | collective-permute-start | bytes 786440 | tf_op jit(solution)/shard_map/ppermute | solution.py:505
  4.0 8.5 %collective-permute-start.1 = (bf16[64,1024]{1,0:T(8,128)(2,1)S(1)}, bf16[64,1024]{1,0:T(8,128)(2,1)S(1)}, u32[]{:S(2)}, u32[]{:S(2)}) collective-permute-start(bf16[64,1024]{1,0:T(8,128)(2,1)S(1)} %pick.1), channel_id=1, source_target_pairs={{0,8},{4,12},{8,0},{12,4},{1,9},{5,13},{9,1},{13,5},{2,10},{6,14},... | collective-permute-start | bytes 393224 | tf_op jit(solution)/shard_map/ppermute | solution.py:505
  6.6 10.1 %collective-permute-start = (bf16[256,512]{1,0:T(8,128)(2,1)}, bf16[256,512]{1,0:T(8,128)(2,1)S(1)}, u32[]{:S(2)}, u32[]{:S(2)}) collective-permute-start(bf16[256,512]{1,0:T(8,128)(2,1)} %bitcast.9), channel_id=1, source_target_pairs={{0,2},{2,0},{1,3},{3,1},{4,6},{6,4},{5,7},{7,5},{8,10},{10,8},{9,1... | collective-permute-start | bytes 786440 | tf_op jit(solution)/shard_map/ppermute | solution.py:509
  12.2 7.8 %collective-permute-start.5 = (bf16[64,1024]{1,0:T(8,128)(2,1)S(1)}, bf16[64,1024]{1,0:T(8,128)(2,1)S(1)}, u32[]{:S(2)}, u32[]{:S(2)}) collective-permute-start(bf16[64,1024]{1,0:T(8,128)(2,1)S(1)} %get-tuple-element.44), channel_id=1, source_target_pairs={{0,12},{4,8},{8,4},{12,0},{1,13},{5,9},{9,5},{13,1},{2,14},{6,10},... | collective-permute-start | bytes 393224 | tf_op jit(solution)/shard_map/ppermute | solution.py:505
  12.5 6.2 %collective-permute-start.2 = (bf16[64,1024]{1,0:T(8,128)(2,1)S(1)}, bf16[64,1024]{1,0:T(8,128)(2,1)S(1)}, u32[]{:S(2)}, u32[]{:S(2)}) collective-permute-start(bf16[64,1024]{1,0:T(8,128)(2,1)S(1)} %collective-permute-done.1.refs_2_), channel_id=1, source_target_pairs={{0,2},{2,0},{1,3},{3,1},{4,6},{6,4},{5,7},{7,5},{8,10},{10,8},{9,1... | collective-permute-start | bytes 393224 | tf_op jit(solution)/shard_map/ppermute | solution.py:509
  13.9 7.5 %collective-permute-start.4 = (bf16[64,1024]{1,0:T(8,128)(2,1)S(1)}, bf16[64,1024]{1,0:T(8,128)(2,1)S(1)}, u32[]{:S(2)}, u32[]{:S(2)}) collective-permute-start(bf16[64,1024]{1,0:T(8,128)(2,1)S(1)} %collective-permute-done.1.refs_2_), channel_id=1, source_target_pairs={{0,4},{4,0},{8,12},{12,8},{1,5},{5,1},{9,13},{13,9},{2,6},{6,2},{1... | collective-permute-start | bytes 393224 | tf_op jit(solution)/shard_map/ppermute | solution.py:505
  16.7 2.1 %copy-start = (bf16[1024,512]{1,0:T(8,128)(2,1)S(1)}, bf16[1024,512]{1,0:T(8,128)(2,1)}, u32[]{:S(2)}) copy-start(bf16[1024,512]{1,0:T(8,128)(2,1)} %refs_4_.3) | copy-start | bytes 3145732
  16.7 2.1 %copy-start.1 = (bf16[1024,512]{1,0:T(8,128)(2,1)S(1)}, bf16[1024,512]{1,0:T(8,128)(2,1)}, u32[]{:S(2)}) copy-start(bf16[1024,512]{1,0:T(8,128)(2,1)} %refs_5_.3) | copy-start | bytes 3145732
  19.8 3.6 %collective-permute-start.7 = (bf16[384,1024]{1,0:T(8,128)(2,1)S(1)}, bf16[384,1024]{1,0:T(8,128)(2,1)S(1)}, u32[]{:S(2)}, u32[]{:S(2)}) collective-permute-start(bf16[384,1024]{1,0:T(8,128)(2,1)S(1)} %project.3), channel_id=1, source_target_pairs={{0,1},{1,0},{2,3},{3,2},{4,5},{5,4},{6,7},{7,6},{8,9},{9,8},{10,11... | collective-permute-start | bytes 2359304 | tf_op jit(solution)/shard_map/ppermute | solution.py:509
  21.8 1.7 %collective-permute-start.6 = (bf16[128,1024]{1,0:T(8,128)(2,1)S(1)}, bf16[128,1024]{1,0:T(8,128)(2,1)S(1)}, u32[]{:S(2)}, u32[]{:S(2)}) collective-permute-start(bf16[128,1024]{1,0:T(8,128)(2,1)S(1)} %project.2), channel_id=1, source_target_pairs={{0,1},{1,0},{2,3},{3,2},{4,5},{5,4},{6,7},{7,6},{8,9},{9,8},{10,11... | collective-permute-start | bytes 786440 | tf_op jit(solution)/shard_map/ppermute | solution.py:509
  21.9 1.7 %copy-start.2 = (bf16[512,1024]{1,0:T(8,128)(2,1)S(1)}, bf16[512,1024]{1,0:T(8,128)(2,1)}, u32[]{:S(2)}) copy-start(bf16[512,1024]{1,0:T(8,128)(2,1)} %wo.3) | copy-start | bytes 3145732
  21.9 1.7 %copy-start.4 = (s32[4,8]{1,0:T(4,128)S(1)}, s32[4,8]{1,0:T(4,128)}, u32[]{:S(2)}) copy-start(s32[4,8]{1,0:T(4,128)} %adjacency.1) | copy-start | bytes 388
  26.1 5.7 %collective-permute-start.9 = (bf16[4,96,128]{2,1,0:T(8,128)(2,1)S(1)}, bf16[4,96,128]{2,1,0:T(8,128)(2,1)S(1)}, u32[]{:S(2)}, u32[]{:S(2)}) collective-permute-start(bf16[4,96,128]{2,1,0:T(8,128)(2,1)S(1)} %get-tuple-element.58), channel_id=1, source_target_pairs={{0,2},{2,0},{1,3},{3,1},{4,6},{6,4},{5,7},{7,5},{8,10},{10,8},{9,1... | collective-permute-start | bytes 294920 | tf_op jit(solution)/shard_map/ppermute | solution.py:509
  26.7 2.0 %copy-start.5 = (s32[4,1]{0,1:T(1,128)S(1)}, s32[4,1]{0,1:T(1,128)}, u32[]{:S(2)}) copy-start(s32[4,1]{0,1:T(1,128)} %param.12) | copy-start | bytes 52
  26.7 5.1 %copy-start.3 = (bf16[4,64,512]{2,1,0:T(8,128)(2,1)S(1)}, bf16[4,64,512]{2,1,0:T(8,128)(2,1)}, u32[]{:S(2)}) copy-start(bf16[4,64,512]{2,1,0:T(8,128)(2,1)} %grid_features.5) | copy-start | bytes 786436
  27.1 7.7 %collective-permute-start.8 = (bf16[4,160,128]{2,1,0:T(8,128)(2,1)S(1)}, bf16[4,160,128]{2,1,0:T(8,128)(2,1)S(1)}, u32[]{:S(2)}, u32[]{:S(2)}) collective-permute-start(bf16[4,160,128]{2,1,0:T(8,128)(2,1)S(1)} %get-tuple-element.56), channel_id=1, source_target_pairs={{0,2},{2,0},{1,3},{3,1},{4,6},{6,4},{5,7},{7,5},{8,10},{10,8},{9,1... | collective-permute-start | bytes 491528 | tf_op jit(solution)/shard_map/ppermute | solution.py:509
  31.9 7.8 %collective-permute-start.13 = (bf16[2,96,128]{2,1,0:T(8,128)(2,1)S(1)}, bf16[2,96,128]{2,1,0:T(8,128)(2,1)S(1)}, u32[]{:S(2)}, u32[]{:S(2)}) collective-permute-start(bf16[2,96,128]{2,1,0:T(8,128)(2,1)S(1)} %get-tuple-element.59), channel_id=1, source_target_pairs={{0,8},{4,12},{8,0},{12,4},{1,9},{5,13},{9,1},{13,5},{2,10},{6,14},... | collective-permute-start | bytes 147464 | tf_op jit(solution)/shard_map/ppermute | solution.py:505
  32.9 6.8 %collective-permute-start.14 = (bf16[2,96,128]{2,1,0:T(8,128)(2,1)S(1)}, bf16[2,96,128]{2,1,0:T(8,128)(2,1)S(1)}, u32[]{:S(2)}, u32[]{:S(2)}) collective-permute-start(bf16[2,96,128]{2,1,0:T(8,128)(2,1)S(1)} %get-tuple-element.65), channel_id=1, source_target_pairs={{0,12},{4,8},{8,4},{12,0},{1,13},{5,9},{9,5},{13,1},{2,14},{6,10},... | collective-permute-start | bytes 147464 | tf_op jit(solution)/shard_map/ppermute | solution.py:505
  35.0 7.7 %collective-permute-start.10 = (bf16[2,160,128]{2,1,0:T(8,128)(2,1)S(1)}, bf16[2,160,128]{2,1,0:T(8,128)(2,1)S(1)}, u32[]{:S(2)}, u32[]{:S(2)}) collective-permute-start(bf16[2,160,128]{2,1,0:T(8,128)(2,1)S(1)} %get-tuple-element.61), channel_id=1, source_target_pairs={{0,8},{4,12},{8,0},{12,4},{1,9},{5,13},{9,1},{13,5},{2,10},{6,14},... | collective-permute-start | bytes 245768 | tf_op jit(solution)/shard_map/ppermute | solution.py:505
  36.2 8.9 %collective-permute-start.12 = (bf16[2,256,128]{2,1,0:T(8,128)(2,1)S(1)}, bf16[2,256,128]{2,1,0:T(8,128)(2,1)S(1)}, u32[]{:S(2)}, u32[]{:S(2)}) collective-permute-start(bf16[2,256,128]{2,1,0:T(8,128)(2,1)S(1)} %get-tuple-element.64), channel_id=1, source_target_pairs={{0,4},{4,0},{8,12},{12,8},{1,5},{5,1},{9,13},{13,9},{2,6},{6,2},{1... | collective-permute-start | bytes 393224 | tf_op jit(solution)/shard_map/ppermute | solution.py:505
  37.7 7.3 %collective-permute-start.11 = (bf16[2,160,128]{2,1,0:T(8,128)(2,1)S(1)}, bf16[2,160,128]{2,1,0:T(8,128)(2,1)S(1)}, u32[]{:S(2)}, u32[]{:S(2)}) collective-permute-start(bf16[2,160,128]{2,1,0:T(8,128)(2,1)S(1)} %get-tuple-element.62), channel_id=1, source_target_pairs={{0,12},{4,8},{8,4},{12,0},{1,13},{5,9},{9,5},{13,1},{2,14},{6,10},... | collective-permute-start | bytes 245768 | tf_op jit(solution)/shard_map/ppermute | solution.py:505

commit v26 on v20

--- a/solution.py
+++ b/solution.py
@@ -15,7 +15,7 @@
 QUAD = 4
 WIDE = QUAD * HEAD_DIM
 TILE = 128
-CHUNKS = ((0, 96), (96, 256))
+CHUNKS = ((0, 80), (80, 256))
 MIB = 1 << 20
 
 
@@ -370,8 +370,8 @@
 
 def plan_kernel(owners, masks):
     s = lax.axis_index("shard")
-    count = owners.shape[0]
-    names = [owners[t, 0] for t in range(count)]
+    count = owners.shape[1]
+    names = [owners[0, t] for t in range(count)]
     for t in range(count):
         same = [(names[e] == names[t]).astype(jnp.int32) for e in range(t)]
         rank = sum(same, jnp.int32(0))
@@ -384,7 +384,7 @@
 def run_plan(owners, shards):
     return pl.pallas_call(
         plan_kernel,
-        out_shape=jax.ShapeDtypeStruct((shards, CAP, owners.shape[0], 8, 128), jnp.float32),
+        out_shape=jax.ShapeDtypeStruct((shards, CAP, owners.shape[1], 8, 128), jnp.float32),
         in_specs=[whole(pltpu.SMEM)],
         out_specs=whole(pltpu.VMEM),
         compiler_params=params(4),
@@ -532,7 +532,7 @@
         adjacency, queries, mine_b.reshape(blocked), sibling_b.reshape(blocked), table, mlp, output_weight
     )
     named, _ = lax.optimization_barrier((owners, att))
-    masks = run_plan(named, shards)
+    masks = run_plan(named.T, shards)
     keeps, swaps, slots, placed = [], [], [], []
     shape = (shards * CAP, rows, half)
     every = tuple(range(len(CHUNKS)))

time: 45.4 us -> 45.5 us (level)
  transfers between devices with their start and end apart: 15 -> 15, of which waited for: 10 -> 10; matrix products, arithmetic and copies ran while one was open for 0% -> 0% of each run, Pallas kernels for 25% -> 24%
where the time goes in v26:
time: 45.5 us; the launch traced here: 45.3 us
  starting transfers between devices  18.1 us (40%)
  Pallas kernels  15.3 us (34%)
  waiting for transfers between devices  11.6 us (25%)
    ppermute x9, starting transfers between devices, crossed(): return lax.ppermute(x, 'shard', [(i, i ^ distance) for i in range(size)])  13.8 us
    ppermute x9, waiting for transfers between devices, crossed(): return lax.ppermute(x, 'shard', [(i, i ^ distance) for i in range(size)])  7.39 us
    ppermute x6, starting transfers between devices, swapped(): return lax.ppermute(x, axis, [(0, 1), (1, 0)])  4.27 us
    ppermute x6, waiting for transfers between devices, swapped(): return lax.ppermute(x, axis, [(0, 1), (1, 0)])  4.17 us
    pallas_call x1, Pallas kernels, run_stage(): pl.pallas_call(functools.partial(stage_kernel, axes), out_shape=tuple((ja...  4.1 us
    pallas_call x1, Pallas kernels, run_mlp(): pl.pallas_call(mlp_kernel, out_shape=(jax.ShapeDtypeStruct((rows, wq.shap...  3.33 us
    pallas_call x1, Pallas kernels, run_attend(): pl.pallas_call(attend_kernel, out_shape=(part, part, jax.ShapeDtypeStruct...  2.51 us
    pallas_call x2, Pallas kernels, run_place(): pl.pallas_call(functools.partial(place_kernel, spots), out_shape=jax.Shap...  1.56 us
  transfers between devices with their start and end apart: 15, of which 10 were waited for; matrix products, arithmetic and copies ran while one was open for 0% of the time, Pallas kernels for 24%

profile of v26, /device:TPU:0, one launch (start us, length us, event | category | flops | bytes accessed | tf_op | source)
XLA Modules:
  0.0 45.3 jit_solution(13208645670282146384)
XLA Ops:
  0.0 0.9 %pick.1 = bf16[64,1024]{1,0:T(8,128)(2,1)S(1)} custom-call(bf16[128,1024]{1,0:T(8,128)(2,1)} %mesh.1), custom_call_target="tpu_custom_call" | custom-call | bytes 524288 | tf_op jit(solution)/shard_map/pick/pallas_call | solution.py:113
  0.9 4.1 %collective-permute-start.1 = (bf16[64,1024]{1,0:T(8,128)(2,1)S(1)}, bf16[64,1024]{1,0:T(8,128)(2,1)S(1)}, u32[]{:S(2)}, u32[]{:S(2)}) collective-permute-start(bf16[64,1024]{1,0:T(8,128)(2,1)S(1)} %pick.1), channel_id=1, source_target_pairs={{0,8},{4,12},{8,0},{12,4},{1,9},{5,13},{9,1},{13,5},{2,10},{6,14},... | collective-permute-start | bytes 393224 | tf_op jit(solution)/shard_map/ppermute | solution.py:478
  5.0 1.5 %collective-permute-start = (bf16[256,512]{1,0:T(8,128)(2,1)}, bf16[256,512]{1,0:T(8,128)(2,1)S(1)}, u32[]{:S(2)}, u32[]{:S(2)}) collective-permute-start(bf16[256,512]{1,0:T(8,128)(2,1)} %bitcast.10), channel_id=1, source_target_pairs={{0,2},{2,0},{1,3},{3,1},{4,6},{6,4},{5,7},{7,5},{8,10},{10,8},{9,1... | collective-permute-start | bytes 786440 | tf_op jit(solution)/shard_map/ppermute | solution.py:482
  6.5 1.6 %collective-permute-start.3 = (bf16[128,1024]{1,0:T(8,128)(2,1)}, bf16[128,1024]{1,0:T(8,128)(2,1)S(1)}, u32[]{:S(2)}, u32[]{:S(2)}) collective-permute-start(bf16[128,1024]{1,0:T(8,128)(2,1)} %mesh.1), channel_id=1, source_target_pairs={{0,4},{4,0},{8,12},{12,8},{1,5},{5,1},{9,13},{13,9},{2,6},{6,2},{1... | collective-permute-start | bytes 786440 | tf_op jit(solution)/shard_map/ppermute | solution.py:478
  8.1 4.1 %stage.1 = (bf16[256,512]{1,0:T(8,128)(2,1)S(1)}, f32[1,1024]{1,0:T(1,128)S(1)}, bf16[1024,512]{1,0:T(8,128)(2,1)S(1)}, bf16[1024,2048]{1,0:T(8,128)(2,1)S(1)}, ...) custom-call(bf16[256,512]{1,0:T(8,128)(2,1)} %bitcast.11, ...), custom_call_target="tpu_custom_call" | custom-call | flops 20451328000 | bytes 204513280 | tf_op jit(solution)/shard_map/stage/pallas_call | solution.py:163
  12.2 0.3 collective-permute-start.5
  12.5 0.0 collective-permute-done.1.refs_2_
  12.5 0.5 %collective-permute-start.2 = (bf16[64,1024]{1,0:T(8,128)(2,1)S(1)}, bf16[64,1024]{1,0:T(8,128)(2,1)S(1)}, u32[]{:S(2)}, u32[]{:S(2)}) collective-permute-start(bf16[64,1024]{1,0:T(8,128)(2,1)S(1)} %collective-permute-done.1.refs_2_), channel_id=1, source_target_pairs={{0,2},{2,0},{1,3},{3,1},{4,6},{6,4},{5,7},{7,5},{8,10},{10,8},{9,1... | collective-permute-start | bytes 393224 | tf_op jit(solution)/shard_map/ppermute | solution.py:482
  13.0 0.7 %collective-permute-start.4 = (bf16[64,1024]{1,0:T(8,128)(2,1)S(1)}, bf16[64,1024]{1,0:T(8,128)(2,1)S(1)}, u32[]{:S(2)}, u32[]{:S(2)}) collective-permute-start(bf16[64,1024]{1,0:T(8,128)(2,1)S(1)} %collective-permute-done.1.refs_2_), channel_id=1, source_target_pairs={{0,4},{4,0},{8,12},{12,8},{1,5},{5,1},{9,13},{13,9},{2,6},{6,2},{1... | collective-permute-start | bytes 393224 | tf_op jit(solution)/shard_map/ppermute | solution.py:478
  13.7 0.0 collective-permute-done.other
  13.7 0.0 copy-start.1
  13.7 0.0 copy-start.2
  13.7 3.3 %mlp.1 = (bf16[256,512]{1,0:T(8,128)(2,1)S(1)}, f32[256,1024]{1,0:T(8,128)S(1)}) custom-call(bf16[256,512]{1,0:T(8,128)(2,1)S(1)} %get-tuple-element.35.own, bf16[256,512]{1,0:T(8,128)(2,1)S(1)} %collective-permute-done.other, f32[1,1024]{1,0:T(1,128)S(1)} %get-tuple-element.37.gain, bf16[1024,512]{1,0:T(8,128)(2,1)S(1)} %get-tuple-element.38.wq, ...), custom_call_target="tpu_custom_call" | custom-call | flops 2415919104 | bytes 9437184 | tf_op jit(solution)/shard_map/mlp/pallas_call | solution.py:86
  17.1 0.4 collective-permute-done.2.refs_3_
  17.5 1.2 %collective-permute-done.3.refs_1_ = bf16[128,1024]{1,0:T(8,128)(2,1)S(1)} collective-permute-done((bf16[128,1024]{1,0:T(8,128)(2,1)}, bf16[128,1024]{1,0:T(8,128)(2,1)S(1)}, u32[]{:S(2)}, u32[]{:S(2)}) %collective-permute-start.3) | collective-permute-done | bytes 262176 | tf_op jit(solution)/shard_map/ppermute | solution.py:478
  18.7 0.0 copy-done.1
  18.7 0.0 copy-done.2
  18.7 1.0 %project.3 = bf16[384,1024]{1,0:T(8,128)(2,1)S(1)} custom-call(bf16[128,1024]{1,0:T(8,128)(2,1)S(1)} %get-tuple-element.47.refs_0_, bf16[128,1024]{1,0:T(8,128)(2,1)S(1)} %collective-permute-done.3.refs_1_, bf16[64,1024]{1,0:T(8,128)(2,1)S(1)} %collective-permute-done.1.refs_2_, bf16[64,1024]{1,0:T(8,128)(2,1)S(1)} %collective-permute-done.2.refs_3_, ...), custom_call_target="tpu_custom_call" | custom-call | flops 60397977600 | bytes 275251200 | tf_op jit(solution)/shard_map/project/pallas_call | solution.py:191
  19.7 0.0 copy-start.3
  19.7 0.0 copy-start.5
  19.7 0.1 collective-permute-start.7
  19.8 0.2 collective-permute-done.5.refs_1_
  20.0 1.5 %collective-permute-done.4.refs_0_ = bf16[64,1024]{1,0:T(8,128)(2,1)S(1)} collective-permute-done((bf16[64,1024]{1,0:T(8,128)(2,1)S(1)}, bf16[64,1024]{1,0:T(8,128)(2,1)S(1)}, u32[]{:S(2)}, u32[]{:S(2)}) %collective-permute-start.4) | collective-permute-done | bytes 131104 | tf_op jit(solution)/shard_map/ppermute | solution.py:478
  21.5 0.4 project.2
  21.9 0.1 collective-permute-start.6
  22.0 0.1 collective-permute-done.7
  22.1 0.1 table.1.table_in
  22.2 1.4 %collective-permute-done.6 = bf16[128,1024]{1,0:T(8,128)(2,1)S(1)} collective-permute-done((bf16[128,1024]{1,0:T(8,128)(2,1)S(1)}, bf16[128,1024]{1,0:T(8,128)(2,1)S(1)}, u32[]{:S(2)}, u32[]{:S(2)}) %collective-permute-start.6) | collective-permute-done | bytes 262176 | tf_op jit(solution)/shard_map/ppermute | solution.py:482
  23.5 0.0 copy-done.3
  23.5 0.0 copy-done.5
  23.5 2.5 %attend.1 = (bf16[4,80,128]{2,1,0:T(8,128)(2,1)S(1)}, bf16[4,80,128]{2,1,0:T(8,128)(2,1)S(1)}, bf16[256,512]{1,0:T(8,128)(2,1)S(1)}, bf16[2,8,64,1024]{3,2,1,0:T(8,128)(2,1)S(1)}) custom-call(s32[4,8]{1,0:T(4,128)S(1)} %copy-done.5, bf16[256,512]{1,0:T(8,128)(2,1)S(1)} %get-tuple-element.46.q, ...), custom_call_target="tpu_custom_call", output_to_operand_aliasing={{3}: (4, {})} | custom-call | flops 13421772800 | bytes 41943040 | tf_op jit(solution)/shard_map/attend/pallas_call | solution.py:325
  26.1 0.6 %collective-permute-start.9 = (bf16[4,80,128]{2,1,0:T(8,128)(2,1)S(1)}, bf16[4,80,128]{2,1,0:T(8,128)(2,1)S(1)}, u32[]{:S(2)}, u32[]{:S(2)}) collective-permute-start(bf16[4,80,128]{2,1,0:T(8,128)(2,1)S(1)} %get-tuple-element.56), channel_id=1, source_target_pairs={{0,2},{2,0},{1,3},{3,1},{4,6},{6,4},{5,7},{7,5},{8,10},{10,8},{9,1... | collective-permute-start | bytes 245768 | tf_op jit(solution)/shard_map/ppermute | solution.py:482
  26.7 0.0 copy-start
  26.7 0.0 copy-start.4
  26.7 0.4 project_out.1
  27.1 0.2 copy-done
  27.3 0.6 %plan.1.masks = f32[4,2,4,8,128]{4,3,2,1,0:T(8,128)S(1)} custom-call(s32[1,4]{1,0:T(1,128)S(1)} %bitcast.9), custom_call_target="tpu_custom_call" | custom-call | bytes 262144 | tf_op jit(solution)/shard_map/plan/pallas_call | solution.py:385
  27.9 1.5 %collective-permute-start.8 = (bf16[4,176,128]{2,1,0:T(8,128)(2,1)S(1)}, bf16[4,176,128]{2,1,0:T(8,128)(2,1)S(1)}, u32[]{:S(2)}, u32[]{:S(2)}) collective-permute-start(bf16[4,176,128]{2,1,0:T(8,128)(2,1)S(1)} %get-tuple-element.54), channel_id=1, source_target_pairs={{0,2},{2,0},{1,3},{3,1},{4,6},{6,4},{5,7},{7,5},{8,10},{10,8},{9,1... | collective-permute-start | bytes 540680 | tf_op jit(solution)/shard_map/ppermute | solution.py:482
  29.5 1.3 %collective-permute-done.9.refs_1_.refs_2_ = bf16[4,80,128]{2,1,0:T(8,128)(2,1)S(1)} collective-permute-done((bf16[4,80,128]{2,1,0:T(8,128)(2,1)S(1)}, bf16[4,80,128]{2,1,0:T(8,128)(2,1)S(1)}, u32[]{:S(2)}, u32[]{:S(2)}) %collective-permute-start.9) | collective-permute-done | bytes 81952 | tf_op jit(solution)/shard_map/ppermute | solution.py:482
  30.8 0.0 copy-done.4
  30.8 0.1 combine.3
  30.8 0.7 %collective-permute-start.13 = (bf16[2,80,128]{2,1,0:T(8,128)(2,1)S(1)}, bf16[2,80,128]{2,1,0:T(8,128)(2,1)S(1)}, u32[]{:S(2)}, u32[]{:S(2)}) collective-permute-start(bf16[2,80,128]{2,1,0:T(8,128)(2,1)S(1)} %get-tuple-element.57), channel_id=1, source_target_pairs={{0,8},{4,12},{8,0},{12,4},{1,9},{5,13},{9,1},{13,5},{2,10},{6,14},... | collective-permute-start | bytes 122888 | tf_op jit(solution)/shard_map/ppermute | solution.py:478
  31.5 1.9 %collective-permute-start.14 = (bf16[2,80,128]{2,1,0:T(8,128)(2,1)S(1)}, bf16[2,80,128]{2,1,0:T(8,128)(2,1)S(1)}, u32[]{:S(2)}, u32[]{:S(2)}) collective-permute-start(bf16[2,80,128]{2,1,0:T(8,128)(2,1)S(1)} %get-tuple-element.63), channel_id=1, source_target_pairs={{0,12},{4,8},{8,4},{12,0},{1,13},{5,9},{9,5},{13,1},{2,14},{6,10},... | collective-permute-start | bytes 122888 | tf_op jit(solution)/shard_map/ppermute | solution.py:478
  33.4 1.0 %collective-permute-done.8.refs_1_.refs_3_ = bf16[4,176,128]{2,1,0:T(8,128)(2,1)S(1)} collective-permute-done((bf16[4,176,128]{2,1,0:T(8,128)(2,1)S(1)}, bf16[4,176,128]{2,1,0:T(8,128)(2,1)S(1)}, u32[]{:S(2)}, u32[]{:S(2)}) %collective-permute-start.8) | collective-permute-done | bytes 180256 | tf_op jit(solution)/shard_map/ppermute | solution.py:482
  34.5 0.1 combine.4
  34.6 1.6 %collective-permute-start.10 = (bf16[2,176,128]{2,1,0:T(8,128)(2,1)S(1)}, bf16[2,176,128]{2,1,0:T(8,128)(2,1)S(1)}, u32[]{:S(2)}, u32[]{:S(2)}) collective-permute-start(bf16[2,176,128]{2,1,0:T(8,128)(2,1)S(1)} %get-tuple-element.59), channel_id=1, source_target_pairs={{0,8},{4,12},{8,0},{12,4},{1,9},{5,13},{9,1},{13,5},{2,10},{6,14},... | collective-permute-start | bytes 270344 | tf_op jit(solution)/shard_map/ppermute | solution.py:478
  36.2 0.2 combine.5
  36.4 1.5 %collective-permute-start.12 = (bf16[2,256,128]{2,1,0:T(8,128)(2,1)S(1)}, bf16[2,256,128]{2,1,0:T(8,128)(2,1)S(1)}, u32[]{:S(2)}, u32[]{:S(2)}) collective-permute-start(bf16[2,256,128]{2,1,0:T(8,128)(2,1)S(1)} %get-tuple-element.62), channel_id=1, source_target_pairs={{0,4},{4,0},{8,12},{12,8},{1,5},{5,1},{9,13},{13,9},{2,6},{6,2},{1... | collective-permute-start | bytes 393224 | tf_op jit(solution)/shard_map/ppermute | solution.py:478
  37.9 1.4 %collective-permute-start.11 = (bf16[2,176,128]{2,1,0:T(8,128)(2,1)S(1)}, bf16[2,176,128]{2,1,0:T(8,128)(2,1)S(1)}, u32[]{:S(2)}, u32[]{:S(2)}) collective-permute-start(bf16[2,176,128]{2,1,0:T(8,128)(2,1)S(1)} %get-tuple-element.60), channel_id=1, source_target_pairs={{0,12},{4,8},{8,4},{12,0},{1,13},{5,9},{9,5},{13,1},{2,14},{6,10},... | collective-permute-start | bytes 270344 | tf_op jit(solution)/shard_map/ppermute | solution.py:478
  39.3 0.0 collective-permute-done.13.refs_0_
  39.3 0.0 collective-permute-done.14.refs_1_
  39.3 0.8 %place.2.refs_3_ = bf16[8,64,512]{2,1,0:T(8,128)(2,1)} custom-call(bf16[2,80,128]{2,1,0:T(8,128)(2,1)S(1)} %collective-permute-done.13.refs_0_, bf16[2,80,128]{2,1,0:T(8,128)(2,1)S(1)} %collective-permute-done.14.refs_1_, bf16[2,256,128]{2,1,0:T(8,128)(2,1)S(1)} %get-tuple-element.64.refs_2_), custom_call_target="tpu_custom_call" | custom-call | flops 42598400000 | tf_op jit(solution)/shard_map/place/pallas_call | solution.py:462
  40.1 2.9 %collective-permute-done.10.refs_0_ = bf16[2,176,128]{2,1,0:T(8,128)(2,1)S(1)} collective-permute-done((bf16[2,176,128]{2,1,0:T(8,128)(2,1)S(1)}, bf16[2,176,128]{2,1,0:T(8,128)(2,1)S(1)}, u32[]{:S(2)}, u32[]{:S(2)}) %collective-permute-start.10) | collective-permute-done | bytes 90144 | tf_op jit(solution)/shard_map/ppermute | solution.py:478
  43.0 1.5 %collective-permute-done.11.refs_1_ = bf16[2,176,128]{2,1,0:T(8,128)(2,1)S(1)} collective-permute-done((bf16[2,176,128]{2,1,0:T(8,128)(2,1)S(1)}, bf16[2,176,128]{2,1,0:T(8,128)(2,1)S(1)}, u32[]{:S(2)}, u32[]{:S(2)}) %collective-permute-start.11) | collective-permute-done | bytes 90144 | tf_op jit(solution)/shard_map/ppermute | solution.py:478
  44.5 0.0 collective-permute-done.12.refs_2_
  44.5 0.8 %place.3 = bf16[8,64,512]{2,1,0:T(8,128)(2,1)} custom-call(bf16[2,176,128]{2,1,0:T(8,128)(2,1)S(1)} %collective-permute-done.10.refs_0_, bf16[2,176,128]{2,1,0:T(8,128)(2,1)S(1)} %collective-permute-done.11.refs_1_, bf16[2,256,128]{2,1,0:T(8,128)(2,1)S(1)} %collective-permute-done.12.refs_2_, ...), custom_call_target="tpu_custom_call", output_to_operand_aliasing={{}: (3, {})} | custom-call | flops 62259200000 | tf_op jit(solution)/shard_map/place/pallas_call | solution.py:462
Async XLA Ops:
  0.9 11.6 %collective-permute-start.1 = (bf16[64,1024]{1,0:T(8,128)(2,1)S(1)}, bf16[64,1024]{1,0:T(8,128)(2,1)S(1)}, u32[]{:S(2)}, u32[]{:S(2)}) collective-permute-start(bf16[64,1024]{1,0:T(8,128)(2,1)S(1)} %pick.1), channel_id=1, source_target_pairs={{0,8},{4,12},{8,0},{12,4},{1,9},{5,13},{9,1},{13,5},{2,10},{6,14},... | collective-permute-start | bytes 393224 | tf_op jit(solution)/shard_map/ppermute | solution.py:478
  5.0 8.7 %collective-permute-start = (bf16[256,512]{1,0:T(8,128)(2,1)}, bf16[256,512]{1,0:T(8,128)(2,1)S(1)}, u32[]{:S(2)}, u32[]{:S(2)}) collective-permute-start(bf16[256,512]{1,0:T(8,128)(2,1)} %bitcast.10), channel_id=1, source_target_pairs={{0,2},{2,0},{1,3},{3,1},{4,6},{6,4},{5,7},{7,5},{8,10},{10,8},{9,1... | collective-permute-start | bytes 786440 | tf_op jit(solution)/shard_map/ppermute | solution.py:482
  6.5 12.2 %collective-permute-start.3 = (bf16[128,1024]{1,0:T(8,128)(2,1)}, bf16[128,1024]{1,0:T(8,128)(2,1)S(1)}, u32[]{:S(2)}, u32[]{:S(2)}) collective-permute-start(bf16[128,1024]{1,0:T(8,128)(2,1)} %mesh.1), channel_id=1, source_target_pairs={{0,4},{4,0},{8,12},{12,8},{1,5},{5,1},{9,13},{13,9},{2,6},{6,2},{1... | collective-permute-start | bytes 786440 | tf_op jit(solution)/shard_map/ppermute | solution.py:478
  12.2 7.8 %collective-permute-start.5 = (bf16[64,1024]{1,0:T(8,128)(2,1)S(1)}, bf16[64,1024]{1,0:T(8,128)(2,1)S(1)}, u32[]{:S(2)}, u32[]{:S(2)}) collective-permute-start(bf16[64,1024]{1,0:T(8,128)(2,1)S(1)} %get-tuple-element.43), channel_id=1, source_target_pairs={{0,12},{4,8},{8,4},{12,0},{1,13},{5,9},{9,5},{13,1},{2,14},{6,10},... | collective-permute-start | bytes 393224 | tf_op jit(solution)/shard_map/ppermute | solution.py:478
  12.5 5.0 %collective-permute-start.2 = (bf16[64,1024]{1,0:T(8,128)(2,1)S(1)}, bf16[64,1024]{1,0:T(8,128)(2,1)S(1)}, u32[]{:S(2)}, u32[]{:S(2)}) collective-permute-start(bf16[64,1024]{1,0:T(8,128)(2,1)S(1)} %collective-permute-done.1.refs_2_), channel_id=1, source_target_pairs={{0,2},{2,0},{1,3},{3,1},{4,6},{6,4},{5,7},{7,5},{8,10},{10,8},{9,1... | collective-permute-start | bytes 393224 | tf_op jit(solution)/shard_map/ppermute | solution.py:482
  13.0 8.5 %collective-permute-start.4 = (bf16[64,1024]{1,0:T(8,128)(2,1)S(1)}, bf16[64,1024]{1,0:T(8,128)(2,1)S(1)}, u32[]{:S(2)}, u32[]{:S(2)}) collective-permute-start(bf16[64,1024]{1,0:T(8,128)(2,1)S(1)} %collective-permute-done.1.refs_2_), channel_id=1, source_target_pairs={{0,4},{4,0},{8,12},{12,8},{1,5},{5,1},{9,13},{13,9},{2,6},{6,2},{1... | collective-permute-start | bytes 393224 | tf_op jit(solution)/shard_map/ppermute | solution.py:478
  13.7 5.0 %copy-start.1 = (bf16[1024,512]{1,0:T(8,128)(2,1)S(1)}, bf16[1024,512]{1,0:T(8,128)(2,1)}, u32[]{:S(2)}) copy-start(bf16[1024,512]{1,0:T(8,128)(2,1)} %refs_4_.3) | copy-start | bytes 3145732
  13.7 5.0 %copy-start.2 = (bf16[1024,512]{1,0:T(8,128)(2,1)S(1)}, bf16[1024,512]{1,0:T(8,128)(2,1)}, u32[]{:S(2)}) copy-start(bf16[1024,512]{1,0:T(8,128)(2,1)} %refs_5_.3) | copy-start | bytes 3145732
  19.7 3.8 %copy-start.3 = (bf16[512,1024]{1,0:T(8,128)(2,1)S(1)}, bf16[512,1024]{1,0:T(8,128)(2,1)}, u32[]{:S(2)}) copy-start(bf16[512,1024]{1,0:T(8,128)(2,1)} %wo.3) | copy-start | bytes 3145732
  19.7 3.8 %copy-start.5 = (s32[4,8]{1,0:T(4,128)S(1)}, s32[4,8]{1,0:T(4,128)}, u32[]{:S(2)}) copy-start(s32[4,8]{1,0:T(4,128)} %adjacency.1) | copy-start | bytes 388
  19.7 2.4 %collective-permute-start.7 = (bf16[384,1024]{1,0:T(8,128)(2,1)S(1)}, bf16[384,1024]{1,0:T(8,128)(2,1)S(1)}, u32[]{:S(2)}, u32[]{:S(2)}) collective-permute-start(bf16[384,1024]{1,0:T(8,128)(2,1)S(1)} %project.3), channel_id=1, source_target_pairs={{0,1},{1,0},{2,3},{3,2},{4,5},{5,4},{6,7},{7,6},{8,9},{9,8},{10,11... | collective-permute-start | bytes 2359304 | tf_op jit(solution)/shard_map/ppermute | solution.py:482
  21.9 1.6 %collective-permute-start.6 = (bf16[128,1024]{1,0:T(8,128)(2,1)S(1)}, bf16[128,1024]{1,0:T(8,128)(2,1)S(1)}, u32[]{:S(2)}, u32[]{:S(2)}) collective-permute-start(bf16[128,1024]{1,0:T(8,128)(2,1)S(1)} %project.2), channel_id=1, source_target_pairs={{0,1},{1,0},{2,3},{3,2},{4,5},{5,4},{6,7},{7,6},{8,9},{9,8},{10,11... | collective-permute-start | bytes 786440 | tf_op jit(solution)/shard_map/ppermute | solution.py:482
  26.1 4.7 %collective-permute-start.9 = (bf16[4,80,128]{2,1,0:T(8,128)(2,1)S(1)}, bf16[4,80,128]{2,1,0:T(8,128)(2,1)S(1)}, u32[]{:S(2)}, u32[]{:S(2)}) collective-permute-start(bf16[4,80,128]{2,1,0:T(8,128)(2,1)S(1)} %get-tuple-element.56), channel_id=1, source_target_pairs={{0,2},{2,0},{1,3},{3,1},{4,6},{6,4},{5,7},{7,5},{8,10},{10,8},{9,1... | collective-permute-start | bytes 245768 | tf_op jit(solution)/shard_map/ppermute | solution.py:482
  26.7 0.7 %copy-start = (s32[4,1]{0,1:T(1,128)S(1)}, s32[4,1]{0,1:T(1,128)}, u32[]{:S(2)}) copy-start(s32[4,1]{0,1:T(1,128)} %param.12) | copy-start | bytes 52
  26.7 4.1 %copy-start.4 = (bf16[4,64,512]{2,1,0:T(8,128)(2,1)S(1)}, bf16[4,64,512]{2,1,0:T(8,128)(2,1)}, u32[]{:S(2)}) copy-start(bf16[4,64,512]{2,1,0:T(8,128)(2,1)} %grid_features.5) | copy-start | bytes 786436
  27.9 6.5 %collective-permute-start.8 = (bf16[4,176,128]{2,1,0:T(8,128)(2,1)S(1)}, bf16[4,176,128]{2,1,0:T(8,128)(2,1)S(1)}, u32[]{:S(2)}, u32[]{:S(2)}) collective-permute-start(bf16[4,176,128]{2,1,0:T(8,128)(2,1)S(1)} %get-tuple-element.54), channel_id=1, source_target_pairs={{0,2},{2,0},{1,3},{3,1},{4,6},{6,4},{5,7},{7,5},{8,10},{10,8},{9,1... | collective-permute-start | bytes 540680 | tf_op jit(solution)/shard_map/ppermute | solution.py:482
  30.8 8.4 %collective-permute-start.13 = (bf16[2,80,128]{2,1,0:T(8,128)(2,1)S(1)}, bf16[2,80,128]{2,1,0:T(8,128)(2,1)S(1)}, u32[]{:S(2)}, u32[]{:S(2)}) collective-permute-start(bf16[2,80,128]{2,1,0:T(8,128)(2,1)S(1)} %get-tuple-element.57), channel_id=1, source_target_pairs={{0,8},{4,12},{8,0},{12,4},{1,9},{5,13},{9,1},{13,5},{2,10},{6,14},... | collective-permute-start | bytes 122888 | tf_op jit(solution)/shard_map/ppermute | solution.py:478
  31.5 7.8 %collective-permute-start.14 = (bf16[2,80,128]{2,1,0:T(8,128)(2,1)S(1)}, bf16[2,80,128]{2,1,0:T(8,128)(2,1)S(1)}, u32[]{:S(2)}, u32[]{:S(2)}) collective-permute-start(bf16[2,80,128]{2,1,0:T(8,128)(2,1)S(1)} %get-tuple-element.63), channel_id=1, source_target_pairs={{0,12},{4,8},{8,4},{12,0},{1,13},{5,9},{9,5},{13,1},{2,14},{6,10},... | collective-permute-start | bytes 122888 | tf_op jit(solution)/shard_map/ppermute | solution.py:478
  34.6 8.4 %collective-permute-start.10 = (bf16[2,176,128]{2,1,0:T(8,128)(2,1)S(1)}, bf16[2,176,128]{2,1,0:T(8,128)(2,1)S(1)}, u32[]{:S(2)}, u32[]{:S(2)}) collective-permute-start(bf16[2,176,128]{2,1,0:T(8,128)(2,1)S(1)} %get-tuple-element.59), channel_id=1, source_target_pairs={{0,8},{4,12},{8,0},{12,4},{1,9},{5,13},{9,1},{13,5},{2,10},{6,14},... | collective-permute-start | bytes 270344 | tf_op jit(solution)/shard_map/ppermute | solution.py:478
  36.4 8.1 %collective-permute-start.12 = (bf16[2,256,128]{2,1,0:T(8,128)(2,1)S(1)}, bf16[2,256,128]{2,1,0:T(8,128)(2,1)S(1)}, u32[]{:S(2)}, u32[]{:S(2)}) collective-permute-start(bf16[2,256,128]{2,1,0:T(8,128)(2,1)S(1)} %get-tuple-element.62), channel_id=1, source_target_pairs={{0,4},{4,0},{8,12},{12,8},{1,5},{5,1},{9,13},{13,9},{2,6},{6,2},{1... | collective-permute-start | bytes 393224 | tf_op jit(solution)/shard_map/ppermute | solution.py:478
  37.9 6.6 %collective-permute-start.11 = (bf16[2,176,128]{2,1,0:T(8,128)(2,1)S(1)}, bf16[2,176,128]{2,1,0:T(8,128)(2,1)S(1)}, u32[]{:S(2)}, u32[]{:S(2)}) collective-permute-start(bf16[2,176,128]{2,1,0:T(8,128)(2,1)S(1)} %get-tuple-element.60), channel_id=1, source_target_pairs={{0,12},{4,8},{8,4},{12,0},{1,13},{5,9},{9,5},{13,1},{2,14},{6,10},... | collective-permute-start | bytes 270344 | tf_op jit(solution)/shard_map/ppermute | solution.py:478

commit v27 on v26

--- a/solution.py
+++ b/solution.py
@@ -203,23 +203,24 @@
     )(*pieces, in_vmem(wk), in_vmem(wv))
 
 
-def table_kernel(mine, sibling, table):
-    table[0, : mine.shape[0]] = mine[...]
-    table[1, : mine.shape[0]] = sibling[...]
-
-
-def run_table(mine, sibling, blocks):
+def table_kernel(mine, sibling, mine_last, sibling_last, table):
+    for i, (first, last) in enumerate(((mine, mine_last), (sibling, sibling_last))):
+        table[i, : first.shape[0]] = first[...]
+        table[i, table.shape[1] - last.shape[0] :] = last[...]
+
+
+def run_table(mine, sibling, mine_last, sibling_last, blocks):
     return pl.pallas_call(
         table_kernel,
         out_shape=jax.ShapeDtypeStruct((2, blocks) + mine.shape[1:], jnp.bfloat16),
-        in_specs=vmem(2),
+        in_specs=vmem(4),
         out_specs=whole(pltpu.VMEM),
         compiler_params=params(8),
         cost_estimate=pl.CostEstimate(
             flops=0, bytes_accessed=80 * mine.size, transcendentals=0
         ),
         name="table",
-    )(mine, sibling)
+    )(mine, sibling, mine_last, sibling_last)
 
 
 def pieces_of(c):
@@ -261,11 +262,11 @@
     h = lax.axis_index("head")
     u = lax.axis_index("sub")
     half = wo.shape[0]
-    ready = table.shape[1] - mine.shape[0]
+    ready = table.shape[1] - 2 * mine.shape[0]
     copy = pltpu.make_async_copy(adjacency, near_s, sem)
     copy.start()
     for i, part in enumerate((mine, sibling)):
-        table[i, ready:] = part[...]
+        table[i, ready : ready + part.shape[0]] = part[...]
     rows_of = lax.broadcasted_iota(jnp.int32, (WIDE, WIDE), 0) // BLOCK
     lanes_of = lax.broadcasted_iota(jnp.int32, (WIDE, WIDE), 1) // HEAD_DIM
     diagonal = rows_of == lanes_of
@@ -525,8 +526,13 @@
     blocked = (-1, BLOCK, 2 * half)
     mine_a = run_project((mesh, near, far, far_pair), key_weight, value_weight)
     sibling_a = swapped(mine_a, "sub")
-    table = run_table(mine_a.reshape(blocked), sibling_a.reshape(blocked), 2 * shards)
-    mine_b = run_project((farther, straight), key_weight, value_weight)
+    straight, _ = lax.optimization_barrier((straight, mine_a))
+    mine_m = run_project((straight,), key_weight, value_weight)
+    sibling_m = swapped(mine_m, "sub")
+    parts = [part.reshape(blocked) for part in (mine_a, sibling_a, mine_m, sibling_m)]
+    table = run_table(*parts, 2 * shards)
+    farther, _ = lax.optimization_barrier((farther, mine_m))
+    mine_b = run_project((farther,), key_weight, value_weight)
     sibling_b = swapped(mine_b, "sub")
     send, keep, att = run_attend(
         adjacency, queries, mine_b.reshape(blocked), sibling_b.reshape(blocked), table, mlp, output_weight

time: 45.5 us -> 45.6 us (level)
  waiting for transfers between devices: 11.6 us -> 10.8 us
  Pallas kernels: 15.3 us -> 15.8 us
    ppermute x9, waiting for transfers between devices: 7.39 us -> 6.84 us  [crossed(): return lax.ppermute(x, 'shard', [(i, i ^ distance) for i in range(size)])]
    pallas_call x2 -> x3, Pallas kernels: 1.42 us -> 1.92 us  [run_project(): pl.pallas_call(project_kernel, out_shape=jax.ShapeDtypeStruct((rows, 2 *...]
    ppermute x6 -> x7, starting transfers between devices: 4.27 us -> 4.63 us  [swapped(): return lax.ppermute(x, axis, [(0, 1), (1, 0)])]
    ppermute x6 -> x7, waiting for transfers between devices: 4.17 us -> 3.96 us  [swapped(): return lax.ppermute(x, axis, [(0, 1), (1, 0)])]
  transfers between devices with their start and end apart: 15 -> 16, of which waited for: 10 -> 11; matrix products, arithmetic and copies ran while one was open for 0% -> 0% of each run, Pallas kernels for 24% -> 26%
where the time goes in v27:
time: 45.6 us; the launch traced here: 45.5 us
  starting transfers between devices  18.4 us (40%)
  Pallas kernels  15.8 us (35%)
  waiting for transfers between devices  10.8 us (24%)
    ppermute x9, starting transfers between devices, crossed(): return lax.ppermute(x, 'shard', [(i, i ^ distance) for i in range(size)])  13.8 us
    ppermute x9, waiting for transfers between devices, crossed(): return lax.ppermute(x, 'shard', [(i, i ^ distance) for i in range(size)])  6.84 us
    ppermute x7, starting transfers between devices, swapped(): return lax.ppermute(x, axis, [(0, 1), (1, 0)])  4.63 us
    pallas_call x1, Pallas kernels, run_stage(): pl.pallas_call(functools.partial(stage_kernel, axes), out_shape=tuple((ja...  4.1 us
    ppermute x7, waiting for transfers between devices, swapped(): return lax.ppermute(x, axis, [(0, 1), (1, 0)])  3.96 us
    pallas_call x1, Pallas kernels, run_mlp(): pl.pallas_call(mlp_kernel, out_shape=(jax.ShapeDtypeStruct((rows, wq.shap...  3.33 us
    pallas_call x1, Pallas kernels, run_attend(): pl.pallas_call(attend_kernel, out_shape=(part, part, jax.ShapeDtypeStruct...  2.51 us
    pallas_call x3, Pallas kernels, run_project(): pl.pallas_call(project_kernel, out_shape=jax.ShapeDtypeStruct((rows, 2 *...  1.92 us
  transfers between devices with their start and end apart: 16, of which 11 were waited for; matrix products, arithmetic and copies ran while one was open for 0% of the time, Pallas kernels for 26%

profile of v27, /device:TPU:0, one launch (start us, length us, event | category | flops | bytes accessed | tf_op | source)
XLA Modules:
  0.0 45.5 jit_solution(14998729954998645644)
XLA Ops:
  0.0 0.9 %pick.1 = bf16[64,1024]{1,0:T(8,128)(2,1)S(1)} custom-call(bf16[128,1024]{1,0:T(8,128)(2,1)} %mesh.1), custom_call_target="tpu_custom_call" | custom-call | bytes 524288 | tf_op jit(solution)/shard_map/pick/pallas_call | solution.py:113
  0.9 4.1 %collective-permute-start.1 = (bf16[64,1024]{1,0:T(8,128)(2,1)S(1)}, bf16[64,1024]{1,0:T(8,128)(2,1)S(1)}, u32[]{:S(2)}, u32[]{:S(2)}) collective-permute-start(bf16[64,1024]{1,0:T(8,128)(2,1)S(1)} %pick.1), channel_id=1, source_target_pairs={{0,8},{4,12},{8,0},{12,4},{1,9},{5,13},{9,1},{13,5},{2,10},{6,14},... | collective-permute-start | bytes 393224 | tf_op jit(solution)/shard_map/ppermute | solution.py:479
  5.0 1.5 %collective-permute-start = (bf16[256,512]{1,0:T(8,128)(2,1)}, bf16[256,512]{1,0:T(8,128)(2,1)S(1)}, u32[]{:S(2)}, u32[]{:S(2)}) collective-permute-start(bf16[256,512]{1,0:T(8,128)(2,1)} %bitcast.14), channel_id=1, source_target_pairs={{0,2},{2,0},{1,3},{3,1},{4,6},{6,4},{5,7},{7,5},{8,10},{10,8},{9,1... | collective-permute-start | bytes 786440 | tf_op jit(solution)/shard_map/ppermute | solution.py:483
  6.5 1.6 %collective-permute-start.3 = (bf16[128,1024]{1,0:T(8,128)(2,1)}, bf16[128,1024]{1,0:T(8,128)(2,1)S(1)}, u32[]{:S(2)}, u32[]{:S(2)}) collective-permute-start(bf16[128,1024]{1,0:T(8,128)(2,1)} %mesh.1), channel_id=1, source_target_pairs={{0,4},{4,0},{8,12},{12,8},{1,5},{5,1},{9,13},{13,9},{2,6},{6,2},{1... | collective-permute-start | bytes 786440 | tf_op jit(solution)/shard_map/ppermute | solution.py:479
  8.1 4.1 %stage.1 = (bf16[256,512]{1,0:T(8,128)(2,1)S(1)}, f32[1,1024]{1,0:T(1,128)S(1)}, bf16[1024,512]{1,0:T(8,128)(2,1)S(1)}, bf16[1024,2048]{1,0:T(8,128)(2,1)S(1)}, ...) custom-call(bf16[256,512]{1,0:T(8,128)(2,1)} %bitcast.15, ...), custom_call_target="tpu_custom_call" | custom-call | flops 20451328000 | bytes 204513280 | tf_op jit(solution)/shard_map/stage/pallas_call | solution.py:163
  12.2 0.3 collective-permute-start.5
  12.5 0.0 collective-permute-done.1.refs_2_
  12.5 0.5 %collective-permute-start.2 = (bf16[64,1024]{1,0:T(8,128)(2,1)S(1)}, bf16[64,1024]{1,0:T(8,128)(2,1)S(1)}, u32[]{:S(2)}, u32[]{:S(2)}) collective-permute-start(bf16[64,1024]{1,0:T(8,128)(2,1)S(1)} %collective-permute-done.1.refs_2_), channel_id=1, source_target_pairs={{0,2},{2,0},{1,3},{3,1},{4,6},{6,4},{5,7},{7,5},{8,10},{10,8},{9,1... | collective-permute-start | bytes 393224 | tf_op jit(solution)/shard_map/ppermute | solution.py:483
  13.0 0.7 %collective-permute-start.4 = (bf16[64,1024]{1,0:T(8,128)(2,1)S(1)}, bf16[64,1024]{1,0:T(8,128)(2,1)S(1)}, u32[]{:S(2)}, u32[]{:S(2)}) collective-permute-start(bf16[64,1024]{1,0:T(8,128)(2,1)S(1)} %collective-permute-done.1.refs_2_), channel_id=1, source_target_pairs={{0,4},{4,0},{8,12},{12,8},{1,5},{5,1},{9,13},{13,9},{2,6},{6,2},{1... | collective-permute-start | bytes 393224 | tf_op jit(solution)/shard_map/ppermute | solution.py:479
  13.7 0.0 collective-permute-done.other
  13.7 0.0 copy-start.1
  13.7 0.0 copy-start.2
  13.7 3.3 %mlp.1 = (bf16[256,512]{1,0:T(8,128)(2,1)S(1)}, f32[256,1024]{1,0:T(8,128)S(1)}) custom-call(bf16[256,512]{1,0:T(8,128)(2,1)S(1)} %get-tuple-element.37.own, bf16[256,512]{1,0:T(8,128)(2,1)S(1)} %collective-permute-done.other, f32[1,1024]{1,0:T(1,128)S(1)} %get-tuple-element.39.gain, bf16[1024,512]{1,0:T(8,128)(2,1)S(1)} %get-tuple-element.40.wq, ...), custom_call_target="tpu_custom_call" | custom-call | flops 2415919104 | bytes 9437184 | tf_op jit(solution)/shard_map/mlp/pallas_call | solution.py:86
  17.1 0.4 collective-permute-done.2.refs_3_
  17.5 1.2 %collective-permute-done.3.refs_1_ = bf16[128,1024]{1,0:T(8,128)(2,1)S(1)} collective-permute-done((bf16[128,1024]{1,0:T(8,128)(2,1)}, bf16[128,1024]{1,0:T(8,128)(2,1)S(1)}, u32[]{:S(2)}, u32[]{:S(2)}) %collective-permute-start.3) | collective-permute-done | bytes 262176 | tf_op jit(solution)/shard_map/ppermute | solution.py:479
  18.7 0.0 copy-done.1
  18.7 0.0 copy-done.2
  18.7 1.0 %project.3 = bf16[384,1024]{1,0:T(8,128)(2,1)S(1)} custom-call(bf16[128,1024]{1,0:T(8,128)(2,1)S(1)} %get-tuple-element.49.refs_0_, bf16[128,1024]{1,0:T(8,128)(2,1)S(1)} %collective-permute-done.3.refs_1_, bf16[64,1024]{1,0:T(8,128)(2,1)S(1)} %collective-permute-done.1.refs_2_, bf16[64,1024]{1,0:T(8,128)(2,1)S(1)} %collective-permute-done.2.refs_3_, ...), custom_call_target="tpu_custom_call" | custom-call | flops 60397977600 | bytes 275251200 | tf_op jit(solution)/shard_map/project/pallas_call | solution.py:191
  19.7 0.1 collective-permute-start.7
  19.8 0.2 collective-permute-done.5.refs_0_
  20.0 0.5 %project.4 = bf16[64,1024]{1,0:T(8,128)(2,1)S(1)} custom-call(bf16[64,1024]{1,0:T(8,128)(2,1)S(1)} %collective-permute-done.5.refs_0_, bf16[1024,512]{1,0:T(8,128)(2,1)S(1)} %copy-done.1, bf16[1024,512]{1,0:T(8,128)(2,1)S(1)} %copy-done.2), custom_call_target="tpu_custom_call" | custom-call | flops 10066329600 | bytes 176947200 | tf_op jit(solution)/shard_map/project/pallas_call | solution.py:191
  20.4 0.0 copy-start.3
  20.5 0.0 copy-start.5
  20.5 0.4 collective-permute-start.8
  20.8 0.6 %collective-permute-done.4.refs_0_ = bf16[64,1024]{1,0:T(8,128)(2,1)S(1)} collective-permute-done((bf16[64,1024]{1,0:T(8,128)(2,1)S(1)}, bf16[64,1024]{1,0:T(8,128)(2,1)S(1)}, u32[]{:S(2)}, u32[]{:S(2)}) %collective-permute-start.4) | collective-permute-done | bytes 131104 | tf_op jit(solution)/shard_map/ppermute | solution.py:479
  21.5 0.5 %project.5 = bf16[64,1024]{1,0:T(8,128)(2,1)S(1)} custom-call(bf16[64,1024]{1,0:T(8,128)(2,1)S(1)} %collective-permute-done.4.refs_0_, bf16[1024,512]{1,0:T(8,128)(2,1)S(1)} %copy-done.1, bf16[1024,512]{1,0:T(8,128)(2,1)S(1)} %copy-done.2), custom_call_target="tpu_custom_call" | custom-call | flops 10066329600 | bytes 176947200 | tf_op jit(solution)/shard_map/project/pallas_call | solution.py:191
  22.0 0.1 collective-permute-start.6
  22.0 0.2 collective-permute-done.8
  22.2 0.0 collective-permute-done.7
  22.2 0.1 table.1.table_in
  22.3 1.0 %collective-permute-done.6 = bf16[64,1024]{1,0:T(8,128)(2,1)S(1)} collective-permute-done((bf16[64,1024]{1,0:T(8,128)(2,1)S(1)}, bf16[64,1024]{1,0:T(8,128)(2,1)S(1)}, u32[]{:S(2)}, u32[]{:S(2)}) %collective-permute-start.6) | collective-permute-done | bytes 131104 | tf_op jit(solution)/shard_map/ppermute | solution.py:483
  23.4 0.0 copy-done.3
  23.4 0.0 copy-done.5
  23.4 2.5 %attend.1 = (bf16[4,80,128]{2,1,0:T(8,128)(2,1)S(1)}, bf16[4,80,128]{2,1,0:T(8,128)(2,1)S(1)}, bf16[256,512]{1,0:T(8,128)(2,1)S(1)}, bf16[2,8,64,1024]{3,2,1,0:T(8,128)(2,1)S(1)}) custom-call(s32[4,8]{1,0:T(4,128)S(1)} %copy-done.5, bf16[256,512]{1,0:T(8,128)(2,1)S(1)} %get-tuple-element.48.q, ...), custom_call_target="tpu_custom_call", output_to_operand_aliasing={{3}: (4, {})} | custom-call | flops 13421772800 | bytes 41943040 | tf_op jit(solution)/shard_map/attend/pallas_call | solution.py:326
  25.9 0.6 %collective-permute-start.10 = (bf16[4,80,128]{2,1,0:T(8,128)(2,1)S(1)}, bf16[4,80,128]{2,1,0:T(8,128)(2,1)S(1)}, u32[]{:S(2)}, u32[]{:S(2)}) collective-permute-start(bf16[4,80,128]{2,1,0:T(8,128)(2,1)S(1)} %get-tuple-element.60), channel_id=1, source_target_pairs={{0,2},{2,0},{1,3},{3,1},{4,6},{6,4},{5,7},{7,5},{8,10},{10,8},{9,1... | collective-permute-start | bytes 245768 | tf_op jit(solution)/shard_map/ppermute | solution.py:483
  26.5 0.0 copy-start
  26.5 0.0 copy-start.4
  26.5 0.4 project_out.1
  27.0 0.2 copy-done
  27.2 0.6 %plan.1.masks = f32[4,2,4,8,128]{4,3,2,1,0:T(8,128)S(1)} custom-call(s32[1,4]{1,0:T(1,128)S(1)} %bitcast.13), custom_call_target="tpu_custom_call" | custom-call | bytes 262144 | tf_op jit(solution)/shard_map/plan/pallas_call | solution.py:386
  27.8 1.5 %collective-permute-start.9 = (bf16[4,176,128]{2,1,0:T(8,128)(2,1)S(1)}, bf16[4,176,128]{2,1,0:T(8,128)(2,1)S(1)}, u32[]{:S(2)}, u32[]{:S(2)}) collective-permute-start(bf16[4,176,128]{2,1,0:T(8,128)(2,1)S(1)} %get-tuple-element.58), channel_id=1, source_target_pairs={{0,2},{2,0},{1,3},{3,1},{4,6},{6,4},{5,7},{7,5},{8,10},{10,8},{9,1... | collective-permute-start | bytes 540680 | tf_op jit(solution)/shard_map/ppermute | solution.py:483
  29.3 1.3 %collective-permute-done.10.refs_1_.refs_2_ = bf16[4,80,128]{2,1,0:T(8,128)(2,1)S(1)} collective-permute-done((bf16[4,80,128]{2,1,0:T(8,128)(2,1)S(1)}, bf16[4,80,128]{2,1,0:T(8,128)(2,1)S(1)}, u32[]{:S(2)}, u32[]{:S(2)}) %collective-permute-start.10) | collective-permute-done | bytes 81952 | tf_op jit(solution)/shard_map/ppermute | solution.py:483
  30.6 0.0 copy-done.4
  30.6 0.1 combine.3
  30.7 1.1 %collective-permute-start.14 = (bf16[2,80,128]{2,1,0:T(8,128)(2,1)S(1)}, bf16[2,80,128]{2,1,0:T(8,128)(2,1)S(1)}, u32[]{:S(2)}, u32[]{:S(2)}) collective-permute-start(bf16[2,80,128]{2,1,0:T(8,128)(2,1)S(1)} %get-tuple-element.61), channel_id=1, source_target_pairs={{0,8},{4,12},{8,0},{12,4},{1,9},{5,13},{9,1},{13,5},{2,10},{6,14},... | collective-permute-start | bytes 122888 | tf_op jit(solution)/shard_map/ppermute | solution.py:479
  31.8 1.5 %collective-permute-start.15 = (bf16[2,80,128]{2,1,0:T(8,128)(2,1)S(1)}, bf16[2,80,128]{2,1,0:T(8,128)(2,1)S(1)}, u32[]{:S(2)}, u32[]{:S(2)}) collective-permute-start(bf16[2,80,128]{2,1,0:T(8,128)(2,1)S(1)} %get-tuple-element.67), channel_id=1, source_target_pairs={{0,12},{4,8},{8,4},{12,0},{1,13},{5,9},{9,5},{13,1},{2,14},{6,10},... | collective-permute-start | bytes 122888 | tf_op jit(solution)/shard_map/ppermute | solution.py:479
  33.3 1.0 %collective-permute-done.9.refs_1_.refs_3_ = bf16[4,176,128]{2,1,0:T(8,128)(2,1)S(1)} collective-permute-done((bf16[4,176,128]{2,1,0:T(8,128)(2,1)S(1)}, bf16[4,176,128]{2,1,0:T(8,128)(2,1)S(1)}, u32[]{:S(2)}, u32[]{:S(2)}) %collective-permute-start.9) | collective-permute-done | bytes 180256 | tf_op jit(solution)/shard_map/ppermute | solution.py:483
  34.3 0.1 combine.4
  34.4 2.1 %collective-permute-start.11 = (bf16[2,176,128]{2,1,0:T(8,128)(2,1)S(1)}, bf16[2,176,128]{2,1,0:T(8,128)(2,1)S(1)}, u32[]{:S(2)}, u32[]{:S(2)}) collective-permute-start(bf16[2,176,128]{2,1,0:T(8,128)(2,1)S(1)} %get-tuple-element.63), channel_id=1, source_target_pairs={{0,8},{4,12},{8,0},{12,4},{1,9},{5,13},{9,1},{13,5},{2,10},{6,14},... | collective-permute-start | bytes 270344 | tf_op jit(solution)/shard_map/ppermute | solution.py:479
  36.5 0.2 combine.5
  36.7 1.1 %collective-permute-start.13 = (bf16[2,256,128]{2,1,0:T(8,128)(2,1)S(1)}, bf16[2,256,128]{2,1,0:T(8,128)(2,1)S(1)}, u32[]{:S(2)}, u32[]{:S(2)}) collective-permute-start(bf16[2,256,128]{2,1,0:T(8,128)(2,1)S(1)} %get-tuple-element.66), channel_id=1, source_target_pairs={{0,4},{4,0},{8,12},{12,8},{1,5},{5,1},{9,13},{13,9},{2,6},{6,2},{1... | collective-permute-start | bytes 393224 | tf_op jit(solution)/shard_map/ppermute | solution.py:479
  37.8 1.3 %collective-permute-start.12 = (bf16[2,176,128]{2,1,0:T(8,128)(2,1)S(1)}, bf16[2,176,128]{2,1,0:T(8,128)(2,1)S(1)}, u32[]{:S(2)}, u32[]{:S(2)}) collective-permute-start(bf16[2,176,128]{2,1,0:T(8,128)(2,1)S(1)} %get-tuple-element.64), channel_id=1, source_target_pairs={{0,12},{4,8},{8,4},{12,0},{1,13},{5,9},{9,5},{13,1},{2,14},{6,10},... | collective-permute-start | bytes 270344 | tf_op jit(solution)/shard_map/ppermute | solution.py:479
  39.1 0.0 collective-permute-done.14.refs_0_
  39.1 0.0 collective-permute-done.15.refs_1_
  39.1 0.8 %place.2.refs_3_ = bf16[8,64,512]{2,1,0:T(8,128)(2,1)} custom-call(bf16[2,80,128]{2,1,0:T(8,128)(2,1)S(1)} %collective-permute-done.14.refs_0_, bf16[2,80,128]{2,1,0:T(8,128)(2,1)S(1)} %collective-permute-done.15.refs_1_, bf16[2,256,128]{2,1,0:T(8,128)(2,1)S(1)} %get-tuple-element.68.refs_2_), custom_call_target="tpu_custom_call" | custom-call | flops 42598400000 | tf_op jit(solution)/shard_map/place/pallas_call | solution.py:463
  39.9 2.9 %collective-permute-done.11.refs_0_ = bf16[2,176,128]{2,1,0:T(8,128)(2,1)S(1)} collective-permute-done((bf16[2,176,128]{2,1,0:T(8,128)(2,1)S(1)}, bf16[2,176,128]{2,1,0:T(8,128)(2,1)S(1)}, u32[]{:S(2)}, u32[]{:S(2)}) %collective-permute-start.11) | collective-permute-done | bytes 90144 | tf_op jit(solution)/shard_map/ppermute | solution.py:479
  42.8 1.7 %collective-permute-done.12.refs_1_ = bf16[2,176,128]{2,1,0:T(8,128)(2,1)S(1)} collective-permute-done((bf16[2,176,128]{2,1,0:T(8,128)(2,1)S(1)}, bf16[2,176,128]{2,1,0:T(8,128)(2,1)S(1)}, u32[]{:S(2)}, u32[]{:S(2)}) %collective-permute-start.12) | collective-permute-done | bytes 90144 | tf_op jit(solution)/shard_map/ppermute | solution.py:479
  44.5 0.1 collective-permute-done.13.refs_2_
  44.6 0.8 %place.3 = bf16[8,64,512]{2,1,0:T(8,128)(2,1)} custom-call(bf16[2,176,128]{2,1,0:T(8,128)(2,1)S(1)} %collective-permute-done.11.refs_0_, bf16[2,176,128]{2,1,0:T(8,128)(2,1)S(1)} %collective-permute-done.12.refs_1_, bf16[2,256,128]{2,1,0:T(8,128)(2,1)S(1)} %collective-permute-done.13.refs_2_, ...), custom_call_target="tpu_custom_call", output_to_operand_aliasing={{}: (3, {})} | custom-call | flops 62259200000 | tf_op jit(solution)/shard_map/place/pallas_call | solution.py:463
Async XLA Ops:
  0.9 11.6 %collective-permute-start.1 = (bf16[64,1024]{1,0:T(8,128)(2,1)S(1)}, bf16[64,1024]{1,0:T(8,128)(2,1)S(1)}, u32[]{:S(2)}, u32[]{:S(2)}) collective-permute-start(bf16[64,1024]{1,0:T(8,128)(2,1)S(1)} %pick.1), channel_id=1, source_target_pairs={{0,8},{4,12},{8,0},{12,4},{1,9},{5,13},{9,1},{13,5},{2,10},{6,14},... | collective-permute-start | bytes 393224 | tf_op jit(solution)/shard_map/ppermute | solution.py:479
  5.0 8.7 %collective-permute-start = (bf16[256,512]{1,0:T(8,128)(2,1)}, bf16[256,512]{1,0:T(8,128)(2,1)S(1)}, u32[]{:S(2)}, u32[]{:S(2)}) collective-permute-start(bf16[256,512]{1,0:T(8,128)(2,1)} %bitcast.14), channel_id=1, source_target_pairs={{0,2},{2,0},{1,3},{3,1},{4,6},{6,4},{5,7},{7,5},{8,10},{10,8},{9,1... | collective-permute-start | bytes 786440 | tf_op jit(solution)/shard_map/ppermute | solution.py:483
  6.5 12.2 %collective-permute-start.3 = (bf16[128,1024]{1,0:T(8,128)(2,1)}, bf16[128,1024]{1,0:T(8,128)(2,1)S(1)}, u32[]{:S(2)}, u32[]{:S(2)}) collective-permute-start(bf16[128,1024]{1,0:T(8,128)(2,1)} %mesh.1), channel_id=1, source_target_pairs={{0,4},{4,0},{8,12},{12,8},{1,5},{5,1},{9,13},{13,9},{2,6},{6,2},{1... | collective-permute-start | bytes 786440 | tf_op jit(solution)/shard_map/ppermute | solution.py:479
  12.2 7.8 %collective-permute-start.5 = (bf16[64,1024]{1,0:T(8,128)(2,1)S(1)}, bf16[64,1024]{1,0:T(8,128)(2,1)S(1)}, u32[]{:S(2)}, u32[]{:S(2)}) collective-permute-start(bf16[64,1024]{1,0:T(8,128)(2,1)S(1)} %get-tuple-element.45), channel_id=1, source_target_pairs={{0,12},{4,8},{8,4},{12,0},{1,13},{5,9},{9,5},{13,1},{2,14},{6,10},... | collective-permute-start | bytes 393224 | tf_op jit(solution)/shard_map/ppermute | solution.py:479
  12.5 5.0 %collective-permute-start.2 = (bf16[64,1024]{1,0:T(8,128)(2,1)S(1)}, bf16[64,1024]{1,0:T(8,128)(2,1)S(1)}, u32[]{:S(2)}, u32[]{:S(2)}) collective-permute-start(bf16[64,1024]{1,0:T(8,128)(2,1)S(1)} %collective-permute-done.1.refs_2_), channel_id=1, source_target_pairs={{0,2},{2,0},{1,3},{3,1},{4,6},{6,4},{5,7},{7,5},{8,10},{10,8},{9,1... | collective-permute-start | bytes 393224 | tf_op jit(solution)/shard_map/ppermute | solution.py:483
  13.0 8.5 %collective-permute-start.4 = (bf16[64,1024]{1,0:T(8,128)(2,1)S(1)}, bf16[64,1024]{1,0:T(8,128)(2,1)S(1)}, u32[]{:S(2)}, u32[]{:S(2)}) collective-permute-start(bf16[64,1024]{1,0:T(8,128)(2,1)S(1)} %collective-permute-done.1.refs_2_), channel_id=1, source_target_pairs={{0,4},{4,0},{8,12},{12,8},{1,5},{5,1},{9,13},{13,9},{2,6},{6,2},{1... | collective-permute-start | bytes 393224 | tf_op jit(solution)/shard_map/ppermute | solution.py:479
  13.7 5.0 %copy-start.1 = (bf16[1024,512]{1,0:T(8,128)(2,1)S(1)}, bf16[1024,512]{1,0:T(8,128)(2,1)}, u32[]{:S(2)}) copy-start(bf16[1024,512]{1,0:T(8,128)(2,1)} %refs_1_.3) | copy-start | bytes 3145732
  13.7 5.0 %copy-start.2 = (bf16[1024,512]{1,0:T(8,128)(2,1)S(1)}, bf16[1024,512]{1,0:T(8,128)(2,1)}, u32[]{:S(2)}) copy-start(bf16[1024,512]{1,0:T(8,128)(2,1)} %refs_2_.5) | copy-start | bytes 3145732
  19.7 2.5 %collective-permute-start.7 = (bf16[384,1024]{1,0:T(8,128)(2,1)S(1)}, bf16[384,1024]{1,0:T(8,128)(2,1)S(1)}, u32[]{:S(2)}, u32[]{:S(2)}) collective-permute-start(bf16[384,1024]{1,0:T(8,128)(2,1)S(1)} %project.3), channel_id=1, source_target_pairs={{0,1},{1,0},{2,3},{3,2},{4,5},{5,4},{6,7},{7,6},{8,9},{9,8},{10,11... | collective-permute-start | bytes 2359304 | tf_op jit(solution)/shard_map/ppermute | solution.py:483
  20.4 2.9 %copy-start.3 = (bf16[512,1024]{1,0:T(8,128)(2,1)S(1)}, bf16[512,1024]{1,0:T(8,128)(2,1)}, u32[]{:S(2)}) copy-start(bf16[512,1024]{1,0:T(8,128)(2,1)} %wo.3) | copy-start | bytes 3145732
  20.5 2.9 %copy-start.5 = (s32[4,8]{1,0:T(4,128)S(1)}, s32[4,8]{1,0:T(4,128)}, u32[]{:S(2)}) copy-start(s32[4,8]{1,0:T(4,128)} %adjacency.1) | copy-start | bytes 388
  20.5 1.7 %collective-permute-start.8 = (bf16[64,1024]{1,0:T(8,128)(2,1)S(1)}, bf16[64,1024]{1,0:T(8,128)(2,1)S(1)}, u32[]{:S(2)}, u32[]{:S(2)}) collective-permute-start(bf16[64,1024]{1,0:T(8,128)(2,1)S(1)} %project.4), channel_id=1, source_target_pairs={{0,1},{1,0},{2,3},{3,2},{4,5},{5,4},{6,7},{7,6},{8,9},{9,8},{10,11... | collective-permute-start | bytes 393224 | tf_op jit(solution)/shard_map/ppermute | solution.py:483
  22.0 1.4 %collective-permute-start.6 = (bf16[64,1024]{1,0:T(8,128)(2,1)S(1)}, bf16[64,1024]{1,0:T(8,128)(2,1)S(1)}, u32[]{:S(2)}, u32[]{:S(2)}) collective-permute-start(bf16[64,1024]{1,0:T(8,128)(2,1)S(1)} %project.5), channel_id=1, source_target_pairs={{0,1},{1,0},{2,3},{3,2},{4,5},{5,4},{6,7},{7,6},{8,9},{9,8},{10,11... | collective-permute-start | bytes 393224 | tf_op jit(solution)/shard_map/ppermute | solution.py:483
  25.9 4.7 %collective-permute-start.10 = (bf16[4,80,128]{2,1,0:T(8,128)(2,1)S(1)}, bf16[4,80,128]{2,1,0:T(8,128)(2,1)S(1)}, u32[]{:S(2)}, u32[]{:S(2)}) collective-permute-start(bf16[4,80,128]{2,1,0:T(8,128)(2,1)S(1)} %get-tuple-element.60), channel_id=1, source_target_pairs={{0,2},{2,0},{1,3},{3,1},{4,6},{6,4},{5,7},{7,5},{8,10},{10,8},{9,1... | collective-permute-start | bytes 245768 | tf_op jit(solution)/shard_map/ppermute | solution.py:483
  26.5 0.7 %copy-start = (s32[4,1]{0,1:T(1,128)S(1)}, s32[4,1]{0,1:T(1,128)}, u32[]{:S(2)}) copy-start(s32[4,1]{0,1:T(1,128)} %param.12) | copy-start | bytes 52
  26.5 4.1 %copy-start.4 = (bf16[4,64,512]{2,1,0:T(8,128)(2,1)S(1)}, bf16[4,64,512]{2,1,0:T(8,128)(2,1)}, u32[]{:S(2)}) copy-start(bf16[4,64,512]{2,1,0:T(8,128)(2,1)} %grid_features.5) | copy-start | bytes 786436
  27.8 6.5 %collective-permute-start.9 = (bf16[4,176,128]{2,1,0:T(8,128)(2,1)S(1)}, bf16[4,176,128]{2,1,0:T(8,128)(2,1)S(1)}, u32[]{:S(2)}, u32[]{:S(2)}) collective-permute-start(bf16[4,176,128]{2,1,0:T(8,128)(2,1)S(1)} %get-tuple-element.58), channel_id=1, source_target_pairs={{0,2},{2,0},{1,3},{3,1},{4,6},{6,4},{5,7},{7,5},{8,10},{10,8},{9,1... | collective-permute-start | bytes 540680 | tf_op jit(solution)/shard_map/ppermute | solution.py:483
  30.7 8.4 %collective-permute-start.14 = (bf16[2,80,128]{2,1,0:T(8,128)(2,1)S(1)}, bf16[2,80,128]{2,1,0:T(8,128)(2,1)S(1)}, u32[]{:S(2)}, u32[]{:S(2)}) collective-permute-start(bf16[2,80,128]{2,1,0:T(8,128)(2,1)S(1)} %get-tuple-element.61), channel_id=1, source_target_pairs={{0,8},{4,12},{8,0},{12,4},{1,9},{5,13},{9,1},{13,5},{2,10},{6,14},... | collective-permute-start | bytes 122888 | tf_op jit(solution)/shard_map/ppermute | solution.py:479
  31.8 7.3 %collective-permute-start.15 = (bf16[2,80,128]{2,1,0:T(8,128)(2,1)S(1)}, bf16[2,80,128]{2,1,0:T(8,128)(2,1)S(1)}, u32[]{:S(2)}, u32[]{:S(2)}) collective-permute-start(bf16[2,80,128]{2,1,0:T(8,128)(2,1)S(1)} %get-tuple-element.67), channel_id=1, source_target_pairs={{0,12},{4,8},{8,4},{12,0},{1,13},{5,9},{9,5},{13,1},{2,14},{6,10},... | collective-permute-start | bytes 122888 | tf_op jit(solution)/shard_map/ppermute | solution.py:479
  34.4 8.4 %collective-permute-start.11 = (bf16[2,176,128]{2,1,0:T(8,128)(2,1)S(1)}, bf16[2,176,128]{2,1,0:T(8,128)(2,1)S(1)}, u32[]{:S(2)}, u32[]{:S(2)}) collective-permute-start(bf16[2,176,128]{2,1,0:T(8,128)(2,1)S(1)} %get-tuple-element.63), channel_id=1, source_target_pairs={{0,8},{4,12},{8,0},{12,4},{1,9},{5,13},{9,1},{13,5},{2,10},{6,14},... | collective-permute-start | bytes 270344 | tf_op jit(solution)/shard_map/ppermute | solution.py:479
  36.7 7.9 %collective-permute-start.13 = (bf16[2,256,128]{2,1,0:T(8,128)(2,1)S(1)}, bf16[2,256,128]{2,1,0:T(8,128)(2,1)S(1)}, u32[]{:S(2)}, u32[]{:S(2)}) collective-permute-start(bf16[2,256,128]{2,1,0:T(8,128)(2,1)S(1)} %get-tuple-element.66), channel_id=1, source_target_pairs={{0,4},{4,0},{8,12},{12,8},{1,5},{5,1},{9,13},{13,9},{2,6},{6,2},{1... | collective-permute-start | bytes 393224 | tf_op jit(solution)/shard_map/ppermute | solution.py:479
  37.8 6.7 %collective-permute-start.12 = (bf16[2,176,128]{2,1,0:T(8,128)(2,1)S(1)}, bf16[2,176,128]{2,1,0:T(8,128)(2,1)S(1)}, u32[]{:S(2)}, u32[]{:S(2)}) collective-permute-start(bf16[2,176,128]{2,1,0:T(8,128)(2,1)S(1)} %get-tuple-element.64), channel_id=1, source_target_pairs={{0,12},{4,8},{8,4},{12,0},{1,13},{5,9},{9,5},{13,1},{2,14},{6,10},... | collective-permute-start | bytes 270344 | tf_op jit(solution)/shard_map/ppermute | solution.py:479

commit v28 on v27

--- a/solution.py
+++ b/solution.py
@@ -50,8 +50,15 @@
     return pltpu.CompilerParams(vmem_limit_bytes=mib * MIB)
 
 
-def mlp_kernel(own, other, gain, wq, wup, wdn, q_out, mlp_out, normed_s):
+def mlp_kernel(own, other, gain, wq, wup, wdn, q_out, mlp_out, normed_s, wq_s, sem):
     half = own.shape[1]
+    h = lax.axis_index("head")
+    copies = []
+    for part, head in enumerate((1 - h, h)):
+        rows = pl.ds(pl.multiple_of(head * half, half), half)
+        target = wq_s.at[pl.ds(part * half, half), :]
+        copies.append(pltpu.make_async_copy(wq.at[rows, :], target, sem.at[part]))
+        copies[part].start()
     units = wup.shape[1]
     chunk = units // 4
     x_other = other[...].astype(jnp.float32)
@@ -68,7 +75,6 @@
     normed_s[:, :half] = (x_other * factor * gain[:, :half]).astype(jnp.bfloat16)
     normed_s[:, half:] = (x_own * factor * gain[:, half:]).astype(jnp.bfloat16)
     normed = normed_s[...]
-    q_out[...] = dot(normed, wq[...]).astype(jnp.bfloat16)
     for c in range(units // chunk):
         span = slice(c * chunk, (c + 1) * chunk)
         hidden = gelu(dot(normed, wup[:, span])).astype(jnp.bfloat16)
@@ -77,6 +83,9 @@
             mlp_out[...] = term
         else:
             mlp_out[...] += term
+    for copy in copies:
+        copy.wait()
+    q_out[...] = dot(normed, wq_s[...]).astype(jnp.bfloat16)
 
 
 def run_mlp(own, other, gain, wq, wup, wdn):
@@ -89,9 +98,13 @@
             jax.ShapeDtypeStruct((rows, wq.shape[1]), jnp.bfloat16),
             jax.ShapeDtypeStruct((rows, width), jnp.float32),
         ),
-        in_specs=vmem(6),
+        in_specs=vmem(3) + [whole(pltpu.HBM)] + vmem(2),
         out_specs=tuple(vmem(2)),
-        scratch_shapes=[pltpu.VMEM((rows, width), jnp.bfloat16)],
+        scratch_shapes=[
+            pltpu.VMEM((rows, width), jnp.bfloat16),
+            pltpu.VMEM(wq.shape, jnp.bfloat16),
+            pltpu.SemaphoreType.DMA((2,)),
+        ],
         compiler_params=params(16),
         cost_estimate=pl.CostEstimate(
             flops=2 * rows * width * (wq.shape[1] + 2 * units),
@@ -99,7 +112,7 @@
             transcendentals=rows * units,
         ),
         name="mlp",
-    )(own, other, gain, wq, wup, wdn)
+    )(own, other, gain, in_hbm(wq), wup, wdn)
 
 
 def pick_kernel(mesh, out, sem):
@@ -505,26 +518,18 @@
     near = crossed(waiting, 1, shards)
     waiting, _ = lax.optimization_barrier((flat, half_unit))
     other = swapped(waiting, "head")
-    flat, gain, wq, wup, wdn, mesh, rest = run_stage(
-        (
-            flat,
-            norm_gain.reshape(1, -1),
-            query_weight,
-            up_weight,
-            down_weight,
-            mesh_nodes,
-            mesh_nodes,
-        ),
-        (None, 1, 0, 0, 1, None, "rest"),
+    flat, gain, wup, wdn, rest = run_stage(
+        (flat, norm_gain.reshape(1, -1), up_weight, down_weight, mesh_nodes),
+        (None, 1, 0, 1, "rest"),
     )
     straight = crossed(rest, 3, shards)
     far, _ = lax.optimization_barrier((far, rest))
     farther = crossed(far, 1, shards)
     far_pair = swapped(far, "head")
-    queries, mlp = run_mlp(flat, other, gain, wq, wup, wdn)
+    queries, mlp = run_mlp(flat, other, gain, query_weight, wup, wdn)
     queries, mlp, far_pair, near = lax.optimization_barrier((queries, mlp, far_pair, near))
     blocked = (-1, BLOCK, 2 * half)
-    mine_a = run_project((mesh, near, far, far_pair), key_weight, value_weight)
+    mine_a = run_project((in_vmem(mesh_nodes), near, far, far_pair), key_weight, value_weight)
     sibling_a = swapped(mine_a, "sub")
     straight, _ = lax.optimization_barrier((straight, mine_a))
     mine_m = run_project((straight,), key_weight, value_weight)

time: 45.6 us -> 46.3 us (1.015)
  starting transfers between devices: 18.4 us -> 19.2 us
  waiting for transfers between devices: 10.8 us -> 10.1 us
  Pallas kernels: 15.8 us -> 16.4 us
    pallas_call x1, Pallas kernels: 3.33 us -> 4.34 us  [run_mlp(): pl.pallas_call(mlp_kernel, out_shape=(jax.ShapeDtypeStruct((rows, wq.shap...]
    ppermute x7, starting transfers between devices: 4.63 us -> 5.23 us  [swapped(): return lax.ppermute(x, axis, [(0, 1), (1, 0)])]
    ppermute x7, waiting for transfers between devices: 3.96 us -> 3.4 us  [swapped(): return lax.ppermute(x, axis, [(0, 1), (1, 0)])]
  transfers between devices with their start and end apart: 16 -> 16, of which waited for: 11 -> 9; matrix products, arithmetic and copies ran while one was open for 0% -> 0% of each run, Pallas kernels for 26% -> 26%
where the time goes in v28:
time: 46.3 us; the launch traced here: 46.1 us
  starting transfers between devices  19.2 us (41%)
  Pallas kernels  16.4 us (35%)
  waiting for transfers between devices  10.1 us (22%)
    ppermute x9, starting transfers between devices, crossed(): return lax.ppermute(x, 'shard', [(i, i ^ distance) for i in range(size)])  13.9 us
    ppermute x9, waiting for transfers between devices, crossed(): return lax.ppermute(x, 'shard', [(i, i ^ distance) for i in range(size)])  6.67 us
    ppermute x7, starting transfers between devices, swapped(): return lax.ppermute(x, axis, [(0, 1), (1, 0)])  5.23 us
    pallas_call x1, Pallas kernels, run_mlp(): pl.pallas_call(mlp_kernel, out_shape=(jax.ShapeDtypeStruct((rows, wq.shap...  4.34 us
    pallas_call x1, Pallas kernels, run_stage(): pl.pallas_call(functools.partial(stage_kernel, axes), out_shape=tuple((ja...  3.7 us
    ppermute x7, waiting for transfers between devices, swapped(): return lax.ppermute(x, axis, [(0, 1), (1, 0)])  3.4 us
    pallas_call x1, Pallas kernels, run_attend(): pl.pallas_call(attend_kernel, out_shape=(part, part, jax.ShapeDtypeStruct...  2.51 us
    pallas_call x3, Pallas kernels, run_project(): pl.pallas_call(project_kernel, out_shape=jax.ShapeDtypeStruct((rows, 2 *...  1.92 us
  transfers between devices with their start and end apart: 16, of which 9 were waited for; matrix products, arithmetic and copies ran while one was open for 0% of the time, Pallas kernels for 26%

profile of v28, /device:TPU:0, one launch (start us, length us, event | category | flops | bytes accessed | tf_op | source)
XLA Modules:
  0.0 46.1 jit_solution(3211613069543020605)
XLA Ops:
  0.0 0.9 %pick.1 = bf16[64,1024]{1,0:T(8,128)(2,1)S(1)} custom-call(bf16[128,1024]{1,0:T(8,128)(2,1)} %refs_0_.1), custom_call_target="tpu_custom_call" | custom-call | bytes 524288 | tf_op jit(solution)/shard_map/pick/pallas_call | solution.py:126
  0.9 4.1 %collective-permute-start.1 = (bf16[64,1024]{1,0:T(8,128)(2,1)S(1)}, bf16[64,1024]{1,0:T(8,128)(2,1)S(1)}, u32[]{:S(2)}, u32[]{:S(2)}) collective-permute-start(bf16[64,1024]{1,0:T(8,128)(2,1)S(1)} %pick.1), channel_id=1, source_target_pairs={{0,8},{4,12},{8,0},{12,4},{1,9},{5,13},{9,1},{13,5},{2,10},{6,14},... | collective-permute-start | bytes 393224 | tf_op jit(solution)/shard_map/ppermute | solution.py:492
  5.0 1.5 %collective-permute-start = (bf16[256,512]{1,0:T(8,128)(2,1)}, bf16[256,512]{1,0:T(8,128)(2,1)S(1)}, u32[]{:S(2)}, u32[]{:S(2)}) collective-permute-start(bf16[256,512]{1,0:T(8,128)(2,1)} %bitcast.14), channel_id=1, source_target_pairs={{0,2},{2,0},{1,3},{3,1},{4,6},{6,4},{5,7},{7,5},{8,10},{10,8},{9,1... | collective-permute-start | bytes 786440 | tf_op jit(solution)/shard_map/ppermute | solution.py:496
  6.5 1.6 %collective-permute-start.3 = (bf16[128,1024]{1,0:T(8,128)(2,1)}, bf16[128,1024]{1,0:T(8,128)(2,1)S(1)}, u32[]{:S(2)}, u32[]{:S(2)}) collective-permute-start(bf16[128,1024]{1,0:T(8,128)(2,1)} %refs_0_.1), channel_id=1, source_target_pairs={{0,4},{4,0},{8,12},{12,8},{1,5},{5,1},{9,13},{13,9},{2,6},{6,2},{1... | collective-permute-start | bytes 786440 | tf_op jit(solution)/shard_map/ppermute | solution.py:492
  8.1 3.7 %stage.1 = (bf16[256,512]{1,0:T(8,128)(2,1)S(1)}, f32[1,1024]{1,0:T(1,128)S(1)}, bf16[1024,2048]{1,0:T(8,128)(2,1)S(1)}, bf16[2048,1024]{1,0:T(8,128)(2,1)S(1)}, bf16[64,1024]{1,0:T(8,128)(2,1)S(1)}) custom-call(bf16[256,512]{1,0:T(8,128)(2,1)} %bitcast.15, f32[1,1024]{1,0:T(1,128)} %bitcast.18, bf16[1024,2048]{1,0:T(8,128)(2,1)} %refs_2_.3, ...), custom_call_target="tpu_custom_call" | custom-call | flops 17829888000 | bytes 178298880 | tf_op jit(solution)/shard_map/stage/pallas_call | solution.py:176
  11.8 0.3 collective-permute-start.5
  12.1 0.0 collective-permute-done.1.refs_2_
  12.1 0.9 %collective-permute-start.2 = (bf16[64,1024]{1,0:T(8,128)(2,1)S(1)}, bf16[64,1024]{1,0:T(8,128)(2,1)S(1)}, u32[]{:S(2)}, u32[]{:S(2)}) collective-permute-start(bf16[64,1024]{1,0:T(8,128)(2,1)S(1)} %collective-permute-done.1.refs_2_), channel_id=1, source_target_pairs={{0,2},{2,0},{1,3},{3,1},{4,6},{6,4},{5,7},{7,5},{8,10},{10,8},{9,1... | collective-permute-start | bytes 393224 | tf_op jit(solution)/shard_map/ppermute | solution.py:496
  13.0 0.7 %collective-permute-start.4 = (bf16[64,1024]{1,0:T(8,128)(2,1)S(1)}, bf16[64,1024]{1,0:T(8,128)(2,1)S(1)}, u32[]{:S(2)}, u32[]{:S(2)}) collective-permute-start(bf16[64,1024]{1,0:T(8,128)(2,1)S(1)} %collective-permute-done.1.refs_2_), channel_id=1, source_target_pairs={{0,4},{4,0},{8,12},{12,8},{1,5},{5,1},{9,13},{13,9},{2,6},{6,2},{1... | collective-permute-start | bytes 393224 | tf_op jit(solution)/shard_map/ppermute | solution.py:492
  13.7 0.0 collective-permute-done.other
  13.7 0.0 copy-start
  13.7 0.0 copy-start.2
  13.7 0.0 copy-start.3
  13.7 4.3 %mlp.1 = (bf16[256,512]{1,0:T(8,128)(2,1)S(1)}, f32[256,1024]{1,0:T(8,128)S(1)}) custom-call(bf16[256,512]{1,0:T(8,128)(2,1)S(1)} %get-tuple-element.35.own, bf16[256,512]{1,0:T(8,128)(2,1)S(1)} %collective-permute-done.other, f32[1,1024]{1,0:T(1,128)S(1)} %get-tuple-element.37.gain, bf16[1024,512]{1,0:T(8,128)(2,1)} %wq.1, ...), custom_call_target="tpu_custom_call" | custom-call | flops 2415919104 | bytes 9437184 | tf_op jit(solution)/shard_map/mlp/pallas_call | solution.py:95
  18.0 0.0 collective-permute-done.2.refs_3_
  18.0 1.1 %collective-permute-done.3.refs_1_ = bf16[128,1024]{1,0:T(8,128)(2,1)S(1)} collective-permute-done((bf16[128,1024]{1,0:T(8,128)(2,1)}, bf16[128,1024]{1,0:T(8,128)(2,1)S(1)}, u32[]{:S(2)}, u32[]{:S(2)}) %collective-permute-start.3) | collective-permute-done | bytes 262176 | tf_op jit(solution)/shard_map/ppermute | solution.py:492
  19.2 0.0 copy-done
  19.2 0.0 copy-done.2
  19.2 0.0 copy-done.3
  19.2 1.0 %project.3 = bf16[384,1024]{1,0:T(8,128)(2,1)S(1)} custom-call(bf16[128,1024]{1,0:T(8,128)(2,1)S(1)} %copy-done, bf16[128,1024]{1,0:T(8,128)(2,1)S(1)} %collective-permute-done.3.refs_1_, bf16[64,1024]{1,0:T(8,128)(2,1)S(1)} %collective-permute-done.1.refs_2_, bf16[64,1024]{1,0:T(8,128)(2,1)S(1)} %collective-permute-done.2.refs_3_, ...), custom_call_target="tpu_custom_call" | custom-call | flops 60397977600 | bytes 275251200 | tf_op jit(solution)/shard_map/project/pallas_call | solution.py:204
  20.2 0.1 collective-permute-start.7
  20.2 0.0 collective-permute-done.5.refs_0_
  20.2 0.5 %project.4 = bf16[64,1024]{1,0:T(8,128)(2,1)S(1)} custom-call(bf16[64,1024]{1,0:T(8,128)(2,1)S(1)} %collective-permute-done.5.refs_0_, bf16[1024,512]{1,0:T(8,128)(2,1)S(1)} %copy-done.2, bf16[1024,512]{1,0:T(8,128)(2,1)S(1)} %copy-done.3), custom_call_target="tpu_custom_call" | custom-call | flops 10066329600 | bytes 176947200 | tf_op jit(solution)/shard_map/project/pallas_call | solution.py:204
  20.7 0.0 copy-start.4
  20.7 0.0 copy-start.6
  20.8 0.6 %collective-permute-start.8 = (bf16[64,1024]{1,0:T(8,128)(2,1)S(1)}, bf16[64,1024]{1,0:T(8,128)(2,1)S(1)}, u32[]{:S(2)}, u32[]{:S(2)}) collective-permute-start(bf16[64,1024]{1,0:T(8,128)(2,1)S(1)} %project.4), channel_id=1, source_target_pairs={{0,1},{1,0},{2,3},{3,2},{4,5},{5,4},{6,7},{7,6},{8,9},{9,8},{10,11... | collective-permute-start | bytes 393224 | tf_op jit(solution)/shard_map/ppermute | solution.py:496
  21.3 0.2 collective-permute-done.4.refs_0_
  21.5 0.5 %project.5 = bf16[64,1024]{1,0:T(8,128)(2,1)S(1)} custom-call(bf16[64,1024]{1,0:T(8,128)(2,1)S(1)} %collective-permute-done.4.refs_0_, bf16[1024,512]{1,0:T(8,128)(2,1)S(1)} %copy-done.2, bf16[1024,512]{1,0:T(8,128)(2,1)S(1)} %copy-done.3), custom_call_target="tpu_custom_call" | custom-call | flops 10066329600 | bytes 176947200 | tf_op jit(solution)/shard_map/project/pallas_call | solution.py:204
  22.0 0.1 collective-permute-start.6
  22.0 0.7 %collective-permute-done.8 = bf16[64,1024]{1,0:T(8,128)(2,1)S(1)} collective-permute-done((bf16[64,1024]{1,0:T(8,128)(2,1)S(1)}, bf16[64,1024]{1,0:T(8,128)(2,1)S(1)}, u32[]{:S(2)}, u32[]{:S(2)}) %collective-permute-start.8) | collective-permute-done | bytes 131104 | tf_op jit(solution)/shard_map/ppermute | solution.py:496
  22.7 0.0 collective-permute-done.7
  22.7 0.1 table.1.table_in
  22.8 0.5 %collective-permute-done.6 = bf16[64,1024]{1,0:T(8,128)(2,1)S(1)} collective-permute-done((bf16[64,1024]{1,0:T(8,128)(2,1)S(1)}, bf16[64,1024]{1,0:T(8,128)(2,1)S(1)}, u32[]{:S(2)}, u32[]{:S(2)}) %collective-permute-start.6) | collective-permute-done | bytes 131104 | tf_op jit(solution)/shard_map/ppermute | solution.py:496
  23.4 0.0 copy-done.4
  23.4 0.0 copy-done.6
  23.4 2.5 %attend.1 = (bf16[4,80,128]{2,1,0:T(8,128)(2,1)S(1)}, bf16[4,80,128]{2,1,0:T(8,128)(2,1)S(1)}, bf16[256,512]{1,0:T(8,128)(2,1)S(1)}, bf16[2,8,64,1024]{3,2,1,0:T(8,128)(2,1)S(1)}) custom-call(s32[4,8]{1,0:T(4,128)S(1)} %copy-done.6, bf16[256,512]{1,0:T(8,128)(2,1)S(1)} %get-tuple-element.45.q, ...), custom_call_target="tpu_custom_call", output_to_operand_aliasing={{3}: (4, {})} | custom-call | flops 13421772800 | bytes 41943040 | tf_op jit(solution)/shard_map/attend/pallas_call | solution.py:339
  25.9 0.8 %collective-permute-start.10 = (bf16[4,80,128]{2,1,0:T(8,128)(2,1)S(1)}, bf16[4,80,128]{2,1,0:T(8,128)(2,1)S(1)}, u32[]{:S(2)}, u32[]{:S(2)}) collective-permute-start(bf16[4,80,128]{2,1,0:T(8,128)(2,1)S(1)} %get-tuple-element.56), channel_id=1, source_target_pairs={{0,2},{2,0},{1,3},{3,1},{4,6},{6,4},{5,7},{7,5},{8,10},{10,8},{9,1... | collective-permute-start | bytes 245768 | tf_op jit(solution)/shard_map/ppermute | solution.py:496
  26.7 0.0 copy-start.1
  26.7 0.0 copy-start.5
  26.7 0.4 project_out.1
  27.1 0.2 copy-done.1
  27.3 0.6 %plan.1.masks = f32[4,2,4,8,128]{4,3,2,1,0:T(8,128)S(1)} custom-call(s32[1,4]{1,0:T(1,128)S(1)} %bitcast.13), custom_call_target="tpu_custom_call" | custom-call | bytes 262144 | tf_op jit(solution)/shard_map/plan/pallas_call | solution.py:399
  27.9 1.4 %collective-permute-start.9 = (bf16[4,176,128]{2,1,0:T(8,128)(2,1)S(1)}, bf16[4,176,128]{2,1,0:T(8,128)(2,1)S(1)}, u32[]{:S(2)}, u32[]{:S(2)}) collective-permute-start(bf16[4,176,128]{2,1,0:T(8,128)(2,1)S(1)} %get-tuple-element.54), channel_id=1, source_target_pairs={{0,2},{2,0},{1,3},{3,1},{4,6},{6,4},{5,7},{7,5},{8,10},{10,8},{9,1... | collective-permute-start | bytes 540680 | tf_op jit(solution)/shard_map/ppermute | solution.py:496
  29.3 1.2 %collective-permute-done.10.refs_1_.refs_2_ = bf16[4,80,128]{2,1,0:T(8,128)(2,1)S(1)} collective-permute-done((bf16[4,80,128]{2,1,0:T(8,128)(2,1)S(1)}, bf16[4,80,128]{2,1,0:T(8,128)(2,1)S(1)}, u32[]{:S(2)}, u32[]{:S(2)}) %collective-permute-start.10) | collective-permute-done | bytes 81952 | tf_op jit(solution)/shard_map/ppermute | solution.py:496
  30.5 0.0 copy-done.5
  30.5 0.1 combine.3
  30.5 2.2 %collective-permute-start.14 = (bf16[2,80,128]{2,1,0:T(8,128)(2,1)S(1)}, bf16[2,80,128]{2,1,0:T(8,128)(2,1)S(1)}, u32[]{:S(2)}, u32[]{:S(2)}) collective-permute-start(bf16[2,80,128]{2,1,0:T(8,128)(2,1)S(1)} %get-tuple-element.57), channel_id=1, source_target_pairs={{0,8},{4,12},{8,0},{12,4},{1,9},{5,13},{9,1},{13,5},{2,10},{6,14},... | collective-permute-start | bytes 122888 | tf_op jit(solution)/shard_map/ppermute | solution.py:492
  32.7 0.6 %collective-permute-start.15 = (bf16[2,80,128]{2,1,0:T(8,128)(2,1)S(1)}, bf16[2,80,128]{2,1,0:T(8,128)(2,1)S(1)}, u32[]{:S(2)}, u32[]{:S(2)}) collective-permute-start(bf16[2,80,128]{2,1,0:T(8,128)(2,1)S(1)} %get-tuple-element.63), channel_id=1, source_target_pairs={{0,12},{4,8},{8,4},{12,0},{1,13},{5,9},{9,5},{13,1},{2,14},{6,10},... | collective-permute-start | bytes 122888 | tf_op jit(solution)/shard_map/ppermute | solution.py:492
  33.3 1.0 %collective-permute-done.9.refs_1_.refs_3_ = bf16[4,176,128]{2,1,0:T(8,128)(2,1)S(1)} collective-permute-done((bf16[4,176,128]{2,1,0:T(8,128)(2,1)S(1)}, bf16[4,176,128]{2,1,0:T(8,128)(2,1)S(1)}, u32[]{:S(2)}, u32[]{:S(2)}) %collective-permute-start.9) | collective-permute-done | bytes 180256 | tf_op jit(solution)/shard_map/ppermute | solution.py:496
  34.3 0.1 combine.4
  34.4 2.7 %collective-permute-start.11 = (bf16[2,176,128]{2,1,0:T(8,128)(2,1)S(1)}, bf16[2,176,128]{2,1,0:T(8,128)(2,1)S(1)}, u32[]{:S(2)}, u32[]{:S(2)}) collective-permute-start(bf16[2,176,128]{2,1,0:T(8,128)(2,1)S(1)} %get-tuple-element.59), channel_id=1, source_target_pairs={{0,8},{4,12},{8,0},{12,4},{1,9},{5,13},{9,1},{13,5},{2,10},{6,14},... | collective-permute-start | bytes 270344 | tf_op jit(solution)/shard_map/ppermute | solution.py:492
  37.1 0.2 combine.5
  37.3 0.5 %collective-permute-start.13 = (bf16[2,256,128]{2,1,0:T(8,128)(2,1)S(1)}, bf16[2,256,128]{2,1,0:T(8,128)(2,1)S(1)}, u32[]{:S(2)}, u32[]{:S(2)}) collective-permute-start(bf16[2,256,128]{2,1,0:T(8,128)(2,1)S(1)} %get-tuple-element.62), channel_id=1, source_target_pairs={{0,4},{4,0},{8,12},{12,8},{1,5},{5,1},{9,13},{13,9},{2,6},{6,2},{1... | collective-permute-start | bytes 393224 | tf_op jit(solution)/shard_map/ppermute | solution.py:492
  37.8 1.3 %collective-permute-start.12 = (bf16[2,176,128]{2,1,0:T(8,128)(2,1)S(1)}, bf16[2,176,128]{2,1,0:T(8,128)(2,1)S(1)}, u32[]{:S(2)}, u32[]{:S(2)}) collective-permute-start(bf16[2,176,128]{2,1,0:T(8,128)(2,1)S(1)} %get-tuple-element.60), channel_id=1, source_target_pairs={{0,12},{4,8},{8,4},{12,0},{1,13},{5,9},{9,5},{13,1},{2,14},{6,10},... | collective-permute-start | bytes 270344 | tf_op jit(solution)/shard_map/ppermute | solution.py:492
  39.1 0.0 collective-permute-done.14.refs_0_
  39.1 0.0 collective-permute-done.15.refs_1_
  39.1 0.8 %place.2.refs_3_ = bf16[8,64,512]{2,1,0:T(8,128)(2,1)} custom-call(bf16[2,80,128]{2,1,0:T(8,128)(2,1)S(1)} %collective-permute-done.14.refs_0_, bf16[2,80,128]{2,1,0:T(8,128)(2,1)S(1)} %collective-permute-done.15.refs_1_, bf16[2,256,128]{2,1,0:T(8,128)(2,1)S(1)} %get-tuple-element.64.refs_2_), custom_call_target="tpu_custom_call" | custom-call | flops 42598400000 | tf_op jit(solution)/shard_map/place/pallas_call | solution.py:476
  39.9 2.8 %collective-permute-done.11.refs_0_ = bf16[2,176,128]{2,1,0:T(8,128)(2,1)S(1)} collective-permute-done((bf16[2,176,128]{2,1,0:T(8,128)(2,1)S(1)}, bf16[2,176,128]{2,1,0:T(8,128)(2,1)S(1)}, u32[]{:S(2)}, u32[]{:S(2)}) %collective-permute-start.11) | collective-permute-done | bytes 90144 | tf_op jit(solution)/shard_map/ppermute | solution.py:492
  42.7 1.9 %collective-permute-done.12.refs_1_ = bf16[2,176,128]{2,1,0:T(8,128)(2,1)S(1)} collective-permute-done((bf16[2,176,128]{2,1,0:T(8,128)(2,1)S(1)}, bf16[2,176,128]{2,1,0:T(8,128)(2,1)S(1)}, u32[]{:S(2)}, u32[]{:S(2)}) %collective-permute-start.12) | collective-permute-done | bytes 90144 | tf_op jit(solution)/shard_map/ppermute | solution.py:492
  44.6 0.7 %collective-permute-done.13.refs_2_ = bf16[2,256,128]{2,1,0:T(8,128)(2,1)S(1)} collective-permute-done((bf16[2,256,128]{2,1,0:T(8,128)(2,1)S(1)}, bf16[2,256,128]{2,1,0:T(8,128)(2,1)S(1)}, u32[]{:S(2)}, u32[]{:S(2)}) %collective-permute-start.13) | collective-permute-done | bytes 131104 | tf_op jit(solution)/shard_map/ppermute | solution.py:492
  45.3 0.8 %place.3 = bf16[8,64,512]{2,1,0:T(8,128)(2,1)} custom-call(bf16[2,176,128]{2,1,0:T(8,128)(2,1)S(1)} %collective-permute-done.11.refs_0_, bf16[2,176,128]{2,1,0:T(8,128)(2,1)S(1)} %collective-permute-done.12.refs_1_, bf16[2,256,128]{2,1,0:T(8,128)(2,1)S(1)} %collective-permute-done.13.refs_2_, ...), custom_call_target="tpu_custom_call", output_to_operand_aliasing={{}: (3, {})} | custom-call | flops 62259200000 | tf_op jit(solution)/shard_map/place/pallas_call | solution.py:476
Async XLA Ops:
  0.9 11.2 %collective-permute-start.1 = (bf16[64,1024]{1,0:T(8,128)(2,1)S(1)}, bf16[64,1024]{1,0:T(8,128)(2,1)S(1)}, u32[]{:S(2)}, u32[]{:S(2)}) collective-permute-start(bf16[64,1024]{1,0:T(8,128)(2,1)S(1)} %pick.1), channel_id=1, source_target_pairs={{0,8},{4,12},{8,0},{12,4},{1,9},{5,13},{9,1},{13,5},{2,10},{6,14},... | collective-permute-start | bytes 393224 | tf_op jit(solution)/shard_map/ppermute | solution.py:492
  5.0 8.7 %collective-permute-start = (bf16[256,512]{1,0:T(8,128)(2,1)}, bf16[256,512]{1,0:T(8,128)(2,1)S(1)}, u32[]{:S(2)}, u32[]{:S(2)}) collective-permute-start(bf16[256,512]{1,0:T(8,128)(2,1)} %bitcast.14), channel_id=1, source_target_pairs={{0,2},{2,0},{1,3},{3,1},{4,6},{6,4},{5,7},{7,5},{8,10},{10,8},{9,1... | collective-permute-start | bytes 786440 | tf_op jit(solution)/shard_map/ppermute | solution.py:496
  6.5 12.6 %collective-permute-start.3 = (bf16[128,1024]{1,0:T(8,128)(2,1)}, bf16[128,1024]{1,0:T(8,128)(2,1)S(1)}, u32[]{:S(2)}, u32[]{:S(2)}) collective-permute-start(bf16[128,1024]{1,0:T(8,128)(2,1)} %refs_0_.1), channel_id=1, source_target_pairs={{0,4},{4,0},{8,12},{12,8},{1,5},{5,1},{9,13},{13,9},{2,6},{6,2},{1... | collective-permute-start | bytes 786440 | tf_op jit(solution)/shard_map/ppermute | solution.py:492
  11.8 8.4 %collective-permute-start.5 = (bf16[64,1024]{1,0:T(8,128)(2,1)S(1)}, bf16[64,1024]{1,0:T(8,128)(2,1)S(1)}, u32[]{:S(2)}, u32[]{:S(2)}) collective-permute-start(bf16[64,1024]{1,0:T(8,128)(2,1)S(1)} %get-tuple-element.42), channel_id=1, source_target_pairs={{0,12},{4,8},{8,4},{12,0},{1,13},{5,9},{9,5},{13,1},{2,14},{6,10},... | collective-permute-start | bytes 393224 | tf_op jit(solution)/shard_map/ppermute | solution.py:492
  12.1 6.0 %collective-permute-start.2 = (bf16[64,1024]{1,0:T(8,128)(2,1)S(1)}, bf16[64,1024]{1,0:T(8,128)(2,1)S(1)}, u32[]{:S(2)}, u32[]{:S(2)}) collective-permute-start(bf16[64,1024]{1,0:T(8,128)(2,1)S(1)} %collective-permute-done.1.refs_2_), channel_id=1, source_target_pairs={{0,2},{2,0},{1,3},{3,1},{4,6},{6,4},{5,7},{7,5},{8,10},{10,8},{9,1... | collective-permute-start | bytes 393224 | tf_op jit(solution)/shard_map/ppermute | solution.py:496
  13.0 8.5 %collective-permute-start.4 = (bf16[64,1024]{1,0:T(8,128)(2,1)S(1)}, bf16[64,1024]{1,0:T(8,128)(2,1)S(1)}, u32[]{:S(2)}, u32[]{:S(2)}) collective-permute-start(bf16[64,1024]{1,0:T(8,128)(2,1)S(1)} %collective-permute-done.1.refs_2_), channel_id=1, source_target_pairs={{0,4},{4,0},{8,12},{12,8},{1,5},{5,1},{9,13},{13,9},{2,6},{6,2},{1... | collective-permute-start | bytes 393224 | tf_op jit(solution)/shard_map/ppermute | solution.py:492
  13.7 5.5 %copy-start = (bf16[128,1024]{1,0:T(8,128)(2,1)S(1)}, bf16[128,1024]{1,0:T(8,128)(2,1)}, u32[]{:S(2)}) copy-start(bf16[128,1024]{1,0:T(8,128)(2,1)} %refs_0_.1) | copy-start | bytes 786436
  13.7 5.5 %copy-start.2 = (bf16[1024,512]{1,0:T(8,128)(2,1)S(1)}, bf16[1024,512]{1,0:T(8,128)(2,1)}, u32[]{:S(2)}) copy-start(bf16[1024,512]{1,0:T(8,128)(2,1)} %refs_1_.3) | copy-start | bytes 3145732
  13.7 5.5 %copy-start.3 = (bf16[1024,512]{1,0:T(8,128)(2,1)S(1)}, bf16[1024,512]{1,0:T(8,128)(2,1)}, u32[]{:S(2)}) copy-start(bf16[1024,512]{1,0:T(8,128)(2,1)} %refs_2_.5) | copy-start | bytes 3145732
  20.2 2.5 %collective-permute-start.7 = (bf16[384,1024]{1,0:T(8,128)(2,1)S(1)}, bf16[384,1024]{1,0:T(8,128)(2,1)S(1)}, u32[]{:S(2)}, u32[]{:S(2)}) collective-permute-start(bf16[384,1024]{1,0:T(8,128)(2,1)S(1)} %project.3), channel_id=1, source_target_pairs={{0,1},{1,0},{2,3},{3,2},{4,5},{5,4},{6,7},{7,6},{8,9},{9,8},{10,11... | collective-permute-start | bytes 2359304 | tf_op jit(solution)/shard_map/ppermute | solution.py:496
  20.7 2.6 %copy-start.4 = (bf16[512,1024]{1,0:T(8,128)(2,1)S(1)}, bf16[512,1024]{1,0:T(8,128)(2,1)}, u32[]{:S(2)}) copy-start(bf16[512,1024]{1,0:T(8,128)(2,1)} %wo.3) | copy-start | bytes 3145732
  20.7 2.6 %copy-start.6 = (s32[4,8]{1,0:T(4,128)S(1)}, s32[4,8]{1,0:T(4,128)}, u32[]{:S(2)}) copy-start(s32[4,8]{1,0:T(4,128)} %adjacency.1) | copy-start | bytes 388
  20.8 1.9 %collective-permute-start.8 = (bf16[64,1024]{1,0:T(8,128)(2,1)S(1)}, bf16[64,1024]{1,0:T(8,128)(2,1)S(1)}, u32[]{:S(2)}, u32[]{:S(2)}) collective-permute-start(bf16[64,1024]{1,0:T(8,128)(2,1)S(1)} %project.4), channel_id=1, source_target_pairs={{0,1},{1,0},{2,3},{3,2},{4,5},{5,4},{6,7},{7,6},{8,9},{9,8},{10,11... | collective-permute-start | bytes 393224 | tf_op jit(solution)/shard_map/ppermute | solution.py:496
  22.0 1.4 %collective-permute-start.6 = (bf16[64,1024]{1,0:T(8,128)(2,1)S(1)}, bf16[64,1024]{1,0:T(8,128)(2,1)S(1)}, u32[]{:S(2)}, u32[]{:S(2)}) collective-permute-start(bf16[64,1024]{1,0:T(8,128)(2,1)S(1)} %project.5), channel_id=1, source_target_pairs={{0,1},{1,0},{2,3},{3,2},{4,5},{5,4},{6,7},{7,6},{8,9},{9,8},{10,11... | collective-permute-start | bytes 393224 | tf_op jit(solution)/shard_map/ppermute | solution.py:496
  25.9 4.6 %collective-permute-start.10 = (bf16[4,80,128]{2,1,0:T(8,128)(2,1)S(1)}, bf16[4,80,128]{2,1,0:T(8,128)(2,1)S(1)}, u32[]{:S(2)}, u32[]{:S(2)}) collective-permute-start(bf16[4,80,128]{2,1,0:T(8,128)(2,1)S(1)} %get-tuple-element.56), channel_id=1, source_target_pairs={{0,2},{2,0},{1,3},{3,1},{4,6},{6,4},{5,7},{7,5},{8,10},{10,8},{9,1... | collective-permute-start | bytes 245768 | tf_op jit(solution)/shard_map/ppermute | solution.py:496
  26.7 0.7 %copy-start.1 = (s32[4,1]{0,1:T(1,128)S(1)}, s32[4,1]{0,1:T(1,128)}, u32[]{:S(2)}) copy-start(s32[4,1]{0,1:T(1,128)} %param.12) | copy-start | bytes 52
  26.7 3.8 %copy-start.5 = (bf16[4,64,512]{2,1,0:T(8,128)(2,1)S(1)}, bf16[4,64,512]{2,1,0:T(8,128)(2,1)}, u32[]{:S(2)}) copy-start(bf16[4,64,512]{2,1,0:T(8,128)(2,1)} %grid_features.5) | copy-start | bytes 786436
  27.9 6.4 %collective-permute-start.9 = (bf16[4,176,128]{2,1,0:T(8,128)(2,1)S(1)}, bf16[4,176,128]{2,1,0:T(8,128)(2,1)S(1)}, u32[]{:S(2)}, u32[]{:S(2)}) collective-permute-start(bf16[4,176,128]{2,1,0:T(8,128)(2,1)S(1)} %get-tuple-element.54), channel_id=1, source_target_pairs={{0,2},{2,0},{1,3},{3,1},{4,6},{6,4},{5,7},{7,5},{8,10},{10,8},{9,1... | collective-permute-start | bytes 540680 | tf_op jit(solution)/shard_map/ppermute | solution.py:496
  30.5 8.6 %collective-permute-start.14 = (bf16[2,80,128]{2,1,0:T(8,128)(2,1)S(1)}, bf16[2,80,128]{2,1,0:T(8,128)(2,1)S(1)}, u32[]{:S(2)}, u32[]{:S(2)}) collective-permute-start(bf16[2,80,128]{2,1,0:T(8,128)(2,1)S(1)} %get-tuple-element.57), channel_id=1, source_target_pairs={{0,8},{4,12},{8,0},{12,4},{1,9},{5,13},{9,1},{13,5},{2,10},{6,14},... | collective-permute-start | bytes 122888 | tf_op jit(solution)/shard_map/ppermute | solution.py:492
  32.7 6.4 %collective-permute-start.15 = (bf16[2,80,128]{2,1,0:T(8,128)(2,1)S(1)}, bf16[2,80,128]{2,1,0:T(8,128)(2,1)S(1)}, u32[]{:S(2)}, u32[]{:S(2)}) collective-permute-start(bf16[2,80,128]{2,1,0:T(8,128)(2,1)S(1)} %get-tuple-element.63), channel_id=1, source_target_pairs={{0,12},{4,8},{8,4},{12,0},{1,13},{5,9},{9,5},{13,1},{2,14},{6,10},... | collective-permute-start | bytes 122888 | tf_op jit(solution)/shard_map/ppermute | solution.py:492
  34.4 8.3 %collective-permute-start.11 = (bf16[2,176,128]{2,1,0:T(8,128)(2,1)S(1)}, bf16[2,176,128]{2,1,0:T(8,128)(2,1)S(1)}, u32[]{:S(2)}, u32[]{:S(2)}) collective-permute-start(bf16[2,176,128]{2,1,0:T(8,128)(2,1)S(1)} %get-tuple-element.59), channel_id=1, source_target_pairs={{0,8},{4,12},{8,0},{12,4},{1,9},{5,13},{9,1},{13,5},{2,10},{6,14},... | collective-permute-start | bytes 270344 | tf_op jit(solution)/shard_map/ppermute | solution.py:492
  37.3 8.0 %collective-permute-start.13 = (bf16[2,256,128]{2,1,0:T(8,128)(2,1)S(1)}, bf16[2,256,128]{2,1,0:T(8,128)(2,1)S(1)}, u32[]{:S(2)}, u32[]{:S(2)}) collective-permute-start(bf16[2,256,128]{2,1,0:T(8,128)(2,1)S(1)} %get-tuple-element.62), channel_id=1, source_target_pairs={{0,4},{4,0},{8,12},{12,8},{1,5},{5,1},{9,13},{13,9},{2,6},{6,2},{1... | collective-permute-start | bytes 393224 | tf_op jit(solution)/shard_map/ppermute | solution.py:492
  37.8 6.8 %collective-permute-start.12 = (bf16[2,176,128]{2,1,0:T(8,128)(2,1)S(1)}, bf16[2,176,128]{2,1,0:T(8,128)(2,1)S(1)}, u32[]{:S(2)}, u32[]{:S(2)}) collective-permute-start(bf16[2,176,128]{2,1,0:T(8,128)(2,1)S(1)} %get-tuple-element.60), channel_id=1, source_target_pairs={{0,12},{4,8},{8,4},{12,0},{1,13},{5,9},{9,5},{13,1},{2,14},{6,10},... | collective-permute-start | bytes 270344 | tf_op jit(solution)/shard_map/ppermute | solution.py:492

commit v29 on v27

--- a/solution.py
+++ b/solution.py
@@ -68,7 +68,12 @@
     normed_s[:, :half] = (x_other * factor * gain[:, :half]).astype(jnp.bfloat16)
     normed_s[:, half:] = (x_own * factor * gain[:, half:]).astype(jnp.bfloat16)
     normed = normed_s[...]
-    q_out[...] = dot(normed, wq[...]).astype(jnp.bfloat16)
+    h = lax.axis_index("head")
+    queries = jnp.zeros(q_out.shape, jnp.float32)
+    for part, head in enumerate((1 - h, h)):
+        rows = pl.ds(pl.multiple_of(head * half, half), half)
+        queries += dot(normed_s[:, part * half : (part + 1) * half], wq[rows, :])
+    q_out[...] = queries.astype(jnp.bfloat16)
     for c in range(units // chunk):
         span = slice(c * chunk, (c + 1) * chunk)
         hidden = gelu(dot(normed, wup[:, span])).astype(jnp.bfloat16)
@@ -99,7 +104,7 @@
             transcendentals=rows * units,
         ),
         name="mlp",
-    )(own, other, gain, wq, wup, wdn)
+    )(own, other, gain, in_vmem(wq), wup, wdn)
 
 
 def pick_kernel(mesh, out, sem):
@@ -505,26 +510,18 @@
     near = crossed(waiting, 1, shards)
     waiting, _ = lax.optimization_barrier((flat, half_unit))
     other = swapped(waiting, "head")
-    flat, gain, wq, wup, wdn, mesh, rest = run_stage(
-        (
-            flat,
-            norm_gain.reshape(1, -1),
-            query_weight,
-            up_weight,
-            down_weight,
-            mesh_nodes,
-            mesh_nodes,
-        ),
-        (None, 1, 0, 0, 1, None, "rest"),
+    flat, gain, wup, wdn, rest = run_stage(
+        (flat, norm_gain.reshape(1, -1), up_weight, down_weight, mesh_nodes),
+        (None, 1, 0, 1, "rest"),
     )
     straight = crossed(rest, 3, shards)
     far, _ = lax.optimization_barrier((far, rest))
     farther = crossed(far, 1, shards)
     far_pair = swapped(far, "head")
-    queries, mlp = run_mlp(flat, other, gain, wq, wup, wdn)
+    queries, mlp = run_mlp(flat, other, gain, query_weight, wup, wdn)
     queries, mlp, far_pair, near = lax.optimization_barrier((queries, mlp, far_pair, near))
     blocked = (-1, BLOCK, 2 * half)
-    mine_a = run_project((mesh, near, far, far_pair), key_weight, value_weight)
+    mine_a = run_project((in_vmem(mesh_nodes), near, far, far_pair), key_weight, value_weight)
     sibling_a = swapped(mine_a, "sub")
     straight, _ = lax.optimization_barrier((straight, mine_a))
     mine_m = run_project((straight,), key_weight, value_weight)

time: 45.6 us -> 45.5 us (level)
  starting transfers between devices: 18.4 us -> 18.9 us
    ppermute x7, starting transfers between devices: 4.63 us -> 5.15 us  [swapped(): return lax.ppermute(x, axis, [(0, 1), (1, 0)])]
  transfers between devices with their start and end apart: 16 -> 16, of which waited for: 11 -> 10; matrix products, arithmetic and copies ran while one was open for 0% -> 0% of each run, Pallas kernels for 26% -> 25%
where the time goes in v29:
time: 45.5 us; the launch traced here: 45.3 us
  starting transfers between devices  18.9 us (42%)
  Pallas kernels  15.5 us (34%)
  waiting for transfers between devices  10.4 us (23%)
    ppermute x9, starting transfers between devices, crossed(): return lax.ppermute(x, 'shard', [(i, i ^ distance) for i in range(size)])  13.8 us
    ppermute x9, waiting for transfers between devices, crossed(): return lax.ppermute(x, 'shard', [(i, i ^ distance) for i in range(size)])  6.8 us
    ppermute x7, starting transfers between devices, swapped(): return lax.ppermute(x, axis, [(0, 1), (1, 0)])  5.15 us
    pallas_call x1, Pallas kernels, run_stage(): pl.pallas_call(functools.partial(stage_kernel, axes), out_shape=tuple((ja...  3.77 us
    ppermute x7, waiting for transfers between devices, swapped(): return lax.ppermute(x, axis, [(0, 1), (1, 0)])  3.63 us
    pallas_call x1, Pallas kernels, run_mlp(): pl.pallas_call(mlp_kernel, out_shape=(jax.ShapeDtypeStruct((rows, wq.shap...  3.34 us
    pallas_call x1, Pallas kernels, run_attend(): pl.pallas_call(attend_kernel, out_shape=(part, part, jax.ShapeDtypeStruct...  2.51 us
    pallas_call x3, Pallas kernels, run_project(): pl.pallas_call(project_kernel, out_shape=jax.ShapeDtypeStruct((rows, 2 *...  1.92 us
  transfers between devices with their start and end apart: 16, of which 10 were waited for; matrix products, arithmetic and copies ran while one was open for 0% of the time, Pallas kernels for 25%

profile of v29, /device:TPU:0, one launch (start us, length us, event | category | flops | bytes accessed | tf_op | source)
XLA Modules:
  0.0 45.3 jit_solution(45392611437900471)
XLA Ops:
  0.0 0.9 %pick.1 = bf16[64,1024]{1,0:T(8,128)(2,1)S(1)} custom-call(bf16[128,1024]{1,0:T(8,128)(2,1)} %refs_0_.1), custom_call_target="tpu_custom_call" | custom-call | bytes 524288 | tf_op jit(solution)/shard_map/pick/pallas_call | solution.py:118
  0.9 4.1 %collective-permute-start.1 = (bf16[64,1024]{1,0:T(8,128)(2,1)S(1)}, bf16[64,1024]{1,0:T(8,128)(2,1)S(1)}, u32[]{:S(2)}, u32[]{:S(2)}) collective-permute-start(bf16[64,1024]{1,0:T(8,128)(2,1)S(1)} %pick.1), channel_id=1, source_target_pairs={{0,8},{4,12},{8,0},{12,4},{1,9},{5,13},{9,1},{13,5},{2,10},{6,14},... | collective-permute-start | bytes 393224 | tf_op jit(solution)/shard_map/ppermute | solution.py:484
  5.0 1.5 %collective-permute-start = (bf16[256,512]{1,0:T(8,128)(2,1)}, bf16[256,512]{1,0:T(8,128)(2,1)S(1)}, u32[]{:S(2)}, u32[]{:S(2)}) collective-permute-start(bf16[256,512]{1,0:T(8,128)(2,1)} %bitcast.14), channel_id=1, source_target_pairs={{0,2},{2,0},{1,3},{3,1},{4,6},{6,4},{5,7},{7,5},{8,10},{10,8},{9,1... | collective-permute-start | bytes 786440 | tf_op jit(solution)/shard_map/ppermute | solution.py:488
  6.5 1.6 %collective-permute-start.3 = (bf16[128,1024]{1,0:T(8,128)(2,1)}, bf16[128,1024]{1,0:T(8,128)(2,1)S(1)}, u32[]{:S(2)}, u32[]{:S(2)}) collective-permute-start(bf16[128,1024]{1,0:T(8,128)(2,1)} %refs_0_.1), channel_id=1, source_target_pairs={{0,4},{4,0},{8,12},{12,8},{1,5},{5,1},{9,13},{13,9},{2,6},{6,2},{1... | collective-permute-start | bytes 786440 | tf_op jit(solution)/shard_map/ppermute | solution.py:484
  8.1 0.0 copy-start
  8.1 3.8 %stage.1 = (bf16[256,512]{1,0:T(8,128)(2,1)S(1)}, f32[1,1024]{1,0:T(1,128)S(1)}, bf16[1024,2048]{1,0:T(8,128)(2,1)S(1)}, bf16[2048,1024]{1,0:T(8,128)(2,1)S(1)}, bf16[64,1024]{1,0:T(8,128)(2,1)S(1)}) custom-call(bf16[256,512]{1,0:T(8,128)(2,1)} %bitcast.15, f32[1,1024]{1,0:T(1,128)} %bitcast.18, bf16[1024,2048]{1,0:T(8,128)(2,1)} %refs_2_.3, ...), custom_call_target="tpu_custom_call" | custom-call | flops 17829888000 | bytes 178298880 | tf_op jit(solution)/shard_map/stage/pallas_call | solution.py:168
  11.9 0.3 collective-permute-start.5
  12.2 0.0 collective-permute-done.1.refs_2_
  12.2 0.8 %collective-permute-start.2 = (bf16[64,1024]{1,0:T(8,128)(2,1)S(1)}, bf16[64,1024]{1,0:T(8,128)(2,1)S(1)}, u32[]{:S(2)}, u32[]{:S(2)}) collective-permute-start(bf16[64,1024]{1,0:T(8,128)(2,1)S(1)} %collective-permute-done.1.refs_2_), channel_id=1, source_target_pairs={{0,2},{2,0},{1,3},{3,1},{4,6},{6,4},{5,7},{7,5},{8,10},{10,8},{9,1... | collective-permute-start | bytes 393224 | tf_op jit(solution)/shard_map/ppermute | solution.py:488
  13.0 0.7 %collective-permute-start.4 = (bf16[64,1024]{1,0:T(8,128)(2,1)S(1)}, bf16[64,1024]{1,0:T(8,128)(2,1)S(1)}, u32[]{:S(2)}, u32[]{:S(2)}) collective-permute-start(bf16[64,1024]{1,0:T(8,128)(2,1)S(1)} %collective-permute-done.1.refs_2_), channel_id=1, source_target_pairs={{0,4},{4,0},{8,12},{12,8},{1,5},{5,1},{9,13},{13,9},{2,6},{6,2},{1... | collective-permute-start | bytes 393224 | tf_op jit(solution)/shard_map/ppermute | solution.py:484
  13.7 0.0 collective-permute-done.other
  13.7 0.0 copy-done
  13.7 0.0 copy-start.1
  13.7 0.0 copy-start.3
  13.7 0.0 copy-start.4
  13.7 3.3 %mlp.1 = (bf16[256,512]{1,0:T(8,128)(2,1)S(1)}, f32[256,1024]{1,0:T(8,128)S(1)}) custom-call(bf16[256,512]{1,0:T(8,128)(2,1)S(1)} %get-tuple-element.35.own, bf16[256,512]{1,0:T(8,128)(2,1)S(1)} %collective-permute-done.other, f32[1,1024]{1,0:T(1,128)S(1)} %get-tuple-element.37.gain, bf16[1024,512]{1,0:T(8,128)(2,1)S(1)} %copy-done, ...), custom_call_target="tpu_custom_call" | custom-call | flops 2415919104 | bytes 9437184 | tf_op jit(solution)/shard_map/mlp/pallas_call | solution.py:91
  17.1 0.1 collective-permute-done.2.refs_3_
  17.1 2.0 %collective-permute-done.3.refs_1_ = bf16[128,1024]{1,0:T(8,128)(2,1)S(1)} collective-permute-done((bf16[128,1024]{1,0:T(8,128)(2,1)}, bf16[128,1024]{1,0:T(8,128)(2,1)S(1)}, u32[]{:S(2)}, u32[]{:S(2)}) %collective-permute-start.3) | collective-permute-done | bytes 262176 | tf_op jit(solution)/shard_map/ppermute | solution.py:484
  19.1 0.0 copy-done.1
  19.1 0.0 copy-done.3
  19.1 0.0 copy-done.4
  19.1 1.0 %project.3 = bf16[384,1024]{1,0:T(8,128)(2,1)S(1)} custom-call(bf16[128,1024]{1,0:T(8,128)(2,1)S(1)} %copy-done.1, bf16[128,1024]{1,0:T(8,128)(2,1)S(1)} %collective-permute-done.3.refs_1_, bf16[64,1024]{1,0:T(8,128)(2,1)S(1)} %collective-permute-done.1.refs_2_, bf16[64,1024]{1,0:T(8,128)(2,1)S(1)} %collective-permute-done.2.refs_3_, ...), custom_call_target="tpu_custom_call" | custom-call | flops 60397977600 | bytes 275251200 | tf_op jit(solution)/shard_map/project/pallas_call | solution.py:196
  20.1 0.1 collective-permute-start.7
  20.2 0.0 collective-permute-done.5.refs_0_
  20.2 0.5 %project.4 = bf16[64,1024]{1,0:T(8,128)(2,1)S(1)} custom-call(bf16[64,1024]{1,0:T(8,128)(2,1)S(1)} %collective-permute-done.5.refs_0_, bf16[1024,512]{1,0:T(8,128)(2,1)S(1)} %copy-done.3, bf16[1024,512]{1,0:T(8,128)(2,1)S(1)} %copy-done.4), custom_call_target="tpu_custom_call" | custom-call | flops 10066329600 | bytes 176947200 | tf_op jit(solution)/shard_map/project/pallas_call | solution.py:196
  20.6 0.0 copy-start.5
  20.7 0.0 copy-start.7
  20.7 0.6 %collective-permute-start.8 = (bf16[64,1024]{1,0:T(8,128)(2,1)S(1)}, bf16[64,1024]{1,0:T(8,128)(2,1)S(1)}, u32[]{:S(2)}, u32[]{:S(2)}) collective-permute-start(bf16[64,1024]{1,0:T(8,128)(2,1)S(1)} %project.4), channel_id=1, source_target_pairs={{0,1},{1,0},{2,3},{3,2},{4,5},{5,4},{6,7},{7,6},{8,9},{9,8},{10,11... | collective-permute-start | bytes 393224 | tf_op jit(solution)/shard_map/ppermute | solution.py:488
  21.2 0.2 collective-permute-done.4.refs_0_
  21.5 0.5 %project.5 = bf16[64,1024]{1,0:T(8,128)(2,1)S(1)} custom-call(bf16[64,1024]{1,0:T(8,128)(2,1)S(1)} %collective-permute-done.4.refs_0_, bf16[1024,512]{1,0:T(8,128)(2,1)S(1)} %copy-done.3, bf16[1024,512]{1,0:T(8,128)(2,1)S(1)} %copy-done.4), custom_call_target="tpu_custom_call" | custom-call | flops 10066329600 | bytes 176947200 | tf_op jit(solution)/shard_map/project/pallas_call | solution.py:196
  22.0 0.1 collective-permute-start.6
  22.0 0.6 %collective-permute-done.8 = bf16[64,1024]{1,0:T(8,128)(2,1)S(1)} collective-permute-done((bf16[64,1024]{1,0:T(8,128)(2,1)S(1)}, bf16[64,1024]{1,0:T(8,128)(2,1)S(1)}, u32[]{:S(2)}, u32[]{:S(2)}) %collective-permute-start.8) | collective-permute-done | bytes 131104 | tf_op jit(solution)/shard_map/ppermute | solution.py:488
  22.6 0.0 collective-permute-done.7
  22.6 0.1 table.1.table_in
  22.7 0.6 %collective-permute-done.6 = bf16[64,1024]{1,0:T(8,128)(2,1)S(1)} collective-permute-done((bf16[64,1024]{1,0:T(8,128)(2,1)S(1)}, bf16[64,1024]{1,0:T(8,128)(2,1)S(1)}, u32[]{:S(2)}, u32[]{:S(2)}) %collective-permute-start.6) | collective-permute-done | bytes 131104 | tf_op jit(solution)/shard_map/ppermute | solution.py:488
  23.4 0.0 copy-done.5
  23.4 0.0 copy-done.7
  23.4 2.5 %attend.1 = (bf16[4,80,128]{2,1,0:T(8,128)(2,1)S(1)}, bf16[4,80,128]{2,1,0:T(8,128)(2,1)S(1)}, bf16[256,512]{1,0:T(8,128)(2,1)S(1)}, bf16[2,8,64,1024]{3,2,1,0:T(8,128)(2,1)S(1)}) custom-call(s32[4,8]{1,0:T(4,128)S(1)} %copy-done.7, bf16[256,512]{1,0:T(8,128)(2,1)S(1)} %get-tuple-element.45.q, ...), custom_call_target="tpu_custom_call", output_to_operand_aliasing={{3}: (4, {})} | custom-call | flops 13421772800 | bytes 41943040 | tf_op jit(solution)/shard_map/attend/pallas_call | solution.py:331
  25.9 0.6 %collective-permute-start.10 = (bf16[4,80,128]{2,1,0:T(8,128)(2,1)S(1)}, bf16[4,80,128]{2,1,0:T(8,128)(2,1)S(1)}, u32[]{:S(2)}, u32[]{:S(2)}) collective-permute-start(bf16[4,80,128]{2,1,0:T(8,128)(2,1)S(1)} %get-tuple-element.56), channel_id=1, source_target_pairs={{0,2},{2,0},{1,3},{3,1},{4,6},{6,4},{5,7},{7,5},{8,10},{10,8},{9,1... | collective-permute-start | bytes 245768 | tf_op jit(solution)/shard_map/ppermute | solution.py:488
  26.5 0.0 copy-start.2
  26.5 0.0 copy-start.6
  26.5 0.4 project_out.1
  27.0 0.2 copy-done.2
  27.2 0.6 %plan.1.masks = f32[4,2,4,8,128]{4,3,2,1,0:T(8,128)S(1)} custom-call(s32[1,4]{1,0:T(1,128)S(1)} %bitcast.13), custom_call_target="tpu_custom_call" | custom-call | bytes 262144 | tf_op jit(solution)/shard_map/plan/pallas_call | solution.py:391
  27.8 1.5 %collective-permute-start.9 = (bf16[4,176,128]{2,1,0:T(8,128)(2,1)S(1)}, bf16[4,176,128]{2,1,0:T(8,128)(2,1)S(1)}, u32[]{:S(2)}, u32[]{:S(2)}) collective-permute-start(bf16[4,176,128]{2,1,0:T(8,128)(2,1)S(1)} %get-tuple-element.54), channel_id=1, source_target_pairs={{0,2},{2,0},{1,3},{3,1},{4,6},{6,4},{5,7},{7,5},{8,10},{10,8},{9,1... | collective-permute-start | bytes 540680 | tf_op jit(solution)/shard_map/ppermute | solution.py:488
  29.3 1.3 %collective-permute-done.10.refs_1_.refs_2_ = bf16[4,80,128]{2,1,0:T(8,128)(2,1)S(1)} collective-permute-done((bf16[4,80,128]{2,1,0:T(8,128)(2,1)S(1)}, bf16[4,80,128]{2,1,0:T(8,128)(2,1)S(1)}, u32[]{:S(2)}, u32[]{:S(2)}) %collective-permute-start.10) | collective-permute-done | bytes 81952 | tf_op jit(solution)/shard_map/ppermute | solution.py:488
  30.6 0.0 copy-done.6
  30.6 0.1 combine.3
  30.7 1.1 %collective-permute-start.14 = (bf16[2,80,128]{2,1,0:T(8,128)(2,1)S(1)}, bf16[2,80,128]{2,1,0:T(8,128)(2,1)S(1)}, u32[]{:S(2)}, u32[]{:S(2)}) collective-permute-start(bf16[2,80,128]{2,1,0:T(8,128)(2,1)S(1)} %get-tuple-element.57), channel_id=1, source_target_pairs={{0,8},{4,12},{8,0},{12,4},{1,9},{5,13},{9,1},{13,5},{2,10},{6,14},... | collective-permute-start | bytes 122888 | tf_op jit(solution)/shard_map/ppermute | solution.py:484
  31.7 1.6 %collective-permute-start.15 = (bf16[2,80,128]{2,1,0:T(8,128)(2,1)S(1)}, bf16[2,80,128]{2,1,0:T(8,128)(2,1)S(1)}, u32[]{:S(2)}, u32[]{:S(2)}) collective-permute-start(bf16[2,80,128]{2,1,0:T(8,128)(2,1)S(1)} %get-tuple-element.63), channel_id=1, source_target_pairs={{0,12},{4,8},{8,4},{12,0},{1,13},{5,9},{9,5},{13,1},{2,14},{6,10},... | collective-permute-start | bytes 122888 | tf_op jit(solution)/shard_map/ppermute | solution.py:484
  33.3 1.0 %collective-permute-done.9.refs_1_.refs_3_ = bf16[4,176,128]{2,1,0:T(8,128)(2,1)S(1)} collective-permute-done((bf16[4,176,128]{2,1,0:T(8,128)(2,1)S(1)}, bf16[4,176,128]{2,1,0:T(8,128)(2,1)S(1)}, u32[]{:S(2)}, u32[]{:S(2)}) %collective-permute-start.9) | collective-permute-done | bytes 180256 | tf_op jit(solution)/shard_map/ppermute | solution.py:488
  34.3 0.1 combine.4
  34.4 1.8 %collective-permute-start.11 = (bf16[2,176,128]{2,1,0:T(8,128)(2,1)S(1)}, bf16[2,176,128]{2,1,0:T(8,128)(2,1)S(1)}, u32[]{:S(2)}, u32[]{:S(2)}) collective-permute-start(bf16[2,176,128]{2,1,0:T(8,128)(2,1)S(1)} %get-tuple-element.59), channel_id=1, source_target_pairs={{0,8},{4,12},{8,0},{12,4},{1,9},{5,13},{9,1},{13,5},{2,10},{6,14},... | collective-permute-start | bytes 270344 | tf_op jit(solution)/shard_map/ppermute | solution.py:484
  36.2 0.2 combine.5
  36.4 1.4 %collective-permute-start.13 = (bf16[2,256,128]{2,1,0:T(8,128)(2,1)S(1)}, bf16[2,256,128]{2,1,0:T(8,128)(2,1)S(1)}, u32[]{:S(2)}, u32[]{:S(2)}) collective-permute-start(bf16[2,256,128]{2,1,0:T(8,128)(2,1)S(1)} %get-tuple-element.62), channel_id=1, source_target_pairs={{0,4},{4,0},{8,12},{12,8},{1,5},{5,1},{9,13},{13,9},{2,6},{6,2},{1... | collective-permute-start | bytes 393224 | tf_op jit(solution)/shard_map/ppermute | solution.py:484
  37.8 1.3 %collective-permute-start.12 = (bf16[2,176,128]{2,1,0:T(8,128)(2,1)S(1)}, bf16[2,176,128]{2,1,0:T(8,128)(2,1)S(1)}, u32[]{:S(2)}, u32[]{:S(2)}) collective-permute-start(bf16[2,176,128]{2,1,0:T(8,128)(2,1)S(1)} %get-tuple-element.60), channel_id=1, source_target_pairs={{0,12},{4,8},{8,4},{12,0},{1,13},{5,9},{9,5},{13,1},{2,14},{6,10},... | collective-permute-start | bytes 270344 | tf_op jit(solution)/shard_map/ppermute | solution.py:484
  39.1 0.0 collective-permute-done.14.refs_0_
  39.1 0.0 collective-permute-done.15.refs_1_
  39.1 0.8 %place.2.refs_3_ = bf16[8,64,512]{2,1,0:T(8,128)(2,1)} custom-call(bf16[2,80,128]{2,1,0:T(8,128)(2,1)S(1)} %collective-permute-done.14.refs_0_, bf16[2,80,128]{2,1,0:T(8,128)(2,1)S(1)} %collective-permute-done.15.refs_1_, bf16[2,256,128]{2,1,0:T(8,128)(2,1)S(1)} %get-tuple-element.64.refs_2_), custom_call_target="tpu_custom_call" | custom-call | flops 42598400000 | tf_op jit(solution)/shard_map/place/pallas_call | solution.py:468
  39.9 2.9 %collective-permute-done.11.refs_0_ = bf16[2,176,128]{2,1,0:T(8,128)(2,1)S(1)} collective-permute-done((bf16[2,176,128]{2,1,0:T(8,128)(2,1)S(1)}, bf16[2,176,128]{2,1,0:T(8,128)(2,1)S(1)}, u32[]{:S(2)}, u32[]{:S(2)}) %collective-permute-start.11) | collective-permute-done | bytes 90144 | tf_op jit(solution)/shard_map/ppermute | solution.py:484
  42.8 1.6 %collective-permute-done.12.refs_1_ = bf16[2,176,128]{2,1,0:T(8,128)(2,1)S(1)} collective-permute-done((bf16[2,176,128]{2,1,0:T(8,128)(2,1)S(1)}, bf16[2,176,128]{2,1,0:T(8,128)(2,1)S(1)}, u32[]{:S(2)}, u32[]{:S(2)}) %collective-permute-start.12) | collective-permute-done | bytes 90144 | tf_op jit(solution)/shard_map/ppermute | solution.py:484
  44.4 0.1 collective-permute-done.13.refs_2_
  44.5 0.8 %place.3 = bf16[8,64,512]{2,1,0:T(8,128)(2,1)} custom-call(bf16[2,176,128]{2,1,0:T(8,128)(2,1)S(1)} %collective-permute-done.11.refs_0_, bf16[2,176,128]{2,1,0:T(8,128)(2,1)S(1)} %collective-permute-done.12.refs_1_, bf16[2,256,128]{2,1,0:T(8,128)(2,1)S(1)} %collective-permute-done.13.refs_2_, ...), custom_call_target="tpu_custom_call", output_to_operand_aliasing={{}: (3, {})} | custom-call | flops 62259200000 | tf_op jit(solution)/shard_map/place/pallas_call | solution.py:468
Async XLA Ops:
  0.9 11.2 %collective-permute-start.1 = (bf16[64,1024]{1,0:T(8,128)(2,1)S(1)}, bf16[64,1024]{1,0:T(8,128)(2,1)S(1)}, u32[]{:S(2)}, u32[]{:S(2)}) collective-permute-start(bf16[64,1024]{1,0:T(8,128)(2,1)S(1)} %pick.1), channel_id=1, source_target_pairs={{0,8},{4,12},{8,0},{12,4},{1,9},{5,13},{9,1},{13,5},{2,10},{6,14},... | collective-permute-start | bytes 393224 | tf_op jit(solution)/shard_map/ppermute | solution.py:484
  5.0 8.7 %collective-permute-start = (bf16[256,512]{1,0:T(8,128)(2,1)}, bf16[256,512]{1,0:T(8,128)(2,1)S(1)}, u32[]{:S(2)}, u32[]{:S(2)}) collective-permute-start(bf16[256,512]{1,0:T(8,128)(2,1)} %bitcast.14), channel_id=1, source_target_pairs={{0,2},{2,0},{1,3},{3,1},{4,6},{6,4},{5,7},{7,5},{8,10},{10,8},{9,1... | collective-permute-start | bytes 786440 | tf_op jit(solution)/shard_map/ppermute | solution.py:488
  6.5 12.6 %collective-permute-start.3 = (bf16[128,1024]{1,0:T(8,128)(2,1)}, bf16[128,1024]{1,0:T(8,128)(2,1)S(1)}, u32[]{:S(2)}, u32[]{:S(2)}) collective-permute-start(bf16[128,1024]{1,0:T(8,128)(2,1)} %refs_0_.1), channel_id=1, source_target_pairs={{0,4},{4,0},{8,12},{12,8},{1,5},{5,1},{9,13},{13,9},{2,6},{6,2},{1... | collective-permute-start | bytes 786440 | tf_op jit(solution)/shard_map/ppermute | solution.py:484
  8.1 5.6 %copy-start = (bf16[1024,512]{1,0:T(8,128)(2,1)S(1)}, bf16[1024,512]{1,0:T(8,128)(2,1)}, u32[]{:S(2)}) copy-start(bf16[1024,512]{1,0:T(8,128)(2,1)} %wq.1) | copy-start | bytes 3145732
  11.9 8.3 %collective-permute-start.5 = (bf16[64,1024]{1,0:T(8,128)(2,1)S(1)}, bf16[64,1024]{1,0:T(8,128)(2,1)S(1)}, u32[]{:S(2)}, u32[]{:S(2)}) collective-permute-start(bf16[64,1024]{1,0:T(8,128)(2,1)S(1)} %get-tuple-element.42), channel_id=1, source_target_pairs={{0,12},{4,8},{8,4},{12,0},{1,13},{5,9},{9,5},{13,1},{2,14},{6,10},... | collective-permute-start | bytes 393224 | tf_op jit(solution)/shard_map/ppermute | solution.py:484
  12.2 5.0 %collective-permute-start.2 = (bf16[64,1024]{1,0:T(8,128)(2,1)S(1)}, bf16[64,1024]{1,0:T(8,128)(2,1)S(1)}, u32[]{:S(2)}, u32[]{:S(2)}) collective-permute-start(bf16[64,1024]{1,0:T(8,128)(2,1)S(1)} %collective-permute-done.1.refs_2_), channel_id=1, source_target_pairs={{0,2},{2,0},{1,3},{3,1},{4,6},{6,4},{5,7},{7,5},{8,10},{10,8},{9,1... | collective-permute-start | bytes 393224 | tf_op jit(solution)/shard_map/ppermute | solution.py:488
  13.0 8.5 %collective-permute-start.4 = (bf16[64,1024]{1,0:T(8,128)(2,1)S(1)}, bf16[64,1024]{1,0:T(8,128)(2,1)S(1)}, u32[]{:S(2)}, u32[]{:S(2)}) collective-permute-start(bf16[64,1024]{1,0:T(8,128)(2,1)S(1)} %collective-permute-done.1.refs_2_), channel_id=1, source_target_pairs={{0,4},{4,0},{8,12},{12,8},{1,5},{5,1},{9,13},{13,9},{2,6},{6,2},{1... | collective-permute-start | bytes 393224 | tf_op jit(solution)/shard_map/ppermute | solution.py:484
  13.7 5.4 %copy-start.1 = (bf16[128,1024]{1,0:T(8,128)(2,1)S(1)}, bf16[128,1024]{1,0:T(8,128)(2,1)}, u32[]{:S(2)}) copy-start(bf16[128,1024]{1,0:T(8,128)(2,1)} %refs_0_.1) | copy-start | bytes 786436
  13.7 5.4 %copy-start.3 = (bf16[1024,512]{1,0:T(8,128)(2,1)S(1)}, bf16[1024,512]{1,0:T(8,128)(2,1)}, u32[]{:S(2)}) copy-start(bf16[1024,512]{1,0:T(8,128)(2,1)} %refs_1_.3) | copy-start | bytes 3145732
  13.7 5.4 %copy-start.4 = (bf16[1024,512]{1,0:T(8,128)(2,1)S(1)}, bf16[1024,512]{1,0:T(8,128)(2,1)}, u32[]{:S(2)}) copy-start(bf16[1024,512]{1,0:T(8,128)(2,1)} %refs_2_.5) | copy-start | bytes 3145732
  20.1 2.5 %collective-permute-start.7 = (bf16[384,1024]{1,0:T(8,128)(2,1)S(1)}, bf16[384,1024]{1,0:T(8,128)(2,1)S(1)}, u32[]{:S(2)}, u32[]{:S(2)}) collective-permute-start(bf16[384,1024]{1,0:T(8,128)(2,1)S(1)} %project.3), channel_id=1, source_target_pairs={{0,1},{1,0},{2,3},{3,2},{4,5},{5,4},{6,7},{7,6},{8,9},{9,8},{10,11... | collective-permute-start | bytes 2359304 | tf_op jit(solution)/shard_map/ppermute | solution.py:488
  20.6 2.7 %copy-start.5 = (bf16[512,1024]{1,0:T(8,128)(2,1)S(1)}, bf16[512,1024]{1,0:T(8,128)(2,1)}, u32[]{:S(2)}) copy-start(bf16[512,1024]{1,0:T(8,128)(2,1)} %wo.3) | copy-start | bytes 3145732
  20.7 2.7 %copy-start.7 = (s32[4,8]{1,0:T(4,128)S(1)}, s32[4,8]{1,0:T(4,128)}, u32[]{:S(2)}) copy-start(s32[4,8]{1,0:T(4,128)} %adjacency.1) | copy-start | bytes 388
  20.7 1.9 %collective-permute-start.8 = (bf16[64,1024]{1,0:T(8,128)(2,1)S(1)}, bf16[64,1024]{1,0:T(8,128)(2,1)S(1)}, u32[]{:S(2)}, u32[]{:S(2)}) collective-permute-start(bf16[64,1024]{1,0:T(8,128)(2,1)S(1)} %project.4), channel_id=1, source_target_pairs={{0,1},{1,0},{2,3},{3,2},{4,5},{5,4},{6,7},{7,6},{8,9},{9,8},{10,11... | collective-permute-start | bytes 393224 | tf_op jit(solution)/shard_map/ppermute | solution.py:488
  22.0 1.4 %collective-permute-start.6 = (bf16[64,1024]{1,0:T(8,128)(2,1)S(1)}, bf16[64,1024]{1,0:T(8,128)(2,1)S(1)}, u32[]{:S(2)}, u32[]{:S(2)}) collective-permute-start(bf16[64,1024]{1,0:T(8,128)(2,1)S(1)} %project.5), channel_id=1, source_target_pairs={{0,1},{1,0},{2,3},{3,2},{4,5},{5,4},{6,7},{7,6},{8,9},{9,8},{10,11... | collective-permute-start | bytes 393224 | tf_op jit(solution)/shard_map/ppermute | solution.py:488
  25.9 4.7 %collective-permute-start.10 = (bf16[4,80,128]{2,1,0:T(8,128)(2,1)S(1)}, bf16[4,80,128]{2,1,0:T(8,128)(2,1)S(1)}, u32[]{:S(2)}, u32[]{:S(2)}) collective-permute-start(bf16[4,80,128]{2,1,0:T(8,128)(2,1)S(1)} %get-tuple-element.56), channel_id=1, source_target_pairs={{0,2},{2,0},{1,3},{3,1},{4,6},{6,4},{5,7},{7,5},{8,10},{10,8},{9,1... | collective-permute-start | bytes 245768 | tf_op jit(solution)/shard_map/ppermute | solution.py:488
  26.5 0.7 %copy-start.2 = (s32[4,1]{0,1:T(1,128)S(1)}, s32[4,1]{0,1:T(1,128)}, u32[]{:S(2)}) copy-start(s32[4,1]{0,1:T(1,128)} %param.12) | copy-start | bytes 52
  26.5 4.1 %copy-start.6 = (bf16[4,64,512]{2,1,0:T(8,128)(2,1)S(1)}, bf16[4,64,512]{2,1,0:T(8,128)(2,1)}, u32[]{:S(2)}) copy-start(bf16[4,64,512]{2,1,0:T(8,128)(2,1)} %grid_features.5) | copy-start | bytes 786436
  27.8 6.5 %collective-permute-start.9 = (bf16[4,176,128]{2,1,0:T(8,128)(2,1)S(1)}, bf16[4,176,128]{2,1,0:T(8,128)(2,1)S(1)}, u32[]{:S(2)}, u32[]{:S(2)}) collective-permute-start(bf16[4,176,128]{2,1,0:T(8,128)(2,1)S(1)} %get-tuple-element.54), channel_id=1, source_target_pairs={{0,2},{2,0},{1,3},{3,1},{4,6},{6,4},{5,7},{7,5},{8,10},{10,8},{9,1... | collective-permute-start | bytes 540680 | tf_op jit(solution)/shard_map/ppermute | solution.py:488
  30.7 8.4 %collective-permute-start.14 = (bf16[2,80,128]{2,1,0:T(8,128)(2,1)S(1)}, bf16[2,80,128]{2,1,0:T(8,128)(2,1)S(1)}, u32[]{:S(2)}, u32[]{:S(2)}) collective-permute-start(bf16[2,80,128]{2,1,0:T(8,128)(2,1)S(1)} %get-tuple-element.57), channel_id=1, source_target_pairs={{0,8},{4,12},{8,0},{12,4},{1,9},{5,13},{9,1},{13,5},{2,10},{6,14},... | collective-permute-start | bytes 122888 | tf_op jit(solution)/shard_map/ppermute | solution.py:484
  31.7 7.4 %collective-permute-start.15 = (bf16[2,80,128]{2,1,0:T(8,128)(2,1)S(1)}, bf16[2,80,128]{2,1,0:T(8,128)(2,1)S(1)}, u32[]{:S(2)}, u32[]{:S(2)}) collective-permute-start(bf16[2,80,128]{2,1,0:T(8,128)(2,1)S(1)} %get-tuple-element.63), channel_id=1, source_target_pairs={{0,12},{4,8},{8,4},{12,0},{1,13},{5,9},{9,5},{13,1},{2,14},{6,10},... | collective-permute-start | bytes 122888 | tf_op jit(solution)/shard_map/ppermute | solution.py:484
  34.4 8.4 %collective-permute-start.11 = (bf16[2,176,128]{2,1,0:T(8,128)(2,1)S(1)}, bf16[2,176,128]{2,1,0:T(8,128)(2,1)S(1)}, u32[]{:S(2)}, u32[]{:S(2)}) collective-permute-start(bf16[2,176,128]{2,1,0:T(8,128)(2,1)S(1)} %get-tuple-element.59), channel_id=1, source_target_pairs={{0,8},{4,12},{8,0},{12,4},{1,9},{5,13},{9,1},{13,5},{2,10},{6,14},... | collective-permute-start | bytes 270344 | tf_op jit(solution)/shard_map/ppermute | solution.py:484
  36.4 8.1 %collective-permute-start.13 = (bf16[2,256,128]{2,1,0:T(8,128)(2,1)S(1)}, bf16[2,256,128]{2,1,0:T(8,128)(2,1)S(1)}, u32[]{:S(2)}, u32[]{:S(2)}) collective-permute-start(bf16[2,256,128]{2,1,0:T(8,128)(2,1)S(1)} %get-tuple-element.62), channel_id=1, source_target_pairs={{0,4},{4,0},{8,12},{12,8},{1,5},{5,1},{9,13},{13,9},{2,6},{6,2},{1... | collective-permute-start | bytes 393224 | tf_op jit(solution)/shard_map/ppermute | solution.py:484
  37.8 6.6 %collective-permute-start.12 = (bf16[2,176,128]{2,1,0:T(8,128)(2,1)S(1)}, bf16[2,176,128]{2,1,0:T(8,128)(2,1)S(1)}, u32[]{:S(2)}, u32[]{:S(2)}) collective-permute-start(bf16[2,176,128]{2,1,0:T(8,128)(2,1)S(1)} %get-tuple-element.60), channel_id=1, source_target_pairs={{0,12},{4,8},{8,4},{12,0},{1,13},{5,9},{9,5},{13,1},{2,14},{6,10},... | collective-permute-start | bytes 270344 | tf_op jit(solution)/shard_map/ppermute | solution.py:484

commit v30 on v29

--- a/solution.py
+++ b/solution.py
@@ -15,7 +15,7 @@
 QUAD = 4
 WIDE = QUAD * HEAD_DIM
 TILE = 128
-CHUNKS = ((0, 80), (80, 256))
+CHUNKS = ((0, 96), (96, 256))
 MIB = 1 << 20
 
 

time: 45.5 us -> 45.5 us (level)
  transfers between devices with their start and end apart: 16 -> 16, of which waited for: 10 -> 9; matrix products, arithmetic and copies ran while one was open for 0% -> 0% of each run, Pallas kernels for 25% -> 25%
where the time goes in v30:
time: 45.5 us; the launch traced here: 45.3 us
  starting transfers between devices  18.9 us (42%)
  Pallas kernels  15.5 us (34%)
  waiting for transfers between devices  10.4 us (23%)
    ppermute x9, starting transfers between devices, crossed(): return lax.ppermute(x, 'shard', [(i, i ^ distance) for i in range(size)])  13.8 us
    ppermute x9, waiting for transfers between devices, crossed(): return lax.ppermute(x, 'shard', [(i, i ^ distance) for i in range(size)])  6.81 us
    ppermute x7, starting transfers between devices, swapped(): return lax.ppermute(x, axis, [(0, 1), (1, 0)])  5.15 us
    pallas_call x1, Pallas kernels, run_stage(): pl.pallas_call(functools.partial(stage_kernel, axes), out_shape=tuple((ja...  3.77 us
    ppermute x7, waiting for transfers between devices, swapped(): return lax.ppermute(x, axis, [(0, 1), (1, 0)])  3.62 us
    pallas_call x1, Pallas kernels, run_mlp(): pl.pallas_call(mlp_kernel, out_shape=(jax.ShapeDtypeStruct((rows, wq.shap...  3.34 us
    pallas_call x1, Pallas kernels, run_attend(): pl.pallas_call(attend_kernel, out_shape=(part, part, jax.ShapeDtypeStruct...  2.51 us
    pallas_call x3, Pallas kernels, run_project(): pl.pallas_call(project_kernel, out_shape=jax.ShapeDtypeStruct((rows, 2 *...  1.92 us
  transfers between devices with their start and end apart: 16, of which 9 were waited for; matrix products, arithmetic and copies ran while one was open for 0% of the time, Pallas kernels for 25%

profile of v30, /device:TPU:0, one launch (start us, length us, event | category | flops | bytes accessed | tf_op | source)
XLA Modules:
  0.0 45.3 jit_solution(16856811069124038830)
XLA Ops:
  0.0 0.9 %pick.1 = bf16[64,1024]{1,0:T(8,128)(2,1)S(1)} custom-call(bf16[128,1024]{1,0:T(8,128)(2,1)} %refs_0_.1), custom_call_target="tpu_custom_call" | custom-call | bytes 524288 | tf_op jit(solution)/shard_map/pick/pallas_call | solution.py:118
  0.9 4.1 %collective-permute-start.1 = (bf16[64,1024]{1,0:T(8,128)(2,1)S(1)}, bf16[64,1024]{1,0:T(8,128)(2,1)S(1)}, u32[]{:S(2)}, u32[]{:S(2)}) collective-permute-start(bf16[64,1024]{1,0:T(8,128)(2,1)S(1)} %pick.1), channel_id=1, source_target_pairs={{0,8},{4,12},{8,0},{12,4},{1,9},{5,13},{9,1},{13,5},{2,10},{6,14},... | collective-permute-start | bytes 393224 | tf_op jit(solution)/shard_map/ppermute | solution.py:484
  5.0 1.5 %collective-permute-start = (bf16[256,512]{1,0:T(8,128)(2,1)}, bf16[256,512]{1,0:T(8,128)(2,1)S(1)}, u32[]{:S(2)}, u32[]{:S(2)}) collective-permute-start(bf16[256,512]{1,0:T(8,128)(2,1)} %bitcast.14), channel_id=1, source_target_pairs={{0,2},{2,0},{1,3},{3,1},{4,6},{6,4},{5,7},{7,5},{8,10},{10,8},{9,1... | collective-permute-start | bytes 786440 | tf_op jit(solution)/shard_map/ppermute | solution.py:488
  6.5 1.6 %collective-permute-start.3 = (bf16[128,1024]{1,0:T(8,128)(2,1)}, bf16[128,1024]{1,0:T(8,128)(2,1)S(1)}, u32[]{:S(2)}, u32[]{:S(2)}) collective-permute-start(bf16[128,1024]{1,0:T(8,128)(2,1)} %refs_0_.1), channel_id=1, source_target_pairs={{0,4},{4,0},{8,12},{12,8},{1,5},{5,1},{9,13},{13,9},{2,6},{6,2},{1... | collective-permute-start | bytes 786440 | tf_op jit(solution)/shard_map/ppermute | solution.py:484
  8.1 0.0 copy-start
  8.1 3.8 %stage.1 = (bf16[256,512]{1,0:T(8,128)(2,1)S(1)}, f32[1,1024]{1,0:T(1,128)S(1)}, bf16[1024,2048]{1,0:T(8,128)(2,1)S(1)}, bf16[2048,1024]{1,0:T(8,128)(2,1)S(1)}, bf16[64,1024]{1,0:T(8,128)(2,1)S(1)}) custom-call(bf16[256,512]{1,0:T(8,128)(2,1)} %bitcast.15, f32[1,1024]{1,0:T(1,128)} %bitcast.18, bf16[1024,2048]{1,0:T(8,128)(2,1)} %refs_2_.3, ...), custom_call_target="tpu_custom_call" | custom-call | flops 17829888000 | bytes 178298880 | tf_op jit(solution)/shard_map/stage/pallas_call | solution.py:168
  11.9 0.3 collective-permute-start.5
  12.2 0.0 collective-permute-done.1.refs_2_
  12.2 0.8 %collective-permute-start.2 = (bf16[64,1024]{1,0:T(8,128)(2,1)S(1)}, bf16[64,1024]{1,0:T(8,128)(2,1)S(1)}, u32[]{:S(2)}, u32[]{:S(2)}) collective-permute-start(bf16[64,1024]{1,0:T(8,128)(2,1)S(1)} %collective-permute-done.1.refs_2_), channel_id=1, source_target_pairs={{0,2},{2,0},{1,3},{3,1},{4,6},{6,4},{5,7},{7,5},{8,10},{10,8},{9,1... | collective-permute-start | bytes 393224 | tf_op jit(solution)/shard_map/ppermute | solution.py:488
  13.0 0.7 %collective-permute-start.4 = (bf16[64,1024]{1,0:T(8,128)(2,1)S(1)}, bf16[64,1024]{1,0:T(8,128)(2,1)S(1)}, u32[]{:S(2)}, u32[]{:S(2)}) collective-permute-start(bf16[64,1024]{1,0:T(8,128)(2,1)S(1)} %collective-permute-done.1.refs_2_), channel_id=1, source_target_pairs={{0,4},{4,0},{8,12},{12,8},{1,5},{5,1},{9,13},{13,9},{2,6},{6,2},{1... | collective-permute-start | bytes 393224 | tf_op jit(solution)/shard_map/ppermute | solution.py:484
  13.7 0.0 collective-permute-done.other
  13.7 0.0 copy-done
  13.7 0.0 copy-start.1
  13.7 0.0 copy-start.3
  13.7 0.0 copy-start.4
  13.7 3.3 %mlp.1 = (bf16[256,512]{1,0:T(8,128)(2,1)S(1)}, f32[256,1024]{1,0:T(8,128)S(1)}) custom-call(bf16[256,512]{1,0:T(8,128)(2,1)S(1)} %get-tuple-element.35.own, bf16[256,512]{1,0:T(8,128)(2,1)S(1)} %collective-permute-done.other, f32[1,1024]{1,0:T(1,128)S(1)} %get-tuple-element.37.gain, bf16[1024,512]{1,0:T(8,128)(2,1)S(1)} %copy-done, ...), custom_call_target="tpu_custom_call" | custom-call | flops 2415919104 | bytes 9437184 | tf_op jit(solution)/shard_map/mlp/pallas_call | solution.py:91
  17.1 0.1 collective-permute-done.2.refs_3_
  17.1 2.0 %collective-permute-done.3.refs_1_ = bf16[128,1024]{1,0:T(8,128)(2,1)S(1)} collective-permute-done((bf16[128,1024]{1,0:T(8,128)(2,1)}, bf16[128,1024]{1,0:T(8,128)(2,1)S(1)}, u32[]{:S(2)}, u32[]{:S(2)}) %collective-permute-start.3) | collective-permute-done | bytes 262176 | tf_op jit(solution)/shard_map/ppermute | solution.py:484
  19.1 0.0 copy-done.1
  19.1 0.0 copy-done.3
  19.1 0.0 copy-done.4
  19.1 1.0 %project.3 = bf16[384,1024]{1,0:T(8,128)(2,1)S(1)} custom-call(bf16[128,1024]{1,0:T(8,128)(2,1)S(1)} %copy-done.1, bf16[128,1024]{1,0:T(8,128)(2,1)S(1)} %collective-permute-done.3.refs_1_, bf16[64,1024]{1,0:T(8,128)(2,1)S(1)} %collective-permute-done.1.refs_2_, bf16[64,1024]{1,0:T(8,128)(2,1)S(1)} %collective-permute-done.2.refs_3_, ...), custom_call_target="tpu_custom_call" | custom-call | flops 60397977600 | bytes 275251200 | tf_op jit(solution)/shard_map/project/pallas_call | solution.py:196
  20.1 0.1 collective-permute-start.7
  20.2 0.0 collective-permute-done.5.refs_0_
  20.2 0.5 %project.4 = bf16[64,1024]{1,0:T(8,128)(2,1)S(1)} custom-call(bf16[64,1024]{1,0:T(8,128)(2,1)S(1)} %collective-permute-done.5.refs_0_, bf16[1024,512]{1,0:T(8,128)(2,1)S(1)} %copy-done.3, bf16[1024,512]{1,0:T(8,128)(2,1)S(1)} %copy-done.4), custom_call_target="tpu_custom_call" | custom-call | flops 10066329600 | bytes 176947200 | tf_op jit(solution)/shard_map/project/pallas_call | solution.py:196
  20.6 0.0 copy-start.5
  20.7 0.0 copy-start.7
  20.7 0.6 %collective-permute-start.8 = (bf16[64,1024]{1,0:T(8,128)(2,1)S(1)}, bf16[64,1024]{1,0:T(8,128)(2,1)S(1)}, u32[]{:S(2)}, u32[]{:S(2)}) collective-permute-start(bf16[64,1024]{1,0:T(8,128)(2,1)S(1)} %project.4), channel_id=1, source_target_pairs={{0,1},{1,0},{2,3},{3,2},{4,5},{5,4},{6,7},{7,6},{8,9},{9,8},{10,11... | collective-permute-start | bytes 393224 | tf_op jit(solution)/shard_map/ppermute | solution.py:488
  21.2 0.2 collective-permute-done.4.refs_0_
  21.5 0.5 %project.5 = bf16[64,1024]{1,0:T(8,128)(2,1)S(1)} custom-call(bf16[64,1024]{1,0:T(8,128)(2,1)S(1)} %collective-permute-done.4.refs_0_, bf16[1024,512]{1,0:T(8,128)(2,1)S(1)} %copy-done.3, bf16[1024,512]{1,0:T(8,128)(2,1)S(1)} %copy-done.4), custom_call_target="tpu_custom_call" | custom-call | flops 10066329600 | bytes 176947200 | tf_op jit(solution)/shard_map/project/pallas_call | solution.py:196
  22.0 0.1 collective-permute-start.6
  22.0 0.6 %collective-permute-done.8 = bf16[64,1024]{1,0:T(8,128)(2,1)S(1)} collective-permute-done((bf16[64,1024]{1,0:T(8,128)(2,1)S(1)}, bf16[64,1024]{1,0:T(8,128)(2,1)S(1)}, u32[]{:S(2)}, u32[]{:S(2)}) %collective-permute-start.8) | collective-permute-done | bytes 131104 | tf_op jit(solution)/shard_map/ppermute | solution.py:488
  22.6 0.0 collective-permute-done.7
  22.6 0.1 table.1.table_in
  22.7 0.6 %collective-permute-done.6 = bf16[64,1024]{1,0:T(8,128)(2,1)S(1)} collective-permute-done((bf16[64,1024]{1,0:T(8,128)(2,1)S(1)}, bf16[64,1024]{1,0:T(8,128)(2,1)S(1)}, u32[]{:S(2)}, u32[]{:S(2)}) %collective-permute-start.6) | collective-permute-done | bytes 131104 | tf_op jit(solution)/shard_map/ppermute | solution.py:488
  23.4 0.0 copy-done.5
  23.4 0.0 copy-done.7
  23.4 2.5 %attend.1 = (bf16[4,96,128]{2,1,0:T(8,128)(2,1)S(1)}, bf16[4,96,128]{2,1,0:T(8,128)(2,1)S(1)}, bf16[256,512]{1,0:T(8,128)(2,1)S(1)}, bf16[2,8,64,1024]{3,2,1,0:T(8,128)(2,1)S(1)}) custom-call(s32[4,8]{1,0:T(4,128)S(1)} %copy-done.7, bf16[256,512]{1,0:T(8,128)(2,1)S(1)} %get-tuple-element.45.q, ...), custom_call_target="tpu_custom_call", output_to_operand_aliasing={{3}: (4, {})} | custom-call | flops 13421772800 | bytes 41943040 | tf_op jit(solution)/shard_map/attend/pallas_call | solution.py:331
  25.9 0.6 %collective-permute-start.10 = (bf16[4,96,128]{2,1,0:T(8,128)(2,1)S(1)}, bf16[4,96,128]{2,1,0:T(8,128)(2,1)S(1)}, u32[]{:S(2)}, u32[]{:S(2)}) collective-permute-start(bf16[4,96,128]{2,1,0:T(8,128)(2,1)S(1)} %get-tuple-element.56), channel_id=1, source_target_pairs={{0,2},{2,0},{1,3},{3,1},{4,6},{6,4},{5,7},{7,5},{8,10},{10,8},{9,1... | collective-permute-start | bytes 294920 | tf_op jit(solution)/shard_map/ppermute | solution.py:488
  26.5 0.0 copy-start.2
  26.5 0.0 copy-start.6
  26.5 0.4 project_out.1
  27.0 0.2 copy-done.2
  27.2 0.6 %plan.1.masks = f32[4,2,4,8,128]{4,3,2,1,0:T(8,128)S(1)} custom-call(s32[1,4]{1,0:T(1,128)S(1)} %bitcast.13), custom_call_target="tpu_custom_call" | custom-call | bytes 262144 | tf_op jit(solution)/shard_map/plan/pallas_call | solution.py:391
  27.8 1.5 %collective-permute-start.9 = (bf16[4,160,128]{2,1,0:T(8,128)(2,1)S(1)}, bf16[4,160,128]{2,1,0:T(8,128)(2,1)S(1)}, u32[]{:S(2)}, u32[]{:S(2)}) collective-permute-start(bf16[4,160,128]{2,1,0:T(8,128)(2,1)S(1)} %get-tuple-element.54), channel_id=1, source_target_pairs={{0,2},{2,0},{1,3},{3,1},{4,6},{6,4},{5,7},{7,5},{8,10},{10,8},{9,1... | collective-permute-start | bytes 491528 | tf_op jit(solution)/shard_map/ppermute | solution.py:488
  29.3 2.0 %collective-permute-done.10.refs_1_.refs_2_ = bf16[4,96,128]{2,1,0:T(8,128)(2,1)S(1)} collective-permute-done((bf16[4,96,128]{2,1,0:T(8,128)(2,1)S(1)}, bf16[4,96,128]{2,1,0:T(8,128)(2,1)S(1)}, u32[]{:S(2)}, u32[]{:S(2)}) %collective-permute-start.10) | collective-permute-done | bytes 98336 | tf_op jit(solution)/shard_map/ppermute | solution.py:488
  31.3 0.0 copy-done.6
  31.3 0.1 combine.3
  31.4 0.7 %collective-permute-start.14 = (bf16[2,96,128]{2,1,0:T(8,128)(2,1)S(1)}, bf16[2,96,128]{2,1,0:T(8,128)(2,1)S(1)}, u32[]{:S(2)}, u32[]{:S(2)}) collective-permute-start(bf16[2,96,128]{2,1,0:T(8,128)(2,1)S(1)} %get-tuple-element.57), channel_id=1, source_target_pairs={{0,8},{4,12},{8,0},{12,4},{1,9},{5,13},{9,1},{13,5},{2,10},{6,14},... | collective-permute-start | bytes 147464 | tf_op jit(solution)/shard_map/ppermute | solution.py:484
  32.1 1.9 %collective-permute-start.15 = (bf16[2,96,128]{2,1,0:T(8,128)(2,1)S(1)}, bf16[2,96,128]{2,1,0:T(8,128)(2,1)S(1)}, u32[]{:S(2)}, u32[]{:S(2)}) collective-permute-start(bf16[2,96,128]{2,1,0:T(8,128)(2,1)S(1)} %get-tuple-element.63), channel_id=1, source_target_pairs={{0,12},{4,8},{8,4},{12,0},{1,13},{5,9},{9,5},{13,1},{2,14},{6,10},... | collective-permute-start | bytes 147464 | tf_op jit(solution)/shard_map/ppermute | solution.py:484
  34.0 0.3 collective-permute-done.9.refs_1_.refs_3_
  34.3 0.1 combine.4
  34.4 1.7 %collective-permute-start.11 = (bf16[2,160,128]{2,1,0:T(8,128)(2,1)S(1)}, bf16[2,160,128]{2,1,0:T(8,128)(2,1)S(1)}, u32[]{:S(2)}, u32[]{:S(2)}) collective-permute-start(bf16[2,160,128]{2,1,0:T(8,128)(2,1)S(1)} %get-tuple-element.59), channel_id=1, source_target_pairs={{0,8},{4,12},{8,0},{12,4},{1,9},{5,13},{9,1},{13,5},{2,10},{6,14},... | collective-permute-start | bytes 245768 | tf_op jit(solution)/shard_map/ppermute | solution.py:484
  36.1 0.2 combine.5
  36.3 1.5 %collective-permute-start.13 = (bf16[2,256,128]{2,1,0:T(8,128)(2,1)S(1)}, bf16[2,256,128]{2,1,0:T(8,128)(2,1)S(1)}, u32[]{:S(2)}, u32[]{:S(2)}) collective-permute-start(bf16[2,256,128]{2,1,0:T(8,128)(2,1)S(1)} %get-tuple-element.62), channel_id=1, source_target_pairs={{0,4},{4,0},{8,12},{12,8},{1,5},{5,1},{9,13},{13,9},{2,6},{6,2},{1... | collective-permute-start | bytes 393224 | tf_op jit(solution)/shard_map/ppermute | solution.py:484
  37.8 1.3 %collective-permute-start.12 = (bf16[2,160,128]{2,1,0:T(8,128)(2,1)S(1)}, bf16[2,160,128]{2,1,0:T(8,128)(2,1)S(1)}, u32[]{:S(2)}, u32[]{:S(2)}) collective-permute-start(bf16[2,160,128]{2,1,0:T(8,128)(2,1)S(1)} %get-tuple-element.60), channel_id=1, source_target_pairs={{0,12},{4,8},{8,4},{12,0},{1,13},{5,9},{9,5},{13,1},{2,14},{6,10},... | collective-permute-start | bytes 245768 | tf_op jit(solution)/shard_map/ppermute | solution.py:484
  39.1 0.0 collective-permute-done.14.refs_0_
  39.1 0.0 collective-permute-done.15.refs_1_
  39.1 0.8 %place.2.refs_3_ = bf16[8,64,512]{2,1,0:T(8,128)(2,1)} custom-call(bf16[2,96,128]{2,1,0:T(8,128)(2,1)S(1)} %collective-permute-done.14.refs_0_, bf16[2,96,128]{2,1,0:T(8,128)(2,1)S(1)} %collective-permute-done.15.refs_1_, bf16[2,256,128]{2,1,0:T(8,128)(2,1)S(1)} %get-tuple-element.64.refs_2_), custom_call_target="tpu_custom_call" | custom-call | flops 45875200000 | tf_op jit(solution)/shard_map/place/pallas_call | solution.py:468
  39.9 3.3 %collective-permute-done.11.refs_0_ = bf16[2,160,128]{2,1,0:T(8,128)(2,1)S(1)} collective-permute-done((bf16[2,160,128]{2,1,0:T(8,128)(2,1)S(1)}, bf16[2,160,128]{2,1,0:T(8,128)(2,1)S(1)}, u32[]{:S(2)}, u32[]{:S(2)}) %collective-permute-start.11) | collective-permute-done | bytes 81952 | tf_op jit(solution)/shard_map/ppermute | solution.py:484
  43.2 1.3 %collective-permute-done.12.refs_1_ = bf16[2,160,128]{2,1,0:T(8,128)(2,1)S(1)} collective-permute-done((bf16[2,160,128]{2,1,0:T(8,128)(2,1)S(1)}, bf16[2,160,128]{2,1,0:T(8,128)(2,1)S(1)}, u32[]{:S(2)}, u32[]{:S(2)}) %collective-permute-start.12) | collective-permute-done | bytes 81952 | tf_op jit(solution)/shard_map/ppermute | solution.py:484
  44.5 0.0 collective-permute-done.13.refs_2_
  44.5 0.8 %place.3 = bf16[8,64,512]{2,1,0:T(8,128)(2,1)} custom-call(bf16[2,160,128]{2,1,0:T(8,128)(2,1)S(1)} %collective-permute-done.11.refs_0_, bf16[2,160,128]{2,1,0:T(8,128)(2,1)S(1)} %collective-permute-done.12.refs_1_, bf16[2,256,128]{2,1,0:T(8,128)(2,1)S(1)} %collective-permute-done.13.refs_2_, ...), custom_call_target="tpu_custom_call", output_to_operand_aliasing={{}: (3, {})} | custom-call | flops 58982400000 | tf_op jit(solution)/shard_map/place/pallas_call | solution.py:468
Async XLA Ops:
  0.9 11.2 %collective-permute-start.1 = (bf16[64,1024]{1,0:T(8,128)(2,1)S(1)}, bf16[64,1024]{1,0:T(8,128)(2,1)S(1)}, u32[]{:S(2)}, u32[]{:S(2)}) collective-permute-start(bf16[64,1024]{1,0:T(8,128)(2,1)S(1)} %pick.1), channel_id=1, source_target_pairs={{0,8},{4,12},{8,0},{12,4},{1,9},{5,13},{9,1},{13,5},{2,10},{6,14},... | collective-permute-start | bytes 393224 | tf_op jit(solution)/shard_map/ppermute | solution.py:484
  5.0 8.7 %collective-permute-start = (bf16[256,512]{1,0:T(8,128)(2,1)}, bf16[256,512]{1,0:T(8,128)(2,1)S(1)}, u32[]{:S(2)}, u32[]{:S(2)}) collective-permute-start(bf16[256,512]{1,0:T(8,128)(2,1)} %bitcast.14), channel_id=1, source_target_pairs={{0,2},{2,0},{1,3},{3,1},{4,6},{6,4},{5,7},{7,5},{8,10},{10,8},{9,1... | collective-permute-start | bytes 786440 | tf_op jit(solution)/shard_map/ppermute | solution.py:488
  6.5 12.6 %collective-permute-start.3 = (bf16[128,1024]{1,0:T(8,128)(2,1)}, bf16[128,1024]{1,0:T(8,128)(2,1)S(1)}, u32[]{:S(2)}, u32[]{:S(2)}) collective-permute-start(bf16[128,1024]{1,0:T(8,128)(2,1)} %refs_0_.1), channel_id=1, source_target_pairs={{0,4},{4,0},{8,12},{12,8},{1,5},{5,1},{9,13},{13,9},{2,6},{6,2},{1... | collective-permute-start | bytes 786440 | tf_op jit(solution)/shard_map/ppermute | solution.py:484
  8.1 5.6 %copy-start = (bf16[1024,512]{1,0:T(8,128)(2,1)S(1)}, bf16[1024,512]{1,0:T(8,128)(2,1)}, u32[]{:S(2)}) copy-start(bf16[1024,512]{1,0:T(8,128)(2,1)} %wq.1) | copy-start | bytes 3145732
  11.9 8.3 %collective-permute-start.5 = (bf16[64,1024]{1,0:T(8,128)(2,1)S(1)}, bf16[64,1024]{1,0:T(8,128)(2,1)S(1)}, u32[]{:S(2)}, u32[]{:S(2)}) collective-permute-start(bf16[64,1024]{1,0:T(8,128)(2,1)S(1)} %get-tuple-element.42), channel_id=1, source_target_pairs={{0,12},{4,8},{8,4},{12,0},{1,13},{5,9},{9,5},{13,1},{2,14},{6,10},... | collective-permute-start | bytes 393224 | tf_op jit(solution)/shard_map/ppermute | solution.py:484
  12.2 5.0 %collective-permute-start.2 = (bf16[64,1024]{1,0:T(8,128)(2,1)S(1)}, bf16[64,1024]{1,0:T(8,128)(2,1)S(1)}, u32[]{:S(2)}, u32[]{:S(2)}) collective-permute-start(bf16[64,1024]{1,0:T(8,128)(2,1)S(1)} %collective-permute-done.1.refs_2_), channel_id=1, source_target_pairs={{0,2},{2,0},{1,3},{3,1},{4,6},{6,4},{5,7},{7,5},{8,10},{10,8},{9,1... | collective-permute-start | bytes 393224 | tf_op jit(solution)/shard_map/ppermute | solution.py:488
  13.0 8.5 %collective-permute-start.4 = (bf16[64,1024]{1,0:T(8,128)(2,1)S(1)}, bf16[64,1024]{1,0:T(8,128)(2,1)S(1)}, u32[]{:S(2)}, u32[]{:S(2)}) collective-permute-start(bf16[64,1024]{1,0:T(8,128)(2,1)S(1)} %collective-permute-done.1.refs_2_), channel_id=1, source_target_pairs={{0,4},{4,0},{8,12},{12,8},{1,5},{5,1},{9,13},{13,9},{2,6},{6,2},{1... | collective-permute-start | bytes 393224 | tf_op jit(solution)/shard_map/ppermute | solution.py:484
  13.7 5.4 %copy-start.1 = (bf16[128,1024]{1,0:T(8,128)(2,1)S(1)}, bf16[128,1024]{1,0:T(8,128)(2,1)}, u32[]{:S(2)}) copy-start(bf16[128,1024]{1,0:T(8,128)(2,1)} %refs_0_.1) | copy-start | bytes 786436
  13.7 5.4 %copy-start.3 = (bf16[1024,512]{1,0:T(8,128)(2,1)S(1)}, bf16[1024,512]{1,0:T(8,128)(2,1)}, u32[]{:S(2)}) copy-start(bf16[1024,512]{1,0:T(8,128)(2,1)} %refs_1_.3) | copy-start | bytes 3145732
  13.7 5.4 %copy-start.4 = (bf16[1024,512]{1,0:T(8,128)(2,1)S(1)}, bf16[1024,512]{1,0:T(8,128)(2,1)}, u32[]{:S(2)}) copy-start(bf16[1024,512]{1,0:T(8,128)(2,1)} %refs_2_.5) | copy-start | bytes 3145732
  20.1 2.5 %collective-permute-start.7 = (bf16[384,1024]{1,0:T(8,128)(2,1)S(1)}, bf16[384,1024]{1,0:T(8,128)(2,1)S(1)}, u32[]{:S(2)}, u32[]{:S(2)}) collective-permute-start(bf16[384,1024]{1,0:T(8,128)(2,1)S(1)} %project.3), channel_id=1, source_target_pairs={{0,1},{1,0},{2,3},{3,2},{4,5},{5,4},{6,7},{7,6},{8,9},{9,8},{10,11... | collective-permute-start | bytes 2359304 | tf_op jit(solution)/shard_map/ppermute | solution.py:488
  20.6 2.7 %copy-start.5 = (bf16[512,1024]{1,0:T(8,128)(2,1)S(1)}, bf16[512,1024]{1,0:T(8,128)(2,1)}, u32[]{:S(2)}) copy-start(bf16[512,1024]{1,0:T(8,128)(2,1)} %wo.3) | copy-start | bytes 3145732
  20.7 2.7 %copy-start.7 = (s32[4,8]{1,0:T(4,128)S(1)}, s32[4,8]{1,0:T(4,128)}, u32[]{:S(2)}) copy-start(s32[4,8]{1,0:T(4,128)} %adjacency.1) | copy-start | bytes 388
  20.7 1.9 %collective-permute-start.8 = (bf16[64,1024]{1,0:T(8,128)(2,1)S(1)}, bf16[64,1024]{1,0:T(8,128)(2,1)S(1)}, u32[]{:S(2)}, u32[]{:S(2)}) collective-permute-start(bf16[64,1024]{1,0:T(8,128)(2,1)S(1)} %project.4), channel_id=1, source_target_pairs={{0,1},{1,0},{2,3},{3,2},{4,5},{5,4},{6,7},{7,6},{8,9},{9,8},{10,11... | collective-permute-start | bytes 393224 | tf_op jit(solution)/shard_map/ppermute | solution.py:488
  22.0 1.4 %collective-permute-start.6 = (bf16[64,1024]{1,0:T(8,128)(2,1)S(1)}, bf16[64,1024]{1,0:T(8,128)(2,1)S(1)}, u32[]{:S(2)}, u32[]{:S(2)}) collective-permute-start(bf16[64,1024]{1,0:T(8,128)(2,1)S(1)} %project.5), channel_id=1, source_target_pairs={{0,1},{1,0},{2,3},{3,2},{4,5},{5,4},{6,7},{7,6},{8,9},{9,8},{10,11... | collective-permute-start | bytes 393224 | tf_op jit(solution)/shard_map/ppermute | solution.py:488
  25.9 5.4 %collective-permute-start.10 = (bf16[4,96,128]{2,1,0:T(8,128)(2,1)S(1)}, bf16[4,96,128]{2,1,0:T(8,128)(2,1)S(1)}, u32[]{:S(2)}, u32[]{:S(2)}) collective-permute-start(bf16[4,96,128]{2,1,0:T(8,128)(2,1)S(1)} %get-tuple-element.56), channel_id=1, source_target_pairs={{0,2},{2,0},{1,3},{3,1},{4,6},{6,4},{5,7},{7,5},{8,10},{10,8},{9,1... | collective-permute-start | bytes 294920 | tf_op jit(solution)/shard_map/ppermute | solution.py:488
  26.5 0.7 %copy-start.2 = (s32[4,1]{0,1:T(1,128)S(1)}, s32[4,1]{0,1:T(1,128)}, u32[]{:S(2)}) copy-start(s32[4,1]{0,1:T(1,128)} %param.12) | copy-start | bytes 52
  26.5 4.8 %copy-start.6 = (bf16[4,64,512]{2,1,0:T(8,128)(2,1)S(1)}, bf16[4,64,512]{2,1,0:T(8,128)(2,1)}, u32[]{:S(2)}) copy-start(bf16[4,64,512]{2,1,0:T(8,128)(2,1)} %grid_features.5) | copy-start | bytes 786436
  27.8 6.5 %collective-permute-start.9 = (bf16[4,160,128]{2,1,0:T(8,128)(2,1)S(1)}, bf16[4,160,128]{2,1,0:T(8,128)(2,1)S(1)}, u32[]{:S(2)}, u32[]{:S(2)}) collective-permute-start(bf16[4,160,128]{2,1,0:T(8,128)(2,1)S(1)} %get-tuple-element.54), channel_id=1, source_target_pairs={{0,2},{2,0},{1,3},{3,1},{4,6},{6,4},{5,7},{7,5},{8,10},{10,8},{9,1... | collective-permute-start | bytes 491528 | tf_op jit(solution)/shard_map/ppermute | solution.py:488
  31.4 7.7 %collective-permute-start.14 = (bf16[2,96,128]{2,1,0:T(8,128)(2,1)S(1)}, bf16[2,96,128]{2,1,0:T(8,128)(2,1)S(1)}, u32[]{:S(2)}, u32[]{:S(2)}) collective-permute-start(bf16[2,96,128]{2,1,0:T(8,128)(2,1)S(1)} %get-tuple-element.57), channel_id=1, source_target_pairs={{0,8},{4,12},{8,0},{12,4},{1,9},{5,13},{9,1},{13,5},{2,10},{6,14},... | collective-permute-start | bytes 147464 | tf_op jit(solution)/shard_map/ppermute | solution.py:484
  32.1 7.0 %collective-permute-start.15 = (bf16[2,96,128]{2,1,0:T(8,128)(2,1)S(1)}, bf16[2,96,128]{2,1,0:T(8,128)(2,1)S(1)}, u32[]{:S(2)}, u32[]{:S(2)}) collective-permute-start(bf16[2,96,128]{2,1,0:T(8,128)(2,1)S(1)} %get-tuple-element.63), channel_id=1, source_target_pairs={{0,12},{4,8},{8,4},{12,0},{1,13},{5,9},{9,5},{13,1},{2,14},{6,10},... | collective-permute-start | bytes 147464 | tf_op jit(solution)/shard_map/ppermute | solution.py:484
  34.4 8.8 %collective-permute-start.11 = (bf16[2,160,128]{2,1,0:T(8,128)(2,1)S(1)}, bf16[2,160,128]{2,1,0:T(8,128)(2,1)S(1)}, u32[]{:S(2)}, u32[]{:S(2)}) collective-permute-start(bf16[2,160,128]{2,1,0:T(8,128)(2,1)S(1)} %get-tuple-element.59), channel_id=1, source_target_pairs={{0,8},{4,12},{8,0},{12,4},{1,9},{5,13},{9,1},{13,5},{2,10},{6,14},... | collective-permute-start | bytes 245768 | tf_op jit(solution)/shard_map/ppermute | solution.py:484
  36.3 8.2 %collective-permute-start.13 = (bf16[2,256,128]{2,1,0:T(8,128)(2,1)S(1)}, bf16[2,256,128]{2,1,0:T(8,128)(2,1)S(1)}, u32[]{:S(2)}, u32[]{:S(2)}) collective-permute-start(bf16[2,256,128]{2,1,0:T(8,128)(2,1)S(1)} %get-tuple-element.62), channel_id=1, source_target_pairs={{0,4},{4,0},{8,12},{12,8},{1,5},{5,1},{9,13},{13,9},{2,6},{6,2},{1... | collective-permute-start | bytes 393224 | tf_op jit(solution)/shard_map/ppermute | solution.py:484
  37.8 6.7 %collective-permute-start.12 = (bf16[2,160,128]{2,1,0:T(8,128)(2,1)S(1)}, bf16[2,160,128]{2,1,0:T(8,128)(2,1)S(1)}, u32[]{:S(2)}, u32[]{:S(2)}) collective-permute-start(bf16[2,160,128]{2,1,0:T(8,128)(2,1)S(1)} %get-tuple-element.60), channel_id=1, source_target_pairs={{0,12},{4,8},{8,4},{12,0},{1,13},{5,9},{9,5},{13,1},{2,14},{6,10},... | collective-permute-start | bytes 245768 | tf_op jit(solution)/shard_map/ppermute | solution.py:484
